TPU v7x, 32 devices: a whole 2x2x4 slice. The times are simulated.
32 devices in a mesh: groups: 2 (over y), batch: 4 (over z), ctx: 2 (over x), head: 2 (over core).
Axes of the slice: x: 2, y: 2, z: 4, core: 2. Of those that a mesh axis runs over, the one named last changes fastest.
Arguments:
- tokens: bfloat16 [2048, 16384], P(('groups', 'batch'), ('ctx', 'head')), parts along dimension 0, may hold values from -6 to 6
- key_weight: bfloat16 [2, 2, 4096, 4, 2, 128], P('ctx', 'head', 'batch'), may hold values from -0.046875 to 0.046875
- value_weight: bfloat16 [2, 2, 4096, 4, 2, 128], P('ctx', 'head', 'batch'), may hold values from -0.09375 to 0.09375
- queries: bfloat16 [2048, 4, 2, 2048], P(('groups', 'batch'), 'ctx', 'head'), parts along dimension 0, may hold values from -8 to 8
- prefix_pool: bfloat16 [32, 128, 4, 2, 256], P(('groups', 'ctx'), None, None, 'head'), parts along dimension 0, may hold values from -8 to 8
- block_table: int32 [8, 8], P(('groups', 'batch')), parts along dimension 0, may hold values from 0 to 15, as said below
- lengths: int32 [8], P(('groups', 'batch')), parts along dimension 0, may hold values from 128 to 256, as said below
Outputs:
- attended: bfloat16 [2048, 4, 2, 2048], P(('groups', 'batch'), 'ctx', 'head'), parts along dimension 0
There are 2 independent parts, one for each index of `groups`. A program takes and returns all parts, laid end to end along the dimension named above; an argument that names none is the same for every part. Nothing has to cross between parts.
Inputs may be any that keep to these rules, and one draw needn't show every extreme that they name: `block_table`: each row names 8 different pool blocks. `lengths`: each a multiple of 128; some prompt has 256 and some has 128.
All inputs are finite; a program needn't handle non-finite values.
Results may differ from a plain program's by a relative error of at most 0.0073.
Values may be sent and summed in bfloat16 or wider, within the bound.
No kernel may reach another device: no remote copies, remote signals or barrier semaphores. Data moves between devices by JAX's collectives and lax.ppermute only.
A program may use at most 128 MiB of HBM per device.

v0:
```python
import jax
import jax.numpy as jnp
from jax import lax
from jax.sharding import PartitionSpec as P


def attend_head(query_rows, prefix, fresh_rows, length):
    token_count = query_rows.shape[0]
    head_width = prefix.shape[1] // 2
    group_size = query_rows.shape[1] // head_width
    prefix_len = prefix.shape[0]
    key_rows = jnp.concatenate([prefix[:, :head_width], fresh_rows[:, :head_width]], 0)
    value_rows = jnp.concatenate([prefix[:, head_width:], fresh_rows[:, head_width:]], 0)
    block_len = min(token_count, 64)
    pieces = []
    for first_row in range(0, token_count, block_len):
        block_rows = query_rows[first_row : first_row + block_len].reshape(
            block_len * group_size, head_width
        )
        scores = jnp.dot(
            block_rows, key_rows.T, preferred_element_type=jnp.float32
        ) * head_width ** (-0.5)
        position = first_row + jnp.arange(block_len * group_size) // group_size
        column = jnp.arange(prefix_len + token_count) - prefix_len
        allowed = column[None, :] <= position[:, None]
        scores = jnp.where(allowed, scores, -jnp.inf)
        row_max = jnp.max(scores, axis=1, keepdims=True)
        weights = jnp.exp(scores - row_max)
        row_total = jnp.sum(weights, axis=1, keepdims=True)
        probs_bf = (weights / row_total).astype(jnp.bfloat16)
        mixed_rows = jnp.dot(probs_bf, value_rows, preferred_element_type=jnp.float32)
        is_live = position < length
        mixed_rows = jnp.where(is_live[:, None], mixed_rows, 0.0)
        pieces.append(mixed_rows.astype(jnp.bfloat16).reshape(block_len, group_size * head_width))
    return jnp.concatenate(pieces, 0)


def shards(tokens, key_weight, value_weight, queries, prefix_pool, block_table, lengths):
    token_count = tokens.shape[0]
    local_heads = queries.shape[1]
    head_width = prefix_pool.shape[4] // 2
    ctx_count = lax.axis_size("ctx")
    head_count = lax.axis_size("head")
    features = lax.all_gather(tokens, ("ctx", "head"), axis=1, tiled=True)
    key_cols, value_cols = (
        lax.all_to_all(
            lax.all_to_all(key_weight, "ctx", split_axis=3, concat_axis=0, tiled=True),
            "head",
            split_axis=4,
            concat_axis=1,
            tiled=True,
        ),
        lax.all_to_all(
            lax.all_to_all(value_weight, "ctx", split_axis=3, concat_axis=0, tiled=True),
            "head",
            split_axis=4,
            concat_axis=1,
            tiled=True,
        ),
    )
    span_len = features.shape[1] // (ctx_count * head_count)
    feature_view = features.reshape(token_count, ctx_count, head_count, span_len)
    pieces = (
        lax.all_gather(key_cols, "batch", axis=2, tiled=True),
        lax.all_gather(value_cols, "batch", axis=2, tiled=True),
    )
    row_count = pieces[0].shape[2]

    def one_term(weight_piece):
        shaped = weight_piece.reshape(ctx_count, head_count, row_count, local_heads * head_width)
        return jnp.einsum("tchr,chrk->tk", feature_view, shaped, preferred_element_type=jnp.float32)

    key_sum = one_term(pieces[0])
    value_sum = one_term(pieces[1])
    new_keys = key_sum.astype(jnp.bfloat16).reshape(token_count, local_heads, head_width)
    new_values = value_sum.astype(jnp.bfloat16).reshape(token_count, local_heads, head_width)
    fresh_all = jnp.concatenate([new_keys, new_values], 2)
    pool_heads = lax.all_to_all(prefix_pool, "ctx", split_axis=2, concat_axis=0, tiled=True)
    chosen = jnp.take(pool_heads, block_table[0], axis=0)
    chosen = chosen.reshape(-1, local_heads, 2 * head_width)
    outputs = [
        attend_head(
            queries[:, head_idx, 0], chosen[:, head_idx], fresh_all[:, head_idx], lengths[0]
        )
        for head_idx in range(local_heads)
    ]
    return jnp.stack(outputs, 1)[:, :, None, :]


def solution(mesh):
    return jax.shard_map(
        shards,
        mesh=mesh,
        in_specs=(
            P(("groups", "batch"), ("ctx", "head")),
            P("ctx", "head", "batch", None, None, None),
            P("ctx", "head", "batch", None, None, None),
            P(("groups", "batch"), "ctx", "head", None),
            P(("groups", "ctx"), None, None, "head", None),
            P(("groups", "batch"), None),
            P(("groups", "batch")),
        ),
        out_specs=P(("groups", "batch"), "ctx", "head", None),
        check_vma=False,
    )
```

profile of v0, /device:TPU:0, one launch (start us, length us, event | category | flops | bytes accessed | tf_op | source)
XLA Modules:
  0.0 460.3 jit_solution(12912880093840343157)
XLA Ops:
  6.5 3.0 copy.38
  9.6 28.9 %all_to_all.90 = bf16[1,1,1024,4,2,128]{5,4,2,1,0,3:T(2,128)(2,1)S(1)} all-to-all(bf16[1,1,1024,4,2,128]{5,4,2,1,0,3:T(2,128)(2,1)S(1)} %copy.38), channel_id=1, replica_groups=mesh['groups'=2,'batch'=4,'ctx'=2,'head'=2] {'ctx'}, dimensions={3} | all-to-all | bytes 4194304 | tf_op jit(solution)/shard_map/all_to_all | solution.py:47
  38.4 3.8 copy.39
  42.2 8.7 %all_to_all.91 = bf16[2,1,1024,2,2,128]{2,5,3,0,1,4:T(8,128)(2,1)} all-to-all(bf16[2,1,1024,2,2,128]{2,5,3,0,1,4:T(8,128)(2,1)} %bitcast.95), channel_id=1, replica_groups=mesh['groups'=2,'batch'=4,'ctx'=2,'head'=2] {'head'}, dimensions={4} | all-to-all | bytes 4194304 | tf_op jit(solution)/shard_map/all_to_all | solution.py:46
  51.0 2.5 copy.37
  53.5 3.0 copy.42
  56.6 28.0 %all_to_all.92 = bf16[1,1,1024,4,2,128]{5,4,2,1,0,3:T(2,128)(2,1)S(1)} all-to-all(bf16[1,1,1024,4,2,128]{5,4,2,1,0,3:T(2,128)(2,1)S(1)} %copy.42), channel_id=1, replica_groups=mesh['groups'=2,'batch'=4,'ctx'=2,'head'=2] {'ctx'}, dimensions={3} | all-to-all | bytes 4194304 | tf_op jit(solution)/shard_map/all_to_all | solution.py:54
  84.5 3.8 copy.43
  88.3 8.6 %all_to_all.93 = bf16[2,1,1024,2,2,128]{2,5,3,0,1,4:T(8,128)(2,1)} all-to-all(bf16[2,1,1024,2,2,128]{2,5,3,0,1,4:T(8,128)(2,1)} %bitcast.97), channel_id=1, replica_groups=mesh['groups'=2,'batch'=4,'ctx'=2,'head'=2] {'head'}, dimensions={4} | all-to-all | bytes 4194304 | tf_op jit(solution)/shard_map/all_to_all | solution.py:53
  96.9 3.5 copy.33
  100.4 4.8 %all-to-all-start = ((bf16[8,128,4,1,256]{4,1,0,3,2:T(8,128)(2,1)}), bf16[8,128,4,1,256]{4,1,0,3,2:T(8,128)(2,1)}, u32[]{:S(2)}, u32[]{:S(2)}) async-start(bf16[8,128,4,1,256]{4,1,0,3,2:T(8,128)(2,1)} %copy.33), calls=%async_computation | async-start | bytes 4194304 | tf_op jit(solution)/shard_map/all_to_all | solution.py:78
  106.0 12.8 %slice_reduce_fusion.7 = (bf16[64,2048]{1,0:T(8,128)(2,1)}, bf16[64,2048]{1,0:T(8,128)(2,1)S(1)}, bf16[64,2048]{1,0:T(8,128)(2,1)S(1)}, bf16[64,2048]{1,0:T(8,12...) fusion(bf16[256,2,1,2048]{3,1,2,0:T(2,128)(2,1)S(1)} %copy-done), kind=kLoop, calls=%fused_computation.74 | loop fusion | bytes 4194304 | tf_op jit(solution)/shard_map/slice | solution.py:17
  118.8 1.8 reshape.177
  120.5 1.8 reshape.179
  122.3 1.8 reshape.181
  124.1 0.8 reshape.183
  124.9 0.8 reshape.185
  125.7 0.8 reshape.187
  126.6 0.8 reshape.189
  127.7 3.1 all-to-all-done
  130.7 1.7 copy.34
  133.8 67.5 %all-gather.8.cloned.1.call-done = bf16[2,2,1,4096,2,1,128]{3,6,4,0,1,5,2:T(8,128)(2,1)} async-done(((bf16[2,2,1,1024,2,1,128]{3,6,4,0,1,5,2:T(8,128)(2,1)}), bf16[2,2,1,4096,2,1,128]{3,6,4,0,1,5,2:T(8,128)(2,1)}) %all-gather.8.cloned.1.call-update) | async-done | bytes 8388624 | tf_op jit(solution)/shard_map/all_gather | solution.py:64
  201.3 8.5 %copy.40 = bf16[2,2,1,4096,2,1,128]{3,6,4,1,0,5,2:T(8,128)(2,1)} copy(bf16[2,2,1,4096,2,1,128]{3,6,4,0,1,5,2:T(8,128)(2,1)} %all-gather.8.cloned.1.call-done) | data formatting | bytes 16777216 | tf_op jit(solution)/shard_map/all_gather | solution.py:64
  209.8 49.6 %all-gather.6.cloned.1.call-done = bf16[256,16384]{0,1:T(8,128)(2,1)} async-done(((bf16[256,4096]{0,1:T(8,128)(2,1)}), bf16[256,16384]{0,1:T(8,128)(2,1)}) %all-gather.6.cloned.1.call-update) | async-done | bytes 8388624 | tf_op jit(solution)/shard_map/all_gather | solution.py:44
  259.4 8.1 %fusion.32 = bf16[256,256]{0,1:T(8,128)(2,1)S(1)} fusion(bf16[2,2,4096,256]{2,3,1,0:T(8,128)(2,1)} %bitcast.90, bf16[256,2,2,4096]{0,3,2,1:T(8,128)(2,1)} %bitcast.102), kind=kOutput, calls=%fused_computation.60 | convolution fusion | flops 2147549184 | bytes 16908288 | tf_op jit(solution)/shard_map/tchr,chrk->tk/dot_general | solution.py:71
  267.6 143.0 %all-gather.10.cloned.1.call-done = bf16[2,2,1,4096,2,1,128]{3,6,4,0,1,5,2:T(8,128)(2,1)} async-done(((bf16[2,2,1,1024,2,1,128]{3,6,4,0,1,5,2:T(8,128)(2,1)}), bf16[2,2,1,4096,2,1,128]{3,6,4,0,1,5,2:T(8,128)(2,1)}) %all-gather.10.cloned.1.call-update) | async-done | bytes 8388624 | tf_op jit(solution)/shard_map/all_gather | solution.py:65
  410.6 7.7 %copy.44 = bf16[2,2,1,4096,2,1,128]{3,6,4,1,0,5,2:T(8,128)(2,1)} copy(bf16[2,2,1,4096,2,1,128]{3,6,4,0,1,5,2:T(8,128)(2,1)} %all-gather.10.cloned.1.call-done) | data formatting | bytes 16777216 | tf_op jit(solution)/shard_map/all_gather | solution.py:65
  418.3 8.1 %fusion.33 = bf16[256,256]{0,1:T(8,128)(2,1)S(1)} fusion(bf16[2,2,4096,256]{2,3,1,0:T(8,128)(2,1)} %bitcast.91, bf16[256,2,2,4096]{0,3,2,1:T(8,128)(2,1)} %bitcast.103), kind=kOutput, calls=%fused_computation.61 | convolution fusion | flops 2147549184 | bytes 16908288 | tf_op jit(solution)/shard_map/tchr,chrk->tk/dot_general | solution.py:71
  426.7 0.9 fusion.52
  427.6 0.8 fusion
  428.3 1.0 fusion.31
  429.5 0.9 fusion.51
  430.4 1.0 fusion.1
  431.3 1.0 fusion.29
  432.5 0.9 fusion.50
  433.4 0.8 fusion.2
  434.1 1.0 fusion.27
  435.3 0.9 fusion.49
  436.9 1.0 fusion.25
  438.1 0.9 fusion.48
  439.7 1.0 fusion.23
  440.9 0.9 fusion.47
  442.5 1.3 fusion.21
  443.9 0.9 fusion.46
  445.6 1.0 fusion.19
  446.7 0.9 fusion.45
  448.3 1.0 fusion.17
  449.8 3.5 copy.48
  (64 shorter events, 7.1 us)
Async XLA Ops:
  6.5 194.8 %all-gather.8.cloned.1.call-start = ((), (), s32[]{:S(2)}) async-start(), calls=%async_computation.6 | async-start | bytes 10485760 | tf_op jit(solution)/shard_map/all_gather | solution.py:64
  42.2 8.8 %copy-start.1 = (bf16[256,4096]{1,0:T(8,128)(2,1)S(1)}, bf16[256,4096]{1,0:T(8,128)(2,1)}, u32[]{:S(2)}) copy-start(bf16[256,4096]{1,0:T(8,128)(2,1)} %param.7) | copy-start | bytes 6291460
  50.9 208.4 %all-gather.6.cloned.1.call-start = ((), (), s32[]{:S(2)}) async-start(), calls=%async_computation.5 | async-start | bytes 10485760 | tf_op jit(solution)/shard_map/all_gather | solution.py:44
  53.5 357.1 %all-gather.10.cloned.1.call-start = ((), (), s32[]{:S(2)}) async-start(), calls=%async_computation.7 | async-start | bytes 10485760 | tf_op jit(solution)/shard_map/all_gather | solution.py:65
  96.9 9.0 %copy-start = (bf16[256,2,1,2048]{3,1,2,0:T(2,128)(2,1)S(1)}, bf16[256,2,1,2048]{3,1,2,0:T(2,128)(2,1)}, u32[]{:S(2)}) copy-start(bf16[256,2,1,2048]{3,1,2,0:T(2,128)(2,1)} %param.10) | copy-start | bytes 6291460
  100.4 30.3 %all-to-all-start = ((bf16[8,128,4,1,256]{4,1,0,3,2:T(8,128)(2,1)}), bf16[8,128,4,1,256]{4,1,0,3,2:T(8,128)(2,1)}, u32[]{:S(2)}, u32[]{:S(2)}) async-start(bf16[8,128,4,1,256]{4,1,0,3,2:T(8,128)(2,1)} %copy.33), calls=%async_computation | async-start | bytes 4194304 | tf_op jit(solution)/shard_map/all_to_all | solution.py:78
  105.9 21.6 %copy-start.9 = (s32[1,8]{1,0:T(1,128)S(1)}, s32[1,8]{1,0:T(1,128)}, u32[]{:S(2)}) copy-start(s32[1,8]{1,0:T(1,128)} %param.12) | copy-start | bytes 100
  418.3 8.4 %copy-start.8 = (bf16[1024,128]{1,0:T(8,128)(2,1)S(1)}, bf16[1024,128]{1,0:T(8,128)(2,1)}, u32[]{:S(2)}) copy-start(bf16[1024,128]{1,0:T(8,128)(2,1)} %reshape.177) | copy-start | bytes 786436
  428.3 1.1 copy-start.7
  431.3 1.1 copy-start.6
  434.1 1.1 copy-start.5
  436.9 1.1 copy-start.4
  439.7 1.1 copy-start.3
  442.5 1.4 copy-start.2
Sparse Core Ops, SparseCore 0:
  51.1 150.1 all-gather.7
  202.9 56.4 all-gather.5
  260.9 149.6 all-gather.9
where the time goes:
time: 468 us; the launch traced here: 460 us
  waiting for transfers between devices  263 us (56%)
  blocking collectives  74.1 us (16%)
  local copies, waits for them, and re-layouts  64.9 us (14%)
  matrix products  31.5 us (7%)
  between operations  14.7 us (3%)
  other arithmetic  6.98 us (1%)
  starting transfers between devices  4.9 us (1%)
    all_gather x1, waiting for transfers between devices, shards(): lax.all_gather(value_cols, 'batch', axis=2, tiled=True)  143 us
    all_gather x1, waiting for transfers between devices, shards(): lax.all_gather(key_cols, 'batch', axis=2, tiled=True)  67.5 us
    all_gather x1, waiting for transfers between devices, shards(): features = lax.all_gather(tokens, ('ctx', 'head'), axis=1, tiled=True)  49.6 us
    all_to_all x1, blocking collectives, shards(): lax.all_to_all(key_weight, 'ctx', split_axis=3, concat_axis=0, tiled=True)  28.9 us
    all_to_all x1, blocking collectives, shards(): lax.all_to_all(value_weight, 'ctx', split_axis=3, concat_axis=0, tiled=True)  28 us
    dot_general x2, matrix products, one_term(): jnp.einsum('tchr,chrk->tk', feature_view, shaped, preferred_element_type=...  16.2 us
    slice x1, local copies, waits for them, and re-layouts, attend_head(): query_rows[first_row:first_row + block_len]  12.8 us
    unnamed x24, local copies, waits for them, and re-layouts  12 us
  transfers between devices with their start and end apart: 4, of which 4 were waited for; matrix products, arithmetic and copies ran while one was open for 12% of the time, Pallas kernels for 0%

commit v1 on v0

--- a/solution.py
+++ b/solution.py
@@ -1,7 +1,15 @@
+import functools
+import math
+
 import jax
 import jax.numpy as jnp
 from jax import lax
+from jax.experimental import pallas as pl
+from jax.experimental.pallas import tpu as pltpu
 from jax.sharding import PartitionSpec as P
+
+CHUNKS = 2
+VMEM_BYTES = 48 * 1024 * 1024
 
 
 def attend_head(query_rows, prefix, fresh_rows, length):
@@ -35,7 +43,7 @@
     return jnp.concatenate(pieces, 0)
 
 
-def shards(tokens, key_weight, value_weight, queries, prefix_pool, block_table, lengths):
+def gathered_shards(tokens, key_weight, value_weight, queries, prefix_pool, block_table, lengths):
     token_count = tokens.shape[0]
     local_heads = queries.shape[1]
     head_width = prefix_pool.shape[4] // 2
@@ -44,19 +52,13 @@
     features = lax.all_gather(tokens, ("ctx", "head"), axis=1, tiled=True)
     key_cols, value_cols = (
         lax.all_to_all(
-            lax.all_to_all(key_weight, "ctx", split_axis=3, concat_axis=0, tiled=True),
+            lax.all_to_all(weight, "ctx", split_axis=3, concat_axis=0, tiled=True),
             "head",
             split_axis=4,
             concat_axis=1,
             tiled=True,
-        ),
-        lax.all_to_all(
-            lax.all_to_all(value_weight, "ctx", split_axis=3, concat_axis=0, tiled=True),
-            "head",
-            split_axis=4,
-            concat_axis=1,
-            tiled=True,
-        ),
+        )
+        for weight in (key_weight, value_weight)
     )
     span_len = features.shape[1] // (ctx_count * head_count)
     feature_view = features.reshape(token_count, ctx_count, head_count, span_len)
@@ -70,10 +72,8 @@
         shaped = weight_piece.reshape(ctx_count, head_count, row_count, local_heads * head_width)
         return jnp.einsum("tchr,chrk->tk", feature_view, shaped, preferred_element_type=jnp.float32)
 
-    key_sum = one_term(pieces[0])
-    value_sum = one_term(pieces[1])
-    new_keys = key_sum.astype(jnp.bfloat16).reshape(token_count, local_heads, head_width)
-    new_values = value_sum.astype(jnp.bfloat16).reshape(token_count, local_heads, head_width)
+    new_keys = one_term(pieces[0]).astype(jnp.bfloat16).reshape(token_count, local_heads, head_width)
+    new_values = one_term(pieces[1]).astype(jnp.bfloat16).reshape(token_count, local_heads, head_width)
     fresh_all = jnp.concatenate([new_keys, new_values], 2)
     pool_heads = lax.all_to_all(prefix_pool, "ctx", split_axis=2, concat_axis=0, tiled=True)
     chosen = jnp.take(pool_heads, block_table[0], axis=0)
@@ -87,7 +87,268 @@
     return jnp.stack(outputs, 1)[:, :, None, :]
 
 
+def shift(array, axis, step):
+    count = lax.axis_size(axis)
+    return lax.ppermute(array, axis, [(i, (i + step) % count) for i in range(count)])
+
+
+def project_kernel(place_ref, *refs):
+    weight_ref, out_ref = refs[-2], refs[-1]
+    rows = refs[0].shape[0]
+    for index, token_ref in enumerate(refs[:-2]):
+        out_ref[pl.ds(index * rows, rows), :] = jnp.dot(
+            token_ref[...], weight_ref[0, 0], preferred_element_type=jnp.float32
+        ).astype(out_ref.dtype)
+
+
+def project(place, tokens, received, weights, chunk, head_step, out_dtype):
+    head_count, ctx_count, depth, width = weights.shape
+    rows = tokens.shape[0] // CHUNKS
+    row_total = rows * (1 + len(received))
+
+    return pl.pallas_call(
+        project_kernel,
+        grid_spec=pltpu.PrefetchScalarGridSpec(
+            num_scalar_prefetch=1,
+            grid=(ctx_count,),
+            in_specs=[pl.BlockSpec((rows, depth), lambda j, place: (chunk, place[0]))]
+            + [pl.BlockSpec((rows, depth), lambda j, place: (0, 0)) for _ in received]
+            + [
+                pl.BlockSpec(
+                    (1, 1, depth, width),
+                    lambda j, place: (
+                        lax.rem(place[2] + head_step, head_count),
+                        lax.rem(place[1] + j, ctx_count),
+                        0,
+                        0,
+                    ),
+                )
+            ],
+            out_specs=pl.BlockSpec((row_total, width), lambda j, place: (0, j)),
+        ),
+        out_shape=jax.ShapeDtypeStruct((row_total, ctx_count * width), out_dtype),
+        compiler_params=pltpu.CompilerParams(vmem_limit_bytes=VMEM_BYTES),
+        cost_estimate=pl.CostEstimate(
+            flops=2 * row_total * depth * ctx_count * width,
+            bytes_accessed=2 * depth * (ctx_count * width + row_total),
+            transcendentals=0,
+        ),
+        name="project",
+    )(place, tokens, *received, weights)
+
+
+def split_heads(block, heads):
+    if heads == 1:
+        return block
+    head_of = lax.broadcasted_iota(jnp.int32, block.shape, 0) % heads
+    zero = jnp.zeros_like(block)
+    return jnp.concatenate([jnp.where(head_of == i, block, zero) for i in range(heads)], 1)
+
+
+def own_head(block, heads):
+    width = block.shape[1] // heads
+    result = block[:, :width]
+    head_of = lax.broadcasted_iota(jnp.int32, result.shape, 0) % heads
+    for i in range(1, heads):
+        result = jnp.where(head_of == i, block[:, i * width : (i + 1) * width], result)
+    return result
+
+
+def dot_keys(query_block, keys):
+    return lax.dot_general(
+        query_block, keys, (((1,), (1,)), ((), ())), preferred_element_type=jnp.float32
+    )
+
+
+def prefix_kernel(scale, heads, query_ref, key_ref, value_ref, acc_ref, stat_ref):
+    scores = dot_keys(split_heads(query_ref[...], heads), key_ref[...]) * scale
+    row_max = jnp.max(scores, axis=1, keepdims=True)
+    weights = jnp.exp2(scores - row_max)
+    row_total = jnp.sum(weights, axis=1, keepdims=True)
+    mixed = jnp.dot(
+        weights.astype(jnp.bfloat16), value_ref[...], preferred_element_type=jnp.float32
+    )
+    acc_ref[...] = own_head(mixed, heads)
+    lane = lax.broadcasted_iota(jnp.int32, stat_ref.shape, 1)
+    stat_ref[...] = jnp.where(lane < stat_ref.shape[1] // 2, row_max, row_total)
+
+
+def fresh_kernel(
+    scale, heads, per_token, first_row, length_ref, query_ref, acc_ref, stat_ref, fresh_ref, *rest
+):
+    out_ref = rest[-1]
+    rows, width = query_ref.shape
+    wide = heads * width
+    step = pl.program_id(0)
+    keys, values = fresh_ref[:, :wide], fresh_ref[:, wide:]
+    scores = dot_keys(split_heads(query_ref[...], heads), keys) * scale
+    row_at = lax.broadcasted_iota(jnp.int32, scores.shape, 0)
+    position = first_row + step * (rows // per_token) + row_at // per_token
+    column = lax.broadcasted_iota(jnp.int32, scores.shape, 1)
+    scores = jnp.where(column <= position, scores, -jnp.inf)
+    old_max, old_total = stat_ref[:, :1], stat_ref[:, width // 2 : width // 2 + 1]
+    row_max = jnp.maximum(jnp.max(scores, axis=1, keepdims=True), old_max)
+    weights = jnp.exp2(scores - row_max)
+    fade = jnp.exp2(old_max - row_max)
+    row_total = old_total * fade + jnp.sum(weights, axis=1, keepdims=True)
+    mixed = own_head(
+        jnp.dot(weights.astype(jnp.bfloat16), values, preferred_element_type=jnp.float32), heads
+    )
+    result = (acc_ref[...] * fade + mixed) / row_total
+    token = first_row + step * (rows // per_token)
+    token = token + lax.broadcasted_iota(jnp.int32, result.shape, 0) // per_token
+    out_ref[...] = jnp.where(token < length_ref[0], result, 0.0).astype(out_ref.dtype)
+
+
+def prefix_attend(query_rows, keys, values, scale, heads):
+    row_total, width = query_rows.shape
+    rows = min(512, row_total)
+    key_count = keys.shape[0]
+    whole = pl.BlockSpec(keys.shape, lambda i: (0, 0))
+    block = pl.BlockSpec((rows, width), lambda i: (i, 0))
+    return pl.pallas_call(
+        functools.partial(prefix_kernel, scale, heads),
+        grid=(row_total // rows,),
+        in_specs=[block, whole, whole],
+        out_specs=[block, block],
+        out_shape=[jax.ShapeDtypeStruct((row_total, width), jnp.float32)] * 2,
+        compiler_params=pltpu.CompilerParams(vmem_limit_bytes=VMEM_BYTES),
+        cost_estimate=pl.CostEstimate(
+            flops=4 * row_total * key_count * keys.shape[1],
+            bytes_accessed=row_total * width * 10,
+            transcendentals=row_total * key_count,
+        ),
+        name="prefix_attend",
+    )(query_rows, keys, values)
+
+
+def fresh_attend(length, query_rows, acc, stat, fresh, earlier, chunk, scale, heads, per_token):
+    row_total, width = query_rows.shape
+    chunk_rows = row_total // CHUNKS
+    rows = min(512, chunk_rows)
+    steps = chunk_rows // rows
+    block = pl.BlockSpec((rows, width), lambda i, length: (chunk * steps + i, 0))
+    in_specs = [block, block, block, pl.BlockSpec(fresh.shape, lambda i, length: (0, 0))]
+    operands = [length, query_rows, acc, stat, fresh]
+    aliases = {}
+    if earlier is not None:
+        in_specs.append(pl.BlockSpec(memory_space=pl.ANY))
+        operands.append(earlier)
+        aliases = {5: 0}
+    return pl.pallas_call(
+        functools.partial(
+            fresh_kernel, scale, heads, per_token, chunk * (chunk_rows // per_token)
+        ),
+        grid_spec=pltpu.PrefetchScalarGridSpec(
+            num_scalar_prefetch=1, grid=(steps,), in_specs=in_specs, out_specs=block
+        ),
+        out_shape=jax.ShapeDtypeStruct((row_total, width), jnp.bfloat16),
+        input_output_aliases=aliases,
+        compiler_params=pltpu.CompilerParams(vmem_limit_bytes=VMEM_BYTES),
+        cost_estimate=pl.CostEstimate(
+            flops=2 * chunk_rows * fresh.shape[0] * fresh.shape[1],
+            bytes_accessed=chunk_rows * width * 12,
+            transcendentals=chunk_rows * fresh.shape[0],
+        ),
+        name="fresh_attend",
+    )(*operands)
+
+
+def reduced_shards(tokens, key_weight, value_weight, queries, prefix_pool, block_table, lengths):
+    batch_count = lax.axis_size("batch")
+    ctx_count = lax.axis_size("ctx")
+    head_count = lax.axis_size("head")
+    batch_at, ctx_at, head_at = (lax.axis_index(a) for a in ("batch", "ctx", "head"))
+    place = jnp.stack([batch_at, ctx_at, head_at]).astype(jnp.int32)
+    token_count = tokens.shape[0]
+    heads = queries.shape[1]
+    width = prefix_pool.shape[4] // 2
+    group = queries.shape[3] // width
+    per_token = heads * group
+    depth = key_weight.shape[2]
+    rows = token_count // CHUNKS
+    scale = math.log2(math.e) / math.sqrt(width)
+
+    received = []
+    for chunk in range(CHUNKS):
+        arrived = []
+        for step in range(1, batch_count):
+            target = lax.rem(batch_at + step, batch_count)
+            piece = lax.dynamic_slice(tokens, (chunk * rows, target * depth), (rows, depth))
+            arrived.append(shift(piece, "batch", step))
+        received.append(arrived)
+
+    pool = prefix_pool[:, :, :, 0, :]
+    blocks, block_len = pool.shape[0], pool.shape[1]
+    parts = []
+    for step in range(ctx_count):
+        target = lax.rem(ctx_at + step, ctx_count)
+        part = lax.dynamic_slice_in_dim(pool, target * heads, heads, 2)
+        parts.append(shift(part, "ctx", step) if step else part)
+    pool_rows = jnp.stack(parts)
+    table = block_table[0]
+    source = lax.rem(ctx_at - table // blocks + ctx_count, ctx_count)
+    pool_rows = pool_rows.reshape(ctx_count * blocks, block_len, heads, 2 * width)
+    chosen = jnp.take(pool_rows, source * blocks + table % blocks, axis=0, mode="clip")
+    chosen = chosen.reshape(-1, heads, 2, width)
+    prefix_keys = chosen[:, :, 0].reshape(-1, heads * width)
+    prefix_values = chosen[:, :, 1].reshape(-1, heads * width)
+
+    def arranged(weight):
+        view = weight.reshape(depth, ctx_count, heads, head_count, width)
+        return view.transpose(3, 1, 0, 2, 4).reshape(head_count, ctx_count, depth, heads * width)
+
+    weights = jnp.concatenate([arranged(key_weight), arranged(value_weight)], 3)
+
+    query_rows = queries.reshape(token_count, heads, group, width)
+    query_rows = query_rows.transpose(0, 2, 1, 3).reshape(-1, width)
+    acc, stat = prefix_attend(query_rows, prefix_keys, prefix_values, scale, heads)
+
+    fresh_parts = []
+    result = None
+    cols = weights.shape[3]
+    for chunk in range(CHUNKS):
+        sent = [
+            project(place, tokens, received[chunk], weights, chunk, step, jnp.bfloat16)
+            for step in range(1, head_count)
+        ]
+        sent = [shift(part, "head", step + 1) for step, part in enumerate(sent)]
+        total = project(place, tokens, received[chunk], weights, chunk, 0, jnp.float32)
+        for part in sent:
+            total = total + part.astype(jnp.float32)
+        mine = total[:, :cols]
+        for step in range(1, ctx_count):
+            part = total[:, step * cols : (step + 1) * cols].astype(jnp.bfloat16)
+            mine = mine + shift(part, "ctx", step).astype(jnp.float32)
+        fresh = mine[:rows]
+        for step in range(1, batch_count):
+            part = mine[step * rows : (step + 1) * rows].astype(jnp.bfloat16)
+            fresh = fresh + shift(part, "batch", -step).astype(jnp.float32)
+        fresh_parts.append(fresh.astype(jnp.bfloat16))
+        result = fresh_attend(
+            lengths,
+            query_rows,
+            acc,
+            stat,
+            jnp.concatenate(fresh_parts, 0),
+            result,
+            chunk,
+            scale,
+            heads,
+            per_token,
+        )
+    result = result.reshape(token_count, group, heads, width).transpose(0, 2, 1, 3)
+    return result.reshape(token_count, heads, 1, group * width)
+
+
 def solution(mesh):
+    def shards(tokens, key_weight, value_weight, *rest):
+        prompts = mesh.shape["batch"]
+        columns = 2 * math.prod(key_weight.shape[3:])
+        few_tokens = prompts * tokens.shape[0] <= columns
+        form = reduced_shards if few_tokens else gathered_shards
+        return form(tokens, key_weight, value_weight, *rest)
+
     return jax.shard_map(
         shards,
         mesh=mesh,

time: 468 us -> 170 us (0.36); the launches traced: 460 us -> 169 us
  waiting for transfers between devices: 263 us -> 30.1 us
  blocking collectives: 74.1 us -> 0 us
  Pallas kernels: 0 us -> 73 us
  local copies, waits for them, and re-layouts: 64.9 us -> 32.5 us
  matrix products: 31.5 us -> 0 us
  starting transfers between devices: 4.9 us -> 24.3 us
  between operations: 14.7 us -> 1.04 us
    all_gather x3 -> x0, waiting for transfers between devices: 260 us -> none  [the longest x1 143 us: shards(): lax.all_gather(value_cols, 'batch', axis=2, tiled=True)]
    all_to_all x4 -> x0, blocking collectives: 74.1 us -> none  [the longest x1 28.9 us: shards(): lax.all_to_all(key_weight, 'ctx', split_axis=3, concat_axis=0, tiled=True)]
    pallas_call x0 -> x7, Pallas kernels: none -> 73 us  [the longest x2 32.1 us: fresh_attend(): pl.pallas_call(functools.partial(fresh_kernel, scale, heads, per_token, c...]
    dot_general x18 -> x0, matrix products: 31.5 us -> none  [the longest x2 16.2 us: one_term(): jnp.einsum('tchr,chrk->tk', feature_view, shaped, preferred_element_type=...]
    ppermute x0 -> x17, waiting for transfers between devices: none -> 30.1 us  [shift(): lax.ppermute(array, axis, [(i, (i + step) % count) for i in range(count)])]
    ppermute x0 -> x17, starting transfers between devices: none -> 24.3 us  [shift(): lax.ppermute(array, axis, [(i, (i + step) % count) for i in range(count)])]
    all_gather x2 -> x0, local copies, waits for them, and re-layouts: 16.2 us -> none  [the longest x1 8.5 us: shards(): lax.all_gather(key_cols, 'batch', axis=2, tiled=True)]
    slice x3 -> x5, local copies, waits for them, and re-layouts: 13 us -> 1.24 us  [the longest x1 1.04 us: reduced_shards(): prefix_values = chosen[:, :, 1].reshape(-1, heads * width)]
  transfers between devices with their start and end apart: 4 -> 17, of which waited for: 4 -> 6; matrix products, arithmetic and copies ran while one was open for 12% -> 22% of each run, Pallas kernels for 0% -> 24%
where the time goes in v1:
time: 170 us; the launch traced here: 169 us
  Pallas kernels  73 us (43%)
  local copies, waits for them, and re-layouts  32.5 us (19%)
  waiting for transfers between devices  30.1 us (18%)
  starting transfers between devices  24.3 us (14%)
  other arithmetic  8.11 us (5%)
    pallas_call x2, Pallas kernels, fresh_attend(): pl.pallas_call(functools.partial(fresh_kernel, scale, heads, per_token, c...  32.1 us
    ppermute x17, waiting for transfers between devices, shift(): lax.ppermute(array, axis, [(i, (i + step) % count) for i in range(count)])  30.1 us
    pallas_call x1, Pallas kernels, prefix_attend(): pl.pallas_call(functools.partial(prefix_kernel, scale, heads), grid=(row_...  25.7 us
    ppermute x17, starting transfers between devices, shift(): lax.ppermute(array, axis, [(i, (i + step) % count) for i in range(count)])  24.3 us
    pallas_call x4, Pallas kernels, project(): pl.pallas_call(project_kernel, grid_spec=pltpu.PrefetchScalarGridSpec(num...  15.2 us
    reshape x2, local copies, waits for them, and re-layouts, arranged(): view.transpose(3, 1, 0, 2, 4)  6.3 us
    unnamed x21, local copies, waits for them, and re-layouts  5.12 us
    reshape x2, local copies, waits for them, and re-layouts, arranged(): view = weight.reshape(depth, ctx_count, heads, head_count, width)  4.8 us
  transfers between devices with their start and end apart: 17, of which 6 were waited for; matrix products, arithmetic and copies ran while one was open for 22% of the time, Pallas kernels for 24%

profile of v1, /device:TPU:0, one launch (start us, length us, event | category | flops | bytes accessed | tf_op | source)
XLA Modules:
  0.0 169.0 jit_solution(4937667381713522732)
XLA Ops:
  0.0 2.6 %constant_dynamic-slice_fusion = (bf16[128,1024]{1,0:T(8,128)(2,1)}, bf16[128,1024]{1,0:T(8,128)(2,1)}, bf16[128,1024]{1,0:T(8,128)(2,1)}, bf16[128,1024]{1,0:T(...) fusion(bf16[256,4096]{1,0:T(8,128)(2,1)} %refs_0_.7, s32[]{:T(128)S(6)} %select_n.50, ...), kind=kLoop, calls=%fused_computation.28 | loop fusion | bytes 3145740 | tf_op jit(solution)/shard_map/dynamic_slice | solution.py:277
  2.6 5.0 %collective-permute-start.3 = (bf16[128,1024]{1,0:T(8,128)(2,1)}, bf16[128,1024]{1,0:T(8,128)(2,1)S(1)}, u32[]{:S(2)}, u32[]{:S(2)}) collective-permute-start(bf16[128,1024]{1,0:T(8,128)(2,1)} %get-tuple-element.13), channel_id=1, source_target_pairs={{0,12},{4,0},{8,4},{12,8},{1,13},{5,1},{9,5},{13,9},{2,14},{6,2},{... | collective-permute-start | bytes 786440 | tf_op jit(solution)/shard_map/ppermute | solution.py:92
  7.7 0.4 collective-permute-start.11
  8.1 1.6 collective-permute-start.9
  9.7 3.2 %constant_dynamic-slice_fusion.4 = (bf16[8,128,2,1,256]{4,2,3,1,0:T(2,128)(2,1)}, bf16[8,128,2,1,256]{4,2,3,1,0:T(2,128)(2,1)S(1)}) fusion(bf16[8,128,4,1,256]{4,2,3,1,0:T(4,128)(2,1)S(1)} %copy-done.4, s32[]{:T(128)S(6)} %select_n.44, s32[]{:T(128)S(6)} %select_n.45), kind=kLoop, calls=%fused_computation.32 | loop fusion | bytes 4194312 | tf_op jit(solution)/shard_map/dynamic_slice | solution.py:286
  13.0 1.2 copy.45
  14.1 1.5 collective-permute-start
  15.6 2.4 %copy.44 = bf16[1024,2,2,2,128]{4,2,0,1,3:T(2,128)(2,1)} copy(bf16[1024,2,2,2,128]{4,3,2,1,0:T(2,128)(2,1)S(1)} %bitcast.59) | data formatting | bytes 4194304 | tf_op jit(solution)/shard_map/reshape | solution.py:298
  18.0 3.2 %reshape.163 = bf16[2,2,1024,256]{3,2,1,0:T(8,128)(2,1)S(1)} reshape(bf16[2,2,1024,2,128]{4,3,2,1,0:T(2,128)(2,1)} %bitcast.55) | data formatting | bytes 4194304 | tf_op jit(solution)/shard_map/reshape | solution.py:299
  21.2 1.5 constant_dynamic-update-slice_fusion.1
  23.5 2.4 %copy.46 = bf16[8,128,2,1,256]{4,1,3,2,0:T(8,128)(2,1)} copy(bf16[8,128,2,1,256]{4,2,3,1,0:T(2,128)(2,1)} %get-tuple-element.19) | data formatting | bytes 2097152
  25.9 2.4 %copy.43 = bf16[1024,2,2,2,128]{4,2,0,1,3:T(2,128)(2,1)} copy(bf16[1024,2,2,2,128]{4,3,2,1,0:T(2,128)(2,1)S(1)} %bitcast.60) | data formatting | bytes 4194304 | tf_op jit(solution)/shard_map/reshape | solution.py:298
  28.3 3.2 %reshape.165 = bf16[2,2,1024,256]{3,2,1,0:T(8,128)(2,1)S(1)} reshape(bf16[2,2,1024,2,128]{4,3,2,1,0:T(2,128)(2,1)} %bitcast.56) | data formatting | bytes 4194304 | tf_op jit(solution)/shard_map/reshape | solution.py:299
  31.4 0.1 pad_add_fusion.place_ref
  31.5 1.5 constant_dynamic-update-slice_fusion.refs_4_
  33.1 2.9 %collective-permute-start.2 = (bf16[128,1024]{1,0:T(8,128)(2,1)S(1)}, bf16[128,1024]{1,0:T(8,128)(2,1)S(1)}, u32[]{:S(2)}, u32[]{:S(2)}) collective-permute-start(bf16[128,1024]{1,0:T(8,128)(2,1)S(1)} %copy-done.7), channel_id=1, source_target_pairs={{0,8},{4,12},{8,0},{12,4},{1,9},{5,13},{9,1},{13,5},{2,10},{6,14},... | collective-permute-start | bytes 786440 | tf_op jit(solution)/shard_map/ppermute | solution.py:92
  36.0 0.3 collective-permute-done.10.refs_2_
  36.3 4.2 %project.7 = bf16[512,1024]{1,0:T(8,128)(2,1)} custom-call(s32[3]{0:T(128)S(1)} %pad_add_fusion.place_ref, bf16[256,4096]{1,0:T(8,128)(2,1)S(1)} %copy-done, bf16[128,1024]{1,0:T(8,128)(2,1)S(1)} %collective-permute-done.9.refs_1_, bf16[128,1024]{1,0:T(8,128)(2,1)S(1)} %collective-permute-done.10.refs_2_, ...), custom_call_target="tpu_custom_call" | custom-call | flops 1073741824 | bytes 3145728 | tf_op jit(solution)/shard_map/project/pallas_call | solution.py:109
  40.5 12.1 %collective-permute-done.2.refs_2_ = bf16[128,1024]{1,0:T(8,128)(2,1)S(1)} collective-permute-done((bf16[128,1024]{1,0:T(8,128)(2,1)S(1)}, bf16[128,1024]{1,0:T(8,128)(2,1)S(1)}, u32[]{:S(2)}, u32[]{:S(2)}) %collective-permute-start.2) | collective-permute-done | bytes 262176 | tf_op jit(solution)/shard_map/ppermute | solution.py:92
  52.7 4.1 %project.5 = bf16[512,1024]{1,0:T(8,128)(2,1)} custom-call(s32[3]{0:T(128)S(1)} %pad_add_fusion.place_ref, bf16[256,4096]{1,0:T(8,128)(2,1)S(1)} %copy-done, bf16[128,1024]{1,0:T(8,128)(2,1)S(1)} %collective-permute-done.1.refs_1_, bf16[128,1024]{1,0:T(8,128)(2,1)S(1)} %collective-permute-done.2.refs_2_, ...), custom_call_target="tpu_custom_call" | custom-call | flops 1073741824 | bytes 3145728 | tf_op jit(solution)/shard_map/project/pallas_call | solution.py:109
  56.8 3.5 %project.4 = f32[512,1024]{1,0:T(8,128)S(1)} custom-call(s32[3]{0:T(128)S(1)} %pad_add_fusion.place_ref, bf16[256,4096]{1,0:T(8,128)(2,1)S(1)} %copy-done, bf16[128,1024]{1,0:T(8,128)(2,1)S(1)} %collective-permute-done.1.refs_1_, bf16[128,1024]{1,0:T(8,128)(2,1)S(1)} %collective-permute-done.2.refs_2_, bf16[128,1024]{1,0:T(8,128)(2,1)S(1)} %collective-permute-done.3.refs_3_, ...), custom_call_target="tpu_custom_call" | custom-call | flops 1073741824 | bytes 3145728 | tf_op jit(solution)/shard_map/project/pallas_call | solution.py:109
  60.3 3.4 %project.6 = f32[512,1024]{1,0:T(8,128)S(1)} custom-call(s32[3]{0:T(128)S(1)} %pad_add_fusion.place_ref, bf16[256,4096]{1,0:T(8,128)(2,1)S(1)} %copy-done, bf16[128,1024]{1,0:T(8,128)(2,1)S(1)} %collective-permute-done.9.refs_1_, bf16[128,1024]{1,0:T(8,128)(2,1)S(1)} %collective-permute-done.10.refs_2_, ...), custom_call_target="tpu_custom_call" | custom-call | flops 1073741824 | bytes 3145728 | tf_op jit(solution)/shard_map/project/pallas_call | solution.py:109
  63.7 3.5 %pad_maximum_fusion = bf16[2,8,128,2,256]{4,2,3,1,0:T(8,128)(2,1)} fusion(bf16[1,8,128,2,256]{4,2,3,1,0:T(8,128)(2,1)} %bitcast.7, bf16[1,8,128,2,256]{4,2,3,1,0:T(8,128)(2,1)S(1)} %bitcast.58), kind=kLoop, calls=%fused_computation.1 | loop fusion | flops 1048576 | bytes 4194304 | tf_op jit(solution)/shard_map/stack | solution.py:288
  67.2 2.2 %gather_fusion = bf16[8,128,2,256]{3,1,2,0:T(8,128)(2,1)S(1)} fusion(bf16[16,128,2,256]{3,1,2,0:T(8,128)(2,1)} %bitcast.57, s32[1024]{0:T(1024)S(1)} %pad_clamp_fusion), kind=kCustom, calls=%fused_computation | custom fusion | bytes 2097184 | tf_op jit(solution)/shard_map/jit(_take)/gather | solution.py:292
  69.4 1.5 copy.29
  70.9 1.5 reshape.161
  72.4 1.0 fusion.12
  73.5 1.2 copy.36.value_ref
  74.7 1.2 copy.35.key_ref
  76.0 2.4 %convert_add_fusion = f32[512,1024]{1,0:T(8,128)S(1)} fusion(f32[512,1024]{1,0:T(8,128)} %copy-done.2, bf16[512,1024]{1,0:T(8,128)(2,1)} %collective-permute-done.12), kind=kLoop, calls=%fused_computation.4 | loop fusion | flops 1048576 | bytes 5242880 | tf_op jit(solution)/shard_map/add | solution.py:318
  78.5 2.2 %collective-permute-start.13 = (bf16[512,512]{1,0:T(8,128)(2,1)S(1)}, bf16[512,512]{1,0:T(8,128)(2,1)S(1)}, u32[]{:S(2)}, u32[]{:S(2)}) collective-permute-start(bf16[512,512]{1,0:T(8,128)(2,1)S(1)} %slice.98), channel_id=1, source_target_pairs={{0,2},{2,0},{1,3},{3,1},{4,6},{6,4},{5,7},{7,5},{8,10},{10,8},{9,1... | collective-permute-start | bytes 1572872 | tf_op jit(solution)/shard_map/ppermute | solution.py:92
  80.7 25.7 %prefix_attend.1 = (f32[8192,128]{1,0:T(8,128)}, f32[8192,128]{1,0:T(8,128)}) custom-call(bf16[8192,128]{1,0:T(8,128)(2,1)S(1)} %bitcast.52, bf16[1024,256]{1,0:T(8,128)(2,1)S(1)} %copy.35.key_ref, bf16[1024,256]{1,0:T(8,128)(2,1)S(1)} %copy.36.value_ref), custom_call_target="tpu_custom_call" | custom-call | flops 8589934592 | bytes 10485760 | tf_op jit(solution)/shard_map/prefix_attend/pallas_call | solution.py:209
  106.4 1.5 convert_add_fusion.1
  108.0 0.1 collective-permute-start.5
  108.1 0.2 fusion.11
  108.4 1.0 collective-permute-start.14
  109.4 1.1 collective-permute-start.16
  110.5 3.4 %collective-permute-start.15 = (bf16[128,512]{1,0:T(8,128)(2,1)S(1)}, bf16[128,512]{1,0:T(8,128)(2,1)S(1)}, u32[]{:S(2)}, u32[]{:S(2)}) collective-permute-start(bf16[128,512]{1,0:T(8,128)(2,1)S(1)} %get-tuple-element.28), channel_id=1, source_target_pairs={{0,8},{4,12},{8,0},{12,4},{1,9},{5,13},{9,1},{13,5},{2,10},{6,14},... | collective-permute-start | bytes 393224 | tf_op jit(solution)/shard_map/ppermute | solution.py:92
  113.9 8.3 %collective-permute-done.5 = bf16[512,512]{1,0:T(8,128)(2,1)S(1)} collective-permute-done((bf16[512,512]{1,0:T(8,128)(2,1)S(1)}, bf16[512,512]{1,0:T(8,128)(2,1)S(1)}, u32[]{:S(2)}, u32[]{:S(2)}) %collective-permute-start.5) | collective-permute-done | bytes 524320 | tf_op jit(solution)/shard_map/ppermute | solution.py:92
  122.1 0.2 fusion.10
  122.4 1.0 collective-permute-start.6
  123.4 1.0 collective-permute-start.8
  124.5 2.9 %collective-permute-start.7 = (bf16[128,512]{1,0:T(8,128)(2,1)S(1)}, bf16[128,512]{1,0:T(8,128)(2,1)S(1)}, u32[]{:S(2)}, u32[]{:S(2)}) collective-permute-start(bf16[128,512]{1,0:T(8,128)(2,1)S(1)} %get-tuple-element.25), channel_id=1, source_target_pairs={{0,8},{4,12},{8,0},{12,4},{1,9},{5,13},{9,1},{13,5},{2,10},{6,14},... | collective-permute-start | bytes 393224 | tf_op jit(solution)/shard_map/ppermute | solution.py:92
  127.5 0.3 collective-permute-done.6
  127.8 6.1 %collective-permute-done.8 = bf16[128,512]{1,0:T(8,128)(2,1)S(1)} collective-permute-done((bf16[128,512]{1,0:T(8,128)(2,1)S(1)}, bf16[128,512]{1,0:T(8,128)(2,1)S(1)}, u32[]{:S(2)}, u32[]{:S(2)}) %collective-permute-start.8) | collective-permute-done | bytes 131104 | tf_op jit(solution)/shard_map/ppermute | solution.py:92
  133.8 3.0 %collective-permute-done.7 = bf16[128,512]{1,0:T(8,128)(2,1)S(1)} collective-permute-done((bf16[128,512]{1,0:T(8,128)(2,1)S(1)}, bf16[128,512]{1,0:T(8,128)(2,1)S(1)}, u32[]{:S(2)}, u32[]{:S(2)}) %collective-permute-start.7) | collective-permute-done | bytes 131104 | tf_op jit(solution)/shard_map/ppermute | solution.py:92
  136.9 15.9 %fresh_attend.2.rest_0_ = bf16[8192,128]{1,0:T(8,128)(2,1)} custom-call(s32[1]{0:T(128)S(6)} %copy.49.length_ref, bf16[8192,128]{1,0:T(8,128)(2,1)S(1)} %bitcast.53, f32[8192,128]{1,0:T(8,128)} %get-tuple-element.7.acc_ref, f32[8192,128]{1,0:T(8,128)} %get-tuple-element.8.stat_ref, bf16[128,512]{1,0:T(8,128)(2,1)S(1)} %fusion.5.fresh_ref), custom_call_target="tpu_custom_call" | custom-call | flops 536870912 | bytes 6291456 | tf_op jit(solution)/shard_map/fresh_attend/pallas_call | solution.py:238
  152.9 16.2 %fresh_attend.3 = bf16[8192,128]{1,0:T(8,128)(2,1)} custom-call(s32[1]{0:T(128)S(6)} %copy.49.length_ref, bf16[8192,128]{1,0:T(8,128)(2,1)S(1)} %bitcast.54, f32[8192,128]{1,0:T(8,128)} %get-tuple-element.7.acc_ref, f32[8192,128]{1,0:T(8,128)} %get-tuple-element.8.stat_ref, ...), custom_call_target="tpu_custom_call", output_to_operand_aliasing={{}: (5, {})} | custom-call | flops 1073741824 | bytes 6291456 | tf_op jit(solution)/shard_map/fresh_attend/pallas_call | solution.py:238
  (42 shorter events, 0.4 us)
Async XLA Ops:
  0.0 9.7 %copy-start.4 = (bf16[8,128,4,1,256]{4,2,3,1,0:T(4,128)(2,1)S(1)}, bf16[8,128,4,1,256]{4,2,3,1,0:T(4,128)(2,1)}, u32[]{:S(2)}) copy-start(bf16[8,128,4,1,256]{4,2,3,1,0:T(4,128)(2,1)} %param.11) | copy-start | bytes 6291460
  2.6 37.9 %collective-permute-start.3 = (bf16[128,1024]{1,0:T(8,128)(2,1)}, bf16[128,1024]{1,0:T(8,128)(2,1)S(1)}, u32[]{:S(2)}, u32[]{:S(2)}) collective-permute-start(bf16[128,1024]{1,0:T(8,128)(2,1)} %get-tuple-element.13), channel_id=1, source_target_pairs={{0,12},{4,0},{8,4},{12,8},{1,13},{5,1},{9,5},{13,9},{2,14},{6,2},{... | collective-permute-start | bytes 786440 | tf_op jit(solution)/shard_map/ppermute | solution.py:92
  7.7 25.4 %collective-permute-start.11 = (bf16[128,1024]{1,0:T(8,128)(2,1)}, bf16[128,1024]{1,0:T(8,128)(2,1)S(1)}, u32[]{:S(2)}, u32[]{:S(2)}) collective-permute-start(bf16[128,1024]{1,0:T(8,128)(2,1)} %get-tuple-element.14), channel_id=1, source_target_pairs={{0,12},{4,0},{8,4},{12,8},{1,13},{5,1},{9,5},{13,9},{2,14},{6,2},{... | collective-permute-start | bytes 786440 | tf_op jit(solution)/shard_map/ppermute | solution.py:92
  8.1 28.2 %collective-permute-start.10 = (bf16[128,1024]{1,0:T(8,128)(2,1)}, bf16[128,1024]{1,0:T(8,128)(2,1)S(1)}, u32[]{:S(2)}, u32[]{:S(2)}) collective-permute-start(bf16[128,1024]{1,0:T(8,128)(2,1)} %get-tuple-element.15), channel_id=1, source_target_pairs={{0,8},{4,12},{8,0},{12,4},{1,9},{5,13},{9,1},{13,5},{2,10},{6,14},... | collective-permute-start | bytes 786440 | tf_op jit(solution)/shard_map/ppermute | solution.py:92
  8.1 28.2 %collective-permute-start.9 = (bf16[128,1024]{1,0:T(8,128)(2,1)}, bf16[128,1024]{1,0:T(8,128)(2,1)S(1)}, u32[]{:S(2)}, u32[]{:S(2)}) collective-permute-start(bf16[128,1024]{1,0:T(8,128)(2,1)} %get-tuple-element.16), channel_id=1, source_target_pairs={{0,4},{4,8},{8,12},{12,0},{1,5},{5,9},{9,13},{13,1},{2,6},{6,10},{... | collective-permute-start | bytes 786440 | tf_op jit(solution)/shard_map/ppermute | solution.py:92
  13.0 2.7 %copy-start.5 = (bf16[1,1,1024,4,2,128]{5,4,3,2,1,0:T(2,128)(2,1)S(1)}, bf16[1,1,1024,4,2,128]{5,4,3,2,1,0:T(2,128)(2,1)}, u32[]{:S(2)}) copy-start(bf16[1,1,1024,4,2,128]{5,4,3,2,1,0:T(2,128)(2,1)} %param.8) | copy-start | bytes 6291460
  14.1 49.6 %collective-permute-start = (bf16[8,128,2,256]{3,1,2,0:T(8,128)(2,1)}, bf16[8,128,2,256]{3,1,2,0:T(8,128)(2,1)}, u32[]{:S(2)}, u32[]{:S(2)}) collective-permute-start(bf16[8,128,2,256]{3,1,2,0:T(8,128)(2,1)} %bitcast.50), channel_id=1, source_target_pairs={{0,2},{2,0},{1,3},{3,1},{4,6},{6,4},{5,7},{7,5},{8,10},{10,8},{9,1... | collective-permute-start | bytes 3145736 | tf_op jit(solution)/shard_map/ppermute | solution.py:92
  22.7 3.2 %copy-start.6 = (bf16[1,1,1024,4,2,128]{5,4,3,2,1,0:T(2,128)(2,1)S(1)}, bf16[1,1,1024,4,2,128]{5,4,3,2,1,0:T(2,128)(2,1)}, u32[]{:S(2)}) copy-start(bf16[1,1,1024,4,2,128]{5,4,3,2,1,0:T(2,128)(2,1)} %param.9) | copy-start | bytes 6291460
  31.5 1.5 copy-start.7
  31.5 4.8 %copy-start = (bf16[256,4096]{1,0:T(8,128)(2,1)S(1)}, bf16[256,4096]{1,0:T(8,128)(2,1)}, u32[]{:S(2)}) copy-start(bf16[256,4096]{1,0:T(8,128)(2,1)} %refs_0_.7) | copy-start | bytes 6291460
  33.1 19.6 %collective-permute-start.2 = (bf16[128,1024]{1,0:T(8,128)(2,1)S(1)}, bf16[128,1024]{1,0:T(8,128)(2,1)S(1)}, u32[]{:S(2)}, u32[]{:S(2)}) collective-permute-start(bf16[128,1024]{1,0:T(8,128)(2,1)S(1)} %copy-done.7), channel_id=1, source_target_pairs={{0,8},{4,12},{8,0},{12,4},{1,9},{5,13},{9,1},{13,5},{2,10},{6,14},... | collective-permute-start | bytes 786440 | tf_op jit(solution)/shard_map/ppermute | solution.py:92
  36.3 4.2 %copy-start.8 = (s32[1,8]{1,0:T(1,128)S(1)}, s32[1,8]{1,0:T(1,128)}, u32[]{:S(2)}) copy-start(s32[1,8]{1,0:T(1,128)} %param.12) | copy-start | bytes 100
  36.3 16.4 %collective-permute-start.1 = (bf16[128,1024]{1,0:T(8,128)(2,1)S(1)}, bf16[128,1024]{1,0:T(8,128)(2,1)S(1)}, u32[]{:S(2)}, u32[]{:S(2)}) collective-permute-start(bf16[128,1024]{1,0:T(8,128)(2,1)S(1)} %get-tuple-element.18), channel_id=1, source_target_pairs={{0,4},{4,8},{8,12},{12,0},{1,5},{5,9},{9,13},{13,1},{2,6},{6,10},{... | collective-permute-start | bytes 786440 | tf_op jit(solution)/shard_map/ppermute | solution.py:92
  40.5 35.5 %collective-permute-start.12 = (bf16[512,1024]{1,0:T(8,128)(2,1)}, bf16[512,1024]{1,0:T(8,128)(2,1)}, u32[]{:S(2)}, u32[]{:S(2)}) collective-permute-start(bf16[512,1024]{1,0:T(8,128)(2,1)} %project.7), channel_id=1, source_target_pairs={{0,1},{1,0},{2,3},{3,2},{4,5},{5,4},{6,7},{7,6},{8,9},{9,8},{10,11... | collective-permute-start | bytes 3145736 | tf_op jit(solution)/shard_map/ppermute | solution.py:92
  56.8 49.6 %collective-permute-start.4 = (bf16[512,1024]{1,0:T(8,128)(2,1)}, bf16[512,1024]{1,0:T(8,128)(2,1)}, u32[]{:S(2)}, u32[]{:S(2)}) collective-permute-start(bf16[512,1024]{1,0:T(8,128)(2,1)} %project.5), channel_id=1, source_target_pairs={{0,1},{1,0},{2,3},{3,2},{4,5},{5,4},{6,7},{7,6},{8,9},{9,8},{10,11... | collective-permute-start | bytes 3145736 | tf_op jit(solution)/shard_map/ppermute | solution.py:92
  60.3 3.5 %copy-start.3 = (bf16[8,128,2,1,256]{4,1,3,2,0:T(8,128)(2,1)S(1)}, bf16[8,128,2,1,256]{4,1,3,2,0:T(8,128)(2,1)}, u32[]{:S(2)}) copy-start(bf16[8,128,2,1,256]{4,1,3,2,0:T(8,128)(2,1)} %copy.46) | copy-start | bytes 3145732
  63.7 3.5 %copy-start.2 = (f32[512,1024]{1,0:T(8,128)}, f32[512,1024]{1,0:T(8,128)S(1)}, u32[]{:S(2)}) copy-start(f32[512,1024]{1,0:T(8,128)S(1)} %project.6) | copy-start | bytes 6291460
  76.0 4.7 %copy-start.1 = (bf16[256,2,1,2048]{3,1,2,0:T(2,128)(2,1)S(1)}, bf16[256,2,1,2048]{3,1,2,0:T(2,128)(2,1)}, u32[]{:S(2)}) copy-start(bf16[256,2,1,2048]{3,1,2,0:T(2,128)(2,1)} %param.10) | copy-start | bytes 6291460
  78.5 29.6 %collective-permute-start.13 = (bf16[512,512]{1,0:T(8,128)(2,1)S(1)}, bf16[512,512]{1,0:T(8,128)(2,1)S(1)}, u32[]{:S(2)}, u32[]{:S(2)}) collective-permute-start(bf16[512,512]{1,0:T(8,128)(2,1)S(1)} %slice.98), channel_id=1, source_target_pairs={{0,2},{2,0},{1,3},{3,1},{4,6},{6,4},{5,7},{7,5},{8,10},{10,8},{9,1... | collective-permute-start | bytes 1572872 | tf_op jit(solution)/shard_map/ppermute | solution.py:92
  108.0 14.1 %collective-permute-start.5 = (bf16[512,512]{1,0:T(8,128)(2,1)S(1)}, bf16[512,512]{1,0:T(8,128)(2,1)S(1)}, u32[]{:S(2)}, u32[]{:S(2)}) collective-permute-start(bf16[512,512]{1,0:T(8,128)(2,1)S(1)} %slice.99), channel_id=1, source_target_pairs={{0,2},{2,0},{1,3},{3,1},{4,6},{6,4},{5,7},{7,5},{8,10},{10,8},{9,1... | collective-permute-start | bytes 1572872 | tf_op jit(solution)/shard_map/ppermute | solution.py:92
  108.4 16.1 %collective-permute-start.14 = (bf16[128,512]{1,0:T(8,128)(2,1)S(1)}, bf16[128,512]{1,0:T(8,128)(2,1)S(1)}, u32[]{:S(2)}, u32[]{:S(2)}) collective-permute-start(bf16[128,512]{1,0:T(8,128)(2,1)S(1)} %get-tuple-element.26), channel_id=1, source_target_pairs={{0,12},{4,0},{8,4},{12,8},{1,13},{5,1},{9,5},{13,9},{2,14},{6,2},{... | collective-permute-start | bytes 393224 | tf_op jit(solution)/shard_map/ppermute | solution.py:92
  109.4 18.0 %collective-permute-start.16 = (bf16[128,512]{1,0:T(8,128)(2,1)S(1)}, bf16[128,512]{1,0:T(8,128)(2,1)S(1)}, u32[]{:S(2)}, u32[]{:S(2)}) collective-permute-start(bf16[128,512]{1,0:T(8,128)(2,1)S(1)} %get-tuple-element.27), channel_id=1, source_target_pairs={{0,4},{4,8},{8,12},{12,0},{1,5},{5,9},{9,13},{13,1},{2,6},{6,10},{... | collective-permute-start | bytes 393224 | tf_op jit(solution)/shard_map/ppermute | solution.py:92
  110.5 16.9 %collective-permute-start.15 = (bf16[128,512]{1,0:T(8,128)(2,1)S(1)}, bf16[128,512]{1,0:T(8,128)(2,1)S(1)}, u32[]{:S(2)}, u32[]{:S(2)}) collective-permute-start(bf16[128,512]{1,0:T(8,128)(2,1)S(1)} %get-tuple-element.28), channel_id=1, source_target_pairs={{0,8},{4,12},{8,0},{12,4},{1,9},{5,13},{9,1},{13,5},{2,10},{6,14},... | collective-permute-start | bytes 393224 | tf_op jit(solution)/shard_map/ppermute | solution.py:92
  122.4 5.4 %collective-permute-start.6 = (bf16[128,512]{1,0:T(8,128)(2,1)S(1)}, bf16[128,512]{1,0:T(8,128)(2,1)S(1)}, u32[]{:S(2)}, u32[]{:S(2)}) collective-permute-start(bf16[128,512]{1,0:T(8,128)(2,1)S(1)} %get-tuple-element.23), channel_id=1, source_target_pairs={{0,12},{4,0},{8,4},{12,8},{1,13},{5,1},{9,5},{13,9},{2,14},{6,2},{... | collective-permute-start | bytes 393224 | tf_op jit(solution)/shard_map/ppermute | solution.py:92
  123.4 10.4 %collective-permute-start.8 = (bf16[128,512]{1,0:T(8,128)(2,1)S(1)}, bf16[128,512]{1,0:T(8,128)(2,1)S(1)}, u32[]{:S(2)}, u32[]{:S(2)}) collective-permute-start(bf16[128,512]{1,0:T(8,128)(2,1)S(1)} %get-tuple-element.24), channel_id=1, source_target_pairs={{0,4},{4,8},{8,12},{12,0},{1,5},{5,9},{9,13},{13,1},{2,6},{6,10},{... | collective-permute-start | bytes 393224 | tf_op jit(solution)/shard_map/ppermute | solution.py:92
  124.5 12.4 %collective-permute-start.7 = (bf16[128,512]{1,0:T(8,128)(2,1)S(1)}, bf16[128,512]{1,0:T(8,128)(2,1)S(1)}, u32[]{:S(2)}, u32[]{:S(2)}) collective-permute-start(bf16[128,512]{1,0:T(8,128)(2,1)S(1)} %get-tuple-element.25), channel_id=1, source_target_pairs={{0,8},{4,12},{8,0},{12,4},{1,9},{5,13},{9,1},{13,5},{2,10},{6,14},... | collective-permute-start | bytes 393224 | tf_op jit(solution)/shard_map/ppermute | solution.py:92

commit v2 on v1

--- a/solution.py
+++ b/solution.py
@@ -92,63 +92,24 @@
     return lax.ppermute(array, axis, [(i, (i + step) % count) for i in range(count)])
 
 
-def project_kernel(place_ref, *refs):
-    weight_ref, out_ref = refs[-2], refs[-1]
-    rows = refs[0].shape[0]
-    for index, token_ref in enumerate(refs[:-2]):
-        out_ref[pl.ds(index * rows, rows), :] = jnp.dot(
-            token_ref[...], weight_ref[0, 0], preferred_element_type=jnp.float32
-        ).astype(out_ref.dtype)
-
-
-def project(place, tokens, received, weights, chunk, head_step, out_dtype):
-    head_count, ctx_count, depth, width = weights.shape
-    rows = tokens.shape[0] // CHUNKS
-    row_total = rows * (1 + len(received))
-
-    return pl.pallas_call(
-        project_kernel,
-        grid_spec=pltpu.PrefetchScalarGridSpec(
-            num_scalar_prefetch=1,
-            grid=(ctx_count,),
-            in_specs=[pl.BlockSpec((rows, depth), lambda j, place: (chunk, place[0]))]
-            + [pl.BlockSpec((rows, depth), lambda j, place: (0, 0)) for _ in received]
-            + [
-                pl.BlockSpec(
-                    (1, 1, depth, width),
-                    lambda j, place: (
-                        lax.rem(place[2] + head_step, head_count),
-                        lax.rem(place[1] + j, ctx_count),
-                        0,
-                        0,
-                    ),
-                )
-            ],
-            out_specs=pl.BlockSpec((row_total, width), lambda j, place: (0, j)),
-        ),
-        out_shape=jax.ShapeDtypeStruct((row_total, ctx_count * width), out_dtype),
-        compiler_params=pltpu.CompilerParams(vmem_limit_bytes=VMEM_BYTES),
-        cost_estimate=pl.CostEstimate(
-            flops=2 * row_total * depth * ctx_count * width,
-            bytes_accessed=2 * depth * (ctx_count * width + row_total),
-            transcendentals=0,
-        ),
-        name="project",
-    )(place, tokens, *received, weights)
-
-
-def split_heads(block, heads):
-    if heads == 1:
-        return block
-    head_of = lax.broadcasted_iota(jnp.int32, block.shape, 0) % heads
-    zero = jnp.zeros_like(block)
-    return jnp.concatenate([jnp.where(head_of == i, block, zero) for i in range(heads)], 1)
+def unit_index(shape, unit):
+    row = lax.broadcasted_iota(jnp.int32, shape, 0)
+    if unit & (unit - 1):
+        return row // unit, row % unit
+    return row >> (unit.bit_length() - 1), row & (unit - 1)
+
+
+def head_mask(shape, heads):
+    column = lax.broadcasted_iota(jnp.int32, shape, 1)
+    low = unit_index(shape, heads)[1] * (shape[1] // heads)
+    inside = (column >= low) & (column < low + shape[1] // heads)
+    return jnp.where(inside, 1.0, 0.0).astype(jnp.bfloat16)
 
 
 def own_head(block, heads):
     width = block.shape[1] // heads
     result = block[:, :width]
-    head_of = lax.broadcasted_iota(jnp.int32, result.shape, 0) % heads
+    head_of = unit_index(result.shape, heads)[1]
     for i in range(1, heads):
         result = jnp.where(head_of == i, block[:, i * width : (i + 1) * width], result)
     return result
@@ -160,30 +121,237 @@
     )
 
 
-def prefix_kernel(scale, heads, query_ref, key_ref, value_ref, acc_ref, stat_ref):
-    scores = dot_keys(split_heads(query_ref[...], heads), key_ref[...]) * scale
-    row_max = jnp.max(scores, axis=1, keepdims=True)
-    weights = jnp.exp2(scores - row_max)
-    row_total = jnp.sum(weights, axis=1, keepdims=True)
-    mixed = jnp.dot(
-        weights.astype(jnp.bfloat16), value_ref[...], preferred_element_type=jnp.float32
-    )
-    acc_ref[...] = own_head(mixed, heads)
-    lane = lax.broadcasted_iota(jnp.int32, stat_ref.shape, 1)
-    stat_ref[...] = jnp.where(lane < stat_ref.shape[1] // 2, row_max, row_total)
+def params():
+    return pltpu.CompilerParams(vmem_limit_bytes=VMEM_BYTES)
+
+
+def weight_kernel(ctx_count, heads, head_count, key_ref, value_ref, out_ref, flat):
+    depth, slots, width = key_ref.shape
+    for kind, ref in enumerate((key_ref, value_ref)):
+        flat[...] = ref[...].astype(jnp.float32).reshape(depth * slots, width)
+        for ctx in range(ctx_count):
+            for head in range(heads):
+                for core in range(head_count):
+                    slot = (ctx * heads + head) * head_count + core
+                    at = (kind * heads + head) * width
+                    out_ref[core, ctx, :, at : at + width] = flat[
+                        pl.ds(slot, depth, stride=slots), :
+                    ].astype(out_ref.dtype)
+
+
+def arrange_weights(key_weight, value_weight, ctx_count, heads, head_count):
+    depth, width = key_weight.shape[2], key_weight.shape[5]
+    slots = ctx_count * heads * head_count
+    rows = min(128, depth)
+    views = [w.reshape(depth, slots, width) for w in (key_weight, value_weight)]
+    block = pl.BlockSpec((rows, slots, width), lambda i: (i, 0, 0))
+    columns = 2 * heads * width
+    return pl.pallas_call(
+        functools.partial(weight_kernel, ctx_count, heads, head_count),
+        grid=(depth // rows,),
+        in_specs=[block, block],
+        out_specs=pl.BlockSpec((head_count, ctx_count, rows, columns), lambda i: (0, 0, i, 0)),
+        out_shape=jax.ShapeDtypeStruct((head_count, ctx_count, depth, columns), jnp.bfloat16),
+        scratch_shapes=[pltpu.VMEM((rows * slots, width), jnp.float32)],
+        compiler_params=params(),
+        cost_estimate=pl.CostEstimate(
+            flops=0, bytes_accessed=8 * depth * slots * width, transcendentals=0
+        ),
+        name="arrange_weights",
+    )(*views)
+
+
+def pool_kernel(ctx_count, heads, place_ref, pool_ref, *refs):
+    flat, outs = refs[-1], refs[:-1]
+    length, slots, width = pool_ref.shape[1:]
+    flat[...] = pool_ref[0].astype(jnp.float32).reshape(length * slots, width)
+    for kind in range(2):
+        for head in range(heads):
+            at = (kind * heads + head) * width
+            held = []
+            for ctx in range(ctx_count):
+                slot = (kind * ctx_count + ctx) * heads + head
+                held.append(flat[pl.ds(slot, length, stride=slots), :])
+            for step, out_ref in enumerate(outs):
+                target = lax.rem(place_ref[1] + step, ctx_count)
+                value = held[0]
+                for ctx in range(1, ctx_count):
+                    value = jnp.where(target == ctx, held[ctx], value)
+                out_ref[0, :, at : at + width] = value.astype(out_ref.dtype)
+
+
+def arrange_pool(place, prefix_pool, ctx_count, heads):
+    blocks, length, all_heads, _, double = prefix_pool.shape
+    width = double // 2
+    slots = 2 * all_heads
+    view = prefix_pool.reshape(blocks, length, all_heads, 2, width)
+    view = view.transpose(0, 1, 3, 2, 4).reshape(blocks, length, slots, width)
+    columns = 2 * heads * width
+    out = pl.BlockSpec((1, length, columns), lambda i, place: (i, 0, 0))
+    return pl.pallas_call(
+        functools.partial(pool_kernel, ctx_count, heads),
+        grid_spec=pltpu.PrefetchScalarGridSpec(
+            num_scalar_prefetch=1,
+            grid=(blocks,),
+            in_specs=[pl.BlockSpec((1, length, slots, width), lambda i, place: (i, 0, 0, 0))],
+            out_specs=[out] * ctx_count,
+            scratch_shapes=[pltpu.VMEM((length * slots, width), jnp.float32)],
+        ),
+        out_shape=[jax.ShapeDtypeStruct((blocks, length, columns), jnp.bfloat16)] * ctx_count,
+        compiler_params=params(),
+        cost_estimate=pl.CostEstimate(
+            flops=0, bytes_accessed=4 * blocks * length * slots * width, transcendentals=0
+        ),
+        name="arrange_pool",
+    )(place, view)
+
+
+def project_kernel(parts, has_term, place_ref, *refs):
+    token_refs, weight_ref = refs[:parts], refs[parts]
+    out_ref, stacked = refs[-2], refs[-1]
+    rows = token_refs[0].shape[0]
+
+    @pl.when(pl.program_id(0) == 0)
+    def _():
+        for index, token_ref in enumerate(token_refs):
+            stacked[index * rows : (index + 1) * rows, :] = token_ref[...]
+
+    total = jnp.dot(stacked[...], weight_ref[0, 0], preferred_element_type=jnp.float32)
+    if has_term:
+        total = total + refs[parts + 1][...].astype(jnp.float32)
+    out_ref[...] = total.astype(out_ref.dtype)
+
+
+def project(place, tokens, received, weights, chunk, head_step, ctx_steps, term, out_dtype):
+    head_count, ctx_count, depth, width = weights.shape
+    rows = tokens.shape[0] // CHUNKS
+    row_total = rows * (1 + len(received))
+    tile = min(256, width)
+    tiles = width // tile
+    first, last = ctx_steps
+    in_specs = [pl.BlockSpec((rows, depth), lambda j, place: (chunk, place[0]))]
+    in_specs += [pl.BlockSpec((rows, depth), lambda j, place: (0, 0)) for _ in received]
+    in_specs += [
+        pl.BlockSpec(
+            (1, 1, depth, tile),
+            lambda j, place: (
+                lax.rem(place[2] + head_step, head_count),
+                lax.rem(place[1] + first + j // tiles, ctx_count),
+                0,
+                j % tiles,
+            ),
+        )
+    ]
+    operands = [place, tokens, *received, weights]
+    if term is not None:
+        in_specs.append(
+            pl.BlockSpec((row_total, tile), lambda j, place: (0, first * tiles + j))
+        )
+        operands.append(term)
+    columns = (last - first) * width
+    return pl.pallas_call(
+        functools.partial(project_kernel, 1 + len(received), term is not None),
+        grid_spec=pltpu.PrefetchScalarGridSpec(
+            num_scalar_prefetch=1,
+            grid=(columns // tile,),
+            in_specs=in_specs,
+            out_specs=pl.BlockSpec((row_total, tile), lambda j, place: (0, j)),
+            scratch_shapes=[pltpu.VMEM((row_total, depth), tokens.dtype)],
+        ),
+        out_shape=jax.ShapeDtypeStruct((row_total, columns), out_dtype),
+        compiler_params=params(),
+        cost_estimate=pl.CostEstimate(
+            flops=2 * row_total * depth * columns,
+            bytes_accessed=2 * (depth * (columns + row_total) + 2 * row_total * columns),
+            transcendentals=0,
+        ),
+        name="project",
+    )(*operands)
+
+
+def prefix_kernel(scale, heads, ctx_count, place_ref, table_ref, query_ref, *refs):
+    pool_refs = refs[:ctx_count]
+    acc_ref, stat_ref, keys, values, mask = refs[ctx_count:]
+    blocks, length, columns = pool_refs[0].shape
+    rows, width = query_ref.shape
+    half = rows // 2
+
+    @pl.when(pl.program_id(0) == 0)
+    def _():
+        mask[...] = head_mask(mask.shape, heads)
+        for at in range(table_ref.shape[0]):
+            entry = table_ref[at]
+            step = lax.rem(place_ref[1] - entry // blocks + ctx_count, ctx_count)
+            for ctx_step, pool_ref in enumerate(pool_refs):
+
+                @pl.when(step == ctx_step)
+                def _():
+                    block = pool_ref[entry % blocks]
+                    keys[at * length : (at + 1) * length, :] = block[:, : columns // 2]
+                    values[at * length : (at + 1) * length, :] = block[:, columns // 2 :]
+
+    lane = lax.broadcasted_iota(jnp.int32, (half, width), 1)
+    for part in range(2):
+        here = slice(part * half, (part + 1) * half)
+        query_block = jnp.concatenate([query_ref[here, :]] * heads, 1) * mask[...]
+        scores = dot_keys(query_block, keys[...]) * scale
+        row_max = jnp.max(scores, axis=1, keepdims=True)
+        weights = jnp.exp2(scores - row_max)
+        row_total = jnp.sum(weights, axis=1, keepdims=True)
+        mixed = jnp.dot(
+            weights.astype(jnp.bfloat16), values[...], preferred_element_type=jnp.float32
+        )
+        acc_ref[here, :] = own_head(mixed, heads)
+        stat_ref[here, :] = jnp.where(lane < width // 2, row_max, row_total)
+
+
+def prefix_attend(place, table, query_rows, pools, scale, heads):
+    row_total, width = query_rows.shape
+    rows = min(1024, row_total)
+    length, columns = pools[0].shape[1:]
+    key_count = table.shape[0] * length
+    block = pl.BlockSpec((rows, width), lambda i, *_: (i, 0))
+    return pl.pallas_call(
+        functools.partial(prefix_kernel, scale, heads, len(pools)),
+        grid_spec=pltpu.PrefetchScalarGridSpec(
+            num_scalar_prefetch=2,
+            grid=(row_total // rows,),
+            in_specs=[block] + [pl.BlockSpec(p.shape, lambda i, *_: (0, 0, 0)) for p in pools],
+            out_specs=[block, block],
+            scratch_shapes=[
+                pltpu.VMEM((key_count, columns // 2), jnp.bfloat16),
+                pltpu.VMEM((key_count, columns // 2), jnp.bfloat16),
+                pltpu.VMEM((rows // 2, columns // 2), jnp.bfloat16),
+            ],
+        ),
+        out_shape=[jax.ShapeDtypeStruct((row_total, width), jnp.float32)] * 2,
+        compiler_params=params(),
+        cost_estimate=pl.CostEstimate(
+            flops=2 * row_total * key_count * columns,
+            bytes_accessed=row_total * width * 10,
+            transcendentals=row_total * key_count,
+        ),
+        name="prefix_attend",
+    )(place, table, query_rows, *pools)
 
 
 def fresh_kernel(
     scale, heads, per_token, first_row, length_ref, query_ref, acc_ref, stat_ref, fresh_ref, *rest
 ):
-    out_ref = rest[-1]
+    out_ref, mask = rest[-2:]
     rows, width = query_ref.shape
     wide = heads * width
     step = pl.program_id(0)
+
+    @pl.when(step == 0)
+    def _():
+        mask[...] = head_mask(mask.shape, heads)
+
     keys, values = fresh_ref[:, :wide], fresh_ref[:, wide:]
-    scores = dot_keys(split_heads(query_ref[...], heads), keys) * scale
-    row_at = lax.broadcasted_iota(jnp.int32, scores.shape, 0)
-    position = first_row + step * (rows // per_token) + row_at // per_token
+    query_block = jnp.concatenate([query_ref[...]] * heads, 1) * mask[...]
+    scores = dot_keys(query_block, keys) * scale
+    token = first_row + step * (rows // per_token)
+    position = token + unit_index(scores.shape, per_token)[0]
     column = lax.broadcasted_iota(jnp.int32, scores.shape, 1)
     scores = jnp.where(column <= position, scores, -jnp.inf)
     old_max, old_total = stat_ref[:, :1], stat_ref[:, width // 2 : width // 2 + 1]
@@ -194,32 +362,9 @@
     mixed = own_head(
         jnp.dot(weights.astype(jnp.bfloat16), values, preferred_element_type=jnp.float32), heads
     )
-    result = (acc_ref[...] * fade + mixed) / row_total
-    token = first_row + step * (rows // per_token)
-    token = token + lax.broadcasted_iota(jnp.int32, result.shape, 0) // per_token
-    out_ref[...] = jnp.where(token < length_ref[0], result, 0.0).astype(out_ref.dtype)
-
-
-def prefix_attend(query_rows, keys, values, scale, heads):
-    row_total, width = query_rows.shape
-    rows = min(512, row_total)
-    key_count = keys.shape[0]
-    whole = pl.BlockSpec(keys.shape, lambda i: (0, 0))
-    block = pl.BlockSpec((rows, width), lambda i: (i, 0))
-    return pl.pallas_call(
-        functools.partial(prefix_kernel, scale, heads),
-        grid=(row_total // rows,),
-        in_specs=[block, whole, whole],
-        out_specs=[block, block],
-        out_shape=[jax.ShapeDtypeStruct((row_total, width), jnp.float32)] * 2,
-        compiler_params=pltpu.CompilerParams(vmem_limit_bytes=VMEM_BYTES),
-        cost_estimate=pl.CostEstimate(
-            flops=4 * row_total * key_count * keys.shape[1],
-            bytes_accessed=row_total * width * 10,
-            transcendentals=row_total * key_count,
-        ),
-        name="prefix_attend",
-    )(query_rows, keys, values)
+    live = token + unit_index((rows, 1), per_token)[0] < length_ref[0]
+    share = jnp.where(live, 1.0 / row_total, 0.0)
+    out_ref[...] = ((acc_ref[...] * fade + mixed) * share).astype(out_ref.dtype)
 
 
 def fresh_attend(length, query_rows, acc, stat, fresh, earlier, chunk, scale, heads, per_token):
@@ -240,11 +385,15 @@
             fresh_kernel, scale, heads, per_token, chunk * (chunk_rows // per_token)
         ),
         grid_spec=pltpu.PrefetchScalarGridSpec(
-            num_scalar_prefetch=1, grid=(steps,), in_specs=in_specs, out_specs=block
+            num_scalar_prefetch=1,
+            grid=(steps,),
+            in_specs=in_specs,
+            out_specs=block,
+            scratch_shapes=[pltpu.VMEM((rows, heads * width), jnp.bfloat16)],
         ),
         out_shape=jax.ShapeDtypeStruct((row_total, width), jnp.bfloat16),
         input_output_aliases=aliases,
-        compiler_params=pltpu.CompilerParams(vmem_limit_bytes=VMEM_BYTES),
+        compiler_params=params(),
         cost_estimate=pl.CostEstimate(
             flops=2 * chunk_rows * fresh.shape[0] * fresh.shape[1],
             bytes_accessed=chunk_rows * width * 12,
@@ -278,47 +427,29 @@
             arrived.append(shift(piece, "batch", step))
         received.append(arrived)
 
-    pool = prefix_pool[:, :, :, 0, :]
-    blocks, block_len = pool.shape[0], pool.shape[1]
-    parts = []
-    for step in range(ctx_count):
-        target = lax.rem(ctx_at + step, ctx_count)
-        part = lax.dynamic_slice_in_dim(pool, target * heads, heads, 2)
-        parts.append(shift(part, "ctx", step) if step else part)
-    pool_rows = jnp.stack(parts)
-    table = block_table[0]
-    source = lax.rem(ctx_at - table // blocks + ctx_count, ctx_count)
-    pool_rows = pool_rows.reshape(ctx_count * blocks, block_len, heads, 2 * width)
-    chosen = jnp.take(pool_rows, source * blocks + table % blocks, axis=0, mode="clip")
-    chosen = chosen.reshape(-1, heads, 2, width)
-    prefix_keys = chosen[:, :, 0].reshape(-1, heads * width)
-    prefix_values = chosen[:, :, 1].reshape(-1, heads * width)
-
-    def arranged(weight):
-        view = weight.reshape(depth, ctx_count, heads, head_count, width)
-        return view.transpose(3, 1, 0, 2, 4).reshape(head_count, ctx_count, depth, heads * width)
-
-    weights = jnp.concatenate([arranged(key_weight), arranged(value_weight)], 3)
+    pools = arrange_pool(place, prefix_pool, ctx_count, heads)
+    pools, key_weight, value_weight = lax.optimization_barrier((pools, key_weight, value_weight))
+    pools = [shift(part, "ctx", step) if step else part for step, part in enumerate(pools)]
+
+    weights = arrange_weights(key_weight, value_weight, ctx_count, heads, head_count)
 
     query_rows = queries.reshape(token_count, heads, group, width)
     query_rows = query_rows.transpose(0, 2, 1, 3).reshape(-1, width)
-    acc, stat = prefix_attend(query_rows, prefix_keys, prefix_values, scale, heads)
+    acc, stat = prefix_attend(place, block_table[0], query_rows, pools, scale, heads)
 
     fresh_parts = []
     result = None
     cols = weights.shape[3]
     for chunk in range(CHUNKS):
-        sent = [
-            project(place, tokens, received[chunk], weights, chunk, step, jnp.bfloat16)
-            for step in range(1, head_count)
-        ]
-        sent = [shift(part, "head", step + 1) for step, part in enumerate(sent)]
-        total = project(place, tokens, received[chunk], weights, chunk, 0, jnp.float32)
-        for part in sent:
-            total = total + part.astype(jnp.float32)
-        mine = total[:, :cols]
+        call = functools.partial(project, place, tokens, received[chunk], weights, chunk)
+        term = None
+        for step in range(1, head_count):
+            part = shift(call(step, (0, ctx_count), None, jnp.bfloat16), "head", step)
+            term = part if term is None else term.astype(jnp.float32) + part.astype(jnp.float32)
+        sent = call(0, (1, ctx_count), term, jnp.bfloat16)
+        mine = call(0, (0, 1), term, jnp.float32)
         for step in range(1, ctx_count):
-            part = total[:, step * cols : (step + 1) * cols].astype(jnp.bfloat16)
+            part = sent[:, (step - 1) * cols : step * cols]
             mine = mine + shift(part, "ctx", step).astype(jnp.float32)
         fresh = mine[:rows]
         for step in range(1, batch_count):

time: 170 us -> 157 us (0.924)
  local copies, waits for them, and re-layouts: 32.5 us -> 4.19 us
  waiting for transfers between devices: 30.1 us -> 54.6 us
  other arithmetic: 8.11 us -> 0.63 us
  starting transfers between devices: 24.3 us -> 19.2 us
  Pallas kernels: 73 us -> 76.8 us
    ppermute x17, waiting for transfers between devices: 30.1 us -> 54.6 us  [shift(): lax.ppermute(array, axis, [(i, (i + step) % count) for i in range(count)])]
    reshape x5 -> x0, local copies, waits for them, and re-layouts: 12.6 us -> none  [the longest x2 6.3 us: arranged(): view.transpose(3, 1, 0, 2, 4)]
    ppermute x17, starting transfers between devices: 24.3 us -> 19.2 us  [shift(): lax.ppermute(array, axis, [(i, (i + step) % count) for i in range(count)])]
    pallas_call x5 -> x9, Pallas kernels: 40.9 us -> 45.3 us  [the longest x1 19.6 us: prefix_attend(): pl.pallas_call(functools.partial(prefix_kernel, scale, heads, len(pools))...]
    add x3 -> x0, other arithmetic: 3.97 us -> none  [the longest x2 3.95 us: reduced_shards(): total = total + part.astype(jnp.float32)]
    gather x2 -> x0, local copies, waits for them, and re-layouts: 3.67 us -> none  [reduced_shards(): jnp.take(pool_rows, source * blocks + table % blocks, axis=0, mode='clip')]
    another operation x3 -> x2, other arithmetic: 3.91 us -> 0.4 us  [the longest x1 3.48 us: reduced_shards(): pool_rows = jnp.stack(parts)]
    unnamed x21 -> x14, local copies, waits for them, and re-layouts: 5.12 us -> 1.61 us
  transfers between devices with their start and end apart: 17 -> 17, of which waited for: 6 -> 6; matrix products, arithmetic and copies ran while one was open for 22% -> 0% of each run, Pallas kernels for 24% -> 26%
where the time goes in v2:
time: 157 us; the launch traced here: 156 us
  Pallas kernels  76.8 us (49%)
  waiting for transfers between devices  54.6 us (35%)
  starting transfers between devices  19.2 us (12%)
  local copies, waits for them, and re-layouts  4.19 us (3%)
    ppermute x17, waiting for transfers between devices, shift(): lax.ppermute(array, axis, [(i, (i + step) % count) for i in range(count)])  54.6 us
    pallas_call x2, Pallas kernels, fresh_attend(): pl.pallas_call(functools.partial(fresh_kernel, scale, heads, per_token, c...  31.5 us
    pallas_call x1, Pallas kernels, prefix_attend(): pl.pallas_call(functools.partial(prefix_kernel, scale, heads, len(pools))...  19.6 us
    pallas_call x6, Pallas kernels, project(): pl.pallas_call(functools.partial(project_kernel, 1 + len(received), term...  19.4 us
    ppermute x17, starting transfers between devices, shift(): lax.ppermute(array, axis, [(i, (i + step) % count) for i in range(count)])  19.2 us
    pallas_call x1, Pallas kernels, arrange_weights(): pl.pallas_call(functools.partial(weight_kernel, ctx_count, heads, head_co...  4.59 us
  transfers between devices with their start and end apart: 17, of which 6 were waited for; matrix products, arithmetic and copies ran while one was open for 0% of the time, Pallas kernels for 26%

profile of v2, /device:TPU:0, one launch (start us, length us, event | category | flops | bytes accessed | tf_op | source)
XLA Modules:
  0.0 156.3 jit_solution(12351980831466326443)
XLA Ops:
  0.0 2.5 %constant_dynamic-slice_fusion.3 = (bf16[128,1024]{1,0:T(8,128)(2,1)}, bf16[128,1024]{1,0:T(8,128)(2,1)}, bf16[128,1024]{1,0:T(8,128)(2,1)S(1)}, bf16[128,1024]{...) fusion(bf16[256,4096]{1,0:T(8,128)(2,1)} %refs_0_.11, s32[]{:T(128)S(6)} %select_n.14, ...), kind=kLoop, calls=%fused_computation.14 | loop fusion | bytes 3145740 | tf_op jit(solution)/shard_map/dynamic_slice | solution.py:426
  2.5 5.0 %collective-permute-start.3 = (bf16[128,1024]{1,0:T(8,128)(2,1)}, bf16[128,1024]{1,0:T(8,128)(2,1)S(1)}, u32[]{:S(2)}, u32[]{:S(2)}) collective-permute-start(bf16[128,1024]{1,0:T(8,128)(2,1)} %get-tuple-element.25), channel_id=1, source_target_pairs={{0,12},{4,0},{8,4},{12,8},{1,13},{5,1},{9,5},{13,9},{2,14},{6,2},{... | collective-permute-start | bytes 786440 | tf_op jit(solution)/shard_map/ppermute | solution.py:92
  7.6 0.0 collective-permute-start.2
  7.6 1.0 collective-permute-start.1
  8.6 0.1 pad_add_fusion.place_ref
  8.7 1.7 %arrange_pool.1 = (bf16[8,128,512]{2,1,0:T(8,128)(2,1)S(1)}, bf16[8,128,512]{2,1,0:T(8,128)(2,1)S(1)}) custom-call(s32[3]{0:T(128)S(1)} %pad_add_fusion.place_ref, bf16[8,128,8,128]{3,2,1,0:T(8,128)(2,1)S(1)} %bitcast.24), custom_call_target="tpu_custom_call" | custom-call | bytes 4194304 | tf_op jit(solution)/shard_map/arrange_pool/pallas_call | solution.py:191
  10.4 0.0 copy-start.4
  10.4 1.6 %copy-done.4 = bf16[1,1,1024,4,2,128]{5,4,3,2,1,0:T(2,128)(2,1)S(1)} copy-done((bf16[1,1,1024,4,2,128]{5,4,3,2,1,0:T(2,128)(2,1)S(1)}, bf16[1,1,1024,4,2,128]{5,4,3,2,1,0:T(2,128)(2,1)}, u32[]{:S(2)}) %copy-start.4) | copy-done | bytes 2097176
  12.0 4.6 %arrange_weights.1.refs_4_ = bf16[2,2,1024,512]{3,2,1,0:T(8,128)(2,1)} custom-call(bf16[1024,8,128]{2,1,0:T(8,128)(2,1)S(1)} %bitcast.25, bf16[1024,8,128]{2,1,0:T(8,128)(2,1)S(1)} %bitcast.26), custom_call_target="tpu_custom_call" | custom-call | bytes 8388608 | tf_op jit(solution)/shard_map/arrange_weights/pallas_call | solution.py:149
  16.6 0.0 collective-permute-done.3.refs_3_
  16.6 13.5 %collective-permute-done.2.refs_2_ = bf16[128,1024]{1,0:T(8,128)(2,1)S(1)} collective-permute-done((bf16[128,1024]{1,0:T(8,128)(2,1)}, bf16[128,1024]{1,0:T(8,128)(2,1)S(1)}, u32[]{:S(2)}, u32[]{:S(2)}) %collective-permute-start.2) | collective-permute-done | bytes 262176 | tf_op jit(solution)/shard_map/ppermute | solution.py:92
  30.1 0.0 collective-permute-done.1.refs_1_
  30.1 4.3 %project.6 = bf16[512,1024]{1,0:T(8,128)(2,1)S(1)} custom-call(s32[3]{0:T(128)S(1)} %pad_add_fusion.place_ref, bf16[256,4096]{1,0:T(8,128)(2,1)S(1)} %copy-done, bf16[128,1024]{1,0:T(8,128)(2,1)S(1)} %collective-permute-done.1.refs_1_, bf16[128,1024]{1,0:T(8,128)(2,1)S(1)} %collective-permute-done.2.refs_2_, ...), custom_call_target="tpu_custom_call" | custom-call | flops 1073741824 | bytes 5242880 | tf_op jit(solution)/shard_map/project/pallas_call | solution.py:252
  34.4 0.1 collective-permute-start.4
  34.5 1.6 collective-permute-start
  36.0 2.8 %collective-permute-start.10 = (bf16[128,1024]{1,0:T(8,128)(2,1)S(1)}, bf16[128,1024]{1,0:T(8,128)(2,1)S(1)}, u32[]{:S(2)}, u32[]{:S(2)}) collective-permute-start(bf16[128,1024]{1,0:T(8,128)(2,1)S(1)} %get-tuple-element.27), channel_id=1, source_target_pairs={{0,8},{4,12},{8,0},{12,4},{1,9},{5,13},{9,1},{13,5},{2,10},{6,14},... | collective-permute-start | bytes 786440 | tf_op jit(solution)/shard_map/ppermute | solution.py:92
  38.8 2.0 %collective-permute-start.9 = (bf16[128,1024]{1,0:T(8,128)(2,1)S(1)}, bf16[128,1024]{1,0:T(8,128)(2,1)S(1)}, u32[]{:S(2)}, u32[]{:S(2)}) collective-permute-start(bf16[128,1024]{1,0:T(8,128)(2,1)S(1)} %get-tuple-element.28), channel_id=1, source_target_pairs={{0,4},{4,8},{8,12},{12,0},{1,5},{5,9},{9,13},{13,1},{2,6},{6,10},{... | collective-permute-start | bytes 786440 | tf_op jit(solution)/shard_map/ppermute | solution.py:92
  40.8 3.5 %collective-permute-done.11.refs_3_ = bf16[128,1024]{1,0:T(8,128)(2,1)S(1)} collective-permute-done((bf16[128,1024]{1,0:T(8,128)(2,1)S(1)}, bf16[128,1024]{1,0:T(8,128)(2,1)S(1)}, u32[]{:S(2)}, u32[]{:S(2)}) %collective-permute-start.11) | collective-permute-done | bytes 262176 | tf_op jit(solution)/shard_map/ppermute | solution.py:92
  44.4 17.9 %collective-permute-done.10.refs_2_ = bf16[128,1024]{1,0:T(8,128)(2,1)S(1)} collective-permute-done((bf16[128,1024]{1,0:T(8,128)(2,1)S(1)}, bf16[128,1024]{1,0:T(8,128)(2,1)S(1)}, u32[]{:S(2)}, u32[]{:S(2)}) %collective-permute-start.10) | collective-permute-done | bytes 262176 | tf_op jit(solution)/shard_map/ppermute | solution.py:92
  62.3 0.0 collective-permute-done.9.refs_1_
  62.3 4.3 %project.9 = bf16[512,1024]{1,0:T(8,128)(2,1)S(1)} custom-call(s32[3]{0:T(128)S(1)} %pad_add_fusion.place_ref, bf16[256,4096]{1,0:T(8,128)(2,1)S(1)} %copy-done, bf16[128,1024]{1,0:T(8,128)(2,1)S(1)} %collective-permute-done.9.refs_1_, bf16[128,1024]{1,0:T(8,128)(2,1)S(1)} %collective-permute-done.10.refs_2_, ...), custom_call_target="tpu_custom_call" | custom-call | flops 1073741824 | bytes 5242880 | tf_op jit(solution)/shard_map/project/pallas_call | solution.py:252
  66.6 0.1 collective-permute-start.12
  67.3 0.0 copy-start.1
  67.3 0.0 copy-start.5
  67.3 2.7 %project.8 = bf16[512,512]{1,0:T(8,128)(2,1)S(1)} custom-call(s32[3]{0:T(128)S(1)} %pad_add_fusion.place_ref, bf16[256,4096]{1,0:T(8,128)(2,1)S(1)} %copy-done, bf16[128,1024]{1,0:T(8,128)(2,1)S(1)} %collective-permute-done.1.refs_1_, bf16[128,1024]{1,0:T(8,128)(2,1)S(1)} %collective-permute-done.2.refs_2_, ...), custom_call_target="tpu_custom_call" | custom-call | flops 536870912 | bytes 3145728 | tf_op jit(solution)/shard_map/project/pallas_call | solution.py:252
  70.1 0.6 collective-permute-start.5
  70.7 19.6 %prefix_attend.1 = (f32[8192,128]{1,0:T(8,128)}, f32[8192,128]{1,0:T(8,128)}) custom-call(s32[3]{0:T(128)S(1)} %pad_add_fusion.place_ref, s32[8]{0:T(128)S(1)} %bitcast.27, bf16[8192,128]{1,0:T(8,128)(2,1)S(1)} %bitcast.21, bf16[8,128,512]{2,1,0:T(8,128)(2,1)S(1)} %get-tuple-element.15.refs_0_, bf16[8,128,512]{2,1,0:T(8,128)(2,1)S(1)} %collective-permute-done.refs_1_), custom_call_target="tpu_custom_call" | custom-call | flops 8589934592 | bytes 10485760 | tf_op jit(solution)/shard_map/prefix_attend/pallas_call | solution.py:314
  90.3 0.0 collective-permute-done.12.refs_5_
  90.3 2.7 %project.11 = bf16[512,512]{1,0:T(8,128)(2,1)S(1)} custom-call(s32[3]{0:T(128)S(1)} %pad_add_fusion.place_ref, bf16[256,4096]{1,0:T(8,128)(2,1)S(1)} %copy-done, bf16[128,1024]{1,0:T(8,128)(2,1)S(1)} %collective-permute-done.9.refs_1_, bf16[128,1024]{1,0:T(8,128)(2,1)S(1)} %collective-permute-done.10.refs_2_, ...), custom_call_target="tpu_custom_call" | custom-call | flops 536870912 | bytes 3145728 | tf_op jit(solution)/shard_map/project/pallas_call | solution.py:252
  93.0 1.6 collective-permute-start.13
  94.5 2.7 %project.7 = f32[512,512]{1,0:T(8,128)S(1)} custom-call(s32[3]{0:T(128)S(1)} %pad_add_fusion.place_ref, bf16[256,4096]{1,0:T(8,128)(2,1)S(1)} %copy-done, bf16[128,1024]{1,0:T(8,128)(2,1)S(1)} %collective-permute-done.1.refs_1_, bf16[128,1024]{1,0:T(8,128)(2,1)S(1)} %collective-permute-done.2.refs_2_, bf16[128,1024]{1,0:T(8,128)(2,1)S(1)} %collective-permute-done.3.refs_3_, ...), custom_call_target="tpu_custom_call" | custom-call | flops 536870912 | bytes 3145728 | tf_op jit(solution)/shard_map/project/pallas_call | solution.py:252
  97.2 2.7 %project.10 = f32[512,512]{1,0:T(8,128)S(1)} custom-call(s32[3]{0:T(128)S(1)} %pad_add_fusion.place_ref, bf16[256,4096]{1,0:T(8,128)(2,1)S(1)} %copy-done, bf16[128,1024]{1,0:T(8,128)(2,1)S(1)} %collective-permute-done.9.refs_1_, bf16[128,1024]{1,0:T(8,128)(2,1)S(1)} %collective-permute-done.10.refs_2_, ...), custom_call_target="tpu_custom_call" | custom-call | flops 536870912 | bytes 3145728 | tf_op jit(solution)/shard_map/project/pallas_call | solution.py:252
  100.0 0.2 fusion.6
  100.2 0.1 collective-permute-start.6
  100.3 2.0 %collective-permute-start.8 = (bf16[128,512]{1,0:T(8,128)(2,1)S(1)}, bf16[128,512]{1,0:T(8,128)(2,1)S(1)}, u32[]{:S(2)}, u32[]{:S(2)}) collective-permute-start(bf16[128,512]{1,0:T(8,128)(2,1)S(1)} %get-tuple-element.32), channel_id=1, source_target_pairs={{0,4},{4,8},{8,12},{12,0},{1,5},{5,9},{9,13},{13,1},{2,6},{6,10},{... | collective-permute-start | bytes 393224 | tf_op jit(solution)/shard_map/ppermute | solution.py:92
  102.3 0.2 collective-permute-start.7
  102.5 4.6 %collective-permute-done.13 = bf16[512,512]{1,0:T(8,128)(2,1)S(1)} collective-permute-done((bf16[512,512]{1,0:T(8,128)(2,1)S(1)}, bf16[512,512]{1,0:T(8,128)(2,1)S(1)}, u32[]{:S(2)}, u32[]{:S(2)}) %collective-permute-start.13) | collective-permute-done | bytes 524320 | tf_op jit(solution)/shard_map/ppermute | solution.py:92
  107.1 0.2 fusion.7
  107.3 0.1 collective-permute-start.14
  107.4 2.0 %collective-permute-start.16 = (bf16[128,512]{1,0:T(8,128)(2,1)S(1)}, bf16[128,512]{1,0:T(8,128)(2,1)S(1)}, u32[]{:S(2)}, u32[]{:S(2)}) collective-permute-start(bf16[128,512]{1,0:T(8,128)(2,1)S(1)} %get-tuple-element.35), channel_id=1, source_target_pairs={{0,4},{4,8},{8,12},{12,0},{1,5},{5,9},{9,13},{13,1},{2,6},{6,10},{... | collective-permute-start | bytes 393224 | tf_op jit(solution)/shard_map/ppermute | solution.py:92
  109.4 0.0 collective-permute-done.6
  109.4 0.2 collective-permute-start.15
  109.6 10.0 %collective-permute-done.7 = bf16[128,512]{1,0:T(8,128)(2,1)S(1)} collective-permute-done((bf16[128,512]{1,0:T(8,128)(2,1)S(1)}, bf16[128,512]{1,0:T(8,128)(2,1)S(1)}, u32[]{:S(2)}, u32[]{:S(2)}) %collective-permute-start.7) | collective-permute-done | bytes 131104 | tf_op jit(solution)/shard_map/ppermute | solution.py:92
  119.5 0.1 fusion.5.fresh_ref
  119.6 5.1 %collective-permute-done.15 = bf16[128,512]{1,0:T(8,128)(2,1)S(1)} collective-permute-done((bf16[128,512]{1,0:T(8,128)(2,1)S(1)}, bf16[128,512]{1,0:T(8,128)(2,1)S(1)}, u32[]{:S(2)}, u32[]{:S(2)}) %collective-permute-start.15) | collective-permute-done | bytes 131104 | tf_op jit(solution)/shard_map/ppermute | solution.py:92
  124.7 0.1 fusion.2
  124.8 15.6 %fresh_attend.2.rest_0_ = bf16[8192,128]{1,0:T(8,128)(2,1)} custom-call(s32[1]{0:T(128)S(6)} %copy.13.length_ref, bf16[8192,128]{1,0:T(8,128)(2,1)S(1)} %bitcast.22, f32[8192,128]{1,0:T(8,128)} %get-tuple-element.17.acc_ref, f32[8192,128]{1,0:T(8,128)} %get-tuple-element.18.stat_ref, bf16[128,512]{1,0:T(8,128)(2,1)S(1)} %fusion.5.fresh_ref), custom_call_target="tpu_custom_call" | custom-call | flops 536870912 | bytes 6291456 | tf_op jit(solution)/shard_map/fresh_attend/pallas_call | solution.py:383
  140.4 15.9 %fresh_attend.3 = bf16[8192,128]{1,0:T(8,128)(2,1)} custom-call(s32[1]{0:T(128)S(6)} %copy.13.length_ref, bf16[8192,128]{1,0:T(8,128)(2,1)S(1)} %bitcast.23, f32[8192,128]{1,0:T(8,128)} %get-tuple-element.17.acc_ref, f32[8192,128]{1,0:T(8,128)} %get-tuple-element.18.stat_ref, ...), custom_call_target="tpu_custom_call", output_to_operand_aliasing={{}: (5, {})} | custom-call | flops 1073741824 | bytes 6291456 | tf_op jit(solution)/shard_map/fresh_attend/pallas_call | solution.py:383
  (20 shorter events, 0.1 us)
Async XLA Ops:
  0.0 8.7 %copy-start.2 = (bf16[8,128,4,1,256]{4,2,3,1,0:T(4,128)(2,1)S(1)}, bf16[8,128,4,1,256]{4,2,3,1,0:T(4,128)(2,1)}, u32[]{:S(2)}) copy-start(bf16[8,128,4,1,256]{4,2,3,1,0:T(4,128)(2,1)} %param.11) | copy-start | bytes 6291460
  2.5 14.1 %collective-permute-start.3 = (bf16[128,1024]{1,0:T(8,128)(2,1)}, bf16[128,1024]{1,0:T(8,128)(2,1)S(1)}, u32[]{:S(2)}, u32[]{:S(2)}) collective-permute-start(bf16[128,1024]{1,0:T(8,128)(2,1)} %get-tuple-element.25), channel_id=1, source_target_pairs={{0,12},{4,0},{8,4},{12,8},{1,13},{5,1},{9,5},{13,9},{2,14},{6,2},{... | collective-permute-start | bytes 786440 | tf_op jit(solution)/shard_map/ppermute | solution.py:92
  7.6 22.5 %collective-permute-start.2 = (bf16[128,1024]{1,0:T(8,128)(2,1)}, bf16[128,1024]{1,0:T(8,128)(2,1)S(1)}, u32[]{:S(2)}, u32[]{:S(2)}) collective-permute-start(bf16[128,1024]{1,0:T(8,128)(2,1)} %get-tuple-element.29), channel_id=1, source_target_pairs={{0,8},{4,12},{8,0},{12,4},{1,9},{5,13},{9,1},{13,5},{2,10},{6,14},... | collective-permute-start | bytes 786440 | tf_op jit(solution)/shard_map/ppermute | solution.py:92
  7.6 22.5 %collective-permute-start.1 = (bf16[128,1024]{1,0:T(8,128)(2,1)}, bf16[128,1024]{1,0:T(8,128)(2,1)S(1)}, u32[]{:S(2)}, u32[]{:S(2)}) collective-permute-start(bf16[128,1024]{1,0:T(8,128)(2,1)} %get-tuple-element.30), channel_id=1, source_target_pairs={{0,4},{4,8},{8,12},{12,0},{1,5},{5,9},{9,13},{13,1},{2,6},{6,10},{... | collective-permute-start | bytes 786440 | tf_op jit(solution)/shard_map/ppermute | solution.py:92
  8.6 1.8 %copy-start.3 = (bf16[1,1,1024,4,2,128]{5,4,3,2,1,0:T(2,128)(2,1)S(1)}, bf16[1,1,1024,4,2,128]{5,4,3,2,1,0:T(2,128)(2,1)}, u32[]{:S(2)}) copy-start(bf16[1,1,1024,4,2,128]{5,4,3,2,1,0:T(2,128)(2,1)} %param.8) | copy-start | bytes 6291460
  10.4 1.6 %copy-start.4 = (bf16[1,1,1024,4,2,128]{5,4,3,2,1,0:T(2,128)(2,1)S(1)}, bf16[1,1,1024,4,2,128]{5,4,3,2,1,0:T(2,128)(2,1)}, u32[]{:S(2)}) copy-start(bf16[1,1,1024,4,2,128]{5,4,3,2,1,0:T(2,128)(2,1)} %param.9) | copy-start | bytes 6291460
  12.0 18.1 %copy-start = (bf16[256,4096]{1,0:T(8,128)(2,1)S(1)}, bf16[256,4096]{1,0:T(8,128)(2,1)}, u32[]{:S(2)}) copy-start(bf16[256,4096]{1,0:T(8,128)(2,1)} %refs_0_.11) | copy-start | bytes 6291460
  16.6 19.4 %copy-start.6 = (bf16[128,1024]{1,0:T(8,128)(2,1)S(1)}, bf16[128,1024]{1,0:T(8,128)(2,1)}, u32[]{:S(2)}) copy-start(bf16[128,1024]{1,0:T(8,128)(2,1)} %get-tuple-element.26) | copy-start | bytes 786436
  34.4 33.0 %collective-permute-start.4 = (bf16[512,1024]{1,0:T(8,128)(2,1)S(1)}, bf16[512,1024]{1,0:T(8,128)(2,1)S(1)}, u32[]{:S(2)}, u32[]{:S(2)}) collective-permute-start(bf16[512,1024]{1,0:T(8,128)(2,1)S(1)} %project.6), channel_id=1, source_target_pairs={{0,1},{1,0},{2,3},{3,2},{4,5},{5,4},{6,7},{7,6},{8,9},{9,8},{10,11... | collective-permute-start | bytes 3145736 | tf_op jit(solution)/shard_map/ppermute | solution.py:92
  34.5 36.2 %collective-permute-start = (bf16[8,128,512]{2,1,0:T(8,128)(2,1)S(1)}, bf16[8,128,512]{2,1,0:T(8,128)(2,1)S(1)}, u32[]{:S(2)}, u32[]{:S(2)}) collective-permute-start(bf16[8,128,512]{2,1,0:T(8,128)(2,1)S(1)} %get-tuple-element.16), channel_id=1, source_target_pairs={{0,2},{2,0},{1,3},{3,1},{4,6},{6,4},{5,7},{7,5},{8,10},{10,8},{9,1... | collective-permute-start | bytes 3145736 | tf_op jit(solution)/shard_map/ppermute | solution.py:92
  36.0 8.4 %collective-permute-start.11 = (bf16[128,1024]{1,0:T(8,128)(2,1)S(1)}, bf16[128,1024]{1,0:T(8,128)(2,1)S(1)}, u32[]{:S(2)}, u32[]{:S(2)}) collective-permute-start(bf16[128,1024]{1,0:T(8,128)(2,1)S(1)} %copy-done.6), channel_id=1, source_target_pairs={{0,12},{4,0},{8,4},{12,8},{1,13},{5,1},{9,5},{13,9},{2,14},{6,2},{... | collective-permute-start | bytes 786440 | tf_op jit(solution)/shard_map/ppermute | solution.py:92
  36.0 26.3 %collective-permute-start.10 = (bf16[128,1024]{1,0:T(8,128)(2,1)S(1)}, bf16[128,1024]{1,0:T(8,128)(2,1)S(1)}, u32[]{:S(2)}, u32[]{:S(2)}) collective-permute-start(bf16[128,1024]{1,0:T(8,128)(2,1)S(1)} %get-tuple-element.27), channel_id=1, source_target_pairs={{0,8},{4,12},{8,0},{12,4},{1,9},{5,13},{9,1},{13,5},{2,10},{6,14},... | collective-permute-start | bytes 786440 | tf_op jit(solution)/shard_map/ppermute | solution.py:92
  38.8 23.5 %collective-permute-start.9 = (bf16[128,1024]{1,0:T(8,128)(2,1)S(1)}, bf16[128,1024]{1,0:T(8,128)(2,1)S(1)}, u32[]{:S(2)}, u32[]{:S(2)}) collective-permute-start(bf16[128,1024]{1,0:T(8,128)(2,1)S(1)} %get-tuple-element.28), channel_id=1, source_target_pairs={{0,4},{4,8},{8,12},{12,0},{1,5},{5,9},{9,13},{13,1},{2,6},{6,10},{... | collective-permute-start | bytes 786440 | tf_op jit(solution)/shard_map/ppermute | solution.py:92
  66.6 23.7 %collective-permute-start.12 = (bf16[512,1024]{1,0:T(8,128)(2,1)S(1)}, bf16[512,1024]{1,0:T(8,128)(2,1)S(1)}, u32[]{:S(2)}, u32[]{:S(2)}) collective-permute-start(bf16[512,1024]{1,0:T(8,128)(2,1)S(1)} %project.9), channel_id=1, source_target_pairs={{0,1},{1,0},{2,3},{3,2},{4,5},{5,4},{6,7},{7,6},{8,9},{9,8},{10,11... | collective-permute-start | bytes 3145736 | tf_op jit(solution)/shard_map/ppermute | solution.py:92
  67.3 3.4 %copy-start.1 = (bf16[256,2,1,2048]{3,1,2,0:T(2,128)(2,1)S(1)}, bf16[256,2,1,2048]{3,1,2,0:T(2,128)(2,1)}, u32[]{:S(2)}) copy-start(bf16[256,2,1,2048]{3,1,2,0:T(2,128)(2,1)} %param.10) | copy-start | bytes 6291460
  67.3 3.4 %copy-start.5 = (s32[1,8]{1,0:T(1,128)S(1)}, s32[1,8]{1,0:T(1,128)}, u32[]{:S(2)}) copy-start(s32[1,8]{1,0:T(1,128)} %param.12) | copy-start | bytes 100
  70.1 29.9 %collective-permute-start.5 = (bf16[512,512]{1,0:T(8,128)(2,1)S(1)}, bf16[512,512]{1,0:T(8,128)(2,1)S(1)}, u32[]{:S(2)}, u32[]{:S(2)}) collective-permute-start(bf16[512,512]{1,0:T(8,128)(2,1)S(1)} %project.8), channel_id=1, source_target_pairs={{0,2},{2,0},{1,3},{3,1},{4,6},{6,4},{5,7},{7,5},{8,10},{10,8},{9,1... | collective-permute-start | bytes 1572872 | tf_op jit(solution)/shard_map/ppermute | solution.py:92
  93.0 14.1 %collective-permute-start.13 = (bf16[512,512]{1,0:T(8,128)(2,1)S(1)}, bf16[512,512]{1,0:T(8,128)(2,1)S(1)}, u32[]{:S(2)}, u32[]{:S(2)}) collective-permute-start(bf16[512,512]{1,0:T(8,128)(2,1)S(1)} %project.11), channel_id=1, source_target_pairs={{0,2},{2,0},{1,3},{3,1},{4,6},{6,4},{5,7},{7,5},{8,10},{10,8},{9,1... | collective-permute-start | bytes 1572872 | tf_op jit(solution)/shard_map/ppermute | solution.py:92
  100.2 9.2 %collective-permute-start.6 = (bf16[128,512]{1,0:T(8,128)(2,1)S(1)}, bf16[128,512]{1,0:T(8,128)(2,1)S(1)}, u32[]{:S(2)}, u32[]{:S(2)}) collective-permute-start(bf16[128,512]{1,0:T(8,128)(2,1)S(1)} %get-tuple-element.31), channel_id=1, source_target_pairs={{0,12},{4,0},{8,4},{12,8},{1,13},{5,1},{9,5},{13,9},{2,14},{6,2},{... | collective-permute-start | bytes 393224 | tf_op jit(solution)/shard_map/ppermute | solution.py:92
  100.3 9.3 %collective-permute-start.8 = (bf16[128,512]{1,0:T(8,128)(2,1)S(1)}, bf16[128,512]{1,0:T(8,128)(2,1)S(1)}, u32[]{:S(2)}, u32[]{:S(2)}) collective-permute-start(bf16[128,512]{1,0:T(8,128)(2,1)S(1)} %get-tuple-element.32), channel_id=1, source_target_pairs={{0,4},{4,8},{8,12},{12,0},{1,5},{5,9},{9,13},{13,1},{2,6},{6,10},{... | collective-permute-start | bytes 393224 | tf_op jit(solution)/shard_map/ppermute | solution.py:92
  102.3 17.2 %collective-permute-start.7 = (bf16[128,512]{1,0:T(8,128)(2,1)S(1)}, bf16[128,512]{1,0:T(8,128)(2,1)S(1)}, u32[]{:S(2)}, u32[]{:S(2)}) collective-permute-start(bf16[128,512]{1,0:T(8,128)(2,1)S(1)} %get-tuple-element.33), channel_id=1, source_target_pairs={{0,8},{4,12},{8,0},{12,4},{1,9},{5,13},{9,1},{13,5},{2,10},{6,14},... | collective-permute-start | bytes 393224 | tf_op jit(solution)/shard_map/ppermute | solution.py:92
  107.3 12.3 %collective-permute-start.14 = (bf16[128,512]{1,0:T(8,128)(2,1)S(1)}, bf16[128,512]{1,0:T(8,128)(2,1)S(1)}, u32[]{:S(2)}, u32[]{:S(2)}) collective-permute-start(bf16[128,512]{1,0:T(8,128)(2,1)S(1)} %get-tuple-element.34), channel_id=1, source_target_pairs={{0,12},{4,0},{8,4},{12,8},{1,13},{5,1},{9,5},{13,9},{2,14},{6,2},{... | collective-permute-start | bytes 393224 | tf_op jit(solution)/shard_map/ppermute | solution.py:92
  107.4 12.2 %collective-permute-start.16 = (bf16[128,512]{1,0:T(8,128)(2,1)S(1)}, bf16[128,512]{1,0:T(8,128)(2,1)S(1)}, u32[]{:S(2)}, u32[]{:S(2)}) collective-permute-start(bf16[128,512]{1,0:T(8,128)(2,1)S(1)} %get-tuple-element.35), channel_id=1, source_target_pairs={{0,4},{4,8},{8,12},{12,0},{1,5},{5,9},{9,13},{13,1},{2,6},{6,10},{... | collective-permute-start | bytes 393224 | tf_op jit(solution)/shard_map/ppermute | solution.py:92
  109.4 15.3 %collective-permute-start.15 = (bf16[128,512]{1,0:T(8,128)(2,1)S(1)}, bf16[128,512]{1,0:T(8,128)(2,1)S(1)}, u32[]{:S(2)}, u32[]{:S(2)}) collective-permute-start(bf16[128,512]{1,0:T(8,128)(2,1)S(1)} %get-tuple-element.36), channel_id=1, source_target_pairs={{0,8},{4,12},{8,0},{12,4},{1,9},{5,13},{9,1},{13,5},{2,10},{6,14},... | collective-permute-start | bytes 393224 | tf_op jit(solution)/shard_map/ppermute | solution.py:92

commit v3 on v2

--- a/solution.py
+++ b/solution.py
@@ -92,6 +92,17 @@
     return lax.ppermute(array, axis, [(i, (i + step) % count) for i in range(count)])
 
 
+def trade(array, axis, bits):
+    return lax.ppermute(array, axis, [(i, i ^ bits) for i in range(lax.axis_size(axis))])
+
+
+def halving_order(count):
+    order, bit = [0], count // 2
+    while bit:
+        order, bit = order + [i ^ bit for i in order], bit // 2
+    return order
+
+
 def unit_index(shape, unit):
     row = lax.broadcasted_iota(jnp.int32, shape, 0)
     if unit & (unit - 1):
@@ -106,18 +117,25 @@
     return jnp.where(inside, 1.0, 0.0).astype(jnp.bfloat16)
 
 
-def own_head(block, heads):
-    width = block.shape[1] // heads
-    result = block[:, :width]
-    head_of = unit_index(result.shape, heads)[1]
+def own_head(block, heads, width):
+    result = block[:width]
+    row = lax.broadcasted_iota(jnp.int32, result.shape, 1)
+    head_of = row % heads if heads & (heads - 1) else row & (heads - 1)
     for i in range(1, heads):
-        result = jnp.where(head_of == i, block[:, i * width : (i + 1) * width], result)
+        result = jnp.where(head_of == i, block[i * width : (i + 1) * width], result)
     return result
 
 
-def dot_keys(query_block, keys):
+def softmax_parts(scores, old_max=None):
+    row_max = jnp.max(scores, axis=0, keepdims=True)
+    if old_max is not None:
+        row_max = jnp.maximum(row_max, old_max)
+    return row_max, jnp.exp2(scores - row_max).astype(jnp.bfloat16)
+
+
+def dot_queries(keys, query_block):
     return lax.dot_general(
-        query_block, keys, (((1,), (1,)), ((), ())), preferred_element_type=jnp.float32
+        keys, query_block, (((1,), (1,)), ((), ())), preferred_element_type=jnp.float32
     )
 
 
@@ -177,6 +195,7 @@
                 value = held[0]
                 for ctx in range(1, ctx_count):
                     value = jnp.where(target == ctx, held[ctx], value)
+                value = value.T if kind else value
                 out_ref[0, :, at : at + width] = value.astype(out_ref.dtype)
 
 
@@ -274,35 +293,38 @@
     acc_ref, stat_ref, keys, values, mask = refs[ctx_count:]
     blocks, length, columns = pool_refs[0].shape
     rows, width = query_ref.shape
-    half = rows // 2
+    part_rows = mask.shape[0]
+    wide = heads * width
 
     @pl.when(pl.program_id(0) == 0)
     def _():
         mask[...] = head_mask(mask.shape, heads)
+        values[wide:, :] = jnp.ones_like(values[wide:, :])
         for at in range(table_ref.shape[0]):
             entry = table_ref[at]
+            here = slice(at * length, (at + 1) * length)
             step = lax.rem(place_ref[1] - entry // blocks + ctx_count, ctx_count)
             for ctx_step, pool_ref in enumerate(pool_refs):
 
                 @pl.when(step == ctx_step)
                 def _():
                     block = pool_ref[entry % blocks]
-                    keys[at * length : (at + 1) * length, :] = block[:, : columns // 2]
-                    values[at * length : (at + 1) * length, :] = block[:, columns // 2 :]
-
-    lane = lax.broadcasted_iota(jnp.int32, (half, width), 1)
-    for part in range(2):
-        here = slice(part * half, (part + 1) * half)
+                    keys[here, :] = block[:, :wide]
+                    for head in range(heads):
+                        low = wide + head * length
+                        values[head * width : (head + 1) * width, here] = block[
+                            :, low : low + length
+                        ]
+
+    for part in range(rows // part_rows):
+        here = slice(part * part_rows, (part + 1) * part_rows)
         query_block = jnp.concatenate([query_ref[here, :]] * heads, 1) * mask[...]
-        scores = dot_keys(query_block, keys[...]) * scale
-        row_max = jnp.max(scores, axis=1, keepdims=True)
-        weights = jnp.exp2(scores - row_max)
-        row_total = jnp.sum(weights, axis=1, keepdims=True)
-        mixed = jnp.dot(
-            weights.astype(jnp.bfloat16), values[...], preferred_element_type=jnp.float32
-        )
-        acc_ref[here, :] = own_head(mixed, heads)
-        stat_ref[here, :] = jnp.where(lane < width // 2, row_max, row_total)
+        row_max, weights = softmax_parts(dot_queries(keys[...], query_block) * scale)
+        mixed = jnp.dot(values[...], weights, preferred_element_type=jnp.float32)
+        acc_ref[:, here] = own_head(mixed, heads, width)
+        half = stat_ref.shape[0] // 2
+        stat_ref[:half, here] = jnp.broadcast_to(row_max, (half, part_rows))
+        stat_ref[half:, here] = jnp.broadcast_to(mixed[wide : wide + 1], (half, part_rows))
 
 
 def prefix_attend(place, table, query_rows, pools, scale, heads):
@@ -310,25 +332,32 @@
     rows = min(1024, row_total)
     length, columns = pools[0].shape[1:]
     key_count = table.shape[0] * length
-    block = pl.BlockSpec((rows, width), lambda i, *_: (i, 0))
+    wide = columns // 2
     return pl.pallas_call(
         functools.partial(prefix_kernel, scale, heads, len(pools)),
         grid_spec=pltpu.PrefetchScalarGridSpec(
             num_scalar_prefetch=2,
             grid=(row_total // rows,),
-            in_specs=[block] + [pl.BlockSpec(p.shape, lambda i, *_: (0, 0, 0)) for p in pools],
-            out_specs=[block, block],
+            in_specs=[pl.BlockSpec((rows, width), lambda i, *_: (i, 0))]
+            + [pl.BlockSpec(p.shape, lambda i, *_: (0, 0, 0)) for p in pools],
+            out_specs=[
+                pl.BlockSpec((width, rows), lambda i, *_: (0, i)),
+                pl.BlockSpec((8, rows), lambda i, *_: (0, i)),
+            ],
             scratch_shapes=[
-                pltpu.VMEM((key_count, columns // 2), jnp.bfloat16),
-                pltpu.VMEM((key_count, columns // 2), jnp.bfloat16),
-                pltpu.VMEM((rows // 2, columns // 2), jnp.bfloat16),
+                pltpu.VMEM((key_count, wide), jnp.bfloat16),
+                pltpu.VMEM((wide + 16, key_count), jnp.bfloat16),
+                pltpu.VMEM((min(256, rows), wide), jnp.bfloat16),
             ],
         ),
-        out_shape=[jax.ShapeDtypeStruct((row_total, width), jnp.float32)] * 2,
+        out_shape=[
+            jax.ShapeDtypeStruct((width, row_total), jnp.float32),
+            jax.ShapeDtypeStruct((8, row_total), jnp.float32),
+        ],
         compiler_params=params(),
         cost_estimate=pl.CostEstimate(
             flops=2 * row_total * key_count * columns,
-            bytes_accessed=row_total * width * 10,
+            bytes_accessed=row_total * width * 6,
             transcendentals=row_total * key_count,
         ),
         name="prefix_attend",
@@ -338,7 +367,7 @@
 def fresh_kernel(
     scale, heads, per_token, first_row, length_ref, query_ref, acc_ref, stat_ref, fresh_ref, *rest
 ):
-    out_ref, mask = rest[-2:]
+    out_ref, values, mask = rest[-3:]
     rows, width = query_ref.shape
     wide = heads * width
     step = pl.program_id(0)
@@ -346,25 +375,27 @@
     @pl.when(step == 0)
     def _():
         mask[...] = head_mask(mask.shape, heads)
-
-    keys, values = fresh_ref[:, :wide], fresh_ref[:, wide:]
+        values[wide:, :] = jnp.ones_like(values[wide:, :])
+        values[:wide, :] = fresh_ref[:, wide:].astype(jnp.float32).T.astype(jnp.bfloat16)
+
     query_block = jnp.concatenate([query_ref[...]] * heads, 1) * mask[...]
-    scores = dot_keys(query_block, keys) * scale
+    scores = dot_queries(fresh_ref[:, :wide], query_block) * scale
     token = first_row + step * (rows // per_token)
-    position = token + unit_index(scores.shape, per_token)[0]
-    column = lax.broadcasted_iota(jnp.int32, scores.shape, 1)
-    scores = jnp.where(column <= position, scores, -jnp.inf)
-    old_max, old_total = stat_ref[:, :1], stat_ref[:, width // 2 : width // 2 + 1]
-    row_max = jnp.maximum(jnp.max(scores, axis=1, keepdims=True), old_max)
-    weights = jnp.exp2(scores - row_max)
+    row = lax.broadcasted_iota(jnp.int32, (1, rows), 1)
+    token = token + (
+        row // per_token if per_token & (per_token - 1) else row >> (per_token.bit_length() - 1)
+    )
+    key_at = lax.broadcasted_iota(jnp.int32, scores.shape, 0)
+    scores = jnp.where(key_at <= token, scores, -jnp.inf)
+    half = stat_ref.shape[0] // 2
+    old_max, old_total = stat_ref[:1, :], stat_ref[half : half + 1, :]
+    row_max, weights = softmax_parts(scores, old_max)
     fade = jnp.exp2(old_max - row_max)
-    row_total = old_total * fade + jnp.sum(weights, axis=1, keepdims=True)
-    mixed = own_head(
-        jnp.dot(weights.astype(jnp.bfloat16), values, preferred_element_type=jnp.float32), heads
-    )
-    live = token + unit_index((rows, 1), per_token)[0] < length_ref[0]
-    share = jnp.where(live, 1.0 / row_total, 0.0)
-    out_ref[...] = ((acc_ref[...] * fade + mixed) * share).astype(out_ref.dtype)
+    mixed = jnp.dot(values[...], weights, preferred_element_type=jnp.float32)
+    row_total = old_total * fade + mixed[wide : wide + 1]
+    share = jnp.where(token < length_ref[0], 1.0 / row_total, 0.0)
+    result = acc_ref[...] * (fade * share) + own_head(mixed, heads, width) * share
+    out_ref[...] = result.T.astype(out_ref.dtype)
 
 
 def fresh_attend(length, query_rows, acc, stat, fresh, earlier, chunk, scale, heads, per_token):
@@ -373,7 +404,12 @@
     rows = min(512, chunk_rows)
     steps = chunk_rows // rows
     block = pl.BlockSpec((rows, width), lambda i, length: (chunk * steps + i, 0))
-    in_specs = [block, block, block, pl.BlockSpec(fresh.shape, lambda i, length: (0, 0))]
+    in_specs = [
+        block,
+        pl.BlockSpec((width, rows), lambda i, length: (0, chunk * steps + i)),
+        pl.BlockSpec((stat.shape[0], rows), lambda i, length: (0, chunk * steps + i)),
+        pl.BlockSpec(fresh.shape, lambda i, length: (0, 0)),
+    ]
     operands = [length, query_rows, acc, stat, fresh]
     aliases = {}
     if earlier is not None:
@@ -389,14 +425,17 @@
             grid=(steps,),
             in_specs=in_specs,
             out_specs=block,
-            scratch_shapes=[pltpu.VMEM((rows, heads * width), jnp.bfloat16)],
+            scratch_shapes=[
+                pltpu.VMEM((heads * width + 16, fresh.shape[0]), jnp.bfloat16),
+                pltpu.VMEM((rows, heads * width), jnp.bfloat16),
+            ],
         ),
         out_shape=jax.ShapeDtypeStruct((row_total, width), jnp.bfloat16),
         input_output_aliases=aliases,
         compiler_params=params(),
         cost_estimate=pl.CostEstimate(
             flops=2 * chunk_rows * fresh.shape[0] * fresh.shape[1],
-            bytes_accessed=chunk_rows * width * 12,
+            bytes_accessed=chunk_rows * width * 8,
             transcendentals=chunk_rows * fresh.shape[0],
         ),
         name="fresh_attend",
@@ -418,13 +457,14 @@
     rows = token_count // CHUNKS
     scale = math.log2(math.e) / math.sqrt(width)
 
+    order = halving_order(batch_count)
     received = []
     for chunk in range(CHUNKS):
         arrived = []
-        for step in range(1, batch_count):
-            target = lax.rem(batch_at + step, batch_count)
-            piece = lax.dynamic_slice(tokens, (chunk * rows, target * depth), (rows, depth))
-            arrived.append(shift(piece, "batch", step))
+        for bits in order[1:]:
+            start = (batch_at ^ bits) * depth
+            piece = lax.dynamic_slice(tokens, (chunk * rows, start), (rows, depth))
+            arrived.append(trade(piece, "batch", bits))
         received.append(arrived)
 
     pools = arrange_pool(place, prefix_pool, ctx_count, heads)
@@ -451,11 +491,13 @@
         for step in range(1, ctx_count):
             part = sent[:, (step - 1) * cols : step * cols]
             mine = mine + shift(part, "ctx", step).astype(jnp.float32)
-        fresh = mine[:rows]
-        for step in range(1, batch_count):
-            part = mine[step * rows : (step + 1) * rows].astype(jnp.bfloat16)
-            fresh = fresh + shift(part, "batch", -step).astype(jnp.float32)
-        fresh_parts.append(fresh.astype(jnp.bfloat16))
+        bit = 1
+        while bit < batch_count:
+            half = mine.shape[0] // 2
+            part = trade(mine[half:].astype(jnp.bfloat16), "batch", bit)
+            mine = mine[:half] + part.astype(jnp.float32)
+            bit *= 2
+        fresh_parts.append(mine.astype(jnp.bfloat16))
         result = fresh_attend(
             lengths,
             query_rows,
@@ -476,7 +518,7 @@
     def shards(tokens, key_weight, value_weight, *rest):
         prompts = mesh.shape["batch"]
         columns = 2 * math.prod(key_weight.shape[3:])
-        few_tokens = prompts * tokens.shape[0] <= columns
+        few_tokens = prompts * tokens.shape[0] <= columns and not prompts & (prompts - 1)
         form = reduced_shards if few_tokens else gathered_shards
         return form(tokens, key_weight, value_weight, *rest)
 

time: 157 us -> 160 us (1.019)
  Pallas kernels: 76.8 us -> 62.6 us
  starting transfers between devices: 19.2 us -> 29.8 us
  waiting for transfers between devices: 54.6 us -> 60.4 us
    ppermute x0 -> x10, waiting for transfers between devices: none -> 30.8 us  [trade(): lax.ppermute(array, axis, [(i, i ^ bits) for i in range(lax.axis_size(axi...]
    ppermute x0 -> x10, starting transfers between devices: none -> 25.7 us  [trade(): lax.ppermute(array, axis, [(i, i ^ bits) for i in range(lax.axis_size(axi...]
    ppermute x17 -> x5, waiting for transfers between devices: 54.6 us -> 29.6 us  [shift(): lax.ppermute(array, axis, [(i, (i + step) % count) for i in range(count)])]
    ppermute x17 -> x5, starting transfers between devices: 19.2 us -> 4.13 us  [shift(): lax.ppermute(array, axis, [(i, (i + step) % count) for i in range(count)])]
    pallas_call x2, Pallas kernels: 31.5 us -> 16.5 us  [fresh_attend(): pl.pallas_call(functools.partial(fresh_kernel, scale, heads, per_token, c...]
  transfers between devices with their start and end apart: 17 -> 15, of which waited for: 6 -> 7; matrix products, arithmetic and copies ran while one was open for 0% -> 0% of each run, Pallas kernels for 26% -> 29%
where the time goes in v3:
time: 160 us
  Pallas kernels  62.6 us (39%)
  waiting for transfers between devices  60.4 us (38%)
  starting transfers between devices  29.8 us (19%)
  local copies, waits for them, and re-layouts  5.39 us (3%)
    ppermute x10, waiting for transfers between devices, trade(): lax.ppermute(array, axis, [(i, i ^ bits) for i in range(lax.axis_size(axi...  30.8 us
    ppermute x5, waiting for transfers between devices, shift(): lax.ppermute(array, axis, [(i, (i + step) % count) for i in range(count)])  29.6 us
    ppermute x10, starting transfers between devices, trade(): lax.ppermute(array, axis, [(i, i ^ bits) for i in range(lax.axis_size(axi...  25.7 us
    pallas_call x1, Pallas kernels, prefix_attend(): pl.pallas_call(functools.partial(prefix_kernel, scale, heads, len(pools))...  20.1 us
    pallas_call x6, Pallas kernels, project(): pl.pallas_call(functools.partial(project_kernel, 1 + len(received), term...  19.3 us
    pallas_call x2, Pallas kernels, fresh_attend(): pl.pallas_call(functools.partial(fresh_kernel, scale, heads, per_token, c...  16.5 us
    pallas_call x1, Pallas kernels, arrange_weights(): pl.pallas_call(functools.partial(weight_kernel, ctx_count, heads, head_co...  4.63 us
    ppermute x5, starting transfers between devices, shift(): lax.ppermute(array, axis, [(i, (i + step) % count) for i in range(count)])  4.13 us
  transfers between devices with their start and end apart: 15, of which 7 were waited for; matrix products, arithmetic and copies ran while one was open for 0% of the time, Pallas kernels for 29%

profile of v3, /device:TPU:0, one launch (start us, length us, event | category | flops | bytes accessed | tf_op | source)
XLA Modules:
  0.0 159.7 jit_solution(7821470530928553260)
XLA Ops:
  0.0 2.7 %constant_dynamic-slice_fusion.3 = (bf16[128,1024]{1,0:T(8,128)(2,1)}, bf16[128,1024]{1,0:T(8,128)(2,1)}, bf16[128,1024]{1,0:T(8,128)(2,1)}, bf16[128,1024]{1,0:...) fusion(bf16[256,4096]{1,0:T(8,128)(2,1)} %refs_0_.11, s32[]{:T(128)S(6)} %select_n.14, ...), kind=kLoop, calls=%fused_computation.16 | loop fusion | bytes 3145740 | tf_op jit(solution)/shard_map/dynamic_slice | solution.py:466
  2.7 4.0 %collective-permute-start.8 = (bf16[128,1024]{1,0:T(8,128)(2,1)}, bf16[128,1024]{1,0:T(8,128)(2,1)S(1)}, u32[]{:S(2)}, u32[]{:S(2)}) collective-permute-start(bf16[128,1024]{1,0:T(8,128)(2,1)} %get-tuple-element.24), channel_id=1, source_target_pairs={{0,8},{4,12},{8,0},{12,4},{1,9},{5,13},{9,1},{13,5},{2,10},{6,14},... | collective-permute-start | bytes 786440 | tf_op jit(solution)/shard_map/ppermute | solution.py:96
  6.7 1.6 collective-permute-start.9
  8.3 1.9 %collective-permute-start.1 = (bf16[128,1024]{1,0:T(8,128)(2,1)}, bf16[128,1024]{1,0:T(8,128)(2,1)S(1)}, u32[]{:S(2)}, u32[]{:S(2)}) collective-permute-start(bf16[128,1024]{1,0:T(8,128)(2,1)} %get-tuple-element.26), channel_id=1, source_target_pairs={{0,8},{4,12},{8,0},{12,4},{1,9},{5,13},{9,1},{13,5},{2,10},{6,14},... | collective-permute-start | bytes 786440 | tf_op jit(solution)/shard_map/ppermute | solution.py:96
  10.2 2.5 %collective-permute-start.2 = (bf16[128,1024]{1,0:T(8,128)(2,1)}, bf16[128,1024]{1,0:T(8,128)(2,1)S(1)}, u32[]{:S(2)}, u32[]{:S(2)}) collective-permute-start(bf16[128,1024]{1,0:T(8,128)(2,1)} %get-tuple-element.25), channel_id=1, source_target_pairs={{0,4},{4,0},{8,12},{12,8},{1,5},{5,1},{9,13},{13,9},{2,6},{6,2},{1... | collective-permute-start | bytes 786440 | tf_op jit(solution)/shard_map/ppermute | solution.py:96
  12.7 0.1 pad_add_fusion.place_ref
  12.8 2.1 %arrange_pool.1 = (bf16[8,128,512]{2,1,0:T(8,128)(2,1)S(1)}, bf16[8,128,512]{2,1,0:T(8,128)(2,1)S(1)}) custom-call(s32[3]{0:T(128)S(1)} %pad_add_fusion.place_ref, bf16[8,128,8,128]{3,2,1,0:T(8,128)(2,1)S(1)} %bitcast.24), custom_call_target="tpu_custom_call" | custom-call | bytes 4194304 | tf_op jit(solution)/shard_map/arrange_pool/pallas_call | solution.py:210
  14.9 0.0 copy-start.5
  14.9 1.0 copy-done.5
  15.9 1.6 copy-done.4
  17.5 4.6 %arrange_weights.1.refs_4_ = bf16[2,2,1024,512]{3,2,1,0:T(8,128)(2,1)} custom-call(bf16[1024,8,128]{2,1,0:T(8,128)(2,1)S(1)} %bitcast.25, bf16[1024,8,128]{2,1,0:T(8,128)(2,1)S(1)} %bitcast.26), custom_call_target="tpu_custom_call" | custom-call | bytes 8388608 | tf_op jit(solution)/shard_map/arrange_weights/pallas_call | solution.py:167
  22.1 1.6 %collective-permute-start.3 = (bf16[128,1024]{1,0:T(8,128)(2,1)S(1)}, bf16[128,1024]{1,0:T(8,128)(2,1)S(1)}, u32[]{:S(2)}, u32[]{:S(2)}) collective-permute-start(bf16[128,1024]{1,0:T(8,128)(2,1)S(1)} %copy-done.8), channel_id=1, source_target_pairs={{0,12},{4,8},{8,4},{12,0},{1,13},{5,9},{9,5},{13,1},{2,14},{6,10},... | collective-permute-start | bytes 786440 | tf_op jit(solution)/shard_map/ppermute | solution.py:96
  23.7 2.0 %collective-permute-done.9.refs_2_ = bf16[128,1024]{1,0:T(8,128)(2,1)S(1)} collective-permute-done((bf16[128,1024]{1,0:T(8,128)(2,1)}, bf16[128,1024]{1,0:T(8,128)(2,1)S(1)}, u32[]{:S(2)}, u32[]{:S(2)}) %collective-permute-start.9) | collective-permute-done | bytes 262176 | tf_op jit(solution)/shard_map/ppermute | solution.py:96
  25.7 1.1 collective-permute-done.10.refs_3_
  26.8 4.3 %project.9 = bf16[512,1024]{1,0:T(8,128)(2,1)S(1)} custom-call(s32[3]{0:T(128)S(1)} %pad_add_fusion.place_ref, bf16[256,4096]{1,0:T(8,128)(2,1)S(1)} %copy-done, bf16[128,1024]{1,0:T(8,128)(2,1)S(1)} %collective-permute-done.8.refs_1_, bf16[128,1024]{1,0:T(8,128)(2,1)S(1)} %collective-permute-done.9.refs_2_, ...), custom_call_target="tpu_custom_call" | custom-call | flops 1073741824 | bytes 5242880 | tf_op jit(solution)/shard_map/project/pallas_call | solution.py:271
  31.1 0.1 collective-permute-start.11
  31.2 16.7 %collective-permute-done.1.refs_1_ = bf16[128,1024]{1,0:T(8,128)(2,1)S(1)} collective-permute-done((bf16[128,1024]{1,0:T(8,128)(2,1)}, bf16[128,1024]{1,0:T(8,128)(2,1)S(1)}, u32[]{:S(2)}, u32[]{:S(2)}) %collective-permute-start.1) | collective-permute-done | bytes 262176 | tf_op jit(solution)/shard_map/ppermute | solution.py:96
  47.8 4.3 %project.6 = bf16[512,1024]{1,0:T(8,128)(2,1)S(1)} custom-call(s32[3]{0:T(128)S(1)} %pad_add_fusion.place_ref, bf16[256,4096]{1,0:T(8,128)(2,1)S(1)} %copy-done, bf16[128,1024]{1,0:T(8,128)(2,1)S(1)} %collective-permute-done.1.refs_1_, bf16[128,1024]{1,0:T(8,128)(2,1)S(1)} %collective-permute-done.2.refs_2_, ...), custom_call_target="tpu_custom_call" | custom-call | flops 1073741824 | bytes 5242880 | tf_op jit(solution)/shard_map/project/pallas_call | solution.py:271
  52.1 0.0 copy-start.6
  52.1 0.1 collective-permute-start.4
  52.2 0.0 collective-permute-done.11.refs_5_
  52.2 2.7 %project.11 = bf16[512,512]{1,0:T(8,128)(2,1)S(1)} custom-call(s32[3]{0:T(128)S(1)} %pad_add_fusion.place_ref, bf16[256,4096]{1,0:T(8,128)(2,1)S(1)} %copy-done, bf16[128,1024]{1,0:T(8,128)(2,1)S(1)} %collective-permute-done.8.refs_1_, bf16[128,1024]{1,0:T(8,128)(2,1)S(1)} %collective-permute-done.9.refs_2_, ...), custom_call_target="tpu_custom_call" | custom-call | flops 536870912 | bytes 3145728 | tf_op jit(solution)/shard_map/project/pallas_call | solution.py:271
  54.9 1.9 %collective-permute-start.12 = (bf16[512,512]{1,0:T(8,128)(2,1)S(1)}, bf16[512,512]{1,0:T(8,128)(2,1)S(1)}, u32[]{:S(2)}, u32[]{:S(2)}) collective-permute-start(bf16[512,512]{1,0:T(8,128)(2,1)S(1)} %project.11), channel_id=1, source_target_pairs={{0,2},{2,0},{1,3},{3,1},{4,6},{6,4},{5,7},{7,5},{8,10},{10,8},{9,1... | collective-permute-start | bytes 1572872 | tf_op jit(solution)/shard_map/ppermute | solution.py:92
  56.8 0.2 collective-permute-start
  57.0 0.0 collective-permute-done.4.refs_5_
  57.0 2.7 %project.8 = bf16[512,512]{1,0:T(8,128)(2,1)S(1)} custom-call(s32[3]{0:T(128)S(1)} %pad_add_fusion.place_ref, bf16[256,4096]{1,0:T(8,128)(2,1)S(1)} %copy-done, bf16[128,1024]{1,0:T(8,128)(2,1)S(1)} %collective-permute-done.1.refs_1_, bf16[128,1024]{1,0:T(8,128)(2,1)S(1)} %collective-permute-done.2.refs_2_, ...), custom_call_target="tpu_custom_call" | custom-call | flops 536870912 | bytes 3145728 | tf_op jit(solution)/shard_map/project/pallas_call | solution.py:271
  59.7 1.9 %collective-permute-start.5 = (bf16[512,512]{1,0:T(8,128)(2,1)S(1)}, bf16[512,512]{1,0:T(8,128)(2,1)S(1)}, u32[]{:S(2)}, u32[]{:S(2)}) collective-permute-start(bf16[512,512]{1,0:T(8,128)(2,1)S(1)} %project.8), channel_id=1, source_target_pairs={{0,2},{2,0},{1,3},{3,1},{4,6},{6,4},{5,7},{7,5},{8,10},{10,8},{9,1... | collective-permute-start | bytes 1572872 | tf_op jit(solution)/shard_map/ppermute | solution.py:92
  62.3 2.7 %project.10 = f32[512,512]{1,0:T(8,128)S(1)} custom-call(s32[3]{0:T(128)S(1)} %pad_add_fusion.place_ref, bf16[256,4096]{1,0:T(8,128)(2,1)S(1)} %copy-done, bf16[128,1024]{1,0:T(8,128)(2,1)S(1)} %collective-permute-done.8.refs_1_, bf16[128,1024]{1,0:T(8,128)(2,1)S(1)} %collective-permute-done.9.refs_2_, ...), custom_call_target="tpu_custom_call" | custom-call | flops 536870912 | bytes 3145728 | tf_op jit(solution)/shard_map/project/pallas_call | solution.py:271
  65.0 2.7 %project.7 = f32[512,512]{1,0:T(8,128)S(1)} custom-call(s32[3]{0:T(128)S(1)} %pad_add_fusion.place_ref, bf16[256,4096]{1,0:T(8,128)(2,1)S(1)} %copy-done, bf16[128,1024]{1,0:T(8,128)(2,1)S(1)} %collective-permute-done.1.refs_1_, bf16[128,1024]{1,0:T(8,128)(2,1)S(1)} %collective-permute-done.2.refs_2_, bf16[128,1024]{1,0:T(8,128)(2,1)S(1)} %collective-permute-done.3.refs_3_, ...), custom_call_target="tpu_custom_call" | custom-call | flops 536870912 | bytes 3145728 | tf_op jit(solution)/shard_map/project/pallas_call | solution.py:271
  67.7 2.0 %collective-permute-done.12 = bf16[512,512]{1,0:T(8,128)(2,1)S(1)} collective-permute-done((bf16[512,512]{1,0:T(8,128)(2,1)S(1)}, bf16[512,512]{1,0:T(8,128)(2,1)S(1)}, u32[]{:S(2)}, u32[]{:S(2)}) %collective-permute-start.12) | collective-permute-done | bytes 524320 | tf_op jit(solution)/shard_map/ppermute | solution.py:92
  69.7 0.2 convert_add_fusion
  69.8 0.0 copy-start.1
  69.9 0.0 copy-start.7
  69.9 5.6 %collective-permute-start.13 = (bf16[256,512]{1,0:T(8,128)(2,1)S(1)}, bf16[256,512]{1,0:T(8,128)(2,1)S(1)}, u32[]{:S(2)}, u32[]{:S(2)}) collective-permute-start(bf16[256,512]{1,0:T(8,128)(2,1)S(1)} %slice.56), channel_id=1, source_target_pairs={{0,4},{4,0},{8,12},{12,8},{1,5},{5,1},{9,13},{13,9},{2,6},{6,2},{1... | collective-permute-start | bytes 786440 | tf_op jit(solution)/shard_map/ppermute | solution.py:96
  75.5 27.6 %collective-permute-done.5 = bf16[512,512]{1,0:T(8,128)(2,1)S(1)} collective-permute-done((bf16[512,512]{1,0:T(8,128)(2,1)S(1)}, bf16[512,512]{1,0:T(8,128)(2,1)S(1)}, u32[]{:S(2)}, u32[]{:S(2)}) %collective-permute-start.5) | collective-permute-done | bytes 524320 | tf_op jit(solution)/shard_map/ppermute | solution.py:92
  103.1 0.2 convert_add_fusion.1
  103.3 5.5 %collective-permute-start.6 = (bf16[256,512]{1,0:T(8,128)(2,1)S(1)}, bf16[256,512]{1,0:T(8,128)(2,1)S(1)}, u32[]{:S(2)}, u32[]{:S(2)}) collective-permute-start(bf16[256,512]{1,0:T(8,128)(2,1)S(1)} %slice.57), channel_id=1, source_target_pairs={{0,4},{4,0},{8,12},{12,8},{1,5},{5,1},{9,13},{13,9},{2,6},{6,2},{1... | collective-permute-start | bytes 786440 | tf_op jit(solution)/shard_map/ppermute | solution.py:96
  108.8 0.0 collective-permute-done.refs_1_
  108.8 20.1 %prefix_attend.1 = (f32[128,8192]{1,0:T(8,128)}, f32[8,8192]{1,0:T(8,128)S(1)}) custom-call(s32[3]{0:T(128)S(1)} %pad_add_fusion.place_ref, s32[8]{0:T(128)S(1)} %bitcast.27, bf16[8192,128]{1,0:T(8,128)(2,1)S(1)} %bitcast.21, bf16[8,128,512]{2,1,0:T(8,128)(2,1)S(1)} %get-tuple-element.15.refs_0_, bf16[8,128,512]{2,1,0:T(8,128)(2,1)S(1)} %collective-permute-done.refs_1_), custom_call_target="tpu_custom_call" | custom-call | flops 8589934592 | bytes 6291456 | tf_op jit(solution)/shard_map/prefix_attend/pallas_call | solution.py:336
  128.9 0.0 collective-permute-done.13
  128.9 0.1 slice_add_fusion
  129.0 2.0 %collective-permute-start.14 = (bf16[128,512]{1,0:T(8,128)(2,1)S(1)}, bf16[128,512]{1,0:T(8,128)(2,1)S(1)}, u32[]{:S(2)}, u32[]{:S(2)}) collective-permute-start(bf16[128,512]{1,0:T(8,128)(2,1)S(1)} %slice.58), channel_id=1, source_target_pairs={{0,8},{4,12},{8,0},{12,4},{1,9},{5,13},{9,1},{13,5},{2,10},{6,14},... | collective-permute-start | bytes 393224 | tf_op jit(solution)/shard_map/ppermute | solution.py:96
  131.0 0.1 slice_add_fusion.1
  131.1 1.0 collective-permute-start.7
  132.2 9.1 %collective-permute-done.14 = bf16[128,512]{1,0:T(8,128)(2,1)S(1)} collective-permute-done((bf16[128,512]{1,0:T(8,128)(2,1)S(1)}, bf16[128,512]{1,0:T(8,128)(2,1)S(1)}, u32[]{:S(2)}, u32[]{:S(2)}) %collective-permute-start.14) | collective-permute-done | bytes 131104 | tf_op jit(solution)/shard_map/ppermute | solution.py:96
  141.3 1.9 %collective-permute-done.7 = bf16[128,512]{1,0:T(8,128)(2,1)S(1)} collective-permute-done((bf16[128,512]{1,0:T(8,128)(2,1)S(1)}, bf16[128,512]{1,0:T(8,128)(2,1)S(1)}, u32[]{:S(2)}, u32[]{:S(2)}) %collective-permute-start.7) | collective-permute-done | bytes 131104 | tf_op jit(solution)/shard_map/ppermute | solution.py:96
  143.3 8.0 %fresh_attend.2.rest_0_ = bf16[8192,128]{1,0:T(8,128)(2,1)} custom-call(s32[1]{0:T(128)S(6)} %copy.13.length_ref, bf16[8192,128]{1,0:T(8,128)(2,1)S(1)} %bitcast.22, f32[128,8192]{1,0:T(8,128)} %get-tuple-element.17.acc_ref, f32[8,8192]{1,0:T(8,128)S(1)} %get-tuple-element.18.stat_ref, bf16[128,512]{1,0:T(8,128)(2,1)S(1)} %fusion.1.fresh_ref), custom_call_target="tpu_custom_call" | custom-call | flops 536870912 | bytes 4194304 | tf_op jit(solution)/shard_map/fresh_attend/pallas_call | solution.py:419
  151.3 8.4 %fresh_attend.3 = bf16[8192,128]{1,0:T(8,128)(2,1)} custom-call(s32[1]{0:T(128)S(6)} %copy.13.length_ref, bf16[8192,128]{1,0:T(8,128)(2,1)S(1)} %bitcast.23, f32[128,8192]{1,0:T(8,128)} %get-tuple-element.17.acc_ref, f32[8,8192]{1,0:T(8,128)S(1)} %get-tuple-element.18.stat_ref, ...), custom_call_target="tpu_custom_call", output_to_operand_aliasing={{}: (5, {})} | custom-call | flops 1073741824 | bytes 4194304 | tf_op jit(solution)/shard_map/fresh_attend/pallas_call | solution.py:419
  (24 shorter events, 0.2 us)
Async XLA Ops:
  0.0 12.8 %copy-start.2 = (bf16[8,128,4,1,256]{4,2,3,1,0:T(4,128)(2,1)S(1)}, bf16[8,128,4,1,256]{4,2,3,1,0:T(4,128)(2,1)}, u32[]{:S(2)}) copy-start(bf16[8,128,4,1,256]{4,2,3,1,0:T(4,128)(2,1)} %param.11) | copy-start | bytes 6291460
  2.7 19.4 %collective-permute-start.8 = (bf16[128,1024]{1,0:T(8,128)(2,1)}, bf16[128,1024]{1,0:T(8,128)(2,1)S(1)}, u32[]{:S(2)}, u32[]{:S(2)}) collective-permute-start(bf16[128,1024]{1,0:T(8,128)(2,1)} %get-tuple-element.24), channel_id=1, source_target_pairs={{0,8},{4,12},{8,0},{12,4},{1,9},{5,13},{9,1},{13,5},{2,10},{6,14},... | collective-permute-start | bytes 786440 | tf_op jit(solution)/shard_map/ppermute | solution.py:96
  6.7 18.9 %collective-permute-start.9 = (bf16[128,1024]{1,0:T(8,128)(2,1)}, bf16[128,1024]{1,0:T(8,128)(2,1)S(1)}, u32[]{:S(2)}, u32[]{:S(2)}) collective-permute-start(bf16[128,1024]{1,0:T(8,128)(2,1)} %get-tuple-element.23), channel_id=1, source_target_pairs={{0,4},{4,0},{8,12},{12,8},{1,5},{5,1},{9,13},{13,9},{2,6},{6,2},{1... | collective-permute-start | bytes 786440 | tf_op jit(solution)/shard_map/ppermute | solution.py:96
  8.3 18.5 %collective-permute-start.10 = (bf16[128,1024]{1,0:T(8,128)(2,1)}, bf16[128,1024]{1,0:T(8,128)(2,1)S(1)}, u32[]{:S(2)}, u32[]{:S(2)}) collective-permute-start(bf16[128,1024]{1,0:T(8,128)(2,1)} %get-tuple-element.22), channel_id=1, source_target_pairs={{0,12},{4,8},{8,4},{12,0},{1,13},{5,9},{9,5},{13,1},{2,14},{6,10},... | collective-permute-start | bytes 786440 | tf_op jit(solution)/shard_map/ppermute | solution.py:96
  8.3 39.5 %collective-permute-start.1 = (bf16[128,1024]{1,0:T(8,128)(2,1)}, bf16[128,1024]{1,0:T(8,128)(2,1)S(1)}, u32[]{:S(2)}, u32[]{:S(2)}) collective-permute-start(bf16[128,1024]{1,0:T(8,128)(2,1)} %get-tuple-element.26), channel_id=1, source_target_pairs={{0,8},{4,12},{8,0},{12,4},{1,9},{5,13},{9,1},{13,5},{2,10},{6,14},... | collective-permute-start | bytes 786440 | tf_op jit(solution)/shard_map/ppermute | solution.py:96
  10.2 37.6 %collective-permute-start.2 = (bf16[128,1024]{1,0:T(8,128)(2,1)}, bf16[128,1024]{1,0:T(8,128)(2,1)S(1)}, u32[]{:S(2)}, u32[]{:S(2)}) collective-permute-start(bf16[128,1024]{1,0:T(8,128)(2,1)} %get-tuple-element.25), channel_id=1, source_target_pairs={{0,4},{4,0},{8,12},{12,8},{1,5},{5,1},{9,13},{13,9},{2,6},{6,2},{1... | collective-permute-start | bytes 786440 | tf_op jit(solution)/shard_map/ppermute | solution.py:96
  12.7 3.2 %copy-start.3 = (bf16[1,1,1024,4,2,128]{5,4,3,2,1,0:T(2,128)(2,1)S(1)}, bf16[1,1,1024,4,2,128]{5,4,3,2,1,0:T(2,128)(2,1)}, u32[]{:S(2)}) copy-start(bf16[1,1,1024,4,2,128]{5,4,3,2,1,0:T(2,128)(2,1)} %param.8) | copy-start | bytes 6291460
  14.9 1.0 copy-start.5
  15.9 1.6 copy-start.4
  17.5 4.6 %copy-start.8 = (bf16[128,1024]{1,0:T(8,128)(2,1)S(1)}, bf16[128,1024]{1,0:T(8,128)(2,1)}, u32[]{:S(2)}) copy-start(bf16[128,1024]{1,0:T(8,128)(2,1)} %get-tuple-element.21) | copy-start | bytes 786436
  17.5 9.3 %copy-start = (bf16[256,4096]{1,0:T(8,128)(2,1)S(1)}, bf16[256,4096]{1,0:T(8,128)(2,1)}, u32[]{:S(2)}) copy-start(bf16[256,4096]{1,0:T(8,128)(2,1)} %refs_0_.11) | copy-start | bytes 6291460
  22.1 25.7 %collective-permute-start.3 = (bf16[128,1024]{1,0:T(8,128)(2,1)S(1)}, bf16[128,1024]{1,0:T(8,128)(2,1)S(1)}, u32[]{:S(2)}, u32[]{:S(2)}) collective-permute-start(bf16[128,1024]{1,0:T(8,128)(2,1)S(1)} %copy-done.8), channel_id=1, source_target_pairs={{0,12},{4,8},{8,4},{12,0},{1,13},{5,9},{9,5},{13,1},{2,14},{6,10},... | collective-permute-start | bytes 786440 | tf_op jit(solution)/shard_map/ppermute | solution.py:96
  31.1 21.1 %collective-permute-start.11 = (bf16[512,1024]{1,0:T(8,128)(2,1)S(1)}, bf16[512,1024]{1,0:T(8,128)(2,1)S(1)}, u32[]{:S(2)}, u32[]{:S(2)}) collective-permute-start(bf16[512,1024]{1,0:T(8,128)(2,1)S(1)} %project.9), channel_id=1, source_target_pairs={{0,1},{1,0},{2,3},{3,2},{4,5},{5,4},{6,7},{7,6},{8,9},{9,8},{10,11... | collective-permute-start | bytes 3145736 | tf_op jit(solution)/shard_map/ppermute | solution.py:92
  52.1 4.7 %copy-start.6 = (bf16[8,128,512]{2,1,0:T(8,128)(2,1)S(1)}, bf16[8,128,512]{2,1,0:T(8,128)(2,1)}, u32[]{:S(2)}) copy-start(bf16[8,128,512]{2,1,0:T(8,128)(2,1)} %copy-done.5) | copy-start | bytes 3145732
  52.1 4.9 %collective-permute-start.4 = (bf16[512,1024]{1,0:T(8,128)(2,1)S(1)}, bf16[512,1024]{1,0:T(8,128)(2,1)S(1)}, u32[]{:S(2)}, u32[]{:S(2)}) collective-permute-start(bf16[512,1024]{1,0:T(8,128)(2,1)S(1)} %project.6), channel_id=1, source_target_pairs={{0,1},{1,0},{2,3},{3,2},{4,5},{5,4},{6,7},{7,6},{8,9},{9,8},{10,11... | collective-permute-start | bytes 3145736 | tf_op jit(solution)/shard_map/ppermute | solution.py:92
  54.9 14.8 %collective-permute-start.12 = (bf16[512,512]{1,0:T(8,128)(2,1)S(1)}, bf16[512,512]{1,0:T(8,128)(2,1)S(1)}, u32[]{:S(2)}, u32[]{:S(2)}) collective-permute-start(bf16[512,512]{1,0:T(8,128)(2,1)S(1)} %project.11), channel_id=1, source_target_pairs={{0,2},{2,0},{1,3},{3,1},{4,6},{6,4},{5,7},{7,5},{8,10},{10,8},{9,1... | collective-permute-start | bytes 1572872 | tf_op jit(solution)/shard_map/ppermute | solution.py:92
  56.8 52.0 %collective-permute-start = (bf16[8,128,512]{2,1,0:T(8,128)(2,1)S(1)}, bf16[8,128,512]{2,1,0:T(8,128)(2,1)S(1)}, u32[]{:S(2)}, u32[]{:S(2)}) collective-permute-start(bf16[8,128,512]{2,1,0:T(8,128)(2,1)S(1)} %copy-done.6), channel_id=1, source_target_pairs={{0,2},{2,0},{1,3},{3,1},{4,6},{6,4},{5,7},{7,5},{8,10},{10,8},{9,1... | collective-permute-start | bytes 3145736 | tf_op jit(solution)/shard_map/ppermute | solution.py:92
  59.7 43.4 %collective-permute-start.5 = (bf16[512,512]{1,0:T(8,128)(2,1)S(1)}, bf16[512,512]{1,0:T(8,128)(2,1)S(1)}, u32[]{:S(2)}, u32[]{:S(2)}) collective-permute-start(bf16[512,512]{1,0:T(8,128)(2,1)S(1)} %project.8), channel_id=1, source_target_pairs={{0,2},{2,0},{1,3},{3,1},{4,6},{6,4},{5,7},{7,5},{8,10},{10,8},{9,1... | collective-permute-start | bytes 1572872 | tf_op jit(solution)/shard_map/ppermute | solution.py:92
  69.8 38.9 %copy-start.1 = (bf16[256,2,1,2048]{3,1,2,0:T(2,128)(2,1)S(1)}, bf16[256,2,1,2048]{3,1,2,0:T(2,128)(2,1)}, u32[]{:S(2)}) copy-start(bf16[256,2,1,2048]{3,1,2,0:T(2,128)(2,1)} %param.10) | copy-start | bytes 6291460
  69.9 38.9 %copy-start.7 = (s32[1,8]{1,0:T(1,128)S(1)}, s32[1,8]{1,0:T(1,128)}, u32[]{:S(2)}) copy-start(s32[1,8]{1,0:T(1,128)} %param.12) | copy-start | bytes 100
  69.9 59.0 %collective-permute-start.13 = (bf16[256,512]{1,0:T(8,128)(2,1)S(1)}, bf16[256,512]{1,0:T(8,128)(2,1)S(1)}, u32[]{:S(2)}, u32[]{:S(2)}) collective-permute-start(bf16[256,512]{1,0:T(8,128)(2,1)S(1)} %slice.56), channel_id=1, source_target_pairs={{0,4},{4,0},{8,12},{12,8},{1,5},{5,1},{9,13},{13,9},{2,6},{6,2},{1... | collective-permute-start | bytes 786440 | tf_op jit(solution)/shard_map/ppermute | solution.py:96
  103.3 27.7 %collective-permute-start.6 = (bf16[256,512]{1,0:T(8,128)(2,1)S(1)}, bf16[256,512]{1,0:T(8,128)(2,1)S(1)}, u32[]{:S(2)}, u32[]{:S(2)}) collective-permute-start(bf16[256,512]{1,0:T(8,128)(2,1)S(1)} %slice.57), channel_id=1, source_target_pairs={{0,4},{4,0},{8,12},{12,8},{1,5},{5,1},{9,13},{13,9},{2,6},{6,2},{1... | collective-permute-start | bytes 786440 | tf_op jit(solution)/shard_map/ppermute | solution.py:96
  129.0 12.3 %collective-permute-start.14 = (bf16[128,512]{1,0:T(8,128)(2,1)S(1)}, bf16[128,512]{1,0:T(8,128)(2,1)S(1)}, u32[]{:S(2)}, u32[]{:S(2)}) collective-permute-start(bf16[128,512]{1,0:T(8,128)(2,1)S(1)} %slice.58), channel_id=1, source_target_pairs={{0,8},{4,12},{8,0},{12,4},{1,9},{5,13},{9,1},{13,5},{2,10},{6,14},... | collective-permute-start | bytes 393224 | tf_op jit(solution)/shard_map/ppermute | solution.py:96
  131.1 12.1 %collective-permute-start.7 = (bf16[128,512]{1,0:T(8,128)(2,1)S(1)}, bf16[128,512]{1,0:T(8,128)(2,1)S(1)}, u32[]{:S(2)}, u32[]{:S(2)}) collective-permute-start(bf16[128,512]{1,0:T(8,128)(2,1)S(1)} %slice.59), channel_id=1, source_target_pairs={{0,8},{4,12},{8,0},{12,4},{1,9},{5,13},{9,1},{13,5},{2,10},{6,14},... | collective-permute-start | bytes 393224 | tf_op jit(solution)/shard_map/ppermute | solution.py:96

commit v4 on v3

--- a/solution.py
+++ b/solution.py
@@ -10,6 +10,7 @@
 
 CHUNKS = 2
 VMEM_BYTES = 48 * 1024 * 1024
+LONG = pl.CostEstimate(flops=10**11, bytes_accessed=1, transcendentals=0)
 
 
 def attend_head(query_rows, prefix, fresh_rows, length):
@@ -172,9 +173,7 @@
         out_shape=jax.ShapeDtypeStruct((head_count, ctx_count, depth, columns), jnp.bfloat16),
         scratch_shapes=[pltpu.VMEM((rows * slots, width), jnp.float32)],
         compiler_params=params(),
-        cost_estimate=pl.CostEstimate(
-            flops=0, bytes_accessed=8 * depth * slots * width, transcendentals=0
-        ),
+        cost_estimate=LONG,
         name="arrange_weights",
     )(*views)
 
@@ -218,16 +217,13 @@
         ),
         out_shape=[jax.ShapeDtypeStruct((blocks, length, columns), jnp.bfloat16)] * ctx_count,
         compiler_params=params(),
-        cost_estimate=pl.CostEstimate(
-            flops=0, bytes_accessed=4 * blocks * length * slots * width, transcendentals=0
-        ),
+        cost_estimate=LONG,
         name="arrange_pool",
     )(place, view)
 
 
-def project_kernel(parts, has_term, place_ref, *refs):
-    token_refs, weight_ref = refs[:parts], refs[parts]
-    out_ref, stacked = refs[-2], refs[-1]
+def project_kernel(place_ref, *refs):
+    token_refs, (weight_ref, out_ref, stacked) = refs[:-3], refs[-3:]
     rows = token_refs[0].shape[0]
 
     @pl.when(pl.program_id(0) == 0)
@@ -235,63 +231,91 @@
         for index, token_ref in enumerate(token_refs):
             stacked[index * rows : (index + 1) * rows, :] = token_ref[...]
 
-    total = jnp.dot(stacked[...], weight_ref[0, 0], preferred_element_type=jnp.float32)
-    if has_term:
-        total = total + refs[parts + 1][...].astype(jnp.float32)
-    out_ref[...] = total.astype(out_ref.dtype)
-
-
-def project(place, tokens, received, weights, chunk, head_step, ctx_steps, term, out_dtype):
+    out_ref[...] = jnp.dot(
+        stacked[...], weight_ref[0, 0], preferred_element_type=jnp.float32
+    ).astype(out_ref.dtype)
+
+
+def project(place, tokens, received, weights, chunk, head_step, out_dtype):
     head_count, ctx_count, depth, width = weights.shape
     rows = tokens.shape[0] // CHUNKS
     row_total = rows * (1 + len(received))
-    tile = min(256, width)
-    tiles = width // tile
-    first, last = ctx_steps
-    in_specs = [pl.BlockSpec((rows, depth), lambda j, place: (chunk, place[0]))]
-    in_specs += [pl.BlockSpec((rows, depth), lambda j, place: (0, 0)) for _ in received]
-    in_specs += [
-        pl.BlockSpec(
-            (1, 1, depth, tile),
-            lambda j, place: (
-                lax.rem(place[2] + head_step, head_count),
-                lax.rem(place[1] + first + j // tiles, ctx_count),
-                0,
-                j % tiles,
-            ),
-        )
-    ]
-    operands = [place, tokens, *received, weights]
-    if term is not None:
-        in_specs.append(
-            pl.BlockSpec((row_total, tile), lambda j, place: (0, first * tiles + j))
-        )
-        operands.append(term)
-    columns = (last - first) * width
+    columns = ctx_count * width
     return pl.pallas_call(
-        functools.partial(project_kernel, 1 + len(received), term is not None),
+        project_kernel,
         grid_spec=pltpu.PrefetchScalarGridSpec(
             num_scalar_prefetch=1,
-            grid=(columns // tile,),
-            in_specs=in_specs,
-            out_specs=pl.BlockSpec((row_total, tile), lambda j, place: (0, j)),
+            grid=(ctx_count,),
+            in_specs=[pl.BlockSpec((rows, depth), lambda j, place: (chunk, place[0]))]
+            + [pl.BlockSpec((rows, depth), lambda j, place: (0, 0)) for _ in received]
+            + [
+                pl.BlockSpec(
+                    (1, 1, depth, width),
+                    lambda j, place: (
+                        lax.rem(place[2] + head_step, head_count),
+                        lax.rem(place[1] + j, ctx_count),
+                        0,
+                        0,
+                    ),
+                )
+            ],
+            out_specs=pl.BlockSpec((row_total, width), lambda j, place: (0, j)),
             scratch_shapes=[pltpu.VMEM((row_total, depth), tokens.dtype)],
         ),
         out_shape=jax.ShapeDtypeStruct((row_total, columns), out_dtype),
         compiler_params=params(),
-        cost_estimate=pl.CostEstimate(
-            flops=2 * row_total * depth * columns,
-            bytes_accessed=2 * (depth * (columns + row_total) + 2 * row_total * columns),
-            transcendentals=0,
+        cost_estimate=LONG,
+        name="project",
+    )(place, tokens, *received, weights)
+
+
+def pick_kernel(heads, ctx_count, place_ref, table_ref, *refs):
+    pool_refs, (keys, values) = refs[:ctx_count], refs[ctx_count:]
+    blocks, length, columns = pool_refs[0].shape
+    wide = columns // 2
+    width = wide // heads
+    values[wide:, :] = jnp.ones_like(values[wide:, :])
+    for at in range(table_ref.shape[0]):
+        entry = table_ref[at]
+        here = slice(at * length, (at + 1) * length)
+        step = lax.rem(place_ref[1] - entry // blocks + ctx_count, ctx_count)
+        for ctx_step, pool_ref in enumerate(pool_refs):
+
+            @pl.when(step == ctx_step)
+            def _():
+                block = pool_ref[entry % blocks]
+                keys[here, :] = block[:, :wide]
+                for head in range(heads):
+                    low = wide + head * length
+                    values[head * width : (head + 1) * width, here] = block[:, low : low + length]
+
+
+def pick_blocks(place, table, pools, heads):
+    length, columns = pools[0].shape[1:]
+    count = table.shape[0] * length
+    wide = columns // 2
+    return pl.pallas_call(
+        functools.partial(pick_kernel, heads, len(pools)),
+        grid_spec=pltpu.PrefetchScalarGridSpec(
+            num_scalar_prefetch=2,
+            grid=(1,),
+            in_specs=[pl.BlockSpec(p.shape, lambda i, *_: (0, 0, 0)) for p in pools],
+            out_specs=[
+                pl.BlockSpec((count, wide), lambda i, *_: (0, 0)),
+                pl.BlockSpec((wide + 16, count), lambda i, *_: (0, 0)),
+            ],
         ),
-        name="project",
-    )(*operands)
-
-
-def prefix_kernel(scale, heads, ctx_count, place_ref, table_ref, query_ref, *refs):
-    pool_refs = refs[:ctx_count]
-    acc_ref, stat_ref, keys, values, mask = refs[ctx_count:]
-    blocks, length, columns = pool_refs[0].shape
+        out_shape=[
+            jax.ShapeDtypeStruct((count, wide), jnp.bfloat16),
+            jax.ShapeDtypeStruct((wide + 16, count), jnp.bfloat16),
+        ],
+        compiler_params=params(),
+        cost_estimate=LONG,
+        name="pick_blocks",
+    )(place, table, *pools)
+
+
+def prefix_kernel(scale, heads, query_ref, keys, values, acc_ref, stat_ref, mask):
     rows, width = query_ref.shape
     part_rows = mask.shape[0]
     wide = heads * width
@@ -299,22 +323,6 @@
     @pl.when(pl.program_id(0) == 0)
     def _():
         mask[...] = head_mask(mask.shape, heads)
-        values[wide:, :] = jnp.ones_like(values[wide:, :])
-        for at in range(table_ref.shape[0]):
-            entry = table_ref[at]
-            here = slice(at * length, (at + 1) * length)
-            step = lax.rem(place_ref[1] - entry // blocks + ctx_count, ctx_count)
-            for ctx_step, pool_ref in enumerate(pool_refs):
-
-                @pl.when(step == ctx_step)
-                def _():
-                    block = pool_ref[entry % blocks]
-                    keys[here, :] = block[:, :wide]
-                    for head in range(heads):
-                        low = wide + head * length
-                        values[head * width : (head + 1) * width, here] = block[
-                            :, low : low + length
-                        ]
 
     for part in range(rows // part_rows):
         here = slice(part * part_rows, (part + 1) * part_rows)
@@ -327,41 +335,33 @@
         stat_ref[half:, here] = jnp.broadcast_to(mixed[wide : wide + 1], (half, part_rows))
 
 
-def prefix_attend(place, table, query_rows, pools, scale, heads):
-    row_total, width = query_rows.shape
+def prefix_attend(query_rows, keys, values, chunk, scale, heads):
+    all_rows, width = query_rows.shape
+    row_total = all_rows // CHUNKS
     rows = min(1024, row_total)
-    length, columns = pools[0].shape[1:]
-    key_count = table.shape[0] * length
-    wide = columns // 2
+    steps = row_total // rows
+    key_count, wide = keys.shape
     return pl.pallas_call(
-        functools.partial(prefix_kernel, scale, heads, len(pools)),
-        grid_spec=pltpu.PrefetchScalarGridSpec(
-            num_scalar_prefetch=2,
-            grid=(row_total // rows,),
-            in_specs=[pl.BlockSpec((rows, width), lambda i, *_: (i, 0))]
-            + [pl.BlockSpec(p.shape, lambda i, *_: (0, 0, 0)) for p in pools],
-            out_specs=[
-                pl.BlockSpec((width, rows), lambda i, *_: (0, i)),
-                pl.BlockSpec((8, rows), lambda i, *_: (0, i)),
-            ],
-            scratch_shapes=[
-                pltpu.VMEM((key_count, wide), jnp.bfloat16),
-                pltpu.VMEM((wide + 16, key_count), jnp.bfloat16),
-                pltpu.VMEM((min(256, rows), wide), jnp.bfloat16),
-            ],
-        ),
+        functools.partial(prefix_kernel, scale, heads),
+        grid=(steps,),
+        in_specs=[
+            pl.BlockSpec((rows, width), lambda i: (chunk * steps + i, 0)),
+            pl.BlockSpec(keys.shape, lambda i: (0, 0)),
+            pl.BlockSpec(values.shape, lambda i: (0, 0)),
+        ],
+        out_specs=[
+            pl.BlockSpec((width, rows), lambda i: (0, i)),
+            pl.BlockSpec((8, rows), lambda i: (0, i)),
+        ],
         out_shape=[
             jax.ShapeDtypeStruct((width, row_total), jnp.float32),
             jax.ShapeDtypeStruct((8, row_total), jnp.float32),
         ],
+        scratch_shapes=[pltpu.VMEM((min(512, rows), wide), jnp.bfloat16)],
         compiler_params=params(),
-        cost_estimate=pl.CostEstimate(
-            flops=2 * row_total * key_count * columns,
-            bytes_accessed=row_total * width * 6,
-            transcendentals=row_total * key_count,
-        ),
+        cost_estimate=LONG,
         name="prefix_attend",
-    )(place, table, query_rows, *pools)
+    )(query_rows, keys, values)
 
 
 def fresh_kernel(
@@ -378,36 +378,38 @@
         values[wide:, :] = jnp.ones_like(values[wide:, :])
         values[:wide, :] = fresh_ref[:, wide:].astype(jnp.float32).T.astype(jnp.bfloat16)
 
-    query_block = jnp.concatenate([query_ref[...]] * heads, 1) * mask[...]
-    scores = dot_queries(fresh_ref[:, :wide], query_block) * scale
-    token = first_row + step * (rows // per_token)
-    row = lax.broadcasted_iota(jnp.int32, (1, rows), 1)
-    token = token + (
-        row // per_token if per_token & (per_token - 1) else row >> (per_token.bit_length() - 1)
-    )
-    key_at = lax.broadcasted_iota(jnp.int32, scores.shape, 0)
-    scores = jnp.where(key_at <= token, scores, -jnp.inf)
+    part_rows = mask.shape[0]
     half = stat_ref.shape[0] // 2
-    old_max, old_total = stat_ref[:1, :], stat_ref[half : half + 1, :]
-    row_max, weights = softmax_parts(scores, old_max)
-    fade = jnp.exp2(old_max - row_max)
-    mixed = jnp.dot(values[...], weights, preferred_element_type=jnp.float32)
-    row_total = old_total * fade + mixed[wide : wide + 1]
-    share = jnp.where(token < length_ref[0], 1.0 / row_total, 0.0)
-    result = acc_ref[...] * (fade * share) + own_head(mixed, heads, width) * share
-    out_ref[...] = result.T.astype(out_ref.dtype)
+    for part in range(rows // part_rows):
+        here = slice(part * part_rows, (part + 1) * part_rows)
+        query_block = jnp.concatenate([query_ref[here, :]] * heads, 1) * mask[...]
+        scores = dot_queries(fresh_ref[:, :wide], query_block) * scale
+        row = part * part_rows + lax.broadcasted_iota(jnp.int32, (1, part_rows), 1)
+        token = first_row + step * (rows // per_token) + (
+            row // per_token if per_token & (per_token - 1) else row >> (per_token.bit_length() - 1)
+        )
+        key_at = lax.broadcasted_iota(jnp.int32, scores.shape, 0)
+        scores = jnp.where(key_at <= token, scores, -jnp.inf)
+        old_max, old_total = stat_ref[:1, here], stat_ref[half : half + 1, here]
+        row_max, weights = softmax_parts(scores, old_max)
+        fade = jnp.exp2(old_max - row_max)
+        mixed = jnp.dot(values[...], weights, preferred_element_type=jnp.float32)
+        row_total = old_total * fade + mixed[wide : wide + 1]
+        share = jnp.where(token < length_ref[0], 1.0 / row_total, 0.0)
+        result = acc_ref[:, here] * (fade * share) + own_head(mixed, heads, width) * share
+        out_ref[here, :] = result.T.astype(out_ref.dtype)
 
 
 def fresh_attend(length, query_rows, acc, stat, fresh, earlier, chunk, scale, heads, per_token):
     row_total, width = query_rows.shape
     chunk_rows = row_total // CHUNKS
-    rows = min(512, chunk_rows)
+    rows = min(1024, chunk_rows)
     steps = chunk_rows // rows
     block = pl.BlockSpec((rows, width), lambda i, length: (chunk * steps + i, 0))
     in_specs = [
         block,
-        pl.BlockSpec((width, rows), lambda i, length: (0, chunk * steps + i)),
-        pl.BlockSpec((stat.shape[0], rows), lambda i, length: (0, chunk * steps + i)),
+        pl.BlockSpec((width, rows), lambda i, length: (0, i)),
+        pl.BlockSpec((stat.shape[0], rows), lambda i, length: (0, i)),
         pl.BlockSpec(fresh.shape, lambda i, length: (0, 0)),
     ]
     operands = [length, query_rows, acc, stat, fresh]
@@ -427,17 +429,13 @@
             out_specs=block,
             scratch_shapes=[
                 pltpu.VMEM((heads * width + 16, fresh.shape[0]), jnp.bfloat16),
-                pltpu.VMEM((rows, heads * width), jnp.bfloat16),
+                pltpu.VMEM((min(512, rows), heads * width), jnp.bfloat16),
             ],
         ),
         out_shape=jax.ShapeDtypeStruct((row_total, width), jnp.bfloat16),
         input_output_aliases=aliases,
         compiler_params=params(),
-        cost_estimate=pl.CostEstimate(
-            flops=2 * chunk_rows * fresh.shape[0] * fresh.shape[1],
-            bytes_accessed=chunk_rows * width * 8,
-            transcendentals=chunk_rows * fresh.shape[0],
-        ),
+        cost_estimate=LONG,
         name="fresh_attend",
     )(*operands)
 
@@ -475,26 +473,37 @@
 
     query_rows = queries.reshape(token_count, heads, group, width)
     query_rows = query_rows.transpose(0, 2, 1, 3).reshape(-1, width)
-    acc, stat = prefix_attend(place, block_table[0], query_rows, pools, scale, heads)
-
+    keys = values = None
     fresh_parts = []
     result = None
     cols = weights.shape[3]
     for chunk in range(CHUNKS):
         call = functools.partial(project, place, tokens, received[chunk], weights, chunk)
-        term = None
-        for step in range(1, head_count):
-            part = shift(call(step, (0, ctx_count), None, jnp.bfloat16), "head", step)
-            term = part if term is None else term.astype(jnp.float32) + part.astype(jnp.float32)
-        sent = call(0, (1, ctx_count), term, jnp.bfloat16)
-        mine = call(0, (0, 1), term, jnp.float32)
-        for step in range(1, ctx_count):
-            part = sent[:, (step - 1) * cols : step * cols]
-            mine = mine + shift(part, "ctx", step).astype(jnp.float32)
+        terms = [
+            shift(call(step, jnp.bfloat16), "head", step).astype(jnp.float32)
+            for step in range(1, head_count)
+        ]
+        own = call(0, jnp.float32)
+        mine = sum(terms, own[:, :])
+        parts = [
+            mine[:, step * cols : (step + 1) * cols].astype(jnp.bfloat16)
+            for step in range(1, ctx_count)
+        ]
+        parts, pools, query_rows = lax.optimization_barrier((parts, pools, query_rows))
+        parts = [shift(part, "ctx", step + 1) for step, part in enumerate(parts)]
+        if keys is None:
+            keys, values = pick_blocks(place, block_table[0], pools, heads)
+        acc, stat = prefix_attend(query_rows, keys, values, chunk, scale, heads)
+        if chunk + 1 < CHUNKS:
+            acc, received[chunk + 1] = lax.optimization_barrier((acc, received[chunk + 1]))
+        parts, acc, stat = lax.optimization_barrier((parts, acc, stat))
+        mine = sum((part.astype(jnp.float32) for part in parts), mine[:, :cols])
         bit = 1
         while bit < batch_count:
             half = mine.shape[0] // 2
             part = trade(mine[half:].astype(jnp.bfloat16), "batch", bit)
+            if result is not None and bit == 1:
+                part, result = lax.optimization_barrier((part, result))
             mine = mine[:half] + part.astype(jnp.float32)
             bit *= 2
         fresh_parts.append(mine.astype(jnp.bfloat16))

time: 160 us -> 114 us (0.71)
  waiting for transfers between devices: 60.4 us -> 24.4 us
  Pallas kernels: 62.6 us -> 52.8 us
  other arithmetic: 0.63 us -> 2.47 us
    ppermute x5, waiting for transfers between devices: 29.6 us -> 7.68 us  [shift(): lax.ppermute(array, axis, [(i, (i + step) % count) for i in range(count)])]
    ppermute x10, waiting for transfers between devices: 30.8 us -> 16.7 us  [trade(): lax.ppermute(array, axis, [(i, i ^ bits) for i in range(lax.axis_size(axi...]
    pallas_call x7, Pallas kernels: 39.4 us -> 33.4 us  [the longest x2 16.6 us: prefix_attend(): pl.pallas_call(functools.partial(prefix_kernel, scale, heads), grid=(step...]
    pallas_call x2, Pallas kernels: 16.5 us -> 10.6 us  [fresh_attend(): pl.pallas_call(functools.partial(fresh_kernel, scale, heads, per_token, c...]
    ppermute x10, starting transfers between devices: 25.7 us -> 22.7 us  [trade(): lax.ppermute(array, axis, [(i, i ^ bits) for i in range(lax.axis_size(axi...]
    ppermute x5, starting transfers between devices: 4.13 us -> 6.78 us  [shift(): lax.ppermute(array, axis, [(i, (i + step) % count) for i in range(count)])]
    unnamed x18 -> x26, local copies, waits for them, and re-layouts: 2.59 us -> 0.06 us
    pallas_call x1, Pallas kernels: 2.11 us -> 4.14 us  [arrange_pool(): pl.pallas_call(functools.partial(pool_kernel, ctx_count, heads), grid_spe...]
  transfers between devices with their start and end apart: 15 -> 15, of which waited for: 7 -> 8; matrix products, arithmetic and copies ran while one was open for 0% -> 1% of each run, Pallas kernels for 29% -> 41%
where the time goes in v4:
time: 114 us
  Pallas kernels  52.8 us (46%)
  starting transfers between devices  29.5 us (26%)
  waiting for transfers between devices  24.4 us (21%)
  local copies, waits for them, and re-layouts  3.87 us (3%)
  other arithmetic  2.47 us (2%)
    ppermute x10, starting transfers between devices, trade(): lax.ppermute(array, axis, [(i, i ^ bits) for i in range(lax.axis_size(axi...  22.7 us
    ppermute x10, waiting for transfers between devices, trade(): lax.ppermute(array, axis, [(i, i ^ bits) for i in range(lax.axis_size(axi...  16.7 us
    pallas_call x2, Pallas kernels, prefix_attend(): pl.pallas_call(functools.partial(prefix_kernel, scale, heads), grid=(step...  16.6 us
    pallas_call x4, Pallas kernels, project(): pl.pallas_call(project_kernel, grid_spec=pltpu.PrefetchScalarGridSpec(num...  14.5 us
    pallas_call x2, Pallas kernels, fresh_attend(): pl.pallas_call(functools.partial(fresh_kernel, scale, heads, per_token, c...  10.6 us
    ppermute x5, waiting for transfers between devices, shift(): lax.ppermute(array, axis, [(i, (i + step) % count) for i in range(count)])  7.68 us
    ppermute x5, starting transfers between devices, shift(): lax.ppermute(array, axis, [(i, (i + step) % count) for i in range(count)])  6.78 us
    pallas_call x1, Pallas kernels, arrange_weights(): pl.pallas_call(functools.partial(weight_kernel, ctx_count, heads, head_co...  4.62 us
  transfers between devices with their start and end apart: 15, of which 8 were waited for; matrix products, arithmetic and copies ran while one was open for 1% of the time, Pallas kernels for 41%

profile of v4, /device:TPU:0, one launch (start us, length us, event | category | flops | bytes accessed | tf_op | source)
XLA Modules:
  0.0 114.0 jit_solution(9652039310263381913)
XLA Ops:
  0.0 2.7 %constant_dynamic-slice_fusion = (bf16[128,1024]{1,0:T(8,128)(2,1)}, bf16[128,1024]{1,0:T(8,128)(2,1)}, bf16[128,1024]{1,0:T(8,128)(2,1)}, bf16[128,1024]{1,0:T(...) fusion(bf16[256,4096]{1,0:T(8,128)(2,1)} %refs_0_.7, s32[]{:T(128)S(6)} %select_n.14, s32[]{:T(128)S(6)} %select_n.13, ...), kind=kLoop, calls=%fused_computation.17 | loop fusion | bytes 3145740 | tf_op jit(solution)/shard_map/dynamic_slice | solution.py:464
  2.7 4.0 %collective-permute-start = (bf16[128,1024]{1,0:T(8,128)(2,1)}, bf16[128,1024]{1,0:T(8,128)(2,1)}, u32[]{:S(2)}, u32[]{:S(2)}) collective-permute-start(bf16[128,1024]{1,0:T(8,128)(2,1)} %get-tuple-element.70), channel_id=1, source_target_pairs={{0,8},{4,12},{8,0},{12,4},{1,9},{5,13},{9,1},{13,5},{2,10},{6,14},... | collective-permute-start | bytes 786440 | tf_op jit(solution)/shard_map/ppermute | solution.py:97
  6.7 1.6 %collective-permute-start.1 = (bf16[128,1024]{1,0:T(8,128)(2,1)}, bf16[128,1024]{1,0:T(8,128)(2,1)}, u32[]{:S(2)}, u32[]{:S(2)}) collective-permute-start(bf16[128,1024]{1,0:T(8,128)(2,1)} %get-tuple-element.69), channel_id=1, source_target_pairs={{0,4},{4,0},{8,12},{12,8},{1,5},{5,1},{9,13},{13,9},{2,6},{6,2},{1... | collective-permute-start | bytes 786440 | tf_op jit(solution)/shard_map/ppermute | solution.py:97
  8.3 0.0 collective-permute-start.2
  8.3 0.1 pad_add_fusion.place_ref
  8.4 4.1 %arrange_pool.1 = (bf16[8,128,512]{2,1,0:T(8,128)(2,1)S(1)}, bf16[8,128,512]{2,1,0:T(8,128)(2,1)}) custom-call(s32[3]{0:T(128)S(1)} %pad_add_fusion.place_ref, bf16[8,128,8,128]{3,2,1,0:T(8,128)(2,1)S(1)} %bitcast.21), custom_call_target="tpu_custom_call" | custom-call | flops 99999997952 | bytes 1 | tf_op jit(solution)/shard_map/arrange_pool/pallas_call | solution.py:209
  12.5 1.7 %collective-permute-start.4 = (bf16[8,128,512]{2,1,0:T(8,128)(2,1)}, bf16[8,128,512]{2,1,0:T(8,128)(2,1)}, u32[]{:S(2)}, u32[]{:S(2)}) collective-permute-start(bf16[8,128,512]{2,1,0:T(8,128)(2,1)} %get-tuple-element.40), channel_id=1, source_target_pairs={{0,2},{2,0},{1,3},{3,1},{4,6},{6,4},{5,7},{7,5},{8,10},{10,8},{9,1... | collective-permute-start | bytes 3145736 | tf_op jit(solution)/shard_map/ppermute | solution.py:93
  14.2 1.7 %collective-permute-start.5 = (bf16[128,1024]{1,0:T(8,128)(2,1)}, bf16[128,1024]{1,0:T(8,128)(2,1)}, u32[]{:S(2)}, u32[]{:S(2)}) collective-permute-start(bf16[128,1024]{1,0:T(8,128)(2,1)} %get-tuple-element.67), channel_id=1, source_target_pairs={{0,8},{4,12},{8,0},{12,4},{1,9},{5,13},{9,1},{13,5},{2,10},{6,14},... | collective-permute-start | bytes 786440 | tf_op jit(solution)/shard_map/ppermute | solution.py:97
  15.9 4.6 %arrange_weights.1.refs_4_ = bf16[2,2,1024,512]{3,2,1,0:T(8,128)(2,1)} custom-call(bf16[1024,8,128]{2,1,0:T(8,128)(2,1)S(1)} %bitcast.22, bf16[1024,8,128]{2,1,0:T(8,128)(2,1)S(1)} %bitcast.23), custom_call_target="tpu_custom_call" | custom-call | flops 99999997952 | bytes 1 | tf_op jit(solution)/shard_map/arrange_weights/pallas_call | solution.py:168
  21.2 2.5 %collective-permute-start.6 = (bf16[128,1024]{1,0:T(8,128)(2,1)}, bf16[128,1024]{1,0:T(8,128)(2,1)}, u32[]{:S(2)}, u32[]{:S(2)}) collective-permute-start(bf16[128,1024]{1,0:T(8,128)(2,1)} %get-tuple-element.66), channel_id=1, source_target_pairs={{0,4},{4,0},{8,12},{12,8},{1,5},{5,1},{9,13},{13,9},{2,6},{6,2},{1... | collective-permute-start | bytes 786440 | tf_op jit(solution)/shard_map/ppermute | solution.py:97
  23.7 0.2 collective-permute-start.7
  24.0 2.9 %collective-permute-done.2.refs_3_ = bf16[128,1024]{1,0:T(8,128)(2,1)} collective-permute-done((bf16[128,1024]{1,0:T(8,128)(2,1)}, bf16[128,1024]{1,0:T(8,128)(2,1)}, u32[]{:S(2)}, u32[]{:S(2)}) %collective-permute-start.2) | collective-permute-done | bytes 262176 | tf_op jit(solution)/shard_map/ppermute | solution.py:97
  26.9 3.6 %project.5 = bf16[512,1024]{1,0:T(8,128)(2,1)S(1)} custom-call(s32[3]{0:T(128)S(1)} %pad_add_fusion.place_ref, bf16[256,4096]{1,0:T(8,128)(2,1)S(1)} %copy-done, bf16[128,1024]{1,0:T(8,128)(2,1)} %collective-permute-done.refs_1_, bf16[128,1024]{1,0:T(8,128)(2,1)} %collective-permute-done.1.refs_2_, bf16[128,1024]{1,0:T(8,128)(2,1)} %collective-permute-done.2.refs_3_, ...), custom_call_target="tpu_custom_call" | custom-call | flops 99999997952 | bytes 1 | tf_op jit(solution)/shard_map/project/pallas_call | solution.py:244
  30.5 0.1 collective-permute-start.3
  30.6 3.7 %project.4 = f32[512,1024]{1,0:T(8,128)S(1)} custom-call(s32[3]{0:T(128)S(1)} %pad_add_fusion.place_ref, bf16[256,4096]{1,0:T(8,128)(2,1)S(1)} %copy-done, bf16[128,1024]{1,0:T(8,128)(2,1)} %collective-permute-done.refs_1_, bf16[128,1024]{1,0:T(8,128)(2,1)} %collective-permute-done.1.refs_2_, bf16[128,1024]{1,0:T(8,128)(2,1)} %collective-permute-done.2.refs_3_, ...), custom_call_target="tpu_custom_call" | custom-call | flops 99999997952 | bytes 1 | tf_op jit(solution)/shard_map/project/pallas_call | solution.py:244
  34.2 0.0 copy-start.6
  34.3 0.5 convert_add_fusion.1
  34.7 0.0 copy-start.11
  34.7 1.0 slice.83
  35.7 1.5 %collective-permute-done.4.refs_1_ = bf16[8,128,512]{2,1,0:T(8,128)(2,1)} collective-permute-done((bf16[8,128,512]{2,1,0:T(8,128)(2,1)}, bf16[8,128,512]{2,1,0:T(8,128)(2,1)}, u32[]{:S(2)}, u32[]{:S(2)}) %collective-permute-start.4) | collective-permute-done | bytes 1048608 | tf_op jit(solution)/shard_map/ppermute | solution.py:93
  37.2 3.6 %collective-permute-start.10 = (bf16[512,512]{1,0:T(8,128)(2,1)}, bf16[512,512]{1,0:T(8,128)(2,1)}, u32[]{:S(2)}, u32[]{:S(2)}) collective-permute-start(bf16[512,512]{1,0:T(8,128)(2,1)} %slice.83), channel_id=1, source_target_pairs={{0,2},{2,0},{1,3},{3,1},{4,6},{6,4},{5,7},{7,5},{8,10},{10,8},{9,1... | collective-permute-start | bytes 1572872 | tf_op jit(solution)/shard_map/ppermute | solution.py:93
  40.7 2.3 %pick_blocks.1 = (bf16[1024,256]{1,0:T(8,128)(2,1)S(1)}, bf16[272,1024]{1,0:T(8,128)(2,1)S(1)}) custom-call(s32[3]{0:T(128)S(1)} %pad_add_fusion.place_ref, s32[8]{0:T(128)S(1)} %bitcast.28, bf16[8,128,512]{2,1,0:T(8,128)(2,1)S(1)} %get-tuple-element.42.refs_0_, bf16[8,128,512]{2,1,0:T(8,128)(2,1)} %collective-permute-done.4.refs_1_), custom_call_target="tpu_custom_call" | custom-call | flops 99999997952 | bytes 1 | tf_op jit(solution)/shard_map/pick_blocks/pallas_call | solution.py:297
  43.1 0.0 copy-start.12
  43.1 8.4 %prefix_attend.2 = (f32[128,4096]{1,0:T(8,128)S(1)}, f32[8,4096]{1,0:T(8,128)S(1)}) custom-call(bf16[8192,128]{1,0:T(8,128)(2,1)S(1)} %bitcast.24, bf16[1024,256]{1,0:T(8,128)(2,1)S(1)} %get-tuple-element.44.keys, bf16[272,1024]{1,0:T(8,128)(2,1)S(1)} %get-tuple-element.45.values), custom_call_target="tpu_custom_call" | custom-call | flops 99999997952 | bytes 1 | tf_op jit(solution)/shard_map/prefix_attend/pallas_call | solution.py:344
  51.5 0.0 copy-start.1
  51.5 2.1 %collective-permute-done.10 = bf16[512,512]{1,0:T(8,128)(2,1)} collective-permute-done((bf16[512,512]{1,0:T(8,128)(2,1)}, bf16[512,512]{1,0:T(8,128)(2,1)}, u32[]{:S(2)}, u32[]{:S(2)}) %collective-permute-start.10) | collective-permute-done | bytes 524320 | tf_op jit(solution)/shard_map/ppermute | solution.py:93
  53.6 1.2 %slice_add_fusion.1 = f32[512,512]{1,0:T(8,128)S(1)} fusion(f32[512,1024]{1,0:T(8,128)S(1)} %copy-done.12, bf16[512,512]{1,0:T(8,128)(2,1)} %collective-permute-done.10), kind=kLoop, calls=%fused_computation.3 | loop fusion | flops 524288 | bytes 2621440 | tf_op jit(solution)/shard_map/add | solution.py:500
  54.9 8.4 %collective-permute-start.11 = (bf16[256,512]{1,0:T(8,128)(2,1)S(1)}, bf16[256,512]{1,0:T(8,128)(2,1)S(1)}, u32[]{:S(2)}, u32[]{:S(2)}) collective-permute-start(bf16[256,512]{1,0:T(8,128)(2,1)S(1)} %slice.85), channel_id=1, source_target_pairs={{0,4},{4,0},{8,12},{12,8},{1,5},{5,1},{9,13},{13,9},{2,6},{6,2},{1... | collective-permute-start | bytes 786440 | tf_op jit(solution)/shard_map/ppermute | solution.py:97
  63.2 3.6 %project.7 = bf16[512,1024]{1,0:T(8,128)(2,1)S(1)} custom-call(s32[3]{0:T(128)S(1)} %pad_add_fusion.place_ref, bf16[256,4096]{1,0:T(8,128)(2,1)S(1)} %copy-done.1, bf16[128,1024]{1,0:T(8,128)(2,1)} %collective-permute-done.5.refs_1_, bf16[128,1024]{1,0:T(8,128)(2,1)} %collective-permute-done.6.refs_2_, bf16[128,1024]{1,0:T(8,128)(2,1)} %collective-permute-done.7.refs_3_, ...), custom_call_target="tpu_custom_call" | custom-call | flops 99999997952 | bytes 1 | tf_op jit(solution)/shard_map/project/pallas_call | solution.py:244
  66.8 0.1 collective-permute-start.8
  66.9 2.7 %collective-permute-done.11 = bf16[256,512]{1,0:T(8,128)(2,1)S(1)} collective-permute-done((bf16[256,512]{1,0:T(8,128)(2,1)S(1)}, bf16[256,512]{1,0:T(8,128)(2,1)S(1)}, u32[]{:S(2)}, u32[]{:S(2)}) %collective-permute-start.11) | collective-permute-done | bytes 262176 | tf_op jit(solution)/shard_map/ppermute | solution.py:97
  69.6 0.1 slice_add_fusion.3
  69.7 3.9 %collective-permute-start.12 = (bf16[128,512]{1,0:T(8,128)(2,1)S(1)}, bf16[128,512]{1,0:T(8,128)(2,1)S(1)}, u32[]{:S(2)}, u32[]{:S(2)}) collective-permute-start(bf16[128,512]{1,0:T(8,128)(2,1)S(1)} %slice.87), channel_id=1, source_target_pairs={{0,8},{4,12},{8,0},{12,4},{1,9},{5,13},{9,1},{13,5},{2,10},{6,14},... | collective-permute-start | bytes 393224 | tf_op jit(solution)/shard_map/ppermute | solution.py:97
  73.7 3.7 %project.6 = f32[512,1024]{1,0:T(8,128)S(1)} custom-call(s32[3]{0:T(128)S(1)} %pad_add_fusion.place_ref, bf16[256,4096]{1,0:T(8,128)(2,1)S(1)} %copy-done.1, bf16[128,1024]{1,0:T(8,128)(2,1)} %collective-permute-done.5.refs_1_, bf16[128,1024]{1,0:T(8,128)(2,1)} %collective-permute-done.6.refs_2_, bf16[128,1024]{1,0:T(8,128)(2,1)} %collective-permute-done.7.refs_3_, ...), custom_call_target="tpu_custom_call" | custom-call | flops 99999997952 | bytes 1 | tf_op jit(solution)/shard_map/project/pallas_call | solution.py:244
  77.3 1.9 %collective-permute-done.12 = bf16[128,512]{1,0:T(8,128)(2,1)S(1)} collective-permute-done((bf16[128,512]{1,0:T(8,128)(2,1)S(1)}, bf16[128,512]{1,0:T(8,128)(2,1)S(1)}, u32[]{:S(2)}, u32[]{:S(2)}) %collective-permute-start.12) | collective-permute-done | bytes 131104 | tf_op jit(solution)/shard_map/ppermute | solution.py:97
  79.3 0.4 convert_add_fusion
  79.6 0.1 slice.82
  79.7 1.4 %collective-permute-start.9 = (bf16[512,512]{1,0:T(8,128)(2,1)S(1)}, bf16[512,512]{1,0:T(8,128)(2,1)S(1)}, u32[]{:S(2)}, u32[]{:S(2)}) collective-permute-start(bf16[512,512]{1,0:T(8,128)(2,1)S(1)} %slice.82), channel_id=1, source_target_pairs={{0,2},{2,0},{1,3},{3,1},{4,6},{6,4},{5,7},{7,5},{8,10},{10,8},{9,1... | collective-permute-start | bytes 1572872 | tf_op jit(solution)/shard_map/ppermute | solution.py:93
  81.1 8.3 %prefix_attend.3 = (f32[128,4096]{1,0:T(8,128)S(1)}, f32[8,4096]{1,0:T(8,128)S(1)}) custom-call(bf16[8192,128]{1,0:T(8,128)(2,1)S(1)} %bitcast.25, bf16[1024,256]{1,0:T(8,128)(2,1)S(1)} %copy-done.10, bf16[272,1024]{1,0:T(8,128)(2,1)S(1)} %copy-done.8), custom_call_target="tpu_custom_call" | custom-call | flops 99999997952 | bytes 1 | tf_op jit(solution)/shard_map/prefix_attend/pallas_call | solution.py:344
  89.4 4.1 %collective-permute-done.9 = bf16[512,512]{1,0:T(8,128)(2,1)S(1)} collective-permute-done((bf16[512,512]{1,0:T(8,128)(2,1)S(1)}, bf16[512,512]{1,0:T(8,128)(2,1)S(1)}, u32[]{:S(2)}, u32[]{:S(2)}) %collective-permute-start.9) | collective-permute-done | bytes 524320 | tf_op jit(solution)/shard_map/ppermute | solution.py:93
  93.5 0.2 slice_add_fusion
  93.7 0.1 collective-permute-start.13
  93.8 5.0 %fresh_attend.2.rest_0_ = bf16[8192,128]{1,0:T(8,128)(2,1)} custom-call(s32[1]{0:T(128)S(6)} %copy.13.length_ref, bf16[8192,128]{1,0:T(8,128)(2,1)S(1)} %bitcast.26, f32[128,4096]{1,0:T(8,128)S(1)} %get-tuple-element.61.acc_ref, f32[8,4096]{1,0:T(8,128)S(1)} %get-tuple-element.62.stat_ref, bf16[128,512]{1,0:T(8,128)(2,1)S(1)} %fusion.1.fresh_ref), custom_call_target="tpu_custom_call" | custom-call | flops 99999997952 | bytes 1 | tf_op jit(solution)/shard_map/fresh_attend/pallas_call | solution.py:421
  98.7 2.2 %collective-permute-done.13 = bf16[256,512]{1,0:T(8,128)(2,1)S(1)} collective-permute-done((bf16[256,512]{1,0:T(8,128)(2,1)S(1)}, bf16[256,512]{1,0:T(8,128)(2,1)S(1)}, u32[]{:S(2)}, u32[]{:S(2)}) %collective-permute-start.13) | collective-permute-done | bytes 262176 | tf_op jit(solution)/shard_map/ppermute | solution.py:97
  101.0 0.1 slice_add_fusion.2
  101.1 0.3 collective-permute-start.14
  101.3 7.0 %collective-permute-done.14 = bf16[128,512]{1,0:T(8,128)(2,1)S(1)} collective-permute-done((bf16[128,512]{1,0:T(8,128)(2,1)S(1)}, bf16[128,512]{1,0:T(8,128)(2,1)S(1)}, u32[]{:S(2)}, u32[]{:S(2)}) %collective-permute-start.14) | collective-permute-done | bytes 131104 | tf_op jit(solution)/shard_map/ppermute | solution.py:97
  108.4 5.6 %fresh_attend.3 = bf16[8192,128]{1,0:T(8,128)(2,1)} custom-call(s32[1]{0:T(128)S(6)} %copy.13.length_ref, bf16[8192,128]{1,0:T(8,128)(2,1)S(1)} %bitcast.27, f32[128,4096]{1,0:T(8,128)S(1)} %get-tuple-element.54.acc_ref, f32[8,4096]{1,0:T(8,128)S(1)} %get-tuple-element.55.stat_ref, ...), custom_call_target="tpu_custom_call", output_to_operand_aliasing={{}: (5, {})} | custom-call | flops 99999997952 | bytes 1 | tf_op jit(solution)/shard_map/fresh_attend/pallas_call | solution.py:421
  (36 shorter events, 0.2 us)
Async XLA Ops:
  0.0 8.4 %copy-start.2 = (bf16[8,128,4,1,256]{4,2,3,1,0:T(4,128)(2,1)S(1)}, bf16[8,128,4,1,256]{4,2,3,1,0:T(4,128)(2,1)}, u32[]{:S(2)}) copy-start(bf16[8,128,4,1,256]{4,2,3,1,0:T(4,128)(2,1)} %param.11) | copy-start | bytes 6291460
  2.7 18.5 %collective-permute-start = (bf16[128,1024]{1,0:T(8,128)(2,1)}, bf16[128,1024]{1,0:T(8,128)(2,1)}, u32[]{:S(2)}, u32[]{:S(2)}) collective-permute-start(bf16[128,1024]{1,0:T(8,128)(2,1)} %get-tuple-element.70), channel_id=1, source_target_pairs={{0,8},{4,12},{8,0},{12,4},{1,9},{5,13},{9,1},{13,5},{2,10},{6,14},... | collective-permute-start | bytes 786440 | tf_op jit(solution)/shard_map/ppermute | solution.py:97
  6.7 17.0 %collective-permute-start.1 = (bf16[128,1024]{1,0:T(8,128)(2,1)}, bf16[128,1024]{1,0:T(8,128)(2,1)}, u32[]{:S(2)}, u32[]{:S(2)}) collective-permute-start(bf16[128,1024]{1,0:T(8,128)(2,1)} %get-tuple-element.69), channel_id=1, source_target_pairs={{0,4},{4,0},{8,12},{12,8},{1,5},{5,1},{9,13},{13,9},{2,6},{6,2},{1... | collective-permute-start | bytes 786440 | tf_op jit(solution)/shard_map/ppermute | solution.py:97
  8.3 18.6 %collective-permute-start.2 = (bf16[128,1024]{1,0:T(8,128)(2,1)}, bf16[128,1024]{1,0:T(8,128)(2,1)}, u32[]{:S(2)}, u32[]{:S(2)}) collective-permute-start(bf16[128,1024]{1,0:T(8,128)(2,1)} %get-tuple-element.68), channel_id=1, source_target_pairs={{0,12},{4,8},{8,4},{12,0},{1,13},{5,9},{9,5},{13,1},{2,14},{6,10},... | collective-permute-start | bytes 786440 | tf_op jit(solution)/shard_map/ppermute | solution.py:97
  8.4 7.5 %copy-start.3 = (bf16[1,1,1024,4,2,128]{5,4,3,2,1,0:T(2,128)(2,1)S(1)}, bf16[1,1,1024,4,2,128]{5,4,3,2,1,0:T(2,128)(2,1)}, u32[]{:S(2)}) copy-start(bf16[1,1,1024,4,2,128]{5,4,3,2,1,0:T(2,128)(2,1)} %param.8) | copy-start | bytes 6291460
  8.4 7.5 %copy-start.4 = (bf16[1,1,1024,4,2,128]{5,4,3,2,1,0:T(2,128)(2,1)S(1)}, bf16[1,1,1024,4,2,128]{5,4,3,2,1,0:T(2,128)(2,1)}, u32[]{:S(2)}) copy-start(bf16[1,1,1024,4,2,128]{5,4,3,2,1,0:T(2,128)(2,1)} %param.9) | copy-start | bytes 6291460
  12.5 24.7 %collective-permute-start.4 = (bf16[8,128,512]{2,1,0:T(8,128)(2,1)}, bf16[8,128,512]{2,1,0:T(8,128)(2,1)}, u32[]{:S(2)}, u32[]{:S(2)}) collective-permute-start(bf16[8,128,512]{2,1,0:T(8,128)(2,1)} %get-tuple-element.40), channel_id=1, source_target_pairs={{0,2},{2,0},{1,3},{3,1},{4,6},{6,4},{5,7},{7,5},{8,10},{10,8},{9,1... | collective-permute-start | bytes 3145736 | tf_op jit(solution)/shard_map/ppermute | solution.py:93
  14.2 37.3 %collective-permute-start.5 = (bf16[128,1024]{1,0:T(8,128)(2,1)}, bf16[128,1024]{1,0:T(8,128)(2,1)}, u32[]{:S(2)}, u32[]{:S(2)}) collective-permute-start(bf16[128,1024]{1,0:T(8,128)(2,1)} %get-tuple-element.67), channel_id=1, source_target_pairs={{0,8},{4,12},{8,0},{12,4},{1,9},{5,13},{9,1},{13,5},{2,10},{6,14},... | collective-permute-start | bytes 786440 | tf_op jit(solution)/shard_map/ppermute | solution.py:97
  15.9 11.0 %copy-start = (bf16[256,4096]{1,0:T(8,128)(2,1)S(1)}, bf16[256,4096]{1,0:T(8,128)(2,1)}, u32[]{:S(2)}) copy-start(bf16[256,4096]{1,0:T(8,128)(2,1)} %refs_0_.7) | copy-start | bytes 6291460
  21.2 30.3 %collective-permute-start.6 = (bf16[128,1024]{1,0:T(8,128)(2,1)}, bf16[128,1024]{1,0:T(8,128)(2,1)}, u32[]{:S(2)}, u32[]{:S(2)}) collective-permute-start(bf16[128,1024]{1,0:T(8,128)(2,1)} %get-tuple-element.66), channel_id=1, source_target_pairs={{0,4},{4,0},{8,12},{12,8},{1,5},{5,1},{9,13},{13,9},{2,6},{6,2},{1... | collective-permute-start | bytes 786440 | tf_op jit(solution)/shard_map/ppermute | solution.py:97
  23.7 27.8 %collective-permute-start.7 = (bf16[128,1024]{1,0:T(8,128)(2,1)}, bf16[128,1024]{1,0:T(8,128)(2,1)}, u32[]{:S(2)}, u32[]{:S(2)}) collective-permute-start(bf16[128,1024]{1,0:T(8,128)(2,1)} %get-tuple-element.65), channel_id=1, source_target_pairs={{0,12},{4,8},{8,4},{12,0},{1,13},{5,9},{9,5},{13,1},{2,14},{6,10},... | collective-permute-start | bytes 786440 | tf_op jit(solution)/shard_map/ppermute | solution.py:97
  30.5 3.8 %collective-permute-start.3 = (bf16[512,1024]{1,0:T(8,128)(2,1)S(1)}, bf16[512,1024]{1,0:T(8,128)(2,1)S(1)}, u32[]{:S(2)}, u32[]{:S(2)}) collective-permute-start(bf16[512,1024]{1,0:T(8,128)(2,1)S(1)} %project.5), channel_id=1, source_target_pairs={{0,1},{1,0},{2,3},{3,2},{4,5},{5,4},{6,7},{7,6},{8,9},{9,8},{10,11... | collective-permute-start | bytes 3145736 | tf_op jit(solution)/shard_map/ppermute | solution.py:93
  34.2 6.5 %copy-start.6 = (s32[1,8]{1,0:T(1,128)S(1)}, s32[1,8]{1,0:T(1,128)}, u32[]{:S(2)}) copy-start(s32[1,8]{1,0:T(1,128)} %param.12) | copy-start | bytes 100
  34.7 8.3 %copy-start.11 = (f32[512,1024]{1,0:T(8,128)}, f32[512,1024]{1,0:T(8,128)S(1)}, u32[]{:S(2)}) copy-start(f32[512,1024]{1,0:T(8,128)S(1)} %convert_add_fusion.1) | copy-start | bytes 6291460
  37.2 16.4 %collective-permute-start.10 = (bf16[512,512]{1,0:T(8,128)(2,1)}, bf16[512,512]{1,0:T(8,128)(2,1)}, u32[]{:S(2)}, u32[]{:S(2)}) collective-permute-start(bf16[512,512]{1,0:T(8,128)(2,1)} %slice.83), channel_id=1, source_target_pairs={{0,2},{2,0},{1,3},{3,1},{4,6},{6,4},{5,7},{7,5},{8,10},{10,8},{9,1... | collective-permute-start | bytes 1572872 | tf_op jit(solution)/shard_map/ppermute | solution.py:93
  40.7 2.3 %copy-start.5 = (bf16[256,2,1,2048]{3,1,2,0:T(2,128)(2,1)S(1)}, bf16[256,2,1,2048]{3,1,2,0:T(2,128)(2,1)}, u32[]{:S(2)}) copy-start(bf16[256,2,1,2048]{3,1,2,0:T(2,128)(2,1)} %param.10) | copy-start | bytes 6291460
  43.0 8.4 %copy-start.7 = (bf16[272,1024]{1,0:T(8,128)(2,1)}, bf16[272,1024]{1,0:T(8,128)(2,1)S(1)}, u32[]{:S(2)}) copy-start(bf16[272,1024]{1,0:T(8,128)(2,1)S(1)} %get-tuple-element.45.values) | copy-start | bytes 1671172
  43.0 8.4 %copy-start.9 = (bf16[1024,256]{1,0:T(8,128)(2,1)}, bf16[1024,256]{1,0:T(8,128)(2,1)S(1)}, u32[]{:S(2)}) copy-start(bf16[1024,256]{1,0:T(8,128)(2,1)S(1)} %get-tuple-element.44.keys) | copy-start | bytes 1572868
  43.1 10.5 %copy-start.12 = (f32[512,1024]{1,0:T(8,128)S(1)}, f32[512,1024]{1,0:T(8,128)}, u32[]{:S(2)}) copy-start(f32[512,1024]{1,0:T(8,128)} %copy-done.11) | copy-start | bytes 6291460
  51.5 11.8 %copy-start.1 = (bf16[256,4096]{1,0:T(8,128)(2,1)S(1)}, bf16[256,4096]{1,0:T(8,128)(2,1)}, u32[]{:S(2)}) copy-start(bf16[256,4096]{1,0:T(8,128)(2,1)} %refs_0_.7) | copy-start | bytes 6291460
  54.9 14.7 %collective-permute-start.11 = (bf16[256,512]{1,0:T(8,128)(2,1)S(1)}, bf16[256,512]{1,0:T(8,128)(2,1)S(1)}, u32[]{:S(2)}, u32[]{:S(2)}) collective-permute-start(bf16[256,512]{1,0:T(8,128)(2,1)S(1)} %slice.85), channel_id=1, source_target_pairs={{0,4},{4,0},{8,12},{12,8},{1,5},{5,1},{9,13},{13,9},{2,6},{6,2},{1... | collective-permute-start | bytes 786440 | tf_op jit(solution)/shard_map/ppermute | solution.py:97
  66.8 12.4 %collective-permute-start.8 = (bf16[512,1024]{1,0:T(8,128)(2,1)S(1)}, bf16[512,1024]{1,0:T(8,128)(2,1)S(1)}, u32[]{:S(2)}, u32[]{:S(2)}) collective-permute-start(bf16[512,1024]{1,0:T(8,128)(2,1)S(1)} %project.7), channel_id=1, source_target_pairs={{0,1},{1,0},{2,3},{3,2},{4,5},{5,4},{6,7},{7,6},{8,9},{9,8},{10,11... | collective-permute-start | bytes 3145736 | tf_op jit(solution)/shard_map/ppermute | solution.py:93
  69.7 9.5 %collective-permute-start.12 = (bf16[128,512]{1,0:T(8,128)(2,1)S(1)}, bf16[128,512]{1,0:T(8,128)(2,1)S(1)}, u32[]{:S(2)}, u32[]{:S(2)}) collective-permute-start(bf16[128,512]{1,0:T(8,128)(2,1)S(1)} %slice.87), channel_id=1, source_target_pairs={{0,8},{4,12},{8,0},{12,4},{1,9},{5,13},{9,1},{13,5},{2,10},{6,14},... | collective-permute-start | bytes 393224 | tf_op jit(solution)/shard_map/ppermute | solution.py:97
  79.2 1.8 %copy-start.8 = (bf16[272,1024]{1,0:T(8,128)(2,1)S(1)}, bf16[272,1024]{1,0:T(8,128)(2,1)}, u32[]{:S(2)}) copy-start(bf16[272,1024]{1,0:T(8,128)(2,1)} %copy-done.7) | copy-start | bytes 1671172
  79.2 1.8 %copy-start.10 = (bf16[1024,256]{1,0:T(8,128)(2,1)S(1)}, bf16[1024,256]{1,0:T(8,128)(2,1)}, u32[]{:S(2)}) copy-start(bf16[1024,256]{1,0:T(8,128)(2,1)} %copy-done.9) | copy-start | bytes 1572868
  79.7 13.8 %collective-permute-start.9 = (bf16[512,512]{1,0:T(8,128)(2,1)S(1)}, bf16[512,512]{1,0:T(8,128)(2,1)S(1)}, u32[]{:S(2)}, u32[]{:S(2)}) collective-permute-start(bf16[512,512]{1,0:T(8,128)(2,1)S(1)} %slice.82), channel_id=1, source_target_pairs={{0,2},{2,0},{1,3},{3,1},{4,6},{6,4},{5,7},{7,5},{8,10},{10,8},{9,1... | collective-permute-start | bytes 1572872 | tf_op jit(solution)/shard_map/ppermute | solution.py:93
  93.7 7.3 %collective-permute-start.13 = (bf16[256,512]{1,0:T(8,128)(2,1)S(1)}, bf16[256,512]{1,0:T(8,128)(2,1)S(1)}, u32[]{:S(2)}, u32[]{:S(2)}) collective-permute-start(bf16[256,512]{1,0:T(8,128)(2,1)S(1)} %slice.84), channel_id=1, source_target_pairs={{0,4},{4,0},{8,12},{12,8},{1,5},{5,1},{9,13},{13,9},{2,6},{6,2},{1... | collective-permute-start | bytes 786440 | tf_op jit(solution)/shard_map/ppermute | solution.py:97
  101.1 7.3 %collective-permute-start.14 = (bf16[128,512]{1,0:T(8,128)(2,1)S(1)}, bf16[128,512]{1,0:T(8,128)(2,1)S(1)}, u32[]{:S(2)}, u32[]{:S(2)}) collective-permute-start(bf16[128,512]{1,0:T(8,128)(2,1)S(1)} %slice.86), channel_id=1, source_target_pairs={{0,8},{4,12},{8,0},{12,4},{1,9},{5,13},{9,1},{13,5},{2,10},{6,14},... | collective-permute-start | bytes 393224 | tf_op jit(solution)/shard_map/ppermute | solution.py:97

commit v5 on v4

--- a/solution.py
+++ b/solution.py
@@ -9,7 +9,7 @@
 from jax.sharding import PartitionSpec as P
 
 CHUNKS = 2
-VMEM_BYTES = 48 * 1024 * 1024
+VMEM_BYTES = 32 * 1024 * 1024
 LONG = pl.CostEstimate(flops=10**11, bytes_accessed=1, transcendentals=0)
 
 
@@ -97,13 +97,6 @@
     return lax.ppermute(array, axis, [(i, i ^ bits) for i in range(lax.axis_size(axis))])
 
 
-def halving_order(count):
-    order, bit = [0], count // 2
-    while bit:
-        order, bit = order + [i ^ bit for i in order], bit // 2
-    return order
-
-
 def unit_index(shape, unit):
     row = lax.broadcasted_iota(jnp.int32, shape, 0)
     if unit & (unit - 1):
@@ -236,18 +229,23 @@
     ).astype(out_ref.dtype)
 
 
-def project(place, tokens, received, weights, chunk, head_step, out_dtype):
+def project(place, blocks, weights, head_step, out_dtype):
     head_count, ctx_count, depth, width = weights.shape
-    rows = tokens.shape[0] // CHUNKS
-    row_total = rows * (1 + len(received))
+    rows = blocks[0].shape[0]
+    row_total = rows * len(blocks)
     columns = ctx_count * width
+
+    def block_spec(block):
+        if block.shape[1] == depth:
+            return pl.BlockSpec((rows, depth), lambda j, place: (0, 0))
+        return pl.BlockSpec((rows, depth), lambda j, place: (0, place[0]))
+
     return pl.pallas_call(
         project_kernel,
         grid_spec=pltpu.PrefetchScalarGridSpec(
             num_scalar_prefetch=1,
             grid=(ctx_count,),
-            in_specs=[pl.BlockSpec((rows, depth), lambda j, place: (chunk, place[0]))]
-            + [pl.BlockSpec((rows, depth), lambda j, place: (0, 0)) for _ in received]
+            in_specs=[block_spec(block) for block in blocks]
             + [
                 pl.BlockSpec(
                     (1, 1, depth, width),
@@ -260,13 +258,13 @@
                 )
             ],
             out_specs=pl.BlockSpec((row_total, width), lambda j, place: (0, j)),
-            scratch_shapes=[pltpu.VMEM((row_total, depth), tokens.dtype)],
+            scratch_shapes=[pltpu.VMEM((row_total, depth), weights.dtype)],
         ),
         out_shape=jax.ShapeDtypeStruct((row_total, columns), out_dtype),
         compiler_params=params(),
         cost_estimate=LONG,
         name="project",
-    )(place, tokens, *received, weights)
+    )(place, *blocks, weights)
 
 
 def pick_kernel(heads, ctx_count, place_ref, table_ref, *refs):
@@ -335,7 +333,7 @@
         stat_ref[half:, here] = jnp.broadcast_to(mixed[wide : wide + 1], (half, part_rows))
 
 
-def prefix_attend(query_rows, keys, values, chunk, scale, heads):
+def prefix_attend(query_rows, keys, values, piece, scale, heads):
     all_rows, width = query_rows.shape
     row_total = all_rows // CHUNKS
     rows = min(1024, row_total)
@@ -345,7 +343,7 @@
         functools.partial(prefix_kernel, scale, heads),
         grid=(steps,),
         in_specs=[
-            pl.BlockSpec((rows, width), lambda i: (chunk * steps + i, 0)),
+            pl.BlockSpec((rows, width), lambda i: (piece * steps + i, 0)),
             pl.BlockSpec(keys.shape, lambda i: (0, 0)),
             pl.BlockSpec(values.shape, lambda i: (0, 0)),
         ],
@@ -400,12 +398,12 @@
         out_ref[here, :] = result.T.astype(out_ref.dtype)
 
 
-def fresh_attend(length, query_rows, acc, stat, fresh, earlier, chunk, scale, heads, per_token):
+def fresh_attend(length, query_rows, acc, stat, fresh, earlier, piece, scale, heads, per_token):
     row_total, width = query_rows.shape
-    chunk_rows = row_total // CHUNKS
-    rows = min(1024, chunk_rows)
-    steps = chunk_rows // rows
-    block = pl.BlockSpec((rows, width), lambda i, length: (chunk * steps + i, 0))
+    piece_rows = row_total // CHUNKS
+    rows = min(1024, piece_rows)
+    steps = piece_rows // rows
+    block = pl.BlockSpec((rows, width), lambda i, length: (piece * steps + i, 0))
     in_specs = [
         block,
         pl.BlockSpec((width, rows), lambda i, length: (0, i)),
@@ -420,7 +418,7 @@
         aliases = {5: 0}
     return pl.pallas_call(
         functools.partial(
-            fresh_kernel, scale, heads, per_token, chunk * (chunk_rows // per_token)
+            fresh_kernel, scale, heads, per_token, piece * (piece_rows // per_token)
         ),
         grid_spec=pltpu.PrefetchScalarGridSpec(
             num_scalar_prefetch=1,
@@ -455,69 +453,89 @@
     rows = token_count // CHUNKS
     scale = math.log2(math.e) / math.sqrt(width)
 
-    order = halving_order(batch_count)
-    received = []
-    for chunk in range(CHUNKS):
-        arrived = []
-        for bits in order[1:]:
-            start = (batch_at ^ bits) * depth
-            piece = lax.dynamic_slice(tokens, (chunk * rows, start), (rows, depth))
-            arrived.append(trade(piece, "batch", bits))
-        received.append(arrived)
+    def leaving(bits):
+        start = (batch_at ^ bits) * depth
+        return lax.dynamic_slice(tokens, (0, start), (token_count, depth))
+
+    top = batch_count // 2
+    steps = [bits for bits in range(1, batch_count) if bits != top]
+    near = [trade(leaving(bits), "batch", bits) for bits in steps]
 
     pools = arrange_pool(place, prefix_pool, ctx_count, heads)
-    pools, key_weight, value_weight = lax.optimization_barrier((pools, key_weight, value_weight))
+    pools, key_weight, value_weight, tokens = lax.optimization_barrier(
+        (pools, key_weight, value_weight, tokens)
+    )
+    last = trade(leaving(top), "batch", top)
     pools = [shift(part, "ctx", step) if step else part for step, part in enumerate(pools)]
 
     weights = arrange_weights(key_weight, value_weight, ctx_count, heads, head_count)
 
     query_rows = queries.reshape(token_count, heads, group, width)
     query_rows = query_rows.transpose(0, 2, 1, 3).reshape(-1, width)
-    keys = values = None
-    fresh_parts = []
-    result = None
     cols = weights.shape[3]
-    for chunk in range(CHUNKS):
-        call = functools.partial(project, place, tokens, received[chunk], weights, chunk)
+
+    def projected(blocks):
         terms = [
-            shift(call(step, jnp.bfloat16), "head", step).astype(jnp.float32)
+            shift(project(place, blocks, weights, step, jnp.bfloat16), "head", step)
             for step in range(1, head_count)
         ]
-        own = call(0, jnp.float32)
-        mine = sum(terms, own[:, :])
-        parts = [
-            mine[:, step * cols : (step + 1) * cols].astype(jnp.bfloat16)
+        total = project(place, blocks, weights, 0, jnp.float32)
+        total = sum((term.astype(jnp.float32) for term in terms), total)
+        others = [
+            total[:, step * cols : (step + 1) * cols].astype(jnp.bfloat16)
             for step in range(1, ctx_count)
         ]
-        parts, pools, query_rows = lax.optimization_barrier((parts, pools, query_rows))
-        parts = [shift(part, "ctx", step + 1) for step, part in enumerate(parts)]
-        if keys is None:
-            keys, values = pick_blocks(place, block_table[0], pools, heads)
-        acc, stat = prefix_attend(query_rows, keys, values, chunk, scale, heads)
-        if chunk + 1 < CHUNKS:
-            acc, received[chunk + 1] = lax.optimization_barrier((acc, received[chunk + 1]))
-        parts, acc, stat = lax.optimization_barrier((parts, acc, stat))
-        mine = sum((part.astype(jnp.float32) for part in parts), mine[:, :cols])
-        bit = 1
-        while bit < batch_count:
-            half = mine.shape[0] // 2
-            part = trade(mine[half:].astype(jnp.bfloat16), "batch", bit)
-            if result is not None and bit == 1:
-                part, result = lax.optimization_barrier((part, result))
-            mine = mine[:half] + part.astype(jnp.float32)
-            bit *= 2
-        fresh_parts.append(mine.astype(jnp.bfloat16))
+        return total[:, :cols], others
+
+    def spread(others):
+        return [shift(other, "ctx", step + 1) for step, other in enumerate(others)]
+
+    def summed(mine, others):
+        return sum((other.astype(jnp.float32) for other in others), mine)
+
+    def after(first, second):
+        return lax.optimization_barrier((first, second))[1]
+
+    def halves(block):
+        return [block[i * rows : (i + 1) * rows] for i in range(CHUNKS)]
+
+    early, others = projected([*near, tokens])
+    pools = after(others, pools)
+    own_at = len(near) * token_count
+    keys, values = pick_blocks(place, block_table[0], pools, heads)
+    if near:
+        away = summed(early[:own_at], spread([other[:own_at] for other in others]))
+        away = trade(away.astype(jnp.bfloat16), "batch", 1).astype(jnp.float32)
+    home = summed(early[own_at:], spread([other[own_at:] for other in others]))
+    states = [prefix_attend(query_rows, keys, values, 0, scale, heads)]
+    last = after(states[0], last)
+
+    mine, others = projected([last])
+    keys, values = after(others, (keys, values))
+    for chunk in range(1, CHUNKS):
+        states.append(prefix_attend(query_rows, keys, values, chunk, scale, heads))
+    mine = halves(mine)
+    others = [spread(list(o)) for o in zip(*(halves(other) for other in others))]
+    if near:
+        home = home + away[:token_count]
+        mine = [a + b for a, b in zip(mine, halves(away[token_count:]))]
+    home = halves(home)
+    parts = []
+    for chunk in range(CHUNKS):
+        if parts:
+            others[chunk] = after(parts[-1], others[chunk])
+        parts.append(summed(mine[chunk], others[chunk]).astype(jnp.bfloat16))
+    parts = [trade(part, "batch", top) for part in parts]
+
+    result = None
+    fresh_parts = []
+    for chunk in range(CHUNKS):
+        if chunk:
+            parts[chunk] = after(result, parts[chunk])
+        fresh_parts.append((parts[chunk].astype(jnp.float32) + home[chunk]).astype(jnp.bfloat16))
+        fresh = jnp.concatenate(fresh_parts, 0)
         result = fresh_attend(
-            lengths,
-            query_rows,
-            acc,
-            stat,
-            jnp.concatenate(fresh_parts, 0),
-            result,
-            chunk,
-            scale,
-            heads,
-            per_token,
+            lengths, query_rows, *states[chunk], fresh, result, chunk, scale, heads, per_token
         )
     result = result.reshape(token_count, group, heads, width).transpose(0, 2, 1, 3)
     return result.reshape(token_count, heads, 1, group * width)
@@ -527,7 +545,7 @@
     def shards(tokens, key_weight, value_weight, *rest):
         prompts = mesh.shape["batch"]
         columns = 2 * math.prod(key_weight.shape[3:])
-        few_tokens = prompts * tokens.shape[0] <= columns and not prompts & (prompts - 1)
+        few_tokens = prompts * tokens.shape[0] <= columns and prompts in (2, 4)
         form = reduced_shards if few_tokens else gathered_shards
         return form(tokens, key_weight, value_weight, *rest)
 

time: 114 us -> 124 us (1.088)
  waiting for transfers between devices: 24.4 us -> 39 us
  Pallas kernels: 52.8 us -> 47.5 us
  starting transfers between devices: 29.5 us -> 25.2 us
  local copies, waits for them, and re-layouts: 3.87 us -> 7.79 us
    ppermute x10 -> x6, waiting for transfers between devices: 16.7 us -> 25.3 us  [trade(): lax.ppermute(array, axis, [(i, i ^ bits) for i in range(lax.axis_size(axi...]
    ppermute x5 -> x7, waiting for transfers between devices: 7.68 us -> 13.7 us  [shift(): lax.ppermute(array, axis, [(i, (i + step) % count) for i in range(count)])]
    unnamed x26 -> x28, local copies, waits for them, and re-layouts: 0.06 us -> 5.8 us
    ppermute x10 -> x6, starting transfers between devices: 22.7 us -> 17.8 us  [trade(): lax.ppermute(array, axis, [(i, i ^ bits) for i in range(lax.axis_size(axi...]
    pallas_call x4, Pallas kernels: 14.5 us -> 11.6 us  [project(): pl.pallas_call(project_kernel, grid_spec=pltpu.PrefetchScalarGridSpec(num...]
    another operation x0 -> x2, other arithmetic: none -> 2.43 us
    add x6 -> x1, other arithmetic: 2.32 us -> 0.13 us  [reduced_shards(): home = home + away[:token_count]]
    pallas_call x1, Pallas kernels: 4.62 us -> 2.47 us  [arrange_weights(): pl.pallas_call(functools.partial(weight_kernel, ctx_count, heads, head_co...]
  transfers between devices with their start and end apart: 15 -> 13, of which waited for: 8 -> 7; matrix products, arithmetic and copies ran while one was open for 1% -> 4% of each run, Pallas kernels for 41% -> 31%
where the time goes in v5:
time: 124 us; the launch traced here: 123 us
  Pallas kernels  47.5 us (38%)
  waiting for transfers between devices  39 us (31%)
  starting transfers between devices  25.2 us (20%)
  local copies, waits for them, and re-layouts  7.79 us (6%)
  other arithmetic  3.1 us (2%)
    ppermute x6, waiting for transfers between devices, trade(): lax.ppermute(array, axis, [(i, i ^ bits) for i in range(lax.axis_size(axi...  25.3 us
    ppermute x6, starting transfers between devices, trade(): lax.ppermute(array, axis, [(i, i ^ bits) for i in range(lax.axis_size(axi...  17.8 us
    pallas_call x2, Pallas kernels, prefix_attend(): pl.pallas_call(functools.partial(prefix_kernel, scale, heads), grid=(step...  16.5 us
    ppermute x7, waiting for transfers between devices, shift(): lax.ppermute(array, axis, [(i, (i + step) % count) for i in range(count)])  13.7 us
    pallas_call x4, Pallas kernels, project(): pl.pallas_call(project_kernel, grid_spec=pltpu.PrefetchScalarGridSpec(num...  11.6 us
    pallas_call x2, Pallas kernels, fresh_attend(): pl.pallas_call(functools.partial(fresh_kernel, scale, heads, per_token, p...  10.6 us
    ppermute x7, starting transfers between devices, shift(): lax.ppermute(array, axis, [(i, (i + step) % count) for i in range(count)])  7.32 us
    unnamed x28, local copies, waits for them, and re-layouts  5.8 us
  transfers between devices with their start and end apart: 13, of which 7 were waited for; matrix products, arithmetic and copies ran while one was open for 4% of the time, Pallas kernels for 31%

profile of v5, /device:TPU:0, one launch (start us, length us, event | category | flops | bytes accessed | tf_op | source)
XLA Modules:
  0.0 123.5 jit_solution(467068231894188117)
XLA Ops:
  0.0 0.1 pad_add_fusion.place_ref
  0.1 1.6 %copy-done.1 = bf16[8,128,4,1,256]{4,2,3,1,0:T(4,128)(2,1)S(1)} copy-done((bf16[8,128,4,1,256]{4,2,3,1,0:T(4,128)(2,1)S(1)}, bf16[8,128,4,1,256]{4,2,3,1,0:T(4,128)(2,1)}, u32[]{:S(2)}) %copy-start.1) | copy-done | bytes 2097176
  1.7 4.1 %arrange_pool.1 = (bf16[8,128,512]{2,1,0:T(8,128)(2,1)S(1)}, bf16[8,128,512]{2,1,0:T(8,128)(2,1)}) custom-call(s32[3]{0:T(128)S(1)} %pad_add_fusion.place_ref, bf16[8,128,8,128]{3,2,1,0:T(8,128)(2,1)S(1)} %bitcast.21), custom_call_target="tpu_custom_call" | custom-call | flops 99999997952 | bytes 1 | tf_op jit(solution)/shard_map/arrange_pool/pallas_call | solution.py:202
  5.8 1.0 copy-done.8
  6.8 2.9 %collective-permute-start = (bf16[8,128,512]{2,1,0:T(8,128)(2,1)}, bf16[8,128,512]{2,1,0:T(8,128)(2,1)}, u32[]{:S(2)}, u32[]{:S(2)}) collective-permute-start(bf16[8,128,512]{2,1,0:T(8,128)(2,1)} %get-tuple-element.28), channel_id=1, source_target_pairs={{0,2},{2,0},{1,3},{3,1},{4,6},{6,4},{5,7},{7,5},{8,10},{10,8},{9,1... | collective-permute-start | bytes 3145736 | tf_op jit(solution)/shard_map/ppermute | solution.py:93
  9.7 1.1 constant_dynamic-slice_fusion
  10.8 1.6 %collective-permute-start.3 = (bf16[256,1024]{1,0:T(8,128)(2,1)}, bf16[256,1024]{1,0:T(8,128)(2,1)S(1)}, u32[]{:S(2)}, u32[]{:S(2)}) collective-permute-start(bf16[256,1024]{1,0:T(8,128)(2,1)} %get-tuple-element.50), channel_id=1, source_target_pairs={{0,4},{4,0},{8,12},{12,8},{1,5},{5,1},{9,13},{13,9},{2,6},{6,2},{1... | collective-permute-start | bytes 1572872 | tf_op jit(solution)/shard_map/ppermute | solution.py:97
  12.4 2.5 %collective-permute-start.4 = (bf16[256,1024]{1,0:T(8,128)(2,1)}, bf16[256,1024]{1,0:T(8,128)(2,1)S(1)}, u32[]{:S(2)}, u32[]{:S(2)}) collective-permute-start(bf16[256,1024]{1,0:T(8,128)(2,1)} %get-tuple-element.49), channel_id=1, source_target_pairs={{0,12},{4,8},{8,4},{12,0},{1,13},{5,9},{9,5},{13,1},{2,14},{6,10},... | collective-permute-start | bytes 1572872 | tf_op jit(solution)/shard_map/ppermute | solution.py:97
  14.9 0.8 constant_dynamic-slice_fusion.2
  15.7 0.1 collective-permute-start.1
  15.8 1.6 %copy-done.2 = bf16[1,1,1024,4,2,128]{5,4,3,2,1,0:T(2,128)(2,1)S(1)} copy-done((bf16[1,1,1024,4,2,128]{5,4,3,2,1,0:T(2,128)(2,1)S(1)}, bf16[1,1,1024,4,2,128]{5,4,3,2,1,0:T(2,128)(2,1)}, u32[]{:S(2)}) %copy-start.2) | copy-done | bytes 2097176
  17.4 1.6 %copy-done.3 = bf16[1,1,1024,4,2,128]{5,4,3,2,1,0:T(2,128)(2,1)S(1)} copy-done((bf16[1,1,1024,4,2,128]{5,4,3,2,1,0:T(2,128)(2,1)S(1)}, bf16[1,1,1024,4,2,128]{5,4,3,2,1,0:T(2,128)(2,1)}, u32[]{:S(2)}) %copy-start.3) | copy-done | bytes 2097176
  19.0 2.5 %arrange_weights.1.refs_1_.refs_3_ = bf16[2,2,1024,512]{3,2,1,0:T(8,128)(2,1)S(1)} custom-call(bf16[1024,8,128]{2,1,0:T(8,128)(2,1)S(1)} %bitcast.22, bf16[1024,8,128]{2,1,0:T(8,128)(2,1)S(1)} %bitcast.23), custom_call_target="tpu_custom_call" | custom-call | flops 99999997952 | bytes 1 | tf_op jit(solution)/shard_map/arrange_weights/pallas_call | solution.py:161
  22.1 3.0 %collective-permute-done.3.refs_0_ = bf16[256,1024]{1,0:T(8,128)(2,1)S(1)} collective-permute-done((bf16[256,1024]{1,0:T(8,128)(2,1)}, bf16[256,1024]{1,0:T(8,128)(2,1)S(1)}, u32[]{:S(2)}, u32[]{:S(2)}) %collective-permute-start.3) | collective-permute-done | bytes 524320 | tf_op jit(solution)/shard_map/ppermute | solution.py:97
  25.1 14.2 %collective-permute-done.4.refs_1_ = bf16[256,1024]{1,0:T(8,128)(2,1)S(1)} collective-permute-done((bf16[256,1024]{1,0:T(8,128)(2,1)}, bf16[256,1024]{1,0:T(8,128)(2,1)S(1)}, u32[]{:S(2)}, u32[]{:S(2)}) %collective-permute-start.4) | collective-permute-done | bytes 524320 | tf_op jit(solution)/shard_map/ppermute | solution.py:97
  39.2 3.6 %project.7 = bf16[768,1024]{1,0:T(8,128)(2,1)} custom-call(s32[3]{0:T(128)S(1)} %pad_add_fusion.place_ref, bf16[256,1024]{1,0:T(8,128)(2,1)S(1)} %collective-permute-done.3.refs_0_, bf16[256,1024]{1,0:T(8,128)(2,1)S(1)} %collective-permute-done.4.refs_1_, bf16[256,4096]{1,0:T(8,128)(2,1)S(1)} %copy-done, ...), custom_call_target="tpu_custom_call" | custom-call | flops 99999997952 | bytes 1 | tf_op jit(solution)/shard_map/project/pallas_call | solution.py:243
  42.8 0.0 collective-permute-start.5
  42.8 2.9 %project.6 = f32[768,1024]{1,0:T(8,128)S(1)} custom-call(s32[3]{0:T(128)S(1)} %pad_add_fusion.place_ref, bf16[256,1024]{1,0:T(8,128)(2,1)S(1)} %collective-permute-done.3.refs_0_, bf16[256,1024]{1,0:T(8,128)(2,1)S(1)} %collective-permute-done.4.refs_1_, bf16[256,4096]{1,0:T(8,128)(2,1)S(1)} %copy-done, ...), custom_call_target="tpu_custom_call" | custom-call | flops 99999997952 | bytes 1 | tf_op jit(solution)/shard_map/project/pallas_call | solution.py:243
  45.8 0.0 copy-start.4
  45.8 2.1 %pick_blocks.1 = (bf16[1024,256]{1,0:T(8,128)(2,1)S(1)}, bf16[272,1024]{1,0:T(8,128)(2,1)S(1)}) custom-call(s32[3]{0:T(128)S(1)} %pad_add_fusion.place_ref, s32[8]{0:T(128)S(1)} %bitcast.28, bf16[8,128,512]{2,1,0:T(8,128)(2,1)S(1)} %copy-done.9, bf16[8,128,512]{2,1,0:T(8,128)(2,1)} %collective-permute-done.refs_1_), custom_call_target="tpu_custom_call" | custom-call | flops 99999997952 | bytes 1 | tf_op jit(solution)/shard_map/pick_blocks/pallas_call | solution.py:295
  48.0 8.3 %prefix_attend.3 = (f32[128,4096]{1,0:T(8,128)S(1)}, f32[8,4096]{1,0:T(8,128)S(1)}) custom-call(bf16[8192,128]{1,0:T(8,128)(2,1)S(1)} %bitcast.24, bf16[1024,256]{1,0:T(8,128)(2,1)S(1)} %get-tuple-element.35.keys, bf16[272,1024]{1,0:T(8,128)(2,1)S(1)} %get-tuple-element.32.values), custom_call_target="tpu_custom_call" | custom-call | flops 99999997952 | bytes 1 | tf_op jit(solution)/shard_map/prefix_attend/pallas_call | solution.py:342
  56.3 4.1 %collective-permute-done.1.refs_0_ = bf16[256,1024]{1,0:T(8,128)(2,1)} collective-permute-done((bf16[256,1024]{1,0:T(8,128)(2,1)}, bf16[256,1024]{1,0:T(8,128)(2,1)}, u32[]{:S(2)}, u32[]{:S(2)}) %collective-permute-start.1) | collective-permute-done | bytes 524320 | tf_op jit(solution)/shard_map/ppermute | solution.py:97
  60.4 2.6 %project.5 = bf16[256,1024]{1,0:T(8,128)(2,1)S(1)} custom-call(s32[3]{0:T(128)S(1)} %pad_add_fusion.place_ref, bf16[256,1024]{1,0:T(8,128)(2,1)} %collective-permute-done.1.refs_0_, bf16[2,2,1024,512]{3,2,1,0:T(8,128)(2,1)S(1)} %copy-done.7), custom_call_target="tpu_custom_call" | custom-call | flops 99999997952 | bytes 1 | tf_op jit(solution)/shard_map/project/pallas_call | solution.py:243
  62.9 0.1 collective-permute-start.2
  63.0 2.6 %project.4 = f32[256,1024]{1,0:T(8,128)S(1)} custom-call(s32[3]{0:T(128)S(1)} %pad_add_fusion.place_ref, bf16[256,1024]{1,0:T(8,128)(2,1)} %collective-permute-done.1.refs_0_, bf16[2,2,1024,512]{3,2,1,0:T(8,128)(2,1)S(1)} %copy-done.7), custom_call_target="tpu_custom_call" | custom-call | flops 99999997952 | bytes 1 | tf_op jit(solution)/shard_map/project/pallas_call | solution.py:243
  65.6 0.0 collective-permute-done.5
  65.6 2.2 %fusion.8 = (bf16[768,1024]{1,0:T(8,128)(2,1)S(1)}, f32[768,1024]{1,0:T(8,128)S(1)}) fusion(f32[768,1024]{1,0:T(8,128)S(1)} %project.6, bf16[768,1024]{1,0:T(8,128)(2,1)} %collective-permute-done.5), kind=kLoop, calls=%fused_computation.22 | loop fusion | flops 2359296 | bytes 9437184 | tf_op jit(solution)/shard_map/convert.1
  67.9 0.6 collective-permute-start.6
  68.6 0.0 collective-permute-done.2
  68.6 0.2 fusion.7
  68.8 1.5 %collective-permute-start.8 = (bf16[128,512]{1,0:T(8,128)(2,1)S(1)}, bf16[128,512]{1,0:T(8,128)(2,1)S(1)}, u32[]{:S(2)}, u32[]{:S(2)}) collective-permute-start(bf16[128,512]{1,0:T(8,128)(2,1)S(1)} %get-tuple-element.52), channel_id=1, source_target_pairs={{0,2},{2,0},{1,3},{3,1},{4,6},{6,4},{5,7},{7,5},{8,10},{10,8},{9,1... | collective-permute-start | bytes 393224 | tf_op jit(solution)/shard_map/ppermute | solution.py:93
  70.3 12.4 %collective-permute-done.6 = bf16[512,512]{1,0:T(8,128)(2,1)S(1)} collective-permute-done((bf16[512,512]{1,0:T(8,128)(2,1)S(1)}, bf16[512,512]{1,0:T(8,128)(2,1)S(1)}, u32[]{:S(2)}, u32[]{:S(2)}) %collective-permute-start.6) | collective-permute-done | bytes 524320 | tf_op jit(solution)/shard_map/ppermute | solution.py:93
  82.7 0.2 fusion
  82.9 8.4 %collective-permute-start.7 = (bf16[512,512]{1,0:T(8,128)(2,1)S(1)}, bf16[512,512]{1,0:T(8,128)(2,1)S(1)}, u32[]{:S(2)}, u32[]{:S(2)}) collective-permute-start(bf16[512,512]{1,0:T(8,128)(2,1)S(1)} %fusion), channel_id=1, source_target_pairs={{0,4},{4,0},{8,12},{12,8},{1,5},{5,1},{9,13},{13,9},{2,6},{6,2},{1... | collective-permute-start | bytes 1572872 | tf_op jit(solution)/shard_map/ppermute | solution.py:97
  91.3 8.3 %prefix_attend.2 = (f32[128,4096]{1,0:T(8,128)S(1)}, f32[8,4096]{1,0:T(8,128)S(1)}) custom-call(bf16[8192,128]{1,0:T(8,128)(2,1)S(1)} %bitcast.25, bf16[1024,256]{1,0:T(8,128)(2,1)S(1)} %copy-done.13, bf16[272,1024]{1,0:T(8,128)(2,1)S(1)} %copy-done.11), custom_call_target="tpu_custom_call" | custom-call | flops 99999997952 | bytes 1 | tf_op jit(solution)/shard_map/prefix_attend/pallas_call | solution.py:342
  99.5 0.6 collective-permute-start.11
  100.2 1.6 %collective-permute-start.10 = (bf16[256,512]{1,0:T(8,128)(2,1)S(1)}, bf16[256,512]{1,0:T(8,128)(2,1)S(1)}, u32[]{:S(2)}, u32[]{:S(2)}) collective-permute-start(bf16[256,512]{1,0:T(8,128)(2,1)S(1)} %slice.75), channel_id=1, source_target_pairs={{0,2},{2,0},{1,3},{3,1},{4,6},{6,4},{5,7},{7,5},{8,10},{10,8},{9,1... | collective-permute-start | bytes 786440 | tf_op jit(solution)/shard_map/ppermute | solution.py:93
  101.7 0.1 convert_element_type.48
  101.9 0.1 fusion.6
  101.9 3.5 %collective-permute-start.9 = (bf16[128,512]{1,0:T(8,128)(2,1)S(1)}, bf16[128,512]{1,0:T(8,128)(2,1)S(1)}, u32[]{:S(2)}, u32[]{:S(2)}) collective-permute-start(bf16[128,512]{1,0:T(8,128)(2,1)S(1)} %fusion.6), channel_id=1, source_target_pairs={{0,8},{4,12},{8,0},{12,4},{1,9},{5,13},{9,1},{13,5},{2,10},{6,14},... | collective-permute-start | bytes 393224 | tf_op jit(solution)/shard_map/ppermute | solution.py:97
  105.4 0.4 collective-permute-done.11
  105.8 0.1 fusion.3
  105.8 1.8 %collective-permute-start.12 = (bf16[128,512]{1,0:T(8,128)(2,1)S(1)}, bf16[128,512]{1,0:T(8,128)(2,1)S(1)}, u32[]{:S(2)}, u32[]{:S(2)}) collective-permute-start(bf16[128,512]{1,0:T(8,128)(2,1)S(1)} %fusion.3), channel_id=1, source_target_pairs={{0,8},{4,12},{8,0},{12,4},{1,9},{5,13},{9,1},{13,5},{2,10},{6,14},... | collective-permute-start | bytes 393224 | tf_op jit(solution)/shard_map/ppermute | solution.py:97
  107.7 0.9 collective-permute-done.10
  108.6 0.1 slice_add_fusion.1
  108.7 4.1 %collective-permute-done.9 = bf16[128,512]{1,0:T(8,128)(2,1)S(1)} collective-permute-done((bf16[128,512]{1,0:T(8,128)(2,1)S(1)}, bf16[128,512]{1,0:T(8,128)(2,1)S(1)}, u32[]{:S(2)}, u32[]{:S(2)}) %collective-permute-start.9) | collective-permute-done | bytes 131104 | tf_op jit(solution)/shard_map/ppermute | solution.py:97
  112.8 4.9 %fresh_attend.2.rest_0_ = bf16[8192,128]{1,0:T(8,128)(2,1)} custom-call(s32[1]{0:T(128)S(6)} %copy.13.length_ref, bf16[8192,128]{1,0:T(8,128)(2,1)S(1)} %bitcast.26, f32[128,4096]{1,0:T(8,128)S(1)} %get-tuple-element.37.acc_ref, f32[8,4096]{1,0:T(8,128)S(1)} %get-tuple-element.38.stat_ref, bf16[128,512]{1,0:T(8,128)(2,1)S(1)} %fusion.4.fresh_ref), custom_call_target="tpu_custom_call" | custom-call | flops 99999997952 | bytes 1 | tf_op jit(solution)/shard_map/fresh_attend/pallas_call | solution.py:419
  117.9 5.6 %fresh_attend.3 = bf16[8192,128]{1,0:T(8,128)(2,1)} custom-call(s32[1]{0:T(128)S(6)} %copy.13.length_ref, bf16[8192,128]{1,0:T(8,128)(2,1)S(1)} %bitcast.27, f32[128,4096]{1,0:T(8,128)S(1)} %get-tuple-element.33.acc_ref, f32[8,4096]{1,0:T(8,128)S(1)} %get-tuple-element.34.stat_ref, ...), custom_call_target="tpu_custom_call", output_to_operand_aliasing={{}: (5, {})} | custom-call | flops 99999997952 | bytes 1 | tf_op jit(solution)/shard_map/fresh_attend/pallas_call | solution.py:419
  (33 shorter events, 0.2 us)
Async XLA Ops:
  0.1 1.6 %copy-start.1 = (bf16[8,128,4,1,256]{4,2,3,1,0:T(4,128)(2,1)S(1)}, bf16[8,128,4,1,256]{4,2,3,1,0:T(4,128)(2,1)}, u32[]{:S(2)}) copy-start(bf16[8,128,4,1,256]{4,2,3,1,0:T(4,128)(2,1)} %param.11) | copy-start | bytes 6291460
  1.7 8.1 %copy-start = (bf16[256,4096]{1,0:T(8,128)(2,1)S(1)}, bf16[256,4096]{1,0:T(8,128)(2,1)}, u32[]{:S(2)}) copy-start(bf16[256,4096]{1,0:T(8,128)(2,1)} %refs_2_.1) | copy-start | bytes 6291460
  5.8 1.0 copy-start.8
  6.8 39.0 %collective-permute-start = (bf16[8,128,512]{2,1,0:T(8,128)(2,1)}, bf16[8,128,512]{2,1,0:T(8,128)(2,1)}, u32[]{:S(2)}, u32[]{:S(2)}) collective-permute-start(bf16[8,128,512]{2,1,0:T(8,128)(2,1)} %get-tuple-element.28), channel_id=1, source_target_pairs={{0,2},{2,0},{1,3},{3,1},{4,6},{6,4},{5,7},{7,5},{8,10},{10,8},{9,1... | collective-permute-start | bytes 3145736 | tf_op jit(solution)/shard_map/ppermute | solution.py:93
  10.8 14.3 %collective-permute-start.3 = (bf16[256,1024]{1,0:T(8,128)(2,1)}, bf16[256,1024]{1,0:T(8,128)(2,1)S(1)}, u32[]{:S(2)}, u32[]{:S(2)}) collective-permute-start(bf16[256,1024]{1,0:T(8,128)(2,1)} %get-tuple-element.50), channel_id=1, source_target_pairs={{0,4},{4,0},{8,12},{12,8},{1,5},{5,1},{9,13},{13,9},{2,6},{6,2},{1... | collective-permute-start | bytes 1572872 | tf_op jit(solution)/shard_map/ppermute | solution.py:97
  12.4 26.8 %collective-permute-start.4 = (bf16[256,1024]{1,0:T(8,128)(2,1)}, bf16[256,1024]{1,0:T(8,128)(2,1)S(1)}, u32[]{:S(2)}, u32[]{:S(2)}) collective-permute-start(bf16[256,1024]{1,0:T(8,128)(2,1)} %get-tuple-element.49), channel_id=1, source_target_pairs={{0,12},{4,8},{8,4},{12,0},{1,13},{5,9},{9,5},{13,1},{2,14},{6,10},... | collective-permute-start | bytes 1572872 | tf_op jit(solution)/shard_map/ppermute | solution.py:97
  15.7 44.7 %collective-permute-start.1 = (bf16[256,1024]{1,0:T(8,128)(2,1)}, bf16[256,1024]{1,0:T(8,128)(2,1)}, u32[]{:S(2)}, u32[]{:S(2)}) collective-permute-start(bf16[256,1024]{1,0:T(8,128)(2,1)} %constant_dynamic-slice_fusion.2), channel_id=1, source_target_pairs={{0,8},{4,12},{8,0},{12,4},{1,9},{5,13},{9,1},{13,5},{2,10},{6,14},... | collective-permute-start | bytes 1572872 | tf_op jit(solution)/shard_map/ppermute | solution.py:97
  15.8 1.6 %copy-start.2 = (bf16[1,1,1024,4,2,128]{5,4,3,2,1,0:T(2,128)(2,1)S(1)}, bf16[1,1,1024,4,2,128]{5,4,3,2,1,0:T(2,128)(2,1)}, u32[]{:S(2)}) copy-start(bf16[1,1,1024,4,2,128]{5,4,3,2,1,0:T(2,128)(2,1)} %param.8) | copy-start | bytes 6291460
  17.4 1.6 %copy-start.3 = (bf16[1,1,1024,4,2,128]{5,4,3,2,1,0:T(2,128)(2,1)S(1)}, bf16[1,1,1024,4,2,128]{5,4,3,2,1,0:T(2,128)(2,1)}, u32[]{:S(2)}) copy-start(bf16[1,1,1024,4,2,128]{5,4,3,2,1,0:T(2,128)(2,1)} %param.9) | copy-start | bytes 6291460
  21.5 21.4 %copy-start.6 = (bf16[2,2,1024,512]{3,2,1,0:T(8,128)(2,1)}, bf16[2,2,1024,512]{3,2,1,0:T(8,128)(2,1)S(1)}, u32[]{:S(2)}) copy-start(bf16[2,2,1024,512]{3,2,1,0:T(8,128)(2,1)S(1)} %arrange_weights.1.refs_1_.refs_3_) | copy-start | bytes 12582916
  42.8 2.9 %copy-start.5 = (s32[1,8]{1,0:T(1,128)S(1)}, s32[1,8]{1,0:T(1,128)}, u32[]{:S(2)}) copy-start(s32[1,8]{1,0:T(1,128)} %param.12) | copy-start | bytes 100
  42.8 2.9 %copy-start.9 = (bf16[8,128,512]{2,1,0:T(8,128)(2,1)S(1)}, bf16[8,128,512]{2,1,0:T(8,128)(2,1)}, u32[]{:S(2)}) copy-start(bf16[8,128,512]{2,1,0:T(8,128)(2,1)} %copy-done.8) | copy-start | bytes 3145732
  42.8 22.8 %collective-permute-start.5 = (bf16[768,1024]{1,0:T(8,128)(2,1)}, bf16[768,1024]{1,0:T(8,128)(2,1)}, u32[]{:S(2)}, u32[]{:S(2)}) collective-permute-start(bf16[768,1024]{1,0:T(8,128)(2,1)} %project.7), channel_id=1, source_target_pairs={{0,1},{1,0},{2,3},{3,2},{4,5},{5,4},{6,7},{7,6},{8,9},{9,8},{10,11... | collective-permute-start | bytes 4718600 | tf_op jit(solution)/shard_map/ppermute | solution.py:93
  45.8 2.2 %copy-start.4 = (bf16[256,2,1,2048]{3,1,2,0:T(2,128)(2,1)S(1)}, bf16[256,2,1,2048]{3,1,2,0:T(2,128)(2,1)}, u32[]{:S(2)}) copy-start(bf16[256,2,1,2048]{3,1,2,0:T(2,128)(2,1)} %param.10) | copy-start | bytes 6291460
  47.9 8.3 %copy-start.10 = (bf16[272,1024]{1,0:T(8,128)(2,1)}, bf16[272,1024]{1,0:T(8,128)(2,1)S(1)}, u32[]{:S(2)}) copy-start(bf16[272,1024]{1,0:T(8,128)(2,1)S(1)} %get-tuple-element.32.values) | copy-start | bytes 1671172
  47.9 8.3 %copy-start.12 = (bf16[1024,256]{1,0:T(8,128)(2,1)}, bf16[1024,256]{1,0:T(8,128)(2,1)S(1)}, u32[]{:S(2)}) copy-start(bf16[1024,256]{1,0:T(8,128)(2,1)S(1)} %get-tuple-element.35.keys) | copy-start | bytes 1572868
  47.9 12.4 %copy-start.7 = (bf16[2,2,1024,512]{3,2,1,0:T(8,128)(2,1)S(1)}, bf16[2,2,1024,512]{3,2,1,0:T(8,128)(2,1)}, u32[]{:S(2)}) copy-start(bf16[2,2,1024,512]{3,2,1,0:T(8,128)(2,1)} %copy-done.6) | copy-start | bytes 12582916
  62.9 5.6 %collective-permute-start.2 = (bf16[256,1024]{1,0:T(8,128)(2,1)S(1)}, bf16[256,1024]{1,0:T(8,128)(2,1)S(1)}, u32[]{:S(2)}, u32[]{:S(2)}) collective-permute-start(bf16[256,1024]{1,0:T(8,128)(2,1)S(1)} %project.5), channel_id=1, source_target_pairs={{0,1},{1,0},{2,3},{3,2},{4,5},{5,4},{6,7},{7,6},{8,9},{9,8},{10,11... | collective-permute-start | bytes 1572872 | tf_op jit(solution)/shard_map/ppermute | solution.py:93
  67.9 14.8 %collective-permute-start.6 = (bf16[512,512]{1,0:T(8,128)(2,1)S(1)}, bf16[512,512]{1,0:T(8,128)(2,1)S(1)}, u32[]{:S(2)}, u32[]{:S(2)}) collective-permute-start(bf16[512,512]{1,0:T(8,128)(2,1)S(1)} %slice.71), channel_id=1, source_target_pairs={{0,2},{2,0},{1,3},{3,1},{4,6},{6,4},{5,7},{7,5},{8,10},{10,8},{9,1... | collective-permute-start | bytes 1572872 | tf_op jit(solution)/shard_map/ppermute | solution.py:93
  68.7 22.5 %copy-start.11 = (bf16[272,1024]{1,0:T(8,128)(2,1)S(1)}, bf16[272,1024]{1,0:T(8,128)(2,1)}, u32[]{:S(2)}) copy-start(bf16[272,1024]{1,0:T(8,128)(2,1)} %copy-done.10) | copy-start | bytes 1671172
  68.8 22.5 %copy-start.13 = (bf16[1024,256]{1,0:T(8,128)(2,1)S(1)}, bf16[1024,256]{1,0:T(8,128)(2,1)}, u32[]{:S(2)}) copy-start(bf16[1024,256]{1,0:T(8,128)(2,1)} %copy-done.12) | copy-start | bytes 1572868
  68.8 33.1 %collective-permute-start.8 = (bf16[128,512]{1,0:T(8,128)(2,1)S(1)}, bf16[128,512]{1,0:T(8,128)(2,1)S(1)}, u32[]{:S(2)}, u32[]{:S(2)}) collective-permute-start(bf16[128,512]{1,0:T(8,128)(2,1)S(1)} %get-tuple-element.52), channel_id=1, source_target_pairs={{0,2},{2,0},{1,3},{3,1},{4,6},{6,4},{5,7},{7,5},{8,10},{10,8},{9,1... | collective-permute-start | bytes 393224 | tf_op jit(solution)/shard_map/ppermute | solution.py:93
  82.9 18.8 %collective-permute-start.7 = (bf16[512,512]{1,0:T(8,128)(2,1)S(1)}, bf16[512,512]{1,0:T(8,128)(2,1)S(1)}, u32[]{:S(2)}, u32[]{:S(2)}) collective-permute-start(bf16[512,512]{1,0:T(8,128)(2,1)S(1)} %fusion), channel_id=1, source_target_pairs={{0,4},{4,0},{8,12},{12,8},{1,5},{5,1},{9,13},{13,9},{2,6},{6,2},{1... | collective-permute-start | bytes 1572872 | tf_op jit(solution)/shard_map/ppermute | solution.py:97
  99.5 6.2 %collective-permute-start.11 = (bf16[128,512]{1,0:T(8,128)(2,1)S(1)}, bf16[128,512]{1,0:T(8,128)(2,1)S(1)}, u32[]{:S(2)}, u32[]{:S(2)}) collective-permute-start(bf16[128,512]{1,0:T(8,128)(2,1)S(1)} %get-tuple-element.51), channel_id=1, source_target_pairs={{0,2},{2,0},{1,3},{3,1},{4,6},{6,4},{5,7},{7,5},{8,10},{10,8},{9,1... | collective-permute-start | bytes 393224 | tf_op jit(solution)/shard_map/ppermute | solution.py:93
  100.2 8.4 %collective-permute-start.10 = (bf16[256,512]{1,0:T(8,128)(2,1)S(1)}, bf16[256,512]{1,0:T(8,128)(2,1)S(1)}, u32[]{:S(2)}, u32[]{:S(2)}) collective-permute-start(bf16[256,512]{1,0:T(8,128)(2,1)S(1)} %slice.75), channel_id=1, source_target_pairs={{0,2},{2,0},{1,3},{3,1},{4,6},{6,4},{5,7},{7,5},{8,10},{10,8},{9,1... | collective-permute-start | bytes 786440 | tf_op jit(solution)/shard_map/ppermute | solution.py:93
  101.9 10.9 %collective-permute-start.9 = (bf16[128,512]{1,0:T(8,128)(2,1)S(1)}, bf16[128,512]{1,0:T(8,128)(2,1)S(1)}, u32[]{:S(2)}, u32[]{:S(2)}) collective-permute-start(bf16[128,512]{1,0:T(8,128)(2,1)S(1)} %fusion.6), channel_id=1, source_target_pairs={{0,8},{4,12},{8,0},{12,4},{1,9},{5,13},{9,1},{13,5},{2,10},{6,14},... | collective-permute-start | bytes 393224 | tf_op jit(solution)/shard_map/ppermute | solution.py:97
  105.8 12.0 %collective-permute-start.12 = (bf16[128,512]{1,0:T(8,128)(2,1)S(1)}, bf16[128,512]{1,0:T(8,128)(2,1)S(1)}, u32[]{:S(2)}, u32[]{:S(2)}) collective-permute-start(bf16[128,512]{1,0:T(8,128)(2,1)S(1)} %fusion.3), channel_id=1, source_target_pairs={{0,8},{4,12},{8,0},{12,4},{1,9},{5,13},{9,1},{13,5},{2,10},{6,14},... | collective-permute-start | bytes 393224 | tf_op jit(solution)/shard_map/ppermute | solution.py:97

commit v6 on v5

--- a/solution.py
+++ b/solution.py
@@ -9,7 +9,7 @@
 from jax.sharding import PartitionSpec as P
 
 CHUNKS = 2
-VMEM_BYTES = 32 * 1024 * 1024
+VMEM_BYTES = 24 * 1024 * 1024
 LONG = pl.CostEstimate(flops=10**11, bytes_accessed=1, transcendentals=0)
 
 
@@ -97,6 +97,10 @@
     return lax.ppermute(array, axis, [(i, i ^ bits) for i in range(lax.axis_size(axis))])
 
 
+def after(first, second):
+    return lax.optimization_barrier((first, second))
+
+
 def unit_index(shape, unit):
     row = lax.broadcasted_iota(jnp.int32, shape, 0)
     if unit & (unit - 1):
@@ -217,28 +221,28 @@
 
 def project_kernel(place_ref, *refs):
     token_refs, (weight_ref, out_ref, stacked) = refs[:-3], refs[-3:]
-    rows = token_refs[0].shape[0]
 
     @pl.when(pl.program_id(0) == 0)
     def _():
-        for index, token_ref in enumerate(token_refs):
-            stacked[index * rows : (index + 1) * rows, :] = token_ref[...]
-
-    out_ref[...] = jnp.dot(
+        at = 0
+        for token_ref in token_refs:
+            rows = token_ref.shape[0]
+            stacked[at : at + rows, :] = token_ref[...]
+            at += rows
+
+    out_ref[0] = jnp.dot(
         stacked[...], weight_ref[0, 0], preferred_element_type=jnp.float32
     ).astype(out_ref.dtype)
 
 
 def project(place, blocks, weights, head_step, out_dtype):
     head_count, ctx_count, depth, width = weights.shape
-    rows = blocks[0].shape[0]
-    row_total = rows * len(blocks)
-    columns = ctx_count * width
+    row_total = sum(block.shape[0] for block in blocks)
 
     def block_spec(block):
         if block.shape[1] == depth:
-            return pl.BlockSpec((rows, depth), lambda j, place: (0, 0))
-        return pl.BlockSpec((rows, depth), lambda j, place: (0, place[0]))
+            return pl.BlockSpec(block.shape, lambda j, place: (0, 0))
+        return pl.BlockSpec((block.shape[0], depth), lambda j, place: (0, place[0]))
 
     return pl.pallas_call(
         project_kernel,
@@ -257,10 +261,10 @@
                     ),
                 )
             ],
-            out_specs=pl.BlockSpec((row_total, width), lambda j, place: (0, j)),
+            out_specs=pl.BlockSpec((1, row_total, width), lambda j, place: (j, 0, 0)),
             scratch_shapes=[pltpu.VMEM((row_total, depth), weights.dtype)],
         ),
-        out_shape=jax.ShapeDtypeStruct((row_total, columns), out_dtype),
+        out_shape=jax.ShapeDtypeStruct((ctx_count, row_total, width), out_dtype),
         compiler_params=params(),
         cost_estimate=LONG,
         name="project",
@@ -363,9 +367,9 @@
 
 
 def fresh_kernel(
-    scale, heads, per_token, first_row, length_ref, query_ref, acc_ref, stat_ref, fresh_ref, *rest
+    scale, heads, per_token, first_row, parts, length_ref, query_ref, acc_ref, stat_ref, *rest
 ):
-    out_ref, values, mask = rest[-3:]
+    out_ref, keys, values, mask = rest[-4:]
     rows, width = query_ref.shape
     wide = heads * width
     step = pl.program_id(0)
@@ -374,14 +378,19 @@
     def _():
         mask[...] = head_mask(mask.shape, heads)
         values[wide:, :] = jnp.ones_like(values[wide:, :])
-        values[:wide, :] = fresh_ref[:, wide:].astype(jnp.float32).T.astype(jnp.bfloat16)
+        for index in range(parts):
+            one, other = rest[2 * index], rest[2 * index + 1]
+            here = slice(index * one.shape[0], (index + 1) * one.shape[0])
+            fresh = (one[...].astype(jnp.float32) + other[...]).astype(jnp.bfloat16)
+            keys[here, :] = fresh[:, :wide]
+            values[:wide, here] = fresh[:, wide:].astype(jnp.float32).T.astype(jnp.bfloat16)
 
     part_rows = mask.shape[0]
     half = stat_ref.shape[0] // 2
     for part in range(rows // part_rows):
         here = slice(part * part_rows, (part + 1) * part_rows)
         query_block = jnp.concatenate([query_ref[here, :]] * heads, 1) * mask[...]
-        scores = dot_queries(fresh_ref[:, :wide], query_block) * scale
+        scores = dot_queries(keys[...], query_block) * scale
         row = part * part_rows + lax.broadcasted_iota(jnp.int32, (1, part_rows), 1)
         token = first_row + step * (rows // per_token) + (
             row // per_token if per_token & (per_token - 1) else row >> (per_token.bit_length() - 1)
@@ -398,27 +407,28 @@
         out_ref[here, :] = result.T.astype(out_ref.dtype)
 
 
-def fresh_attend(length, query_rows, acc, stat, fresh, earlier, piece, scale, heads, per_token):
+def fresh_attend(length, query_rows, acc, stat, parts, earlier, chunk, scale, heads, per_token):
     row_total, width = query_rows.shape
-    piece_rows = row_total // CHUNKS
-    rows = min(1024, piece_rows)
-    steps = piece_rows // rows
-    block = pl.BlockSpec((rows, width), lambda i, length: (piece * steps + i, 0))
+    chunk_rows = row_total // CHUNKS
+    rows = min(1024, chunk_rows)
+    steps = chunk_rows // rows
+    block = pl.BlockSpec((rows, width), lambda i, length: (chunk * steps + i, 0))
+    terms = [term for pair in parts for term in pair]
+    key_count = sum(pair[0].shape[0] for pair in parts)
     in_specs = [
         block,
         pl.BlockSpec((width, rows), lambda i, length: (0, i)),
         pl.BlockSpec((stat.shape[0], rows), lambda i, length: (0, i)),
-        pl.BlockSpec(fresh.shape, lambda i, length: (0, 0)),
-    ]
-    operands = [length, query_rows, acc, stat, fresh]
+    ] + [pl.BlockSpec(term.shape, lambda i, length: (0, 0)) for term in terms]
+    operands = [length, query_rows, acc, stat, *terms]
     aliases = {}
     if earlier is not None:
         in_specs.append(pl.BlockSpec(memory_space=pl.ANY))
+        aliases = {len(operands): 0}
         operands.append(earlier)
-        aliases = {5: 0}
     return pl.pallas_call(
         functools.partial(
-            fresh_kernel, scale, heads, per_token, piece * (piece_rows // per_token)
+            fresh_kernel, scale, heads, per_token, chunk * (chunk_rows // per_token), len(parts)
         ),
         grid_spec=pltpu.PrefetchScalarGridSpec(
             num_scalar_prefetch=1,
@@ -426,7 +436,8 @@
             in_specs=in_specs,
             out_specs=block,
             scratch_shapes=[
-                pltpu.VMEM((heads * width + 16, fresh.shape[0]), jnp.bfloat16),
+                pltpu.VMEM((key_count, heads * width), jnp.bfloat16),
+                pltpu.VMEM((heads * width + 16, key_count), jnp.bfloat16),
                 pltpu.VMEM((min(512, rows), heads * width), jnp.bfloat16),
             ],
         ),
@@ -453,89 +464,82 @@
     rows = token_count // CHUNKS
     scale = math.log2(math.e) / math.sqrt(width)
 
-    def leaving(bits):
+    def leaving(bits, first, count):
         start = (batch_at ^ bits) * depth
-        return lax.dynamic_slice(tokens, (0, start), (token_count, depth))
+        return lax.dynamic_slice(tokens, (first, start), (count, depth))
 
     top = batch_count // 2
     steps = [bits for bits in range(1, batch_count) if bits != top]
-    near = [trade(leaving(bits), "batch", bits) for bits in steps]
+    pieces = [leaving(bits, 0, token_count) for bits in steps] + [leaving(top, 0, rows)]
+    pieces, prefix_pool = after(pieces, prefix_pool)
+    arrived = [trade(piece, "batch", bits) for piece, bits in zip(pieces, [*steps, top])]
+    arrived, last = after(arrived, leaving(top, rows, rows))
+    last = trade(last, "batch", top)
 
     pools = arrange_pool(place, prefix_pool, ctx_count, heads)
-    pools, key_weight, value_weight, tokens = lax.optimization_barrier(
-        (pools, key_weight, value_weight, tokens)
-    )
-    last = trade(leaving(top), "batch", top)
+    pools, (key_weight, value_weight) = after(pools, (key_weight, value_weight))
     pools = [shift(part, "ctx", step) if step else part for step, part in enumerate(pools)]
 
     weights = arrange_weights(key_weight, value_weight, ctx_count, heads, head_count)
 
     query_rows = queries.reshape(token_count, heads, group, width)
     query_rows = query_rows.transpose(0, 2, 1, 3).reshape(-1, width)
-    cols = weights.shape[3]
-
     def projected(blocks):
         terms = [
             shift(project(place, blocks, weights, step, jnp.bfloat16), "head", step)
             for step in range(1, head_count)
         ]
         total = project(place, blocks, weights, 0, jnp.float32)
-        total = sum((term.astype(jnp.float32) for term in terms), total)
-        others = [
-            total[:, step * cols : (step + 1) * cols].astype(jnp.bfloat16)
-            for step in range(1, ctx_count)
-        ]
-        return total[:, :cols], others
-
-    def spread(others):
-        return [shift(other, "ctx", step + 1) for step, other in enumerate(others)]
+
+        def of(step):
+            return sum((term[step].astype(jnp.float32) for term in terms), total[step])
+
+        return of(0), [of(step).astype(jnp.bfloat16) for step in range(1, ctx_count)]
+
+    def spread(others, here=slice(None)):
+        return [shift(other[here], "ctx", step + 1) for step, other in enumerate(others)]
 
     def summed(mine, others):
         return sum((other.astype(jnp.float32) for other in others), mine)
 
-    def after(first, second):
-        return lax.optimization_barrier((first, second))[1]
-
-    def halves(block):
-        return [block[i * rows : (i + 1) * rows] for i in range(CHUNKS)]
-
-    early, others = projected([*near, tokens])
-    pools = after(others, pools)
-    own_at = len(near) * token_count
+    mine, others = projected([*arrived, tokens])
+    far, near = slice(0, len(steps) * token_count), slice(len(steps) * token_count, None)
+    far_others = spread(others, far)
+    others, pools = after(others, pools)
+    near_others = spread(others, near)
     keys, values = pick_blocks(place, block_table[0], pools, heads)
-    if near:
-        away = summed(early[:own_at], spread([other[:own_at] for other in others]))
-        away = trade(away.astype(jnp.bfloat16), "batch", 1).astype(jnp.float32)
-    home = summed(early[own_at:], spread([other[own_at:] for other in others]))
     states = [prefix_attend(query_rows, keys, values, 0, scale, heads)]
-    last = after(states[0], last)
-
-    mine, others = projected([last])
-    keys, values = after(others, (keys, values))
-    for chunk in range(1, CHUNKS):
-        states.append(prefix_attend(query_rows, keys, values, chunk, scale, heads))
-    mine = halves(mine)
-    others = [spread(list(o)) for o in zip(*(halves(other) for other in others))]
-    if near:
-        home = home + away[:token_count]
-        mine = [a + b for a, b in zip(mine, halves(away[token_count:]))]
-    home = halves(home)
-    parts = []
+    states[0], last = after(states[0], last)
+
+    last_mine, last_others = projected([last])
+    last_others, (keys, values) = after(last_others, (keys, values))
+    last_others = spread(last_others)
+    states.append(prefix_attend(query_rows, keys, values, 1, scale, heads))
+
+    mine = [mine[far], summed(mine[near], near_others)]
+    away, home = mine[1][:rows], mine[1][rows:]
+    if steps:
+        far = trade(summed(mine[0], far_others).astype(jnp.bfloat16), "batch", 1)
+        home = home + far[:token_count].astype(jnp.float32)
+        away = away + far[token_count : token_count + rows].astype(jnp.float32)
+        far, last_others = after(far, last_others)
+        last_mine = last_mine + far[token_count + rows :].astype(jnp.float32)
+    away = [away, summed(last_mine, last_others)]
+    away = [trade(part.astype(jnp.bfloat16), "batch", top) for part in away]
+    parts = [(away[0], home[:rows]), (away[1], home[rows:])]
+
+    result = None
     for chunk in range(CHUNKS):
-        if parts:
-            others[chunk] = after(parts[-1], others[chunk])
-        parts.append(summed(mine[chunk], others[chunk]).astype(jnp.bfloat16))
-    parts = [trade(part, "batch", top) for part in parts]
-
-    result = None
-    fresh_parts = []
-    for chunk in range(CHUNKS):
-        if chunk:
-            parts[chunk] = after(result, parts[chunk])
-        fresh_parts.append((parts[chunk].astype(jnp.float32) + home[chunk]).astype(jnp.bfloat16))
-        fresh = jnp.concatenate(fresh_parts, 0)
         result = fresh_attend(
-            lengths, query_rows, *states[chunk], fresh, result, chunk, scale, heads, per_token
+            lengths,
+            query_rows,
+            *states[chunk],
+            parts[: chunk + 1],
+            result,
+            chunk,
+            scale,
+            heads,
+            per_token,
         )
     result = result.reshape(token_count, group, heads, width).transpose(0, 2, 1, 3)
     return result.reshape(token_count, heads, 1, group * width)

time: 124 us -> 115 us (0.927)
  starting transfers between devices: 25.2 us -> 16.5 us
  local copies, waits for them, and re-layouts: 7.79 us -> 6.4 us
    ppermute x6 -> x7, waiting for transfers between devices: 25.3 us -> 39.2 us  [trade(): lax.ppermute(array, axis, [(i, i ^ bits) for i in range(lax.axis_size(axi...]
    ppermute x7 -> x6, waiting for transfers between devices: 13.7 us -> 0.02 us  [shift(): lax.ppermute(array, axis, [(i, (i + step) % count) for i in range(count)])]
    ppermute x6 -> x7, starting transfers between devices: 17.8 us -> 11.2 us  [trade(): lax.ppermute(array, axis, [(i, i ^ bits) for i in range(lax.axis_size(axi...]
    unnamed x28 -> x18, local copies, waits for them, and re-layouts: 5.8 us -> 0.04 us
    another operation x2 -> x0, other arithmetic: 2.43 us -> none
    dynamic_slice x2, local copies, waits for them, and re-layouts: 1.91 us -> 4.28 us  [leaving(): return lax.dynamic_slice(tokens, (first, start), (count, depth))]
    slice x3, local copies, waits for them, and re-layouts: 0.07 us -> 2.08 us  [the longest x2 2.05 us: spread(): other[here]]
    add x1 -> x3, other arithmetic: 0.13 us -> 2.13 us  [the longest x1 1.95 us: of(): return sum((term[step].astype(jnp.float32) for term in terms), total[step])]
  transfers between devices with their start and end apart: 13 -> 13, of which waited for: 7 -> 4; matrix products, arithmetic and copies ran while one was open for 4% -> 5% of each run, Pallas kernels for 31% -> 37%
where the time goes in v6:
time: 115 us
  Pallas kernels  48.5 us (42%)
  waiting for transfers between devices  39.2 us (34%)
  starting transfers between devices  16.5 us (14%)
  local copies, waits for them, and re-layouts  6.4 us (6%)
  other arithmetic  3.52 us (3%)
    ppermute x7, waiting for transfers between devices, trade(): lax.ppermute(array, axis, [(i, i ^ bits) for i in range(lax.axis_size(axi...  39.2 us
    pallas_call x2, Pallas kernels, prefix_attend(): pl.pallas_call(functools.partial(prefix_kernel, scale, heads), grid=(step...  16.5 us
    pallas_call x4, Pallas kernels, project(): pl.pallas_call(project_kernel, grid_spec=pltpu.PrefetchScalarGridSpec(num...  12.8 us
    ppermute x7, starting transfers between devices, trade(): lax.ppermute(array, axis, [(i, i ^ bits) for i in range(lax.axis_size(axi...  11.2 us
    pallas_call x2, Pallas kernels, fresh_attend(): pl.pallas_call(functools.partial(fresh_kernel, scale, heads, per_token, c...  10.6 us
    ppermute x6, starting transfers between devices, shift(): lax.ppermute(array, axis, [(i, (i + step) % count) for i in range(count)])  5.34 us
    dynamic_slice x2, local copies, waits for them, and re-layouts, leaving(): return lax.dynamic_slice(tokens, (first, start), (count, depth))  4.28 us
    pallas_call x1, Pallas kernels, arrange_pool(): pl.pallas_call(functools.partial(pool_kernel, ctx_count, heads), grid_spe...  4.1 us
  transfers between devices with their start and end apart: 13, of which 4 were waited for; matrix products, arithmetic and copies ran while one was open for 5% of the time, Pallas kernels for 37%

profile of v6, /device:TPU:0, one launch (start us, length us, event | category | flops | bytes accessed | tf_op | source)
XLA Modules:
  0.0 115.0 jit_solution(4232613639843729099)
XLA Ops:
  0.0 2.0 %constant_dynamic-slice_fusion.3 = (bf16[128,1024]{1,0:T(8,128)(2,1)}, bf16[128,1024]{1,0:T(8,128)(2,1)}) fusion(bf16[256,4096]{1,0:T(8,128)(2,1)} %refs_3_.3, s32[]{:T(128)S(6)} %select_n.12), kind=kLoop, calls=%fused_computation.24 | loop fusion | bytes 1048580 | tf_op jit(solution)/shard_map/dynamic_slice | solution.py:469
  2.0 2.3 %constant_dynamic-slice_fusion.1 = (bf16[256,1024]{1,0:T(8,128)(2,1)}, bf16[256,1024]{1,0:T(8,128)(2,1)}) fusion(bf16[256,4096]{1,0:T(8,128)(2,1)} %refs_3_.3, s32[]{:T(128)S(6)} %select_n.11, s32[]{:T(128)S(6)} %select_n.10), kind=kLoop, calls=%fused_computation.21 | loop fusion | bytes 2097160 | tf_op jit(solution)/shard_map/dynamic_slice | solution.py:469
  4.3 3.0 %collective-permute-start = (bf16[256,1024]{1,0:T(8,128)(2,1)}, bf16[256,1024]{1,0:T(8,128)(2,1)}, u32[]{:S(2)}, u32[]{:S(2)}) collective-permute-start(bf16[256,1024]{1,0:T(8,128)(2,1)} %get-tuple-element.36), channel_id=1, source_target_pairs={{0,4},{4,0},{8,12},{12,8},{1,5},{5,1},{9,13},{13,9},{2,6},{6,2},{1... | collective-permute-start | bytes 1572872 | tf_op jit(solution)/shard_map/ppermute | solution.py:97
  7.3 2.5 %collective-permute-start.1 = (bf16[256,1024]{1,0:T(8,128)(2,1)}, bf16[256,1024]{1,0:T(8,128)(2,1)}, u32[]{:S(2)}, u32[]{:S(2)}) collective-permute-start(bf16[256,1024]{1,0:T(8,128)(2,1)} %get-tuple-element.37), channel_id=1, source_target_pairs={{0,12},{4,8},{8,4},{12,0},{1,13},{5,9},{9,5},{13,1},{2,14},{6,10},... | collective-permute-start | bytes 1572872 | tf_op jit(solution)/shard_map/ppermute | solution.py:97
  9.8 0.1 collective-permute-start.2
  9.9 0.1 pad_add_fusion.place_ref
  10.0 4.1 %arrange_pool.1 = (bf16[8,128,512]{2,1,0:T(8,128)(2,1)S(1)}, bf16[8,128,512]{2,1,0:T(8,128)(2,1)}) custom-call(s32[3]{0:T(128)S(1)} %pad_add_fusion.place_ref, bf16[8,128,8,128]{3,2,1,0:T(8,128)(2,1)S(1)} %bitcast.44), custom_call_target="tpu_custom_call" | custom-call | flops 99999997952 | bytes 1 | tf_op jit(solution)/shard_map/arrange_pool/pallas_call | solution.py:206
  14.1 1.5 %collective-permute-start.4 = (bf16[8,128,512]{2,1,0:T(8,128)(2,1)}, bf16[8,128,512]{2,1,0:T(8,128)(2,1)}, u32[]{:S(2)}, u32[]{:S(2)}) collective-permute-start(bf16[8,128,512]{2,1,0:T(8,128)(2,1)} %get-tuple-element.48), channel_id=1, source_target_pairs={{0,2},{2,0},{1,3},{3,1},{4,6},{6,4},{5,7},{7,5},{8,10},{10,8},{9,1... | collective-permute-start | bytes 3145736 | tf_op jit(solution)/shard_map/ppermute | solution.py:93
  15.6 2.5 %arrange_weights.1.refs_4_.refs_1_ = bf16[2,2,1024,512]{3,2,1,0:T(8,128)(2,1)S(1)} custom-call(bf16[1024,8,128]{2,1,0:T(8,128)(2,1)S(1)} %bitcast.45, bf16[1024,8,128]{2,1,0:T(8,128)(2,1)S(1)} %bitcast.46), custom_call_target="tpu_custom_call" | custom-call | flops 99999997952 | bytes 1 | tf_op jit(solution)/shard_map/arrange_weights/pallas_call | solution.py:165
  18.7 25.6 %collective-permute-done.2.refs_2_ = bf16[128,1024]{1,0:T(8,128)(2,1)} collective-permute-done((bf16[128,1024]{1,0:T(8,128)(2,1)}, bf16[128,1024]{1,0:T(8,128)(2,1)}, u32[]{:S(2)}, u32[]{:S(2)}) %collective-permute-start.2) | collective-permute-done | bytes 262176 | tf_op jit(solution)/shard_map/ppermute | solution.py:97
  44.3 0.0 collective-permute-done.refs_0_
  44.3 0.0 collective-permute-done.1.refs_1_
  44.3 4.2 %project.5 = bf16[2,896,512]{2,1,0:T(8,128)(2,1)S(1)} custom-call(s32[3]{0:T(128)S(1)} %pad_add_fusion.place_ref, bf16[256,1024]{1,0:T(8,128)(2,1)} %collective-permute-done.refs_0_, bf16[256,1024]{1,0:T(8,128)(2,1)} %collective-permute-done.1.refs_1_, bf16[128,1024]{1,0:T(8,128)(2,1)} %collective-permute-done.2.refs_2_, bf16[256,4096]{1,0:T(8,128)(2,1)S(1)} %copy-done, ...), custom_call_target="tpu_custom_call" | custom-call | flops 99999997952 | bytes 1 | tf_op jit(solution)/shard_map/project/pallas_call | solution.py:247
  48.6 0.1 collective-permute-start.3
  48.6 4.2 %project.4 = f32[2,896,512]{2,1,0:T(8,128)S(1)} custom-call(s32[3]{0:T(128)S(1)} %pad_add_fusion.place_ref, bf16[256,1024]{1,0:T(8,128)(2,1)} %collective-permute-done.refs_0_, bf16[256,1024]{1,0:T(8,128)(2,1)} %collective-permute-done.1.refs_1_, bf16[128,1024]{1,0:T(8,128)(2,1)} %collective-permute-done.2.refs_2_, bf16[256,4096]{1,0:T(8,128)(2,1)S(1)} %copy-done, ...), custom_call_target="tpu_custom_call" | custom-call | flops 99999997952 | bytes 1 | tf_op jit(solution)/shard_map/project/pallas_call | solution.py:247
  52.8 0.0 copy-start.6
  52.9 0.1 collective-permute-start.5
  52.9 0.0 collective-permute-done.3
  52.9 1.9 %slice_add_fusion = (f32[1,896,512]{2,1,0:T(8,128)}, bf16[1,896,512]{2,1,0:T(8,128)(2,1)S(1)}) fusion(f32[2,896,512]{2,1,0:T(8,128)S(1)} %project.4, bf16[2,896,512]{2,1,0:T(8,128)(2,1)S(1)} %collective-permute-done.3), kind=kLoop, calls=%fused_computation | loop fusion | flops 2293760 | bytes 8257536 | tf_op jit(solution)/shard_map/add | solution.py:495
  54.9 0.9 slice_bitcast_fusion.2
  55.8 1.5 %collective-permute-start.8 = (bf16[512,512]{1,0:T(8,128)(2,1)}, bf16[512,512]{1,0:T(8,128)(2,1)}, u32[]{:S(2)}, u32[]{:S(2)}) collective-permute-start(bf16[512,512]{1,0:T(8,128)(2,1)} %slice_bitcast_fusion.2), channel_id=1, source_target_pairs={{0,2},{2,0},{1,3},{3,1},{4,6},{6,4},{5,7},{7,5},{8,10},{10,8},{9,1... | collective-permute-start | bytes 1572872 | tf_op jit(solution)/shard_map/ppermute | solution.py:93
  57.3 0.0 collective-permute-done.4.refs_1_
  57.3 2.1 %pick_blocks.1 = (bf16[1024,256]{1,0:T(8,128)(2,1)S(1)}, bf16[272,1024]{1,0:T(8,128)(2,1)S(1)}) custom-call(s32[3]{0:T(128)S(1)} %pad_add_fusion.place_ref, s32[8]{0:T(128)S(1)} %bitcast.51, bf16[8,128,512]{2,1,0:T(8,128)(2,1)S(1)} %get-tuple-element.49.refs_0_, bf16[8,128,512]{2,1,0:T(8,128)(2,1)} %collective-permute-done.4.refs_1_), custom_call_target="tpu_custom_call" | custom-call | flops 99999997952 | bytes 1 | tf_op jit(solution)/shard_map/pick_blocks/pallas_call | solution.py:299
  59.4 8.2 %prefix_attend.2 = (f32[128,4096]{1,0:T(8,128)S(1)}, f32[8,4096]{1,0:T(8,128)S(1)}) custom-call(bf16[8192,128]{1,0:T(8,128)(2,1)S(1)} %bitcast.47, bf16[1024,256]{1,0:T(8,128)(2,1)S(1)} %get-tuple-element.57.keys, bf16[272,1024]{1,0:T(8,128)(2,1)S(1)} %get-tuple-element.58.values), custom_call_target="tpu_custom_call" | custom-call | flops 99999997952 | bytes 1 | tf_op jit(solution)/shard_map/prefix_attend/pallas_call | solution.py:346
  67.7 0.8 collective-permute-done.5.refs_0_
  68.5 2.2 %project.7 = bf16[2,128,512]{2,1,0:T(8,128)(2,1)S(1)} custom-call(s32[3]{0:T(128)S(1)} %pad_add_fusion.place_ref, bf16[128,1024]{1,0:T(8,128)(2,1)} %collective-permute-done.5.refs_0_, bf16[2,2,1024,512]{3,2,1,0:T(8,128)(2,1)S(1)} %arrange_weights.1.refs_4_.refs_1_), custom_call_target="tpu_custom_call" | custom-call | flops 99999997952 | bytes 1 | tf_op jit(solution)/shard_map/project/pallas_call | solution.py:247
  70.6 0.0 copy-start.7
  70.7 0.1 collective-permute-start.6
  70.8 2.2 %project.6 = f32[2,128,512]{2,1,0:T(8,128)S(1)} custom-call(s32[3]{0:T(128)S(1)} %pad_add_fusion.place_ref, bf16[128,1024]{1,0:T(8,128)(2,1)} %collective-permute-done.5.refs_0_, bf16[2,2,1024,512]{3,2,1,0:T(8,128)(2,1)S(1)} %arrange_weights.1.refs_4_.refs_1_), custom_call_target="tpu_custom_call" | custom-call | flops 99999997952 | bytes 1 | tf_op jit(solution)/shard_map/project/pallas_call | solution.py:247
  73.0 0.0 copy-start.5
  73.0 1.2 %slice.74 = bf16[384,512]{1,0:T(8,128)(2,1)S(1)} slice(bf16[896,512]{1,0:T(8,128)(2,1)} %bitcast.52), slice={[512:896], [0:512]} | slice | bytes 786432 | tf_op jit(solution)/shard_map/slice | solution.py:500
  74.2 1.5 %collective-permute-start.7 = (bf16[384,512]{1,0:T(8,128)(2,1)S(1)}, bf16[384,512]{1,0:T(8,128)(2,1)S(1)}, u32[]{:S(2)}, u32[]{:S(2)}) collective-permute-start(bf16[384,512]{1,0:T(8,128)(2,1)S(1)} %slice.74), channel_id=1, source_target_pairs={{0,2},{2,0},{1,3},{3,1},{4,6},{6,4},{5,7},{7,5},{8,10},{10,8},{9,1... | collective-permute-start | bytes 1179656 | tf_op jit(solution)/shard_map/ppermute | solution.py:93
  75.7 0.0 collective-permute-done.6
  75.7 0.7 collective-permute-start.11
  76.4 0.0 collective-permute-done.8
  76.4 1.2 %fusion.2 = bf16[512,512]{1,0:T(8,128)(2,1)S(1)} fusion(f32[1,896,512]{2,1,0:T(8,128)S(1)} %copy-done.7, bf16[512,512]{1,0:T(8,128)(2,1)} %collective-permute-done.8), kind=kLoop, calls=%fused_computation.5 | loop fusion | flops 786432 | bytes 2097152 | tf_op jit(solution)/shard_map/convert_element_type | solution.py:522
  77.6 2.4 %collective-permute-start.9 = (bf16[512,512]{1,0:T(8,128)(2,1)S(1)}, bf16[512,512]{1,0:T(8,128)(2,1)S(1)}, u32[]{:S(2)}, u32[]{:S(2)}) collective-permute-start(bf16[512,512]{1,0:T(8,128)(2,1)S(1)} %fusion.2), channel_id=1, source_target_pairs={{0,4},{4,0},{8,12},{12,8},{1,5},{5,1},{9,13},{13,9},{2,6},{6,2},{1... | collective-permute-start | bytes 1572872 | tf_op jit(solution)/shard_map/ppermute | solution.py:97
  80.0 8.2 %prefix_attend.3 = (f32[128,4096]{1,0:T(8,128)S(1)}, f32[8,4096]{1,0:T(8,128)S(1)}) custom-call(bf16[8192,128]{1,0:T(8,128)(2,1)S(1)} %bitcast.48, bf16[1024,256]{1,0:T(8,128)(2,1)S(1)} %get-tuple-element.57.keys, bf16[272,1024]{1,0:T(8,128)(2,1)S(1)} %get-tuple-element.58.values), custom_call_target="tpu_custom_call" | custom-call | flops 99999997952 | bytes 1 | tf_op jit(solution)/shard_map/prefix_attend/pallas_call | solution.py:346
  88.2 0.0 collective-permute-done.7
  88.2 0.1 fusion.3
  88.3 3.7 %collective-permute-done.9 = bf16[512,512]{1,0:T(8,128)(2,1)S(1)} collective-permute-done((bf16[512,512]{1,0:T(8,128)(2,1)S(1)}, bf16[512,512]{1,0:T(8,128)(2,1)S(1)}, u32[]{:S(2)}, u32[]{:S(2)}) %collective-permute-start.9) | collective-permute-done | bytes 524320 | tf_op jit(solution)/shard_map/ppermute | solution.py:97
  92.0 1.5 %collective-permute-start.10 = (bf16[128,512]{1,0:T(8,128)(2,1)S(1)}, bf16[128,512]{1,0:T(8,128)(2,1)S(1)}, u32[]{:S(2)}, u32[]{:S(2)}) collective-permute-start(bf16[128,512]{1,0:T(8,128)(2,1)S(1)} %fusion.8), channel_id=1, source_target_pairs={{0,8},{4,12},{8,0},{12,4},{1,9},{5,13},{9,1},{13,5},{2,10},{6,14},... | collective-permute-start | bytes 393224 | tf_op jit(solution)/shard_map/ppermute | solution.py:97
  93.6 0.1 fusion.7
  93.6 1.6 %collective-permute-start.12 = (bf16[128,512]{1,0:T(8,128)(2,1)S(1)}, bf16[128,512]{1,0:T(8,128)(2,1)S(1)}, u32[]{:S(2)}, u32[]{:S(2)}) collective-permute-start(bf16[128,512]{1,0:T(8,128)(2,1)S(1)} %fusion.7), channel_id=1, source_target_pairs={{0,8},{4,12},{8,0},{12,4},{1,9},{5,13},{9,1},{13,5},{2,10},{6,14},... | collective-permute-start | bytes 393224 | tf_op jit(solution)/shard_map/ppermute | solution.py:97
  95.2 0.1 slice_add_fusion.2
  95.3 9.1 %collective-permute-done.10.rest_0_ = bf16[128,512]{1,0:T(8,128)(2,1)S(1)} collective-permute-done((bf16[128,512]{1,0:T(8,128)(2,1)S(1)}, bf16[128,512]{1,0:T(8,128)(2,1)S(1)}, u32[]{:S(2)}, u32[]{:S(2)}) %collective-permute-start.10) | collective-permute-done | bytes 131104 | tf_op jit(solution)/shard_map/ppermute | solution.py:97
  104.4 4.9 %fresh_attend.2.rest_4_ = bf16[8192,128]{1,0:T(8,128)(2,1)} custom-call(s32[1]{0:T(128)S(6)} %copy.13.length_ref, bf16[8192,128]{1,0:T(8,128)(2,1)S(1)} %bitcast.49, f32[128,4096]{1,0:T(8,128)S(1)} %get-tuple-element.65.acc_ref, f32[8,4096]{1,0:T(8,128)S(1)} %get-tuple-element.66.stat_ref, bf16[128,512]{1,0:T(8,128)(2,1)S(1)} %collective-permute-done.10.rest_0_, ...), custom_call_target="tpu_custom_call" | custom-call | flops 99999997952 | bytes 1 | tf_op jit(solution)/shard_map/fresh_attend/pallas_call | solution.py:429
  109.4 5.6 %fresh_attend.3 = bf16[8192,128]{1,0:T(8,128)(2,1)} custom-call(s32[1]{0:T(128)S(6)} %copy.13.length_ref, bf16[8192,128]{1,0:T(8,128)(2,1)S(1)} %bitcast.50, f32[128,4096]{1,0:T(8,128)S(1)} %get-tuple-element.59.acc_ref, f32[8,4096]{1,0:T(8,128)S(1)} %get-tuple-element.60.stat_ref, ...), custom_call_target="tpu_custom_call", output_to_operand_aliasing={{}: (8, {})} | custom-call | flops 99999997952 | bytes 1 | tf_op jit(solution)/shard_map/fresh_attend/pallas_call | solution.py:429
  (20 shorter events, 0.1 us)
Async XLA Ops:
  0.0 10.0 %copy-start.1 = (bf16[8,128,4,1,256]{4,2,3,1,0:T(4,128)(2,1)S(1)}, bf16[8,128,4,1,256]{4,2,3,1,0:T(4,128)(2,1)}, u32[]{:S(2)}) copy-start(bf16[8,128,4,1,256]{4,2,3,1,0:T(4,128)(2,1)} %param.11) | copy-start | bytes 6291460
  4.3 40.0 %collective-permute-start = (bf16[256,1024]{1,0:T(8,128)(2,1)}, bf16[256,1024]{1,0:T(8,128)(2,1)}, u32[]{:S(2)}, u32[]{:S(2)}) collective-permute-start(bf16[256,1024]{1,0:T(8,128)(2,1)} %get-tuple-element.36), channel_id=1, source_target_pairs={{0,4},{4,0},{8,12},{12,8},{1,5},{5,1},{9,13},{13,9},{2,6},{6,2},{1... | collective-permute-start | bytes 1572872 | tf_op jit(solution)/shard_map/ppermute | solution.py:97
  7.3 37.0 %collective-permute-start.1 = (bf16[256,1024]{1,0:T(8,128)(2,1)}, bf16[256,1024]{1,0:T(8,128)(2,1)}, u32[]{:S(2)}, u32[]{:S(2)}) collective-permute-start(bf16[256,1024]{1,0:T(8,128)(2,1)} %get-tuple-element.37), channel_id=1, source_target_pairs={{0,12},{4,8},{8,4},{12,0},{1,13},{5,9},{9,5},{13,1},{2,14},{6,10},... | collective-permute-start | bytes 1572872 | tf_op jit(solution)/shard_map/ppermute | solution.py:97
  9.8 34.5 %collective-permute-start.2 = (bf16[128,1024]{1,0:T(8,128)(2,1)}, bf16[128,1024]{1,0:T(8,128)(2,1)}, u32[]{:S(2)}, u32[]{:S(2)}) collective-permute-start(bf16[128,1024]{1,0:T(8,128)(2,1)} %get-tuple-element.38), channel_id=1, source_target_pairs={{0,8},{4,12},{8,0},{12,4},{1,9},{5,13},{9,1},{13,5},{2,10},{6,14},... | collective-permute-start | bytes 786440 | tf_op jit(solution)/shard_map/ppermute | solution.py:97
  10.0 5.6 %copy-start.2 = (bf16[1,1,1024,4,2,128]{5,4,3,2,1,0:T(2,128)(2,1)S(1)}, bf16[1,1,1024,4,2,128]{5,4,3,2,1,0:T(2,128)(2,1)}, u32[]{:S(2)}) copy-start(bf16[1,1,1024,4,2,128]{5,4,3,2,1,0:T(2,128)(2,1)} %param.8) | copy-start | bytes 6291460
  10.0 5.6 %copy-start.3 = (bf16[1,1,1024,4,2,128]{5,4,3,2,1,0:T(2,128)(2,1)S(1)}, bf16[1,1,1024,4,2,128]{5,4,3,2,1,0:T(2,128)(2,1)}, u32[]{:S(2)}) copy-start(bf16[1,1,1024,4,2,128]{5,4,3,2,1,0:T(2,128)(2,1)} %param.9) | copy-start | bytes 6291460
  14.1 43.2 %collective-permute-start.4 = (bf16[8,128,512]{2,1,0:T(8,128)(2,1)}, bf16[8,128,512]{2,1,0:T(8,128)(2,1)}, u32[]{:S(2)}, u32[]{:S(2)}) collective-permute-start(bf16[8,128,512]{2,1,0:T(8,128)(2,1)} %get-tuple-element.48), channel_id=1, source_target_pairs={{0,2},{2,0},{1,3},{3,1},{4,6},{6,4},{5,7},{7,5},{8,10},{10,8},{9,1... | collective-permute-start | bytes 3145736 | tf_op jit(solution)/shard_map/ppermute | solution.py:93
  15.6 28.8 %copy-start = (bf16[256,4096]{1,0:T(8,128)(2,1)S(1)}, bf16[256,4096]{1,0:T(8,128)(2,1)}, u32[]{:S(2)}) copy-start(bf16[256,4096]{1,0:T(8,128)(2,1)} %refs_3_.3) | copy-start | bytes 6291460
  48.6 4.4 %collective-permute-start.3 = (bf16[2,896,512]{2,1,0:T(8,128)(2,1)S(1)}, bf16[2,896,512]{2,1,0:T(8,128)(2,1)S(1)}, u32[]{:S(2)}, u32[]{:S(2)}) collective-permute-start(bf16[2,896,512]{2,1,0:T(8,128)(2,1)S(1)} %project.5), channel_id=1, source_target_pairs={{0,1},{1,0},{2,3},{3,2},{4,5},{5,4},{6,7},{7,6},{8,9},{9,8},{10,11... | collective-permute-start | bytes 5505032 | tf_op jit(solution)/shard_map/ppermute | solution.py:93
  52.8 4.4 %copy-start.6 = (s32[1,8]{1,0:T(1,128)S(1)}, s32[1,8]{1,0:T(1,128)}, u32[]{:S(2)}) copy-start(s32[1,8]{1,0:T(1,128)} %param.12) | copy-start | bytes 100
  52.9 15.6 %collective-permute-start.5 = (bf16[128,1024]{1,0:T(8,128)(2,1)}, bf16[128,1024]{1,0:T(8,128)(2,1)}, u32[]{:S(2)}, u32[]{:S(2)}) collective-permute-start(bf16[128,1024]{1,0:T(8,128)(2,1)} %get-tuple-element.55), channel_id=1, source_target_pairs={{0,8},{4,12},{8,0},{12,4},{1,9},{5,13},{9,1},{13,5},{2,10},{6,14},... | collective-permute-start | bytes 786440 | tf_op jit(solution)/shard_map/ppermute | solution.py:97
  54.9 4.5 %copy-start.8 = (bf16[1,896,512]{2,1,0:T(8,128)(2,1)}, bf16[1,896,512]{2,1,0:T(8,128)(2,1)S(1)}, u32[]{:S(2)}) copy-start(bf16[1,896,512]{2,1,0:T(8,128)(2,1)S(1)} %get-tuple-element.68) | copy-start | bytes 2752516
  55.8 20.6 %collective-permute-start.8 = (bf16[512,512]{1,0:T(8,128)(2,1)}, bf16[512,512]{1,0:T(8,128)(2,1)}, u32[]{:S(2)}, u32[]{:S(2)}) collective-permute-start(bf16[512,512]{1,0:T(8,128)(2,1)} %slice_bitcast_fusion.2), channel_id=1, source_target_pairs={{0,2},{2,0},{1,3},{3,1},{4,6},{6,4},{5,7},{7,5},{8,10},{10,8},{9,1... | collective-permute-start | bytes 1572872 | tf_op jit(solution)/shard_map/ppermute | solution.py:93
  57.3 2.1 %copy-start.4 = (bf16[256,2,1,2048]{3,1,2,0:T(2,128)(2,1)S(1)}, bf16[256,2,1,2048]{3,1,2,0:T(2,128)(2,1)}, u32[]{:S(2)}) copy-start(bf16[256,2,1,2048]{3,1,2,0:T(2,128)(2,1)} %param.10) | copy-start | bytes 6291460
  70.6 5.7 %copy-start.7 = (f32[1,896,512]{2,1,0:T(8,128)S(1)}, f32[1,896,512]{2,1,0:T(8,128)}, u32[]{:S(2)}) copy-start(f32[1,896,512]{2,1,0:T(8,128)} %get-tuple-element.67) | copy-start | bytes 5505028
  70.7 5.0 %collective-permute-start.6 = (bf16[2,128,512]{2,1,0:T(8,128)(2,1)S(1)}, bf16[2,128,512]{2,1,0:T(8,128)(2,1)S(1)}, u32[]{:S(2)}, u32[]{:S(2)}) collective-permute-start(bf16[2,128,512]{2,1,0:T(8,128)(2,1)S(1)} %project.7), channel_id=1, source_target_pairs={{0,1},{1,0},{2,3},{3,2},{4,5},{5,4},{6,7},{7,6},{8,9},{9,8},{10,11... | collective-permute-start | bytes 786440 | tf_op jit(solution)/shard_map/ppermute | solution.py:93
  73.0 7.0 %copy-start.5 = (bf16[256,2,1,2048]{3,1,2,0:T(2,128)(2,1)S(1)}, bf16[256,2,1,2048]{3,1,2,0:T(2,128)(2,1)}, u32[]{:S(2)}) copy-start(bf16[256,2,1,2048]{3,1,2,0:T(2,128)(2,1)} %param.10) | copy-start | bytes 6291460
  74.2 14.1 %collective-permute-start.7 = (bf16[384,512]{1,0:T(8,128)(2,1)S(1)}, bf16[384,512]{1,0:T(8,128)(2,1)S(1)}, u32[]{:S(2)}, u32[]{:S(2)}) collective-permute-start(bf16[384,512]{1,0:T(8,128)(2,1)S(1)} %slice.74), channel_id=1, source_target_pairs={{0,2},{2,0},{1,3},{3,1},{4,6},{6,4},{5,7},{7,5},{8,10},{10,8},{9,1... | collective-permute-start | bytes 1179656 | tf_op jit(solution)/shard_map/ppermute | solution.py:93
  75.7 17.9 %collective-permute-start.11 = (bf16[128,512]{1,0:T(8,128)(2,1)S(1)}, bf16[128,512]{1,0:T(8,128)(2,1)S(1)}, u32[]{:S(2)}, u32[]{:S(2)}) collective-permute-start(bf16[128,512]{1,0:T(8,128)(2,1)S(1)} %fusion.10), channel_id=1, source_target_pairs={{0,2},{2,0},{1,3},{3,1},{4,6},{6,4},{5,7},{7,5},{8,10},{10,8},{9,1... | collective-permute-start | bytes 393224 | tf_op jit(solution)/shard_map/ppermute | solution.py:93
  77.6 14.4 %collective-permute-start.9 = (bf16[512,512]{1,0:T(8,128)(2,1)S(1)}, bf16[512,512]{1,0:T(8,128)(2,1)S(1)}, u32[]{:S(2)}, u32[]{:S(2)}) collective-permute-start(bf16[512,512]{1,0:T(8,128)(2,1)S(1)} %fusion.2), channel_id=1, source_target_pairs={{0,4},{4,0},{8,12},{12,8},{1,5},{5,1},{9,13},{13,9},{2,6},{6,2},{1... | collective-permute-start | bytes 1572872 | tf_op jit(solution)/shard_map/ppermute | solution.py:97
  92.0 12.4 %collective-permute-start.10 = (bf16[128,512]{1,0:T(8,128)(2,1)S(1)}, bf16[128,512]{1,0:T(8,128)(2,1)S(1)}, u32[]{:S(2)}, u32[]{:S(2)}) collective-permute-start(bf16[128,512]{1,0:T(8,128)(2,1)S(1)} %fusion.8), channel_id=1, source_target_pairs={{0,8},{4,12},{8,0},{12,4},{1,9},{5,13},{9,1},{13,5},{2,10},{6,14},... | collective-permute-start | bytes 393224 | tf_op jit(solution)/shard_map/ppermute | solution.py:97
  93.6 15.8 %collective-permute-start.12 = (bf16[128,512]{1,0:T(8,128)(2,1)S(1)}, bf16[128,512]{1,0:T(8,128)(2,1)S(1)}, u32[]{:S(2)}, u32[]{:S(2)}) collective-permute-start(bf16[128,512]{1,0:T(8,128)(2,1)S(1)} %fusion.7), channel_id=1, source_target_pairs={{0,8},{4,12},{8,0},{12,4},{1,9},{5,13},{9,1},{13,5},{2,10},{6,14},... | collective-permute-start | bytes 393224 | tf_op jit(solution)/shard_map/ppermute | solution.py:97

commit v7 on v6

--- a/solution.py
+++ b/solution.py
@@ -9,8 +9,15 @@
 from jax.sharding import PartitionSpec as P
 
 CHUNKS = 2
+PART = 512
+ONES = 16
 VMEM_BYTES = 24 * 1024 * 1024
 LONG = pl.CostEstimate(flops=10**11, bytes_accessed=1, transcendentals=0)
+COSTS = {}
+
+
+def cost(name):
+    return COSTS.get(name, LONG)
 
 
 def attend_head(query_rows, prefix, fresh_rows, length):
@@ -101,29 +108,6 @@
     return lax.optimization_barrier((first, second))
 
 
-def unit_index(shape, unit):
-    row = lax.broadcasted_iota(jnp.int32, shape, 0)
-    if unit & (unit - 1):
-        return row // unit, row % unit
-    return row >> (unit.bit_length() - 1), row & (unit - 1)
-
-
-def head_mask(shape, heads):
-    column = lax.broadcasted_iota(jnp.int32, shape, 1)
-    low = unit_index(shape, heads)[1] * (shape[1] // heads)
-    inside = (column >= low) & (column < low + shape[1] // heads)
-    return jnp.where(inside, 1.0, 0.0).astype(jnp.bfloat16)
-
-
-def own_head(block, heads, width):
-    result = block[:width]
-    row = lax.broadcasted_iota(jnp.int32, result.shape, 1)
-    head_of = row % heads if heads & (heads - 1) else row & (heads - 1)
-    for i in range(1, heads):
-        result = jnp.where(head_of == i, block[i * width : (i + 1) * width], result)
-    return result
-
-
 def softmax_parts(scores, old_max=None):
     row_max = jnp.max(scores, axis=0, keepdims=True)
     if old_max is not None:
@@ -170,7 +154,7 @@
         out_shape=jax.ShapeDtypeStruct((head_count, ctx_count, depth, columns), jnp.bfloat16),
         scratch_shapes=[pltpu.VMEM((rows * slots, width), jnp.float32)],
         compiler_params=params(),
-        cost_estimate=LONG,
+        cost_estimate=cost("arrange_weights"),
         name="arrange_weights",
     )(*views)
 
@@ -191,7 +175,6 @@
                 value = held[0]
                 for ctx in range(1, ctx_count):
                     value = jnp.where(target == ctx, held[ctx], value)
-                value = value.T if kind else value
                 out_ref[0, :, at : at + width] = value.astype(out_ref.dtype)
 
 
@@ -214,7 +197,7 @@
         ),
         out_shape=[jax.ShapeDtypeStruct((blocks, length, columns), jnp.bfloat16)] * ctx_count,
         compiler_params=params(),
-        cost_estimate=LONG,
+        cost_estimate=cost("arrange_pool"),
         name="arrange_pool",
     )(place, view)
 
@@ -235,7 +218,7 @@
     ).astype(out_ref.dtype)
 
 
-def project(place, blocks, weights, head_step, out_dtype):
+def project(place, blocks, weights, head_step, out_dtype, name):
     head_count, ctx_count, depth, width = weights.shape
     row_total = sum(block.shape[0] for block in blocks)
 
@@ -266,8 +249,8 @@
         ),
         out_shape=jax.ShapeDtypeStruct((ctx_count, row_total, width), out_dtype),
         compiler_params=params(),
-        cost_estimate=LONG,
-        name="project",
+        cost_estimate=cost(name),
+        name=name,
     )(place, *blocks, weights)
 
 
@@ -276,7 +259,7 @@
     blocks, length, columns = pool_refs[0].shape
     wide = columns // 2
     width = wide // heads
-    values[wide:, :] = jnp.ones_like(values[wide:, :])
+    values[...] = jnp.ones_like(values)
     for at in range(table_ref.shape[0]):
         entry = table_ref[at]
         here = slice(at * length, (at + 1) * length)
@@ -287,15 +270,23 @@
             def _():
                 block = pool_ref[entry % blocks]
                 keys[here, :] = block[:, :wide]
-                for head in range(heads):
-                    low = wide + head * length
-                    values[head * width : (head + 1) * width, here] = block[:, low : low + length]
+                put_values(values, here, block[:, wide:], heads)
+
+
+def put_values(values, here, block, heads):
+    width = block.shape[1] // heads
+    for head in range(heads):
+        low = head * (width + ONES)
+        values[low : low + width, here] = (
+            block[:, head * width : (head + 1) * width].astype(jnp.float32).T.astype(jnp.bfloat16)
+        )
 
 
 def pick_blocks(place, table, pools, heads):
     length, columns = pools[0].shape[1:]
     count = table.shape[0] * length
     wide = columns // 2
+    tall = wide + heads * ONES
     return pl.pallas_call(
         functools.partial(pick_kernel, heads, len(pools)),
         grid_spec=pltpu.PrefetchScalarGridSpec(
@@ -304,50 +295,55 @@
             in_specs=[pl.BlockSpec(p.shape, lambda i, *_: (0, 0, 0)) for p in pools],
             out_specs=[
                 pl.BlockSpec((count, wide), lambda i, *_: (0, 0)),
-                pl.BlockSpec((wide + 16, count), lambda i, *_: (0, 0)),
+                pl.BlockSpec((tall, count), lambda i, *_: (0, 0)),
             ],
         ),
         out_shape=[
             jax.ShapeDtypeStruct((count, wide), jnp.bfloat16),
-            jax.ShapeDtypeStruct((wide + 16, count), jnp.bfloat16),
+            jax.ShapeDtypeStruct((tall, count), jnp.bfloat16),
         ],
         compiler_params=params(),
-        cost_estimate=LONG,
+        cost_estimate=cost("pick_blocks"),
         name="pick_blocks",
     )(place, table, *pools)
 
 
-def prefix_kernel(scale, heads, query_ref, keys, values, acc_ref, stat_ref, mask):
+def each_part(rows, heads):
+    part_rows = min(PART, rows)
+    each = part_rows // heads
+    for low in range(0, rows, part_rows):
+        for head in range(heads):
+            at = low + head * each
+            yield head, pl.ds(low + head, each, stride=heads), slice(at, at + each)
+
+
+def prefix_kernel(scale, heads, query_ref, keys, values, acc_ref, stat_ref, flat):
     rows, width = query_ref.shape
-    part_rows = mask.shape[0]
-    wide = heads * width
-
-    @pl.when(pl.program_id(0) == 0)
-    def _():
-        mask[...] = head_mask(mask.shape, heads)
-
-    for part in range(rows // part_rows):
-        here = slice(part * part_rows, (part + 1) * part_rows)
-        query_block = jnp.concatenate([query_ref[here, :]] * heads, 1) * mask[...]
-        row_max, weights = softmax_parts(dot_queries(keys[...], query_block) * scale)
-        mixed = jnp.dot(values[...], weights, preferred_element_type=jnp.float32)
-        acc_ref[:, here] = own_head(mixed, heads, width)
-        half = stat_ref.shape[0] // 2
-        stat_ref[:half, here] = jnp.broadcast_to(row_max, (half, part_rows))
-        stat_ref[half:, here] = jnp.broadcast_to(mixed[wide : wide + 1], (half, part_rows))
-
-
-def prefix_attend(query_rows, keys, values, piece, scale, heads):
+    tall = width + ONES
+    half = stat_ref.shape[0] // 2
+    flat[...] = query_ref[...].astype(jnp.float32)
+    for head, taken, here in each_part(rows, heads):
+        query_block = flat[taken, :].astype(jnp.bfloat16)
+        scores = dot_queries(keys[:, head * width : (head + 1) * width], query_block) * scale
+        row_max, weights = softmax_parts(scores)
+        mixed = jnp.dot(
+            values[head * tall : (head + 1) * tall, :], weights, preferred_element_type=jnp.float32
+        )
+        acc_ref[:, here] = mixed[:width]
+        stat_ref[:half, here] = jnp.broadcast_to(row_max, (half, row_max.shape[1]))
+        stat_ref[half:, here] = jnp.broadcast_to(mixed[width : width + 1], (half, row_max.shape[1]))
+
+
+def prefix_attend(query_rows, keys, values, chunk, scale, heads):
     all_rows, width = query_rows.shape
     row_total = all_rows // CHUNKS
     rows = min(1024, row_total)
     steps = row_total // rows
-    key_count, wide = keys.shape
     return pl.pallas_call(
         functools.partial(prefix_kernel, scale, heads),
         grid=(steps,),
         in_specs=[
-            pl.BlockSpec((rows, width), lambda i: (piece * steps + i, 0)),
+            pl.BlockSpec((rows, width), lambda i: (chunk * steps + i, 0)),
             pl.BlockSpec(keys.shape, lambda i: (0, 0)),
             pl.BlockSpec(values.shape, lambda i: (0, 0)),
         ],
@@ -359,9 +355,9 @@
             jax.ShapeDtypeStruct((width, row_total), jnp.float32),
             jax.ShapeDtypeStruct((8, row_total), jnp.float32),
         ],
-        scratch_shapes=[pltpu.VMEM((min(512, rows), wide), jnp.bfloat16)],
+        scratch_shapes=[pltpu.VMEM((rows, width), jnp.float32)],
         compiler_params=params(),
-        cost_estimate=LONG,
+        cost_estimate=cost("prefix_attend"),
         name="prefix_attend",
     )(query_rows, keys, values)
 
@@ -369,29 +365,27 @@
 def fresh_kernel(
     scale, heads, per_token, first_row, parts, length_ref, query_ref, acc_ref, stat_ref, *rest
 ):
-    out_ref, keys, values, mask = rest[-4:]
+    out_ref, keys, values, flat, mixed_rows = rest[-5:]
     rows, width = query_ref.shape
-    wide = heads * width
+    wide, tall = heads * width, width + ONES
     step = pl.program_id(0)
 
     @pl.when(step == 0)
     def _():
-        mask[...] = head_mask(mask.shape, heads)
-        values[wide:, :] = jnp.ones_like(values[wide:, :])
+        values[...] = jnp.ones_like(values)
         for index in range(parts):
             one, other = rest[2 * index], rest[2 * index + 1]
             here = slice(index * one.shape[0], (index + 1) * one.shape[0])
             fresh = (one[...].astype(jnp.float32) + other[...]).astype(jnp.bfloat16)
             keys[here, :] = fresh[:, :wide]
-            values[:wide, here] = fresh[:, wide:].astype(jnp.float32).T.astype(jnp.bfloat16)
-
-    part_rows = mask.shape[0]
+            put_values(values, here, fresh[:, wide:], heads)
+
     half = stat_ref.shape[0] // 2
-    for part in range(rows // part_rows):
-        here = slice(part * part_rows, (part + 1) * part_rows)
-        query_block = jnp.concatenate([query_ref[here, :]] * heads, 1) * mask[...]
-        scores = dot_queries(keys[...], query_block) * scale
-        row = part * part_rows + lax.broadcasted_iota(jnp.int32, (1, part_rows), 1)
+    flat[...] = query_ref[...].astype(jnp.float32)
+    for head, taken, here in each_part(rows, heads):
+        query_block = flat[taken, :].astype(jnp.bfloat16)
+        scores = dot_queries(keys[:, head * width : (head + 1) * width], query_block) * scale
+        row = taken.start + heads * lax.broadcasted_iota(jnp.int32, (1, taken.size), 1)
         token = first_row + step * (rows // per_token) + (
             row // per_token if per_token & (per_token - 1) else row >> (per_token.bit_length() - 1)
         )
@@ -400,11 +394,14 @@
         old_max, old_total = stat_ref[:1, here], stat_ref[half : half + 1, here]
         row_max, weights = softmax_parts(scores, old_max)
         fade = jnp.exp2(old_max - row_max)
-        mixed = jnp.dot(values[...], weights, preferred_element_type=jnp.float32)
-        row_total = old_total * fade + mixed[wide : wide + 1]
+        mixed = jnp.dot(
+            values[head * tall : (head + 1) * tall, :], weights, preferred_element_type=jnp.float32
+        )
+        row_total = old_total * fade + mixed[width : width + 1]
         share = jnp.where(token < length_ref[0], 1.0 / row_total, 0.0)
-        result = acc_ref[:, here] * (fade * share) + own_head(mixed, heads, width) * share
-        out_ref[here, :] = result.T.astype(out_ref.dtype)
+        result = acc_ref[:, here] * (fade * share) + mixed[:width] * share
+        mixed_rows[taken, :] = result.T
+    out_ref[...] = mixed_rows[...].astype(out_ref.dtype)
 
 
 def fresh_attend(length, query_rows, acc, stat, parts, earlier, chunk, scale, heads, per_token):
@@ -437,16 +434,52 @@
             out_specs=block,
             scratch_shapes=[
                 pltpu.VMEM((key_count, heads * width), jnp.bfloat16),
-                pltpu.VMEM((heads * width + 16, key_count), jnp.bfloat16),
-                pltpu.VMEM((min(512, rows), heads * width), jnp.bfloat16),
+                pltpu.VMEM((heads * (width + ONES), key_count), jnp.bfloat16),
+                pltpu.VMEM((rows, width), jnp.float32),
+                pltpu.VMEM((rows, width), jnp.float32),
             ],
         ),
         out_shape=jax.ShapeDtypeStruct((row_total, width), jnp.bfloat16),
         input_output_aliases=aliases,
         compiler_params=params(),
-        cost_estimate=LONG,
+        cost_estimate=cost("fresh_attend"),
         name="fresh_attend",
     )(*operands)
+
+
+def cut_kernel(depth, bits, place_ref, tokens_ref, *refs):
+    pieces, sems = refs[:-1], refs[-1]
+    copies = []
+    for index, piece in enumerate(pieces):
+        start = pl.multiple_of((place_ref[0] ^ bits[index]) * depth, depth)
+        copies.append(
+            pltpu.make_async_copy(
+                tokens_ref.at[:, pl.ds(start, depth)], piece, sems.at[index]
+            )
+        )
+    for copy in copies:
+        copy.start()
+    for copy in copies:
+        copy.wait()
+
+
+def cut_tokens(place, tokens, depth, bits):
+    anywhere = pl.BlockSpec(memory_space=pl.ANY)
+    piece = jax.ShapeDtypeStruct((tokens.shape[0], depth), tokens.dtype)
+    return pl.pallas_call(
+        functools.partial(cut_kernel, depth, bits),
+        grid_spec=pltpu.PrefetchScalarGridSpec(
+            num_scalar_prefetch=1,
+            grid=(1,),
+            in_specs=[anywhere],
+            out_specs=[anywhere] * len(bits),
+            scratch_shapes=[pltpu.SemaphoreType.DMA((len(bits),))],
+        ),
+        out_shape=[piece] * len(bits),
+        compiler_params=params(),
+        cost_estimate=cost("cut_tokens"),
+        name="cut_tokens",
+    )(place, tokens)
 
 
 def reduced_shards(tokens, key_weight, value_weight, queries, prefix_pool, block_table, lengths):
@@ -464,17 +497,11 @@
     rows = token_count // CHUNKS
     scale = math.log2(math.e) / math.sqrt(width)
 
-    def leaving(bits, first, count):
-        start = (batch_at ^ bits) * depth
-        return lax.dynamic_slice(tokens, (first, start), (count, depth))
-
     top = batch_count // 2
-    steps = [bits for bits in range(1, batch_count) if bits != top]
-    pieces = [leaving(bits, 0, token_count) for bits in steps] + [leaving(top, 0, rows)]
+    steps = list(range(batch_count - 1, top, -1)) + list(range(1, top))
+    pieces = cut_tokens(place, tokens, depth, [*steps, top])
     pieces, prefix_pool = after(pieces, prefix_pool)
-    arrived = [trade(piece, "batch", bits) for piece, bits in zip(pieces, [*steps, top])]
-    arrived, last = after(arrived, leaving(top, rows, rows))
-    last = trade(last, "batch", top)
+    arrived = [trade(piece, "batch", bits) for piece, bits in zip(pieces, steps)]
 
     pools = arrange_pool(place, prefix_pool, ctx_count, heads)
     pools, (key_weight, value_weight) = after(pools, (key_weight, value_weight))
@@ -484,49 +511,70 @@
 
     query_rows = queries.reshape(token_count, heads, group, width)
     query_rows = query_rows.transpose(0, 2, 1, 3).reshape(-1, width)
-    def projected(blocks):
+    def projected(blocks, name):
         terms = [
-            shift(project(place, blocks, weights, step, jnp.bfloat16), "head", step)
+            shift(project(place, blocks, weights, step, jnp.bfloat16, name + "_away"), "head", step)
             for step in range(1, head_count)
         ]
-        total = project(place, blocks, weights, 0, jnp.float32)
-
-        def of(step):
-            return sum((term[step].astype(jnp.float32) for term in terms), total[step])
-
-        return of(0), [of(step).astype(jnp.bfloat16) for step in range(1, ctx_count)]
-
-    def spread(others, here=slice(None)):
-        return [shift(other[here], "ctx", step + 1) for step, other in enumerate(others)]
-
-    def summed(mine, others):
-        return sum((other.astype(jnp.float32) for other in others), mine)
-
-    mine, others = projected([*arrived, tokens])
-    far, near = slice(0, len(steps) * token_count), slice(len(steps) * token_count, None)
-    far_others = spread(others, far)
-    others, pools = after(others, pools)
-    near_others = spread(others, near)
+        return [project(place, blocks, weights, 0, jnp.float32, name + "_kept"), *terms]
+
+    def added(terms, step, here):
+        return sum(term[step, here].astype(jnp.float32) for term in terms)
+
+    def others(terms, here):
+        return [added(terms, step, here).astype(jnp.bfloat16) for step in range(1, ctx_count)]
+
+    def spread(parts):
+        return [shift(part, "ctx", step + 1) for step, part in enumerate(parts)]
+
+    def summed(terms, here, parts):
+        return added(terms, 0, here) + sum(part.astype(jnp.float32) for part in parts)
+
+    every = slice(None)
+    parts_of = [slice(i * rows, (i + 1) * rows) for i in range(CHUNKS)]
+
+    own = projected([tokens], "own")
+    own[0], last = after(own[0], pieces[-1])
+    last = trade(last, "batch", top)
+    own_others = others(own, every)
+    own_others = spread(own_others)
+
+    if steps:
+        early = projected(arrived, "early")
+        cuts = [slice(i * token_count, (i + 1) * token_count) for i in range(len(steps))]
+        far_others = spread(others(early, cuts[0]))
+        near_others, pools = after(others(early, cuts[1]), pools)
+        near_others = spread(near_others)
     keys, values = pick_blocks(place, block_table[0], pools, heads)
     states = [prefix_attend(query_rows, keys, values, 0, scale, heads)]
     states[0], last = after(states[0], last)
-
-    last_mine, last_others = projected([last])
-    last_others, (keys, values) = after(last_others, (keys, values))
-    last_others = spread(last_others)
+    if steps:
+        far = summed(early, cuts[0], far_others).astype(jnp.bfloat16)
+        far, last = after(far, last)
+        far = trade(far, "batch", 1)
+
+    late = projected([last], "late")
+    late_others = [others(late, here) for here in parts_of]
+    waiting = (keys, values, near_others) if steps else (keys, values)
+    late_others[-1], waiting = after(late_others[-1], waiting)
+    keys, values, *near_others = waiting
+    late_others = [spread(part) for part in late_others]
     states.append(prefix_attend(query_rows, keys, values, 1, scale, heads))
-
-    mine = [mine[far], summed(mine[near], near_others)]
-    away, home = mine[1][:rows], mine[1][rows:]
+    states[1], late_others[0] = after(states[1], late_others[0])
+
+    home = summed(own, every, own_others)
     if steps:
-        far = trade(summed(mine[0], far_others).astype(jnp.bfloat16), "batch", 1)
-        home = home + far[:token_count].astype(jnp.float32)
-        away = away + far[token_count : token_count + rows].astype(jnp.float32)
-        far, last_others = after(far, last_others)
-        last_mine = last_mine + far[token_count + rows :].astype(jnp.float32)
-    away = [away, summed(last_mine, last_others)]
-    away = [trade(part.astype(jnp.bfloat16), "batch", top) for part in away]
-    parts = [(away[0], home[:rows]), (away[1], home[rows:])]
+        near_others = near_others[0]
+        near = trade(summed(early, cuts[1], near_others).astype(jnp.bfloat16), "batch", 1)
+        home = home + near.astype(jnp.float32)
+    parts = []
+    for chunk, here in enumerate(parts_of):
+        part = summed(late, here, late_others[chunk])
+        if steps:
+            part = part + far[here].astype(jnp.float32)
+            if chunk + 1 < CHUNKS:
+                (far, late), late_others[chunk + 1] = after((far, late), late_others[chunk + 1])
+        parts.append((trade(part.astype(jnp.bfloat16), "batch", top), home[here]))
 
     result = None
     for chunk in range(CHUNKS):

time: 115 us -> 107 us (0.930)
  waiting for transfers between devices: 39.2 us -> 20.6 us
  Pallas kernels: 48.5 us -> 58.4 us
  local copies, waits for them, and re-layouts: 6.4 us -> 1.72 us
  other arithmetic: 3.52 us -> 6.5 us
  starting transfers between devices: 16.5 us -> 18.4 us
    ppermute x7, waiting for transfers between devices: 39.2 us -> 20.6 us  [trade(): lax.ppermute(array, axis, [(i, i ^ bits) for i in range(lax.axis_size(axi...]
    pallas_call x2, Pallas kernels: 16.5 us -> 21.5 us  [prefix_attend(): pl.pallas_call(functools.partial(prefix_kernel, scale, heads), grid=(step...]
    dynamic_slice x2 -> x0, local copies, waits for them, and re-layouts: 4.28 us -> none  [leaving(): return lax.dynamic_slice(tokens, (first, start), (count, depth))]
    convert_element_type x4 -> x7, other arithmetic: 1.32 us -> 5.35 us  [the longest x1 1.99 us: reduced_shards(): far = summed(early, cuts[0], far_others).astype(jnp.bfloat16)]
    slice x3 -> x1, local copies, waits for them, and re-layouts: 2.08 us -> 0.04 us  [reduced_shards(): parts.append((trade(part.astype(jnp.bfloat16), 'batch', top), home[here]))]
    pallas_call x4 -> x6, Pallas kernels: 12.8 us -> 14.7 us  [project(): pl.pallas_call(project_kernel, grid_spec=pltpu.PrefetchScalarGridSpec(num...]
    ppermute x6 -> x9, starting transfers between devices: 5.34 us -> 7.2 us  [shift(): lax.ppermute(array, axis, [(i, (i + step) % count) for i in range(count)])]
    pallas_call x0 -> x1, Pallas kernels: none -> 1.74 us  [cut_tokens(): pl.pallas_call(functools.partial(cut_kernel, depth, bits), grid_spec=pltp...]
  transfers between devices with their start and end apart: 13 -> 16, of which waited for: 4 -> 3; matrix products, arithmetic and copies ran while one was open for 5% -> 6% of each run, Pallas kernels for 37% -> 47%
where the time goes in v7:
time: 107 us
  Pallas kernels  58.4 us (55%)
  waiting for transfers between devices  20.6 us (19%)
  starting transfers between devices  18.4 us (17%)
  other arithmetic  6.5 us (6%)
  local copies, waits for them, and re-layouts  1.72 us (2%)
    pallas_call x2, Pallas kernels, prefix_attend(): pl.pallas_call(functools.partial(prefix_kernel, scale, heads), grid=(step...  21.5 us
    ppermute x7, waiting for transfers between devices, trade(): lax.ppermute(array, axis, [(i, i ^ bits) for i in range(lax.axis_size(axi...  20.6 us
    pallas_call x6, Pallas kernels, project(): pl.pallas_call(project_kernel, grid_spec=pltpu.PrefetchScalarGridSpec(num...  14.7 us
    pallas_call x2, Pallas kernels, fresh_attend(): pl.pallas_call(functools.partial(fresh_kernel, scale, heads, per_token, c...  11.3 us
    ppermute x7, starting transfers between devices, trade(): lax.ppermute(array, axis, [(i, i ^ bits) for i in range(lax.axis_size(axi...  11.2 us
    ppermute x9, starting transfers between devices, shift(): lax.ppermute(array, axis, [(i, (i + step) % count) for i in range(count)])  7.2 us
    pallas_call x1, Pallas kernels, arrange_pool(): pl.pallas_call(functools.partial(pool_kernel, ctx_count, heads), grid_spe...  3.87 us
    pallas_call x1, Pallas kernels, pick_blocks(): pl.pallas_call(functools.partial(pick_kernel, heads, len(pools)), grid_sp...  2.84 us
  transfers between devices with their start and end apart: 16, of which 3 were waited for; matrix products, arithmetic and copies ran while one was open for 6% of the time, Pallas kernels for 47%

profile of v7, /device:TPU:0, one launch (start us, length us, event | category | flops | bytes accessed | tf_op | source)
XLA Modules:
  0.0 106.6 jit_solution(6302032394691204257)
XLA Ops:
  0.0 0.1 pad_add_fusion.place_ref
  0.1 1.6 %copy-done.6 = bf16[256,4096]{1,0:T(8,128)(2,1)S(1)} copy-done((bf16[256,4096]{1,0:T(8,128)(2,1)S(1)}, bf16[256,4096]{1,0:T(8,128)(2,1)}, u32[]{:S(2)}) %copy-start.6) | copy-done | bytes 2097176
  1.7 1.7 %cut_tokens.1 = (bf16[256,1024]{1,0:T(8,128)(2,1)}, bf16[256,1024]{1,0:T(8,128)(2,1)}, bf16[256,1024]{1,0:T(8,128)(2,1)}) custom-call(s32[3]{0:T(128)S(1)} %pad_add_fusion.place_ref, bf16[256,4096]{1,0:T(8,128)(2,1)S(1)} %copy-done.6), custom_call_target="tpu_custom_call" | custom-call | flops 99999997952 | bytes 1 | tf_op jit(solution)/shard_map/cut_tokens/pallas_call | solution.py:469
  3.4 5.1 %collective-permute-start = (bf16[256,1024]{1,0:T(8,128)(2,1)}, bf16[256,1024]{1,0:T(8,128)(2,1)}, u32[]{:S(2)}, u32[]{:S(2)}) collective-permute-start(bf16[256,1024]{1,0:T(8,128)(2,1)} %get-tuple-element.48), channel_id=1, source_target_pairs={{0,12},{4,8},{8,4},{12,0},{1,13},{5,9},{9,5},{13,1},{2,14},{6,10},... | collective-permute-start | bytes 1572872 | tf_op jit(solution)/shard_map/ppermute | solution.py:104
  8.5 0.0 collective-permute-start.1
  8.5 3.9 %arrange_pool.1 = (bf16[8,128,512]{2,1,0:T(8,128)(2,1)S(1)}, bf16[8,128,512]{2,1,0:T(8,128)(2,1)}) custom-call(s32[3]{0:T(128)S(1)} %pad_add_fusion.place_ref, bf16[8,128,8,128]{3,2,1,0:T(8,128)(2,1)S(1)} %bitcast.61), custom_call_target="tpu_custom_call" | custom-call | flops 99999997952 | bytes 1 | tf_op jit(solution)/shard_map/arrange_pool/pallas_call | solution.py:189
  12.4 1.5 %collective-permute-start.4 = (bf16[8,128,512]{2,1,0:T(8,128)(2,1)}, bf16[8,128,512]{2,1,0:T(8,128)(2,1)}, u32[]{:S(2)}, u32[]{:S(2)}) collective-permute-start(bf16[8,128,512]{2,1,0:T(8,128)(2,1)} %get-tuple-element.56), channel_id=1, source_target_pairs={{0,2},{2,0},{1,3},{3,1},{4,6},{6,4},{5,7},{7,5},{8,10},{10,8},{9,1... | collective-permute-start | bytes 3145736 | tf_op jit(solution)/shard_map/ppermute | solution.py:100
  13.9 2.5 %arrange_weights.1.refs_2_.refs_1_ = bf16[2,2,1024,512]{3,2,1,0:T(8,128)(2,1)S(1)} custom-call(bf16[1024,8,128]{2,1,0:T(8,128)(2,1)S(1)} %bitcast.62, bf16[1024,8,128]{2,1,0:T(8,128)(2,1)S(1)} %bitcast.63), custom_call_target="tpu_custom_call" | custom-call | flops 99999997952 | bytes 1 | tf_op jit(solution)/shard_map/arrange_weights/pallas_call | solution.py:149
  16.4 1.5 %own_kept.1 = f32[2,256,512]{2,1,0:T(8,128)S(1)} custom-call(s32[3]{0:T(128)S(1)} %pad_add_fusion.place_ref, bf16[256,4096]{1,0:T(8,128)(2,1)S(1)} %copy-done.7, bf16[2,2,1024,512]{3,2,1,0:T(8,128)(2,1)S(1)} %arrange_weights.1.refs_2_.refs_1_), custom_call_target="tpu_custom_call" | custom-call | flops 99999997952 | bytes 1 | tf_op jit(solution)/shard_map/own_kept/pallas_call | solution.py:230
  18.0 0.8 collective-permute-start.5
  18.8 1.6 %own_away.1 = bf16[2,256,512]{2,1,0:T(8,128)(2,1)S(1)} custom-call(s32[3]{0:T(128)S(1)} %pad_add_fusion.place_ref, bf16[256,4096]{1,0:T(8,128)(2,1)S(1)} %copy-done.7, bf16[2,2,1024,512]{3,2,1,0:T(8,128)(2,1)S(1)} %arrange_weights.1.refs_2_.refs_1_), custom_call_target="tpu_custom_call" | custom-call | flops 99999997952 | bytes 1 | tf_op jit(solution)/shard_map/own_away/pallas_call | solution.py:230
  20.4 0.1 collective-permute-start.11
  21.1 0.6 collective-permute-done.refs_0_
  21.7 11.5 %collective-permute-done.1.refs_1_ = bf16[256,1024]{1,0:T(8,128)(2,1)} collective-permute-done((bf16[256,1024]{1,0:T(8,128)(2,1)}, bf16[256,1024]{1,0:T(8,128)(2,1)}, u32[]{:S(2)}, u32[]{:S(2)}) %collective-permute-start.1) | collective-permute-done | bytes 524320 | tf_op jit(solution)/shard_map/ppermute | solution.py:104
  33.2 3.3 %early_away.1 = bf16[2,512,512]{2,1,0:T(8,128)(2,1)S(1)} custom-call(s32[3]{0:T(128)S(1)} %pad_add_fusion.place_ref, bf16[256,1024]{1,0:T(8,128)(2,1)} %collective-permute-done.refs_0_, bf16[256,1024]{1,0:T(8,128)(2,1)} %collective-permute-done.1.refs_1_, bf16[2,2,1024,512]{3,2,1,0:T(8,128)(2,1)S(1)} %arrange_weights.1.refs_2_.refs_1_), custom_call_target="tpu_custom_call" | custom-call | flops 99999997952 | bytes 1 | tf_op jit(solution)/shard_map/early_away/pallas_call | solution.py:230
  36.4 0.1 collective-permute-start.2
  36.5 0.0 collective-permute-done.11
  36.6 0.9 fusion.9
  37.4 0.0 copy-done.15
  37.4 1.4 %collective-permute-start.12 = (bf16[256,512]{1,0:T(8,128)(2,1)}, bf16[256,512]{1,0:T(8,128)(2,1)}, u32[]{:S(2)}, u32[]{:S(2)}) collective-permute-start(bf16[256,512]{1,0:T(8,128)(2,1)} %fusion.9), channel_id=1, source_target_pairs={{0,2},{2,0},{1,3},{3,1},{4,6},{6,4},{5,7},{7,5},{8,10},{10,8},{9,1... | collective-permute-start | bytes 786440 | tf_op jit(solution)/shard_map/ppermute | solution.py:100
  38.8 3.3 %early_kept.1 = f32[2,512,512]{2,1,0:T(8,128)S(1)} custom-call(s32[3]{0:T(128)S(1)} %pad_add_fusion.place_ref, bf16[256,1024]{1,0:T(8,128)(2,1)} %collective-permute-done.refs_0_, bf16[256,1024]{1,0:T(8,128)(2,1)} %collective-permute-done.1.refs_1_, bf16[2,2,1024,512]{3,2,1,0:T(8,128)(2,1)S(1)} %arrange_weights.1.refs_2_.refs_1_), custom_call_target="tpu_custom_call" | custom-call | flops 99999997952 | bytes 1 | tf_op jit(solution)/shard_map/early_kept/pallas_call | solution.py:230
  42.1 0.0 copy-start
  42.1 0.0 copy-start.9
  42.2 1.0 fusion.11
  43.1 0.0 collective-permute-done.4.refs_1_
  43.1 0.6 collective-permute-start.3
  43.8 2.8 %pick_blocks.1 = (bf16[1024,256]{1,0:T(8,128)(2,1)S(1)}, bf16[288,1024]{1,0:T(8,128)(2,1)S(1)}) custom-call(s32[3]{0:T(128)S(1)} %pad_add_fusion.place_ref, s32[8]{0:T(128)S(1)} %bitcast.68, bf16[8,128,512]{2,1,0:T(8,128)(2,1)S(1)} %get-tuple-element.57.refs_0_, bf16[8,128,512]{2,1,0:T(8,128)(2,1)} %collective-permute-done.4.refs_1_), custom_call_target="tpu_custom_call" | custom-call | flops 99999997952 | bytes 1 | tf_op jit(solution)/shard_map/pick_blocks/pallas_call | solution.py:290
  46.7 10.8 %prefix_attend.2 = (f32[128,4096]{1,0:T(8,128)S(1)}, f32[8,4096]{1,0:T(8,128)S(1)}) custom-call(bf16[8192,128]{1,0:T(8,128)(2,1)S(1)} %bitcast.64, bf16[1024,256]{1,0:T(8,128)(2,1)S(1)} %get-tuple-element.68.keys, bf16[288,1024]{1,0:T(8,128)(2,1)S(1)} %get-tuple-element.69.values), custom_call_target="tpu_custom_call" | custom-call | flops 99999997952 | bytes 1 | tf_op jit(solution)/shard_map/prefix_attend/pallas_call | solution.py:342
  57.5 1.4 %collective-permute-start.7 = (bf16[256,512]{1,0:T(8,128)(2,1)}, bf16[256,512]{1,0:T(8,128)(2,1)}, u32[]{:S(2)}, u32[]{:S(2)}) collective-permute-start(bf16[256,512]{1,0:T(8,128)(2,1)} %get-tuple-element.67), channel_id=1, source_target_pairs={{0,2},{2,0},{1,3},{3,1},{4,6},{6,4},{5,7},{7,5},{8,10},{10,8},{9,1... | collective-permute-start | bytes 786440 | tf_op jit(solution)/shard_map/ppermute | solution.py:100
  59.0 2.0 %fusion.7 = bf16[256,512]{1,0:T(8,128)(2,1)} fusion(f32[2,512,512]{2,1,0:T(8,128)} %copy-done, bf16[256,512]{1,0:T(8,128)(2,1)} %collective-permute-done.3, bf16[2,512,512]{2,1,0:T(8,128)(2,1)} %copy-done.14), kind=kLoop, calls=%fused_computation.11 | loop fusion | flops 655360 | bytes 1310720 | tf_op jit(solution)/shard_map/convert_element_type | solution.py:552
  61.0 2.5 %late_away.1 = bf16[2,256,512]{2,1,0:T(8,128)(2,1)S(1)} custom-call(s32[3]{0:T(128)S(1)} %pad_add_fusion.place_ref, bf16[256,1024]{1,0:T(8,128)(2,1)} %collective-permute-done.5.refs_0_, bf16[2,2,1024,512]{3,2,1,0:T(8,128)(2,1)S(1)} %arrange_weights.1.refs_2_.refs_1_), custom_call_target="tpu_custom_call" | custom-call | flops 99999997952 | bytes 1 | tf_op jit(solution)/shard_map/late_away/pallas_call | solution.py:230
  63.5 0.1 collective-permute-start.6
  63.6 2.5 %late_kept.1 = f32[2,256,512]{2,1,0:T(8,128)S(1)} custom-call(s32[3]{0:T(128)S(1)} %pad_add_fusion.place_ref, bf16[256,1024]{1,0:T(8,128)(2,1)} %collective-permute-done.5.refs_0_, bf16[2,2,1024,512]{3,2,1,0:T(8,128)(2,1)S(1)} %arrange_weights.1.refs_2_.refs_1_), custom_call_target="tpu_custom_call" | custom-call | flops 99999997952 | bytes 1 | tf_op jit(solution)/shard_map/late_kept/pallas_call | solution.py:230
  66.2 1.9 %collective-permute-start.9 = (bf16[256,512]{1,0:T(8,128)(2,1)S(1)}, bf16[256,512]{1,0:T(8,128)(2,1)S(1)}, u32[]{:S(2)}, u32[]{:S(2)}) collective-permute-start(bf16[256,512]{1,0:T(8,128)(2,1)S(1)} %copy-done.17), channel_id=1, source_target_pairs={{0,4},{4,0},{8,12},{12,8},{1,5},{5,1},{9,13},{13,9},{2,6},{6,2},{1... | collective-permute-start | bytes 786440 | tf_op jit(solution)/shard_map/ppermute | solution.py:104
  68.1 0.1 fusion.21
  68.2 1.3 %fusion.2 = bf16[256,512]{1,0:T(8,128)(2,1)S(1)} fusion(f32[2,512,512]{2,1,0:T(8,128)} %copy-done, bf16[256,512]{1,0:T(8,128)(2,1)} %collective-permute-done.7, bf16[2,512,512]{2,1,0:T(8,128)(2,1)} %copy-done.14), kind=kLoop, calls=%fused_computation.3 | loop fusion | flops 655360 | bytes 1310720 | tf_op jit(solution)/shard_map/convert_element_type | solution.py:568
  69.5 0.2 collective-permute-start.13
  69.7 0.9 collective-permute-start.8
  70.7 1.1 %collective-permute-start.14 = (bf16[128,512]{1,0:T(8,128)(2,1)S(1)}, bf16[128,512]{1,0:T(8,128)(2,1)S(1)}, u32[]{:S(2)}, u32[]{:S(2)}) collective-permute-start(bf16[128,512]{1,0:T(8,128)(2,1)S(1)} %get-tuple-element.78), channel_id=1, source_target_pairs={{0,2},{2,0},{1,3},{3,1},{4,6},{6,4},{5,7},{7,5},{8,10},{10,8},{9,1... | collective-permute-start | bytes 393224 | tf_op jit(solution)/shard_map/ppermute | solution.py:100
  71.8 10.6 %prefix_attend.3 = (f32[128,4096]{1,0:T(8,128)S(1)}, f32[8,4096]{1,0:T(8,128)S(1)}) custom-call(bf16[8192,128]{1,0:T(8,128)(2,1)S(1)} %bitcast.65, bf16[1024,256]{1,0:T(8,128)(2,1)S(1)} %copy-done.13, bf16[288,1024]{1,0:T(8,128)(2,1)S(1)} %copy-done.11), custom_call_target="tpu_custom_call" | custom-call | flops 99999997952 | bytes 1 | tf_op jit(solution)/shard_map/prefix_attend/pallas_call | solution.py:342
  82.4 0.1 fusion.15
  82.5 1.2 %collective-permute-start.10 = (bf16[128,512]{1,0:T(8,128)(2,1)S(1)}, bf16[128,512]{1,0:T(8,128)(2,1)S(1)}, u32[]{:S(2)}, u32[]{:S(2)}) collective-permute-start(bf16[128,512]{1,0:T(8,128)(2,1)S(1)} %fusion.15), channel_id=1, source_target_pairs={{0,8},{4,12},{8,0},{12,4},{1,9},{5,13},{9,1},{13,5},{2,10},{6,14},... | collective-permute-start | bytes 393224 | tf_op jit(solution)/shard_map/ppermute | solution.py:104
  83.7 0.1 fusion.19
  83.8 1.9 %collective-permute-start.15 = (bf16[128,512]{1,0:T(8,128)(2,1)S(1)}, bf16[128,512]{1,0:T(8,128)(2,1)S(1)}, u32[]{:S(2)}, u32[]{:S(2)}) collective-permute-start(bf16[128,512]{1,0:T(8,128)(2,1)S(1)} %fusion.19), channel_id=1, source_target_pairs={{0,8},{4,12},{8,0},{12,4},{1,9},{5,13},{9,1},{13,5},{2,10},{6,14},... | collective-permute-start | bytes 393224 | tf_op jit(solution)/shard_map/ppermute | solution.py:104
  85.7 1.1 %fusion.8 = f32[256,512]{1,0:T(8,128)S(1)} fusion(bf16[256,512]{1,0:T(8,128)(2,1)S(1)} %collective-permute-done.13, bf16[256,512]{1,0:T(8,128)(2,1)} %collective-permute-done.12, f32[2,256,512]{2,1,0:T(8,128)S(1)} %copy-done.2, bf16[2,256,512]{2,1,0:T(8,128)(2,1)S(1)} %copy-done.16), kind=kLoop, calls=%fused_computation.13 | loop fusion | flops 786432 | bytes 1835008 | tf_op jit(solution)/shard_map/add | solution.py:569
  86.8 8.5 %collective-permute-done.10.rest_0_ = bf16[128,512]{1,0:T(8,128)(2,1)S(1)} collective-permute-done((bf16[128,512]{1,0:T(8,128)(2,1)S(1)}, bf16[128,512]{1,0:T(8,128)(2,1)S(1)}, u32[]{:S(2)}, u32[]{:S(2)}) %collective-permute-start.10) | collective-permute-done | bytes 131104 | tf_op jit(solution)/shard_map/ppermute | solution.py:104
  95.3 4.4 %fresh_attend.2.rest_4_ = bf16[8192,128]{1,0:T(8,128)(2,1)} custom-call(s32[1]{0:T(128)S(6)} %copy.13.length_ref, bf16[8192,128]{1,0:T(8,128)(2,1)S(1)} %bitcast.66, f32[128,4096]{1,0:T(8,128)S(1)} %get-tuple-element.83.acc_ref, f32[8,4096]{1,0:T(8,128)S(1)} %get-tuple-element.84.stat_ref, bf16[128,512]{1,0:T(8,128)(2,1)S(1)} %collective-permute-done.10.rest_0_, ...), custom_call_target="tpu_custom_call" | custom-call | flops 99999997952 | bytes 1 | tf_op jit(solution)/shard_map/fresh_attend/pallas_call | solution.py:426
  99.7 6.9 %fresh_attend.3 = bf16[8192,128]{1,0:T(8,128)(2,1)} custom-call(s32[1]{0:T(128)S(6)} %copy.13.length_ref, bf16[8192,128]{1,0:T(8,128)(2,1)S(1)} %bitcast.67, f32[128,4096]{1,0:T(8,128)S(1)} %get-tuple-element.72.acc_ref, f32[8,4096]{1,0:T(8,128)S(1)} %get-tuple-element.73.stat_ref, ...), custom_call_target="tpu_custom_call", output_to_operand_aliasing={{}: (8, {})} | custom-call | flops 99999997952 | bytes 1 | tf_op jit(solution)/shard_map/fresh_attend/pallas_call | solution.py:426
  (44 shorter events, 0.1 us)
Async XLA Ops:
  0.1 1.6 %copy-start.6 = (bf16[256,4096]{1,0:T(8,128)(2,1)S(1)}, bf16[256,4096]{1,0:T(8,128)(2,1)}, u32[]{:S(2)}) copy-start(bf16[256,4096]{1,0:T(8,128)(2,1)} %refs_0_.3) | copy-start | bytes 6291460
  1.7 6.9 %copy-start.3 = (bf16[8,128,4,1,256]{4,2,3,1,0:T(4,128)(2,1)S(1)}, bf16[8,128,4,1,256]{4,2,3,1,0:T(4,128)(2,1)}, u32[]{:S(2)}) copy-start(bf16[8,128,4,1,256]{4,2,3,1,0:T(4,128)(2,1)} %param.11) | copy-start | bytes 6291460
  3.4 18.3 %collective-permute-start = (bf16[256,1024]{1,0:T(8,128)(2,1)}, bf16[256,1024]{1,0:T(8,128)(2,1)}, u32[]{:S(2)}, u32[]{:S(2)}) collective-permute-start(bf16[256,1024]{1,0:T(8,128)(2,1)} %get-tuple-element.48), channel_id=1, source_target_pairs={{0,12},{4,8},{8,4},{12,0},{1,13},{5,9},{9,5},{13,1},{2,14},{6,10},... | collective-permute-start | bytes 1572872 | tf_op jit(solution)/shard_map/ppermute | solution.py:104
  8.5 24.6 %collective-permute-start.1 = (bf16[256,1024]{1,0:T(8,128)(2,1)}, bf16[256,1024]{1,0:T(8,128)(2,1)}, u32[]{:S(2)}, u32[]{:S(2)}) collective-permute-start(bf16[256,1024]{1,0:T(8,128)(2,1)} %get-tuple-element.49), channel_id=1, source_target_pairs={{0,4},{4,0},{8,12},{12,8},{1,5},{5,1},{9,13},{13,9},{2,6},{6,2},{1... | collective-permute-start | bytes 1572872 | tf_op jit(solution)/shard_map/ppermute | solution.py:104
  8.5 5.4 %copy-start.4 = (bf16[1,1,1024,4,2,128]{5,4,3,2,1,0:T(2,128)(2,1)S(1)}, bf16[1,1,1024,4,2,128]{5,4,3,2,1,0:T(2,128)(2,1)}, u32[]{:S(2)}) copy-start(bf16[1,1,1024,4,2,128]{5,4,3,2,1,0:T(2,128)(2,1)} %param.8) | copy-start | bytes 6291460
  8.5 5.4 %copy-start.5 = (bf16[1,1,1024,4,2,128]{5,4,3,2,1,0:T(2,128)(2,1)S(1)}, bf16[1,1,1024,4,2,128]{5,4,3,2,1,0:T(2,128)(2,1)}, u32[]{:S(2)}) copy-start(bf16[1,1,1024,4,2,128]{5,4,3,2,1,0:T(2,128)(2,1)} %param.9) | copy-start | bytes 6291460
  12.4 30.7 %collective-permute-start.4 = (bf16[8,128,512]{2,1,0:T(8,128)(2,1)}, bf16[8,128,512]{2,1,0:T(8,128)(2,1)}, u32[]{:S(2)}, u32[]{:S(2)}) collective-permute-start(bf16[8,128,512]{2,1,0:T(8,128)(2,1)} %get-tuple-element.56), channel_id=1, source_target_pairs={{0,2},{2,0},{1,3},{3,1},{4,6},{6,4},{5,7},{7,5},{8,10},{10,8},{9,1... | collective-permute-start | bytes 3145736 | tf_op jit(solution)/shard_map/ppermute | solution.py:100
  13.9 2.5 %copy-start.7 = (bf16[256,4096]{1,0:T(8,128)(2,1)S(1)}, bf16[256,4096]{1,0:T(8,128)(2,1)}, u32[]{:S(2)}) copy-start(bf16[256,4096]{1,0:T(8,128)(2,1)} %refs_0_.3) | copy-start | bytes 6291460
  18.0 18.6 %copy-start.1 = (f32[2,256,512]{2,1,0:T(8,128)}, f32[2,256,512]{2,1,0:T(8,128)S(1)}, u32[]{:S(2)}) copy-start(f32[2,256,512]{2,1,0:T(8,128)S(1)} %own_kept.1) | copy-start | bytes 3145732
  18.0 39.6 %collective-permute-start.5 = (bf16[256,1024]{1,0:T(8,128)(2,1)}, bf16[256,1024]{1,0:T(8,128)(2,1)}, u32[]{:S(2)}, u32[]{:S(2)}) collective-permute-start(bf16[256,1024]{1,0:T(8,128)(2,1)} %get-tuple-element.64), channel_id=1, source_target_pairs={{0,8},{4,12},{8,0},{12,4},{1,9},{5,13},{9,1},{13,5},{2,10},{6,14},... | collective-permute-start | bytes 1572872 | tf_op jit(solution)/shard_map/ppermute | solution.py:104
  20.4 16.2 %collective-permute-start.11 = (bf16[2,256,512]{2,1,0:T(8,128)(2,1)S(1)}, bf16[2,256,512]{2,1,0:T(8,128)(2,1)S(1)}, u32[]{:S(2)}, u32[]{:S(2)}) collective-permute-start(bf16[2,256,512]{2,1,0:T(8,128)(2,1)S(1)} %own_away.1), channel_id=1, source_target_pairs={{0,1},{1,0},{2,3},{3,2},{4,5},{5,4},{6,7},{7,6},{8,9},{9,8},{10,11... | collective-permute-start | bytes 1572872 | tf_op jit(solution)/shard_map/ppermute | solution.py:100
  36.4 5.7 %collective-permute-start.2 = (bf16[2,512,512]{2,1,0:T(8,128)(2,1)S(1)}, bf16[2,512,512]{2,1,0:T(8,128)(2,1)S(1)}, u32[]{:S(2)}, u32[]{:S(2)}) collective-permute-start(bf16[2,512,512]{2,1,0:T(8,128)(2,1)S(1)} %early_away.1), channel_id=1, source_target_pairs={{0,1},{1,0},{2,3},{3,2},{4,5},{5,4},{6,7},{7,6},{8,9},{9,8},{10,11... | collective-permute-start | bytes 3145736 | tf_op jit(solution)/shard_map/ppermute | solution.py:100
  36.5 0.9 copy-start.15
  37.4 48.2 %collective-permute-start.12 = (bf16[256,512]{1,0:T(8,128)(2,1)}, bf16[256,512]{1,0:T(8,128)(2,1)}, u32[]{:S(2)}, u32[]{:S(2)}) collective-permute-start(bf16[256,512]{1,0:T(8,128)(2,1)} %fusion.9), channel_id=1, source_target_pairs={{0,2},{2,0},{1,3},{3,1},{4,6},{6,4},{5,7},{7,5},{8,10},{10,8},{9,1... | collective-permute-start | bytes 786440 | tf_op jit(solution)/shard_map/ppermute | solution.py:100
  42.1 4.5 %copy-start = (f32[2,512,512]{2,1,0:T(8,128)}, f32[2,512,512]{2,1,0:T(8,128)S(1)}, u32[]{:S(2)}) copy-start(f32[2,512,512]{2,1,0:T(8,128)S(1)} %early_kept.1) | copy-start | bytes 6291460
  42.1 1.7 %copy-start.9 = (s32[1,8]{1,0:T(1,128)S(1)}, s32[1,8]{1,0:T(1,128)}, u32[]{:S(2)}) copy-start(s32[1,8]{1,0:T(1,128)} %param.12) | copy-start | bytes 100
  42.2 1.6 %copy-start.14 = (bf16[2,512,512]{2,1,0:T(8,128)(2,1)}, bf16[2,512,512]{2,1,0:T(8,128)(2,1)S(1)}, u32[]{:S(2)}) copy-start(bf16[2,512,512]{2,1,0:T(8,128)(2,1)S(1)} %collective-permute-done.2) | copy-start | bytes 3145732
  43.1 15.8 %collective-permute-start.3 = (bf16[256,512]{1,0:T(8,128)(2,1)}, bf16[256,512]{1,0:T(8,128)(2,1)}, u32[]{:S(2)}, u32[]{:S(2)}) collective-permute-start(bf16[256,512]{1,0:T(8,128)(2,1)} %get-tuple-element.86), channel_id=1, source_target_pairs={{0,2},{2,0},{1,3},{3,1},{4,6},{6,4},{5,7},{7,5},{8,10},{10,8},{9,1... | collective-permute-start | bytes 786440 | tf_op jit(solution)/shard_map/ppermute | solution.py:100
  43.8 2.9 %copy-start.8 = (bf16[256,2,1,2048]{3,1,2,0:T(2,128)(2,1)S(1)}, bf16[256,2,1,2048]{3,1,2,0:T(2,128)(2,1)}, u32[]{:S(2)}) copy-start(bf16[256,2,1,2048]{3,1,2,0:T(2,128)(2,1)} %param.10) | copy-start | bytes 6291460
  46.6 10.9 %copy-start.10 = (bf16[288,1024]{1,0:T(8,128)(2,1)}, bf16[288,1024]{1,0:T(8,128)(2,1)S(1)}, u32[]{:S(2)}) copy-start(bf16[288,1024]{1,0:T(8,128)(2,1)S(1)} %get-tuple-element.69.values) | copy-start | bytes 1769476
  46.7 10.9 %copy-start.12 = (bf16[1024,256]{1,0:T(8,128)(2,1)}, bf16[1024,256]{1,0:T(8,128)(2,1)S(1)}, u32[]{:S(2)}) copy-start(bf16[1024,256]{1,0:T(8,128)(2,1)S(1)} %get-tuple-element.68.keys) | copy-start | bytes 1572868
  57.5 10.7 %collective-permute-start.7 = (bf16[256,512]{1,0:T(8,128)(2,1)}, bf16[256,512]{1,0:T(8,128)(2,1)}, u32[]{:S(2)}, u32[]{:S(2)}) collective-permute-start(bf16[256,512]{1,0:T(8,128)(2,1)} %get-tuple-element.67), channel_id=1, source_target_pairs={{0,2},{2,0},{1,3},{3,1},{4,6},{6,4},{5,7},{7,5},{8,10},{10,8},{9,1... | collective-permute-start | bytes 786440 | tf_op jit(solution)/shard_map/ppermute | solution.py:100
  63.5 2.6 %copy-start.17 = (bf16[256,512]{1,0:T(8,128)(2,1)S(1)}, bf16[256,512]{1,0:T(8,128)(2,1)}, u32[]{:S(2)}) copy-start(bf16[256,512]{1,0:T(8,128)(2,1)} %fusion.7) | copy-start | bytes 786436
  63.5 4.6 %collective-permute-start.6 = (bf16[2,256,512]{2,1,0:T(8,128)(2,1)S(1)}, bf16[2,256,512]{2,1,0:T(8,128)(2,1)S(1)}, u32[]{:S(2)}, u32[]{:S(2)}) collective-permute-start(bf16[2,256,512]{2,1,0:T(8,128)(2,1)S(1)} %late_away.1), channel_id=1, source_target_pairs={{0,1},{1,0},{2,3},{3,2},{4,5},{5,4},{6,7},{7,6},{8,9},{9,8},{10,11... | collective-permute-start | bytes 1572872 | tf_op jit(solution)/shard_map/ppermute | solution.py:100
  66.2 5.6 %copy-start.11 = (bf16[288,1024]{1,0:T(8,128)(2,1)S(1)}, bf16[288,1024]{1,0:T(8,128)(2,1)}, u32[]{:S(2)}) copy-start(bf16[288,1024]{1,0:T(8,128)(2,1)} %copy-done.10) | copy-start | bytes 1769476
  66.2 5.6 %copy-start.13 = (bf16[1024,256]{1,0:T(8,128)(2,1)S(1)}, bf16[1024,256]{1,0:T(8,128)(2,1)}, u32[]{:S(2)}) copy-start(bf16[1024,256]{1,0:T(8,128)(2,1)} %copy-done.12) | copy-start | bytes 1572868
  66.2 16.2 %collective-permute-start.9 = (bf16[256,512]{1,0:T(8,128)(2,1)S(1)}, bf16[256,512]{1,0:T(8,128)(2,1)S(1)}, u32[]{:S(2)}, u32[]{:S(2)}) collective-permute-start(bf16[256,512]{1,0:T(8,128)(2,1)S(1)} %copy-done.17), channel_id=1, source_target_pairs={{0,4},{4,0},{8,12},{12,8},{1,5},{5,1},{9,13},{13,9},{2,6},{6,2},{1... | collective-permute-start | bytes 786440 | tf_op jit(solution)/shard_map/ppermute | solution.py:104
  69.5 16.2 %collective-permute-start.13 = (bf16[256,512]{1,0:T(8,128)(2,1)S(1)}, bf16[256,512]{1,0:T(8,128)(2,1)S(1)}, u32[]{:S(2)}, u32[]{:S(2)}) collective-permute-start(bf16[256,512]{1,0:T(8,128)(2,1)S(1)} %fusion.2), channel_id=1, source_target_pairs={{0,4},{4,0},{8,12},{12,8},{1,5},{5,1},{9,13},{13,9},{2,6},{6,2},{1... | collective-permute-start | bytes 786440 | tf_op jit(solution)/shard_map/ppermute | solution.py:104
  69.7 15.9 %copy-start.2 = (f32[2,256,512]{2,1,0:T(8,128)S(1)}, f32[2,256,512]{2,1,0:T(8,128)}, u32[]{:S(2)}) copy-start(f32[2,256,512]{2,1,0:T(8,128)} %copy-done.1) | copy-start | bytes 3145732
  69.7 15.9 %copy-start.16 = (bf16[2,256,512]{2,1,0:T(8,128)(2,1)S(1)}, bf16[2,256,512]{2,1,0:T(8,128)(2,1)}, u32[]{:S(2)}) copy-start(bf16[2,256,512]{2,1,0:T(8,128)(2,1)} %copy-done.15) | copy-start | bytes 1572868
  69.7 12.7 %collective-permute-start.8 = (bf16[128,512]{1,0:T(8,128)(2,1)S(1)}, bf16[128,512]{1,0:T(8,128)(2,1)S(1)}, u32[]{:S(2)}, u32[]{:S(2)}) collective-permute-start(bf16[128,512]{1,0:T(8,128)(2,1)S(1)} %get-tuple-element.87), channel_id=1, source_target_pairs={{0,2},{2,0},{1,3},{3,1},{4,6},{6,4},{5,7},{7,5},{8,10},{10,8},{9,1... | collective-permute-start | bytes 393224 | tf_op jit(solution)/shard_map/ppermute | solution.py:100
  70.7 13.1 %collective-permute-start.14 = (bf16[128,512]{1,0:T(8,128)(2,1)S(1)}, bf16[128,512]{1,0:T(8,128)(2,1)S(1)}, u32[]{:S(2)}, u32[]{:S(2)}) collective-permute-start(bf16[128,512]{1,0:T(8,128)(2,1)S(1)} %get-tuple-element.78), channel_id=1, source_target_pairs={{0,2},{2,0},{1,3},{3,1},{4,6},{6,4},{5,7},{7,5},{8,10},{10,8},{9,1... | collective-permute-start | bytes 393224 | tf_op jit(solution)/shard_map/ppermute | solution.py:100
  82.5 12.8 %collective-permute-start.10 = (bf16[128,512]{1,0:T(8,128)(2,1)S(1)}, bf16[128,512]{1,0:T(8,128)(2,1)S(1)}, u32[]{:S(2)}, u32[]{:S(2)}) collective-permute-start(bf16[128,512]{1,0:T(8,128)(2,1)S(1)} %fusion.15), channel_id=1, source_target_pairs={{0,8},{4,12},{8,0},{12,4},{1,9},{5,13},{9,1},{13,5},{2,10},{6,14},... | collective-permute-start | bytes 393224 | tf_op jit(solution)/shard_map/ppermute | solution.py:104
  83.8 15.9 %collective-permute-start.15 = (bf16[128,512]{1,0:T(8,128)(2,1)S(1)}, bf16[128,512]{1,0:T(8,128)(2,1)S(1)}, u32[]{:S(2)}, u32[]{:S(2)}) collective-permute-start(bf16[128,512]{1,0:T(8,128)(2,1)S(1)} %fusion.19), channel_id=1, source_target_pairs={{0,8},{4,12},{8,0},{12,4},{1,9},{5,13},{9,1},{13,5},{2,10},{6,14},... | collective-permute-start | bytes 393224 | tf_op jit(solution)/shard_map/ppermute | solution.py:104

commit v8 on v7

--- a/solution.py
+++ b/solution.py
@@ -9,7 +9,7 @@
 from jax.sharding import PartitionSpec as P
 
 CHUNKS = 2
-PART = 512
+PART = 1024
 ONES = 16
 VMEM_BYTES = 24 * 1024 * 1024
 LONG = pl.CostEstimate(flops=10**11, bytes_accessed=1, transcendentals=0)
@@ -542,29 +542,35 @@
     if steps:
         early = projected(arrived, "early")
         cuts = [slice(i * token_count, (i + 1) * token_count) for i in range(len(steps))]
-        far_others = spread(others(early, cuts[0]))
-        near_others, pools = after(others(early, cuts[1]), pools)
-        near_others = spread(near_others)
+        leaving = [others(early, cut) for cut in cuts]
+        leaving, pools = after(leaving, pools)
+        far_others, near_others = (spread(parts) for parts in leaving)
     keys, values = pick_blocks(place, block_table[0], pools, heads)
     states = [prefix_attend(query_rows, keys, values, 0, scale, heads)]
     states[0], last = after(states[0], last)
     if steps:
+        far_others, last = after(far_others, last)
+
+    terms = [
+        shift(project(place, [last], weights, step, jnp.bfloat16, "late_away"), "head", step)
+        for step in range(1, head_count)
+    ]
+    if steps:
         far = summed(early, cuts[0], far_others).astype(jnp.bfloat16)
         far, last = after(far, last)
         far = trade(far, "batch", 1)
-
-    late = projected([last], "late")
+    late = [project(place, [last], weights, 0, jnp.float32, "late_kept"), *terms]
     late_others = [others(late, here) for here in parts_of]
-    waiting = (keys, values, near_others) if steps else (keys, values)
-    late_others[-1], waiting = after(late_others[-1], waiting)
-    keys, values, *near_others = waiting
+    late_others[-1], (keys, values) = after(late_others[-1], (keys, values))
     late_others = [spread(part) for part in late_others]
     states.append(prefix_attend(query_rows, keys, values, 1, scale, heads))
-    states[1], late_others[0] = after(states[1], late_others[0])
+    if steps:
+        states[1], (late_others[0], near_others) = after(
+            states[1], (late_others[0], near_others)
+        )
 
     home = summed(own, every, own_others)
     if steps:
-        near_others = near_others[0]
         near = trade(summed(early, cuts[1], near_others).astype(jnp.bfloat16), "batch", 1)
         home = home + near.astype(jnp.float32)
     parts = []
@@ -574,7 +580,11 @@
             part = part + far[here].astype(jnp.float32)
             if chunk + 1 < CHUNKS:
                 (far, late), late_others[chunk + 1] = after((far, late), late_others[chunk + 1])
-        parts.append((trade(part.astype(jnp.bfloat16), "batch", top), home[here]))
+        part = part.astype(jnp.bfloat16)
+        if parts:
+            parts[-1], part = after(parts[-1], part)
+        parts.append(trade(part, "batch", top))
+    parts = [(part, home[here]) for part, here in zip(parts, parts_of)]
 
     result = None
     for chunk in range(CHUNKS):

time: 107 us -> 97.6 us (0.912)
  Pallas kernels: 58.4 us -> 51.2 us
  waiting for transfers between devices: 20.6 us -> 16.3 us
  other arithmetic: 6.5 us -> 8.39 us
    pallas_call x2, Pallas kernels: 21.5 us -> 15.6 us  [prefix_attend(): pl.pallas_call(functools.partial(prefix_kernel, scale, heads), grid=(step...]
    ppermute x7, waiting for transfers between devices: 20.6 us -> 16.2 us  [trade(): lax.ppermute(array, axis, [(i, i ^ bits) for i in range(lax.axis_size(axi...]
    convert_element_type x2, other arithmetic: 0.14 us -> 1.93 us  [reduced_shards(): part = part.astype(jnp.bfloat16)]
    pallas_call x2, Pallas kernels: 11.3 us -> 9.95 us  [fresh_attend(): pl.pallas_call(functools.partial(fresh_kernel, scale, heads, per_token, c...]
    ppermute x7, starting transfers between devices: 11.2 us -> 12.5 us  [trade(): lax.ppermute(array, axis, [(i, i ^ bits) for i in range(lax.axis_size(axi...]
  transfers between devices with their start and end apart: 16 -> 16, of which waited for: 3 -> 3; matrix products, arithmetic and copies ran while one was open for 6% -> 9% of each run, Pallas kernels for 47% -> 45%
where the time goes in v8:
time: 97.6 us; the launch traced here: 97.2 us
  Pallas kernels  51.2 us (52%)
  starting transfers between devices  18.7 us (19%)
  waiting for transfers between devices  16.3 us (17%)
  other arithmetic  8.39 us (9%)
  local copies, waits for them, and re-layouts  1.68 us (2%)
    ppermute x7, waiting for transfers between devices, trade(): lax.ppermute(array, axis, [(i, i ^ bits) for i in range(lax.axis_size(axi...  16.2 us
    pallas_call x2, Pallas kernels, prefix_attend(): pl.pallas_call(functools.partial(prefix_kernel, scale, heads), grid=(step...  15.6 us
    pallas_call x6, Pallas kernels, project(): pl.pallas_call(project_kernel, grid_spec=pltpu.PrefetchScalarGridSpec(num...  14.7 us
    ppermute x7, starting transfers between devices, trade(): lax.ppermute(array, axis, [(i, i ^ bits) for i in range(lax.axis_size(axi...  12.5 us
    pallas_call x2, Pallas kernels, fresh_attend(): pl.pallas_call(functools.partial(fresh_kernel, scale, heads, per_token, c...  9.95 us
    ppermute x9, starting transfers between devices, shift(): lax.ppermute(array, axis, [(i, (i + step) % count) for i in range(count)])  6.15 us
    pallas_call x1, Pallas kernels, arrange_pool(): pl.pallas_call(functools.partial(pool_kernel, ctx_count, heads), grid_spe...  3.92 us
    pallas_call x1, Pallas kernels, pick_blocks(): pl.pallas_call(functools.partial(pick_kernel, heads, len(pools)), grid_sp...  2.83 us
  transfers between devices with their start and end apart: 16, of which 3 were waited for; matrix products, arithmetic and copies ran while one was open for 9% of the time, Pallas kernels for 45%

profile of v8, /device:TPU:0, one launch (start us, length us, event | category | flops | bytes accessed | tf_op | source)
XLA Modules:
  0.0 97.2 jit_solution(16424460751346389011)
XLA Ops:
  0.0 0.1 pad_add_fusion.place_ref
  0.1 1.6 %copy-done.6 = bf16[256,4096]{1,0:T(8,128)(2,1)S(1)} copy-done((bf16[256,4096]{1,0:T(8,128)(2,1)S(1)}, bf16[256,4096]{1,0:T(8,128)(2,1)}, u32[]{:S(2)}) %copy-start.6) | copy-done | bytes 2097176
  1.7 1.7 %cut_tokens.1 = (bf16[256,1024]{1,0:T(8,128)(2,1)}, bf16[256,1024]{1,0:T(8,128)(2,1)}, bf16[256,1024]{1,0:T(8,128)(2,1)}) custom-call(s32[3]{0:T(128)S(1)} %pad_add_fusion.place_ref, bf16[256,4096]{1,0:T(8,128)(2,1)S(1)} %copy-done.6), custom_call_target="tpu_custom_call" | custom-call | flops 99999997952 | bytes 1 | tf_op jit(solution)/shard_map/cut_tokens/pallas_call | solution.py:469
  3.4 5.1 %collective-permute-start = (bf16[256,1024]{1,0:T(8,128)(2,1)}, bf16[256,1024]{1,0:T(8,128)(2,1)}, u32[]{:S(2)}, u32[]{:S(2)}) collective-permute-start(bf16[256,1024]{1,0:T(8,128)(2,1)} %get-tuple-element.53), channel_id=1, source_target_pairs={{0,12},{4,8},{8,4},{12,0},{1,13},{5,9},{9,5},{13,1},{2,14},{6,10},... | collective-permute-start | bytes 1572872 | tf_op jit(solution)/shard_map/ppermute | solution.py:104
  8.5 3.9 %arrange_pool.1 = (bf16[8,128,512]{2,1,0:T(8,128)(2,1)S(1)}, bf16[8,128,512]{2,1,0:T(8,128)(2,1)}) custom-call(s32[3]{0:T(128)S(1)} %pad_add_fusion.place_ref, bf16[8,128,8,128]{3,2,1,0:T(8,128)(2,1)S(1)} %bitcast.61), custom_call_target="tpu_custom_call" | custom-call | flops 99999997952 | bytes 1 | tf_op jit(solution)/shard_map/arrange_pool/pallas_call | solution.py:189
  12.5 1.5 %collective-permute-start.3 = (bf16[8,128,512]{2,1,0:T(8,128)(2,1)}, bf16[8,128,512]{2,1,0:T(8,128)(2,1)}, u32[]{:S(2)}, u32[]{:S(2)}) collective-permute-start(bf16[8,128,512]{2,1,0:T(8,128)(2,1)} %get-tuple-element.61), channel_id=1, source_target_pairs={{0,2},{2,0},{1,3},{3,1},{4,6},{6,4},{5,7},{7,5},{8,10},{10,8},{9,1... | collective-permute-start | bytes 3145736 | tf_op jit(solution)/shard_map/ppermute | solution.py:100
  14.0 2.5 %arrange_weights.1.refs_2_.refs_1_ = bf16[2,2,1024,512]{3,2,1,0:T(8,128)(2,1)S(1)} custom-call(bf16[1024,8,128]{2,1,0:T(8,128)(2,1)S(1)} %bitcast.62, bf16[1024,8,128]{2,1,0:T(8,128)(2,1)S(1)} %bitcast.63), custom_call_target="tpu_custom_call" | custom-call | flops 99999997952 | bytes 1 | tf_op jit(solution)/shard_map/arrange_weights/pallas_call | solution.py:149
  16.4 1.6 %own_away.1 = bf16[2,256,512]{2,1,0:T(8,128)(2,1)S(1)} custom-call(s32[3]{0:T(128)S(1)} %pad_add_fusion.place_ref, bf16[256,4096]{1,0:T(8,128)(2,1)S(1)} %copy-done.7, bf16[2,2,1024,512]{3,2,1,0:T(8,128)(2,1)S(1)} %arrange_weights.1.refs_2_.refs_1_), custom_call_target="tpu_custom_call" | custom-call | flops 99999997952 | bytes 1 | tf_op jit(solution)/shard_map/own_away/pallas_call | solution.py:230
  18.0 0.1 collective-permute-start.12
  18.1 1.5 %own_kept.1 = f32[2,256,512]{2,1,0:T(8,128)S(1)} custom-call(s32[3]{0:T(128)S(1)} %pad_add_fusion.place_ref, bf16[256,4096]{1,0:T(8,128)(2,1)S(1)} %copy-done.7, bf16[2,2,1024,512]{3,2,1,0:T(8,128)(2,1)S(1)} %arrange_weights.1.refs_2_.refs_1_), custom_call_target="tpu_custom_call" | custom-call | flops 99999997952 | bytes 1 | tf_op jit(solution)/shard_map/own_kept/pallas_call | solution.py:230
  19.6 0.8 collective-permute-start.5
  21.1 0.0 collective-permute-done.12
  21.2 0.9 fusion.9
  22.0 0.4 collective-permute-start.13
  22.4 0.0 collective-permute-done.refs_0_
  22.4 10.7 %collective-permute-done.1.refs_1_ = bf16[256,1024]{1,0:T(8,128)(2,1)} collective-permute-done((bf16[256,1024]{1,0:T(8,128)(2,1)}, bf16[256,1024]{1,0:T(8,128)(2,1)}, u32[]{:S(2)}, u32[]{:S(2)}) %collective-permute-start.1) | collective-permute-done | bytes 524320 | tf_op jit(solution)/shard_map/ppermute | solution.py:104
  33.1 3.3 %early_away.1 = bf16[2,512,512]{2,1,0:T(8,128)(2,1)S(1)} custom-call(s32[3]{0:T(128)S(1)} %pad_add_fusion.place_ref, bf16[256,1024]{1,0:T(8,128)(2,1)} %collective-permute-done.refs_0_, bf16[256,1024]{1,0:T(8,128)(2,1)} %collective-permute-done.1.refs_1_, bf16[2,2,1024,512]{3,2,1,0:T(8,128)(2,1)S(1)} %arrange_weights.1.refs_2_.refs_1_), custom_call_target="tpu_custom_call" | custom-call | flops 99999997952 | bytes 1 | tf_op jit(solution)/shard_map/early_away/pallas_call | solution.py:230
  36.4 0.1 collective-permute-start.2
  36.5 3.3 %early_kept.1 = f32[2,512,512]{2,1,0:T(8,128)S(1)} custom-call(s32[3]{0:T(128)S(1)} %pad_add_fusion.place_ref, bf16[256,1024]{1,0:T(8,128)(2,1)} %collective-permute-done.refs_0_, bf16[256,1024]{1,0:T(8,128)(2,1)} %collective-permute-done.1.refs_1_, bf16[2,2,1024,512]{3,2,1,0:T(8,128)(2,1)S(1)} %arrange_weights.1.refs_2_.refs_1_), custom_call_target="tpu_custom_call" | custom-call | flops 99999997952 | bytes 1 | tf_op jit(solution)/shard_map/early_kept/pallas_call | solution.py:230
  39.8 0.0 copy-start
  39.8 0.0 copy-start.9
  39.9 1.0 fusion.11
  40.8 0.0 collective-permute-done.3.refs_1_
  40.8 1.4 %collective-permute-start.4 = (bf16[256,512]{1,0:T(8,128)(2,1)}, bf16[256,512]{1,0:T(8,128)(2,1)}, u32[]{:S(2)}, u32[]{:S(2)}) collective-permute-start(bf16[256,512]{1,0:T(8,128)(2,1)} %get-tuple-element.62), channel_id=1, source_target_pairs={{0,2},{2,0},{1,3},{3,1},{4,6},{6,4},{5,7},{7,5},{8,10},{10,8},{9,1... | collective-permute-start | bytes 786440 | tf_op jit(solution)/shard_map/ppermute | solution.py:100
  42.2 0.6 collective-permute-start.8
  42.9 2.8 %pick_blocks.1 = (bf16[1024,256]{1,0:T(8,128)(2,1)S(1)}, bf16[288,1024]{1,0:T(8,128)(2,1)S(1)}) custom-call(s32[3]{0:T(128)S(1)} %pad_add_fusion.place_ref, s32[8]{0:T(128)S(1)} %bitcast.68, bf16[8,128,512]{2,1,0:T(8,128)(2,1)S(1)} %get-tuple-element.63.refs_0_, bf16[8,128,512]{2,1,0:T(8,128)(2,1)} %collective-permute-done.3.refs_1_), custom_call_target="tpu_custom_call" | custom-call | flops 99999997952 | bytes 1 | tf_op jit(solution)/shard_map/pick_blocks/pallas_call | solution.py:290
  45.7 7.8 %prefix_attend.2 = (f32[128,4096]{1,0:T(8,128)S(1)}, f32[8,4096]{1,0:T(8,128)S(1)}) custom-call(bf16[8192,128]{1,0:T(8,128)(2,1)S(1)} %bitcast.64, bf16[1024,256]{1,0:T(8,128)(2,1)S(1)} %get-tuple-element.75.keys, bf16[288,1024]{1,0:T(8,128)(2,1)S(1)} %get-tuple-element.76.values), custom_call_target="tpu_custom_call" | custom-call | flops 99999997952 | bytes 1 | tf_op jit(solution)/shard_map/prefix_attend/pallas_call | solution.py:342
  53.5 0.1 collective-permute-done.5.refs_0_
  53.6 2.5 %late_away.1 = bf16[2,256,512]{2,1,0:T(8,128)(2,1)S(1)} custom-call(s32[3]{0:T(128)S(1)} %pad_add_fusion.place_ref, bf16[256,1024]{1,0:T(8,128)(2,1)} %collective-permute-done.5.refs_0_, bf16[2,2,1024,512]{3,2,1,0:T(8,128)(2,1)S(1)} %arrange_weights.1.refs_2_.refs_1_), custom_call_target="tpu_custom_call" | custom-call | flops 99999997952 | bytes 1 | tf_op jit(solution)/shard_map/late_away/pallas_call | solution.py:230
  56.2 2.0 %fusion.7 = bf16[256,512]{1,0:T(8,128)(2,1)} fusion(f32[2,512,512]{2,1,0:T(8,128)} %copy-done, bf16[256,512]{1,0:T(8,128)(2,1)} %collective-permute-done.4, bf16[2,512,512]{2,1,0:T(8,128)(2,1)} %copy-done.10), kind=kLoop, calls=%fused_computation.11 | loop fusion | flops 655360 | bytes 1310720 | tf_op jit(solution)/shard_map/convert_element_type | solution.py:559
  58.2 1.7 %collective-permute-start.9 = (bf16[256,512]{1,0:T(8,128)(2,1)}, bf16[256,512]{1,0:T(8,128)(2,1)}, u32[]{:S(2)}, u32[]{:S(2)}) collective-permute-start(bf16[256,512]{1,0:T(8,128)(2,1)} %fusion.7), channel_id=1, source_target_pairs={{0,4},{4,0},{8,12},{12,8},{1,5},{5,1},{9,13},{13,9},{2,6},{6,2},{1... | collective-permute-start | bytes 786440 | tf_op jit(solution)/shard_map/ppermute | solution.py:104
  59.8 2.5 %late_kept.1 = f32[2,256,512]{2,1,0:T(8,128)S(1)} custom-call(s32[3]{0:T(128)S(1)} %pad_add_fusion.place_ref, bf16[256,1024]{1,0:T(8,128)(2,1)} %collective-permute-done.5.refs_0_, bf16[2,2,1024,512]{3,2,1,0:T(8,128)(2,1)S(1)} %arrange_weights.1.refs_2_.refs_1_), custom_call_target="tpu_custom_call" | custom-call | flops 99999997952 | bytes 1 | tf_op jit(solution)/shard_map/late_kept/pallas_call | solution.py:230
  62.4 0.0 collective-permute-done.6
  62.4 0.1 fusion.21
  62.5 1.6 %collective-permute-start.11 = (bf16[128,512]{1,0:T(8,128)(2,1)S(1)}, bf16[128,512]{1,0:T(8,128)(2,1)S(1)}, u32[]{:S(2)}, u32[]{:S(2)}) collective-permute-start(bf16[128,512]{1,0:T(8,128)(2,1)S(1)} %get-tuple-element.84), channel_id=1, source_target_pairs={{0,2},{2,0},{1,3},{3,1},{4,6},{6,4},{5,7},{7,5},{8,10},{10,8},{9,1... | collective-permute-start | bytes 393224 | tf_op jit(solution)/shard_map/ppermute | solution.py:100
  64.0 0.5 collective-permute-start.7
  64.6 7.8 %prefix_attend.3 = (f32[128,4096]{1,0:T(8,128)S(1)}, f32[8,4096]{1,0:T(8,128)S(1)}) custom-call(bf16[8192,128]{1,0:T(8,128)(2,1)S(1)} %bitcast.65, bf16[1024,256]{1,0:T(8,128)(2,1)S(1)} %get-tuple-element.75.keys, bf16[288,1024]{1,0:T(8,128)(2,1)S(1)} %get-tuple-element.76.values), custom_call_target="tpu_custom_call" | custom-call | flops 99999997952 | bytes 1 | tf_op jit(solution)/shard_map/prefix_attend/pallas_call | solution.py:342
  72.4 0.0 collective-permute-done.8
  72.4 1.4 %fusion.2 = bf16[256,512]{1,0:T(8,128)(2,1)S(1)} fusion(f32[2,512,512]{2,1,0:T(8,128)} %copy-done, bf16[256,512]{1,0:T(8,128)(2,1)} %collective-permute-done.8, bf16[2,512,512]{2,1,0:T(8,128)(2,1)} %copy-done.10), kind=kLoop, calls=%fused_computation.3 | loop fusion | flops 655360 | bytes 1310720 | tf_op jit(solution)/shard_map/convert_element_type | solution.py:574
  73.8 0.4 collective-permute-start.14
  74.2 1.0 fusion.15
  75.2 1.1 %collective-permute-start.10 = (bf16[128,512]{1,0:T(8,128)(2,1)S(1)}, bf16[128,512]{1,0:T(8,128)(2,1)S(1)}, u32[]{:S(2)}, u32[]{:S(2)}) collective-permute-start(bf16[128,512]{1,0:T(8,128)(2,1)S(1)} %fusion.15), channel_id=1, source_target_pairs={{0,8},{4,12},{8,0},{12,4},{1,9},{5,13},{9,1},{13,5},{2,10},{6,14},... | collective-permute-start | bytes 393224 | tf_op jit(solution)/shard_map/ppermute | solution.py:104
  76.3 1.0 fusion.19
  77.3 5.4 %collective-permute-done.10.rest_0_ = bf16[128,512]{1,0:T(8,128)(2,1)S(1)} collective-permute-done((bf16[128,512]{1,0:T(8,128)(2,1)S(1)}, bf16[128,512]{1,0:T(8,128)(2,1)S(1)}, u32[]{:S(2)}, u32[]{:S(2)}) %collective-permute-start.10) | collective-permute-done | bytes 131104 | tf_op jit(solution)/shard_map/ppermute | solution.py:104
  82.7 3.4 %collective-permute-start.15 = (bf16[128,512]{1,0:T(8,128)(2,1)S(1)}, bf16[128,512]{1,0:T(8,128)(2,1)S(1)}, u32[]{:S(2)}, u32[]{:S(2)}) collective-permute-start(bf16[128,512]{1,0:T(8,128)(2,1)S(1)} %fusion.19), channel_id=1, source_target_pairs={{0,8},{4,12},{8,0},{12,4},{1,9},{5,13},{9,1},{13,5},{2,10},{6,14},... | collective-permute-start | bytes 393224 | tf_op jit(solution)/shard_map/ppermute | solution.py:104
  86.1 1.1 %fusion.8 = f32[256,512]{1,0:T(8,128)S(1)} fusion(bf16[256,512]{1,0:T(8,128)(2,1)S(1)} %collective-permute-done.14, bf16[256,512]{1,0:T(8,128)(2,1)} %collective-permute-done.13, f32[2,256,512]{2,1,0:T(8,128)S(1)} %copy-done.2, bf16[2,256,512]{2,1,0:T(8,128)(2,1)S(1)} %copy-done.12), kind=kLoop, calls=%fused_computation.13 | loop fusion | flops 786432 | bytes 1835008 | tf_op jit(solution)/shard_map/add | solution.py:575
  87.2 4.6 %fresh_attend.2.rest_4_ = bf16[8192,128]{1,0:T(8,128)(2,1)} custom-call(s32[1]{0:T(128)S(6)} %copy.13.length_ref, bf16[8192,128]{1,0:T(8,128)(2,1)S(1)} %bitcast.66, f32[128,4096]{1,0:T(8,128)S(1)} %get-tuple-element.93.acc_ref, f32[8,4096]{1,0:T(8,128)S(1)} %get-tuple-element.94.stat_ref, bf16[128,512]{1,0:T(8,128)(2,1)S(1)} %collective-permute-done.10.rest_0_, ...), custom_call_target="tpu_custom_call" | custom-call | flops 99999997952 | bytes 1 | tf_op jit(solution)/shard_map/fresh_attend/pallas_call | solution.py:426
  91.9 5.3 %fresh_attend.3 = bf16[8192,128]{1,0:T(8,128)(2,1)} custom-call(s32[1]{0:T(128)S(6)} %copy.13.length_ref, bf16[8192,128]{1,0:T(8,128)(2,1)S(1)} %bitcast.67, f32[128,4096]{1,0:T(8,128)S(1)} %get-tuple-element.80.acc_ref, f32[8,4096]{1,0:T(8,128)S(1)} %get-tuple-element.81.stat_ref, ...), custom_call_target="tpu_custom_call", output_to_operand_aliasing={{}: (8, {})} | custom-call | flops 99999997952 | bytes 1 | tf_op jit(solution)/shard_map/fresh_attend/pallas_call | solution.py:426
  (34 shorter events, 0.1 us)
Async XLA Ops:
  0.1 1.6 %copy-start.6 = (bf16[256,4096]{1,0:T(8,128)(2,1)S(1)}, bf16[256,4096]{1,0:T(8,128)(2,1)}, u32[]{:S(2)}) copy-start(bf16[256,4096]{1,0:T(8,128)(2,1)} %refs_0_.3) | copy-start | bytes 6291460
  1.7 6.8 %copy-start.3 = (bf16[8,128,4,1,256]{4,2,3,1,0:T(4,128)(2,1)S(1)}, bf16[8,128,4,1,256]{4,2,3,1,0:T(4,128)(2,1)}, u32[]{:S(2)}) copy-start(bf16[8,128,4,1,256]{4,2,3,1,0:T(4,128)(2,1)} %param.11) | copy-start | bytes 6291460
  3.4 19.0 %collective-permute-start = (bf16[256,1024]{1,0:T(8,128)(2,1)}, bf16[256,1024]{1,0:T(8,128)(2,1)}, u32[]{:S(2)}, u32[]{:S(2)}) collective-permute-start(bf16[256,1024]{1,0:T(8,128)(2,1)} %get-tuple-element.53), channel_id=1, source_target_pairs={{0,12},{4,8},{8,4},{12,0},{1,13},{5,9},{9,5},{13,1},{2,14},{6,10},... | collective-permute-start | bytes 1572872 | tf_op jit(solution)/shard_map/ppermute | solution.py:104
  8.5 24.6 %collective-permute-start.1 = (bf16[256,1024]{1,0:T(8,128)(2,1)}, bf16[256,1024]{1,0:T(8,128)(2,1)}, u32[]{:S(2)}, u32[]{:S(2)}) collective-permute-start(bf16[256,1024]{1,0:T(8,128)(2,1)} %get-tuple-element.54), channel_id=1, source_target_pairs={{0,4},{4,0},{8,12},{12,8},{1,5},{5,1},{9,13},{13,9},{2,6},{6,2},{1... | collective-permute-start | bytes 1572872 | tf_op jit(solution)/shard_map/ppermute | solution.py:104
  8.5 5.4 %copy-start.4 = (bf16[1,1,1024,4,2,128]{5,4,3,2,1,0:T(2,128)(2,1)S(1)}, bf16[1,1,1024,4,2,128]{5,4,3,2,1,0:T(2,128)(2,1)}, u32[]{:S(2)}) copy-start(bf16[1,1,1024,4,2,128]{5,4,3,2,1,0:T(2,128)(2,1)} %param.8) | copy-start | bytes 6291460
  8.5 5.4 %copy-start.5 = (bf16[1,1,1024,4,2,128]{5,4,3,2,1,0:T(2,128)(2,1)S(1)}, bf16[1,1,1024,4,2,128]{5,4,3,2,1,0:T(2,128)(2,1)}, u32[]{:S(2)}) copy-start(bf16[1,1,1024,4,2,128]{5,4,3,2,1,0:T(2,128)(2,1)} %param.9) | copy-start | bytes 6291460
  12.5 28.4 %collective-permute-start.3 = (bf16[8,128,512]{2,1,0:T(8,128)(2,1)}, bf16[8,128,512]{2,1,0:T(8,128)(2,1)}, u32[]{:S(2)}, u32[]{:S(2)}) collective-permute-start(bf16[8,128,512]{2,1,0:T(8,128)(2,1)} %get-tuple-element.61), channel_id=1, source_target_pairs={{0,2},{2,0},{1,3},{3,1},{4,6},{6,4},{5,7},{7,5},{8,10},{10,8},{9,1... | collective-permute-start | bytes 3145736 | tf_op jit(solution)/shard_map/ppermute | solution.py:100
  14.0 2.5 %copy-start.7 = (bf16[256,4096]{1,0:T(8,128)(2,1)S(1)}, bf16[256,4096]{1,0:T(8,128)(2,1)}, u32[]{:S(2)}) copy-start(bf16[256,4096]{1,0:T(8,128)(2,1)} %refs_0_.3) | copy-start | bytes 6291460
  18.0 3.1 %collective-permute-start.12 = (bf16[2,256,512]{2,1,0:T(8,128)(2,1)S(1)}, bf16[2,256,512]{2,1,0:T(8,128)(2,1)S(1)}, u32[]{:S(2)}, u32[]{:S(2)}) collective-permute-start(bf16[2,256,512]{2,1,0:T(8,128)(2,1)S(1)} %own_away.1), channel_id=1, source_target_pairs={{0,1},{1,0},{2,3},{3,2},{4,5},{5,4},{6,7},{7,6},{8,9},{9,8},{10,11... | collective-permute-start | bytes 1572872 | tf_op jit(solution)/shard_map/ppermute | solution.py:100
  19.6 16.8 %copy-start.1 = (f32[2,256,512]{2,1,0:T(8,128)}, f32[2,256,512]{2,1,0:T(8,128)S(1)}, u32[]{:S(2)}) copy-start(f32[2,256,512]{2,1,0:T(8,128)S(1)} %own_kept.1) | copy-start | bytes 3145732
  19.6 34.0 %collective-permute-start.5 = (bf16[256,1024]{1,0:T(8,128)(2,1)}, bf16[256,1024]{1,0:T(8,128)(2,1)}, u32[]{:S(2)}, u32[]{:S(2)}) collective-permute-start(bf16[256,1024]{1,0:T(8,128)(2,1)} %get-tuple-element.70), channel_id=1, source_target_pairs={{0,8},{4,12},{8,0},{12,4},{1,9},{5,13},{9,1},{13,5},{2,10},{6,14},... | collective-permute-start | bytes 1572872 | tf_op jit(solution)/shard_map/ppermute | solution.py:104
  21.1 1.3 %copy-start.11 = (bf16[2,256,512]{2,1,0:T(8,128)(2,1)}, bf16[2,256,512]{2,1,0:T(8,128)(2,1)S(1)}, u32[]{:S(2)}) copy-start(bf16[2,256,512]{2,1,0:T(8,128)(2,1)S(1)} %collective-permute-done.12) | copy-start | bytes 1572868
  22.0 64.1 %collective-permute-start.13 = (bf16[256,512]{1,0:T(8,128)(2,1)}, bf16[256,512]{1,0:T(8,128)(2,1)}, u32[]{:S(2)}, u32[]{:S(2)}) collective-permute-start(bf16[256,512]{1,0:T(8,128)(2,1)} %fusion.9), channel_id=1, source_target_pairs={{0,2},{2,0},{1,3},{3,1},{4,6},{6,4},{5,7},{7,5},{8,10},{10,8},{9,1... | collective-permute-start | bytes 786440 | tf_op jit(solution)/shard_map/ppermute | solution.py:100
  36.4 3.4 %collective-permute-start.2 = (bf16[2,512,512]{2,1,0:T(8,128)(2,1)S(1)}, bf16[2,512,512]{2,1,0:T(8,128)(2,1)S(1)}, u32[]{:S(2)}, u32[]{:S(2)}) collective-permute-start(bf16[2,512,512]{2,1,0:T(8,128)(2,1)S(1)} %early_away.1), channel_id=1, source_target_pairs={{0,1},{1,0},{2,3},{3,2},{4,5},{5,4},{6,7},{7,6},{8,9},{9,8},{10,11... | collective-permute-start | bytes 3145736 | tf_op jit(solution)/shard_map/ppermute | solution.py:100
  39.8 5.9 %copy-start = (f32[2,512,512]{2,1,0:T(8,128)}, f32[2,512,512]{2,1,0:T(8,128)S(1)}, u32[]{:S(2)}) copy-start(f32[2,512,512]{2,1,0:T(8,128)S(1)} %early_kept.1) | copy-start | bytes 6291460
  39.8 3.0 %copy-start.9 = (s32[1,8]{1,0:T(1,128)S(1)}, s32[1,8]{1,0:T(1,128)}, u32[]{:S(2)}) copy-start(s32[1,8]{1,0:T(1,128)} %param.12) | copy-start | bytes 100
  39.8 3.0 %copy-start.10 = (bf16[2,512,512]{2,1,0:T(8,128)(2,1)}, bf16[2,512,512]{2,1,0:T(8,128)(2,1)S(1)}, u32[]{:S(2)}) copy-start(bf16[2,512,512]{2,1,0:T(8,128)(2,1)S(1)} %collective-permute-done.2) | copy-start | bytes 3145732
  40.8 12.8 %collective-permute-start.4 = (bf16[256,512]{1,0:T(8,128)(2,1)}, bf16[256,512]{1,0:T(8,128)(2,1)}, u32[]{:S(2)}, u32[]{:S(2)}) collective-permute-start(bf16[256,512]{1,0:T(8,128)(2,1)} %get-tuple-element.62), channel_id=1, source_target_pairs={{0,2},{2,0},{1,3},{3,1},{4,6},{6,4},{5,7},{7,5},{8,10},{10,8},{9,1... | collective-permute-start | bytes 786440 | tf_op jit(solution)/shard_map/ppermute | solution.py:100
  42.2 30.2 %collective-permute-start.8 = (bf16[256,512]{1,0:T(8,128)(2,1)}, bf16[256,512]{1,0:T(8,128)(2,1)}, u32[]{:S(2)}, u32[]{:S(2)}) collective-permute-start(bf16[256,512]{1,0:T(8,128)(2,1)} %get-tuple-element.79), channel_id=1, source_target_pairs={{0,2},{2,0},{1,3},{3,1},{4,6},{6,4},{5,7},{7,5},{8,10},{10,8},{9,1... | collective-permute-start | bytes 786440 | tf_op jit(solution)/shard_map/ppermute | solution.py:100
  42.9 2.9 %copy-start.8 = (bf16[256,2,1,2048]{3,1,2,0:T(2,128)(2,1)S(1)}, bf16[256,2,1,2048]{3,1,2,0:T(2,128)(2,1)}, u32[]{:S(2)}) copy-start(bf16[256,2,1,2048]{3,1,2,0:T(2,128)(2,1)} %param.10) | copy-start | bytes 6291460
  58.2 16.1 %collective-permute-start.9 = (bf16[256,512]{1,0:T(8,128)(2,1)}, bf16[256,512]{1,0:T(8,128)(2,1)}, u32[]{:S(2)}, u32[]{:S(2)}) collective-permute-start(bf16[256,512]{1,0:T(8,128)(2,1)} %fusion.7), channel_id=1, source_target_pairs={{0,4},{4,0},{8,12},{12,8},{1,5},{5,1},{9,13},{13,9},{2,6},{6,2},{1... | collective-permute-start | bytes 786440 | tf_op jit(solution)/shard_map/ppermute | solution.py:104
  59.8 2.5 %collective-permute-start.6 = (bf16[2,256,512]{2,1,0:T(8,128)(2,1)S(1)}, bf16[2,256,512]{2,1,0:T(8,128)(2,1)S(1)}, u32[]{:S(2)}, u32[]{:S(2)}) collective-permute-start(bf16[2,256,512]{2,1,0:T(8,128)(2,1)S(1)} %late_away.1), channel_id=1, source_target_pairs={{0,1},{1,0},{2,3},{3,2},{4,5},{5,4},{6,7},{7,6},{8,9},{9,8},{10,11... | collective-permute-start | bytes 1572872 | tf_op jit(solution)/shard_map/ppermute | solution.py:100
  62.5 12.7 %collective-permute-start.11 = (bf16[128,512]{1,0:T(8,128)(2,1)S(1)}, bf16[128,512]{1,0:T(8,128)(2,1)S(1)}, u32[]{:S(2)}, u32[]{:S(2)}) collective-permute-start(bf16[128,512]{1,0:T(8,128)(2,1)S(1)} %get-tuple-element.84), channel_id=1, source_target_pairs={{0,2},{2,0},{1,3},{3,1},{4,6},{6,4},{5,7},{7,5},{8,10},{10,8},{9,1... | collective-permute-start | bytes 393224 | tf_op jit(solution)/shard_map/ppermute | solution.py:100
  64.0 8.4 %collective-permute-start.7 = (bf16[128,512]{1,0:T(8,128)(2,1)S(1)}, bf16[128,512]{1,0:T(8,128)(2,1)S(1)}, u32[]{:S(2)}, u32[]{:S(2)}) collective-permute-start(bf16[128,512]{1,0:T(8,128)(2,1)S(1)} %get-tuple-element.97), channel_id=1, source_target_pairs={{0,2},{2,0},{1,3},{3,1},{4,6},{6,4},{5,7},{7,5},{8,10},{10,8},{9,1... | collective-permute-start | bytes 393224 | tf_op jit(solution)/shard_map/ppermute | solution.py:100
  72.4 13.7 %copy-start.2 = (f32[2,256,512]{2,1,0:T(8,128)S(1)}, f32[2,256,512]{2,1,0:T(8,128)}, u32[]{:S(2)}) copy-start(f32[2,256,512]{2,1,0:T(8,128)} %copy-done.1) | copy-start | bytes 3145732
  72.4 13.7 %copy-start.12 = (bf16[2,256,512]{2,1,0:T(8,128)(2,1)S(1)}, bf16[2,256,512]{2,1,0:T(8,128)(2,1)}, u32[]{:S(2)}) copy-start(bf16[2,256,512]{2,1,0:T(8,128)(2,1)} %copy-done.11) | copy-start | bytes 1572868
  73.8 12.3 %collective-permute-start.14 = (bf16[256,512]{1,0:T(8,128)(2,1)S(1)}, bf16[256,512]{1,0:T(8,128)(2,1)S(1)}, u32[]{:S(2)}, u32[]{:S(2)}) collective-permute-start(bf16[256,512]{1,0:T(8,128)(2,1)S(1)} %fusion.2), channel_id=1, source_target_pairs={{0,4},{4,0},{8,12},{12,8},{1,5},{5,1},{9,13},{13,9},{2,6},{6,2},{1... | collective-permute-start | bytes 786440 | tf_op jit(solution)/shard_map/ppermute | solution.py:104
  75.2 7.5 %collective-permute-start.10 = (bf16[128,512]{1,0:T(8,128)(2,1)S(1)}, bf16[128,512]{1,0:T(8,128)(2,1)S(1)}, u32[]{:S(2)}, u32[]{:S(2)}) collective-permute-start(bf16[128,512]{1,0:T(8,128)(2,1)S(1)} %fusion.15), channel_id=1, source_target_pairs={{0,8},{4,12},{8,0},{12,4},{1,9},{5,13},{9,1},{13,5},{2,10},{6,14},... | collective-permute-start | bytes 393224 | tf_op jit(solution)/shard_map/ppermute | solution.py:104
  82.7 9.2 %collective-permute-start.15 = (bf16[128,512]{1,0:T(8,128)(2,1)S(1)}, bf16[128,512]{1,0:T(8,128)(2,1)S(1)}, u32[]{:S(2)}, u32[]{:S(2)}) collective-permute-start(bf16[128,512]{1,0:T(8,128)(2,1)S(1)} %fusion.19), channel_id=1, source_target_pairs={{0,8},{4,12},{8,0},{12,4},{1,9},{5,13},{9,1},{13,5},{2,10},{6,14},... | collective-permute-start | bytes 393224 | tf_op jit(solution)/shard_map/ppermute | solution.py:104

commit v9 on v7

--- a/solution.py
+++ b/solution.py
@@ -9,7 +9,7 @@
 from jax.sharding import PartitionSpec as P
 
 CHUNKS = 2
-PART = 512
+PART = 1024
 ONES = 16
 VMEM_BYTES = 24 * 1024 * 1024
 LONG = pl.CostEstimate(flops=10**11, bytes_accessed=1, transcendentals=0)
@@ -159,10 +159,25 @@
     )(*views)
 
 
-def pool_kernel(ctx_count, heads, place_ref, pool_ref, *refs):
-    flat, outs = refs[-1], refs[:-1]
-    length, slots, width = pool_ref.shape[1:]
-    flat[...] = pool_ref[0].astype(jnp.float32).reshape(length * slots, width)
+def prepare_kernel(ctx_count, heads, cuts, place_ref, tokens_ref, pool_ref, *refs):
+    pieces, outs = refs[: len(cuts)], refs[len(cuts) : len(cuts) + ctx_count]
+    flat, sems = refs[-2:]
+    depth = pieces[0].shape[1]
+
+    def copies():
+        for index, (bits, first) in enumerate(cuts):
+            start = pl.multiple_of((place_ref[0] ^ bits) * depth, depth)
+            source = tokens_ref.at[pl.ds(first, pieces[index].shape[0]), pl.ds(start, depth)]
+            yield pltpu.make_async_copy(source, pieces[index], sems.at[index])
+
+    @pl.when(pl.program_id(0) == 0)
+    def _():
+        for copy in copies():
+            copy.start()
+
+    blocks, length, slots, width = pool_ref.shape
+    length *= blocks
+    flat[...] = pool_ref[...].astype(jnp.float32).reshape(length * slots, width)
     for kind in range(2):
         for head in range(heads):
             at = (kind * heads + head) * width
@@ -175,35 +190,61 @@
                 value = held[0]
                 for ctx in range(1, ctx_count):
                     value = jnp.where(target == ctx, held[ctx], value)
-                out_ref[0, :, at : at + width] = value.astype(out_ref.dtype)
-
-
-def arrange_pool(place, prefix_pool, ctx_count, heads):
+                out_ref[:, :, at : at + width] = value.astype(out_ref.dtype).reshape(
+                    blocks, length // blocks, width
+                )
+
+    @pl.when(pl.program_id(0) == pl.num_programs(0) - 1)
+    def _():
+        for copy in copies():
+            copy.wait()
+
+
+def prepare(place, tokens, depth, cuts, prefix_pool, ctx_count, heads):
     blocks, length, all_heads, _, double = prefix_pool.shape
     width = double // 2
     slots = 2 * all_heads
     view = prefix_pool.reshape(blocks, length, all_heads, 2, width)
     view = view.transpose(0, 1, 3, 2, 4).reshape(blocks, length, slots, width)
     columns = 2 * heads * width
-    out = pl.BlockSpec((1, length, columns), lambda i, place: (i, 0, 0))
-    return pl.pallas_call(
-        functools.partial(pool_kernel, ctx_count, heads),
+    some = 2 if blocks % 2 == 0 else 1
+    out = pl.BlockSpec((some, length, columns), lambda i, place: (i, 0, 0))
+    far = pl.BlockSpec(memory_space=pltpu.HBM)
+    result = pl.pallas_call(
+        functools.partial(
+            prepare_kernel, ctx_count, heads, [(bits, first) for bits, first, _ in cuts]
+        ),
         grid_spec=pltpu.PrefetchScalarGridSpec(
             num_scalar_prefetch=1,
-            grid=(blocks,),
-            in_specs=[pl.BlockSpec((1, length, slots, width), lambda i, place: (i, 0, 0, 0))],
-            out_specs=[out] * ctx_count,
-            scratch_shapes=[pltpu.VMEM((length * slots, width), jnp.float32)],
+            grid=(blocks // some,),
+            in_specs=[
+                far,
+                pl.BlockSpec((some, length, slots, width), lambda i, place: (i, 0, 0, 0)),
+            ],
+            out_specs=[far] * len(cuts) + [out] * ctx_count,
+            scratch_shapes=[
+                pltpu.VMEM((some * length * slots, width), jnp.float32),
+                pltpu.SemaphoreType.DMA((len(cuts),)),
+            ],
         ),
-        out_shape=[jax.ShapeDtypeStruct((blocks, length, columns), jnp.bfloat16)] * ctx_count,
+        out_shape=[jax.ShapeDtypeStruct((rows, depth), tokens.dtype) for _, _, rows in cuts]
+        + [jax.ShapeDtypeStruct((blocks, length, columns), jnp.bfloat16)] * ctx_count,
         compiler_params=params(),
-        cost_estimate=cost("arrange_pool"),
-        name="arrange_pool",
-    )(place, view)
-
-
-def project_kernel(place_ref, *refs):
-    token_refs, (weight_ref, out_ref, stacked) = refs[:-3], refs[-3:]
+        cost_estimate=cost("prepare"),
+        name="prepare",
+    )(place, tokens, view)
+    return result[: len(cuts)], result[len(cuts) :]
+
+
+def total_of(refs):
+    return sum(ref[...].astype(jnp.float32).reshape(ref.shape[-2:]) for ref in refs)
+
+
+def project_kernel(block_count, term_counts, place_ref, *refs):
+    token_refs, weight_ref = refs[:block_count], refs[block_count]
+    terms = refs[block_count + 1 : block_count + 1 + sum(term_counts)]
+    out_ref, *sum_refs = refs[block_count + 1 + sum(term_counts) : -1]
+    stacked = refs[-1]
 
     @pl.when(pl.program_id(0) == 0)
     def _():
@@ -212,13 +253,23 @@
             rows = token_ref.shape[0]
             stacked[at : at + rows, :] = token_ref[...]
             at += rows
+        at = 0
+        for count, sum_ref in zip(term_counts, sum_refs):
+            sum_ref[...] = total_of(terms[at : at + count]).astype(sum_ref.dtype)
+            at += count
 
     out_ref[0] = jnp.dot(
         stacked[...], weight_ref[0, 0], preferred_element_type=jnp.float32
     ).astype(out_ref.dtype)
 
 
-def project(place, blocks, weights, head_step, out_dtype, name):
+def piece_of(array, *index):
+    rows, block, *leading = index
+    shape = (1,) * len(leading) + (rows, array.shape[-1])
+    return array, pl.BlockSpec(shape, lambda j, *_: (*leading, block, 0))
+
+
+def project(place, blocks, weights, head_step, out_dtype, name, sums=()):
     head_count, ctx_count, depth, width = weights.shape
     row_total = sum(block.shape[0] for block in blocks)
 
@@ -227,8 +278,10 @@
             return pl.BlockSpec(block.shape, lambda j, place: (0, 0))
         return pl.BlockSpec((block.shape[0], depth), lambda j, place: (0, place[0]))
 
-    return pl.pallas_call(
-        project_kernel,
+    pieces = [piece for terms in sums for piece in terms]
+    sum_shapes = [terms[0][1].block_shape[-2:] for terms in sums]
+    result = pl.pallas_call(
+        functools.partial(project_kernel, len(blocks), [len(terms) for terms in sums]),
         grid_spec=pltpu.PrefetchScalarGridSpec(
             num_scalar_prefetch=1,
             grid=(ctx_count,),
@@ -243,15 +296,19 @@
                         0,
                     ),
                 )
-            ],
-            out_specs=pl.BlockSpec((1, row_total, width), lambda j, place: (j, 0, 0)),
+            ]
+            + [spec for _, spec in pieces],
+            out_specs=[pl.BlockSpec((1, row_total, width), lambda j, place: (j, 0, 0))]
+            + [pl.BlockSpec(shape, lambda j, place: (0, 0)) for shape in sum_shapes],
             scratch_shapes=[pltpu.VMEM((row_total, depth), weights.dtype)],
         ),
-        out_shape=jax.ShapeDtypeStruct((ctx_count, row_total, width), out_dtype),
+        out_shape=[jax.ShapeDtypeStruct((ctx_count, row_total, width), out_dtype)]
+        + [jax.ShapeDtypeStruct(shape, jnp.bfloat16) for shape in sum_shapes],
         compiler_params=params(),
         cost_estimate=cost(name),
         name=name,
-    )(place, *blocks, weights)
+    )(place, *blocks, weights, *(array for array, _ in pieces))
+    return result if sums else result[0]
 
 
 def pick_kernel(heads, ctx_count, place_ref, table_ref, *refs):
@@ -363,9 +420,11 @@
 
 
 def fresh_kernel(
-    scale, heads, per_token, first_row, parts, length_ref, query_ref, acc_ref, stat_ref, *rest
+    scale, heads, per_token, first_row, counts, length_ref, query_ref, acc_ref, stat_ref, *rest
 ):
-    out_ref, keys, values, flat, mixed_rows = rest[-5:]
+    early_count, term_count = counts
+    earlier, terms = rest[:early_count], rest[early_count : early_count + term_count]
+    out_ref, fresh_ref, keys, values, flat, mixed_rows = rest[-6:]
     rows, width = query_ref.shape
     wide, tall = heads * width, width + ONES
     step = pl.program_id(0)
@@ -373,10 +432,10 @@
     @pl.when(step == 0)
     def _():
         values[...] = jnp.ones_like(values)
-        for index in range(parts):
-            one, other = rest[2 * index], rest[2 * index + 1]
-            here = slice(index * one.shape[0], (index + 1) * one.shape[0])
-            fresh = (one[...].astype(jnp.float32) + other[...]).astype(jnp.bfloat16)
+        fresh_ref[...] = total_of(terms).astype(fresh_ref.dtype)
+        for index, ref in enumerate([*earlier, fresh_ref]):
+            here = slice(index * ref.shape[0], (index + 1) * ref.shape[0])
+            fresh = ref[...]
             keys[here, :] = fresh[:, :wide]
             put_values(values, here, fresh[:, wide:], heads)
 
@@ -404,34 +463,44 @@
     out_ref[...] = mixed_rows[...].astype(out_ref.dtype)
 
 
-def fresh_attend(length, query_rows, acc, stat, parts, earlier, chunk, scale, heads, per_token):
+def fresh_attend(
+    length, query_rows, acc, stat, earlier, pieces, result, chunk, scale, heads, per_token
+):
     row_total, width = query_rows.shape
     chunk_rows = row_total // CHUNKS
     rows = min(1024, chunk_rows)
     steps = chunk_rows // rows
     block = pl.BlockSpec((rows, width), lambda i, length: (chunk * steps + i, 0))
-    terms = [term for pair in parts for term in pair]
-    key_count = sum(pair[0].shape[0] for pair in parts)
+    fresh_shape = pieces[0][1].block_shape[-2:]
+    key_count = (len(earlier) + 1) * fresh_shape[0]
+    whole = pl.BlockSpec(fresh_shape, lambda i, length: (0, 0))
     in_specs = [
         block,
         pl.BlockSpec((width, rows), lambda i, length: (0, i)),
         pl.BlockSpec((stat.shape[0], rows), lambda i, length: (0, i)),
-    ] + [pl.BlockSpec(term.shape, lambda i, length: (0, 0)) for term in terms]
-    operands = [length, query_rows, acc, stat, *terms]
+        *(whole for _ in earlier),
+        *(spec for _, spec in pieces),
+    ]
+    operands = [length, query_rows, acc, stat, *earlier, *(array for array, _ in pieces)]
     aliases = {}
-    if earlier is not None:
+    if result is not None:
         in_specs.append(pl.BlockSpec(memory_space=pl.ANY))
         aliases = {len(operands): 0}
-        operands.append(earlier)
+        operands.append(result)
     return pl.pallas_call(
         functools.partial(
-            fresh_kernel, scale, heads, per_token, chunk * (chunk_rows // per_token), len(parts)
+            fresh_kernel,
+            scale,
+            heads,
+            per_token,
+            chunk * (chunk_rows // per_token),
+            (len(earlier), len(pieces)),
         ),
         grid_spec=pltpu.PrefetchScalarGridSpec(
             num_scalar_prefetch=1,
             grid=(steps,),
             in_specs=in_specs,
-            out_specs=block,
+            out_specs=[block, whole],
             scratch_shapes=[
                 pltpu.VMEM((key_count, heads * width), jnp.bfloat16),
                 pltpu.VMEM((heads * (width + ONES), key_count), jnp.bfloat16),
@@ -439,47 +508,15 @@
                 pltpu.VMEM((rows, width), jnp.float32),
             ],
         ),
-        out_shape=jax.ShapeDtypeStruct((row_total, width), jnp.bfloat16),
+        out_shape=[
+            jax.ShapeDtypeStruct((row_total, width), jnp.bfloat16),
+            jax.ShapeDtypeStruct(fresh_shape, jnp.bfloat16),
+        ],
         input_output_aliases=aliases,
         compiler_params=params(),
         cost_estimate=cost("fresh_attend"),
         name="fresh_attend",
     )(*operands)
-
-
-def cut_kernel(depth, bits, place_ref, tokens_ref, *refs):
-    pieces, sems = refs[:-1], refs[-1]
-    copies = []
-    for index, piece in enumerate(pieces):
-        start = pl.multiple_of((place_ref[0] ^ bits[index]) * depth, depth)
-        copies.append(
-            pltpu.make_async_copy(
-                tokens_ref.at[:, pl.ds(start, depth)], piece, sems.at[index]
-            )
-        )
-    for copy in copies:
-        copy.start()
-    for copy in copies:
-        copy.wait()
-
-
-def cut_tokens(place, tokens, depth, bits):
-    anywhere = pl.BlockSpec(memory_space=pl.ANY)
-    piece = jax.ShapeDtypeStruct((tokens.shape[0], depth), tokens.dtype)
-    return pl.pallas_call(
-        functools.partial(cut_kernel, depth, bits),
-        grid_spec=pltpu.PrefetchScalarGridSpec(
-            num_scalar_prefetch=1,
-            grid=(1,),
-            in_specs=[anywhere],
-            out_specs=[anywhere] * len(bits),
-            scratch_shapes=[pltpu.SemaphoreType.DMA((len(bits),))],
-        ),
-        out_shape=[piece] * len(bits),
-        compiler_params=params(),
-        cost_estimate=cost("cut_tokens"),
-        name="cut_tokens",
-    )(place, tokens)
 
 
 def reduced_shards(tokens, key_weight, value_weight, queries, prefix_pool, block_table, lengths):
@@ -499,11 +536,10 @@
 
     top = batch_count // 2
     steps = list(range(batch_count - 1, top, -1)) + list(range(1, top))
-    pieces = cut_tokens(place, tokens, depth, [*steps, top])
-    pieces, prefix_pool = after(pieces, prefix_pool)
-    arrived = [trade(piece, "batch", bits) for piece, bits in zip(pieces, steps)]
-
-    pools = arrange_pool(place, prefix_pool, ctx_count, heads)
+    cuts = [(bits, i * rows, rows) for bits in steps for i in range(CHUNKS)]
+    cuts.append((top, 0, token_count))
+    pieces, pools = prepare(place, tokens, depth, cuts, prefix_pool, ctx_count, heads)
+    arrived = [trade(piece, "batch", bits) for piece, (bits, _, _) in zip(pieces, cuts[:-1])]
     pools, (key_weight, value_weight) = after(pools, (key_weight, value_weight))
     pools = [shift(part, "ctx", step) if step else part for step, part in enumerate(pools)]
 
@@ -527,68 +563,77 @@
     def spread(parts):
         return [shift(part, "ctx", step + 1) for step, part in enumerate(parts)]
 
-    def summed(terms, here, parts):
-        return added(terms, 0, here) + sum(part.astype(jnp.float32) for part in parts)
-
     every = slice(None)
     parts_of = [slice(i * rows, (i + 1) * rows) for i in range(CHUNKS)]
 
-    own = projected([tokens], "own")
-    own[0], last = after(own[0], pieces[-1])
-    last = trade(last, "batch", top)
-    own_others = others(own, every)
-    own_others = spread(own_others)
-
+    last = trade(pieces[-1], "batch", top)
+
+    sums = [[], []]
     if steps:
         early = projected(arrived, "early")
         cuts = [slice(i * token_count, (i + 1) * token_count) for i in range(len(steps))]
-        far_others = spread(others(early, cuts[0]))
-        near_others, pools = after(others(early, cuts[1]), pools)
-        near_others = spread(near_others)
+        leaving = [others(early, cut) for cut in cuts]
+        leaving, pools = after(leaving, pools)
+        sums = [
+            [
+                [piece_of(t, token_count, i, 0) for t in early]
+                + [piece_of(p, token_count, 0) for p in spread(parts)]
+            ]
+            for i, parts in enumerate(leaving)
+        ]
     keys, values = pick_blocks(place, block_table[0], pools, heads)
     states = [prefix_attend(query_rows, keys, values, 0, scale, heads)]
     states[0], last = after(states[0], last)
-    if steps:
-        far = summed(early, cuts[0], far_others).astype(jnp.bfloat16)
-        far, last = after(far, last)
-        far = trade(far, "batch", 1)
-
-    late = projected([last], "late")
-    late_others = [others(late, here) for here in parts_of]
-    waiting = (keys, values, near_others) if steps else (keys, values)
-    late_others[-1], waiting = after(late_others[-1], waiting)
-    keys, values, *near_others = waiting
-    late_others = [spread(part) for part in late_others]
+
+    def late_project(step, dtype, name, sums):
+        result = project(place, [last, tokens], weights, step, dtype, name, sums)
+        return result if sums else (result,)
+
+    terms = []
+    for step in range(1, head_count):
+        term, *far = late_project(step, jnp.bfloat16, "late_away", sums[0] + sums[1] if step == 1 else [])
+        terms.append(shift(term, "head", step))
+    kept, *_ = late_project(0, jnp.float32, "late_kept", [])
+    far, near = far[:1], far[1:]
+    late = [kept, *terms]
+    far, near = ([trade(part, "batch", 1) for part in parts] for parts in (far, near))
+    own_at = slice(token_count, 2 * token_count)
+    late_others = [others(late, here) for here in [*parts_of, own_at]]
+    late_others[-1], (keys, values) = after(late_others[-1], (keys, values))
+    *late_others, own_others = [spread(part) for part in late_others]
     states.append(prefix_attend(query_rows, keys, values, 1, scale, heads))
     states[1], late_others[0] = after(states[1], late_others[0])
 
-    home = summed(own, every, own_others)
-    if steps:
-        near_others = near_others[0]
-        near = trade(summed(early, cuts[1], near_others).astype(jnp.bfloat16), "batch", 1)
-        home = home + near.astype(jnp.float32)
-    parts = []
+    away = []
     for chunk, here in enumerate(parts_of):
-        part = summed(late, here, late_others[chunk])
-        if steps:
-            part = part + far[here].astype(jnp.float32)
-            if chunk + 1 < CHUNKS:
-                (far, late), late_others[chunk + 1] = after((far, late), late_others[chunk + 1])
-        parts.append((trade(part.astype(jnp.bfloat16), "batch", top), home[here]))
+        part = added(late, 0, here) + sum(p.astype(jnp.float32) for p in late_others[chunk])
+        part = part + sum(p[here].astype(jnp.float32) for p in far)
+        if chunk + 1 < CHUNKS:
+            (far, late), late_others[chunk + 1] = after((far, late), late_others[chunk + 1])
+        part = part.astype(jnp.bfloat16)
+        if away:
+            away[-1], part = after(away[-1], part)
+        away.append(trade(part, "batch", top))
 
     result = None
+    fresh = []
     for chunk in range(CHUNKS):
-        result = fresh_attend(
+        pieces = [piece_of(t, rows, CHUNKS + chunk, 0) for t in late]
+        pieces += [piece_of(part, rows, chunk) for part in (*own_others, *near)]
+        pieces.append(piece_of(away[chunk], rows, 0))
+        result, new = fresh_attend(
             lengths,
             query_rows,
             *states[chunk],
-            parts[: chunk + 1],
+            fresh,
+            pieces,
             result,
             chunk,
             scale,
             heads,
             per_token,
         )
+        fresh.append(new)
     result = result.reshape(token_count, group, heads, width).transpose(0, 2, 1, 3)
     return result.reshape(token_count, heads, 1, group * width)
 

time: 107 us -> 99.9 us (0.934)
  Pallas kernels: 58.4 us -> 44.7 us
  starting transfers between devices: 18.4 us -> 32 us
  other arithmetic: 6.5 us -> 1.58 us
  waiting for transfers between devices: 20.6 us -> 17.3 us
  local copies, waits for them, and re-layouts: 1.72 us -> 3.23 us
    ppermute x7 -> x9, starting transfers between devices: 11.2 us -> 24.5 us  [trade(): lax.ppermute(array, axis, [(i, i ^ bits) for i in range(lax.axis_size(axi...]
    pallas_call x8 -> x5, Pallas kernels: 20.3 us -> 13.8 us  [the longest x4 10.7 us: project(): pl.pallas_call(functools.partial(project_kernel, len(blocks), [len(terms)...]
    pallas_call x2, Pallas kernels: 21.5 us -> 15.6 us  [prefix_attend(): pl.pallas_call(functools.partial(prefix_kernel, scale, heads), grid=(step...]
    ppermute x7 -> x9, waiting for transfers between devices: 20.6 us -> 16.7 us  [trade(): lax.ppermute(array, axis, [(i, i ^ bits) for i in range(lax.axis_size(axi...]
    convert_element_type x4 -> x2, other arithmetic: 3.43 us -> 0.13 us  [reduced_shards(): part = part.astype(jnp.bfloat16)]
    unnamed x36 -> x24, local copies, waits for them, and re-layouts: 1.68 us -> 3.23 us
    pallas_call x2, Pallas kernels: 11.3 us -> 9.98 us  [fresh_attend(): pl.pallas_call(functools.partial(fresh_kernel, scale, heads, per_token, c...]
    add x1 -> x0, other arithmetic: 1.08 us -> none  [reduced_shards(): home = home + near.astype(jnp.float32)]
  transfers between devices with their start and end apart: 16 -> 17, of which waited for: 3 -> 6; matrix products, arithmetic and copies ran while one was open for 6% -> 2% of each run, Pallas kernels for 47% -> 33%
where the time goes in v9:
time: 99.9 us; the launch traced here: 99.6 us
  Pallas kernels  44.7 us (45%)
  starting transfers between devices  32 us (32%)
  waiting for transfers between devices  17.3 us (17%)
  local copies, waits for them, and re-layouts  3.23 us (3%)
  other arithmetic  1.58 us (2%)
    ppermute x9, starting transfers between devices, trade(): lax.ppermute(array, axis, [(i, i ^ bits) for i in range(lax.axis_size(axi...  24.5 us
    ppermute x9, waiting for transfers between devices, trade(): lax.ppermute(array, axis, [(i, i ^ bits) for i in range(lax.axis_size(axi...  16.7 us
    pallas_call x2, Pallas kernels, prefix_attend(): pl.pallas_call(functools.partial(prefix_kernel, scale, heads), grid=(step...  15.6 us
    pallas_call x4, Pallas kernels, project(): pl.pallas_call(functools.partial(project_kernel, len(blocks), [len(terms)...  10.7 us
    pallas_call x2, Pallas kernels, fresh_attend(): pl.pallas_call(functools.partial(fresh_kernel, scale, heads, per_token, c...  9.98 us
    ppermute x8, starting transfers between devices, shift(): lax.ppermute(array, axis, [(i, (i + step) % count) for i in range(count)])  7.5 us
    unnamed x24, local copies, waits for them, and re-layouts  3.23 us
    pallas_call x1, Pallas kernels, prepare(): pl.pallas_call(functools.partial(prepare_kernel, ctx_count, heads, [(bits...  3.14 us
  transfers between devices with their start and end apart: 17, of which 6 were waited for; matrix products, arithmetic and copies ran while one was open for 2% of the time, Pallas kernels for 33%

profile of v9, /device:TPU:0, one launch (start us, length us, event | category | flops | bytes accessed | tf_op | source)
XLA Modules:
  0.0 99.6 jit_solution(12337253431467376363)
XLA Ops:
  0.0 0.1 pad_add_fusion.place_ref
  0.1 1.6 %copy-done.4 = bf16[8,128,4,1,256]{4,2,3,1,0:T(4,128)(2,1)S(1)} copy-done((bf16[8,128,4,1,256]{4,2,3,1,0:T(4,128)(2,1)S(1)}, bf16[8,128,4,1,256]{4,2,3,1,0:T(4,128)(2,1)}, u32[]{:S(2)}) %copy-start.4) | copy-done | bytes 2097176
  1.7 1.6 %copy-done.7 = bf16[256,4096]{1,0:T(8,128)(2,1)S(1)} copy-done((bf16[256,4096]{1,0:T(8,128)(2,1)S(1)}, bf16[256,4096]{1,0:T(8,128)(2,1)}, u32[]{:S(2)}) %copy-start.7) | copy-done | bytes 2097176
  3.3 3.1 %prepare.1 = (bf16[128,1024]{1,0:T(8,128)(2,1)S(1)}, bf16[128,1024]{1,0:T(8,128)(2,1)S(1)}, bf16[128,1024]{1,0:T(8,128)(2,1)S(1)}, bf16[128,1024]{1,0:T(8,128)(2...) custom-call(s32[3]{0:T(128)S(1)} %pad_add_fusion.place_ref, ...), custom_call_target="tpu_custom_call" | custom-call | flops 99999997952 | bytes 1 | tf_op jit(solution)/shard_map/prepare/pallas_call | solution.py:213
  6.4 5.1 %collective-permute-start = (bf16[128,1024]{1,0:T(8,128)(2,1)S(1)}, bf16[128,1024]{1,0:T(8,128)(2,1)S(1)}, u32[]{:S(2)}, u32[]{:S(2)}) collective-permute-start(bf16[128,1024]{1,0:T(8,128)(2,1)S(1)} %get-tuple-element.47), channel_id=1, source_target_pairs={{0,12},{4,8},{8,4},{12,0},{1,13},{5,9},{9,5},{13,1},{2,14},{6,10},... | collective-permute-start | bytes 786440 | tf_op jit(solution)/shard_map/ppermute | solution.py:104
  11.5 0.1 collective-permute-start.1
  11.6 2.0 %collective-permute-start.3 = (bf16[128,1024]{1,0:T(8,128)(2,1)S(1)}, bf16[128,1024]{1,0:T(8,128)(2,1)S(1)}, u32[]{:S(2)}, u32[]{:S(2)}) collective-permute-start(bf16[128,1024]{1,0:T(8,128)(2,1)S(1)} %get-tuple-element.50), channel_id=1, source_target_pairs={{0,4},{4,0},{8,12},{12,8},{1,5},{5,1},{9,13},{13,9},{2,6},{6,2},{1... | collective-permute-start | bytes 786440 | tf_op jit(solution)/shard_map/ppermute | solution.py:104
  13.6 1.6 %collective-permute-start.5 = (bf16[8,128,512]{2,1,0:T(8,128)(2,1)}, bf16[8,128,512]{2,1,0:T(8,128)(2,1)}, u32[]{:S(2)}, u32[]{:S(2)}) collective-permute-start(bf16[8,128,512]{2,1,0:T(8,128)(2,1)} %get-tuple-element.56), channel_id=1, source_target_pairs={{0,2},{2,0},{1,3},{3,1},{4,6},{6,4},{5,7},{7,5},{8,10},{10,8},{9,1... | collective-permute-start | bytes 3145736 | tf_op jit(solution)/shard_map/ppermute | solution.py:100
  15.3 2.5 %arrange_weights.1.refs_4_.refs_2_ = bf16[2,2,1024,512]{3,2,1,0:T(8,128)(2,1)S(1)} custom-call(bf16[1024,8,128]{2,1,0:T(8,128)(2,1)S(1)} %bitcast.46, bf16[1024,8,128]{2,1,0:T(8,128)(2,1)S(1)} %bitcast.47), custom_call_target="tpu_custom_call" | custom-call | flops 99999997952 | bytes 1 | tf_op jit(solution)/shard_map/arrange_weights/pallas_call | solution.py:149
  18.4 0.5 collective-permute-done.refs_0_
  18.9 12.1 %collective-permute-start.6 = (bf16[256,1024]{1,0:T(8,128)(2,1)}, bf16[256,1024]{1,0:T(8,128)(2,1)}, u32[]{:S(2)}, u32[]{:S(2)}) collective-permute-start(bf16[256,1024]{1,0:T(8,128)(2,1)} %get-tuple-element.63), channel_id=1, source_target_pairs={{0,8},{4,12},{8,0},{12,4},{1,9},{5,13},{9,1},{13,5},{2,10},{6,14},... | collective-permute-start | bytes 1572872 | tf_op jit(solution)/shard_map/ppermute | solution.py:104
  30.9 4.9 %collective-permute-done.3.refs_3_ = bf16[128,1024]{1,0:T(8,128)(2,1)S(1)} collective-permute-done((bf16[128,1024]{1,0:T(8,128)(2,1)S(1)}, bf16[128,1024]{1,0:T(8,128)(2,1)S(1)}, u32[]{:S(2)}, u32[]{:S(2)}) %collective-permute-start.3) | collective-permute-done | bytes 262176 | tf_op jit(solution)/shard_map/ppermute | solution.py:104
  35.8 2.1 %early_away.1 = bf16[2,512,512]{2,1,0:T(8,128)(2,1)S(1)} custom-call(s32[3]{0:T(128)S(1)} %pad_add_fusion.place_ref, bf16[128,1024]{1,0:T(8,128)(2,1)S(1)} %collective-permute-done.refs_0_, bf16[128,1024]{1,0:T(8,128)(2,1)S(1)} %collective-permute-done.1.refs_1_, bf16[128,1024]{1,0:T(8,128)(2,1)S(1)} %collective-permute-done.2.refs_2_, ...), custom_call_target="tpu_custom_call" | custom-call | flops 99999997952 | bytes 1 | tf_op jit(solution)/shard_map/early_away/pallas_call | solution.py:283
  37.9 0.1 collective-permute-start.4
  38.0 2.1 %early_kept.1.refs_3_.refs_6_ = f32[2,512,512]{2,1,0:T(8,128)S(1)} custom-call(s32[3]{0:T(128)S(1)} %pad_add_fusion.place_ref, bf16[128,1024]{1,0:T(8,128)(2,1)S(1)} %collective-permute-done.refs_0_, bf16[128,1024]{1,0:T(8,128)(2,1)S(1)} %collective-permute-done.1.refs_1_, bf16[128,1024]{1,0:T(8,128)(2,1)S(1)} %collective-permute-done.2.refs_2_, ...), custom_call_target="tpu_custom_call" | custom-call | flops 99999997952 | bytes 1 | tf_op jit(solution)/shard_map/early_kept/pallas_call | solution.py:283
  40.1 0.0 copy-start
  40.1 0.0 copy-start.11
  40.1 0.5 collective-permute-done.4.refs_4_.refs_7_
  40.6 1.2 %fusion.4 = (bf16[256,512]{1,0:T(8,128)(2,1)}, bf16[256,512]{1,0:T(8,128)(2,1)}) fusion(f32[2,512,512]{2,1,0:T(8,128)S(1)} %early_kept.1.refs_3_.refs_6_, bf16[2,512,512]{2,1,0:T(8,128)(2,1)S(1)} %collective-permute-done.4.refs_4_.refs_7_), kind=kLoop, calls=%fused_computation.7 | loop fusion | flops 786432 | bytes 2097152 | tf_op jit(solution)/shard_map/convert_element_type | solution.py:561
  41.9 0.0 collective-permute-done.5.refs_1_
  41.9 1.4 %collective-permute-start.7 = (bf16[256,512]{1,0:T(8,128)(2,1)}, bf16[256,512]{1,0:T(8,128)(2,1)}, u32[]{:S(2)}, u32[]{:S(2)}) collective-permute-start(bf16[256,512]{1,0:T(8,128)(2,1)} %get-tuple-element.65), channel_id=1, source_target_pairs={{0,2},{2,0},{1,3},{3,1},{4,6},{6,4},{5,7},{7,5},{8,10},{10,8},{9,1... | collective-permute-start | bytes 786440 | tf_op jit(solution)/shard_map/ppermute | solution.py:100
  43.3 0.6 collective-permute-start.8
  43.9 2.8 %pick_blocks.1 = (bf16[1024,256]{1,0:T(8,128)(2,1)S(1)}, bf16[288,1024]{1,0:T(8,128)(2,1)S(1)}) custom-call(s32[3]{0:T(128)S(1)} %pad_add_fusion.place_ref, s32[8]{0:T(128)S(1)} %bitcast.52, bf16[8,128,512]{2,1,0:T(8,128)(2,1)S(1)} %get-tuple-element.57.refs_0_, bf16[8,128,512]{2,1,0:T(8,128)(2,1)} %collective-permute-done.5.refs_1_), custom_call_target="tpu_custom_call" | custom-call | flops 99999997952 | bytes 1 | tf_op jit(solution)/shard_map/pick_blocks/pallas_call | solution.py:347
  46.8 0.0 copy-start.1
  46.8 0.0 copy-start.8
  46.8 7.8 %prefix_attend.2 = (f32[128,4096]{1,0:T(8,128)S(1)}, f32[8,4096]{1,0:T(8,128)S(1)}) custom-call(bf16[8192,128]{1,0:T(8,128)(2,1)S(1)} %bitcast.48, bf16[1024,256]{1,0:T(8,128)(2,1)S(1)} %get-tuple-element.68.keys, bf16[288,1024]{1,0:T(8,128)(2,1)S(1)} %get-tuple-element.69.values), custom_call_target="tpu_custom_call" | custom-call | flops 99999997952 | bytes 1 | tf_op jit(solution)/shard_map/prefix_attend/pallas_call | solution.py:399
  54.6 1.8 %collective-permute-done.6.refs_0_ = bf16[256,1024]{1,0:T(8,128)(2,1)} collective-permute-done((bf16[256,1024]{1,0:T(8,128)(2,1)}, bf16[256,1024]{1,0:T(8,128)(2,1)}, u32[]{:S(2)}, u32[]{:S(2)}) %collective-permute-start.6) | collective-permute-done | bytes 524320 | tf_op jit(solution)/shard_map/ppermute | solution.py:104
  56.4 3.4 %late_away.1 = (bf16[2,512,512]{2,1,0:T(8,128)(2,1)S(1)}, bf16[256,512]{1,0:T(8,128)(2,1)S(1)}, bf16[256,512]{1,0:T(8,128)(2,1)S(1)}) custom-call(s32[3]{0:T(128)S(1)} %pad_add_fusion.place_ref, bf16[256,1024]{1,0:T(8,128)(2,1)} %collective-permute-done.6.refs_0_, bf16[256,4096]{1,0:T(8,128)(2,1)S(1)} %copy-done.8, ...), custom_call_target="tpu_custom_call" | custom-call | flops 99999997952 | bytes 1 | tf_op jit(solution)/shard_map/late_away/pallas_call | solution.py:283
  59.9 0.1 collective-permute-start.9
  60.0 3.1 %late_kept.1.rest_0_.rest_1_ = f32[2,512,512]{2,1,0:T(8,128)S(1)} custom-call(s32[3]{0:T(128)S(1)} %pad_add_fusion.place_ref, bf16[256,1024]{1,0:T(8,128)(2,1)} %collective-permute-done.6.refs_0_, bf16[256,4096]{1,0:T(8,128)(2,1)S(1)} %copy-done.8, bf16[2,2,1024,512]{3,2,1,0:T(8,128)(2,1)S(1)} %arrange_weights.1.refs_4_.refs_2_), custom_call_target="tpu_custom_call" | custom-call | flops 99999997952 | bytes 1 | tf_op jit(solution)/shard_map/late_kept/pallas_call | solution.py:283
  63.1 0.0 copy-start.10
  63.1 1.6 %collective-permute-start.11 = (bf16[256,512]{1,0:T(8,128)(2,1)S(1)}, bf16[256,512]{1,0:T(8,128)(2,1)S(1)}, u32[]{:S(2)}, u32[]{:S(2)}) collective-permute-start(bf16[256,512]{1,0:T(8,128)(2,1)S(1)} %get-tuple-element.76), channel_id=1, source_target_pairs={{0,4},{4,0},{8,12},{12,8},{1,5},{5,1},{9,13},{13,9},{2,6},{6,2},{1... | collective-permute-start | bytes 786440 | tf_op jit(solution)/shard_map/ppermute | solution.py:104
  64.7 0.5 collective-permute-start.14
  65.2 0.0 collective-permute-done.9.rest_1_.rest_2_
  65.2 0.1 fusion.15
  65.3 1.6 %collective-permute-start.12 = (bf16[128,512]{1,0:T(8,128)(2,1)S(1)}, bf16[128,512]{1,0:T(8,128)(2,1)S(1)}, u32[]{:S(2)}, u32[]{:S(2)}) collective-permute-start(bf16[128,512]{1,0:T(8,128)(2,1)S(1)} %get-tuple-element.89), channel_id=1, source_target_pairs={{0,2},{2,0},{1,3},{3,1},{4,6},{6,4},{5,7},{7,5},{8,10},{10,8},{9,1... | collective-permute-start | bytes 393224 | tf_op jit(solution)/shard_map/ppermute | solution.py:100
  66.8 0.5 collective-permute-start.10
  67.4 0.1 fusion.5
  67.4 1.6 %collective-permute-start.13 = (bf16[256,512]{1,0:T(8,128)(2,1)S(1)}, bf16[256,512]{1,0:T(8,128)(2,1)S(1)}, u32[]{:S(2)}, u32[]{:S(2)}) collective-permute-start(bf16[256,512]{1,0:T(8,128)(2,1)S(1)} %fusion.5), channel_id=1, source_target_pairs={{0,2},{2,0},{1,3},{3,1},{4,6},{6,4},{5,7},{7,5},{8,10},{10,8},{9,1... | collective-permute-start | bytes 786440 | tf_op jit(solution)/shard_map/ppermute | solution.py:100
  69.0 7.8 %prefix_attend.3 = (f32[128,4096]{1,0:T(8,128)S(1)}, f32[8,4096]{1,0:T(8,128)S(1)}) custom-call(bf16[8192,128]{1,0:T(8,128)(2,1)S(1)} %bitcast.49, bf16[1024,256]{1,0:T(8,128)(2,1)S(1)} %get-tuple-element.68.keys, bf16[288,1024]{1,0:T(8,128)(2,1)S(1)} %get-tuple-element.69.values), custom_call_target="tpu_custom_call" | custom-call | flops 99999997952 | bytes 1 | tf_op jit(solution)/shard_map/prefix_attend/pallas_call | solution.py:399
  76.8 0.1 fusion.9
  76.9 3.0 %collective-permute-start.15 = (bf16[128,512]{1,0:T(8,128)(2,1)S(1)}, bf16[128,512]{1,0:T(8,128)(2,1)S(1)}, u32[]{:S(2)}, u32[]{:S(2)}) collective-permute-start(bf16[128,512]{1,0:T(8,128)(2,1)S(1)} %fusion.9), channel_id=1, source_target_pairs={{0,8},{4,12},{8,0},{12,4},{1,9},{5,13},{9,1},{13,5},{2,10},{6,14},... | collective-permute-start | bytes 393224 | tf_op jit(solution)/shard_map/ppermute | solution.py:104
  79.9 0.1 fusion.13
  80.0 5.8 %collective-permute-done.15.rest_4_ = bf16[128,512]{1,0:T(8,128)(2,1)S(1)} collective-permute-done((bf16[128,512]{1,0:T(8,128)(2,1)S(1)}, bf16[128,512]{1,0:T(8,128)(2,1)S(1)}, u32[]{:S(2)}, u32[]{:S(2)}) %collective-permute-start.15) | collective-permute-done | bytes 131104 | tf_op jit(solution)/shard_map/ppermute | solution.py:104
  85.8 0.0 collective-permute-start.16
  85.8 4.7 %fresh_attend.2 = (bf16[8192,128]{1,0:T(8,128)(2,1)}, bf16[128,512]{1,0:T(8,128)(2,1)S(1)}) custom-call(s32[1]{0:T(128)S(6)} %copy.13.length_ref, bf16[8192,128]{1,0:T(8,128)(2,1)S(1)} %bitcast.50, f32[128,4096]{1,0:T(8,128)S(1)} %get-tuple-element.74.acc_ref, f32[8,4096]{1,0:T(8,128)S(1)} %get-tuple-element.75.stat_ref, ...), custom_call_target="tpu_custom_call" | custom-call | flops 99999997952 | bytes 1 | tf_op jit(solution)/shard_map/fresh_attend/pallas_call | solution.py:490
  90.5 3.8 %collective-permute-done.16.rest_5_ = bf16[128,512]{1,0:T(8,128)(2,1)S(1)} collective-permute-done((bf16[128,512]{1,0:T(8,128)(2,1)S(1)}, bf16[128,512]{1,0:T(8,128)(2,1)S(1)}, u32[]{:S(2)}, u32[]{:S(2)}) %collective-permute-start.16) | collective-permute-done | bytes 131104 | tf_op jit(solution)/shard_map/ppermute | solution.py:104
  94.3 5.3 %fresh_attend.3 = (bf16[8192,128]{1,0:T(8,128)(2,1)}, bf16[128,512]{1,0:T(8,128)(2,1)}) custom-call(s32[1]{0:T(128)S(6)} %copy.13.length_ref, bf16[8192,128]{1,0:T(8,128)(2,1)S(1)} %bitcast.51, f32[128,4096]{1,0:T(8,128)S(1)} %get-tuple-element.72.acc_ref, f32[8,4096]{1,0:T(8,128)S(1)} %get-tuple-element.73.stat_ref, ...), custom_call_target="tpu_custom_call", output_to_operand_aliasing={{0}: (10, {})} | custom-call | flops 99999997952 | bytes 1 | tf_op jit(solution)/shard_map/fresh_attend/pallas_call | solution.py:490
  (27 shorter events, 0.1 us)
Async XLA Ops:
  0.1 1.6 %copy-start.4 = (bf16[8,128,4,1,256]{4,2,3,1,0:T(4,128)(2,1)S(1)}, bf16[8,128,4,1,256]{4,2,3,1,0:T(4,128)(2,1)}, u32[]{:S(2)}) copy-start(bf16[8,128,4,1,256]{4,2,3,1,0:T(4,128)(2,1)} %param.11) | copy-start | bytes 6291460
  1.7 1.6 %copy-start.7 = (bf16[256,4096]{1,0:T(8,128)(2,1)S(1)}, bf16[256,4096]{1,0:T(8,128)(2,1)}, u32[]{:S(2)}) copy-start(bf16[256,4096]{1,0:T(8,128)(2,1)} %refs_1_.3) | copy-start | bytes 6291460
  3.3 12.0 %copy-start.5 = (bf16[1,1,1024,4,2,128]{5,4,3,2,1,0:T(2,128)(2,1)S(1)}, bf16[1,1,1024,4,2,128]{5,4,3,2,1,0:T(2,128)(2,1)}, u32[]{:S(2)}) copy-start(bf16[1,1,1024,4,2,128]{5,4,3,2,1,0:T(2,128)(2,1)} %param.8) | copy-start | bytes 6291460
  3.3 12.0 %copy-start.6 = (bf16[1,1,1024,4,2,128]{5,4,3,2,1,0:T(2,128)(2,1)S(1)}, bf16[1,1,1024,4,2,128]{5,4,3,2,1,0:T(2,128)(2,1)}, u32[]{:S(2)}) copy-start(bf16[1,1,1024,4,2,128]{5,4,3,2,1,0:T(2,128)(2,1)} %param.9) | copy-start | bytes 6291460
  6.4 12.4 %collective-permute-start = (bf16[128,1024]{1,0:T(8,128)(2,1)S(1)}, bf16[128,1024]{1,0:T(8,128)(2,1)S(1)}, u32[]{:S(2)}, u32[]{:S(2)}) collective-permute-start(bf16[128,1024]{1,0:T(8,128)(2,1)S(1)} %get-tuple-element.47), channel_id=1, source_target_pairs={{0,12},{4,8},{8,4},{12,0},{1,13},{5,9},{9,5},{13,1},{2,14},{6,10},... | collective-permute-start | bytes 786440 | tf_op jit(solution)/shard_map/ppermute | solution.py:104
  11.5 19.4 %collective-permute-start.1 = (bf16[128,1024]{1,0:T(8,128)(2,1)S(1)}, bf16[128,1024]{1,0:T(8,128)(2,1)S(1)}, u32[]{:S(2)}, u32[]{:S(2)}) collective-permute-start(bf16[128,1024]{1,0:T(8,128)(2,1)S(1)} %get-tuple-element.48), channel_id=1, source_target_pairs={{0,12},{4,8},{8,4},{12,0},{1,13},{5,9},{9,5},{13,1},{2,14},{6,10},... | collective-permute-start | bytes 786440 | tf_op jit(solution)/shard_map/ppermute | solution.py:104
  11.6 19.3 %collective-permute-start.2 = (bf16[128,1024]{1,0:T(8,128)(2,1)S(1)}, bf16[128,1024]{1,0:T(8,128)(2,1)S(1)}, u32[]{:S(2)}, u32[]{:S(2)}) collective-permute-start(bf16[128,1024]{1,0:T(8,128)(2,1)S(1)} %get-tuple-element.49), channel_id=1, source_target_pairs={{0,4},{4,0},{8,12},{12,8},{1,5},{5,1},{9,13},{13,9},{2,6},{6,2},{1... | collective-permute-start | bytes 786440 | tf_op jit(solution)/shard_map/ppermute | solution.py:104
  11.6 24.2 %collective-permute-start.3 = (bf16[128,1024]{1,0:T(8,128)(2,1)S(1)}, bf16[128,1024]{1,0:T(8,128)(2,1)S(1)}, u32[]{:S(2)}, u32[]{:S(2)}) collective-permute-start(bf16[128,1024]{1,0:T(8,128)(2,1)S(1)} %get-tuple-element.50), channel_id=1, source_target_pairs={{0,4},{4,0},{8,12},{12,8},{1,5},{5,1},{9,13},{13,9},{2,6},{6,2},{1... | collective-permute-start | bytes 786440 | tf_op jit(solution)/shard_map/ppermute | solution.py:104
  13.6 28.2 %collective-permute-start.5 = (bf16[8,128,512]{2,1,0:T(8,128)(2,1)}, bf16[8,128,512]{2,1,0:T(8,128)(2,1)}, u32[]{:S(2)}, u32[]{:S(2)}) collective-permute-start(bf16[8,128,512]{2,1,0:T(8,128)(2,1)} %get-tuple-element.56), channel_id=1, source_target_pairs={{0,2},{2,0},{1,3},{3,1},{4,6},{6,4},{5,7},{7,5},{8,10},{10,8},{9,1... | collective-permute-start | bytes 3145736 | tf_op jit(solution)/shard_map/ppermute | solution.py:100
  18.9 37.6 %collective-permute-start.6 = (bf16[256,1024]{1,0:T(8,128)(2,1)}, bf16[256,1024]{1,0:T(8,128)(2,1)}, u32[]{:S(2)}, u32[]{:S(2)}) collective-permute-start(bf16[256,1024]{1,0:T(8,128)(2,1)} %get-tuple-element.63), channel_id=1, source_target_pairs={{0,8},{4,12},{8,0},{12,4},{1,9},{5,13},{9,1},{13,5},{2,10},{6,14},... | collective-permute-start | bytes 1572872 | tf_op jit(solution)/shard_map/ppermute | solution.py:104
  37.9 2.7 %collective-permute-start.4 = (bf16[2,512,512]{2,1,0:T(8,128)(2,1)S(1)}, bf16[2,512,512]{2,1,0:T(8,128)(2,1)S(1)}, u32[]{:S(2)}, u32[]{:S(2)}) collective-permute-start(bf16[2,512,512]{2,1,0:T(8,128)(2,1)S(1)} %early_away.1), channel_id=1, source_target_pairs={{0,1},{1,0},{2,3},{3,2},{4,5},{5,4},{6,7},{7,6},{8,9},{9,8},{10,11... | collective-permute-start | bytes 3145736 | tf_op jit(solution)/shard_map/ppermute | solution.py:100
  40.1 6.7 %copy-start = (f32[2,512,512]{2,1,0:T(8,128)}, f32[2,512,512]{2,1,0:T(8,128)S(1)}, u32[]{:S(2)}) copy-start(f32[2,512,512]{2,1,0:T(8,128)S(1)} %early_kept.1.refs_3_.refs_6_) | copy-start | bytes 6291460
  40.1 3.8 %copy-start.11 = (s32[1,8]{1,0:T(1,128)S(1)}, s32[1,8]{1,0:T(1,128)}, u32[]{:S(2)}) copy-start(s32[1,8]{1,0:T(1,128)} %param.12) | copy-start | bytes 100
  40.6 6.1 %copy-start.2 = (bf16[2,512,512]{2,1,0:T(8,128)(2,1)}, bf16[2,512,512]{2,1,0:T(8,128)(2,1)S(1)}, u32[]{:S(2)}) copy-start(bf16[2,512,512]{2,1,0:T(8,128)(2,1)S(1)} %collective-permute-done.4.refs_4_.refs_7_) | copy-start | bytes 3145732
  41.9 14.6 %collective-permute-start.7 = (bf16[256,512]{1,0:T(8,128)(2,1)}, bf16[256,512]{1,0:T(8,128)(2,1)}, u32[]{:S(2)}, u32[]{:S(2)}) collective-permute-start(bf16[256,512]{1,0:T(8,128)(2,1)} %get-tuple-element.65), channel_id=1, source_target_pairs={{0,2},{2,0},{1,3},{3,1},{4,6},{6,4},{5,7},{7,5},{8,10},{10,8},{9,1... | collective-permute-start | bytes 786440 | tf_op jit(solution)/shard_map/ppermute | solution.py:100
  43.3 13.1 %collective-permute-start.8 = (bf16[256,512]{1,0:T(8,128)(2,1)}, bf16[256,512]{1,0:T(8,128)(2,1)}, u32[]{:S(2)}, u32[]{:S(2)}) collective-permute-start(bf16[256,512]{1,0:T(8,128)(2,1)} %get-tuple-element.66), channel_id=1, source_target_pairs={{0,2},{2,0},{1,3},{3,1},{4,6},{6,4},{5,7},{7,5},{8,10},{10,8},{9,1... | collective-permute-start | bytes 786440 | tf_op jit(solution)/shard_map/ppermute | solution.py:100
  43.9 2.9 %copy-start.9 = (bf16[256,2,1,2048]{3,1,2,0:T(2,128)(2,1)S(1)}, bf16[256,2,1,2048]{3,1,2,0:T(2,128)(2,1)}, u32[]{:S(2)}) copy-start(bf16[256,2,1,2048]{3,1,2,0:T(2,128)(2,1)} %param.10) | copy-start | bytes 6291460
  46.8 9.7 %copy-start.1 = (f32[2,512,512]{2,1,0:T(8,128)S(1)}, f32[2,512,512]{2,1,0:T(8,128)}, u32[]{:S(2)}) copy-start(f32[2,512,512]{2,1,0:T(8,128)} %copy-done) | copy-start | bytes 6291460
  46.8 9.6 %copy-start.3 = (bf16[2,512,512]{2,1,0:T(8,128)(2,1)S(1)}, bf16[2,512,512]{2,1,0:T(8,128)(2,1)}, u32[]{:S(2)}) copy-start(bf16[2,512,512]{2,1,0:T(8,128)(2,1)} %copy-done.2) | copy-start | bytes 3145732
  46.8 9.6 %copy-start.8 = (bf16[256,4096]{1,0:T(8,128)(2,1)S(1)}, bf16[256,4096]{1,0:T(8,128)(2,1)}, u32[]{:S(2)}) copy-start(bf16[256,4096]{1,0:T(8,128)(2,1)} %refs_1_.3) | copy-start | bytes 6291460
  59.9 5.3 %collective-permute-start.9 = (bf16[2,512,512]{2,1,0:T(8,128)(2,1)S(1)}, bf16[2,512,512]{2,1,0:T(8,128)(2,1)S(1)}, u32[]{:S(2)}, u32[]{:S(2)}) collective-permute-start(bf16[2,512,512]{2,1,0:T(8,128)(2,1)S(1)} %get-tuple-element.67), channel_id=1, source_target_pairs={{0,1},{1,0},{2,3},{3,2},{4,5},{5,4},{6,7},{7,6},{8,9},{9,8},{10,11... | collective-permute-start | bytes 3145736 | tf_op jit(solution)/shard_map/ppermute | solution.py:100
  63.1 5.9 %copy-start.10 = (bf16[256,2,1,2048]{3,1,2,0:T(2,128)(2,1)S(1)}, bf16[256,2,1,2048]{3,1,2,0:T(2,128)(2,1)}, u32[]{:S(2)}) copy-start(bf16[256,2,1,2048]{3,1,2,0:T(2,128)(2,1)} %param.10) | copy-start | bytes 6291460
  63.1 13.7 %collective-permute-start.11 = (bf16[256,512]{1,0:T(8,128)(2,1)S(1)}, bf16[256,512]{1,0:T(8,128)(2,1)S(1)}, u32[]{:S(2)}, u32[]{:S(2)}) collective-permute-start(bf16[256,512]{1,0:T(8,128)(2,1)S(1)} %get-tuple-element.76), channel_id=1, source_target_pairs={{0,4},{4,0},{8,12},{12,8},{1,5},{5,1},{9,13},{13,9},{2,6},{6,2},{1... | collective-permute-start | bytes 786440 | tf_op jit(solution)/shard_map/ppermute | solution.py:104
  64.7 21.1 %collective-permute-start.14 = (bf16[256,512]{1,0:T(8,128)(2,1)S(1)}, bf16[256,512]{1,0:T(8,128)(2,1)S(1)}, u32[]{:S(2)}, u32[]{:S(2)}) collective-permute-start(bf16[256,512]{1,0:T(8,128)(2,1)S(1)} %get-tuple-element.80), channel_id=1, source_target_pairs={{0,4},{4,0},{8,12},{12,8},{1,5},{5,1},{9,13},{13,9},{2,6},{6,2},{1... | collective-permute-start | bytes 786440 | tf_op jit(solution)/shard_map/ppermute | solution.py:104
  65.3 11.6 %collective-permute-start.12 = (bf16[128,512]{1,0:T(8,128)(2,1)S(1)}, bf16[128,512]{1,0:T(8,128)(2,1)S(1)}, u32[]{:S(2)}, u32[]{:S(2)}) collective-permute-start(bf16[128,512]{1,0:T(8,128)(2,1)S(1)} %get-tuple-element.89), channel_id=1, source_target_pairs={{0,2},{2,0},{1,3},{3,1},{4,6},{6,4},{5,7},{7,5},{8,10},{10,8},{9,1... | collective-permute-start | bytes 393224 | tf_op jit(solution)/shard_map/ppermute | solution.py:100
  66.8 10.0 %collective-permute-start.10 = (bf16[128,512]{1,0:T(8,128)(2,1)S(1)}, bf16[128,512]{1,0:T(8,128)(2,1)S(1)}, u32[]{:S(2)}, u32[]{:S(2)}) collective-permute-start(bf16[128,512]{1,0:T(8,128)(2,1)S(1)} %get-tuple-element.90), channel_id=1, source_target_pairs={{0,2},{2,0},{1,3},{3,1},{4,6},{6,4},{5,7},{7,5},{8,10},{10,8},{9,1... | collective-permute-start | bytes 393224 | tf_op jit(solution)/shard_map/ppermute | solution.py:100
  67.4 18.4 %collective-permute-start.13 = (bf16[256,512]{1,0:T(8,128)(2,1)S(1)}, bf16[256,512]{1,0:T(8,128)(2,1)S(1)}, u32[]{:S(2)}, u32[]{:S(2)}) collective-permute-start(bf16[256,512]{1,0:T(8,128)(2,1)S(1)} %fusion.5), channel_id=1, source_target_pairs={{0,2},{2,0},{1,3},{3,1},{4,6},{6,4},{5,7},{7,5},{8,10},{10,8},{9,1... | collective-permute-start | bytes 786440 | tf_op jit(solution)/shard_map/ppermute | solution.py:100
  76.9 8.9 %collective-permute-start.15 = (bf16[128,512]{1,0:T(8,128)(2,1)S(1)}, bf16[128,512]{1,0:T(8,128)(2,1)S(1)}, u32[]{:S(2)}, u32[]{:S(2)}) collective-permute-start(bf16[128,512]{1,0:T(8,128)(2,1)S(1)} %fusion.9), channel_id=1, source_target_pairs={{0,8},{4,12},{8,0},{12,4},{1,9},{5,13},{9,1},{13,5},{2,10},{6,14},... | collective-permute-start | bytes 393224 | tf_op jit(solution)/shard_map/ppermute | solution.py:104
  85.8 8.5 %collective-permute-start.16 = (bf16[128,512]{1,0:T(8,128)(2,1)S(1)}, bf16[128,512]{1,0:T(8,128)(2,1)S(1)}, u32[]{:S(2)}, u32[]{:S(2)}) collective-permute-start(bf16[128,512]{1,0:T(8,128)(2,1)S(1)} %fusion.13), channel_id=1, source_target_pairs={{0,8},{4,12},{8,0},{12,4},{1,9},{5,13},{9,1},{13,5},{2,10},{6,14},... | collective-permute-start | bytes 393224 | tf_op jit(solution)/shard_map/ppermute | solution.py:104

commit v10 on v9

--- a/solution.py
+++ b/solution.py
@@ -161,8 +161,11 @@
 
 def prepare_kernel(ctx_count, heads, cuts, place_ref, tokens_ref, pool_ref, *refs):
     pieces, outs = refs[: len(cuts)], refs[len(cuts) : len(cuts) + ctx_count]
-    flat, sems = refs[-2:]
+    held_pool, flat, sems, pool_sems = refs[-4:]
     depth = pieces[0].shape[1]
+    step_at = pl.program_id(0)
+    some = outs[0].shape[0]
+    steps = pool_ref.shape[0] // some
 
     def copies():
         for index, (bits, first) in enumerate(cuts):
@@ -170,14 +173,22 @@
             source = tokens_ref.at[pl.ds(first, pieces[index].shape[0]), pl.ds(start, depth)]
             yield pltpu.make_async_copy(source, pieces[index], sems.at[index])
 
-    @pl.when(pl.program_id(0) == 0)
+    def pool_copy(index):
+        here = pl.ds(index * some, some)
+        return pltpu.make_async_copy(pool_ref.at[here], held_pool.at[here], pool_sems.at[index])
+
+    @pl.when(step_at == 0)
     def _():
         for copy in copies():
             copy.start()
-
-    blocks, length, slots, width = pool_ref.shape
-    length *= blocks
-    flat[...] = pool_ref[...].astype(jnp.float32).reshape(length * slots, width)
+        for index in range(steps):
+            pool_copy(index).start()
+
+    pool_copy(step_at).wait()
+    _, length, slots, width = pool_ref.shape
+    length *= some
+    block = held_pool[pl.ds(step_at * some, some)]
+    flat[...] = block.astype(jnp.float32).reshape(length * slots, width)
     for kind in range(2):
         for head in range(heads):
             at = (kind * heads + head) * width
@@ -191,10 +202,10 @@
                 for ctx in range(1, ctx_count):
                     value = jnp.where(target == ctx, held[ctx], value)
                 out_ref[:, :, at : at + width] = value.astype(out_ref.dtype).reshape(
-                    blocks, length // blocks, width
+                    some, length // some, width
                 )
 
-    @pl.when(pl.program_id(0) == pl.num_programs(0) - 1)
+    @pl.when(step_at == steps - 1)
     def _():
         for copy in copies():
             copy.wait()
@@ -217,14 +228,13 @@
         grid_spec=pltpu.PrefetchScalarGridSpec(
             num_scalar_prefetch=1,
             grid=(blocks // some,),
-            in_specs=[
-                far,
-                pl.BlockSpec((some, length, slots, width), lambda i, place: (i, 0, 0, 0)),
-            ],
+            in_specs=[far, far],
             out_specs=[far] * len(cuts) + [out] * ctx_count,
             scratch_shapes=[
+                pltpu.VMEM(view.shape, view.dtype),
                 pltpu.VMEM((some * length * slots, width), jnp.float32),
                 pltpu.SemaphoreType.DMA((len(cuts),)),
+                pltpu.SemaphoreType.DMA((blocks // some,)),
             ],
         ),
         out_shape=[jax.ShapeDtypeStruct((rows, depth), tokens.dtype) for _, _, rows in cuts]
@@ -374,7 +384,8 @@
             yield head, pl.ds(low + head, each, stride=heads), slice(at, at + each)
 
 
-def prefix_kernel(scale, heads, query_ref, keys, values, acc_ref, stat_ref, flat):
+def prefix_kernel(scale, heads, query_ref, keys, values, *refs):
+    acc_ref, stat_ref, flat = refs[-3:]
     rows, width = query_ref.shape
     tall = width + ONES
     half = stat_ref.shape[0] // 2
@@ -391,32 +402,43 @@
         stat_ref[half:, here] = jnp.broadcast_to(mixed[width : width + 1], (half, row_max.shape[1]))
 
 
-def prefix_attend(query_rows, keys, values, chunk, scale, heads):
+def prefix_attend(query_rows, keys, values, chunk, scale, heads, part=(0, 1), state=None):
     all_rows, width = query_rows.shape
     row_total = all_rows // CHUNKS
-    rows = min(1024, row_total)
-    steps = row_total // rows
+    at, count = part
+    rows = min(1024, row_total // count)
+    steps = row_total // rows // count
+    first = chunk * count * steps + at * steps
+    out_specs = [
+        pl.BlockSpec((width, rows), lambda i: (0, at * steps + i)),
+        pl.BlockSpec((8, rows), lambda i: (0, at * steps + i)),
+    ]
+    in_specs = [
+        pl.BlockSpec((rows, width), lambda i: (first + i, 0)),
+        pl.BlockSpec(keys.shape, lambda i: (0, 0)),
+        pl.BlockSpec(values.shape, lambda i: (0, 0)),
+    ]
+    operands = [query_rows, keys, values]
+    aliases = {}
+    if state is not None:
+        in_specs += [pl.BlockSpec(memory_space=pl.ANY)] * 2
+        operands += state
+        aliases = {3: 0, 4: 1}
     return pl.pallas_call(
         functools.partial(prefix_kernel, scale, heads),
         grid=(steps,),
-        in_specs=[
-            pl.BlockSpec((rows, width), lambda i: (chunk * steps + i, 0)),
-            pl.BlockSpec(keys.shape, lambda i: (0, 0)),
-            pl.BlockSpec(values.shape, lambda i: (0, 0)),
-        ],
-        out_specs=[
-            pl.BlockSpec((width, rows), lambda i: (0, i)),
-            pl.BlockSpec((8, rows), lambda i: (0, i)),
-        ],
+        in_specs=in_specs,
+        out_specs=out_specs,
         out_shape=[
             jax.ShapeDtypeStruct((width, row_total), jnp.float32),
             jax.ShapeDtypeStruct((8, row_total), jnp.float32),
         ],
+        input_output_aliases=aliases,
         scratch_shapes=[pltpu.VMEM((rows, width), jnp.float32)],
         compiler_params=params(),
         cost_estimate=cost("prefix_attend"),
         name="prefix_attend",
-    )(query_rows, keys, values)
+    )(*operands)
 
 
 def fresh_kernel(
@@ -536,14 +558,15 @@
 
     top = batch_count // 2
     steps = list(range(batch_count - 1, top, -1)) + list(range(1, top))
-    cuts = [(bits, i * rows, rows) for bits in steps for i in range(CHUNKS)]
-    cuts.append((top, 0, token_count))
+    cuts = [(bits, 0, token_count) for bits in [*steps, top]]
     pieces, pools = prepare(place, tokens, depth, cuts, prefix_pool, ctx_count, heads)
     arrived = [trade(piece, "batch", bits) for piece, (bits, _, _) in zip(pieces, cuts[:-1])]
     pools, (key_weight, value_weight) = after(pools, (key_weight, value_weight))
     pools = [shift(part, "ctx", step) if step else part for step, part in enumerate(pools)]
 
     weights = arrange_weights(key_weight, value_weight, ctx_count, heads, head_count)
+    weights, last = after(weights, pieces[-1])
+    last = trade(last, "batch", top)
 
     query_rows = queries.reshape(token_count, heads, group, width)
     query_rows = query_rows.transpose(0, 2, 1, 3).reshape(-1, width)
@@ -565,8 +588,6 @@
 
     every = slice(None)
     parts_of = [slice(i * rows, (i + 1) * rows) for i in range(CHUNKS)]
-
-    last = trade(pieces[-1], "batch", top)
 
     sums = [[], []]
     if steps:
@@ -596,24 +617,28 @@
     kept, *_ = late_project(0, jnp.float32, "late_kept", [])
     far, near = far[:1], far[1:]
     late = [kept, *terms]
-    far, near = ([trade(part, "batch", 1) for part in parts] for parts in (far, near))
+    far = [trade(part, "batch", 1) for part in far]
     own_at = slice(token_count, 2 * token_count)
-    late_others = [others(late, here) for here in [*parts_of, own_at]]
-    late_others[-1], (keys, values) = after(late_others[-1], (keys, values))
-    *late_others, own_others = [spread(part) for part in late_others]
-    states.append(prefix_attend(query_rows, keys, values, 1, scale, heads))
-    states[1], late_others[0] = after(states[1], late_others[0])
+    *late_others, own_others = [others(late, here) for here in [*parts_of, own_at]]
+    late_others[0] = spread(late_others[0])
+    late_others[1], (keys, values) = after(late_others[1], (keys, values))
+    state = prefix_attend(query_rows, keys, values, 1, scale, heads, (0, 2))
+    state, (late_others[1], own_others, near) = after(state, (late_others[1], own_others, near))
+    late_others[1], own_others = spread(late_others[1]), spread(own_others)
+    near = [trade(part, "batch", 1) for part in near]
 
     away = []
     for chunk, here in enumerate(parts_of):
         part = added(late, 0, here) + sum(p.astype(jnp.float32) for p in late_others[chunk])
         part = part + sum(p[here].astype(jnp.float32) for p in far)
-        if chunk + 1 < CHUNKS:
-            (far, late), late_others[chunk + 1] = after((far, late), late_others[chunk + 1])
         part = part.astype(jnp.bfloat16)
-        if away:
+        if chunk == 0:
+            (far, late), late_others[1] = after((far, late), late_others[1])
+            part, state = after(part, state)
+        else:
             away[-1], part = after(away[-1], part)
         away.append(trade(part, "batch", top))
+    states.append(prefix_attend(query_rows, keys, values, 1, scale, heads, (1, 2), state))
 
     result = None
     fresh = []

time: 99.9 us -> 96.8 us (0.969)
  starting transfers between devices: 32 us -> 19.9 us
  waiting for transfers between devices: 17.3 us -> 23.3 us
  local copies, waits for them, and re-layouts: 3.23 us -> 5.57 us
    ppermute x9 -> x7, starting transfers between devices: 24.5 us -> 12.6 us  [trade(): lax.ppermute(array, axis, [(i, i ^ bits) for i in range(lax.axis_size(axi...]
    ppermute x9 -> x7, waiting for transfers between devices: 16.7 us -> 22.8 us  [trade(): lax.ppermute(array, axis, [(i, i ^ bits) for i in range(lax.axis_size(axi...]
    unnamed x24 -> x36, local copies, waits for them, and re-layouts: 3.23 us -> 5.57 us
    pallas_call x2 -> x3, Pallas kernels: 15.6 us -> 15.6 us  [prefix_attend(): pl.pallas_call(functools.partial(prefix_kernel, scale, heads), grid=(step...]
  transfers between devices with their start and end apart: 17 -> 15, of which waited for: 6 -> 5; matrix products, arithmetic and copies ran while one was open for 2% -> 2% of each run, Pallas kernels for 33% -> 34%
where the time goes in v10:
time: 96.8 us; the launch traced here: 96.6 us
  Pallas kernels  45.1 us (47%)
  waiting for transfers between devices  23.3 us (24%)
  starting transfers between devices  19.9 us (21%)
  local copies, waits for them, and re-layouts  5.57 us (6%)
  other arithmetic  1.74 us (2%)
  between operations  0.97 us (1%)
    ppermute x7, waiting for transfers between devices, trade(): lax.ppermute(array, axis, [(i, i ^ bits) for i in range(lax.axis_size(axi...  22.8 us
    pallas_call x3, Pallas kernels, prefix_attend(): pl.pallas_call(functools.partial(prefix_kernel, scale, heads), grid=(step...  15.6 us
    ppermute x7, starting transfers between devices, trade(): lax.ppermute(array, axis, [(i, i ^ bits) for i in range(lax.axis_size(axi...  12.6 us
    pallas_call x4, Pallas kernels, project(): pl.pallas_call(functools.partial(project_kernel, len(blocks), [len(terms)...  10.7 us
    pallas_call x2, Pallas kernels, fresh_attend(): pl.pallas_call(functools.partial(fresh_kernel, scale, heads, per_token, c...  10 us
    ppermute x8, starting transfers between devices, shift(): lax.ppermute(array, axis, [(i, (i + step) % count) for i in range(count)])  7.36 us
    unnamed x36, local copies, waits for them, and re-layouts  5.57 us
    pallas_call x1, Pallas kernels, prepare(): pl.pallas_call(functools.partial(prepare_kernel, ctx_count, heads, [(bits...  3.26 us
  transfers between devices with their start and end apart: 15, of which 5 were waited for; matrix products, arithmetic and copies ran while one was open for 2% of the time, Pallas kernels for 34%

profile of v10, /device:TPU:0, one launch (start us, length us, event | category | flops | bytes accessed | tf_op | source)
XLA Modules:
  0.0 96.6 jit_solution(8042936234892286498)
XLA Ops:
  0.0 0.1 pad_add_fusion.place_ref
  0.1 1.6 %copy-done.4 = bf16[8,128,4,1,256]{4,2,3,1,0:T(4,128)(2,1)S(1)} copy-done((bf16[8,128,4,1,256]{4,2,3,1,0:T(4,128)(2,1)S(1)}, bf16[8,128,4,1,256]{4,2,3,1,0:T(4,128)(2,1)}, u32[]{:S(2)}) %copy-start.4) | copy-done | bytes 2097176
  1.7 1.6 %copy-done.7 = bf16[256,4096]{1,0:T(8,128)(2,1)S(1)} copy-done((bf16[256,4096]{1,0:T(8,128)(2,1)S(1)}, bf16[256,4096]{1,0:T(8,128)(2,1)}, u32[]{:S(2)}) %copy-start.7) | copy-done | bytes 2097176
  3.3 3.3 %prepare.1 = (bf16[256,1024]{1,0:T(8,128)(2,1)S(1)}, bf16[256,1024]{1,0:T(8,128)(2,1)S(1)}, bf16[256,1024]{1,0:T(8,128)(2,1)}, bf16[8,128,512]{2,1,0:T(8,128)(2,1)S(1)}, bf16[8,128,512]{2,1,0:T(8,128)(2,1)}) custom-call(s32[3]{0:T(128)S(1)} %pad_add_fusion.place_ref, bf16[256,4096]{1,0:T(8,128)(2,1)S(1)} %copy-done.7, bf16[8,128,8,128]{3,2,1,0:T(8,128)(2,1)S(1)} %bitcast.45), custom_call_target="tpu_custom_call" | custom-call | flops 99999997952 | bytes 1 | tf_op jit(solution)/shard_map/prepare/pallas_call | solution.py:224
  6.5 5.1 %collective-permute-start = (bf16[256,1024]{1,0:T(8,128)(2,1)S(1)}, bf16[256,1024]{1,0:T(8,128)(2,1)S(1)}, u32[]{:S(2)}, u32[]{:S(2)}) collective-permute-start(bf16[256,1024]{1,0:T(8,128)(2,1)S(1)} %get-tuple-element.54), channel_id=1, source_target_pairs={{0,12},{4,8},{8,4},{12,0},{1,13},{5,9},{9,5},{13,1},{2,14},{6,10},... | collective-permute-start | bytes 1572872 | tf_op jit(solution)/shard_map/ppermute | solution.py:104
  11.7 0.0 collective-permute-start.1
  11.7 1.5 %collective-permute-start.3 = (bf16[8,128,512]{2,1,0:T(8,128)(2,1)}, bf16[8,128,512]{2,1,0:T(8,128)(2,1)}, u32[]{:S(2)}, u32[]{:S(2)}) collective-permute-start(bf16[8,128,512]{2,1,0:T(8,128)(2,1)} %get-tuple-element.63), channel_id=1, source_target_pairs={{0,2},{2,0},{1,3},{3,1},{4,6},{6,4},{5,7},{7,5},{8,10},{10,8},{9,1... | collective-permute-start | bytes 3145736 | tf_op jit(solution)/shard_map/ppermute | solution.py:100
  13.2 2.5 %arrange_weights.1.refs_2_ = bf16[2,2,1024,512]{3,2,1,0:T(8,128)(2,1)S(1)} custom-call(bf16[1024,8,128]{2,1,0:T(8,128)(2,1)S(1)} %bitcast.46, bf16[1024,8,128]{2,1,0:T(8,128)(2,1)S(1)} %bitcast.47), custom_call_target="tpu_custom_call" | custom-call | flops 99999997952 | bytes 1 | tf_op jit(solution)/shard_map/arrange_weights/pallas_call | solution.py:149
  15.6 0.8 collective-permute-start.4
  17.2 7.3 %collective-permute-done.refs_0_ = bf16[256,1024]{1,0:T(8,128)(2,1)S(1)} collective-permute-done((bf16[256,1024]{1,0:T(8,128)(2,1)S(1)}, bf16[256,1024]{1,0:T(8,128)(2,1)S(1)}, u32[]{:S(2)}, u32[]{:S(2)}) %collective-permute-start) | collective-permute-done | bytes 524320 | tf_op jit(solution)/shard_map/ppermute | solution.py:104
  24.5 11.5 %collective-permute-done.1.refs_1_ = bf16[256,1024]{1,0:T(8,128)(2,1)S(1)} collective-permute-done((bf16[256,1024]{1,0:T(8,128)(2,1)S(1)}, bf16[256,1024]{1,0:T(8,128)(2,1)S(1)}, u32[]{:S(2)}, u32[]{:S(2)}) %collective-permute-start.1) | collective-permute-done | bytes 524320 | tf_op jit(solution)/shard_map/ppermute | solution.py:104
  35.9 2.1 %early_away.1 = bf16[2,512,512]{2,1,0:T(8,128)(2,1)S(1)} custom-call(s32[3]{0:T(128)S(1)} %pad_add_fusion.place_ref, bf16[256,1024]{1,0:T(8,128)(2,1)S(1)} %collective-permute-done.refs_0_, bf16[256,1024]{1,0:T(8,128)(2,1)S(1)} %collective-permute-done.1.refs_1_, bf16[2,2,1024,512]{3,2,1,0:T(8,128)(2,1)S(1)} %arrange_weights.1.refs_2_), custom_call_target="tpu_custom_call" | custom-call | flops 99999997952 | bytes 1 | tf_op jit(solution)/shard_map/early_away/pallas_call | solution.py:293
  38.0 0.1 collective-permute-start.2
  38.1 2.1 %early_kept.1.refs_3_.refs_6_ = f32[2,512,512]{2,1,0:T(8,128)S(1)} custom-call(s32[3]{0:T(128)S(1)} %pad_add_fusion.place_ref, bf16[256,1024]{1,0:T(8,128)(2,1)S(1)} %collective-permute-done.refs_0_, bf16[256,1024]{1,0:T(8,128)(2,1)S(1)} %collective-permute-done.1.refs_1_, bf16[2,2,1024,512]{3,2,1,0:T(8,128)(2,1)S(1)} %arrange_weights.1.refs_2_), custom_call_target="tpu_custom_call" | custom-call | flops 99999997952 | bytes 1 | tf_op jit(solution)/shard_map/early_kept/pallas_call | solution.py:293
  40.2 0.0 copy-start
  40.2 0.0 copy-start.11
  40.2 0.5 collective-permute-done.2.refs_4_.refs_7_
  40.8 1.4 %fusion.4 = (bf16[256,512]{1,0:T(8,128)(2,1)}, bf16[256,512]{1,0:T(8,128)(2,1)}) fusion(f32[2,512,512]{2,1,0:T(8,128)S(1)} %early_kept.1.refs_3_.refs_6_, bf16[2,512,512]{2,1,0:T(8,128)(2,1)S(1)} %collective-permute-done.2.refs_4_.refs_7_), kind=kLoop, calls=%fused_computation.7 | loop fusion | flops 786432 | bytes 2097152 | tf_op jit(solution)/shard_map/convert_element_type | solution.py:584
  42.1 1.4 %collective-permute-start.5 = (bf16[256,512]{1,0:T(8,128)(2,1)}, bf16[256,512]{1,0:T(8,128)(2,1)}, u32[]{:S(2)}, u32[]{:S(2)}) collective-permute-start(bf16[256,512]{1,0:T(8,128)(2,1)} %get-tuple-element.72), channel_id=1, source_target_pairs={{0,2},{2,0},{1,3},{3,1},{4,6},{6,4},{5,7},{7,5},{8,10},{10,8},{9,1... | collective-permute-start | bytes 786440 | tf_op jit(solution)/shard_map/ppermute | solution.py:100
  43.6 0.6 collective-permute-start.6
  44.2 3.0 %pick_blocks.1 = (bf16[1024,256]{1,0:T(8,128)(2,1)S(1)}, bf16[288,1024]{1,0:T(8,128)(2,1)S(1)}) custom-call(s32[3]{0:T(128)S(1)} %pad_add_fusion.place_ref, s32[8]{0:T(128)S(1)} %bitcast.53, bf16[8,128,512]{2,1,0:T(8,128)(2,1)S(1)} %get-tuple-element.64.refs_0_, bf16[8,128,512]{2,1,0:T(8,128)(2,1)} %collective-permute-done.3.refs_1_), custom_call_target="tpu_custom_call" | custom-call | flops 99999997952 | bytes 1 | tf_op jit(solution)/shard_map/pick_blocks/pallas_call | solution.py:357
  47.2 0.0 copy-start.1
  47.3 0.0 copy-start.8
  47.3 7.8 %prefix_attend.3 = (f32[128,4096]{1,0:T(8,128)S(1)}, f32[8,4096]{1,0:T(8,128)S(1)}) custom-call(bf16[8192,128]{1,0:T(8,128)(2,1)S(1)} %bitcast.48, bf16[1024,256]{1,0:T(8,128)(2,1)S(1)} %get-tuple-element.75.keys, bf16[288,1024]{1,0:T(8,128)(2,1)S(1)} %get-tuple-element.76.values), custom_call_target="tpu_custom_call" | custom-call | flops 99999997952 | bytes 1 | tf_op jit(solution)/shard_map/prefix_attend/pallas_call | solution.py:427
  55.1 1.4 %collective-permute-done.4.refs_0_ = bf16[256,1024]{1,0:T(8,128)(2,1)} collective-permute-done((bf16[256,1024]{1,0:T(8,128)(2,1)}, bf16[256,1024]{1,0:T(8,128)(2,1)}, u32[]{:S(2)}, u32[]{:S(2)}) %collective-permute-start.4) | collective-permute-done | bytes 524320 | tf_op jit(solution)/shard_map/ppermute | solution.py:104
  56.6 3.4 %late_away.1 = (bf16[2,512,512]{2,1,0:T(8,128)(2,1)S(1)}, bf16[256,512]{1,0:T(8,128)(2,1)S(1)}, bf16[256,512]{1,0:T(8,128)(2,1)S(1)}) custom-call(s32[3]{0:T(128)S(1)} %pad_add_fusion.place_ref, bf16[256,1024]{1,0:T(8,128)(2,1)} %collective-permute-done.4.refs_0_, bf16[256,4096]{1,0:T(8,128)(2,1)S(1)} %copy-done.8, ...), custom_call_target="tpu_custom_call" | custom-call | flops 99999997952 | bytes 1 | tf_op jit(solution)/shard_map/late_away/pallas_call | solution.py:293
  60.0 0.0 copy-start.10
  60.0 0.1 collective-permute-start.7
  60.1 2.3 %copy-done.13 = bf16[2,2,1024,512]{3,2,1,0:T(8,128)(2,1)S(1)} copy-done((bf16[2,2,1024,512]{3,2,1,0:T(8,128)(2,1)S(1)}, bf16[2,2,1024,512]{3,2,1,0:T(8,128)(2,1)}, u32[]{:S(2)}) %copy-start.13) | copy-done | bytes 4194328
  62.4 3.1 %late_kept.1.rest_0_.rest_1_ = f32[2,512,512]{2,1,0:T(8,128)S(1)} custom-call(s32[3]{0:T(128)S(1)} %pad_add_fusion.place_ref, bf16[256,1024]{1,0:T(8,128)(2,1)} %collective-permute-done.4.refs_0_, bf16[256,4096]{1,0:T(8,128)(2,1)S(1)} %copy-done.8, bf16[2,2,1024,512]{3,2,1,0:T(8,128)(2,1)S(1)} %copy-done.13), custom_call_target="tpu_custom_call" | custom-call | flops 99999997952 | bytes 1 | tf_op jit(solution)/shard_map/late_kept/pallas_call | solution.py:293
  65.6 1.7 %collective-permute-start.9 = (bf16[256,512]{1,0:T(8,128)(2,1)S(1)}, bf16[256,512]{1,0:T(8,128)(2,1)S(1)}, u32[]{:S(2)}, u32[]{:S(2)}) collective-permute-start(bf16[256,512]{1,0:T(8,128)(2,1)S(1)} %get-tuple-element.77), channel_id=1, source_target_pairs={{0,4},{4,0},{8,12},{12,8},{1,5},{5,1},{9,13},{13,9},{2,6},{6,2},{1... | collective-permute-start | bytes 786440 | tf_op jit(solution)/shard_map/ppermute | solution.py:104
  67.2 0.0 collective-permute-done.7.rest_1_.rest_2_
  67.2 0.1 fusion.15
  67.3 1.6 %collective-permute-start.8 = (bf16[128,512]{1,0:T(8,128)(2,1)S(1)}, bf16[128,512]{1,0:T(8,128)(2,1)S(1)}, u32[]{:S(2)}, u32[]{:S(2)}) collective-permute-start(bf16[128,512]{1,0:T(8,128)(2,1)S(1)} %get-tuple-element.103), channel_id=1, source_target_pairs={{0,2},{2,0},{1,3},{3,1},{4,6},{6,4},{5,7},{7,5},{8,10},{10,8},{9,1... | collective-permute-start | bytes 393224 | tf_op jit(solution)/shard_map/ppermute | solution.py:100
  68.9 3.9 %prefix_attend.4 = (f32[128,4096]{1,0:T(8,128)S(1)}, f32[8,4096]{1,0:T(8,128)S(1)}) custom-call(bf16[8192,128]{1,0:T(8,128)(2,1)S(1)} %bitcast.49, bf16[1024,256]{1,0:T(8,128)(2,1)S(1)} %copy-done.17, bf16[288,1024]{1,0:T(8,128)(2,1)S(1)} %copy-done.15), custom_call_target="tpu_custom_call" | custom-call | flops 99999997952 | bytes 1 | tf_op jit(solution)/shard_map/prefix_attend/pallas_call | solution.py:427
  72.8 0.1 fusion.5
  72.9 0.6 collective-permute-start.10
  73.5 1.5 %collective-permute-start.11 = (bf16[256,512]{1,0:T(8,128)(2,1)S(1)}, bf16[256,512]{1,0:T(8,128)(2,1)S(1)}, u32[]{:S(2)}, u32[]{:S(2)}) collective-permute-start(bf16[256,512]{1,0:T(8,128)(2,1)S(1)} %fusion.5), channel_id=1, source_target_pairs={{0,2},{2,0},{1,3},{3,1},{4,6},{6,4},{5,7},{7,5},{8,10},{10,8},{9,1... | collective-permute-start | bytes 786440 | tf_op jit(solution)/shard_map/ppermute | solution.py:100
  75.0 0.4 collective-permute-start.12
  75.4 0.1 fusion.10
  75.5 1.1 %collective-permute-start.13 = (bf16[128,512]{1,0:T(8,128)(2,1)S(1)}, bf16[128,512]{1,0:T(8,128)(2,1)S(1)}, u32[]{:S(2)}, u32[]{:S(2)}) collective-permute-start(bf16[128,512]{1,0:T(8,128)(2,1)S(1)} %fusion.10), channel_id=1, source_target_pairs={{0,8},{4,12},{8,0},{12,4},{1,9},{5,13},{9,1},{13,5},{2,10},{6,14},... | collective-permute-start | bytes 393224 | tf_op jit(solution)/shard_map/ppermute | solution.py:104
  76.6 3.9 %prefix_attend.5 = (f32[128,4096]{1,0:T(8,128)S(1)}, f32[8,4096]{1,0:T(8,128)S(1)}) custom-call(bf16[8192,128]{1,0:T(8,128)(2,1)S(1)} %bitcast.50, bf16[1024,256]{1,0:T(8,128)(2,1)S(1)} %copy-done.17, bf16[288,1024]{1,0:T(8,128)(2,1)S(1)} %copy-done.15, f32[128,4096]{1,0:T(8,128)S(1)} %get-tuple-element.84.refs_0_, ...), custom_call_target="tpu_custom_call", output_to_operand_aliasing={{0}: (3, {}), {1}: (4, {})} | custom-call | flops 99999997952 | bytes 1 | tf_op jit(solution)/shard_map/prefix_attend/pallas_call | solution.py:427
  80.5 0.1 fusion.13
  80.6 2.6 %collective-permute-done.13.rest_4_ = bf16[128,512]{1,0:T(8,128)(2,1)S(1)} collective-permute-done((bf16[128,512]{1,0:T(8,128)(2,1)S(1)}, bf16[128,512]{1,0:T(8,128)(2,1)S(1)}, u32[]{:S(2)}, u32[]{:S(2)}) %collective-permute-start.13) | collective-permute-done | bytes 131104 | tf_op jit(solution)/shard_map/ppermute | solution.py:104
  83.2 3.4 %collective-permute-start.14 = (bf16[128,512]{1,0:T(8,128)(2,1)S(1)}, bf16[128,512]{1,0:T(8,128)(2,1)S(1)}, u32[]{:S(2)}, u32[]{:S(2)}) collective-permute-start(bf16[128,512]{1,0:T(8,128)(2,1)S(1)} %fusion.13), channel_id=1, source_target_pairs={{0,8},{4,12},{8,0},{12,4},{1,9},{5,13},{9,1},{13,5},{2,10},{6,14},... | collective-permute-start | bytes 393224 | tf_op jit(solution)/shard_map/ppermute | solution.py:104
  86.6 0.0 collective-permute-done.11.rest_2_.rest_3_
  86.6 4.7 %fresh_attend.2 = (bf16[8192,128]{1,0:T(8,128)(2,1)}, bf16[128,512]{1,0:T(8,128)(2,1)S(1)}) custom-call(s32[1]{0:T(128)S(6)} %copy.17.length_ref, bf16[8192,128]{1,0:T(8,128)(2,1)S(1)} %bitcast.51, f32[128,4096]{1,0:T(8,128)S(1)} %get-tuple-element.88.acc_ref, f32[8,4096]{1,0:T(8,128)S(1)} %get-tuple-element.89.stat_ref, ...), custom_call_target="tpu_custom_call" | custom-call | flops 99999997952 | bytes 1 | tf_op jit(solution)/shard_map/fresh_attend/pallas_call | solution.py:512
  91.3 5.3 %fresh_attend.3 = (bf16[8192,128]{1,0:T(8,128)(2,1)}, bf16[128,512]{1,0:T(8,128)(2,1)}) custom-call(s32[1]{0:T(128)S(6)} %copy.17.length_ref, bf16[8192,128]{1,0:T(8,128)(2,1)S(1)} %bitcast.52, f32[128,4096]{1,0:T(8,128)S(1)} %get-tuple-element.86.acc_ref, f32[8,4096]{1,0:T(8,128)S(1)} %get-tuple-element.87.stat_ref, ...), custom_call_target="tpu_custom_call", output_to_operand_aliasing={{0}: (10, {})} | custom-call | flops 99999997952 | bytes 1 | tf_op jit(solution)/shard_map/fresh_attend/pallas_call | solution.py:512
  (36 shorter events, 0.1 us)
Async XLA Ops:
  0.1 1.6 %copy-start.4 = (bf16[8,128,4,1,256]{4,2,3,1,0:T(4,128)(2,1)S(1)}, bf16[8,128,4,1,256]{4,2,3,1,0:T(4,128)(2,1)}, u32[]{:S(2)}) copy-start(bf16[8,128,4,1,256]{4,2,3,1,0:T(4,128)(2,1)} %param.11) | copy-start | bytes 6291460
  1.7 1.6 %copy-start.7 = (bf16[256,4096]{1,0:T(8,128)(2,1)S(1)}, bf16[256,4096]{1,0:T(8,128)(2,1)}, u32[]{:S(2)}) copy-start(bf16[256,4096]{1,0:T(8,128)(2,1)} %refs_1_.3) | copy-start | bytes 6291460
  3.3 9.9 %copy-start.5 = (bf16[1,1,1024,4,2,128]{5,4,3,2,1,0:T(2,128)(2,1)S(1)}, bf16[1,1,1024,4,2,128]{5,4,3,2,1,0:T(2,128)(2,1)}, u32[]{:S(2)}) copy-start(bf16[1,1,1024,4,2,128]{5,4,3,2,1,0:T(2,128)(2,1)} %param.8) | copy-start | bytes 6291460
  3.3 9.9 %copy-start.6 = (bf16[1,1,1024,4,2,128]{5,4,3,2,1,0:T(2,128)(2,1)S(1)}, bf16[1,1,1024,4,2,128]{5,4,3,2,1,0:T(2,128)(2,1)}, u32[]{:S(2)}) copy-start(bf16[1,1,1024,4,2,128]{5,4,3,2,1,0:T(2,128)(2,1)} %param.9) | copy-start | bytes 6291460
  6.5 18.0 %collective-permute-start = (bf16[256,1024]{1,0:T(8,128)(2,1)S(1)}, bf16[256,1024]{1,0:T(8,128)(2,1)S(1)}, u32[]{:S(2)}, u32[]{:S(2)}) collective-permute-start(bf16[256,1024]{1,0:T(8,128)(2,1)S(1)} %get-tuple-element.54), channel_id=1, source_target_pairs={{0,12},{4,8},{8,4},{12,0},{1,13},{5,9},{9,5},{13,1},{2,14},{6,10},... | collective-permute-start | bytes 1572872 | tf_op jit(solution)/shard_map/ppermute | solution.py:104
  11.7 24.3 %collective-permute-start.1 = (bf16[256,1024]{1,0:T(8,128)(2,1)S(1)}, bf16[256,1024]{1,0:T(8,128)(2,1)S(1)}, u32[]{:S(2)}, u32[]{:S(2)}) collective-permute-start(bf16[256,1024]{1,0:T(8,128)(2,1)S(1)} %get-tuple-element.55), channel_id=1, source_target_pairs={{0,4},{4,0},{8,12},{12,8},{1,5},{5,1},{9,13},{13,9},{2,6},{6,2},{1... | collective-permute-start | bytes 1572872 | tf_op jit(solution)/shard_map/ppermute | solution.py:104
  11.7 30.5 %collective-permute-start.3 = (bf16[8,128,512]{2,1,0:T(8,128)(2,1)}, bf16[8,128,512]{2,1,0:T(8,128)(2,1)}, u32[]{:S(2)}, u32[]{:S(2)}) collective-permute-start(bf16[8,128,512]{2,1,0:T(8,128)(2,1)} %get-tuple-element.63), channel_id=1, source_target_pairs={{0,2},{2,0},{1,3},{3,1},{4,6},{6,4},{5,7},{7,5},{8,10},{10,8},{9,1... | collective-permute-start | bytes 3145736 | tf_op jit(solution)/shard_map/ppermute | solution.py:100
  15.6 40.9 %copy-start.12 = (bf16[2,2,1024,512]{3,2,1,0:T(8,128)(2,1)}, bf16[2,2,1024,512]{3,2,1,0:T(8,128)(2,1)S(1)}, u32[]{:S(2)}) copy-start(bf16[2,2,1024,512]{3,2,1,0:T(8,128)(2,1)S(1)} %arrange_weights.1.refs_2_) | copy-start | bytes 12582916
  15.6 40.9 %collective-permute-start.4 = (bf16[256,1024]{1,0:T(8,128)(2,1)}, bf16[256,1024]{1,0:T(8,128)(2,1)}, u32[]{:S(2)}, u32[]{:S(2)}) collective-permute-start(bf16[256,1024]{1,0:T(8,128)(2,1)} %get-tuple-element.70), channel_id=1, source_target_pairs={{0,8},{4,12},{8,0},{12,4},{1,9},{5,13},{9,1},{13,5},{2,10},{6,14},... | collective-permute-start | bytes 1572872 | tf_op jit(solution)/shard_map/ppermute | solution.py:104
  38.0 2.7 %collective-permute-start.2 = (bf16[2,512,512]{2,1,0:T(8,128)(2,1)S(1)}, bf16[2,512,512]{2,1,0:T(8,128)(2,1)S(1)}, u32[]{:S(2)}, u32[]{:S(2)}) collective-permute-start(bf16[2,512,512]{2,1,0:T(8,128)(2,1)S(1)} %early_away.1), channel_id=1, source_target_pairs={{0,1},{1,0},{2,3},{3,2},{4,5},{5,4},{6,7},{7,6},{8,9},{9,8},{10,11... | collective-permute-start | bytes 3145736 | tf_op jit(solution)/shard_map/ppermute | solution.py:100
  40.2 7.0 %copy-start = (f32[2,512,512]{2,1,0:T(8,128)}, f32[2,512,512]{2,1,0:T(8,128)S(1)}, u32[]{:S(2)}) copy-start(f32[2,512,512]{2,1,0:T(8,128)S(1)} %early_kept.1.refs_3_.refs_6_) | copy-start | bytes 6291460
  40.2 4.0 %copy-start.11 = (s32[1,8]{1,0:T(1,128)S(1)}, s32[1,8]{1,0:T(1,128)}, u32[]{:S(2)}) copy-start(s32[1,8]{1,0:T(1,128)} %param.12) | copy-start | bytes 100
  40.7 6.5 %copy-start.2 = (bf16[2,512,512]{2,1,0:T(8,128)(2,1)}, bf16[2,512,512]{2,1,0:T(8,128)(2,1)S(1)}, u32[]{:S(2)}) copy-start(bf16[2,512,512]{2,1,0:T(8,128)(2,1)S(1)} %collective-permute-done.2.refs_4_.refs_7_) | copy-start | bytes 3145732
  42.1 14.4 %collective-permute-start.5 = (bf16[256,512]{1,0:T(8,128)(2,1)}, bf16[256,512]{1,0:T(8,128)(2,1)}, u32[]{:S(2)}, u32[]{:S(2)}) collective-permute-start(bf16[256,512]{1,0:T(8,128)(2,1)} %get-tuple-element.72), channel_id=1, source_target_pairs={{0,2},{2,0},{1,3},{3,1},{4,6},{6,4},{5,7},{7,5},{8,10},{10,8},{9,1... | collective-permute-start | bytes 786440 | tf_op jit(solution)/shard_map/ppermute | solution.py:100
  43.6 13.0 %collective-permute-start.6 = (bf16[256,512]{1,0:T(8,128)(2,1)}, bf16[256,512]{1,0:T(8,128)(2,1)}, u32[]{:S(2)}, u32[]{:S(2)}) collective-permute-start(bf16[256,512]{1,0:T(8,128)(2,1)} %get-tuple-element.73), channel_id=1, source_target_pairs={{0,2},{2,0},{1,3},{3,1},{4,6},{6,4},{5,7},{7,5},{8,10},{10,8},{9,1... | collective-permute-start | bytes 786440 | tf_op jit(solution)/shard_map/ppermute | solution.py:100
  44.2 3.1 %copy-start.9 = (bf16[256,2,1,2048]{3,1,2,0:T(2,128)(2,1)S(1)}, bf16[256,2,1,2048]{3,1,2,0:T(2,128)(2,1)}, u32[]{:S(2)}) copy-start(bf16[256,2,1,2048]{3,1,2,0:T(2,128)(2,1)} %param.10) | copy-start | bytes 6291460
  47.2 7.9 %copy-start.14 = (bf16[288,1024]{1,0:T(8,128)(2,1)}, bf16[288,1024]{1,0:T(8,128)(2,1)S(1)}, u32[]{:S(2)}) copy-start(bf16[288,1024]{1,0:T(8,128)(2,1)S(1)} %get-tuple-element.76.values) | copy-start | bytes 1769476
  47.2 7.9 %copy-start.16 = (bf16[1024,256]{1,0:T(8,128)(2,1)}, bf16[1024,256]{1,0:T(8,128)(2,1)S(1)}, u32[]{:S(2)}) copy-start(bf16[1024,256]{1,0:T(8,128)(2,1)S(1)} %get-tuple-element.75.keys) | copy-start | bytes 1572868
  47.2 9.3 %copy-start.1 = (f32[2,512,512]{2,1,0:T(8,128)S(1)}, f32[2,512,512]{2,1,0:T(8,128)}, u32[]{:S(2)}) copy-start(f32[2,512,512]{2,1,0:T(8,128)} %copy-done) | copy-start | bytes 6291460
  47.3 9.3 %copy-start.3 = (bf16[2,512,512]{2,1,0:T(8,128)(2,1)S(1)}, bf16[2,512,512]{2,1,0:T(8,128)(2,1)}, u32[]{:S(2)}) copy-start(bf16[2,512,512]{2,1,0:T(8,128)(2,1)} %copy-done.2) | copy-start | bytes 3145732
  47.3 9.3 %copy-start.8 = (bf16[256,4096]{1,0:T(8,128)(2,1)S(1)}, bf16[256,4096]{1,0:T(8,128)(2,1)}, u32[]{:S(2)}) copy-start(bf16[256,4096]{1,0:T(8,128)(2,1)} %refs_1_.3) | copy-start | bytes 6291460
  60.0 8.8 %copy-start.10 = (bf16[256,2,1,2048]{3,1,2,0:T(2,128)(2,1)S(1)}, bf16[256,2,1,2048]{3,1,2,0:T(2,128)(2,1)}, u32[]{:S(2)}) copy-start(bf16[256,2,1,2048]{3,1,2,0:T(2,128)(2,1)} %param.10) | copy-start | bytes 6291460
  60.0 7.2 %collective-permute-start.7 = (bf16[2,512,512]{2,1,0:T(8,128)(2,1)S(1)}, bf16[2,512,512]{2,1,0:T(8,128)(2,1)S(1)}, u32[]{:S(2)}, u32[]{:S(2)}) collective-permute-start(bf16[2,512,512]{2,1,0:T(8,128)(2,1)S(1)} %get-tuple-element.74), channel_id=1, source_target_pairs={{0,1},{1,0},{2,3},{3,2},{4,5},{5,4},{6,7},{7,6},{8,9},{9,8},{10,11... | collective-permute-start | bytes 3145736 | tf_op jit(solution)/shard_map/ppermute | solution.py:100
  60.1 2.3 %copy-start.13 = (bf16[2,2,1024,512]{3,2,1,0:T(8,128)(2,1)S(1)}, bf16[2,2,1024,512]{3,2,1,0:T(8,128)(2,1)}, u32[]{:S(2)}) copy-start(bf16[2,2,1024,512]{3,2,1,0:T(8,128)(2,1)} %copy-done.12) | copy-start | bytes 12582916
  62.4 6.4 %copy-start.15 = (bf16[288,1024]{1,0:T(8,128)(2,1)S(1)}, bf16[288,1024]{1,0:T(8,128)(2,1)}, u32[]{:S(2)}) copy-start(bf16[288,1024]{1,0:T(8,128)(2,1)} %copy-done.14) | copy-start | bytes 1769476
  62.4 6.4 %copy-start.17 = (bf16[1024,256]{1,0:T(8,128)(2,1)S(1)}, bf16[1024,256]{1,0:T(8,128)(2,1)}, u32[]{:S(2)}) copy-start(bf16[1024,256]{1,0:T(8,128)(2,1)} %copy-done.16) | copy-start | bytes 1572868
  65.6 9.9 %collective-permute-start.9 = (bf16[256,512]{1,0:T(8,128)(2,1)S(1)}, bf16[256,512]{1,0:T(8,128)(2,1)S(1)}, u32[]{:S(2)}, u32[]{:S(2)}) collective-permute-start(bf16[256,512]{1,0:T(8,128)(2,1)S(1)} %get-tuple-element.77), channel_id=1, source_target_pairs={{0,4},{4,0},{8,12},{12,8},{1,5},{5,1},{9,13},{13,9},{2,6},{6,2},{1... | collective-permute-start | bytes 786440 | tf_op jit(solution)/shard_map/ppermute | solution.py:104
  67.3 8.1 %collective-permute-start.8 = (bf16[128,512]{1,0:T(8,128)(2,1)S(1)}, bf16[128,512]{1,0:T(8,128)(2,1)S(1)}, u32[]{:S(2)}, u32[]{:S(2)}) collective-permute-start(bf16[128,512]{1,0:T(8,128)(2,1)S(1)} %get-tuple-element.103), channel_id=1, source_target_pairs={{0,2},{2,0},{1,3},{3,1},{4,6},{6,4},{5,7},{7,5},{8,10},{10,8},{9,1... | collective-permute-start | bytes 393224 | tf_op jit(solution)/shard_map/ppermute | solution.py:100
  72.9 7.6 %collective-permute-start.10 = (bf16[128,512]{1,0:T(8,128)(2,1)S(1)}, bf16[128,512]{1,0:T(8,128)(2,1)S(1)}, u32[]{:S(2)}, u32[]{:S(2)}) collective-permute-start(bf16[128,512]{1,0:T(8,128)(2,1)S(1)} %get-tuple-element.90), channel_id=1, source_target_pairs={{0,2},{2,0},{1,3},{3,1},{4,6},{6,4},{5,7},{7,5},{8,10},{10,8},{9,1... | collective-permute-start | bytes 393224 | tf_op jit(solution)/shard_map/ppermute | solution.py:100
  73.5 13.1 %collective-permute-start.11 = (bf16[256,512]{1,0:T(8,128)(2,1)S(1)}, bf16[256,512]{1,0:T(8,128)(2,1)S(1)}, u32[]{:S(2)}, u32[]{:S(2)}) collective-permute-start(bf16[256,512]{1,0:T(8,128)(2,1)S(1)} %fusion.5), channel_id=1, source_target_pairs={{0,2},{2,0},{1,3},{3,1},{4,6},{6,4},{5,7},{7,5},{8,10},{10,8},{9,1... | collective-permute-start | bytes 786440 | tf_op jit(solution)/shard_map/ppermute | solution.py:100
  75.0 11.6 %collective-permute-start.12 = (bf16[256,512]{1,0:T(8,128)(2,1)S(1)}, bf16[256,512]{1,0:T(8,128)(2,1)S(1)}, u32[]{:S(2)}, u32[]{:S(2)}) collective-permute-start(bf16[256,512]{1,0:T(8,128)(2,1)S(1)} %get-tuple-element.94), channel_id=1, source_target_pairs={{0,4},{4,0},{8,12},{12,8},{1,5},{5,1},{9,13},{13,9},{2,6},{6,2},{1... | collective-permute-start | bytes 786440 | tf_op jit(solution)/shard_map/ppermute | solution.py:104
  75.5 7.7 %collective-permute-start.13 = (bf16[128,512]{1,0:T(8,128)(2,1)S(1)}, bf16[128,512]{1,0:T(8,128)(2,1)S(1)}, u32[]{:S(2)}, u32[]{:S(2)}) collective-permute-start(bf16[128,512]{1,0:T(8,128)(2,1)S(1)} %fusion.10), channel_id=1, source_target_pairs={{0,8},{4,12},{8,0},{12,4},{1,9},{5,13},{9,1},{13,5},{2,10},{6,14},... | collective-permute-start | bytes 393224 | tf_op jit(solution)/shard_map/ppermute | solution.py:104
  83.2 8.1 %collective-permute-start.14 = (bf16[128,512]{1,0:T(8,128)(2,1)S(1)}, bf16[128,512]{1,0:T(8,128)(2,1)S(1)}, u32[]{:S(2)}, u32[]{:S(2)}) collective-permute-start(bf16[128,512]{1,0:T(8,128)(2,1)S(1)} %fusion.13), channel_id=1, source_target_pairs={{0,8},{4,12},{8,0},{12,4},{1,9},{5,13},{9,1},{13,5},{2,10},{6,14},... | collective-permute-start | bytes 393224 | tf_op jit(solution)/shard_map/ppermute | solution.py:104

commit v11 on v10

--- a/solution.py
+++ b/solution.py
@@ -11,7 +11,8 @@
 CHUNKS = 2
 PART = 1024
 ONES = 16
-VMEM_BYTES = 24 * 1024 * 1024
+VMEM_BYTES = 16 * 1024 * 1024
+MOST_VMEM_BYTES = 60 * 1024 * 1024
 LONG = pl.CostEstimate(flops=10**11, bytes_accessed=1, transcendentals=0)
 COSTS = {}
 
@@ -121,8 +122,8 @@
     )
 
 
-def params():
-    return pltpu.CompilerParams(vmem_limit_bytes=VMEM_BYTES)
+def params(limit=None):
+    return pltpu.CompilerParams(vmem_limit_bytes=limit or VMEM_BYTES)
 
 
 def weight_kernel(ctx_count, heads, head_count, key_ref, value_ref, out_ref, flat):
@@ -159,36 +160,44 @@
     )(*views)
 
 
-def prepare_kernel(ctx_count, heads, cuts, place_ref, tokens_ref, pool_ref, *refs):
-    pieces, outs = refs[: len(cuts)], refs[len(cuts) : len(cuts) + ctx_count]
-    held_pool, flat, sems, pool_sems = refs[-4:]
+def cut_kernel(bits, place_ref, tokens_ref, *refs):
+    pieces, sems = refs[:-1], refs[-1]
     depth = pieces[0].shape[1]
-    step_at = pl.program_id(0)
-    some = outs[0].shape[0]
-    steps = pool_ref.shape[0] // some
-
-    def copies():
-        for index, (bits, first) in enumerate(cuts):
-            start = pl.multiple_of((place_ref[0] ^ bits) * depth, depth)
-            source = tokens_ref.at[pl.ds(first, pieces[index].shape[0]), pl.ds(start, depth)]
-            yield pltpu.make_async_copy(source, pieces[index], sems.at[index])
-
-    def pool_copy(index):
-        here = pl.ds(index * some, some)
-        return pltpu.make_async_copy(pool_ref.at[here], held_pool.at[here], pool_sems.at[index])
-
-    @pl.when(step_at == 0)
-    def _():
-        for copy in copies():
-            copy.start()
-        for index in range(steps):
-            pool_copy(index).start()
-
-    pool_copy(step_at).wait()
-    _, length, slots, width = pool_ref.shape
+    copies = []
+    for index, piece in enumerate(pieces):
+        start = pl.multiple_of((place_ref[0] ^ bits[index]) * depth, depth)
+        source = tokens_ref.at[:, pl.ds(start, depth)]
+        copies.append(pltpu.make_async_copy(source, piece, sems.at[index]))
+    for copy in copies:
+        copy.start()
+    for copy in copies:
+        copy.wait()
+
+
+def cut_tokens(place, tokens, depth, bits):
+    far = pl.BlockSpec(memory_space=pltpu.HBM)
+    piece = jax.ShapeDtypeStruct((tokens.shape[0], depth), tokens.dtype)
+    return pl.pallas_call(
+        functools.partial(cut_kernel, bits),
+        grid_spec=pltpu.PrefetchScalarGridSpec(
+            num_scalar_prefetch=1,
+            grid=(1,),
+            in_specs=[far],
+            out_specs=[far] * len(bits),
+            scratch_shapes=[pltpu.SemaphoreType.DMA((len(bits),))],
+        ),
+        out_shape=[piece] * len(bits),
+        compiler_params=params(MOST_VMEM_BYTES),
+        cost_estimate=cost("cut_tokens"),
+        name="cut_tokens",
+    )(place, tokens)
+
+
+def pool_kernel(ctx_count, heads, place_ref, pool_ref, *refs):
+    outs, flat = refs[:-1], refs[-1]
+    some, length, slots, width = pool_ref.shape
     length *= some
-    block = held_pool[pl.ds(step_at * some, some)]
-    flat[...] = block.astype(jnp.float32).reshape(length * slots, width)
+    flat[...] = pool_ref[...].astype(jnp.float32).reshape(length * slots, width)
     for kind in range(2):
         for head in range(heads):
             at = (kind * heads + head) * width
@@ -205,13 +214,8 @@
                     some, length // some, width
                 )
 
-    @pl.when(step_at == steps - 1)
-    def _():
-        for copy in copies():
-            copy.wait()
-
-
-def prepare(place, tokens, depth, cuts, prefix_pool, ctx_count, heads):
+
+def arrange_pool(place, prefix_pool, ctx_count, heads):
     blocks, length, all_heads, _, double = prefix_pool.shape
     width = double // 2
     slots = 2 * all_heads
@@ -220,30 +224,20 @@
     columns = 2 * heads * width
     some = 2 if blocks % 2 == 0 else 1
     out = pl.BlockSpec((some, length, columns), lambda i, place: (i, 0, 0))
-    far = pl.BlockSpec(memory_space=pltpu.HBM)
-    result = pl.pallas_call(
-        functools.partial(
-            prepare_kernel, ctx_count, heads, [(bits, first) for bits, first, _ in cuts]
-        ),
+    return pl.pallas_call(
+        functools.partial(pool_kernel, ctx_count, heads),
         grid_spec=pltpu.PrefetchScalarGridSpec(
             num_scalar_prefetch=1,
             grid=(blocks // some,),
-            in_specs=[far, far],
-            out_specs=[far] * len(cuts) + [out] * ctx_count,
-            scratch_shapes=[
-                pltpu.VMEM(view.shape, view.dtype),
-                pltpu.VMEM((some * length * slots, width), jnp.float32),
-                pltpu.SemaphoreType.DMA((len(cuts),)),
-                pltpu.SemaphoreType.DMA((blocks // some,)),
-            ],
+            in_specs=[pl.BlockSpec((some, length, slots, width), lambda i, place: (i, 0, 0, 0))],
+            out_specs=[out] * ctx_count,
+            scratch_shapes=[pltpu.VMEM((some * length * slots, width), jnp.float32)],
         ),
-        out_shape=[jax.ShapeDtypeStruct((rows, depth), tokens.dtype) for _, _, rows in cuts]
-        + [jax.ShapeDtypeStruct((blocks, length, columns), jnp.bfloat16)] * ctx_count,
+        out_shape=[jax.ShapeDtypeStruct((blocks, length, columns), jnp.bfloat16)] * ctx_count,
         compiler_params=params(),
-        cost_estimate=cost("prepare"),
-        name="prepare",
-    )(place, tokens, view)
-    return result[: len(cuts)], result[len(cuts) :]
+        cost_estimate=cost("arrange_pool"),
+        name="arrange_pool",
+    )(place, view)
 
 
 def total_of(refs):
@@ -558,9 +552,10 @@
 
     top = batch_count // 2
     steps = list(range(batch_count - 1, top, -1)) + list(range(1, top))
-    cuts = [(bits, 0, token_count) for bits in [*steps, top]]
-    pieces, pools = prepare(place, tokens, depth, cuts, prefix_pool, ctx_count, heads)
-    arrived = [trade(piece, "batch", bits) for piece, (bits, _, _) in zip(pieces, cuts[:-1])]
+    pieces = cut_tokens(place, tokens, depth, [*steps, top])
+    pieces, prefix_pool = after(pieces, prefix_pool)
+    arrived = [trade(piece, "batch", bits) for piece, bits in zip(pieces, steps)]
+    pools = arrange_pool(place, prefix_pool, ctx_count, heads)
     pools, (key_weight, value_weight) = after(pools, (key_weight, value_weight))
     pools = [shift(part, "ctx", step) if step else part for step, part in enumerate(pools)]
 

time: 96.8 us -> 140 us (1.45)
  Pallas kernels: 45.1 us -> 96.8 us
  local copies, waits for them, and re-layouts: 5.57 us -> 0.08 us
  waiting for transfers between devices: 23.3 us -> 20.5 us
    pallas_call x1 -> x2, Pallas kernels: 3.26 us -> 52.5 us  [the longest x1 49.6 us: cut_tokens(): pl.pallas_call(functools.partial(cut_kernel, bits), grid_spec=pltpu.Prefe...]
    unnamed x36 -> x32, local copies, waits for them, and re-layouts: 5.57 us -> 0.08 us
    ppermute x7, waiting for transfers between devices: 22.8 us -> 18.8 us  [trade(): lax.ppermute(array, axis, [(i, i ^ bits) for i in range(lax.axis_size(axi...]
    pallas_call x4, Pallas kernels: 10.7 us -> 13.3 us  [project(): pl.pallas_call(functools.partial(project_kernel, len(blocks), [len(terms)...]
  transfers between devices with their start and end apart: 15 -> 15, of which waited for: 5 -> 4; matrix products, arithmetic and copies ran while one was open for 2% -> 1% of each run, Pallas kernels for 34% -> 27%
where the time goes in v11:
time: 140 us
  Pallas kernels  96.8 us (69%)
  waiting for transfers between devices  20.5 us (15%)
  starting transfers between devices  19.8 us (14%)
  other arithmetic  1.87 us (1%)
    pallas_call x1, Pallas kernels, cut_tokens(): pl.pallas_call(functools.partial(cut_kernel, bits), grid_spec=pltpu.Prefe...  49.6 us
    ppermute x7, waiting for transfers between devices, trade(): lax.ppermute(array, axis, [(i, i ^ bits) for i in range(lax.axis_size(axi...  18.8 us
    pallas_call x3, Pallas kernels, prefix_attend(): pl.pallas_call(functools.partial(prefix_kernel, scale, heads), grid=(step...  15.5 us
    pallas_call x4, Pallas kernels, project(): pl.pallas_call(functools.partial(project_kernel, len(blocks), [len(terms)...  13.3 us
    ppermute x7, starting transfers between devices, trade(): lax.ppermute(array, axis, [(i, i ^ bits) for i in range(lax.axis_size(axi...  12.5 us
    pallas_call x2, Pallas kernels, fresh_attend(): pl.pallas_call(functools.partial(fresh_kernel, scale, heads, per_token, c...  10 us
    ppermute x8, starting transfers between devices, shift(): lax.ppermute(array, axis, [(i, (i + step) % count) for i in range(count)])  7.31 us
    pallas_call x1, Pallas kernels, pick_blocks(): pl.pallas_call(functools.partial(pick_kernel, heads, len(pools)), grid_sp...  3.02 us
  transfers between devices with their start and end apart: 15, of which 4 were waited for; matrix products, arithmetic and copies ran while one was open for 1% of the time, Pallas kernels for 27%

profile of v11, /device:TPU:0, one launch (start us, length us, event | category | flops | bytes accessed | tf_op | source)
XLA Modules:
  0.0 140.1 jit_solution(3047398428308659532)
XLA Ops:
  0.0 0.7 pad_add_fusion.place_ref
  0.7 49.6 %cut_tokens.1 = (bf16[256,1024]{1,0:T(8,128)(2,1)}, bf16[256,1024]{1,0:T(8,128)(2,1)}, bf16[256,1024]{1,0:T(8,128)(2,1)}) custom-call(s32[3]{0:T(128)} %pad_add_fusion.place_ref, bf16[256,4096]{1,0:T(8,128)(2,1)} %refs_1_.3), custom_call_target="tpu_custom_call" | custom-call | flops 99999997952 | bytes 1 | tf_op jit(solution)/shard_map/cut_tokens/pallas_call | solution.py:180
  50.2 5.1 %collective-permute-start = (bf16[256,1024]{1,0:T(8,128)(2,1)}, bf16[256,1024]{1,0:T(8,128)(2,1)}, u32[]{:S(2)}, u32[]{:S(2)}) collective-permute-start(bf16[256,1024]{1,0:T(8,128)(2,1)} %get-tuple-element.61), channel_id=1, source_target_pairs={{0,12},{4,8},{8,4},{12,0},{1,13},{5,9},{9,5},{13,1},{2,14},{6,10},... | collective-permute-start | bytes 1572872 | tf_op jit(solution)/shard_map/ppermute | solution.py:105
  55.4 0.0 copy-start.6
  55.4 0.0 copy-start.7
  55.4 3.0 %arrange_pool.1 = (bf16[8,128,512]{2,1,0:T(8,128)(2,1)S(1)}, bf16[8,128,512]{2,1,0:T(8,128)(2,1)}) custom-call(s32[3]{0:T(128)S(1)} %copy-done.4, bf16[8,128,8,128]{3,2,1,0:T(8,128)(2,1)S(1)} %bitcast.45), custom_call_target="tpu_custom_call" | custom-call | flops 99999997952 | bytes 1 | tf_op jit(solution)/shard_map/arrange_pool/pallas_call | solution.py:227
  58.4 1.5 %collective-permute-start.3 = (bf16[8,128,512]{2,1,0:T(8,128)(2,1)}, bf16[8,128,512]{2,1,0:T(8,128)(2,1)}, u32[]{:S(2)}, u32[]{:S(2)}) collective-permute-start(bf16[8,128,512]{2,1,0:T(8,128)(2,1)} %get-tuple-element.71), channel_id=1, source_target_pairs={{0,2},{2,0},{1,3},{3,1},{4,6},{6,4},{5,7},{7,5},{8,10},{10,8},{9,1... | collective-permute-start | bytes 3145736 | tf_op jit(solution)/shard_map/ppermute | solution.py:101
  59.9 2.5 %arrange_weights.1.refs_2_ = bf16[2,2,1024,512]{3,2,1,0:T(8,128)(2,1)S(1)} custom-call(bf16[1024,8,128]{2,1,0:T(8,128)(2,1)S(1)} %bitcast.46, bf16[1024,8,128]{2,1,0:T(8,128)(2,1)S(1)} %bitcast.47), custom_call_target="tpu_custom_call" | custom-call | flops 99999997952 | bytes 1 | tf_op jit(solution)/shard_map/arrange_weights/pallas_call | solution.py:150
  62.3 0.8 collective-permute-start.4
  63.9 4.7 %collective-permute-done.refs_0_ = bf16[256,1024]{1,0:T(8,128)(2,1)} collective-permute-done((bf16[256,1024]{1,0:T(8,128)(2,1)}, bf16[256,1024]{1,0:T(8,128)(2,1)}, u32[]{:S(2)}, u32[]{:S(2)}) %collective-permute-start) | collective-permute-done | bytes 524320 | tf_op jit(solution)/shard_map/ppermute | solution.py:105
  68.5 11.5 %collective-permute-done.1.refs_1_ = bf16[256,1024]{1,0:T(8,128)(2,1)} collective-permute-done((bf16[256,1024]{1,0:T(8,128)(2,1)}, bf16[256,1024]{1,0:T(8,128)(2,1)}, u32[]{:S(2)}, u32[]{:S(2)}) %collective-permute-start.1) | collective-permute-done | bytes 524320 | tf_op jit(solution)/shard_map/ppermute | solution.py:105
  80.0 3.3 %early_away.1 = bf16[2,512,512]{2,1,0:T(8,128)(2,1)S(1)} custom-call(s32[3]{0:T(128)S(1)} %copy-done.4, bf16[256,1024]{1,0:T(8,128)(2,1)} %collective-permute-done.refs_0_, bf16[256,1024]{1,0:T(8,128)(2,1)} %collective-permute-done.1.refs_1_, bf16[2,2,1024,512]{3,2,1,0:T(8,128)(2,1)S(1)} %arrange_weights.1.refs_2_), custom_call_target="tpu_custom_call" | custom-call | flops 99999997952 | bytes 1 | tf_op jit(solution)/shard_map/early_away/pallas_call | solution.py:287
  83.2 0.1 collective-permute-start.2
  83.3 3.3 %early_kept.1.refs_3_.refs_6_ = f32[2,512,512]{2,1,0:T(8,128)S(1)} custom-call(s32[3]{0:T(128)S(1)} %copy-done.4, bf16[256,1024]{1,0:T(8,128)(2,1)} %collective-permute-done.refs_0_, bf16[256,1024]{1,0:T(8,128)(2,1)} %collective-permute-done.1.refs_1_, bf16[2,2,1024,512]{3,2,1,0:T(8,128)(2,1)S(1)} %arrange_weights.1.refs_2_), custom_call_target="tpu_custom_call" | custom-call | flops 99999997952 | bytes 1 | tf_op jit(solution)/shard_map/early_kept/pallas_call | solution.py:287
  86.6 0.0 copy-start
  86.6 0.0 copy-start.11
  86.6 0.0 collective-permute-done.2.refs_4_.refs_7_
  86.7 1.0 fusion.4
  87.6 0.0 collective-permute-done.3.refs_1_
  87.6 1.4 collective-permute-start.5
  89.0 0.6 collective-permute-start.6
  89.6 3.0 %pick_blocks.1 = (bf16[1024,256]{1,0:T(8,128)(2,1)S(1)}, bf16[288,1024]{1,0:T(8,128)(2,1)S(1)}) custom-call(s32[3]{0:T(128)S(1)} %copy-done.4, s32[8]{0:T(128)S(1)} %bitcast.53, bf16[8,128,512]{2,1,0:T(8,128)(2,1)S(1)} %get-tuple-element.72.refs_0_, bf16[8,128,512]{2,1,0:T(8,128)(2,1)} %collective-permute-done.3.refs_1_), custom_call_target="tpu_custom_call" | custom-call | flops 99999997952 | bytes 1 | tf_op jit(solution)/shard_map/pick_blocks/pallas_call | solution.py:351
  92.7 0.0 copy-start.1
  92.7 0.0 copy-start.8
  92.8 7.7 %prefix_attend.3 = (f32[128,4096]{1,0:T(8,128)S(1)}, f32[8,4096]{1,0:T(8,128)S(1)}) custom-call(bf16[8192,128]{1,0:T(8,128)(2,1)S(1)} %bitcast.48, bf16[1024,256]{1,0:T(8,128)(2,1)S(1)} %get-tuple-element.83.keys, bf16[288,1024]{1,0:T(8,128)(2,1)S(1)} %get-tuple-element.84.values), custom_call_target="tpu_custom_call" | custom-call | flops 99999997952 | bytes 1 | tf_op jit(solution)/shard_map/prefix_attend/pallas_call | solution.py:421
  100.5 0.0 collective-permute-done.4.refs_0_
  100.5 1.7 %collective-permute-done.6.refs_8_ = bf16[256,512]{1,0:T(8,128)(2,1)} collective-permute-done((bf16[256,512]{1,0:T(8,128)(2,1)}, bf16[256,512]{1,0:T(8,128)(2,1)}, u32[]{:S(2)}, u32[]{:S(2)}) %collective-permute-start.6) | collective-permute-done | bytes 262176 | tf_op jit(solution)/shard_map/ppermute | solution.py:101
  102.3 3.5 %late_away.1 = (bf16[2,512,512]{2,1,0:T(8,128)(2,1)S(1)}, bf16[256,512]{1,0:T(8,128)(2,1)S(1)}, bf16[256,512]{1,0:T(8,128)(2,1)S(1)}) custom-call(s32[3]{0:T(128)S(1)} %copy-done.4, bf16[256,1024]{1,0:T(8,128)(2,1)} %collective-permute-done.4.refs_0_, bf16[256,4096]{1,0:T(8,128)(2,1)S(1)} %copy-done.8, bf16[2,2,1024,512]{3,2,1,0:T(8,128)(2,1)S(1)} %copy-done.13, ...), custom_call_target="tpu_custom_call" | custom-call | flops 99999997952 | bytes 1 | tf_op jit(solution)/shard_map/late_away/pallas_call | solution.py:287
  105.7 0.0 copy-start.10
  105.8 0.1 collective-permute-start.7
  105.8 3.3 %late_kept.1.rest_0_.rest_1_ = f32[2,512,512]{2,1,0:T(8,128)S(1)} custom-call(s32[3]{0:T(128)S(1)} %copy-done.4, bf16[256,1024]{1,0:T(8,128)(2,1)} %collective-permute-done.4.refs_0_, bf16[256,4096]{1,0:T(8,128)(2,1)S(1)} %copy-done.8, bf16[2,2,1024,512]{3,2,1,0:T(8,128)(2,1)S(1)} %copy-done.13), custom_call_target="tpu_custom_call" | custom-call | flops 99999997952 | bytes 1 | tf_op jit(solution)/shard_map/late_kept/pallas_call | solution.py:287
  109.1 1.8 %collective-permute-start.9 = (bf16[256,512]{1,0:T(8,128)(2,1)S(1)}, bf16[256,512]{1,0:T(8,128)(2,1)S(1)}, u32[]{:S(2)}, u32[]{:S(2)}) collective-permute-start(bf16[256,512]{1,0:T(8,128)(2,1)S(1)} %get-tuple-element.85), channel_id=1, source_target_pairs={{0,4},{4,0},{8,12},{12,8},{1,5},{5,1},{9,13},{13,9},{2,6},{6,2},{1... | collective-permute-start | bytes 786440 | tf_op jit(solution)/shard_map/ppermute | solution.py:105
  110.9 0.0 collective-permute-done.7.rest_1_.rest_2_
  110.9 0.1 fusion.15
  111.0 1.6 %collective-permute-start.8 = (bf16[128,512]{1,0:T(8,128)(2,1)S(1)}, bf16[128,512]{1,0:T(8,128)(2,1)S(1)}, u32[]{:S(2)}, u32[]{:S(2)}) collective-permute-start(bf16[128,512]{1,0:T(8,128)(2,1)S(1)} %get-tuple-element.111), channel_id=1, source_target_pairs={{0,2},{2,0},{1,3},{3,1},{4,6},{6,4},{5,7},{7,5},{8,10},{10,8},{9,1... | collective-permute-start | bytes 393224 | tf_op jit(solution)/shard_map/ppermute | solution.py:101
  112.6 3.9 %prefix_attend.4 = (f32[128,4096]{1,0:T(8,128)S(1)}, f32[8,4096]{1,0:T(8,128)S(1)}) custom-call(bf16[8192,128]{1,0:T(8,128)(2,1)S(1)} %bitcast.49, bf16[1024,256]{1,0:T(8,128)(2,1)S(1)} %copy-done.15, bf16[288,1024]{1,0:T(8,128)(2,1)S(1)} %get-tuple-element.84.values), custom_call_target="tpu_custom_call" | custom-call | flops 99999997952 | bytes 1 | tf_op jit(solution)/shard_map/prefix_attend/pallas_call | solution.py:421
  116.4 0.1 fusion.5
  116.5 0.6 collective-permute-start.10
  117.1 1.5 %collective-permute-start.11 = (bf16[256,512]{1,0:T(8,128)(2,1)S(1)}, bf16[256,512]{1,0:T(8,128)(2,1)S(1)}, u32[]{:S(2)}, u32[]{:S(2)}) collective-permute-start(bf16[256,512]{1,0:T(8,128)(2,1)S(1)} %fusion.5), channel_id=1, source_target_pairs={{0,2},{2,0},{1,3},{3,1},{4,6},{6,4},{5,7},{7,5},{8,10},{10,8},{9,1... | collective-permute-start | bytes 786440 | tf_op jit(solution)/shard_map/ppermute | solution.py:101
  118.6 0.2 collective-permute-start.12
  118.8 0.1 fusion.10
  118.8 1.2 collective-permute-start.13
  120.0 3.9 %prefix_attend.5 = (f32[128,4096]{1,0:T(8,128)S(1)}, f32[8,4096]{1,0:T(8,128)S(1)}) custom-call(bf16[8192,128]{1,0:T(8,128)(2,1)S(1)} %bitcast.50, bf16[1024,256]{1,0:T(8,128)(2,1)S(1)} %copy-done.15, bf16[288,1024]{1,0:T(8,128)(2,1)S(1)} %get-tuple-element.84.values, ...), custom_call_target="tpu_custom_call", output_to_operand_aliasing={{0}: (3, {}), {1}: (4, {})} | custom-call | flops 99999997952 | bytes 1 | tf_op jit(solution)/shard_map/prefix_attend/pallas_call | solution.py:421
  123.9 0.1 fusion.13
  124.0 2.7 %collective-permute-done.13.rest_4_ = bf16[128,512]{1,0:T(8,128)(2,1)S(1)} collective-permute-done((bf16[128,512]{1,0:T(8,128)(2,1)S(1)}, bf16[128,512]{1,0:T(8,128)(2,1)S(1)}, u32[]{:S(2)}, u32[]{:S(2)}) %collective-permute-start.13) | collective-permute-done | bytes 131104 | tf_op jit(solution)/shard_map/ppermute | solution.py:105
  126.7 3.4 %collective-permute-start.14 = (bf16[128,512]{1,0:T(8,128)(2,1)S(1)}, bf16[128,512]{1,0:T(8,128)(2,1)S(1)}, u32[]{:S(2)}, u32[]{:S(2)}) collective-permute-start(bf16[128,512]{1,0:T(8,128)(2,1)S(1)} %fusion.13), channel_id=1, source_target_pairs={{0,8},{4,12},{8,0},{12,4},{1,9},{5,13},{9,1},{13,5},{2,10},{6,14},... | collective-permute-start | bytes 393224 | tf_op jit(solution)/shard_map/ppermute | solution.py:105
  130.1 4.7 %fresh_attend.2 = (bf16[8192,128]{1,0:T(8,128)(2,1)}, bf16[128,512]{1,0:T(8,128)(2,1)S(1)}) custom-call(s32[1]{0:T(128)S(6)} %copy.17.length_ref, bf16[8192,128]{1,0:T(8,128)(2,1)S(1)} %bitcast.51, f32[128,4096]{1,0:T(8,128)S(1)} %get-tuple-element.96.acc_ref, f32[8,4096]{1,0:T(8,128)S(1)} %get-tuple-element.97.stat_ref, ...), custom_call_target="tpu_custom_call" | custom-call | flops 99999997952 | bytes 1 | tf_op jit(solution)/shard_map/fresh_attend/pallas_call | solution.py:506
  134.8 5.3 %fresh_attend.3 = (bf16[8192,128]{1,0:T(8,128)(2,1)}, bf16[128,512]{1,0:T(8,128)(2,1)}) custom-call(s32[1]{0:T(128)S(6)} %copy.17.length_ref, bf16[8192,128]{1,0:T(8,128)(2,1)S(1)} %bitcast.52, f32[128,4096]{1,0:T(8,128)S(1)} %get-tuple-element.94.acc_ref, f32[8,4096]{1,0:T(8,128)S(1)} %get-tuple-element.95.stat_ref, ...), custom_call_target="tpu_custom_call", output_to_operand_aliasing={{0}: (10, {})} | custom-call | flops 99999997952 | bytes 1 | tf_op jit(solution)/shard_map/fresh_attend/pallas_call | solution.py:506
  (33 shorter events, 0.1 us)
Async XLA Ops:
  0.7 54.7 %copy-start.4 = (s32[3]{0:T(128)S(1)}, s32[3]{0:T(128)}, u32[]{:S(2)}) copy-start(s32[3]{0:T(128)} %pad_add_fusion.place_ref) | copy-start | bytes 40
  0.7 54.7 %copy-start.5 = (bf16[8,128,4,1,256]{4,2,3,1,0:T(4,128)(2,1)S(1)}, bf16[8,128,4,1,256]{4,2,3,1,0:T(4,128)(2,1)}, u32[]{:S(2)}) copy-start(bf16[8,128,4,1,256]{4,2,3,1,0:T(4,128)(2,1)} %param.11) | copy-start | bytes 6291460
  50.2 18.3 %collective-permute-start = (bf16[256,1024]{1,0:T(8,128)(2,1)}, bf16[256,1024]{1,0:T(8,128)(2,1)}, u32[]{:S(2)}, u32[]{:S(2)}) collective-permute-start(bf16[256,1024]{1,0:T(8,128)(2,1)} %get-tuple-element.61), channel_id=1, source_target_pairs={{0,12},{4,8},{8,4},{12,0},{1,13},{5,9},{9,5},{13,1},{2,14},{6,10},... | collective-permute-start | bytes 1572872 | tf_op jit(solution)/shard_map/ppermute | solution.py:105
  55.4 24.6 %collective-permute-start.1 = (bf16[256,1024]{1,0:T(8,128)(2,1)}, bf16[256,1024]{1,0:T(8,128)(2,1)}, u32[]{:S(2)}, u32[]{:S(2)}) collective-permute-start(bf16[256,1024]{1,0:T(8,128)(2,1)} %get-tuple-element.62), channel_id=1, source_target_pairs={{0,4},{4,0},{8,12},{12,8},{1,5},{5,1},{9,13},{13,9},{2,6},{6,2},{1... | collective-permute-start | bytes 1572872 | tf_op jit(solution)/shard_map/ppermute | solution.py:105
  55.4 4.5 %copy-start.6 = (bf16[1,1,1024,4,2,128]{5,4,3,2,1,0:T(2,128)(2,1)S(1)}, bf16[1,1,1024,4,2,128]{5,4,3,2,1,0:T(2,128)(2,1)}, u32[]{:S(2)}) copy-start(bf16[1,1,1024,4,2,128]{5,4,3,2,1,0:T(2,128)(2,1)} %param.8) | copy-start | bytes 6291460
  55.4 4.5 %copy-start.7 = (bf16[1,1,1024,4,2,128]{5,4,3,2,1,0:T(2,128)(2,1)S(1)}, bf16[1,1,1024,4,2,128]{5,4,3,2,1,0:T(2,128)(2,1)}, u32[]{:S(2)}) copy-start(bf16[1,1,1024,4,2,128]{5,4,3,2,1,0:T(2,128)(2,1)} %param.9) | copy-start | bytes 6291460
  58.4 29.3 %collective-permute-start.3 = (bf16[8,128,512]{2,1,0:T(8,128)(2,1)}, bf16[8,128,512]{2,1,0:T(8,128)(2,1)}, u32[]{:S(2)}, u32[]{:S(2)}) collective-permute-start(bf16[8,128,512]{2,1,0:T(8,128)(2,1)} %get-tuple-element.71), channel_id=1, source_target_pairs={{0,2},{2,0},{1,3},{3,1},{4,6},{6,4},{5,7},{7,5},{8,10},{10,8},{9,1... | collective-permute-start | bytes 3145736 | tf_op jit(solution)/shard_map/ppermute | solution.py:101
  62.3 21.0 %copy-start.12 = (bf16[2,2,1024,512]{3,2,1,0:T(8,128)(2,1)}, bf16[2,2,1024,512]{3,2,1,0:T(8,128)(2,1)S(1)}, u32[]{:S(2)}) copy-start(bf16[2,2,1024,512]{3,2,1,0:T(8,128)(2,1)S(1)} %arrange_weights.1.refs_2_) | copy-start | bytes 12582916
  62.3 38.2 %collective-permute-start.4 = (bf16[256,1024]{1,0:T(8,128)(2,1)}, bf16[256,1024]{1,0:T(8,128)(2,1)}, u32[]{:S(2)}, u32[]{:S(2)}) collective-permute-start(bf16[256,1024]{1,0:T(8,128)(2,1)} %get-tuple-element.78), channel_id=1, source_target_pairs={{0,8},{4,12},{8,0},{12,4},{1,9},{5,13},{9,1},{13,5},{2,10},{6,14},... | collective-permute-start | bytes 1572872 | tf_op jit(solution)/shard_map/ppermute | solution.py:105
  83.2 3.4 %collective-permute-start.2 = (bf16[2,512,512]{2,1,0:T(8,128)(2,1)S(1)}, bf16[2,512,512]{2,1,0:T(8,128)(2,1)S(1)}, u32[]{:S(2)}, u32[]{:S(2)}) collective-permute-start(bf16[2,512,512]{2,1,0:T(8,128)(2,1)S(1)} %early_away.1), channel_id=1, source_target_pairs={{0,1},{1,0},{2,3},{3,2},{4,5},{5,4},{6,7},{7,6},{8,9},{9,8},{10,11... | collective-permute-start | bytes 3145736 | tf_op jit(solution)/shard_map/ppermute | solution.py:101
  86.6 6.1 %copy-start = (f32[2,512,512]{2,1,0:T(8,128)}, f32[2,512,512]{2,1,0:T(8,128)S(1)}, u32[]{:S(2)}) copy-start(f32[2,512,512]{2,1,0:T(8,128)S(1)} %early_kept.1.refs_3_.refs_6_) | copy-start | bytes 6291460
  86.6 3.0 %copy-start.11 = (s32[1,8]{1,0:T(1,128)S(1)}, s32[1,8]{1,0:T(1,128)}, u32[]{:S(2)}) copy-start(s32[1,8]{1,0:T(1,128)} %param.12) | copy-start | bytes 100
  86.6 6.0 %copy-start.2 = (bf16[2,512,512]{2,1,0:T(8,128)(2,1)}, bf16[2,512,512]{2,1,0:T(8,128)(2,1)S(1)}, u32[]{:S(2)}) copy-start(bf16[2,512,512]{2,1,0:T(8,128)(2,1)S(1)} %collective-permute-done.2.refs_4_.refs_7_) | copy-start | bytes 3145732
  87.6 12.9 %collective-permute-start.5 = (bf16[256,512]{1,0:T(8,128)(2,1)}, bf16[256,512]{1,0:T(8,128)(2,1)}, u32[]{:S(2)}, u32[]{:S(2)}) collective-permute-start(bf16[256,512]{1,0:T(8,128)(2,1)} %get-tuple-element.80), channel_id=1, source_target_pairs={{0,2},{2,0},{1,3},{3,1},{4,6},{6,4},{5,7},{7,5},{8,10},{10,8},{9,1... | collective-permute-start | bytes 786440 | tf_op jit(solution)/shard_map/ppermute | solution.py:101
  89.0 13.2 %collective-permute-start.6 = (bf16[256,512]{1,0:T(8,128)(2,1)}, bf16[256,512]{1,0:T(8,128)(2,1)}, u32[]{:S(2)}, u32[]{:S(2)}) collective-permute-start(bf16[256,512]{1,0:T(8,128)(2,1)} %get-tuple-element.81), channel_id=1, source_target_pairs={{0,2},{2,0},{1,3},{3,1},{4,6},{6,4},{5,7},{7,5},{8,10},{10,8},{9,1... | collective-permute-start | bytes 786440 | tf_op jit(solution)/shard_map/ppermute | solution.py:101
  89.6 3.1 %copy-start.9 = (bf16[256,2,1,2048]{3,1,2,0:T(2,128)(2,1)S(1)}, bf16[256,2,1,2048]{3,1,2,0:T(2,128)(2,1)}, u32[]{:S(2)}) copy-start(bf16[256,2,1,2048]{3,1,2,0:T(2,128)(2,1)} %param.10) | copy-start | bytes 6291460
  92.7 7.8 %copy-start.14 = (bf16[1024,256]{1,0:T(8,128)(2,1)}, bf16[1024,256]{1,0:T(8,128)(2,1)S(1)}, u32[]{:S(2)}) copy-start(bf16[1024,256]{1,0:T(8,128)(2,1)S(1)} %get-tuple-element.83.keys) | copy-start | bytes 1572868
  92.7 9.5 %copy-start.1 = (f32[2,512,512]{2,1,0:T(8,128)S(1)}, f32[2,512,512]{2,1,0:T(8,128)}, u32[]{:S(2)}) copy-start(f32[2,512,512]{2,1,0:T(8,128)} %copy-done) | copy-start | bytes 6291460
  92.7 9.5 %copy-start.3 = (bf16[2,512,512]{2,1,0:T(8,128)(2,1)S(1)}, bf16[2,512,512]{2,1,0:T(8,128)(2,1)}, u32[]{:S(2)}) copy-start(bf16[2,512,512]{2,1,0:T(8,128)(2,1)} %copy-done.2) | copy-start | bytes 3145732
  92.7 9.5 %copy-start.8 = (bf16[256,4096]{1,0:T(8,128)(2,1)S(1)}, bf16[256,4096]{1,0:T(8,128)(2,1)}, u32[]{:S(2)}) copy-start(bf16[256,4096]{1,0:T(8,128)(2,1)} %refs_1_.3) | copy-start | bytes 6291460
  92.7 9.5 %copy-start.13 = (bf16[2,2,1024,512]{3,2,1,0:T(8,128)(2,1)S(1)}, bf16[2,2,1024,512]{3,2,1,0:T(8,128)(2,1)}, u32[]{:S(2)}) copy-start(bf16[2,2,1024,512]{3,2,1,0:T(8,128)(2,1)} %copy-done.12) | copy-start | bytes 12582916
  105.7 6.8 %copy-start.10 = (bf16[256,2,1,2048]{3,1,2,0:T(2,128)(2,1)S(1)}, bf16[256,2,1,2048]{3,1,2,0:T(2,128)(2,1)}, u32[]{:S(2)}) copy-start(bf16[256,2,1,2048]{3,1,2,0:T(2,128)(2,1)} %param.10) | copy-start | bytes 6291460
  105.7 6.8 %copy-start.15 = (bf16[1024,256]{1,0:T(8,128)(2,1)S(1)}, bf16[1024,256]{1,0:T(8,128)(2,1)}, u32[]{:S(2)}) copy-start(bf16[1024,256]{1,0:T(8,128)(2,1)} %copy-done.14) | copy-start | bytes 1572868
  105.8 5.2 %collective-permute-start.7 = (bf16[2,512,512]{2,1,0:T(8,128)(2,1)S(1)}, bf16[2,512,512]{2,1,0:T(8,128)(2,1)S(1)}, u32[]{:S(2)}, u32[]{:S(2)}) collective-permute-start(bf16[2,512,512]{2,1,0:T(8,128)(2,1)S(1)} %get-tuple-element.82), channel_id=1, source_target_pairs={{0,1},{1,0},{2,3},{3,2},{4,5},{5,4},{6,7},{7,6},{8,9},{9,8},{10,11... | collective-permute-start | bytes 3145736 | tf_op jit(solution)/shard_map/ppermute | solution.py:101
  109.1 9.7 %collective-permute-start.9 = (bf16[256,512]{1,0:T(8,128)(2,1)S(1)}, bf16[256,512]{1,0:T(8,128)(2,1)S(1)}, u32[]{:S(2)}, u32[]{:S(2)}) collective-permute-start(bf16[256,512]{1,0:T(8,128)(2,1)S(1)} %get-tuple-element.85), channel_id=1, source_target_pairs={{0,4},{4,0},{8,12},{12,8},{1,5},{5,1},{9,13},{13,9},{2,6},{6,2},{1... | collective-permute-start | bytes 786440 | tf_op jit(solution)/shard_map/ppermute | solution.py:105
  111.0 7.8 %collective-permute-start.8 = (bf16[128,512]{1,0:T(8,128)(2,1)S(1)}, bf16[128,512]{1,0:T(8,128)(2,1)S(1)}, u32[]{:S(2)}, u32[]{:S(2)}) collective-permute-start(bf16[128,512]{1,0:T(8,128)(2,1)S(1)} %get-tuple-element.111), channel_id=1, source_target_pairs={{0,2},{2,0},{1,3},{3,1},{4,6},{6,4},{5,7},{7,5},{8,10},{10,8},{9,1... | collective-permute-start | bytes 393224 | tf_op jit(solution)/shard_map/ppermute | solution.py:101
  116.5 7.4 %collective-permute-start.10 = (bf16[128,512]{1,0:T(8,128)(2,1)S(1)}, bf16[128,512]{1,0:T(8,128)(2,1)S(1)}, u32[]{:S(2)}, u32[]{:S(2)}) collective-permute-start(bf16[128,512]{1,0:T(8,128)(2,1)S(1)} %get-tuple-element.98), channel_id=1, source_target_pairs={{0,2},{2,0},{1,3},{3,1},{4,6},{6,4},{5,7},{7,5},{8,10},{10,8},{9,1... | collective-permute-start | bytes 393224 | tf_op jit(solution)/shard_map/ppermute | solution.py:101
  117.1 13.0 %collective-permute-start.11 = (bf16[256,512]{1,0:T(8,128)(2,1)S(1)}, bf16[256,512]{1,0:T(8,128)(2,1)S(1)}, u32[]{:S(2)}, u32[]{:S(2)}) collective-permute-start(bf16[256,512]{1,0:T(8,128)(2,1)S(1)} %fusion.5), channel_id=1, source_target_pairs={{0,2},{2,0},{1,3},{3,1},{4,6},{6,4},{5,7},{7,5},{8,10},{10,8},{9,1... | collective-permute-start | bytes 786440 | tf_op jit(solution)/shard_map/ppermute | solution.py:101
  118.6 11.5 %collective-permute-start.12 = (bf16[256,512]{1,0:T(8,128)(2,1)S(1)}, bf16[256,512]{1,0:T(8,128)(2,1)S(1)}, u32[]{:S(2)}, u32[]{:S(2)}) collective-permute-start(bf16[256,512]{1,0:T(8,128)(2,1)S(1)} %get-tuple-element.102), channel_id=1, source_target_pairs={{0,4},{4,0},{8,12},{12,8},{1,5},{5,1},{9,13},{13,9},{2,6},{6,2},{1... | collective-permute-start | bytes 786440 | tf_op jit(solution)/shard_map/ppermute | solution.py:105
  118.8 7.8 %collective-permute-start.13 = (bf16[128,512]{1,0:T(8,128)(2,1)S(1)}, bf16[128,512]{1,0:T(8,128)(2,1)S(1)}, u32[]{:S(2)}, u32[]{:S(2)}) collective-permute-start(bf16[128,512]{1,0:T(8,128)(2,1)S(1)} %fusion.10), channel_id=1, source_target_pairs={{0,8},{4,12},{8,0},{12,4},{1,9},{5,13},{9,1},{13,5},{2,10},{6,14},... | collective-permute-start | bytes 393224 | tf_op jit(solution)/shard_map/ppermute | solution.py:105
  126.7 8.1 %collective-permute-start.14 = (bf16[128,512]{1,0:T(8,128)(2,1)S(1)}, bf16[128,512]{1,0:T(8,128)(2,1)S(1)}, u32[]{:S(2)}, u32[]{:S(2)}) collective-permute-start(bf16[128,512]{1,0:T(8,128)(2,1)S(1)} %fusion.13), channel_id=1, source_target_pairs={{0,8},{4,12},{8,0},{12,4},{1,9},{5,13},{9,1},{13,5},{2,10},{6,14},... | collective-permute-start | bytes 393224 | tf_op jit(solution)/shard_map/ppermute | solution.py:105

commit v12 on v11

--- a/solution.py
+++ b/solution.py
@@ -161,16 +161,20 @@
 
 
 def cut_kernel(bits, place_ref, tokens_ref, *refs):
-    pieces, sems = refs[:-1], refs[-1]
+    pieces, (held, sems) = refs[:-2], refs[-2:]
     depth = pieces[0].shape[1]
-    copies = []
+    inward, outward = [], []
     for index, piece in enumerate(pieces):
         start = pl.multiple_of((place_ref[0] ^ bits[index]) * depth, depth)
         source = tokens_ref.at[:, pl.ds(start, depth)]
-        copies.append(pltpu.make_async_copy(source, piece, sems.at[index]))
-    for copy in copies:
+        inward.append(pltpu.make_async_copy(source, held.at[index], sems.at[0, index]))
+        outward.append(pltpu.make_async_copy(held.at[index], piece, sems.at[1, index]))
+    for copy in inward:
         copy.start()
-    for copy in copies:
+    for copy, onward in zip(inward, outward):
+        copy.wait()
+        onward.start()
+    for copy in outward:
         copy.wait()
 
 
@@ -184,7 +188,10 @@
             grid=(1,),
             in_specs=[far],
             out_specs=[far] * len(bits),
-            scratch_shapes=[pltpu.SemaphoreType.DMA((len(bits),))],
+            scratch_shapes=[
+                pltpu.VMEM((len(bits), *piece.shape), tokens.dtype),
+                pltpu.SemaphoreType.DMA((2, len(bits))),
+            ],
         ),
         out_shape=[piece] * len(bits),
         compiler_params=params(MOST_VMEM_BYTES),

time: 140 us -> 93.8 us (0.67)
  Pallas kernels: 96.8 us -> 50.3 us
    pallas_call x1, Pallas kernels: 49.6 us -> 3.08 us  [cut_tokens(): pl.pallas_call(functools.partial(cut_kernel, bits), grid_spec=pltpu.Prefe...]
  transfers between devices with their start and end apart: 15 -> 15, of which waited for: 4 -> 4; matrix products, arithmetic and copies ran while one was open for 1% -> 1% of each run, Pallas kernels for 27% -> 41%
where the time goes in v12:
time: 93.8 us; the launch traced here: 93.6 us
  Pallas kernels  50.3 us (54%)
  waiting for transfers between devices  20.6 us (22%)
  starting transfers between devices  19.8 us (21%)
  other arithmetic  1.87 us (2%)
  between operations  1.01 us (1%)
    ppermute x7, waiting for transfers between devices, trade(): lax.ppermute(array, axis, [(i, i ^ bits) for i in range(lax.axis_size(axi...  18.8 us
    pallas_call x3, Pallas kernels, prefix_attend(): pl.pallas_call(functools.partial(prefix_kernel, scale, heads), grid=(step...  15.5 us
    pallas_call x4, Pallas kernels, project(): pl.pallas_call(functools.partial(project_kernel, len(blocks), [len(terms)...  13.3 us
    ppermute x7, starting transfers between devices, trade(): lax.ppermute(array, axis, [(i, i ^ bits) for i in range(lax.axis_size(axi...  12.5 us
    pallas_call x2, Pallas kernels, fresh_attend(): pl.pallas_call(functools.partial(fresh_kernel, scale, heads, per_token, c...  10 us
    ppermute x8, starting transfers between devices, shift(): lax.ppermute(array, axis, [(i, (i + step) % count) for i in range(count)])  7.3 us
    pallas_call x1, Pallas kernels, cut_tokens(): pl.pallas_call(functools.partial(cut_kernel, bits), grid_spec=pltpu.Prefe...  3.08 us
    pallas_call x1, Pallas kernels, pick_blocks(): pl.pallas_call(functools.partial(pick_kernel, heads, len(pools)), grid_sp...  3.02 us
  transfers between devices with their start and end apart: 15, of which 4 were waited for; matrix products, arithmetic and copies ran while one was open for 1% of the time, Pallas kernels for 41%

profile of v12, /device:TPU:0, one launch (start us, length us, event | category | flops | bytes accessed | tf_op | source)
XLA Modules:
  0.0 93.6 jit_solution(3857081280209072885)
XLA Ops:
  0.0 0.7 pad_add_fusion.place_ref
  0.7 3.1 %cut_tokens.1 = (bf16[256,1024]{1,0:T(8,128)(2,1)}, bf16[256,1024]{1,0:T(8,128)(2,1)}, bf16[256,1024]{1,0:T(8,128)(2,1)}) custom-call(s32[3]{0:T(128)} %pad_add_fusion.place_ref, bf16[256,4096]{1,0:T(8,128)(2,1)} %refs_1_.3), custom_call_target="tpu_custom_call" | custom-call | flops 99999997952 | bytes 1 | tf_op jit(solution)/shard_map/cut_tokens/pallas_call | solution.py:184
  3.7 5.1 %collective-permute-start = (bf16[256,1024]{1,0:T(8,128)(2,1)}, bf16[256,1024]{1,0:T(8,128)(2,1)}, u32[]{:S(2)}, u32[]{:S(2)}) collective-permute-start(bf16[256,1024]{1,0:T(8,128)(2,1)} %get-tuple-element.61), channel_id=1, source_target_pairs={{0,12},{4,8},{8,4},{12,0},{1,13},{5,9},{9,5},{13,1},{2,14},{6,10},... | collective-permute-start | bytes 1572872 | tf_op jit(solution)/shard_map/ppermute | solution.py:105
  8.9 0.0 collective-permute-start.1
  8.9 0.0 copy-start.6
  8.9 0.0 copy-start.7
  8.9 3.0 %arrange_pool.1 = (bf16[8,128,512]{2,1,0:T(8,128)(2,1)S(1)}, bf16[8,128,512]{2,1,0:T(8,128)(2,1)}) custom-call(s32[3]{0:T(128)S(1)} %copy-done.4, bf16[8,128,8,128]{3,2,1,0:T(8,128)(2,1)S(1)} %bitcast.45), custom_call_target="tpu_custom_call" | custom-call | flops 99999997952 | bytes 1 | tf_op jit(solution)/shard_map/arrange_pool/pallas_call | solution.py:234
  11.9 1.5 %collective-permute-start.3 = (bf16[8,128,512]{2,1,0:T(8,128)(2,1)}, bf16[8,128,512]{2,1,0:T(8,128)(2,1)}, u32[]{:S(2)}, u32[]{:S(2)}) collective-permute-start(bf16[8,128,512]{2,1,0:T(8,128)(2,1)} %get-tuple-element.71), channel_id=1, source_target_pairs={{0,2},{2,0},{1,3},{3,1},{4,6},{6,4},{5,7},{7,5},{8,10},{10,8},{9,1... | collective-permute-start | bytes 3145736 | tf_op jit(solution)/shard_map/ppermute | solution.py:101
  13.4 2.5 %arrange_weights.1.refs_2_ = bf16[2,2,1024,512]{3,2,1,0:T(8,128)(2,1)S(1)} custom-call(bf16[1024,8,128]{2,1,0:T(8,128)(2,1)S(1)} %bitcast.46, bf16[1024,8,128]{2,1,0:T(8,128)(2,1)S(1)} %bitcast.47), custom_call_target="tpu_custom_call" | custom-call | flops 99999997952 | bytes 1 | tf_op jit(solution)/shard_map/arrange_weights/pallas_call | solution.py:150
  15.8 0.8 collective-permute-start.4
  17.4 4.7 %collective-permute-done.refs_0_ = bf16[256,1024]{1,0:T(8,128)(2,1)} collective-permute-done((bf16[256,1024]{1,0:T(8,128)(2,1)}, bf16[256,1024]{1,0:T(8,128)(2,1)}, u32[]{:S(2)}, u32[]{:S(2)}) %collective-permute-start) | collective-permute-done | bytes 524320 | tf_op jit(solution)/shard_map/ppermute | solution.py:105
  22.0 11.5 %collective-permute-done.1.refs_1_ = bf16[256,1024]{1,0:T(8,128)(2,1)} collective-permute-done((bf16[256,1024]{1,0:T(8,128)(2,1)}, bf16[256,1024]{1,0:T(8,128)(2,1)}, u32[]{:S(2)}, u32[]{:S(2)}) %collective-permute-start.1) | collective-permute-done | bytes 524320 | tf_op jit(solution)/shard_map/ppermute | solution.py:105
  33.5 3.3 %early_away.1 = bf16[2,512,512]{2,1,0:T(8,128)(2,1)S(1)} custom-call(s32[3]{0:T(128)S(1)} %copy-done.4, bf16[256,1024]{1,0:T(8,128)(2,1)} %collective-permute-done.refs_0_, bf16[256,1024]{1,0:T(8,128)(2,1)} %collective-permute-done.1.refs_1_, bf16[2,2,1024,512]{3,2,1,0:T(8,128)(2,1)S(1)} %arrange_weights.1.refs_2_), custom_call_target="tpu_custom_call" | custom-call | flops 99999997952 | bytes 1 | tf_op jit(solution)/shard_map/early_away/pallas_call | solution.py:294
  36.8 0.1 collective-permute-start.2
  36.8 3.3 %early_kept.1.refs_3_.refs_6_ = f32[2,512,512]{2,1,0:T(8,128)S(1)} custom-call(s32[3]{0:T(128)S(1)} %copy-done.4, bf16[256,1024]{1,0:T(8,128)(2,1)} %collective-permute-done.refs_0_, bf16[256,1024]{1,0:T(8,128)(2,1)} %collective-permute-done.1.refs_1_, bf16[2,2,1024,512]{3,2,1,0:T(8,128)(2,1)S(1)} %arrange_weights.1.refs_2_), custom_call_target="tpu_custom_call" | custom-call | flops 99999997952 | bytes 1 | tf_op jit(solution)/shard_map/early_kept/pallas_call | solution.py:294
  40.1 0.0 copy-start
  40.1 0.0 copy-start.11
  40.1 0.0 collective-permute-done.2.refs_4_.refs_7_
  40.2 1.0 %fusion.4 = (bf16[256,512]{1,0:T(8,128)(2,1)}, bf16[256,512]{1,0:T(8,128)(2,1)}) fusion(f32[2,512,512]{2,1,0:T(8,128)S(1)} %early_kept.1.refs_3_.refs_6_, bf16[2,512,512]{2,1,0:T(8,128)(2,1)S(1)} %collective-permute-done.2.refs_4_.refs_7_), kind=kLoop, calls=%fused_computation.7 | loop fusion | flops 786432 | bytes 2097152 | tf_op jit(solution)/shard_map/convert_element_type | solution.py:586
  41.1 0.0 collective-permute-done.3.refs_1_
  41.1 1.4 %collective-permute-start.5 = (bf16[256,512]{1,0:T(8,128)(2,1)}, bf16[256,512]{1,0:T(8,128)(2,1)}, u32[]{:S(2)}, u32[]{:S(2)}) collective-permute-start(bf16[256,512]{1,0:T(8,128)(2,1)} %get-tuple-element.80), channel_id=1, source_target_pairs={{0,2},{2,0},{1,3},{3,1},{4,6},{6,4},{5,7},{7,5},{8,10},{10,8},{9,1... | collective-permute-start | bytes 786440 | tf_op jit(solution)/shard_map/ppermute | solution.py:101
  42.5 0.6 collective-permute-start.6
  43.1 3.0 %pick_blocks.1 = (bf16[1024,256]{1,0:T(8,128)(2,1)S(1)}, bf16[288,1024]{1,0:T(8,128)(2,1)S(1)}) custom-call(s32[3]{0:T(128)S(1)} %copy-done.4, s32[8]{0:T(128)S(1)} %bitcast.53, bf16[8,128,512]{2,1,0:T(8,128)(2,1)S(1)} %get-tuple-element.72.refs_0_, bf16[8,128,512]{2,1,0:T(8,128)(2,1)} %collective-permute-done.3.refs_1_), custom_call_target="tpu_custom_call" | custom-call | flops 99999997952 | bytes 1 | tf_op jit(solution)/shard_map/pick_blocks/pallas_call | solution.py:358
  46.2 0.0 copy-start.1
  46.2 0.0 copy-start.8
  46.3 7.7 %prefix_attend.3 = (f32[128,4096]{1,0:T(8,128)S(1)}, f32[8,4096]{1,0:T(8,128)S(1)}) custom-call(bf16[8192,128]{1,0:T(8,128)(2,1)S(1)} %bitcast.48, bf16[1024,256]{1,0:T(8,128)(2,1)S(1)} %get-tuple-element.83.keys, bf16[288,1024]{1,0:T(8,128)(2,1)S(1)} %get-tuple-element.84.values), custom_call_target="tpu_custom_call" | custom-call | flops 99999997952 | bytes 1 | tf_op jit(solution)/shard_map/prefix_attend/pallas_call | solution.py:428
  54.0 0.0 collective-permute-done.5.refs_5_
  54.0 1.7 %collective-permute-done.6.refs_8_ = bf16[256,512]{1,0:T(8,128)(2,1)} collective-permute-done((bf16[256,512]{1,0:T(8,128)(2,1)}, bf16[256,512]{1,0:T(8,128)(2,1)}, u32[]{:S(2)}, u32[]{:S(2)}) %collective-permute-start.6) | collective-permute-done | bytes 262176 | tf_op jit(solution)/shard_map/ppermute | solution.py:101
  55.8 3.5 %late_away.1 = (bf16[2,512,512]{2,1,0:T(8,128)(2,1)S(1)}, bf16[256,512]{1,0:T(8,128)(2,1)S(1)}, bf16[256,512]{1,0:T(8,128)(2,1)S(1)}) custom-call(s32[3]{0:T(128)S(1)} %copy-done.4, bf16[256,1024]{1,0:T(8,128)(2,1)} %collective-permute-done.4.refs_0_, bf16[256,4096]{1,0:T(8,128)(2,1)S(1)} %copy-done.8, bf16[2,2,1024,512]{3,2,1,0:T(8,128)(2,1)S(1)} %copy-done.13, ...), custom_call_target="tpu_custom_call" | custom-call | flops 99999997952 | bytes 1 | tf_op jit(solution)/shard_map/late_away/pallas_call | solution.py:294
  59.2 0.0 copy-start.10
  59.3 0.1 collective-permute-start.7
  59.3 3.3 %late_kept.1.rest_0_.rest_1_ = f32[2,512,512]{2,1,0:T(8,128)S(1)} custom-call(s32[3]{0:T(128)S(1)} %copy-done.4, bf16[256,1024]{1,0:T(8,128)(2,1)} %collective-permute-done.4.refs_0_, bf16[256,4096]{1,0:T(8,128)(2,1)S(1)} %copy-done.8, bf16[2,2,1024,512]{3,2,1,0:T(8,128)(2,1)S(1)} %copy-done.13), custom_call_target="tpu_custom_call" | custom-call | flops 99999997952 | bytes 1 | tf_op jit(solution)/shard_map/late_kept/pallas_call | solution.py:294
  62.6 1.8 %collective-permute-start.9 = (bf16[256,512]{1,0:T(8,128)(2,1)S(1)}, bf16[256,512]{1,0:T(8,128)(2,1)S(1)}, u32[]{:S(2)}, u32[]{:S(2)}) collective-permute-start(bf16[256,512]{1,0:T(8,128)(2,1)S(1)} %get-tuple-element.85), channel_id=1, source_target_pairs={{0,4},{4,0},{8,12},{12,8},{1,5},{5,1},{9,13},{13,9},{2,6},{6,2},{1... | collective-permute-start | bytes 786440 | tf_op jit(solution)/shard_map/ppermute | solution.py:105
  64.4 0.1 fusion.15
  64.5 1.6 %collective-permute-start.8 = (bf16[128,512]{1,0:T(8,128)(2,1)S(1)}, bf16[128,512]{1,0:T(8,128)(2,1)S(1)}, u32[]{:S(2)}, u32[]{:S(2)}) collective-permute-start(bf16[128,512]{1,0:T(8,128)(2,1)S(1)} %get-tuple-element.111), channel_id=1, source_target_pairs={{0,2},{2,0},{1,3},{3,1},{4,6},{6,4},{5,7},{7,5},{8,10},{10,8},{9,1... | collective-permute-start | bytes 393224 | tf_op jit(solution)/shard_map/ppermute | solution.py:101
  66.1 3.9 %prefix_attend.4 = (f32[128,4096]{1,0:T(8,128)S(1)}, f32[8,4096]{1,0:T(8,128)S(1)}) custom-call(bf16[8192,128]{1,0:T(8,128)(2,1)S(1)} %bitcast.49, bf16[1024,256]{1,0:T(8,128)(2,1)S(1)} %copy-done.15, bf16[288,1024]{1,0:T(8,128)(2,1)S(1)} %get-tuple-element.84.values), custom_call_target="tpu_custom_call" | custom-call | flops 99999997952 | bytes 1 | tf_op jit(solution)/shard_map/prefix_attend/pallas_call | solution.py:428
  69.9 0.1 fusion.5
  70.0 0.6 collective-permute-start.10
  70.6 1.5 %collective-permute-start.11 = (bf16[256,512]{1,0:T(8,128)(2,1)S(1)}, bf16[256,512]{1,0:T(8,128)(2,1)S(1)}, u32[]{:S(2)}, u32[]{:S(2)}) collective-permute-start(bf16[256,512]{1,0:T(8,128)(2,1)S(1)} %fusion.5), channel_id=1, source_target_pairs={{0,2},{2,0},{1,3},{3,1},{4,6},{6,4},{5,7},{7,5},{8,10},{10,8},{9,1... | collective-permute-start | bytes 786440 | tf_op jit(solution)/shard_map/ppermute | solution.py:101
  72.1 0.2 collective-permute-start.12
  72.3 0.1 fusion.10
  72.4 1.2 %collective-permute-start.13 = (bf16[128,512]{1,0:T(8,128)(2,1)S(1)}, bf16[128,512]{1,0:T(8,128)(2,1)S(1)}, u32[]{:S(2)}, u32[]{:S(2)}) collective-permute-start(bf16[128,512]{1,0:T(8,128)(2,1)S(1)} %fusion.10), channel_id=1, source_target_pairs={{0,8},{4,12},{8,0},{12,4},{1,9},{5,13},{9,1},{13,5},{2,10},{6,14},... | collective-permute-start | bytes 393224 | tf_op jit(solution)/shard_map/ppermute | solution.py:105
  73.5 3.9 %prefix_attend.5 = (f32[128,4096]{1,0:T(8,128)S(1)}, f32[8,4096]{1,0:T(8,128)S(1)}) custom-call(bf16[8192,128]{1,0:T(8,128)(2,1)S(1)} %bitcast.50, bf16[1024,256]{1,0:T(8,128)(2,1)S(1)} %copy-done.15, bf16[288,1024]{1,0:T(8,128)(2,1)S(1)} %get-tuple-element.84.values, ...), custom_call_target="tpu_custom_call", output_to_operand_aliasing={{0}: (3, {}), {1}: (4, {})} | custom-call | flops 99999997952 | bytes 1 | tf_op jit(solution)/shard_map/prefix_attend/pallas_call | solution.py:428
  77.4 0.1 fusion.13
  77.5 2.7 %collective-permute-done.13.rest_4_ = bf16[128,512]{1,0:T(8,128)(2,1)S(1)} collective-permute-done((bf16[128,512]{1,0:T(8,128)(2,1)S(1)}, bf16[128,512]{1,0:T(8,128)(2,1)S(1)}, u32[]{:S(2)}, u32[]{:S(2)}) %collective-permute-start.13) | collective-permute-done | bytes 131104 | tf_op jit(solution)/shard_map/ppermute | solution.py:105
  80.2 3.4 %collective-permute-start.14 = (bf16[128,512]{1,0:T(8,128)(2,1)S(1)}, bf16[128,512]{1,0:T(8,128)(2,1)S(1)}, u32[]{:S(2)}, u32[]{:S(2)}) collective-permute-start(bf16[128,512]{1,0:T(8,128)(2,1)S(1)} %fusion.13), channel_id=1, source_target_pairs={{0,8},{4,12},{8,0},{12,4},{1,9},{5,13},{9,1},{13,5},{2,10},{6,14},... | collective-permute-start | bytes 393224 | tf_op jit(solution)/shard_map/ppermute | solution.py:105
  83.6 4.7 %fresh_attend.2 = (bf16[8192,128]{1,0:T(8,128)(2,1)}, bf16[128,512]{1,0:T(8,128)(2,1)S(1)}) custom-call(s32[1]{0:T(128)S(6)} %copy.17.length_ref, bf16[8192,128]{1,0:T(8,128)(2,1)S(1)} %bitcast.51, f32[128,4096]{1,0:T(8,128)S(1)} %get-tuple-element.96.acc_ref, f32[8,4096]{1,0:T(8,128)S(1)} %get-tuple-element.97.stat_ref, ...), custom_call_target="tpu_custom_call" | custom-call | flops 99999997952 | bytes 1 | tf_op jit(solution)/shard_map/fresh_attend/pallas_call | solution.py:513
  88.3 5.3 %fresh_attend.3 = (bf16[8192,128]{1,0:T(8,128)(2,1)}, bf16[128,512]{1,0:T(8,128)(2,1)}) custom-call(s32[1]{0:T(128)S(6)} %copy.17.length_ref, bf16[8192,128]{1,0:T(8,128)(2,1)S(1)} %bitcast.52, f32[128,4096]{1,0:T(8,128)S(1)} %get-tuple-element.94.acc_ref, f32[8,4096]{1,0:T(8,128)S(1)} %get-tuple-element.95.stat_ref, ...), custom_call_target="tpu_custom_call", output_to_operand_aliasing={{0}: (10, {})} | custom-call | flops 99999997952 | bytes 1 | tf_op jit(solution)/shard_map/fresh_attend/pallas_call | solution.py:513
  (33 shorter events, 0.1 us)
Async XLA Ops:
  0.7 8.2 %copy-start.4 = (s32[3]{0:T(128)S(1)}, s32[3]{0:T(128)}, u32[]{:S(2)}) copy-start(s32[3]{0:T(128)} %pad_add_fusion.place_ref) | copy-start | bytes 40
  0.7 8.2 %copy-start.5 = (bf16[8,128,4,1,256]{4,2,3,1,0:T(4,128)(2,1)S(1)}, bf16[8,128,4,1,256]{4,2,3,1,0:T(4,128)(2,1)}, u32[]{:S(2)}) copy-start(bf16[8,128,4,1,256]{4,2,3,1,0:T(4,128)(2,1)} %param.11) | copy-start | bytes 6291460
  3.7 18.3 %collective-permute-start = (bf16[256,1024]{1,0:T(8,128)(2,1)}, bf16[256,1024]{1,0:T(8,128)(2,1)}, u32[]{:S(2)}, u32[]{:S(2)}) collective-permute-start(bf16[256,1024]{1,0:T(8,128)(2,1)} %get-tuple-element.61), channel_id=1, source_target_pairs={{0,12},{4,8},{8,4},{12,0},{1,13},{5,9},{9,5},{13,1},{2,14},{6,10},... | collective-permute-start | bytes 1572872 | tf_op jit(solution)/shard_map/ppermute | solution.py:105
  8.9 24.6 %collective-permute-start.1 = (bf16[256,1024]{1,0:T(8,128)(2,1)}, bf16[256,1024]{1,0:T(8,128)(2,1)}, u32[]{:S(2)}, u32[]{:S(2)}) collective-permute-start(bf16[256,1024]{1,0:T(8,128)(2,1)} %get-tuple-element.62), channel_id=1, source_target_pairs={{0,4},{4,0},{8,12},{12,8},{1,5},{5,1},{9,13},{13,9},{2,6},{6,2},{1... | collective-permute-start | bytes 1572872 | tf_op jit(solution)/shard_map/ppermute | solution.py:105
  8.9 4.5 %copy-start.6 = (bf16[1,1,1024,4,2,128]{5,4,3,2,1,0:T(2,128)(2,1)S(1)}, bf16[1,1,1024,4,2,128]{5,4,3,2,1,0:T(2,128)(2,1)}, u32[]{:S(2)}) copy-start(bf16[1,1,1024,4,2,128]{5,4,3,2,1,0:T(2,128)(2,1)} %param.8) | copy-start | bytes 6291460
  8.9 4.5 %copy-start.7 = (bf16[1,1,1024,4,2,128]{5,4,3,2,1,0:T(2,128)(2,1)S(1)}, bf16[1,1,1024,4,2,128]{5,4,3,2,1,0:T(2,128)(2,1)}, u32[]{:S(2)}) copy-start(bf16[1,1,1024,4,2,128]{5,4,3,2,1,0:T(2,128)(2,1)} %param.9) | copy-start | bytes 6291460
  11.9 29.3 %collective-permute-start.3 = (bf16[8,128,512]{2,1,0:T(8,128)(2,1)}, bf16[8,128,512]{2,1,0:T(8,128)(2,1)}, u32[]{:S(2)}, u32[]{:S(2)}) collective-permute-start(bf16[8,128,512]{2,1,0:T(8,128)(2,1)} %get-tuple-element.71), channel_id=1, source_target_pairs={{0,2},{2,0},{1,3},{3,1},{4,6},{6,4},{5,7},{7,5},{8,10},{10,8},{9,1... | collective-permute-start | bytes 3145736 | tf_op jit(solution)/shard_map/ppermute | solution.py:101
  15.8 21.0 %copy-start.12 = (bf16[2,2,1024,512]{3,2,1,0:T(8,128)(2,1)}, bf16[2,2,1024,512]{3,2,1,0:T(8,128)(2,1)S(1)}, u32[]{:S(2)}) copy-start(bf16[2,2,1024,512]{3,2,1,0:T(8,128)(2,1)S(1)} %arrange_weights.1.refs_2_) | copy-start | bytes 12582916
  15.8 38.2 %collective-permute-start.4 = (bf16[256,1024]{1,0:T(8,128)(2,1)}, bf16[256,1024]{1,0:T(8,128)(2,1)}, u32[]{:S(2)}, u32[]{:S(2)}) collective-permute-start(bf16[256,1024]{1,0:T(8,128)(2,1)} %get-tuple-element.78), channel_id=1, source_target_pairs={{0,8},{4,12},{8,0},{12,4},{1,9},{5,13},{9,1},{13,5},{2,10},{6,14},... | collective-permute-start | bytes 1572872 | tf_op jit(solution)/shard_map/ppermute | solution.py:105
  36.8 3.4 %collective-permute-start.2 = (bf16[2,512,512]{2,1,0:T(8,128)(2,1)S(1)}, bf16[2,512,512]{2,1,0:T(8,128)(2,1)S(1)}, u32[]{:S(2)}, u32[]{:S(2)}) collective-permute-start(bf16[2,512,512]{2,1,0:T(8,128)(2,1)S(1)} %early_away.1), channel_id=1, source_target_pairs={{0,1},{1,0},{2,3},{3,2},{4,5},{5,4},{6,7},{7,6},{8,9},{9,8},{10,11... | collective-permute-start | bytes 3145736 | tf_op jit(solution)/shard_map/ppermute | solution.py:101
  40.1 6.1 %copy-start = (f32[2,512,512]{2,1,0:T(8,128)}, f32[2,512,512]{2,1,0:T(8,128)S(1)}, u32[]{:S(2)}) copy-start(f32[2,512,512]{2,1,0:T(8,128)S(1)} %early_kept.1.refs_3_.refs_6_) | copy-start | bytes 6291460
  40.1 3.0 %copy-start.11 = (s32[1,8]{1,0:T(1,128)S(1)}, s32[1,8]{1,0:T(1,128)}, u32[]{:S(2)}) copy-start(s32[1,8]{1,0:T(1,128)} %param.12) | copy-start | bytes 100
  40.2 6.0 %copy-start.2 = (bf16[2,512,512]{2,1,0:T(8,128)(2,1)}, bf16[2,512,512]{2,1,0:T(8,128)(2,1)S(1)}, u32[]{:S(2)}) copy-start(bf16[2,512,512]{2,1,0:T(8,128)(2,1)S(1)} %collective-permute-done.2.refs_4_.refs_7_) | copy-start | bytes 3145732
  41.1 12.9 %collective-permute-start.5 = (bf16[256,512]{1,0:T(8,128)(2,1)}, bf16[256,512]{1,0:T(8,128)(2,1)}, u32[]{:S(2)}, u32[]{:S(2)}) collective-permute-start(bf16[256,512]{1,0:T(8,128)(2,1)} %get-tuple-element.80), channel_id=1, source_target_pairs={{0,2},{2,0},{1,3},{3,1},{4,6},{6,4},{5,7},{7,5},{8,10},{10,8},{9,1... | collective-permute-start | bytes 786440 | tf_op jit(solution)/shard_map/ppermute | solution.py:101
  42.5 13.2 %collective-permute-start.6 = (bf16[256,512]{1,0:T(8,128)(2,1)}, bf16[256,512]{1,0:T(8,128)(2,1)}, u32[]{:S(2)}, u32[]{:S(2)}) collective-permute-start(bf16[256,512]{1,0:T(8,128)(2,1)} %get-tuple-element.81), channel_id=1, source_target_pairs={{0,2},{2,0},{1,3},{3,1},{4,6},{6,4},{5,7},{7,5},{8,10},{10,8},{9,1... | collective-permute-start | bytes 786440 | tf_op jit(solution)/shard_map/ppermute | solution.py:101
  43.1 3.1 %copy-start.9 = (bf16[256,2,1,2048]{3,1,2,0:T(2,128)(2,1)S(1)}, bf16[256,2,1,2048]{3,1,2,0:T(2,128)(2,1)}, u32[]{:S(2)}) copy-start(bf16[256,2,1,2048]{3,1,2,0:T(2,128)(2,1)} %param.10) | copy-start | bytes 6291460
  46.2 7.8 %copy-start.14 = (bf16[1024,256]{1,0:T(8,128)(2,1)}, bf16[1024,256]{1,0:T(8,128)(2,1)S(1)}, u32[]{:S(2)}) copy-start(bf16[1024,256]{1,0:T(8,128)(2,1)S(1)} %get-tuple-element.83.keys) | copy-start | bytes 1572868
  46.2 9.5 %copy-start.1 = (f32[2,512,512]{2,1,0:T(8,128)S(1)}, f32[2,512,512]{2,1,0:T(8,128)}, u32[]{:S(2)}) copy-start(f32[2,512,512]{2,1,0:T(8,128)} %copy-done) | copy-start | bytes 6291460
  46.2 9.5 %copy-start.3 = (bf16[2,512,512]{2,1,0:T(8,128)(2,1)S(1)}, bf16[2,512,512]{2,1,0:T(8,128)(2,1)}, u32[]{:S(2)}) copy-start(bf16[2,512,512]{2,1,0:T(8,128)(2,1)} %copy-done.2) | copy-start | bytes 3145732
  46.2 9.5 %copy-start.8 = (bf16[256,4096]{1,0:T(8,128)(2,1)S(1)}, bf16[256,4096]{1,0:T(8,128)(2,1)}, u32[]{:S(2)}) copy-start(bf16[256,4096]{1,0:T(8,128)(2,1)} %refs_1_.3) | copy-start | bytes 6291460
  46.2 9.5 %copy-start.13 = (bf16[2,2,1024,512]{3,2,1,0:T(8,128)(2,1)S(1)}, bf16[2,2,1024,512]{3,2,1,0:T(8,128)(2,1)}, u32[]{:S(2)}) copy-start(bf16[2,2,1024,512]{3,2,1,0:T(8,128)(2,1)} %copy-done.12) | copy-start | bytes 12582916
  59.2 6.8 %copy-start.10 = (bf16[256,2,1,2048]{3,1,2,0:T(2,128)(2,1)S(1)}, bf16[256,2,1,2048]{3,1,2,0:T(2,128)(2,1)}, u32[]{:S(2)}) copy-start(bf16[256,2,1,2048]{3,1,2,0:T(2,128)(2,1)} %param.10) | copy-start | bytes 6291460
  59.2 6.8 %copy-start.15 = (bf16[1024,256]{1,0:T(8,128)(2,1)S(1)}, bf16[1024,256]{1,0:T(8,128)(2,1)}, u32[]{:S(2)}) copy-start(bf16[1024,256]{1,0:T(8,128)(2,1)} %copy-done.14) | copy-start | bytes 1572868
  59.3 5.2 %collective-permute-start.7 = (bf16[2,512,512]{2,1,0:T(8,128)(2,1)S(1)}, bf16[2,512,512]{2,1,0:T(8,128)(2,1)S(1)}, u32[]{:S(2)}, u32[]{:S(2)}) collective-permute-start(bf16[2,512,512]{2,1,0:T(8,128)(2,1)S(1)} %get-tuple-element.82), channel_id=1, source_target_pairs={{0,1},{1,0},{2,3},{3,2},{4,5},{5,4},{6,7},{7,6},{8,9},{9,8},{10,11... | collective-permute-start | bytes 3145736 | tf_op jit(solution)/shard_map/ppermute | solution.py:101
  62.6 9.7 %collective-permute-start.9 = (bf16[256,512]{1,0:T(8,128)(2,1)S(1)}, bf16[256,512]{1,0:T(8,128)(2,1)S(1)}, u32[]{:S(2)}, u32[]{:S(2)}) collective-permute-start(bf16[256,512]{1,0:T(8,128)(2,1)S(1)} %get-tuple-element.85), channel_id=1, source_target_pairs={{0,4},{4,0},{8,12},{12,8},{1,5},{5,1},{9,13},{13,9},{2,6},{6,2},{1... | collective-permute-start | bytes 786440 | tf_op jit(solution)/shard_map/ppermute | solution.py:105
  64.5 7.8 %collective-permute-start.8 = (bf16[128,512]{1,0:T(8,128)(2,1)S(1)}, bf16[128,512]{1,0:T(8,128)(2,1)S(1)}, u32[]{:S(2)}, u32[]{:S(2)}) collective-permute-start(bf16[128,512]{1,0:T(8,128)(2,1)S(1)} %get-tuple-element.111), channel_id=1, source_target_pairs={{0,2},{2,0},{1,3},{3,1},{4,6},{6,4},{5,7},{7,5},{8,10},{10,8},{9,1... | collective-permute-start | bytes 393224 | tf_op jit(solution)/shard_map/ppermute | solution.py:101
  70.0 7.4 %collective-permute-start.10 = (bf16[128,512]{1,0:T(8,128)(2,1)S(1)}, bf16[128,512]{1,0:T(8,128)(2,1)S(1)}, u32[]{:S(2)}, u32[]{:S(2)}) collective-permute-start(bf16[128,512]{1,0:T(8,128)(2,1)S(1)} %get-tuple-element.98), channel_id=1, source_target_pairs={{0,2},{2,0},{1,3},{3,1},{4,6},{6,4},{5,7},{7,5},{8,10},{10,8},{9,1... | collective-permute-start | bytes 393224 | tf_op jit(solution)/shard_map/ppermute | solution.py:101
  70.6 13.0 %collective-permute-start.11 = (bf16[256,512]{1,0:T(8,128)(2,1)S(1)}, bf16[256,512]{1,0:T(8,128)(2,1)S(1)}, u32[]{:S(2)}, u32[]{:S(2)}) collective-permute-start(bf16[256,512]{1,0:T(8,128)(2,1)S(1)} %fusion.5), channel_id=1, source_target_pairs={{0,2},{2,0},{1,3},{3,1},{4,6},{6,4},{5,7},{7,5},{8,10},{10,8},{9,1... | collective-permute-start | bytes 786440 | tf_op jit(solution)/shard_map/ppermute | solution.py:101
  72.1 11.5 %collective-permute-start.12 = (bf16[256,512]{1,0:T(8,128)(2,1)S(1)}, bf16[256,512]{1,0:T(8,128)(2,1)S(1)}, u32[]{:S(2)}, u32[]{:S(2)}) collective-permute-start(bf16[256,512]{1,0:T(8,128)(2,1)S(1)} %get-tuple-element.102), channel_id=1, source_target_pairs={{0,4},{4,0},{8,12},{12,8},{1,5},{5,1},{9,13},{13,9},{2,6},{6,2},{1... | collective-permute-start | bytes 786440 | tf_op jit(solution)/shard_map/ppermute | solution.py:105
  72.4 7.8 %collective-permute-start.13 = (bf16[128,512]{1,0:T(8,128)(2,1)S(1)}, bf16[128,512]{1,0:T(8,128)(2,1)S(1)}, u32[]{:S(2)}, u32[]{:S(2)}) collective-permute-start(bf16[128,512]{1,0:T(8,128)(2,1)S(1)} %fusion.10), channel_id=1, source_target_pairs={{0,8},{4,12},{8,0},{12,4},{1,9},{5,13},{9,1},{13,5},{2,10},{6,14},... | collective-permute-start | bytes 393224 | tf_op jit(solution)/shard_map/ppermute | solution.py:105
  80.2 8.1 %collective-permute-start.14 = (bf16[128,512]{1,0:T(8,128)(2,1)S(1)}, bf16[128,512]{1,0:T(8,128)(2,1)S(1)}, u32[]{:S(2)}, u32[]{:S(2)}) collective-permute-start(bf16[128,512]{1,0:T(8,128)(2,1)S(1)} %fusion.13), channel_id=1, source_target_pairs={{0,8},{4,12},{8,0},{12,4},{1,9},{5,13},{9,1},{13,5},{2,10},{6,14},... | collective-permute-start | bytes 393224 | tf_op jit(solution)/shard_map/ppermute | solution.py:105

commit v13 on v10

--- a/solution.py
+++ b/solution.py
@@ -11,7 +11,8 @@
 CHUNKS = 2
 PART = 1024
 ONES = 16
-VMEM_BYTES = 24 * 1024 * 1024
+VMEM_BYTES = 16 * 1024 * 1024
+MOST_VMEM_BYTES = 60 * 1024 * 1024
 LONG = pl.CostEstimate(flops=10**11, bytes_accessed=1, transcendentals=0)
 COSTS = {}
 
@@ -121,8 +122,8 @@
     )
 
 
-def params():
-    return pltpu.CompilerParams(vmem_limit_bytes=VMEM_BYTES)
+def params(limit=None):
+    return pltpu.CompilerParams(vmem_limit_bytes=limit or VMEM_BYTES)
 
 
 def weight_kernel(ctx_count, heads, head_count, key_ref, value_ref, out_ref, flat):
@@ -159,36 +160,28 @@
     )(*views)
 
 
-def prepare_kernel(ctx_count, heads, cuts, place_ref, tokens_ref, pool_ref, *refs):
-    pieces, outs = refs[: len(cuts)], refs[len(cuts) : len(cuts) + ctx_count]
-    held_pool, flat, sems, pool_sems = refs[-4:]
+def prepare_kernel(ctx_count, heads, bits, place_ref, tokens_ref, pool_ref, *refs):
+    pieces, outs = refs[: len(bits)], refs[len(bits) : len(bits) + ctx_count]
+    held_tokens, flat, sems = refs[-3:]
+    step_at, last_step = pl.program_id(0), pl.num_programs(0) - 1
     depth = pieces[0].shape[1]
-    step_at = pl.program_id(0)
-    some = outs[0].shape[0]
-    steps = pool_ref.shape[0] // some
-
-    def copies():
-        for index, (bits, first) in enumerate(cuts):
-            start = pl.multiple_of((place_ref[0] ^ bits) * depth, depth)
-            source = tokens_ref.at[pl.ds(first, pieces[index].shape[0]), pl.ds(start, depth)]
-            yield pltpu.make_async_copy(source, pieces[index], sems.at[index])
-
-    def pool_copy(index):
-        here = pl.ds(index * some, some)
-        return pltpu.make_async_copy(pool_ref.at[here], held_pool.at[here], pool_sems.at[index])
+
+    def inward(index):
+        start = pl.multiple_of((place_ref[0] ^ bits[index]) * depth, depth)
+        source = tokens_ref.at[:, pl.ds(start, depth)]
+        return pltpu.make_async_copy(source, held_tokens.at[index], sems.at[0, index])
+
+    def outward(index):
+        return pltpu.make_async_copy(held_tokens.at[index], pieces[index], sems.at[1, index])
 
     @pl.when(step_at == 0)
     def _():
-        for copy in copies():
-            copy.start()
-        for index in range(steps):
-            pool_copy(index).start()
-
-    pool_copy(step_at).wait()
-    _, length, slots, width = pool_ref.shape
+        for index in range(len(bits)):
+            inward(index).start()
+
+    some, length, slots, width = pool_ref.shape
     length *= some
-    block = held_pool[pl.ds(step_at * some, some)]
-    flat[...] = block.astype(jnp.float32).reshape(length * slots, width)
+    flat[...] = pool_ref[...].astype(jnp.float32).reshape(length * slots, width)
     for kind in range(2):
         for head in range(heads):
             at = (kind * heads + head) * width
@@ -205,13 +198,19 @@
                     some, length // some, width
                 )
 
-    @pl.when(step_at == steps - 1)
+    @pl.when(step_at == 0)
     def _():
-        for copy in copies():
-            copy.wait()
-
-
-def prepare(place, tokens, depth, cuts, prefix_pool, ctx_count, heads):
+        for index in range(len(bits)):
+            inward(index).wait()
+            outward(index).start()
+
+    @pl.when(step_at == last_step)
+    def _():
+        for index in range(len(bits)):
+            outward(index).wait()
+
+
+def prepare(place, tokens, depth, bits, prefix_pool, ctx_count, heads):
     blocks, length, all_heads, _, double = prefix_pool.shape
     width = double // 2
     slots = 2 * all_heads
@@ -221,29 +220,30 @@
     some = 2 if blocks % 2 == 0 else 1
     out = pl.BlockSpec((some, length, columns), lambda i, place: (i, 0, 0))
     far = pl.BlockSpec(memory_space=pltpu.HBM)
+    piece = jax.ShapeDtypeStruct((tokens.shape[0], depth), tokens.dtype)
     result = pl.pallas_call(
-        functools.partial(
-            prepare_kernel, ctx_count, heads, [(bits, first) for bits, first, _ in cuts]
-        ),
+        functools.partial(prepare_kernel, ctx_count, heads, bits),
         grid_spec=pltpu.PrefetchScalarGridSpec(
             num_scalar_prefetch=1,
             grid=(blocks // some,),
-            in_specs=[far, far],
-            out_specs=[far] * len(cuts) + [out] * ctx_count,
+            in_specs=[
+                far,
+                pl.BlockSpec((some, length, slots, width), lambda i, place: (i, 0, 0, 0)),
+            ],
+            out_specs=[far] * len(bits) + [out] * ctx_count,
             scratch_shapes=[
-                pltpu.VMEM(view.shape, view.dtype),
+                pltpu.VMEM((len(bits), *piece.shape), tokens.dtype),
                 pltpu.VMEM((some * length * slots, width), jnp.float32),
-                pltpu.SemaphoreType.DMA((len(cuts),)),
-                pltpu.SemaphoreType.DMA((blocks // some,)),
+                pltpu.SemaphoreType.DMA((2, len(bits))),
             ],
         ),
-        out_shape=[jax.ShapeDtypeStruct((rows, depth), tokens.dtype) for _, _, rows in cuts]
+        out_shape=[piece] * len(bits)
         + [jax.ShapeDtypeStruct((blocks, length, columns), jnp.bfloat16)] * ctx_count,
-        compiler_params=params(),
+        compiler_params=params(MOST_VMEM_BYTES),
         cost_estimate=cost("prepare"),
         name="prepare",
     )(place, tokens, view)
-    return result[: len(cuts)], result[len(cuts) :]
+    return result[: len(bits)], result[len(bits) :]
 
 
 def total_of(refs):
@@ -558,9 +558,10 @@
 
     top = batch_count // 2
     steps = list(range(batch_count - 1, top, -1)) + list(range(1, top))
-    cuts = [(bits, 0, token_count) for bits in [*steps, top]]
-    pieces, pools = prepare(place, tokens, depth, cuts, prefix_pool, ctx_count, heads)
-    arrived = [trade(piece, "batch", bits) for piece, (bits, _, _) in zip(pieces, cuts[:-1])]
+    pieces, pools = prepare(
+        place, tokens, depth, [*steps, top], prefix_pool, ctx_count, heads
+    )
+    arrived = [trade(piece, "batch", bits) for piece, bits in zip(pieces, steps)]
     pools, (key_weight, value_weight) = after(pools, (key_weight, value_weight))
     pools = [shift(part, "ctx", step) if step else part for step, part in enumerate(pools)]
 
@@ -589,22 +590,26 @@
     every = slice(None)
     parts_of = [slice(i * rows, (i + 1) * rows) for i in range(CHUNKS)]
 
-    sums = [[], []]
+    keys, values = pick_blocks(place, block_table[0], pools, heads)
+    state = prefix_attend(query_rows, keys, values, 0, scale, heads, (0, 2))
+
+    sums, near = [], []
     if steps:
+        state, arrived = after(state, arrived)
         early = projected(arrived, "early")
-        cuts = [slice(i * token_count, (i + 1) * token_count) for i in range(len(steps))]
-        leaving = [others(early, cut) for cut in cuts]
-        leaving, pools = after(leaving, pools)
+        far_rows, near_rows = slice(0, token_count), slice(token_count, 2 * token_count)
+        far = others(early, far_rows)
+        near = sum(term[:, near_rows].astype(jnp.float32) for term in early)
+        near = near.astype(jnp.bfloat16)
+        (far, near), (keys, values) = after((far, near), (keys, values))
+        far, near = spread(far), [trade(near, "batch", 1)]
         sums = [
-            [
-                [piece_of(t, token_count, i, 0) for t in early]
-                + [piece_of(p, token_count, 0) for p in spread(parts)]
-            ]
-            for i, parts in enumerate(leaving)
+            [piece_of(t, token_count, 0, 0) for t in early]
+            + [piece_of(part, token_count, 0) for part in far]
         ]
-    keys, values = pick_blocks(place, block_table[0], pools, heads)
-    states = [prefix_attend(query_rows, keys, values, 0, scale, heads)]
-    states[0], last = after(states[0], last)
+    states = [prefix_attend(query_rows, keys, values, 0, scale, heads, (1, 2), state)]
+    state = prefix_attend(query_rows, keys, values, 1, scale, heads, (0, 2))
+    (states[0], state), last = after((states[0], state), last)
 
     def late_project(step, dtype, name, sums):
         result = project(place, [last, tokens], weights, step, dtype, name, sums)
@@ -612,20 +617,24 @@
 
     terms = []
     for step in range(1, head_count):
-        term, *far = late_project(step, jnp.bfloat16, "late_away", sums[0] + sums[1] if step == 1 else [])
+        term, *far = late_project(step, jnp.bfloat16, "late_away", sums if step == 1 else [])
         terms.append(shift(term, "head", step))
     kept, *_ = late_project(0, jnp.float32, "late_kept", [])
-    far, near = far[:1], far[1:]
     late = [kept, *terms]
     far = [trade(part, "batch", 1) for part in far]
     own_at = slice(token_count, 2 * token_count)
-    *late_others, own_others = [others(late, here) for here in [*parts_of, own_at]]
+    late_others = [others(late, here) for here in parts_of]
     late_others[0] = spread(late_others[0])
-    late_others[1], (keys, values) = after(late_others[1], (keys, values))
-    state = prefix_attend(query_rows, keys, values, 1, scale, heads, (0, 2))
-    state, (late_others[1], own_others, near) = after(state, (late_others[1], own_others, near))
+    own_others = []
+    for step in range(1, ctx_count):
+        part = added(late, step, own_at) + sum(part[step].astype(jnp.float32) for part in near)
+        own_others.append(part.astype(jnp.bfloat16))
+    (late_others[1], own_others), (keys, values) = after(
+        (late_others[1], own_others), (keys, values)
+    )
+    states.append(prefix_attend(query_rows, keys, values, 1, scale, heads, (1, 2), state))
+    states[1], (late_others[1], own_others) = after(states[1], (late_others[1], own_others))
     late_others[1], own_others = spread(late_others[1]), spread(own_others)
-    near = [trade(part, "batch", 1) for part in near]
 
     away = []
     for chunk, here in enumerate(parts_of):
@@ -634,17 +643,16 @@
         part = part.astype(jnp.bfloat16)
         if chunk == 0:
             (far, late), late_others[1] = after((far, late), late_others[1])
-            part, state = after(part, state)
         else:
             away[-1], part = after(away[-1], part)
         away.append(trade(part, "batch", top))
-    states.append(prefix_attend(query_rows, keys, values, 1, scale, heads, (1, 2), state))
 
     result = None
     fresh = []
     for chunk in range(CHUNKS):
         pieces = [piece_of(t, rows, CHUNKS + chunk, 0) for t in late]
-        pieces += [piece_of(part, rows, chunk) for part in (*own_others, *near)]
+        pieces += [piece_of(part, rows, chunk, 0) for part in near]
+        pieces += [piece_of(part, rows, chunk) for part in own_others]
         pieces.append(piece_of(away[chunk], rows, 0))
         result, new = fresh_attend(
             lengths,

time: 96.8 us -> 105 us (1.085)
  waiting for transfers between devices: 23.3 us -> 30.1 us
  Pallas kernels: 45.1 us -> 50.7 us
  starting transfers between devices: 19.9 us -> 14.5 us
  other arithmetic: 1.74 us -> 3.6 us
  local copies, waits for them, and re-layouts: 5.57 us -> 4.39 us
    ppermute x8 -> x7, waiting for transfers between devices: 0.53 us -> 21.3 us  [shift(): lax.ppermute(array, axis, [(i, (i + step) % count) for i in range(count)])]
    ppermute x7, waiting for transfers between devices: 22.8 us -> 8.83 us  [trade(): lax.ppermute(array, axis, [(i, i ^ bits) for i in range(lax.axis_size(axi...]
    ppermute x7, starting transfers between devices: 12.6 us -> 8.73 us  [trade(): lax.ppermute(array, axis, [(i, i ^ bits) for i in range(lax.axis_size(axi...]
    pallas_call x1, Pallas kernels: 3.26 us -> 6.54 us  [prepare(): pl.pallas_call(functools.partial(prepare_kernel, ctx_count, heads, bits),...]
    pallas_call x4, Pallas kernels: 10.7 us -> 13 us  [project(): pl.pallas_call(functools.partial(project_kernel, len(blocks), [len(terms)...]
    convert_element_type x0 -> x2, other arithmetic: none -> 2.02 us  [the longest x1 1.06 us: reduced_shards(): own_others.append(part.astype(jnp.bfloat16))]
    pallas_call x2, Pallas kernels: 10 us -> 11.7 us  [fresh_attend(): pl.pallas_call(functools.partial(fresh_kernel, scale, heads, per_token, c...]
    ppermute x8 -> x7, starting transfers between devices: 7.36 us -> 5.82 us  [shift(): lax.ppermute(array, axis, [(i, (i + step) % count) for i in range(count)])]
  transfers between devices with their start and end apart: 15 -> 14, of which waited for: 5 -> 5; matrix products, arithmetic and copies ran while one was open for 2% -> 3% of each run, Pallas kernels for 34% -> 36%
where the time goes in v13:
time: 105 us; the launch traced here: 104 us
  Pallas kernels  50.7 us (48%)
  waiting for transfers between devices  30.1 us (29%)
  starting transfers between devices  14.5 us (14%)
  local copies, waits for them, and re-layouts  4.39 us (4%)
  other arithmetic  3.6 us (3%)
    ppermute x7, waiting for transfers between devices, shift(): lax.ppermute(array, axis, [(i, (i + step) % count) for i in range(count)])  21.3 us
    pallas_call x4, Pallas kernels, prefix_attend(): pl.pallas_call(functools.partial(prefix_kernel, scale, heads), grid=(step...  15.5 us
    pallas_call x4, Pallas kernels, project(): pl.pallas_call(functools.partial(project_kernel, len(blocks), [len(terms)...  13 us
    pallas_call x2, Pallas kernels, fresh_attend(): pl.pallas_call(functools.partial(fresh_kernel, scale, heads, per_token, c...  11.7 us
    ppermute x7, waiting for transfers between devices, trade(): lax.ppermute(array, axis, [(i, i ^ bits) for i in range(lax.axis_size(axi...  8.83 us
    ppermute x7, starting transfers between devices, trade(): lax.ppermute(array, axis, [(i, i ^ bits) for i in range(lax.axis_size(axi...  8.73 us
    pallas_call x1, Pallas kernels, prepare(): pl.pallas_call(functools.partial(prepare_kernel, ctx_count, heads, bits),...  6.54 us
    ppermute x7, starting transfers between devices, shift(): lax.ppermute(array, axis, [(i, (i + step) % count) for i in range(count)])  5.82 us
  transfers between devices with their start and end apart: 14, of which 5 were waited for; matrix products, arithmetic and copies ran while one was open for 3% of the time, Pallas kernels for 36%

profile of v13, /device:TPU:0, one launch (start us, length us, event | category | flops | bytes accessed | tf_op | source)
XLA Modules:
  0.0 104.4 jit_solution(1542121478192511271)
XLA Ops:
  0.0 0.6 pad_add_fusion.place_ref
  0.6 6.5 %prepare.1 = (bf16[256,1024]{1,0:T(8,128)(2,1)}, bf16[256,1024]{1,0:T(8,128)(2,1)}, bf16[256,1024]{1,0:T(8,128)(2,1)}, bf16[8,128,512]{2,1,0:T(8,128)(2,1)}, bf16[8,128,512]{2,1,0:T(8,128)(2,1)}) custom-call(s32[3]{0:T(128)} %pad_add_fusion.place_ref, bf16[256,4096]{1,0:T(8,128)(2,1)} %refs_1_.3, bf16[8,128,8,128]{3,2,1,0:T(8,128)(2,1)} %bitcast.52), custom_call_target="tpu_custom_call" | custom-call | flops 99999997952 | bytes 1 | tf_op jit(solution)/shard_map/prepare/pallas_call | solution.py:224
  7.2 5.1 %collective-permute-start.1 = (bf16[256,1024]{1,0:T(8,128)(2,1)}, bf16[256,1024]{1,0:T(8,128)(2,1)}, u32[]{:S(2)}, u32[]{:S(2)}) collective-permute-start(bf16[256,1024]{1,0:T(8,128)(2,1)} %get-tuple-element.66), channel_id=1, source_target_pairs={{0,12},{4,8},{8,4},{12,0},{1,13},{5,9},{9,5},{13,1},{2,14},{6,10},... | collective-permute-start | bytes 1572872 | tf_op jit(solution)/shard_map/ppermute | solution.py:105
  12.3 0.0 collective-permute-start.2
  12.3 1.5 %collective-permute-start = (bf16[8,128,512]{2,1,0:T(8,128)(2,1)}, bf16[8,128,512]{2,1,0:T(8,128)(2,1)S(1)}, u32[]{:S(2)}, u32[]{:S(2)}) collective-permute-start(bf16[8,128,512]{2,1,0:T(8,128)(2,1)} %get-tuple-element.61), channel_id=1, source_target_pairs={{0,2},{2,0},{1,3},{3,1},{4,6},{6,4},{5,7},{7,5},{8,10},{10,8},{9,1... | collective-permute-start | bytes 3145736 | tf_op jit(solution)/shard_map/ppermute | solution.py:101
  13.8 1.6 %copy-done.7 = bf16[1,1,1024,4,2,128]{5,4,3,2,1,0:T(2,128)(2,1)S(1)} copy-done((bf16[1,1,1024,4,2,128]{5,4,3,2,1,0:T(2,128)(2,1)S(1)}, bf16[1,1,1024,4,2,128]{5,4,3,2,1,0:T(2,128)(2,1)}, u32[]{:S(2)}) %copy-start.7) | copy-done | bytes 2097176
  15.4 2.5 %arrange_weights.1.refs_2_ = bf16[2,2,1024,512]{3,2,1,0:T(8,128)(2,1)S(1)} custom-call(bf16[1024,8,128]{2,1,0:T(8,128)(2,1)S(1)} %bitcast.43, bf16[1024,8,128]{2,1,0:T(8,128)(2,1)S(1)} %bitcast.44), custom_call_target="tpu_custom_call" | custom-call | flops 99999997952 | bytes 1 | tf_op jit(solution)/shard_map/arrange_weights/pallas_call | solution.py:150
  17.9 0.8 collective-permute-start.4
  19.4 17.7 %collective-permute-done.refs_1_ = bf16[8,128,512]{2,1,0:T(8,128)(2,1)S(1)} collective-permute-done((bf16[8,128,512]{2,1,0:T(8,128)(2,1)}, bf16[8,128,512]{2,1,0:T(8,128)(2,1)S(1)}, u32[]{:S(2)}, u32[]{:S(2)}) %collective-permute-start) | collective-permute-done | bytes 1048608 | tf_op jit(solution)/shard_map/ppermute | solution.py:101
  37.1 0.0 copy-start.9
  37.1 1.5 %pick_blocks.1 = (bf16[1024,256]{1,0:T(8,128)(2,1)S(1)}, bf16[288,1024]{1,0:T(8,128)(2,1)S(1)}) custom-call(s32[3]{0:T(128)S(1)} %copy-done.4, s32[8]{0:T(128)S(1)} %bitcast.51, bf16[8,128,512]{2,1,0:T(8,128)(2,1)S(1)} %copy-done.16, bf16[8,128,512]{2,1,0:T(8,128)(2,1)S(1)} %collective-permute-done.refs_1_), custom_call_target="tpu_custom_call" | custom-call | flops 99999997952 | bytes 1 | tf_op jit(solution)/shard_map/pick_blocks/pallas_call | solution.py:357
  38.7 0.0 copy-done.9
  38.7 3.9 %prefix_attend.4 = (f32[128,4096]{1,0:T(8,128)S(1)}, f32[8,4096]{1,0:T(8,128)S(1)}) custom-call(bf16[8192,128]{1,0:T(8,128)(2,1)S(1)} %bitcast.45, bf16[1024,256]{1,0:T(8,128)(2,1)S(1)} %get-tuple-element.87.keys, bf16[288,1024]{1,0:T(8,128)(2,1)S(1)} %get-tuple-element.88.values), custom_call_target="tpu_custom_call" | custom-call | flops 99999997952 | bytes 1 | tf_op jit(solution)/shard_map/prefix_attend/pallas_call | solution.py:427
  42.6 0.0 collective-permute-done.1.refs_0_
  42.6 3.3 %early_away.1 = bf16[2,512,512]{2,1,0:T(8,128)(2,1)S(1)} custom-call(s32[3]{0:T(128)S(1)} %copy-done.4, bf16[256,1024]{1,0:T(8,128)(2,1)} %collective-permute-done.1.refs_0_, bf16[256,1024]{1,0:T(8,128)(2,1)} %collective-permute-done.2.refs_1_, bf16[2,2,1024,512]{3,2,1,0:T(8,128)(2,1)S(1)} %arrange_weights.1.refs_2_), custom_call_target="tpu_custom_call" | custom-call | flops 99999997952 | bytes 1 | tf_op jit(solution)/shard_map/early_away/pallas_call | solution.py:293
  45.9 0.1 collective-permute-start.3
  46.0 3.3 %early_kept.1.refs_3_ = f32[2,512,512]{2,1,0:T(8,128)S(1)} custom-call(s32[3]{0:T(128)S(1)} %copy-done.4, bf16[256,1024]{1,0:T(8,128)(2,1)} %collective-permute-done.1.refs_0_, bf16[256,1024]{1,0:T(8,128)(2,1)} %collective-permute-done.2.refs_1_, bf16[2,2,1024,512]{3,2,1,0:T(8,128)(2,1)S(1)} %arrange_weights.1.refs_2_), custom_call_target="tpu_custom_call" | custom-call | flops 99999997952 | bytes 1 | tf_op jit(solution)/shard_map/early_kept/pallas_call | solution.py:293
  49.2 0.0 copy-start.10
  49.3 0.8 fusion.4
  50.0 1.0 fusion
  51.0 1.4 %copy-done = f32[2,512,512]{2,1,0:T(8,128)} copy-done((f32[2,512,512]{2,1,0:T(8,128)}, f32[2,512,512]{2,1,0:T(8,128)S(1)}, u32[]{:S(2)}) %copy-start) | copy-done | bytes 2097176
  52.4 1.5 %collective-permute-start.5 = (bf16[256,512]{1,0:T(8,128)(2,1)}, bf16[256,512]{1,0:T(8,128)(2,1)}, u32[]{:S(2)}, u32[]{:S(2)}) collective-permute-start(bf16[256,512]{1,0:T(8,128)(2,1)} %fusion.4), channel_id=1, source_target_pairs={{0,2},{2,0},{1,3},{3,1},{4,6},{6,4},{5,7},{7,5},{8,10},{10,8},{9,1... | collective-permute-start | bytes 786440 | tf_op jit(solution)/shard_map/ppermute | solution.py:101
  53.9 1.7 %collective-permute-start.7 = (bf16[2,256,512]{2,1,0:T(8,128)(2,1)}, bf16[2,256,512]{2,1,0:T(8,128)(2,1)}, u32[]{:S(2)}, u32[]{:S(2)}) collective-permute-start(bf16[2,256,512]{2,1,0:T(8,128)(2,1)} %fusion), channel_id=1, source_target_pairs={{0,4},{4,0},{8,12},{12,8},{1,5},{5,1},{9,13},{13,9},{2,6},{6,2},{1... | collective-permute-start | bytes 1572872 | tf_op jit(solution)/shard_map/ppermute | solution.py:105
  55.6 3.9 %prefix_attend.6 = (f32[128,4096]{1,0:T(8,128)S(1)}, f32[8,4096]{1,0:T(8,128)S(1)}) custom-call(bf16[8192,128]{1,0:T(8,128)(2,1)S(1)} %bitcast.46, bf16[1024,256]{1,0:T(8,128)(2,1)S(1)} %get-tuple-element.87.keys, bf16[288,1024]{1,0:T(8,128)(2,1)S(1)} %get-tuple-element.88.values), custom_call_target="tpu_custom_call" | custom-call | flops 99999997952 | bytes 1 | tf_op jit(solution)/shard_map/prefix_attend/pallas_call | solution.py:427
  59.5 0.0 copy-start.8
  59.6 3.9 %prefix_attend.5 = (f32[128,4096]{1,0:T(8,128)S(1)}, f32[8,4096]{1,0:T(8,128)S(1)}) custom-call(bf16[8192,128]{1,0:T(8,128)(2,1)S(1)} %bitcast.47, bf16[1024,256]{1,0:T(8,128)(2,1)S(1)} %get-tuple-element.87.keys, bf16[288,1024]{1,0:T(8,128)(2,1)S(1)} %get-tuple-element.88.values, ...), custom_call_target="tpu_custom_call", output_to_operand_aliasing={{0}: (3, {}), {1}: (4, {})} | custom-call | flops 99999997952 | bytes 1 | tf_op jit(solution)/shard_map/prefix_attend/pallas_call | solution.py:427
  63.5 0.0 copy-start.14
  63.5 1.3 %copy-done.14 = f32[128,4096]{1,0:T(8,128)} copy-done((f32[128,4096]{1,0:T(8,128)}, f32[128,4096]{1,0:T(8,128)S(1)}, u32[]{:S(2)}) %copy-start.14) | copy-done | bytes 2097176
  64.8 3.3 %late_away.1 = (bf16[2,512,512]{2,1,0:T(8,128)(2,1)S(1)}, bf16[256,512]{1,0:T(8,128)(2,1)S(1)}) custom-call(s32[3]{0:T(128)S(1)} %copy-done.5, bf16[256,1024]{1,0:T(8,128)(2,1)} %collective-permute-done.4.refs_0_, bf16[256,4096]{1,0:T(8,128)(2,1)S(1)} %copy-done.8, bf16[2,2,1024,512]{3,2,1,0:T(8,128)(2,1)S(1)} %copy-done.13, f32[2,512,512]{2,1,0:T(8,128)S(1)} %copy-done.1, ...), custom_call_target="tpu_custom_call" | custom-call | flops 99999997952 | bytes 1 | tf_op jit(solution)/shard_map/late_away/pallas_call | solution.py:293
  68.1 0.1 collective-permute-start.6
  68.2 3.1 %late_kept.1.rest_0_.rest_1_ = f32[2,512,512]{2,1,0:T(8,128)S(1)} custom-call(s32[3]{0:T(128)S(1)} %copy-done.5, bf16[256,1024]{1,0:T(8,128)(2,1)} %collective-permute-done.4.refs_0_, bf16[256,4096]{1,0:T(8,128)(2,1)S(1)} %copy-done.8, bf16[2,2,1024,512]{3,2,1,0:T(8,128)(2,1)S(1)} %copy-done.13), custom_call_target="tpu_custom_call" | custom-call | flops 99999997952 | bytes 1 | tf_op jit(solution)/shard_map/late_kept/pallas_call | solution.py:293
  71.4 0.4 collective-permute-start.8
  71.8 0.1 fusion.15
  71.8 1.1 %fusion.5 = bf16[256,512]{1,0:T(8,128)(2,1)S(1)} fusion(f32[2,512,512]{2,1,0:T(8,128)S(1)} %late_kept.1.rest_0_.rest_1_, bf16[2,256,512]{2,1,0:T(8,128)(2,1)} %collective-permute-done.7.rest_2_.rest_3_, bf16[2,512,512]{2,1,0:T(8,128)(2,1)S(1)} %collective-permute-done.6.rest_1_.rest_2_), kind=kLoop, calls=%fused_computation.8 | loop fusion | flops 655360 | bytes 1310720 | tf_op jit(solution)/shard_map/convert_element_type | solution.py:631
  72.9 0.0 copy-start.15
  72.9 0.6 collective-permute-start.11
  73.5 3.9 %prefix_attend.7 = (f32[128,4096]{1,0:T(8,128)S(1)}, f32[8,4096]{1,0:T(8,128)S(1)}) custom-call(bf16[8192,128]{1,0:T(8,128)(2,1)S(1)} %bitcast.48, bf16[1024,256]{1,0:T(8,128)(2,1)S(1)} %copy-done.20, bf16[288,1024]{1,0:T(8,128)(2,1)S(1)} %copy-done.18, f32[128,4096]{1,0:T(8,128)S(1)} %get-tuple-element.89.refs_0_, ...), custom_call_target="tpu_custom_call", output_to_operand_aliasing={{0}: (3, {}), {1}: (4, {})} | custom-call | flops 99999997952 | bytes 1 | tf_op jit(solution)/shard_map/prefix_attend/pallas_call | solution.py:427
  77.4 1.6 %collective-permute-start.9 = (bf16[128,512]{1,0:T(8,128)(2,1)S(1)}, bf16[128,512]{1,0:T(8,128)(2,1)S(1)}, u32[]{:S(2)}, u32[]{:S(2)}) collective-permute-start(bf16[128,512]{1,0:T(8,128)(2,1)S(1)} %get-tuple-element.100), channel_id=1, source_target_pairs={{0,2},{2,0},{1,3},{3,1},{4,6},{6,4},{5,7},{7,5},{8,10},{10,8},{9,1... | collective-permute-start | bytes 393224 | tf_op jit(solution)/shard_map/ppermute | solution.py:101
  78.9 0.5 collective-permute-start.10
  79.5 0.7 collective-permute-done.8
  80.2 0.1 fusion.10
  80.2 3.6 %collective-permute-done.9 = bf16[128,512]{1,0:T(8,128)(2,1)S(1)} collective-permute-done((bf16[128,512]{1,0:T(8,128)(2,1)S(1)}, bf16[128,512]{1,0:T(8,128)(2,1)S(1)}, u32[]{:S(2)}, u32[]{:S(2)}) %collective-permute-start.9) | collective-permute-done | bytes 131104 | tf_op jit(solution)/shard_map/ppermute | solution.py:101
  83.8 0.7 collective-permute-start.12
  84.5 0.1 fusion.13
  84.5 6.7 %collective-permute-done.12.rest_4_ = bf16[128,512]{1,0:T(8,128)(2,1)S(1)} collective-permute-done((bf16[128,512]{1,0:T(8,128)(2,1)S(1)}, bf16[128,512]{1,0:T(8,128)(2,1)S(1)}, u32[]{:S(2)}, u32[]{:S(2)}) %collective-permute-start.12) | collective-permute-done | bytes 131104 | tf_op jit(solution)/shard_map/ppermute | solution.py:105
  91.3 5.6 %fresh_attend.2 = (bf16[8192,128]{1,0:T(8,128)(2,1)}, bf16[128,512]{1,0:T(8,128)(2,1)S(1)}) custom-call(s32[1]{0:T(128)S(6)} %copy.21.length_ref, bf16[8192,128]{1,0:T(8,128)(2,1)S(1)} %bitcast.49, f32[128,4096]{1,0:T(8,128)S(1)} %copy-done.15, f32[8,4096]{1,0:T(8,128)S(1)} %get-tuple-element.98.stat_ref, f32[2,512,512]{2,1,0:T(8,128)S(1)} %late_kept.1.rest_0_.rest_1_, ...), custom_call_target="tpu_custom_call" | custom-call | flops 99999997952 | bytes 1 | tf_op jit(solution)/shard_map/fresh_attend/pallas_call | solution.py:512
  96.8 1.4 %collective-permute-done.13.rest_5_ = bf16[128,512]{1,0:T(8,128)(2,1)S(1)} collective-permute-done((bf16[128,512]{1,0:T(8,128)(2,1)S(1)}, bf16[128,512]{1,0:T(8,128)(2,1)S(1)}, u32[]{:S(2)}, u32[]{:S(2)}) %collective-permute-start.13) | collective-permute-done | bytes 131104 | tf_op jit(solution)/shard_map/ppermute | solution.py:105
  98.3 6.2 %fresh_attend.3 = (bf16[8192,128]{1,0:T(8,128)(2,1)}, bf16[128,512]{1,0:T(8,128)(2,1)}) custom-call(s32[1]{0:T(128)S(6)} %copy.21.length_ref, bf16[8192,128]{1,0:T(8,128)(2,1)S(1)} %bitcast.50, f32[128,4096]{1,0:T(8,128)S(1)} %get-tuple-element.95.acc_ref, f32[8,4096]{1,0:T(8,128)S(1)} %get-tuple-element.96.stat_ref, ...), custom_call_target="tpu_custom_call", output_to_operand_aliasing={{0}: (10, {})} | custom-call | flops 99999997952 | bytes 1 | tf_op jit(solution)/shard_map/fresh_attend/pallas_call | solution.py:512
  (42 shorter events, 0.1 us)
Async XLA Ops:
  0.6 13.2 %copy-start.6 = (bf16[1,1,1024,4,2,128]{5,4,3,2,1,0:T(2,128)(2,1)S(1)}, bf16[1,1,1024,4,2,128]{5,4,3,2,1,0:T(2,128)(2,1)}, u32[]{:S(2)}) copy-start(bf16[1,1,1024,4,2,128]{5,4,3,2,1,0:T(2,128)(2,1)} %param.8) | copy-start | bytes 6291460
  7.2 35.4 %collective-permute-start.1 = (bf16[256,1024]{1,0:T(8,128)(2,1)}, bf16[256,1024]{1,0:T(8,128)(2,1)}, u32[]{:S(2)}, u32[]{:S(2)}) collective-permute-start(bf16[256,1024]{1,0:T(8,128)(2,1)} %get-tuple-element.66), channel_id=1, source_target_pairs={{0,12},{4,8},{8,4},{12,0},{1,13},{5,9},{9,5},{13,1},{2,14},{6,10},... | collective-permute-start | bytes 1572872 | tf_op jit(solution)/shard_map/ppermute | solution.py:105
  12.3 30.3 %collective-permute-start.2 = (bf16[256,1024]{1,0:T(8,128)(2,1)}, bf16[256,1024]{1,0:T(8,128)(2,1)}, u32[]{:S(2)}, u32[]{:S(2)}) collective-permute-start(bf16[256,1024]{1,0:T(8,128)(2,1)} %get-tuple-element.67), channel_id=1, source_target_pairs={{0,4},{4,0},{8,12},{12,8},{1,5},{5,1},{9,13},{13,9},{2,6},{6,2},{1... | collective-permute-start | bytes 1572872 | tf_op jit(solution)/shard_map/ppermute | solution.py:105
  12.3 24.8 %collective-permute-start = (bf16[8,128,512]{2,1,0:T(8,128)(2,1)}, bf16[8,128,512]{2,1,0:T(8,128)(2,1)S(1)}, u32[]{:S(2)}, u32[]{:S(2)}) collective-permute-start(bf16[8,128,512]{2,1,0:T(8,128)(2,1)} %get-tuple-element.61), channel_id=1, source_target_pairs={{0,2},{2,0},{1,3},{3,1},{4,6},{6,4},{5,7},{7,5},{8,10},{10,8},{9,1... | collective-permute-start | bytes 3145736 | tf_op jit(solution)/shard_map/ppermute | solution.py:101
  13.8 1.6 %copy-start.7 = (bf16[1,1,1024,4,2,128]{5,4,3,2,1,0:T(2,128)(2,1)S(1)}, bf16[1,1,1024,4,2,128]{5,4,3,2,1,0:T(2,128)(2,1)}, u32[]{:S(2)}) copy-start(bf16[1,1,1024,4,2,128]{5,4,3,2,1,0:T(2,128)(2,1)} %param.9) | copy-start | bytes 6291460
  15.4 21.7 %copy-start.4 = (s32[3]{0:T(128)S(1)}, s32[3]{0:T(128)}, u32[]{:S(2)}) copy-start(s32[3]{0:T(128)} %pad_add_fusion.place_ref) | copy-start | bytes 40
  15.4 21.7 %copy-start.11 = (s32[1,8]{1,0:T(1,128)S(1)}, s32[1,8]{1,0:T(1,128)}, u32[]{:S(2)}) copy-start(s32[1,8]{1,0:T(1,128)} %param.12) | copy-start | bytes 100
  15.4 21.7 %copy-start.16 = (bf16[8,128,512]{2,1,0:T(8,128)(2,1)S(1)}, bf16[8,128,512]{2,1,0:T(8,128)(2,1)}, u32[]{:S(2)}) copy-start(bf16[8,128,512]{2,1,0:T(8,128)(2,1)} %get-tuple-element.60.refs_0_) | copy-start | bytes 3145732
  17.8 28.1 %copy-start.12 = (bf16[2,2,1024,512]{3,2,1,0:T(8,128)(2,1)}, bf16[2,2,1024,512]{3,2,1,0:T(8,128)(2,1)S(1)}, u32[]{:S(2)}) copy-start(bf16[2,2,1024,512]{3,2,1,0:T(8,128)(2,1)S(1)} %arrange_weights.1.refs_2_) | copy-start | bytes 12582916
  17.9 46.9 %collective-permute-start.4 = (bf16[256,1024]{1,0:T(8,128)(2,1)}, bf16[256,1024]{1,0:T(8,128)(2,1)}, u32[]{:S(2)}, u32[]{:S(2)}) collective-permute-start(bf16[256,1024]{1,0:T(8,128)(2,1)} %get-tuple-element.82), channel_id=1, source_target_pairs={{0,8},{4,12},{8,0},{12,4},{1,9},{5,13},{9,1},{13,5},{2,10},{6,14},... | collective-permute-start | bytes 1572872 | tf_op jit(solution)/shard_map/ppermute | solution.py:105
  37.1 1.6 %copy-start.9 = (bf16[256,2,1,2048]{3,1,2,0:T(2,128)(2,1)S(1)}, bf16[256,2,1,2048]{3,1,2,0:T(2,128)(2,1)}, u32[]{:S(2)}) copy-start(bf16[256,2,1,2048]{3,1,2,0:T(2,128)(2,1)} %param.10) | copy-start | bytes 6291460
  38.7 20.8 %copy-start.17 = (bf16[288,1024]{1,0:T(8,128)(2,1)}, bf16[288,1024]{1,0:T(8,128)(2,1)S(1)}, u32[]{:S(2)}) copy-start(bf16[288,1024]{1,0:T(8,128)(2,1)S(1)} %get-tuple-element.88.values) | copy-start | bytes 1769476
  38.7 20.8 %copy-start.19 = (bf16[1024,256]{1,0:T(8,128)(2,1)}, bf16[1024,256]{1,0:T(8,128)(2,1)S(1)}, u32[]{:S(2)}) copy-start(bf16[1024,256]{1,0:T(8,128)(2,1)S(1)} %get-tuple-element.87.keys) | copy-start | bytes 1572868
  45.9 3.4 %collective-permute-start.3 = (bf16[2,512,512]{2,1,0:T(8,128)(2,1)S(1)}, bf16[2,512,512]{2,1,0:T(8,128)(2,1)S(1)}, u32[]{:S(2)}, u32[]{:S(2)}) collective-permute-start(bf16[2,512,512]{2,1,0:T(8,128)(2,1)S(1)} %early_away.1), channel_id=1, source_target_pairs={{0,1},{1,0},{2,3},{3,2},{4,5},{5,4},{6,7},{7,6},{8,9},{9,8},{10,11... | collective-permute-start | bytes 3145736 | tf_op jit(solution)/shard_map/ppermute | solution.py:101
  49.2 6.4 %copy-start.10 = (bf16[256,2,1,2048]{3,1,2,0:T(2,128)(2,1)S(1)}, bf16[256,2,1,2048]{3,1,2,0:T(2,128)(2,1)}, u32[]{:S(2)}) copy-start(bf16[256,2,1,2048]{3,1,2,0:T(2,128)(2,1)} %param.10) | copy-start | bytes 6291460
  49.3 6.4 %copy-start.2 = (bf16[2,512,512]{2,1,0:T(8,128)(2,1)}, bf16[2,512,512]{2,1,0:T(8,128)(2,1)S(1)}, u32[]{:S(2)}) copy-start(bf16[2,512,512]{2,1,0:T(8,128)(2,1)S(1)} %collective-permute-done.3.refs_4_) | copy-start | bytes 3145732
  51.0 1.4 %copy-start = (f32[2,512,512]{2,1,0:T(8,128)}, f32[2,512,512]{2,1,0:T(8,128)S(1)}, u32[]{:S(2)}) copy-start(f32[2,512,512]{2,1,0:T(8,128)S(1)} %early_kept.1.refs_3_) | copy-start | bytes 6291460
  52.4 12.4 %collective-permute-start.5 = (bf16[256,512]{1,0:T(8,128)(2,1)}, bf16[256,512]{1,0:T(8,128)(2,1)}, u32[]{:S(2)}, u32[]{:S(2)}) collective-permute-start(bf16[256,512]{1,0:T(8,128)(2,1)} %fusion.4), channel_id=1, source_target_pairs={{0,2},{2,0},{1,3},{3,1},{4,6},{6,4},{5,7},{7,5},{8,10},{10,8},{9,1... | collective-permute-start | bytes 786440 | tf_op jit(solution)/shard_map/ppermute | solution.py:101
  53.9 17.9 %collective-permute-start.7 = (bf16[2,256,512]{2,1,0:T(8,128)(2,1)}, bf16[2,256,512]{2,1,0:T(8,128)(2,1)}, u32[]{:S(2)}, u32[]{:S(2)}) collective-permute-start(bf16[2,256,512]{2,1,0:T(8,128)(2,1)} %fusion), channel_id=1, source_target_pairs={{0,4},{4,0},{8,12},{12,8},{1,5},{5,1},{9,13},{13,9},{2,6},{6,2},{1... | collective-permute-start | bytes 1572872 | tf_op jit(solution)/shard_map/ppermute | solution.py:105
  59.5 5.3 %copy-start.1 = (f32[2,512,512]{2,1,0:T(8,128)S(1)}, f32[2,512,512]{2,1,0:T(8,128)}, u32[]{:S(2)}) copy-start(f32[2,512,512]{2,1,0:T(8,128)} %copy-done) | copy-start | bytes 6291460
  59.5 5.3 %copy-start.3 = (bf16[2,512,512]{2,1,0:T(8,128)(2,1)S(1)}, bf16[2,512,512]{2,1,0:T(8,128)(2,1)}, u32[]{:S(2)}) copy-start(bf16[2,512,512]{2,1,0:T(8,128)(2,1)} %copy-done.2) | copy-start | bytes 3145732
  59.5 5.3 %copy-start.5 = (s32[3]{0:T(128)S(1)}, s32[3]{0:T(128)}, u32[]{:S(2)}) copy-start(s32[3]{0:T(128)} %pad_add_fusion.place_ref) | copy-start | bytes 40
  59.5 5.3 %copy-start.8 = (bf16[256,4096]{1,0:T(8,128)(2,1)S(1)}, bf16[256,4096]{1,0:T(8,128)(2,1)}, u32[]{:S(2)}) copy-start(bf16[256,4096]{1,0:T(8,128)(2,1)} %refs_1_.3) | copy-start | bytes 6291460
  59.6 5.3 %copy-start.13 = (bf16[2,2,1024,512]{3,2,1,0:T(8,128)(2,1)S(1)}, bf16[2,2,1024,512]{3,2,1,0:T(8,128)(2,1)}, u32[]{:S(2)}) copy-start(bf16[2,2,1024,512]{3,2,1,0:T(8,128)(2,1)} %copy-done.12) | copy-start | bytes 12582916
  63.5 1.3 %copy-start.14 = (f32[128,4096]{1,0:T(8,128)}, f32[128,4096]{1,0:T(8,128)S(1)}, u32[]{:S(2)}) copy-start(f32[128,4096]{1,0:T(8,128)S(1)} %get-tuple-element.97.acc_ref) | copy-start | bytes 6291460
  68.1 3.6 %collective-permute-start.6 = (bf16[2,512,512]{2,1,0:T(8,128)(2,1)S(1)}, bf16[2,512,512]{2,1,0:T(8,128)(2,1)S(1)}, u32[]{:S(2)}, u32[]{:S(2)}) collective-permute-start(bf16[2,512,512]{2,1,0:T(8,128)(2,1)S(1)} %get-tuple-element.85), channel_id=1, source_target_pairs={{0,1},{1,0},{2,3},{3,2},{4,5},{5,4},{6,7},{7,6},{8,9},{9,8},{10,11... | collective-permute-start | bytes 3145736 | tf_op jit(solution)/shard_map/ppermute | solution.py:101
  71.4 2.1 %copy-start.18 = (bf16[288,1024]{1,0:T(8,128)(2,1)S(1)}, bf16[288,1024]{1,0:T(8,128)(2,1)}, u32[]{:S(2)}) copy-start(bf16[288,1024]{1,0:T(8,128)(2,1)} %copy-done.17) | copy-start | bytes 1769476
  71.4 2.1 %copy-start.20 = (bf16[1024,256]{1,0:T(8,128)(2,1)S(1)}, bf16[1024,256]{1,0:T(8,128)(2,1)}, u32[]{:S(2)}) copy-start(bf16[1024,256]{1,0:T(8,128)(2,1)} %copy-done.19) | copy-start | bytes 1572868
  71.4 8.8 %collective-permute-start.8 = (bf16[256,512]{1,0:T(8,128)(2,1)S(1)}, bf16[256,512]{1,0:T(8,128)(2,1)S(1)}, u32[]{:S(2)}, u32[]{:S(2)}) collective-permute-start(bf16[256,512]{1,0:T(8,128)(2,1)S(1)} %get-tuple-element.99), channel_id=1, source_target_pairs={{0,4},{4,0},{8,12},{12,8},{1,5},{5,1},{9,13},{13,9},{2,6},{6,2},{1... | collective-permute-start | bytes 786440 | tf_op jit(solution)/shard_map/ppermute | solution.py:105
  72.9 18.4 %copy-start.15 = (f32[128,4096]{1,0:T(8,128)S(1)}, f32[128,4096]{1,0:T(8,128)}, u32[]{:S(2)}) copy-start(f32[128,4096]{1,0:T(8,128)} %copy-done.14) | copy-start | bytes 6291460
  72.9 7.3 %collective-permute-start.11 = (bf16[128,512]{1,0:T(8,128)(2,1)S(1)}, bf16[128,512]{1,0:T(8,128)(2,1)S(1)}, u32[]{:S(2)}, u32[]{:S(2)}) collective-permute-start(bf16[128,512]{1,0:T(8,128)(2,1)S(1)} %get-tuple-element.111), channel_id=1, source_target_pairs={{0,2},{2,0},{1,3},{3,1},{4,6},{6,4},{5,7},{7,5},{8,10},{10,8},{9,1... | collective-permute-start | bytes 393224 | tf_op jit(solution)/shard_map/ppermute | solution.py:101
  77.4 6.4 %collective-permute-start.9 = (bf16[128,512]{1,0:T(8,128)(2,1)S(1)}, bf16[128,512]{1,0:T(8,128)(2,1)S(1)}, u32[]{:S(2)}, u32[]{:S(2)}) collective-permute-start(bf16[128,512]{1,0:T(8,128)(2,1)S(1)} %get-tuple-element.100), channel_id=1, source_target_pairs={{0,2},{2,0},{1,3},{3,1},{4,6},{6,4},{5,7},{7,5},{8,10},{10,8},{9,1... | collective-permute-start | bytes 393224 | tf_op jit(solution)/shard_map/ppermute | solution.py:101
  78.9 12.3 %collective-permute-start.10 = (bf16[256,512]{1,0:T(8,128)(2,1)S(1)}, bf16[256,512]{1,0:T(8,128)(2,1)S(1)}, u32[]{:S(2)}, u32[]{:S(2)}) collective-permute-start(bf16[256,512]{1,0:T(8,128)(2,1)S(1)} %fusion.5), channel_id=1, source_target_pairs={{0,2},{2,0},{1,3},{3,1},{4,6},{6,4},{5,7},{7,5},{8,10},{10,8},{9,1... | collective-permute-start | bytes 786440 | tf_op jit(solution)/shard_map/ppermute | solution.py:101
  83.8 7.4 %collective-permute-start.12 = (bf16[128,512]{1,0:T(8,128)(2,1)S(1)}, bf16[128,512]{1,0:T(8,128)(2,1)S(1)}, u32[]{:S(2)}, u32[]{:S(2)}) collective-permute-start(bf16[128,512]{1,0:T(8,128)(2,1)S(1)} %fusion.10), channel_id=1, source_target_pairs={{0,8},{4,12},{8,0},{12,4},{1,9},{5,13},{9,1},{13,5},{2,10},{6,14},... | collective-permute-start | bytes 393224 | tf_op jit(solution)/shard_map/ppermute | solution.py:105
  91.2 7.0 %collective-permute-start.13 = (bf16[128,512]{1,0:T(8,128)(2,1)S(1)}, bf16[128,512]{1,0:T(8,128)(2,1)S(1)}, u32[]{:S(2)}, u32[]{:S(2)}) collective-permute-start(bf16[128,512]{1,0:T(8,128)(2,1)S(1)} %fusion.13), channel_id=1, source_target_pairs={{0,8},{4,12},{8,0},{12,4},{1,9},{5,13},{9,1},{13,5},{2,10},{6,14},... | collective-permute-start | bytes 393224 | tf_op jit(solution)/shard_map/ppermute | solution.py:105

commit v14 on v12

--- a/solution.py
+++ b/solution.py
@@ -559,7 +559,7 @@
 
     top = batch_count // 2
     steps = list(range(batch_count - 1, top, -1)) + list(range(1, top))
-    pieces = cut_tokens(place, tokens, depth, [*steps, top])
+    pieces = cut_tokens(place, tokens, depth, steps)
     pieces, prefix_pool = after(pieces, prefix_pool)
     arrived = [trade(piece, "batch", bits) for piece, bits in zip(pieces, steps)]
     pools = arrange_pool(place, prefix_pool, ctx_count, heads)
@@ -567,7 +567,8 @@
     pools = [shift(part, "ctx", step) if step else part for step, part in enumerate(pools)]
 
     weights = arrange_weights(key_weight, value_weight, ctx_count, heads, head_count)
-    weights, last = after(weights, pieces[-1])
+    weights, late_tokens = after(weights, tokens)
+    (last,) = cut_tokens(place, late_tokens, depth, [top])
     last = trade(last, "batch", top)
 
     query_rows = queries.reshape(token_count, heads, group, width)
@@ -591,22 +592,22 @@
     every = slice(None)
     parts_of = [slice(i * rows, (i + 1) * rows) for i in range(CHUNKS)]
 
-    sums = [[], []]
+    sums, near = [], []
     if steps:
         early = projected(arrived, "early")
-        cuts = [slice(i * token_count, (i + 1) * token_count) for i in range(len(steps))]
-        leaving = [others(early, cut) for cut in cuts]
-        leaving, pools = after(leaving, pools)
+        far_rows, near_rows = slice(0, token_count), slice(token_count, 2 * token_count)
+        far = others(early, far_rows)
+        near = sum(term[:, near_rows].astype(jnp.float32) for term in early)
+        near = near.astype(jnp.bfloat16)
+        far, pools = after(far, pools)
+        far, near = spread(far), [trade(near, "batch", 1)]
         sums = [
-            [
-                [piece_of(t, token_count, i, 0) for t in early]
-                + [piece_of(p, token_count, 0) for p in spread(parts)]
-            ]
-            for i, parts in enumerate(leaving)
+            [piece_of(t, token_count, 0, 0) for t in early]
+            + [piece_of(part, token_count, 0) for part in far]
         ]
     keys, values = pick_blocks(place, block_table[0], pools, heads)
-    states = [prefix_attend(query_rows, keys, values, 0, scale, heads)]
-    states[0], last = after(states[0], last)
+    state = prefix_attend(query_rows, keys, values, 0, scale, heads, (0, 2))
+    state, last = after(state, last)
 
     def late_project(step, dtype, name, sums):
         result = project(place, [last, tokens], weights, step, dtype, name, sums)
@@ -614,20 +615,24 @@
 
     terms = []
     for step in range(1, head_count):
-        term, *far = late_project(step, jnp.bfloat16, "late_away", sums[0] + sums[1] if step == 1 else [])
+        term, *far = late_project(step, jnp.bfloat16, "late_away", sums if step == 1 else [])
         terms.append(shift(term, "head", step))
     kept, *_ = late_project(0, jnp.float32, "late_kept", [])
-    far, near = far[:1], far[1:]
     late = [kept, *terms]
     far = [trade(part, "batch", 1) for part in far]
     own_at = slice(token_count, 2 * token_count)
-    *late_others, own_others = [others(late, here) for here in [*parts_of, own_at]]
+    late_others = [others(late, here) for here in parts_of]
     late_others[0] = spread(late_others[0])
-    late_others[1], (keys, values) = after(late_others[1], (keys, values))
-    state = prefix_attend(query_rows, keys, values, 1, scale, heads, (0, 2))
-    state, (late_others[1], own_others, near) = after(state, (late_others[1], own_others, near))
+    own_others = []
+    for step in range(1, ctx_count):
+        part = added(late, step, own_at) + sum(part[step].astype(jnp.float32) for part in near)
+        own_others.append(part.astype(jnp.bfloat16))
+    (late_others[1], own_others), (keys, values) = after(
+        (late_others[1], own_others), (keys, values)
+    )
+    states = [prefix_attend(query_rows, keys, values, 0, scale, heads, (1, 2), state)]
+    states[0], (late_others[1], own_others) = after(states[0], (late_others[1], own_others))
     late_others[1], own_others = spread(late_others[1]), spread(own_others)
-    near = [trade(part, "batch", 1) for part in near]
 
     away = []
     for chunk, here in enumerate(parts_of):
@@ -636,17 +641,20 @@
         part = part.astype(jnp.bfloat16)
         if chunk == 0:
             (far, late), late_others[1] = after((far, late), late_others[1])
-            part, state = after(part, state)
+            part, (keys, values) = after(part, (keys, values))
+            state = prefix_attend(query_rows, keys, values, 1, scale, heads, (0, 2))
+            state = prefix_attend(query_rows, keys, values, 1, scale, heads, (1, 2), state)
+            states.append(state)
         else:
             away[-1], part = after(away[-1], part)
         away.append(trade(part, "batch", top))
-    states.append(prefix_attend(query_rows, keys, values, 1, scale, heads, (1, 2), state))
 
     result = None
     fresh = []
     for chunk in range(CHUNKS):
         pieces = [piece_of(t, rows, CHUNKS + chunk, 0) for t in late]
-        pieces += [piece_of(part, rows, chunk) for part in (*own_others, *near)]
+        pieces += [piece_of(part, rows, chunk, 0) for part in near]
+        pieces += [piece_of(part, rows, chunk) for part in own_others]
         pieces.append(piece_of(away[chunk], rows, 0))
         result, new = fresh_attend(
             lengths,

time: 93.8 us -> 99.7 us (1.063)
  waiting for transfers between devices: 20.6 us -> 15.2 us
  other arithmetic: 1.87 us -> 6.59 us
  local copies, waits for them, and re-layouts: 0.08 us -> 4.25 us
  Pallas kernels: 50.3 us -> 54.3 us
  starting transfers between devices: 19.8 us -> 17.8 us
    unnamed x32 -> x50, local copies, waits for them, and re-layouts: 0.08 us -> 4.25 us
    ppermute x7, waiting for transfers between devices: 18.8 us -> 15 us  [trade(): lax.ppermute(array, axis, [(i, i ^ bits) for i in range(lax.axis_size(axi...]
    convert_element_type x0 -> x2, other arithmetic: none -> 2.72 us  [the longest x1 1.74 us: reduced_shards(): own_others.append(part.astype(jnp.bfloat16))]
    pallas_call x1 -> x2, Pallas kernels: 3.08 us -> 5.5 us  [cut_tokens(): pl.pallas_call(functools.partial(cut_kernel, bits), grid_spec=pltpu.Prefe...]
    pallas_call x2, Pallas kernels: 10 us -> 11.9 us  [fresh_attend(): pl.pallas_call(functools.partial(fresh_kernel, scale, heads, per_token, c...]
    convert_element_type x2, other arithmetic: 0.13 us -> 1.73 us  [reduced_shards(): part = part.astype(jnp.bfloat16)]
    ppermute x8 -> x7, waiting for transfers between devices: 1.72 us -> 0.23 us  [shift(): lax.ppermute(array, axis, [(i, (i + step) % count) for i in range(count)])]
    ppermute x7, starting transfers between devices: 12.5 us -> 11.1 us  [trade(): lax.ppermute(array, axis, [(i, i ^ bits) for i in range(lax.axis_size(axi...]
  transfers between devices with their start and end apart: 15 -> 14, of which waited for: 4 -> 4; matrix products, arithmetic and copies ran while one was open for 1% -> 6% of each run, Pallas kernels for 41% -> 46%
where the time goes in v14:
time: 99.7 us; the launch traced here: 99.2 us
  Pallas kernels  54.3 us (54%)
  starting transfers between devices  17.8 us (18%)
  waiting for transfers between devices  15.2 us (15%)
  other arithmetic  6.59 us (7%)
  local copies, waits for them, and re-layouts  4.25 us (4%)
  between operations  1.07 us (1%)
    pallas_call x4, Pallas kernels, prefix_attend(): pl.pallas_call(functools.partial(prefix_kernel, scale, heads), grid=(step...  15.5 us
    ppermute x7, waiting for transfers between devices, trade(): lax.ppermute(array, axis, [(i, i ^ bits) for i in range(lax.axis_size(axi...  15 us
    pallas_call x4, Pallas kernels, project(): pl.pallas_call(functools.partial(project_kernel, len(blocks), [len(terms)...  12.9 us
    pallas_call x2, Pallas kernels, fresh_attend(): pl.pallas_call(functools.partial(fresh_kernel, scale, heads, per_token, c...  11.9 us
    ppermute x7, starting transfers between devices, trade(): lax.ppermute(array, axis, [(i, i ^ bits) for i in range(lax.axis_size(axi...  11.1 us
    ppermute x7, starting transfers between devices, shift(): lax.ppermute(array, axis, [(i, (i + step) % count) for i in range(count)])  6.7 us
    pallas_call x2, Pallas kernels, cut_tokens(): pl.pallas_call(functools.partial(cut_kernel, bits), grid_spec=pltpu.Prefe...  5.5 us
    unnamed x50, local copies, waits for them, and re-layouts  4.25 us
  transfers between devices with their start and end apart: 14, of which 4 were waited for; matrix products, arithmetic and copies ran while one was open for 6% of the time, Pallas kernels for 46%

profile of v14, /device:TPU:0, one launch (start us, length us, event | category | flops | bytes accessed | tf_op | source)
XLA Modules:
  0.0 99.2 jit_solution(4287716203915632309)
XLA Ops:
  0.0 0.7 pad_add_fusion.place_ref
  0.7 2.8 %cut_tokens.2 = (bf16[256,1024]{1,0:T(8,128)(2,1)}, bf16[256,1024]{1,0:T(8,128)(2,1)}) custom-call(s32[3]{0:T(128)} %pad_add_fusion.place_ref, bf16[256,4096]{1,0:T(8,128)(2,1)} %refs_1_.3), custom_call_target="tpu_custom_call" | custom-call | flops 99999997952 | bytes 1 | tf_op jit(solution)/shard_map/cut_tokens/pallas_call | solution.py:184
  3.5 5.1 %collective-permute-start = (bf16[256,1024]{1,0:T(8,128)(2,1)}, bf16[256,1024]{1,0:T(8,128)(2,1)}, u32[]{:S(2)}, u32[]{:S(2)}) collective-permute-start(bf16[256,1024]{1,0:T(8,128)(2,1)} %get-tuple-element.58), channel_id=1, source_target_pairs={{0,12},{4,8},{8,4},{12,0},{1,13},{5,9},{9,5},{13,1},{2,14},{6,10},... | collective-permute-start | bytes 1572872 | tf_op jit(solution)/shard_map/ppermute | solution.py:105
  8.6 0.0 copy-start.11
  8.6 0.0 copy-start.12
  8.7 3.0 %arrange_pool.1 = (bf16[8,128,512]{2,1,0:T(8,128)(2,1)S(1)}, bf16[8,128,512]{2,1,0:T(8,128)(2,1)}) custom-call(s32[3]{0:T(128)S(1)} %copy-done.8, bf16[8,128,8,128]{3,2,1,0:T(8,128)(2,1)S(1)} %bitcast.43), custom_call_target="tpu_custom_call" | custom-call | flops 99999997952 | bytes 1 | tf_op jit(solution)/shard_map/arrange_pool/pallas_call | solution.py:234
  11.6 1.5 %collective-permute-start.3 = (bf16[8,128,512]{2,1,0:T(8,128)(2,1)}, bf16[8,128,512]{2,1,0:T(8,128)(2,1)}, u32[]{:S(2)}, u32[]{:S(2)}) collective-permute-start(bf16[8,128,512]{2,1,0:T(8,128)(2,1)} %get-tuple-element.67), channel_id=1, source_target_pairs={{0,2},{2,0},{1,3},{3,1},{4,6},{6,4},{5,7},{7,5},{8,10},{10,8},{9,1... | collective-permute-start | bytes 3145736 | tf_op jit(solution)/shard_map/ppermute | solution.py:101
  13.1 2.5 %arrange_weights.1.refs_2_ = bf16[2,2,1024,512]{3,2,1,0:T(8,128)(2,1)S(1)} custom-call(bf16[1024,8,128]{2,1,0:T(8,128)(2,1)S(1)} %bitcast.44, bf16[1024,8,128]{2,1,0:T(8,128)(2,1)S(1)} %bitcast.45), custom_call_target="tpu_custom_call" | custom-call | flops 99999997952 | bytes 1 | tf_op jit(solution)/shard_map/arrange_weights/pallas_call | solution.py:150
  15.6 1.9 %copy-done.16 = bf16[2,2,1024,512]{3,2,1,0:T(8,128)(2,1)} copy-done((bf16[2,2,1024,512]{3,2,1,0:T(8,128)(2,1)}, bf16[2,2,1024,512]{3,2,1,0:T(8,128)(2,1)S(1)}, u32[]{:S(2)}) %copy-start.16) | copy-done | bytes 4194328
  17.6 2.7 %cut_tokens.3 = bf16[256,1024]{1,0:T(8,128)(2,1)} custom-call(s32[3]{0:T(128)} %pad_add_fusion.place_ref, bf16[256,4096]{1,0:T(8,128)(2,1)} %refs_1_.3), custom_call_target="tpu_custom_call" | custom-call | flops 99999997952 | bytes 1 | tf_op jit(solution)/shard_map/cut_tokens/pallas_call | solution.py:184
  20.3 0.8 collective-permute-start.4
  21.7 0.0 collective-permute-done.refs_0_
  21.8 11.5 %collective-permute-done.1.refs_1_ = bf16[256,1024]{1,0:T(8,128)(2,1)} collective-permute-done((bf16[256,1024]{1,0:T(8,128)(2,1)}, bf16[256,1024]{1,0:T(8,128)(2,1)}, u32[]{:S(2)}, u32[]{:S(2)}) %collective-permute-start.1) | collective-permute-done | bytes 524320 | tf_op jit(solution)/shard_map/ppermute | solution.py:105
  33.2 2.2 %copy-done.17 = bf16[2,2,1024,512]{3,2,1,0:T(8,128)(2,1)S(1)} copy-done((bf16[2,2,1024,512]{3,2,1,0:T(8,128)(2,1)S(1)}, bf16[2,2,1024,512]{3,2,1,0:T(8,128)(2,1)}, u32[]{:S(2)}) %copy-start.17) | copy-done | bytes 4194328
  35.4 3.3 %early_away.1 = bf16[2,512,512]{2,1,0:T(8,128)(2,1)S(1)} custom-call(s32[3]{0:T(128)S(1)} %copy-done.9, bf16[256,1024]{1,0:T(8,128)(2,1)} %collective-permute-done.refs_0_, bf16[256,1024]{1,0:T(8,128)(2,1)} %collective-permute-done.1.refs_1_, bf16[2,2,1024,512]{3,2,1,0:T(8,128)(2,1)S(1)} %copy-done.17), custom_call_target="tpu_custom_call" | custom-call | flops 99999997952 | bytes 1 | tf_op jit(solution)/shard_map/early_away/pallas_call | solution.py:294
  38.7 0.1 collective-permute-start.2
  38.8 3.3 %early_kept.1.refs_3_ = f32[2,512,512]{2,1,0:T(8,128)S(1)} custom-call(s32[3]{0:T(128)S(1)} %copy-done.9, bf16[256,1024]{1,0:T(8,128)(2,1)} %collective-permute-done.refs_0_, bf16[256,1024]{1,0:T(8,128)(2,1)} %collective-permute-done.1.refs_1_, bf16[2,2,1024,512]{3,2,1,0:T(8,128)(2,1)S(1)} %copy-done.17), custom_call_target="tpu_custom_call" | custom-call | flops 99999997952 | bytes 1 | tf_op jit(solution)/shard_map/early_kept/pallas_call | solution.py:294
  42.1 0.0 copy-start.15
  42.1 1.0 fusion
  43.1 1.7 %collective-permute-start.9 = (bf16[2,256,512]{2,1,0:T(8,128)(2,1)}, bf16[2,256,512]{2,1,0:T(8,128)(2,1)}, u32[]{:S(2)}, u32[]{:S(2)}) collective-permute-start(bf16[2,256,512]{2,1,0:T(8,128)(2,1)} %fusion), channel_id=1, source_target_pairs={{0,4},{4,0},{8,12},{12,8},{1,5},{5,1},{9,13},{13,9},{2,6},{6,2},{1... | collective-permute-start | bytes 1572872 | tf_op jit(solution)/shard_map/ppermute | solution.py:105
  44.8 0.8 fusion.4
  45.6 1.5 %collective-permute-start.5 = (bf16[256,512]{1,0:T(8,128)(2,1)}, bf16[256,512]{1,0:T(8,128)(2,1)}, u32[]{:S(2)}, u32[]{:S(2)}) collective-permute-start(bf16[256,512]{1,0:T(8,128)(2,1)} %fusion.4), channel_id=1, source_target_pairs={{0,2},{2,0},{1,3},{3,1},{4,6},{6,4},{5,7},{7,5},{8,10},{10,8},{9,1... | collective-permute-start | bytes 786440 | tf_op jit(solution)/shard_map/ppermute | solution.py:101
  47.1 3.0 %pick_blocks.1 = (bf16[1024,256]{1,0:T(8,128)(2,1)S(1)}, bf16[288,1024]{1,0:T(8,128)(2,1)S(1)}) custom-call(s32[3]{0:T(128)S(1)} %copy-done.9, s32[8]{0:T(128)S(1)} %bitcast.52, bf16[8,128,512]{2,1,0:T(8,128)(2,1)S(1)} %get-tuple-element.68.refs_0_, bf16[8,128,512]{2,1,0:T(8,128)(2,1)} %collective-permute-done.3.refs_1_), custom_call_target="tpu_custom_call" | custom-call | flops 99999997952 | bytes 1 | tf_op jit(solution)/shard_map/pick_blocks/pallas_call | solution.py:358
  50.2 0.0 copy-start.3
  50.2 0.0 copy-start.13
  50.2 3.9 %prefix_attend.4 = (f32[128,4096]{1,0:T(8,128)S(1)}, f32[8,4096]{1,0:T(8,128)S(1)}) custom-call(bf16[8192,128]{1,0:T(8,128)(2,1)S(1)} %bitcast.46, bf16[1024,256]{1,0:T(8,128)(2,1)S(1)} %get-tuple-element.81.keys, bf16[288,1024]{1,0:T(8,128)(2,1)S(1)} %get-tuple-element.82.values), custom_call_target="tpu_custom_call" | custom-call | flops 99999997952 | bytes 1 | tf_op jit(solution)/shard_map/prefix_attend/pallas_call | solution.py:428
  54.1 0.2 collective-permute-done.5.refs_5_
  54.4 3.3 %late_away.1 = (bf16[2,512,512]{2,1,0:T(8,128)(2,1)S(1)}, bf16[256,512]{1,0:T(8,128)(2,1)S(1)}) custom-call(s32[3]{0:T(128)S(1)} %copy-done.9, bf16[256,1024]{1,0:T(8,128)(2,1)} %collective-permute-done.4.refs_0_, bf16[256,4096]{1,0:T(8,128)(2,1)S(1)} %copy-done.13, bf16[2,2,1024,512]{3,2,1,0:T(8,128)(2,1)S(1)} %copy-done.18, f32[2,512,512]{2,1,0:T(8,128)S(1)} %copy-done.3, ...), custom_call_target="tpu_custom_call" | custom-call | flops 99999997952 | bytes 1 | tf_op jit(solution)/shard_map/late_away/pallas_call | solution.py:294
  57.6 0.1 collective-permute-start.6
  57.7 3.1 %late_kept.1.rest_0_.rest_1_ = f32[2,512,512]{2,1,0:T(8,128)S(1)} custom-call(s32[3]{0:T(128)S(1)} %copy-done.9, bf16[256,1024]{1,0:T(8,128)(2,1)} %collective-permute-done.4.refs_0_, bf16[256,4096]{1,0:T(8,128)(2,1)S(1)} %copy-done.13, bf16[2,2,1024,512]{3,2,1,0:T(8,128)(2,1)S(1)} %copy-done.18), custom_call_target="tpu_custom_call" | custom-call | flops 99999997952 | bytes 1 | tf_op jit(solution)/shard_map/late_kept/pallas_call | solution.py:294
  60.8 0.0 copy-start
  60.9 0.4 collective-permute-start.8
  61.3 0.7 fusion.15
  62.0 2.9 %collective-permute-done.9.rest_2_.rest_3_ = bf16[2,256,512]{2,1,0:T(8,128)(2,1)} collective-permute-done((bf16[2,256,512]{2,1,0:T(8,128)(2,1)}, bf16[2,256,512]{2,1,0:T(8,128)(2,1)}, u32[]{:S(2)}, u32[]{:S(2)}) %collective-permute-start.9) | collective-permute-done | bytes 524320 | tf_op jit(solution)/shard_map/ppermute | solution.py:105
  65.0 1.7 %fusion.5 = bf16[256,512]{1,0:T(8,128)(2,1)} fusion(f32[2,512,512]{2,1,0:T(8,128)S(1)} %late_kept.1.rest_0_.rest_1_, bf16[2,256,512]{2,1,0:T(8,128)(2,1)} %collective-permute-done.9.rest_2_.rest_3_, bf16[2,512,512]{2,1,0:T(8,128)(2,1)S(1)} %collective-permute-done.6.rest_1_.rest_2_), kind=kLoop, calls=%fused_computation.8 | loop fusion | flops 655360 | bytes 1310720 | tf_op jit(solution)/shard_map/convert_element_type | solution.py:629
  66.7 1.5 %collective-permute-start.7 = (bf16[128,512]{1,0:T(8,128)(2,1)S(1)}, bf16[128,512]{1,0:T(8,128)(2,1)S(1)}, u32[]{:S(2)}, u32[]{:S(2)}) collective-permute-start(bf16[128,512]{1,0:T(8,128)(2,1)S(1)} %get-tuple-element.108), channel_id=1, source_target_pairs={{0,2},{2,0},{1,3},{3,1},{4,6},{6,4},{5,7},{7,5},{8,10},{10,8},{9,1... | collective-permute-start | bytes 393224 | tf_op jit(solution)/shard_map/ppermute | solution.py:101
  68.2 3.9 %prefix_attend.7 = (f32[128,4096]{1,0:T(8,128)S(1)}, f32[8,4096]{1,0:T(8,128)S(1)}) custom-call(bf16[8192,128]{1,0:T(8,128)(2,1)S(1)} %bitcast.47, bf16[1024,256]{1,0:T(8,128)(2,1)S(1)} %copy-done.22, bf16[288,1024]{1,0:T(8,128)(2,1)S(1)} %copy-done.20, f32[128,4096]{1,0:T(8,128)S(1)} %get-tuple-element.87.refs_0_, ...), custom_call_target="tpu_custom_call", output_to_operand_aliasing={{0}: (3, {}), {1}: (4, {})} | custom-call | flops 99999997952 | bytes 1 | tf_op jit(solution)/shard_map/prefix_attend/pallas_call | solution.py:428
  72.1 0.6 collective-permute-start.10
  72.7 1.5 %collective-permute-start.11 = (bf16[256,512]{1,0:T(8,128)(2,1)}, bf16[256,512]{1,0:T(8,128)(2,1)}, u32[]{:S(2)}, u32[]{:S(2)}) collective-permute-start(bf16[256,512]{1,0:T(8,128)(2,1)} %fusion.5), channel_id=1, source_target_pairs={{0,2},{2,0},{1,3},{3,1},{4,6},{6,4},{5,7},{7,5},{8,10},{10,8},{9,1... | collective-permute-start | bytes 786440 | tf_op jit(solution)/shard_map/ppermute | solution.py:101
  74.2 0.8 fusion.11
  75.0 0.6 collective-permute-start.12
  75.5 3.8 %prefix_attend.5 = (f32[128,4096]{1,0:T(8,128)S(1)}, f32[8,4096]{1,0:T(8,128)S(1)}) custom-call(bf16[8192,128]{1,0:T(8,128)(2,1)S(1)} %bitcast.48, bf16[1024,256]{1,0:T(8,128)(2,1)S(1)} %copy-done.22, bf16[288,1024]{1,0:T(8,128)(2,1)S(1)} %copy-done.20), custom_call_target="tpu_custom_call" | custom-call | flops 99999997952 | bytes 1 | tf_op jit(solution)/shard_map/prefix_attend/pallas_call | solution.py:428
  79.4 3.9 %prefix_attend.6 = (f32[128,4096]{1,0:T(8,128)S(1)}, f32[8,4096]{1,0:T(8,128)S(1)}) custom-call(bf16[8192,128]{1,0:T(8,128)(2,1)S(1)} %bitcast.49, bf16[1024,256]{1,0:T(8,128)(2,1)S(1)} %copy-done.22, bf16[288,1024]{1,0:T(8,128)(2,1)S(1)} %copy-done.20, f32[128,4096]{1,0:T(8,128)S(1)} %get-tuple-element.83.refs_0_, ...), custom_call_target="tpu_custom_call", output_to_operand_aliasing={{0}: (3, {}), {1}: (4, {})} | custom-call | flops 99999997952 | bytes 1 | tf_op jit(solution)/shard_map/prefix_attend/pallas_call | solution.py:428
  83.4 1.0 fusion.13
  84.3 2.4 %collective-permute-start.13 = (bf16[128,512]{1,0:T(8,128)(2,1)S(1)}, bf16[128,512]{1,0:T(8,128)(2,1)S(1)}, u32[]{:S(2)}, u32[]{:S(2)}) collective-permute-start(bf16[128,512]{1,0:T(8,128)(2,1)S(1)} %fusion.13), channel_id=1, source_target_pairs={{0,8},{4,12},{8,0},{12,4},{1,9},{5,13},{9,1},{13,5},{2,10},{6,14},... | collective-permute-start | bytes 393224 | tf_op jit(solution)/shard_map/ppermute | solution.py:105
  86.8 5.7 %fresh_attend.2 = (bf16[8192,128]{1,0:T(8,128)(2,1)}, bf16[128,512]{1,0:T(8,128)(2,1)S(1)}) custom-call(s32[1]{0:T(128)S(6)} %copy.21.length_ref, bf16[8192,128]{1,0:T(8,128)(2,1)S(1)} %bitcast.50, f32[128,4096]{1,0:T(8,128)S(1)} %get-tuple-element.93.acc_ref, f32[8,4096]{1,0:T(8,128)S(1)} %get-tuple-element.94.stat_ref, f32[2,512,512]{2,1,0:T(8,128)S(1)} %copy-done.1, ...), custom_call_target="tpu_custom_call" | custom-call | flops 99999997952 | bytes 1 | tf_op jit(solution)/shard_map/fresh_attend/pallas_call | solution.py:513
  92.4 0.5 collective-permute-done.13.rest_5_
  93.0 6.3 %fresh_attend.3 = (bf16[8192,128]{1,0:T(8,128)(2,1)}, bf16[128,512]{1,0:T(8,128)(2,1)}) custom-call(s32[1]{0:T(128)S(6)} %copy.21.length_ref, bf16[8192,128]{1,0:T(8,128)(2,1)S(1)} %bitcast.51, f32[128,4096]{1,0:T(8,128)S(1)} %get-tuple-element.85.acc_ref, f32[8,4096]{1,0:T(8,128)S(1)} %get-tuple-element.86.stat_ref, ...), custom_call_target="tpu_custom_call", output_to_operand_aliasing={{0}: (10, {})} | custom-call | flops 99999997952 | bytes 1 | tf_op jit(solution)/shard_map/fresh_attend/pallas_call | solution.py:513
  (52 shorter events, 0.1 us)
Async XLA Ops:
  0.7 8.0 %copy-start.8 = (s32[3]{0:T(128)S(1)}, s32[3]{0:T(128)}, u32[]{:S(2)}) copy-start(s32[3]{0:T(128)} %pad_add_fusion.place_ref) | copy-start | bytes 40
  0.7 8.0 %copy-start.10 = (bf16[8,128,4,1,256]{4,2,3,1,0:T(4,128)(2,1)S(1)}, bf16[8,128,4,1,256]{4,2,3,1,0:T(4,128)(2,1)}, u32[]{:S(2)}) copy-start(bf16[8,128,4,1,256]{4,2,3,1,0:T(4,128)(2,1)} %param.11) | copy-start | bytes 6291460
  3.5 18.3 %collective-permute-start = (bf16[256,1024]{1,0:T(8,128)(2,1)}, bf16[256,1024]{1,0:T(8,128)(2,1)}, u32[]{:S(2)}, u32[]{:S(2)}) collective-permute-start(bf16[256,1024]{1,0:T(8,128)(2,1)} %get-tuple-element.58), channel_id=1, source_target_pairs={{0,12},{4,8},{8,4},{12,0},{1,13},{5,9},{9,5},{13,1},{2,14},{6,10},... | collective-permute-start | bytes 1572872 | tf_op jit(solution)/shard_map/ppermute | solution.py:105
  8.6 24.6 %collective-permute-start.1 = (bf16[256,1024]{1,0:T(8,128)(2,1)}, bf16[256,1024]{1,0:T(8,128)(2,1)}, u32[]{:S(2)}, u32[]{:S(2)}) collective-permute-start(bf16[256,1024]{1,0:T(8,128)(2,1)} %get-tuple-element.59), channel_id=1, source_target_pairs={{0,4},{4,0},{8,12},{12,8},{1,5},{5,1},{9,13},{13,9},{2,6},{6,2},{1... | collective-permute-start | bytes 1572872 | tf_op jit(solution)/shard_map/ppermute | solution.py:105
  8.6 4.5 %copy-start.11 = (bf16[1,1,1024,4,2,128]{5,4,3,2,1,0:T(2,128)(2,1)S(1)}, bf16[1,1,1024,4,2,128]{5,4,3,2,1,0:T(2,128)(2,1)}, u32[]{:S(2)}) copy-start(bf16[1,1,1024,4,2,128]{5,4,3,2,1,0:T(2,128)(2,1)} %param.8) | copy-start | bytes 6291460
  8.6 4.5 %copy-start.12 = (bf16[1,1,1024,4,2,128]{5,4,3,2,1,0:T(2,128)(2,1)S(1)}, bf16[1,1,1024,4,2,128]{5,4,3,2,1,0:T(2,128)(2,1)}, u32[]{:S(2)}) copy-start(bf16[1,1,1024,4,2,128]{5,4,3,2,1,0:T(2,128)(2,1)} %param.9) | copy-start | bytes 6291460
  11.6 33.9 %collective-permute-start.3 = (bf16[8,128,512]{2,1,0:T(8,128)(2,1)}, bf16[8,128,512]{2,1,0:T(8,128)(2,1)}, u32[]{:S(2)}, u32[]{:S(2)}) collective-permute-start(bf16[8,128,512]{2,1,0:T(8,128)(2,1)} %get-tuple-element.67), channel_id=1, source_target_pairs={{0,2},{2,0},{1,3},{3,1},{4,6},{6,4},{5,7},{7,5},{8,10},{10,8},{9,1... | collective-permute-start | bytes 3145736 | tf_op jit(solution)/shard_map/ppermute | solution.py:101
  15.6 2.0 %copy-start.16 = (bf16[2,2,1024,512]{3,2,1,0:T(8,128)(2,1)}, bf16[2,2,1024,512]{3,2,1,0:T(8,128)(2,1)S(1)}, u32[]{:S(2)}) copy-start(bf16[2,2,1024,512]{3,2,1,0:T(8,128)(2,1)S(1)} %arrange_weights.1.refs_2_) | copy-start | bytes 12582916
  17.6 15.7 %copy-start.9 = (s32[3]{0:T(128)S(1)}, s32[3]{0:T(128)}, u32[]{:S(2)}) copy-start(s32[3]{0:T(128)} %pad_add_fusion.place_ref) | copy-start | bytes 40
  20.3 33.9 %collective-permute-start.4 = (bf16[256,1024]{1,0:T(8,128)(2,1)}, bf16[256,1024]{1,0:T(8,128)(2,1)}, u32[]{:S(2)}, u32[]{:S(2)}) collective-permute-start(bf16[256,1024]{1,0:T(8,128)(2,1)} %cut_tokens.3), channel_id=1, source_target_pairs={{0,8},{4,12},{8,0},{12,4},{1,9},{5,13},{9,1},{13,5},{2,10},{6,14},... | collective-permute-start | bytes 1572872 | tf_op jit(solution)/shard_map/ppermute | solution.py:105
  33.2 2.2 %copy-start.17 = (bf16[2,2,1024,512]{3,2,1,0:T(8,128)(2,1)S(1)}, bf16[2,2,1024,512]{3,2,1,0:T(8,128)(2,1)}, u32[]{:S(2)}) copy-start(bf16[2,2,1024,512]{3,2,1,0:T(8,128)(2,1)} %copy-done.16) | copy-start | bytes 12582916
  38.7 3.4 %collective-permute-start.2 = (bf16[2,512,512]{2,1,0:T(8,128)(2,1)S(1)}, bf16[2,512,512]{2,1,0:T(8,128)(2,1)S(1)}, u32[]{:S(2)}, u32[]{:S(2)}) collective-permute-start(bf16[2,512,512]{2,1,0:T(8,128)(2,1)S(1)} %early_away.1), channel_id=1, source_target_pairs={{0,1},{1,0},{2,3},{3,2},{4,5},{5,4},{6,7},{7,6},{8,9},{9,8},{10,11... | collective-permute-start | bytes 3145736 | tf_op jit(solution)/shard_map/ppermute | solution.py:101
  42.1 8.1 %copy-start.2 = (f32[2,512,512]{2,1,0:T(8,128)}, f32[2,512,512]{2,1,0:T(8,128)S(1)}, u32[]{:S(2)}) copy-start(f32[2,512,512]{2,1,0:T(8,128)S(1)} %early_kept.1.refs_3_) | copy-start | bytes 6291460
  42.1 5.0 %copy-start.15 = (s32[1,8]{1,0:T(1,128)S(1)}, s32[1,8]{1,0:T(1,128)}, u32[]{:S(2)}) copy-start(s32[1,8]{1,0:T(1,128)} %param.12) | copy-start | bytes 100
  42.1 8.0 %copy-start.6 = (bf16[2,512,512]{2,1,0:T(8,128)(2,1)}, bf16[2,512,512]{2,1,0:T(8,128)(2,1)S(1)}, u32[]{:S(2)}) copy-start(bf16[2,512,512]{2,1,0:T(8,128)(2,1)S(1)} %collective-permute-done.2.refs_4_) | copy-start | bytes 3145732
  43.1 21.9 %collective-permute-start.9 = (bf16[2,256,512]{2,1,0:T(8,128)(2,1)}, bf16[2,256,512]{2,1,0:T(8,128)(2,1)}, u32[]{:S(2)}, u32[]{:S(2)}) collective-permute-start(bf16[2,256,512]{2,1,0:T(8,128)(2,1)} %fusion), channel_id=1, source_target_pairs={{0,4},{4,0},{8,12},{12,8},{1,5},{5,1},{9,13},{13,9},{2,6},{6,2},{1... | collective-permute-start | bytes 1572872 | tf_op jit(solution)/shard_map/ppermute | solution.py:105
  45.6 8.7 %collective-permute-start.5 = (bf16[256,512]{1,0:T(8,128)(2,1)}, bf16[256,512]{1,0:T(8,128)(2,1)}, u32[]{:S(2)}, u32[]{:S(2)}) collective-permute-start(bf16[256,512]{1,0:T(8,128)(2,1)} %fusion.4), channel_id=1, source_target_pairs={{0,2},{2,0},{1,3},{3,1},{4,6},{6,4},{5,7},{7,5},{8,10},{10,8},{9,1... | collective-permute-start | bytes 786440 | tf_op jit(solution)/shard_map/ppermute | solution.py:101
  47.1 3.1 %copy-start.14 = (bf16[256,2,1,2048]{3,1,2,0:T(2,128)(2,1)S(1)}, bf16[256,2,1,2048]{3,1,2,0:T(2,128)(2,1)}, u32[]{:S(2)}) copy-start(bf16[256,2,1,2048]{3,1,2,0:T(2,128)(2,1)} %param.10) | copy-start | bytes 6291460
  50.1 4.0 %copy-start.19 = (bf16[288,1024]{1,0:T(8,128)(2,1)}, bf16[288,1024]{1,0:T(8,128)(2,1)S(1)}, u32[]{:S(2)}) copy-start(bf16[288,1024]{1,0:T(8,128)(2,1)S(1)} %get-tuple-element.82.values) | copy-start | bytes 1769476
  50.1 4.0 %copy-start.21 = (bf16[1024,256]{1,0:T(8,128)(2,1)}, bf16[1024,256]{1,0:T(8,128)(2,1)S(1)}, u32[]{:S(2)}) copy-start(bf16[1024,256]{1,0:T(8,128)(2,1)S(1)} %get-tuple-element.81.keys) | copy-start | bytes 1572868
  50.2 4.2 %copy-start.3 = (f32[2,512,512]{2,1,0:T(8,128)S(1)}, f32[2,512,512]{2,1,0:T(8,128)}, u32[]{:S(2)}) copy-start(f32[2,512,512]{2,1,0:T(8,128)} %copy-done.2) | copy-start | bytes 6291460
  50.2 4.2 %copy-start.7 = (bf16[2,512,512]{2,1,0:T(8,128)(2,1)S(1)}, bf16[2,512,512]{2,1,0:T(8,128)(2,1)}, u32[]{:S(2)}) copy-start(bf16[2,512,512]{2,1,0:T(8,128)(2,1)} %copy-done.6) | copy-start | bytes 3145732
  50.2 4.2 %copy-start.13 = (bf16[256,4096]{1,0:T(8,128)(2,1)S(1)}, bf16[256,4096]{1,0:T(8,128)(2,1)}, u32[]{:S(2)}) copy-start(bf16[256,4096]{1,0:T(8,128)(2,1)} %refs_1_.3) | copy-start | bytes 6291460
  50.2 4.2 %copy-start.18 = (bf16[2,2,1024,512]{3,2,1,0:T(8,128)(2,1)S(1)}, bf16[2,2,1024,512]{3,2,1,0:T(8,128)(2,1)}, u32[]{:S(2)}) copy-start(bf16[2,2,1024,512]{3,2,1,0:T(8,128)(2,1)} %copy-done.16) | copy-start | bytes 12582916
  57.6 3.7 %collective-permute-start.6 = (bf16[2,512,512]{2,1,0:T(8,128)(2,1)S(1)}, bf16[2,512,512]{2,1,0:T(8,128)(2,1)S(1)}, u32[]{:S(2)}, u32[]{:S(2)}) collective-permute-start(bf16[2,512,512]{2,1,0:T(8,128)(2,1)S(1)} %get-tuple-element.77), channel_id=1, source_target_pairs={{0,1},{1,0},{2,3},{3,2},{4,5},{5,4},{6,7},{7,6},{8,9},{9,8},{10,11... | collective-permute-start | bytes 3145736 | tf_op jit(solution)/shard_map/ppermute | solution.py:101
  60.8 13.3 %copy-start = (f32[2,512,512]{2,1,0:T(8,128)}, f32[2,512,512]{2,1,0:T(8,128)S(1)}, u32[]{:S(2)}) copy-start(f32[2,512,512]{2,1,0:T(8,128)S(1)} %late_kept.1.rest_0_.rest_1_) | copy-start | bytes 6291460
  60.9 7.4 %copy-start.20 = (bf16[288,1024]{1,0:T(8,128)(2,1)S(1)}, bf16[288,1024]{1,0:T(8,128)(2,1)}, u32[]{:S(2)}) copy-start(bf16[288,1024]{1,0:T(8,128)(2,1)} %copy-done.19) | copy-start | bytes 1769476
  60.9 7.3 %copy-start.22 = (bf16[1024,256]{1,0:T(8,128)(2,1)S(1)}, bf16[1024,256]{1,0:T(8,128)(2,1)}, u32[]{:S(2)}) copy-start(bf16[1024,256]{1,0:T(8,128)(2,1)} %copy-done.21) | copy-start | bytes 1572868
  60.9 13.3 %collective-permute-start.8 = (bf16[256,512]{1,0:T(8,128)(2,1)S(1)}, bf16[256,512]{1,0:T(8,128)(2,1)S(1)}, u32[]{:S(2)}, u32[]{:S(2)}) collective-permute-start(bf16[256,512]{1,0:T(8,128)(2,1)S(1)} %get-tuple-element.78), channel_id=1, source_target_pairs={{0,4},{4,0},{8,12},{12,8},{1,5},{5,1},{9,13},{13,9},{2,6},{6,2},{1... | collective-permute-start | bytes 786440 | tf_op jit(solution)/shard_map/ppermute | solution.py:105
  61.3 12.9 %copy-start.4 = (bf16[2,512,512]{2,1,0:T(8,128)(2,1)}, bf16[2,512,512]{2,1,0:T(8,128)(2,1)S(1)}, u32[]{:S(2)}) copy-start(bf16[2,512,512]{2,1,0:T(8,128)(2,1)S(1)} %collective-permute-done.6.rest_1_.rest_2_) | copy-start | bytes 3145732
  66.7 7.5 %collective-permute-start.7 = (bf16[128,512]{1,0:T(8,128)(2,1)S(1)}, bf16[128,512]{1,0:T(8,128)(2,1)S(1)}, u32[]{:S(2)}, u32[]{:S(2)}) collective-permute-start(bf16[128,512]{1,0:T(8,128)(2,1)S(1)} %get-tuple-element.108), channel_id=1, source_target_pairs={{0,2},{2,0},{1,3},{3,1},{4,6},{6,4},{5,7},{7,5},{8,10},{10,8},{9,1... | collective-permute-start | bytes 393224 | tf_op jit(solution)/shard_map/ppermute | solution.py:101
  72.1 11.2 %collective-permute-start.10 = (bf16[128,512]{1,0:T(8,128)(2,1)}, bf16[128,512]{1,0:T(8,128)(2,1)}, u32[]{:S(2)}, u32[]{:S(2)}) collective-permute-start(bf16[128,512]{1,0:T(8,128)(2,1)} %get-tuple-element.95), channel_id=1, source_target_pairs={{0,2},{2,0},{1,3},{3,1},{4,6},{6,4},{5,7},{7,5},{8,10},{10,8},{9,1... | collective-permute-start | bytes 393224 | tf_op jit(solution)/shard_map/ppermute | solution.py:101
  72.7 14.1 %collective-permute-start.11 = (bf16[256,512]{1,0:T(8,128)(2,1)}, bf16[256,512]{1,0:T(8,128)(2,1)}, u32[]{:S(2)}, u32[]{:S(2)}) collective-permute-start(bf16[256,512]{1,0:T(8,128)(2,1)} %fusion.5), channel_id=1, source_target_pairs={{0,2},{2,0},{1,3},{3,1},{4,6},{6,4},{5,7},{7,5},{8,10},{10,8},{9,1... | collective-permute-start | bytes 786440 | tf_op jit(solution)/shard_map/ppermute | solution.py:101
  74.2 5.2 %copy-start.23 = (bf16[256,512]{1,0:T(8,128)(2,1)}, bf16[256,512]{1,0:T(8,128)(2,1)S(1)}, u32[]{:S(2)}) copy-start(bf16[256,512]{1,0:T(8,128)(2,1)S(1)} %collective-permute-done.8) | copy-start | bytes 786436
  75.0 9.4 %collective-permute-start.12 = (bf16[128,512]{1,0:T(8,128)(2,1)}, bf16[128,512]{1,0:T(8,128)(2,1)}, u32[]{:S(2)}, u32[]{:S(2)}) collective-permute-start(bf16[128,512]{1,0:T(8,128)(2,1)} %fusion.11), channel_id=1, source_target_pairs={{0,8},{4,12},{8,0},{12,4},{1,9},{5,13},{9,1},{13,5},{2,10},{6,14},... | collective-permute-start | bytes 393224 | tf_op jit(solution)/shard_map/ppermute | solution.py:105
  79.4 3.9 %copy-start.1 = (f32[2,512,512]{2,1,0:T(8,128)S(1)}, f32[2,512,512]{2,1,0:T(8,128)}, u32[]{:S(2)}) copy-start(f32[2,512,512]{2,1,0:T(8,128)} %copy-done) | copy-start | bytes 6291460
  79.4 3.9 %copy-start.5 = (bf16[2,512,512]{2,1,0:T(8,128)(2,1)S(1)}, bf16[2,512,512]{2,1,0:T(8,128)(2,1)}, u32[]{:S(2)}) copy-start(bf16[2,512,512]{2,1,0:T(8,128)(2,1)} %copy-done.4) | copy-start | bytes 3145732
  79.4 3.9 %copy-start.24 = (bf16[256,512]{1,0:T(8,128)(2,1)S(1)}, bf16[256,512]{1,0:T(8,128)(2,1)}, u32[]{:S(2)}) copy-start(bf16[256,512]{1,0:T(8,128)(2,1)} %copy-done.23) | copy-start | bytes 786436
  84.3 8.6 %collective-permute-start.13 = (bf16[128,512]{1,0:T(8,128)(2,1)S(1)}, bf16[128,512]{1,0:T(8,128)(2,1)S(1)}, u32[]{:S(2)}, u32[]{:S(2)}) collective-permute-start(bf16[128,512]{1,0:T(8,128)(2,1)S(1)} %fusion.13), channel_id=1, source_target_pairs={{0,8},{4,12},{8,0},{12,4},{1,9},{5,13},{9,1},{13,5},{2,10},{6,14},... | collective-permute-start | bytes 393224 | tf_op jit(solution)/shard_map/ppermute | solution.py:105

commit v15 on v12

--- a/solution.py
+++ b/solution.py
@@ -567,33 +567,42 @@
     pools = [shift(part, "ctx", step) if step else part for step, part in enumerate(pools)]
 
     weights = arrange_weights(key_weight, value_weight, ctx_count, heads, head_count)
+
+    query_rows = queries.reshape(token_count, heads, group, width)
+    query_rows = query_rows.transpose(0, 2, 1, 3).reshape(-1, width)
+    def projected(blocks, name, sums=()):
+        terms = [
+            shift(
+                project(place, blocks, weights, step, jnp.bfloat16, name + "_away"), "head", step
+            )
+            for step in range(1, head_count)
+        ]
+        kept = project(place, blocks, weights, 0, jnp.float32, name + "_kept", sums)
+        kept, *made = kept if sums else [kept]
+        return [kept, *terms], made
+
+    def added(terms, step, here):
+        return sum(term[step, here].astype(jnp.float32) for term in terms)
+
+    def others(terms, here):
+        return [added(terms, step, here).astype(jnp.bfloat16) for step in range(1, ctx_count)]
+
+    def spread(parts):
+        return [shift(part, "ctx", step + 1) for step, part in enumerate(parts)]
+
+    every = slice(None)
+    parts_of = [slice(i * rows, (i + 1) * rows) for i in range(CHUNKS)]
+
     weights, last = after(weights, pieces[-1])
     last = trade(last, "batch", top)
-
-    query_rows = queries.reshape(token_count, heads, group, width)
-    query_rows = query_rows.transpose(0, 2, 1, 3).reshape(-1, width)
-    def projected(blocks, name):
-        terms = [
-            shift(project(place, blocks, weights, step, jnp.bfloat16, name + "_away"), "head", step)
-            for step in range(1, head_count)
-        ]
-        return [project(place, blocks, weights, 0, jnp.float32, name + "_kept"), *terms]
-
-    def added(terms, step, here):
-        return sum(term[step, here].astype(jnp.float32) for term in terms)
-
-    def others(terms, here):
-        return [added(terms, step, here).astype(jnp.bfloat16) for step in range(1, ctx_count)]
-
-    def spread(parts):
-        return [shift(part, "ctx", step + 1) for step, part in enumerate(parts)]
-
-    every = slice(None)
-    parts_of = [slice(i * rows, (i + 1) * rows) for i in range(CHUNKS)]
+    own, _ = projected([tokens], "own")
 
     sums = [[], []]
+    own_others = []
     if steps:
-        early = projected(arrived, "early")
+        sums = [[piece_of(t, token_count, 0, step) for t in own] for step in range(1, ctx_count)]
+        early, own_others = projected(arrived, "early", sums)
+        own_others = spread(own_others)
         cuts = [slice(i * token_count, (i + 1) * token_count) for i in range(len(steps))]
         leaving = [others(early, cut) for cut in cuts]
         leaving, pools = after(leaving, pools)
@@ -609,7 +618,7 @@
     states[0], last = after(states[0], last)
 
     def late_project(step, dtype, name, sums):
-        result = project(place, [last, tokens], weights, step, dtype, name, sums)
+        result = project(place, [last], weights, step, dtype, name, sums)
         return result if sums else (result,)
 
     terms = []
@@ -620,14 +629,10 @@
     far, near = far[:1], far[1:]
     late = [kept, *terms]
     far = [trade(part, "batch", 1) for part in far]
-    own_at = slice(token_count, 2 * token_count)
-    *late_others, own_others = [others(late, here) for here in [*parts_of, own_at]]
+    late_others = [others(late, here) for here in parts_of]
     late_others[0] = spread(late_others[0])
     late_others[1], (keys, values) = after(late_others[1], (keys, values))
     state = prefix_attend(query_rows, keys, values, 1, scale, heads, (0, 2))
-    state, (late_others[1], own_others, near) = after(state, (late_others[1], own_others, near))
-    late_others[1], own_others = spread(late_others[1]), spread(own_others)
-    near = [trade(part, "batch", 1) for part in near]
 
     away = []
     for chunk, here in enumerate(parts_of):
@@ -635,17 +640,22 @@
         part = part + sum(p[here].astype(jnp.float32) for p in far)
         part = part.astype(jnp.bfloat16)
         if chunk == 0:
+            state, part = after(state, part)
+            part, (state, late_others[1], near) = after(part, (state, late_others[1], near))
+            late_others[1] = spread(late_others[1])
+            near = [trade(piece, "batch", 1) for piece in near]
             (far, late), late_others[1] = after((far, late), late_others[1])
-            part, state = after(part, state)
+            states.append(
+                prefix_attend(query_rows, keys, values, 1, scale, heads, (1, 2), state)
+            )
         else:
             away[-1], part = after(away[-1], part)
         away.append(trade(part, "batch", top))
-    states.append(prefix_attend(query_rows, keys, values, 1, scale, heads, (1, 2), state))
 
     result = None
     fresh = []
     for chunk in range(CHUNKS):
-        pieces = [piece_of(t, rows, CHUNKS + chunk, 0) for t in late]
+        pieces = [piece_of(t, rows, chunk, 0) for t in own]
         pieces += [piece_of(part, rows, chunk) for part in (*own_others, *near)]
         pieces.append(piece_of(away[chunk], rows, 0))
         result, new = fresh_attend(
@@ -669,7 +679,7 @@
     def shards(tokens, key_weight, value_weight, *rest):
         prompts = mesh.shape["batch"]
         columns = 2 * math.prod(key_weight.shape[3:])
-        few_tokens = prompts * tokens.shape[0] <= columns and prompts in (2, 4)
+        few_tokens = prompts * tokens.shape[0] <= columns and prompts == 4
         form = reduced_shards if few_tokens else gathered_shards
         return form(tokens, key_weight, value_weight, *rest)
 

time: 93.8 us -> 101 us (1.077)
  Pallas kernels: 50.3 us -> 55.1 us
  waiting for transfers between devices: 20.6 us -> 24.9 us
  starting transfers between devices: 19.8 us -> 18.2 us
    ppermute x8 -> x9, waiting for transfers between devices: 1.72 us -> 4.78 us  [shift(): lax.ppermute(array, axis, [(i, (i + step) % count) for i in range(count)])]
    pallas_call x4 -> x6, Pallas kernels: 13.3 us -> 16.2 us  [project(): pl.pallas_call(functools.partial(project_kernel, len(blocks), [len(terms)...]
    ppermute x7, starting transfers between devices: 12.5 us -> 10.1 us  [trade(): lax.ppermute(array, axis, [(i, i ^ bits) for i in range(lax.axis_size(axi...]
    pallas_call x2, Pallas kernels: 10 us -> 11.9 us  [fresh_attend(): pl.pallas_call(functools.partial(fresh_kernel, scale, heads, per_token, c...]
    ppermute x7, waiting for transfers between devices: 18.8 us -> 20.1 us  [trade(): lax.ppermute(array, axis, [(i, i ^ bits) for i in range(lax.axis_size(axi...]
    ppermute x8 -> x9, starting transfers between devices: 7.3 us -> 8.15 us  [shift(): lax.ppermute(array, axis, [(i, (i + step) % count) for i in range(count)])]
  transfers between devices with their start and end apart: 15 -> 16, of which waited for: 4 -> 6; matrix products, arithmetic and copies ran while one was open for 1% -> 1% of each run, Pallas kernels for 41% -> 45%
where the time goes in v15:
time: 101 us
  Pallas kernels  55.1 us (55%)
  waiting for transfers between devices  24.9 us (25%)
  starting transfers between devices  18.2 us (18%)
  other arithmetic  1.97 us (2%)
    ppermute x7, waiting for transfers between devices, trade(): lax.ppermute(array, axis, [(i, i ^ bits) for i in range(lax.axis_size(axi...  20.1 us
    pallas_call x6, Pallas kernels, project(): pl.pallas_call(functools.partial(project_kernel, len(blocks), [len(terms)...  16.2 us
    pallas_call x3, Pallas kernels, prefix_attend(): pl.pallas_call(functools.partial(prefix_kernel, scale, heads), grid=(step...  15.5 us
    pallas_call x2, Pallas kernels, fresh_attend(): pl.pallas_call(functools.partial(fresh_kernel, scale, heads, per_token, c...  11.9 us
    ppermute x7, starting transfers between devices, trade(): lax.ppermute(array, axis, [(i, i ^ bits) for i in range(lax.axis_size(axi...  10.1 us
    ppermute x9, starting transfers between devices, shift(): lax.ppermute(array, axis, [(i, (i + step) % count) for i in range(count)])  8.15 us
    ppermute x9, waiting for transfers between devices, shift(): lax.ppermute(array, axis, [(i, (i + step) % count) for i in range(count)])  4.78 us
    pallas_call x1, Pallas kernels, cut_tokens(): pl.pallas_call(functools.partial(cut_kernel, bits), grid_spec=pltpu.Prefe...  3.09 us
  transfers between devices with their start and end apart: 16, of which 6 were waited for; matrix products, arithmetic and copies ran while one was open for 1% of the time, Pallas kernels for 45%

profile of v15, /device:TPU:0, one launch (start us, length us, event | category | flops | bytes accessed | tf_op | source)
XLA Modules:
  0.0 101.2 jit_solution(8190911713003294307)
XLA Ops:
  0.0 0.6 pad_add_fusion.place_ref
  0.6 3.1 %cut_tokens.1 = (bf16[256,1024]{1,0:T(8,128)(2,1)}, bf16[256,1024]{1,0:T(8,128)(2,1)}, bf16[256,1024]{1,0:T(8,128)(2,1)}) custom-call(s32[3]{0:T(128)} %pad_add_fusion.place_ref, bf16[256,4096]{1,0:T(8,128)(2,1)} %refs_0_.3), custom_call_target="tpu_custom_call" | custom-call | flops 99999997952 | bytes 1 | tf_op jit(solution)/shard_map/cut_tokens/pallas_call | solution.py:184
  3.7 5.1 %collective-permute-start = (bf16[256,1024]{1,0:T(8,128)(2,1)}, bf16[256,1024]{1,0:T(8,128)(2,1)}, u32[]{:S(2)}, u32[]{:S(2)}) collective-permute-start(bf16[256,1024]{1,0:T(8,128)(2,1)} %get-tuple-element.63), channel_id=1, source_target_pairs={{0,12},{4,8},{8,4},{12,0},{1,13},{5,9},{9,5},{13,1},{2,14},{6,10},... | collective-permute-start | bytes 1572872 | tf_op jit(solution)/shard_map/ppermute | solution.py:105
  8.8 0.0 collective-permute-start.1
  8.8 0.0 copy-start.6
  8.8 0.0 copy-start.7
  8.8 3.0 %arrange_pool.1 = (bf16[8,128,512]{2,1,0:T(8,128)(2,1)S(1)}, bf16[8,128,512]{2,1,0:T(8,128)(2,1)}) custom-call(s32[3]{0:T(128)S(1)} %copy-done.4, bf16[8,128,8,128]{3,2,1,0:T(8,128)(2,1)S(1)} %bitcast.43), custom_call_target="tpu_custom_call" | custom-call | flops 99999997952 | bytes 1 | tf_op jit(solution)/shard_map/arrange_pool/pallas_call | solution.py:234
  11.8 2.5 %arrange_weights.1.refs_1_.refs_2_ = bf16[2,2,1024,512]{3,2,1,0:T(8,128)(2,1)S(1)} custom-call(bf16[1024,8,128]{2,1,0:T(8,128)(2,1)S(1)} %bitcast.44, bf16[1024,8,128]{2,1,0:T(8,128)(2,1)S(1)} %bitcast.45), custom_call_target="tpu_custom_call" | custom-call | flops 99999997952 | bytes 1 | tf_op jit(solution)/shard_map/arrange_weights/pallas_call | solution.py:150
  14.3 2.2 %own_away.1 = bf16[2,256,512]{2,1,0:T(8,128)(2,1)} custom-call(s32[3]{0:T(128)S(1)} %copy-done.4, bf16[256,4096]{1,0:T(8,128)(2,1)S(1)} %copy-done.8, bf16[2,2,1024,512]{3,2,1,0:T(8,128)(2,1)S(1)} %arrange_weights.1.refs_1_.refs_2_), custom_call_target="tpu_custom_call" | custom-call | flops 99999997952 | bytes 1 | tf_op jit(solution)/shard_map/own_away/pallas_call | solution.py:294
  16.6 0.0 collective-permute-start.2
  16.6 1.5 %collective-permute-start.4 = (bf16[8,128,512]{2,1,0:T(8,128)(2,1)}, bf16[8,128,512]{2,1,0:T(8,128)(2,1)}, u32[]{:S(2)}, u32[]{:S(2)}) collective-permute-start(bf16[8,128,512]{2,1,0:T(8,128)(2,1)} %get-tuple-element.74), channel_id=1, source_target_pairs={{0,2},{2,0},{1,3},{3,1},{4,6},{6,4},{5,7},{7,5},{8,10},{10,8},{9,1... | collective-permute-start | bytes 3145736 | tf_op jit(solution)/shard_map/ppermute | solution.py:101
  18.1 0.8 collective-permute-start.5
  18.9 1.5 %own_kept.1.refs_3_.rest_0_.rest_1_ = f32[2,256,512]{2,1,0:T(8,128)S(1)} custom-call(s32[3]{0:T(128)S(1)} %copy-done.4, bf16[256,4096]{1,0:T(8,128)(2,1)S(1)} %copy-done.8, bf16[2,2,1024,512]{3,2,1,0:T(8,128)(2,1)S(1)} %arrange_weights.1.refs_1_.refs_2_), custom_call_target="tpu_custom_call" | custom-call | flops 99999997952 | bytes 1 | tf_op jit(solution)/shard_map/own_kept/pallas_call | solution.py:294
  21.1 0.9 collective-permute-done.refs_0_
  22.0 11.5 %collective-permute-done.1.refs_1_ = bf16[256,1024]{1,0:T(8,128)(2,1)} collective-permute-done((bf16[256,1024]{1,0:T(8,128)(2,1)}, bf16[256,1024]{1,0:T(8,128)(2,1)}, u32[]{:S(2)}, u32[]{:S(2)}) %collective-permute-start.1) | collective-permute-done | bytes 524320 | tf_op jit(solution)/shard_map/ppermute | solution.py:105
  33.4 3.3 %early_away.1 = bf16[2,512,512]{2,1,0:T(8,128)(2,1)S(1)} custom-call(s32[3]{0:T(128)S(1)} %copy-done.4, bf16[256,1024]{1,0:T(8,128)(2,1)} %collective-permute-done.refs_0_, bf16[256,1024]{1,0:T(8,128)(2,1)} %collective-permute-done.1.refs_1_, bf16[2,2,1024,512]{3,2,1,0:T(8,128)(2,1)S(1)} %arrange_weights.1.refs_1_.refs_2_), custom_call_target="tpu_custom_call" | custom-call | flops 99999997952 | bytes 1 | tf_op jit(solution)/shard_map/early_away/pallas_call | solution.py:294
  36.7 0.1 collective-permute-start.3
  36.8 0.0 collective-permute-done.2.refs_4_.rest_1_.rest_2_
  36.8 3.7 %early_kept.1 = (f32[2,512,512]{2,1,0:T(8,128)S(1)}, bf16[256,512]{1,0:T(8,128)(2,1)}) custom-call(s32[3]{0:T(128)S(1)} %copy-done.4, bf16[256,1024]{1,0:T(8,128)(2,1)} %collective-permute-done.refs_0_, bf16[256,1024]{1,0:T(8,128)(2,1)} %collective-permute-done.1.refs_1_, bf16[2,2,1024,512]{3,2,1,0:T(8,128)(2,1)S(1)} %arrange_weights.1.refs_1_.refs_2_, ...), custom_call_target="tpu_custom_call" | custom-call | flops 99999997952 | bytes 1 | tf_op jit(solution)/shard_map/early_kept/pallas_call | solution.py:294
  40.5 1.4 %collective-permute-start.11 = (bf16[256,512]{1,0:T(8,128)(2,1)}, bf16[256,512]{1,0:T(8,128)(2,1)}, u32[]{:S(2)}, u32[]{:S(2)}) collective-permute-start(bf16[256,512]{1,0:T(8,128)(2,1)} %get-tuple-element.102), channel_id=1, source_target_pairs={{0,2},{2,0},{1,3},{3,1},{4,6},{6,4},{5,7},{7,5},{8,10},{10,8},{9,1... | collective-permute-start | bytes 786440 | tf_op jit(solution)/shard_map/ppermute | solution.py:101
  41.9 0.0 collective-permute-done.3.refs_3_.refs_6_
  41.9 1.2 %fusion.1 = (bf16[256,512]{1,0:T(8,128)(2,1)}, bf16[256,512]{1,0:T(8,128)(2,1)}) fusion(f32[2,512,512]{2,1,0:T(8,128)S(1)} %get-tuple-element.72.refs_2_.refs_5_, bf16[2,512,512]{2,1,0:T(8,128)(2,1)S(1)} %collective-permute-done.3.refs_3_.refs_6_), kind=kLoop, calls=%fused_computation.3 | loop fusion | flops 786432 | bytes 2097152 | tf_op jit(solution)/shard_map/convert_element_type | solution.py:588
  43.1 0.0 collective-permute-done.4.refs_1_
  43.1 0.9 collective-permute-start.6
  44.0 1.1 %collective-permute-start.7 = (bf16[256,512]{1,0:T(8,128)(2,1)}, bf16[256,512]{1,0:T(8,128)(2,1)}, u32[]{:S(2)}, u32[]{:S(2)}) collective-permute-start(bf16[256,512]{1,0:T(8,128)(2,1)} %get-tuple-element.84), channel_id=1, source_target_pairs={{0,2},{2,0},{1,3},{3,1},{4,6},{6,4},{5,7},{7,5},{8,10},{10,8},{9,1... | collective-permute-start | bytes 786440 | tf_op jit(solution)/shard_map/ppermute | solution.py:101
  45.1 3.0 %pick_blocks.1 = (bf16[1024,256]{1,0:T(8,128)(2,1)S(1)}, bf16[288,1024]{1,0:T(8,128)(2,1)S(1)}) custom-call(s32[3]{0:T(128)S(1)} %copy-done.4, s32[8]{0:T(128)S(1)} %bitcast.51, bf16[8,128,512]{2,1,0:T(8,128)(2,1)S(1)} %get-tuple-element.75.refs_0_, bf16[8,128,512]{2,1,0:T(8,128)(2,1)} %collective-permute-done.4.refs_1_), custom_call_target="tpu_custom_call" | custom-call | flops 99999997952 | bytes 1 | tf_op jit(solution)/shard_map/pick_blocks/pallas_call | solution.py:358
  48.2 0.0 copy-start.1
  48.2 7.7 %prefix_attend.3 = (f32[128,4096]{1,0:T(8,128)S(1)}, f32[8,4096]{1,0:T(8,128)S(1)}) custom-call(bf16[8192,128]{1,0:T(8,128)(2,1)S(1)} %bitcast.46, bf16[1024,256]{1,0:T(8,128)(2,1)S(1)} %get-tuple-element.86.keys, bf16[288,1024]{1,0:T(8,128)(2,1)S(1)} %get-tuple-element.87.values), custom_call_target="tpu_custom_call" | custom-call | flops 99999997952 | bytes 1 | tf_op jit(solution)/shard_map/prefix_attend/pallas_call | solution.py:428
  56.0 4.8 %collective-permute-done.7.refs_7_ = bf16[256,512]{1,0:T(8,128)(2,1)} collective-permute-done((bf16[256,512]{1,0:T(8,128)(2,1)}, bf16[256,512]{1,0:T(8,128)(2,1)}, u32[]{:S(2)}, u32[]{:S(2)}) %collective-permute-start.7) | collective-permute-done | bytes 262176 | tf_op jit(solution)/shard_map/ppermute | solution.py:101
  60.8 2.9 %late_away.1 = (bf16[2,256,512]{2,1,0:T(8,128)(2,1)S(1)}, bf16[256,512]{1,0:T(8,128)(2,1)S(1)}, bf16[256,512]{1,0:T(8,128)(2,1)S(1)}) custom-call(s32[3]{0:T(128)S(1)} %copy-done.4, bf16[256,1024]{1,0:T(8,128)(2,1)} %collective-permute-done.5.refs_0_, bf16[2,2,1024,512]{3,2,1,0:T(8,128)(2,1)S(1)} %copy-done.12, f32[2,512,512]{2,1,0:T(8,128)S(1)} %copy-done.1, ...), custom_call_target="tpu_custom_call" | custom-call | flops 99999997952 | bytes 1 | tf_op jit(solution)/shard_map/late_away/pallas_call | solution.py:294
  63.7 0.1 collective-permute-start.8
  63.8 2.5 %late_kept.1 = f32[2,256,512]{2,1,0:T(8,128)S(1)} custom-call(s32[3]{0:T(128)S(1)} %copy-done.4, bf16[256,1024]{1,0:T(8,128)(2,1)} %collective-permute-done.5.refs_0_, bf16[2,2,1024,512]{3,2,1,0:T(8,128)(2,1)S(1)} %copy-done.12), custom_call_target="tpu_custom_call" | custom-call | flops 99999997952 | bytes 1 | tf_op jit(solution)/shard_map/late_kept/pallas_call | solution.py:294
  66.3 1.8 %collective-permute-start.10 = (bf16[256,512]{1,0:T(8,128)(2,1)S(1)}, bf16[256,512]{1,0:T(8,128)(2,1)S(1)}, u32[]{:S(2)}, u32[]{:S(2)}) collective-permute-start(bf16[256,512]{1,0:T(8,128)(2,1)S(1)} %get-tuple-element.90), channel_id=1, source_target_pairs={{0,4},{4,0},{8,12},{12,8},{1,5},{5,1},{9,13},{13,9},{2,6},{6,2},{1... | collective-permute-start | bytes 786440 | tf_op jit(solution)/shard_map/ppermute | solution.py:105
  68.1 0.1 fusion.11
  68.2 1.6 %collective-permute-start.9 = (bf16[128,512]{1,0:T(8,128)(2,1)S(1)}, bf16[128,512]{1,0:T(8,128)(2,1)S(1)}, u32[]{:S(2)}, u32[]{:S(2)}) collective-permute-start(bf16[128,512]{1,0:T(8,128)(2,1)S(1)} %get-tuple-element.117), channel_id=1, source_target_pairs={{0,2},{2,0},{1,3},{3,1},{4,6},{6,4},{5,7},{7,5},{8,10},{10,8},{9,1... | collective-permute-start | bytes 393224 | tf_op jit(solution)/shard_map/ppermute | solution.py:101
  69.8 3.9 %prefix_attend.4 = (f32[128,4096]{1,0:T(8,128)S(1)}, f32[8,4096]{1,0:T(8,128)S(1)}) custom-call(bf16[8192,128]{1,0:T(8,128)(2,1)S(1)} %bitcast.47, bf16[1024,256]{1,0:T(8,128)(2,1)S(1)} %copy-done.18, bf16[288,1024]{1,0:T(8,128)(2,1)S(1)} %copy-done.16), custom_call_target="tpu_custom_call" | custom-call | flops 99999997952 | bytes 1 | tf_op jit(solution)/shard_map/prefix_attend/pallas_call | solution.py:428
  73.6 1.4 %collective-permute-done.10 = bf16[256,512]{1,0:T(8,128)(2,1)S(1)} collective-permute-done((bf16[256,512]{1,0:T(8,128)(2,1)S(1)}, bf16[256,512]{1,0:T(8,128)(2,1)S(1)}, u32[]{:S(2)}, u32[]{:S(2)}) %collective-permute-start.10) | collective-permute-done | bytes 262176 | tf_op jit(solution)/shard_map/ppermute | solution.py:105
  75.1 0.1 fusion.6
  75.2 1.6 %collective-permute-start.14 = (bf16[128,512]{1,0:T(8,128)(2,1)S(1)}, bf16[128,512]{1,0:T(8,128)(2,1)S(1)}, u32[]{:S(2)}, u32[]{:S(2)}) collective-permute-start(bf16[128,512]{1,0:T(8,128)(2,1)S(1)} %get-tuple-element.105), channel_id=1, source_target_pairs={{0,2},{2,0},{1,3},{3,1},{4,6},{6,4},{5,7},{7,5},{8,10},{10,8},{9,1... | collective-permute-start | bytes 393224 | tf_op jit(solution)/shard_map/ppermute | solution.py:101
  76.7 1.0 collective-permute-start.13
  77.7 1.3 %collective-permute-start.12 = (bf16[256,512]{1,0:T(8,128)(2,1)S(1)}, bf16[256,512]{1,0:T(8,128)(2,1)S(1)}, u32[]{:S(2)}, u32[]{:S(2)}) collective-permute-start(bf16[256,512]{1,0:T(8,128)(2,1)S(1)} %get-tuple-element.103), channel_id=1, source_target_pairs={{0,4},{4,0},{8,12},{12,8},{1,5},{5,1},{9,13},{13,9},{2,6},{6,2},{1... | collective-permute-start | bytes 786440 | tf_op jit(solution)/shard_map/ppermute | solution.py:105
  79.1 3.9 %prefix_attend.5 = (f32[128,4096]{1,0:T(8,128)S(1)}, f32[8,4096]{1,0:T(8,128)S(1)}) custom-call(bf16[8192,128]{1,0:T(8,128)(2,1)S(1)} %bitcast.48, bf16[1024,256]{1,0:T(8,128)(2,1)S(1)} %copy-done.18, bf16[288,1024]{1,0:T(8,128)(2,1)S(1)} %copy-done.16, f32[128,4096]{1,0:T(8,128)S(1)} %get-tuple-element.96.refs_0_, ...), custom_call_target="tpu_custom_call", output_to_operand_aliasing={{0}: (3, {}), {1}: (4, {})} | custom-call | flops 99999997952 | bytes 1 | tf_op jit(solution)/shard_map/prefix_attend/pallas_call | solution.py:428
  82.9 0.1 fusion.9
  83.0 2.4 %collective-permute-done.13.rest_4_ = bf16[128,512]{1,0:T(8,128)(2,1)S(1)} collective-permute-done((bf16[128,512]{1,0:T(8,128)(2,1)S(1)}, bf16[128,512]{1,0:T(8,128)(2,1)S(1)}, u32[]{:S(2)}, u32[]{:S(2)}) %collective-permute-start.13) | collective-permute-done | bytes 131104 | tf_op jit(solution)/shard_map/ppermute | solution.py:105
  85.4 0.0 collective-permute-start.15
  85.4 3.9 %collective-permute-done.12.rest_3_.rest_4_ = bf16[256,512]{1,0:T(8,128)(2,1)S(1)} collective-permute-done((bf16[256,512]{1,0:T(8,128)(2,1)S(1)}, bf16[256,512]{1,0:T(8,128)(2,1)S(1)}, u32[]{:S(2)}, u32[]{:S(2)}) %collective-permute-start.12) | collective-permute-done | bytes 262176 | tf_op jit(solution)/shard_map/ppermute | solution.py:105
  89.3 5.6 %fresh_attend.2 = (bf16[8192,128]{1,0:T(8,128)(2,1)}, bf16[128,512]{1,0:T(8,128)(2,1)S(1)}) custom-call(s32[1]{0:T(128)S(6)} %copy.17.length_ref, bf16[8192,128]{1,0:T(8,128)(2,1)S(1)} %bitcast.49, f32[128,4096]{1,0:T(8,128)S(1)} %get-tuple-element.100.acc_ref, f32[8,4096]{1,0:T(8,128)S(1)} %get-tuple-element.101.stat_ref, f32[2,256,512]{2,1,0:T(8,128)S(1)} %copy-done.14, ...), custom_call_target="tpu_custom_call" | custom-call | flops 99999997952 | bytes 1 | tf_op jit(solution)/shard_map/fresh_attend/pallas_call | solution.py:513
  94.9 6.3 %fresh_attend.3 = (bf16[8192,128]{1,0:T(8,128)(2,1)}, bf16[128,512]{1,0:T(8,128)(2,1)}) custom-call(s32[1]{0:T(128)S(6)} %copy.17.length_ref, bf16[8192,128]{1,0:T(8,128)(2,1)S(1)} %bitcast.50, f32[128,4096]{1,0:T(8,128)S(1)} %get-tuple-element.98.acc_ref, f32[8,4096]{1,0:T(8,128)S(1)} %get-tuple-element.99.stat_ref, ...), custom_call_target="tpu_custom_call", output_to_operand_aliasing={{0}: (10, {})} | custom-call | flops 99999997952 | bytes 1 | tf_op jit(solution)/shard_map/fresh_attend/pallas_call | solution.py:513
  (42 shorter events, 0.1 us)
Async XLA Ops:
  0.6 8.2 %copy-start.4 = (s32[3]{0:T(128)S(1)}, s32[3]{0:T(128)}, u32[]{:S(2)}) copy-start(s32[3]{0:T(128)} %pad_add_fusion.place_ref) | copy-start | bytes 40
  0.6 8.2 %copy-start.5 = (bf16[8,128,4,1,256]{4,2,3,1,0:T(4,128)(2,1)S(1)}, bf16[8,128,4,1,256]{4,2,3,1,0:T(4,128)(2,1)}, u32[]{:S(2)}) copy-start(bf16[8,128,4,1,256]{4,2,3,1,0:T(4,128)(2,1)} %param.11) | copy-start | bytes 6291460
  3.7 18.3 %collective-permute-start = (bf16[256,1024]{1,0:T(8,128)(2,1)}, bf16[256,1024]{1,0:T(8,128)(2,1)}, u32[]{:S(2)}, u32[]{:S(2)}) collective-permute-start(bf16[256,1024]{1,0:T(8,128)(2,1)} %get-tuple-element.63), channel_id=1, source_target_pairs={{0,12},{4,8},{8,4},{12,0},{1,13},{5,9},{9,5},{13,1},{2,14},{6,10},... | collective-permute-start | bytes 1572872 | tf_op jit(solution)/shard_map/ppermute | solution.py:105
  8.8 24.6 %collective-permute-start.1 = (bf16[256,1024]{1,0:T(8,128)(2,1)}, bf16[256,1024]{1,0:T(8,128)(2,1)}, u32[]{:S(2)}, u32[]{:S(2)}) collective-permute-start(bf16[256,1024]{1,0:T(8,128)(2,1)} %get-tuple-element.64), channel_id=1, source_target_pairs={{0,4},{4,0},{8,12},{12,8},{1,5},{5,1},{9,13},{13,9},{2,6},{6,2},{1... | collective-permute-start | bytes 1572872 | tf_op jit(solution)/shard_map/ppermute | solution.py:105
  8.8 3.0 %copy-start.6 = (bf16[1,1,1024,4,2,128]{5,4,3,2,1,0:T(2,128)(2,1)S(1)}, bf16[1,1,1024,4,2,128]{5,4,3,2,1,0:T(2,128)(2,1)}, u32[]{:S(2)}) copy-start(bf16[1,1,1024,4,2,128]{5,4,3,2,1,0:T(2,128)(2,1)} %param.8) | copy-start | bytes 6291460
  8.8 3.0 %copy-start.7 = (bf16[1,1,1024,4,2,128]{5,4,3,2,1,0:T(2,128)(2,1)S(1)}, bf16[1,1,1024,4,2,128]{5,4,3,2,1,0:T(2,128)(2,1)}, u32[]{:S(2)}) copy-start(bf16[1,1,1024,4,2,128]{5,4,3,2,1,0:T(2,128)(2,1)} %param.9) | copy-start | bytes 6291460
  11.8 2.5 %copy-start.8 = (bf16[256,4096]{1,0:T(8,128)(2,1)S(1)}, bf16[256,4096]{1,0:T(8,128)(2,1)}, u32[]{:S(2)}) copy-start(bf16[256,4096]{1,0:T(8,128)(2,1)} %refs_0_.3) | copy-start | bytes 6291460
  14.3 22.5 %copy-start.11 = (bf16[2,2,1024,512]{3,2,1,0:T(8,128)(2,1)}, bf16[2,2,1024,512]{3,2,1,0:T(8,128)(2,1)S(1)}, u32[]{:S(2)}) copy-start(bf16[2,2,1024,512]{3,2,1,0:T(8,128)(2,1)S(1)} %arrange_weights.1.refs_1_.refs_2_) | copy-start | bytes 12582916
  16.6 20.2 %collective-permute-start.2 = (bf16[2,256,512]{2,1,0:T(8,128)(2,1)}, bf16[2,256,512]{2,1,0:T(8,128)(2,1)}, u32[]{:S(2)}, u32[]{:S(2)}) collective-permute-start(bf16[2,256,512]{2,1,0:T(8,128)(2,1)} %own_away.1), channel_id=1, source_target_pairs={{0,1},{1,0},{2,3},{3,2},{4,5},{5,4},{6,7},{7,6},{8,9},{9,8},{10,11... | collective-permute-start | bytes 1572872 | tf_op jit(solution)/shard_map/ppermute | solution.py:101
  16.6 26.5 %collective-permute-start.4 = (bf16[8,128,512]{2,1,0:T(8,128)(2,1)}, bf16[8,128,512]{2,1,0:T(8,128)(2,1)}, u32[]{:S(2)}, u32[]{:S(2)}) collective-permute-start(bf16[8,128,512]{2,1,0:T(8,128)(2,1)} %get-tuple-element.74), channel_id=1, source_target_pairs={{0,2},{2,0},{1,3},{3,1},{4,6},{6,4},{5,7},{7,5},{8,10},{10,8},{9,1... | collective-permute-start | bytes 3145736 | tf_op jit(solution)/shard_map/ppermute | solution.py:101
  18.1 37.9 %collective-permute-start.5 = (bf16[256,1024]{1,0:T(8,128)(2,1)}, bf16[256,1024]{1,0:T(8,128)(2,1)}, u32[]{:S(2)}, u32[]{:S(2)}) collective-permute-start(bf16[256,1024]{1,0:T(8,128)(2,1)} %get-tuple-element.81), channel_id=1, source_target_pairs={{0,8},{4,12},{8,0},{12,4},{1,9},{5,13},{9,1},{13,5},{2,10},{6,14},... | collective-permute-start | bytes 1572872 | tf_op jit(solution)/shard_map/ppermute | solution.py:105
  20.4 16.4 %copy-start.13 = (f32[2,256,512]{2,1,0:T(8,128)}, f32[2,256,512]{2,1,0:T(8,128)S(1)}, u32[]{:S(2)}) copy-start(f32[2,256,512]{2,1,0:T(8,128)S(1)} %own_kept.1.refs_3_.rest_0_.rest_1_) | copy-start | bytes 3145732
  36.7 5.2 %collective-permute-start.3 = (bf16[2,512,512]{2,1,0:T(8,128)(2,1)S(1)}, bf16[2,512,512]{2,1,0:T(8,128)(2,1)S(1)}, u32[]{:S(2)}, u32[]{:S(2)}) collective-permute-start(bf16[2,512,512]{2,1,0:T(8,128)(2,1)S(1)} %early_away.1), channel_id=1, source_target_pairs={{0,1},{1,0},{2,3},{3,2},{4,5},{5,4},{6,7},{7,6},{8,9},{9,8},{10,11... | collective-permute-start | bytes 3145736 | tf_op jit(solution)/shard_map/ppermute | solution.py:101
  40.5 7.6 %copy-start = (f32[2,512,512]{2,1,0:T(8,128)}, f32[2,512,512]{2,1,0:T(8,128)S(1)}, u32[]{:S(2)}) copy-start(f32[2,512,512]{2,1,0:T(8,128)S(1)} %get-tuple-element.72.refs_2_.refs_5_) | copy-start | bytes 6291460
  40.5 4.6 %copy-start.10 = (s32[1,8]{1,0:T(1,128)S(1)}, s32[1,8]{1,0:T(1,128)}, u32[]{:S(2)}) copy-start(s32[1,8]{1,0:T(1,128)} %param.12) | copy-start | bytes 100
  40.5 44.9 %collective-permute-start.11 = (bf16[256,512]{1,0:T(8,128)(2,1)}, bf16[256,512]{1,0:T(8,128)(2,1)}, u32[]{:S(2)}, u32[]{:S(2)}) collective-permute-start(bf16[256,512]{1,0:T(8,128)(2,1)} %get-tuple-element.102), channel_id=1, source_target_pairs={{0,2},{2,0},{1,3},{3,1},{4,6},{6,4},{5,7},{7,5},{8,10},{10,8},{9,1... | collective-permute-start | bytes 786440 | tf_op jit(solution)/shard_map/ppermute | solution.py:101
  41.9 6.2 %copy-start.2 = (bf16[2,512,512]{2,1,0:T(8,128)(2,1)}, bf16[2,512,512]{2,1,0:T(8,128)(2,1)S(1)}, u32[]{:S(2)}) copy-start(bf16[2,512,512]{2,1,0:T(8,128)(2,1)S(1)} %collective-permute-done.3.refs_3_.refs_6_) | copy-start | bytes 3145732
  43.1 12.9 %collective-permute-start.6 = (bf16[256,512]{1,0:T(8,128)(2,1)}, bf16[256,512]{1,0:T(8,128)(2,1)}, u32[]{:S(2)}, u32[]{:S(2)}) collective-permute-start(bf16[256,512]{1,0:T(8,128)(2,1)} %get-tuple-element.83), channel_id=1, source_target_pairs={{0,2},{2,0},{1,3},{3,1},{4,6},{6,4},{5,7},{7,5},{8,10},{10,8},{9,1... | collective-permute-start | bytes 786440 | tf_op jit(solution)/shard_map/ppermute | solution.py:101
  44.0 16.8 %collective-permute-start.7 = (bf16[256,512]{1,0:T(8,128)(2,1)}, bf16[256,512]{1,0:T(8,128)(2,1)}, u32[]{:S(2)}, u32[]{:S(2)}) collective-permute-start(bf16[256,512]{1,0:T(8,128)(2,1)} %get-tuple-element.84), channel_id=1, source_target_pairs={{0,2},{2,0},{1,3},{3,1},{4,6},{6,4},{5,7},{7,5},{8,10},{10,8},{9,1... | collective-permute-start | bytes 786440 | tf_op jit(solution)/shard_map/ppermute | solution.py:101
  45.1 3.1 %copy-start.9 = (bf16[256,2,1,2048]{3,1,2,0:T(2,128)(2,1)S(1)}, bf16[256,2,1,2048]{3,1,2,0:T(2,128)(2,1)}, u32[]{:S(2)}) copy-start(bf16[256,2,1,2048]{3,1,2,0:T(2,128)(2,1)} %param.10) | copy-start | bytes 6291460
  48.1 7.8 %copy-start.15 = (bf16[288,1024]{1,0:T(8,128)(2,1)}, bf16[288,1024]{1,0:T(8,128)(2,1)S(1)}, u32[]{:S(2)}) copy-start(bf16[288,1024]{1,0:T(8,128)(2,1)S(1)} %get-tuple-element.87.values) | copy-start | bytes 1769476
  48.2 7.8 %copy-start.17 = (bf16[1024,256]{1,0:T(8,128)(2,1)}, bf16[1024,256]{1,0:T(8,128)(2,1)S(1)}, u32[]{:S(2)}) copy-start(bf16[1024,256]{1,0:T(8,128)(2,1)S(1)} %get-tuple-element.86.keys) | copy-start | bytes 1572868
  48.2 12.6 %copy-start.1 = (f32[2,512,512]{2,1,0:T(8,128)S(1)}, f32[2,512,512]{2,1,0:T(8,128)}, u32[]{:S(2)}) copy-start(f32[2,512,512]{2,1,0:T(8,128)} %copy-done) | copy-start | bytes 6291460
  48.2 12.6 %copy-start.3 = (bf16[2,512,512]{2,1,0:T(8,128)(2,1)S(1)}, bf16[2,512,512]{2,1,0:T(8,128)(2,1)}, u32[]{:S(2)}) copy-start(bf16[2,512,512]{2,1,0:T(8,128)(2,1)} %copy-done.2) | copy-start | bytes 3145732
  48.2 12.6 %copy-start.12 = (bf16[2,2,1024,512]{3,2,1,0:T(8,128)(2,1)S(1)}, bf16[2,2,1024,512]{3,2,1,0:T(8,128)(2,1)}, u32[]{:S(2)}) copy-start(bf16[2,2,1024,512]{3,2,1,0:T(8,128)(2,1)} %copy-done.11) | copy-start | bytes 12582916
  63.7 6.1 %copy-start.16 = (bf16[288,1024]{1,0:T(8,128)(2,1)S(1)}, bf16[288,1024]{1,0:T(8,128)(2,1)}, u32[]{:S(2)}) copy-start(bf16[288,1024]{1,0:T(8,128)(2,1)} %copy-done.15) | copy-start | bytes 1769476
  63.7 6.1 %copy-start.18 = (bf16[1024,256]{1,0:T(8,128)(2,1)S(1)}, bf16[1024,256]{1,0:T(8,128)(2,1)}, u32[]{:S(2)}) copy-start(bf16[1024,256]{1,0:T(8,128)(2,1)} %copy-done.17) | copy-start | bytes 1572868
  63.7 4.4 %collective-permute-start.8 = (bf16[2,256,512]{2,1,0:T(8,128)(2,1)S(1)}, bf16[2,256,512]{2,1,0:T(8,128)(2,1)S(1)}, u32[]{:S(2)}, u32[]{:S(2)}) collective-permute-start(bf16[2,256,512]{2,1,0:T(8,128)(2,1)S(1)} %get-tuple-element.85), channel_id=1, source_target_pairs={{0,1},{1,0},{2,3},{3,2},{4,5},{5,4},{6,7},{7,6},{8,9},{9,8},{10,11... | collective-permute-start | bytes 1572872 | tf_op jit(solution)/shard_map/ppermute | solution.py:101
  66.3 8.8 %collective-permute-start.10 = (bf16[256,512]{1,0:T(8,128)(2,1)S(1)}, bf16[256,512]{1,0:T(8,128)(2,1)S(1)}, u32[]{:S(2)}, u32[]{:S(2)}) collective-permute-start(bf16[256,512]{1,0:T(8,128)(2,1)S(1)} %get-tuple-element.90), channel_id=1, source_target_pairs={{0,4},{4,0},{8,12},{12,8},{1,5},{5,1},{9,13},{13,9},{2,6},{6,2},{1... | collective-permute-start | bytes 786440 | tf_op jit(solution)/shard_map/ppermute | solution.py:105
  68.2 6.9 %collective-permute-start.9 = (bf16[128,512]{1,0:T(8,128)(2,1)S(1)}, bf16[128,512]{1,0:T(8,128)(2,1)S(1)}, u32[]{:S(2)}, u32[]{:S(2)}) collective-permute-start(bf16[128,512]{1,0:T(8,128)(2,1)S(1)} %get-tuple-element.117), channel_id=1, source_target_pairs={{0,2},{2,0},{1,3},{3,1},{4,6},{6,4},{5,7},{7,5},{8,10},{10,8},{9,1... | collective-permute-start | bytes 393224 | tf_op jit(solution)/shard_map/ppermute | solution.py:101
  75.2 14.2 %copy-start.14 = (f32[2,256,512]{2,1,0:T(8,128)S(1)}, f32[2,256,512]{2,1,0:T(8,128)}, u32[]{:S(2)}) copy-start(f32[2,256,512]{2,1,0:T(8,128)} %copy-done.13) | copy-start | bytes 3145732
  75.2 7.8 %collective-permute-start.14 = (bf16[128,512]{1,0:T(8,128)(2,1)S(1)}, bf16[128,512]{1,0:T(8,128)(2,1)S(1)}, u32[]{:S(2)}, u32[]{:S(2)}) collective-permute-start(bf16[128,512]{1,0:T(8,128)(2,1)S(1)} %get-tuple-element.105), channel_id=1, source_target_pairs={{0,2},{2,0},{1,3},{3,1},{4,6},{6,4},{5,7},{7,5},{8,10},{10,8},{9,1... | collective-permute-start | bytes 393224 | tf_op jit(solution)/shard_map/ppermute | solution.py:101
  76.7 8.7 %collective-permute-start.13 = (bf16[128,512]{1,0:T(8,128)(2,1)S(1)}, bf16[128,512]{1,0:T(8,128)(2,1)S(1)}, u32[]{:S(2)}, u32[]{:S(2)}) collective-permute-start(bf16[128,512]{1,0:T(8,128)(2,1)S(1)} %fusion.6), channel_id=1, source_target_pairs={{0,8},{4,12},{8,0},{12,4},{1,9},{5,13},{9,1},{13,5},{2,10},{6,14},... | collective-permute-start | bytes 393224 | tf_op jit(solution)/shard_map/ppermute | solution.py:105
  77.7 11.6 %collective-permute-start.12 = (bf16[256,512]{1,0:T(8,128)(2,1)S(1)}, bf16[256,512]{1,0:T(8,128)(2,1)S(1)}, u32[]{:S(2)}, u32[]{:S(2)}) collective-permute-start(bf16[256,512]{1,0:T(8,128)(2,1)S(1)} %get-tuple-element.103), channel_id=1, source_target_pairs={{0,4},{4,0},{8,12},{12,8},{1,5},{5,1},{9,13},{13,9},{2,6},{6,2},{1... | collective-permute-start | bytes 786440 | tf_op jit(solution)/shard_map/ppermute | solution.py:105
  85.4 9.5 %collective-permute-start.15 = (bf16[128,512]{1,0:T(8,128)(2,1)S(1)}, bf16[128,512]{1,0:T(8,128)(2,1)S(1)}, u32[]{:S(2)}, u32[]{:S(2)}) collective-permute-start(bf16[128,512]{1,0:T(8,128)(2,1)S(1)} %fusion.9), channel_id=1, source_target_pairs={{0,8},{4,12},{8,0},{12,4},{1,9},{5,13},{9,1},{13,5},{2,10},{6,14},... | collective-permute-start | bytes 393224 | tf_op jit(solution)/shard_map/ppermute | solution.py:105

commit v16 on v12

--- a/solution.py
+++ b/solution.py
@@ -567,8 +567,6 @@
     pools = [shift(part, "ctx", step) if step else part for step, part in enumerate(pools)]
 
     weights = arrange_weights(key_weight, value_weight, ctx_count, heads, head_count)
-    weights, last = after(weights, pieces[-1])
-    last = trade(last, "batch", top)
 
     query_rows = queries.reshape(token_count, heads, group, width)
     query_rows = query_rows.transpose(0, 2, 1, 3).reshape(-1, width)
@@ -590,6 +588,11 @@
 
     every = slice(None)
     parts_of = [slice(i * rows, (i + 1) * rows) for i in range(CHUNKS)]
+
+    weights, last = after(weights, pieces[-1])
+    last = trade(last, "batch", top)
+    own = projected([tokens], "own")
+    own_others = spread(others(own, every))
 
     sums = [[], []]
     if steps:
@@ -609,7 +612,7 @@
     states[0], last = after(states[0], last)
 
     def late_project(step, dtype, name, sums):
-        result = project(place, [last, tokens], weights, step, dtype, name, sums)
+        result = project(place, [last], weights, step, dtype, name, sums)
         return result if sums else (result,)
 
     terms = []
@@ -620,13 +623,12 @@
     far, near = far[:1], far[1:]
     late = [kept, *terms]
     far = [trade(part, "batch", 1) for part in far]
-    own_at = slice(token_count, 2 * token_count)
-    *late_others, own_others = [others(late, here) for here in [*parts_of, own_at]]
+    late_others = [others(late, here) for here in parts_of]
     late_others[0] = spread(late_others[0])
     late_others[1], (keys, values) = after(late_others[1], (keys, values))
     state = prefix_attend(query_rows, keys, values, 1, scale, heads, (0, 2))
-    state, (late_others[1], own_others, near) = after(state, (late_others[1], own_others, near))
-    late_others[1], own_others = spread(late_others[1]), spread(own_others)
+    state, (late_others[1], near) = after(state, (late_others[1], near))
+    late_others[1] = spread(late_others[1])
     near = [trade(part, "batch", 1) for part in near]
 
     away = []
@@ -641,13 +643,13 @@
             away[-1], part = after(away[-1], part)
         away.append(trade(part, "batch", top))
     states.append(prefix_attend(query_rows, keys, values, 1, scale, heads, (1, 2), state))
+    home = added(own, 0, every) + sum(p.astype(jnp.float32) for p in (*own_others, *near))
+    home, away[0] = after(home, away[0])
 
     result = None
     fresh = []
     for chunk in range(CHUNKS):
-        pieces = [piece_of(t, rows, CHUNKS + chunk, 0) for t in late]
-        pieces += [piece_of(part, rows, chunk) for part in (*own_others, *near)]
-        pieces.append(piece_of(away[chunk], rows, 0))
+        pieces = [piece_of(home, rows, chunk), piece_of(away[chunk], rows, 0)]
         result, new = fresh_attend(
             lengths,
             query_rows,

time: 93.8 us -> 96.6 us (1.030)
  starting transfers between devices: 19.8 us -> 16.4 us
  other arithmetic: 1.87 us -> 4.71 us
  Pallas kernels: 50.3 us -> 52.7 us
    ppermute x7, starting transfers between devices: 12.5 us -> 9.19 us  [trade(): lax.ppermute(array, axis, [(i, i ^ bits) for i in range(lax.axis_size(axi...]
    pallas_call x4 -> x6, Pallas kernels: 13.3 us -> 15.7 us  [project(): pl.pallas_call(functools.partial(project_kernel, len(blocks), [len(terms)...]
    convert_element_type x3, other arithmetic: 1.09 us -> 2.77 us  [others(): added(terms, step, here).astype(jnp.bfloat16)]
    add x0 -> x1, other arithmetic: none -> 1.16 us  [reduced_shards(): added(own, 0, every)]
    ppermute x8 -> x9, starting transfers between devices: 7.3 us -> 7.19 us  [shift(): lax.ppermute(array, axis, [(i, (i + step) % count) for i in range(count)])]
  transfers between devices with their start and end apart: 15 -> 16, of which waited for: 4 -> 6; matrix products, arithmetic and copies ran while one was open for 1% -> 4% of each run, Pallas kernels for 41% -> 46%
where the time goes in v16:
time: 96.6 us; the launch traced here: 96.3 us
  Pallas kernels  52.7 us (55%)
  waiting for transfers between devices  21.4 us (22%)
  starting transfers between devices  16.4 us (17%)
  other arithmetic  4.71 us (5%)
  between operations  1 us (1%)
    ppermute x7, waiting for transfers between devices, trade(): lax.ppermute(array, axis, [(i, i ^ bits) for i in range(lax.axis_size(axi...  19.8 us
    pallas_call x6, Pallas kernels, project(): pl.pallas_call(functools.partial(project_kernel, len(blocks), [len(terms)...  15.7 us
    pallas_call x3, Pallas kernels, prefix_attend(): pl.pallas_call(functools.partial(prefix_kernel, scale, heads), grid=(step...  15.6 us
    pallas_call x2, Pallas kernels, fresh_attend(): pl.pallas_call(functools.partial(fresh_kernel, scale, heads, per_token, c...  9.97 us
    ppermute x7, starting transfers between devices, trade(): lax.ppermute(array, axis, [(i, i ^ bits) for i in range(lax.axis_size(axi...  9.19 us
    ppermute x9, starting transfers between devices, shift(): lax.ppermute(array, axis, [(i, (i + step) % count) for i in range(count)])  7.19 us
    pallas_call x1, Pallas kernels, cut_tokens(): pl.pallas_call(functools.partial(cut_kernel, bits), grid_spec=pltpu.Prefe...  3.04 us
    pallas_call x1, Pallas kernels, pick_blocks(): pl.pallas_call(functools.partial(pick_kernel, heads, len(pools)), grid_sp...  3.02 us
  transfers between devices with their start and end apart: 16, of which 6 were waited for; matrix products, arithmetic and copies ran while one was open for 4% of the time, Pallas kernels for 46%

profile of v16, /device:TPU:0, one launch (start us, length us, event | category | flops | bytes accessed | tf_op | source)
XLA Modules:
  0.0 96.3 jit_solution(6144691179310790911)
XLA Ops:
  0.0 0.7 pad_add_fusion.place_ref
  0.7 3.0 %cut_tokens.1 = (bf16[256,1024]{1,0:T(8,128)(2,1)}, bf16[256,1024]{1,0:T(8,128)(2,1)}, bf16[256,1024]{1,0:T(8,128)(2,1)}) custom-call(s32[3]{0:T(128)} %pad_add_fusion.place_ref, bf16[256,4096]{1,0:T(8,128)(2,1)} %refs_0_.3), custom_call_target="tpu_custom_call" | custom-call | flops 99999997952 | bytes 1 | tf_op jit(solution)/shard_map/cut_tokens/pallas_call | solution.py:184
  3.7 5.1 %collective-permute-start = (bf16[256,1024]{1,0:T(8,128)(2,1)}, bf16[256,1024]{1,0:T(8,128)(2,1)}, u32[]{:S(2)}, u32[]{:S(2)}) collective-permute-start(bf16[256,1024]{1,0:T(8,128)(2,1)} %get-tuple-element.62), channel_id=1, source_target_pairs={{0,12},{4,8},{8,4},{12,0},{1,13},{5,9},{9,5},{13,1},{2,14},{6,10},... | collective-permute-start | bytes 1572872 | tf_op jit(solution)/shard_map/ppermute | solution.py:105
  8.8 0.0 collective-permute-start.1
  8.8 0.0 copy-start.8
  8.8 0.0 copy-start.9
  8.9 3.0 %arrange_pool.1 = (bf16[8,128,512]{2,1,0:T(8,128)(2,1)S(1)}, bf16[8,128,512]{2,1,0:T(8,128)(2,1)}) custom-call(s32[3]{0:T(128)S(1)} %copy-done.6, bf16[8,128,8,128]{3,2,1,0:T(8,128)(2,1)S(1)} %bitcast.49), custom_call_target="tpu_custom_call" | custom-call | flops 99999997952 | bytes 1 | tf_op jit(solution)/shard_map/arrange_pool/pallas_call | solution.py:234
  11.8 1.5 %collective-permute-start.3 = (bf16[8,128,512]{2,1,0:T(8,128)(2,1)}, bf16[8,128,512]{2,1,0:T(8,128)(2,1)}, u32[]{:S(2)}, u32[]{:S(2)}) collective-permute-start(bf16[8,128,512]{2,1,0:T(8,128)(2,1)} %get-tuple-element.72), channel_id=1, source_target_pairs={{0,2},{2,0},{1,3},{3,1},{4,6},{6,4},{5,7},{7,5},{8,10},{10,8},{9,1... | collective-permute-start | bytes 3145736 | tf_op jit(solution)/shard_map/ppermute | solution.py:101
  13.3 2.5 %arrange_weights.1.refs_2_.refs_1_ = bf16[2,2,1024,512]{3,2,1,0:T(8,128)(2,1)S(1)} custom-call(bf16[1024,8,128]{2,1,0:T(8,128)(2,1)S(1)} %bitcast.50, bf16[1024,8,128]{2,1,0:T(8,128)(2,1)S(1)} %bitcast.51), custom_call_target="tpu_custom_call" | custom-call | flops 99999997952 | bytes 1 | tf_op jit(solution)/shard_map/arrange_weights/pallas_call | solution.py:150
  15.8 0.8 collective-permute-start.4
  16.6 2.2 %own_away.1 = bf16[2,256,512]{2,1,0:T(8,128)(2,1)} custom-call(s32[3]{0:T(128)S(1)} %copy-done.6, bf16[256,4096]{1,0:T(8,128)(2,1)S(1)} %copy-done.10, bf16[2,2,1024,512]{3,2,1,0:T(8,128)(2,1)S(1)} %arrange_weights.1.refs_2_.refs_1_), custom_call_target="tpu_custom_call" | custom-call | flops 99999997952 | bytes 1 | tf_op jit(solution)/shard_map/own_away/pallas_call | solution.py:294
  18.9 1.5 %own_kept.1 = f32[2,256,512]{2,1,0:T(8,128)S(1)} custom-call(s32[3]{0:T(128)S(1)} %copy-done.6, bf16[256,4096]{1,0:T(8,128)(2,1)S(1)} %copy-done.10, bf16[2,2,1024,512]{3,2,1,0:T(8,128)(2,1)S(1)} %arrange_weights.1.refs_2_.refs_1_), custom_call_target="tpu_custom_call" | custom-call | flops 99999997952 | bytes 1 | tf_op jit(solution)/shard_map/own_kept/pallas_call | solution.py:294
  21.1 0.9 collective-permute-done.refs_0_
  22.0 11.5 %collective-permute-done.1.refs_1_ = bf16[256,1024]{1,0:T(8,128)(2,1)} collective-permute-done((bf16[256,1024]{1,0:T(8,128)(2,1)}, bf16[256,1024]{1,0:T(8,128)(2,1)}, u32[]{:S(2)}, u32[]{:S(2)}) %collective-permute-start.1) | collective-permute-done | bytes 524320 | tf_op jit(solution)/shard_map/ppermute | solution.py:105
  33.4 3.3 %early_away.1 = bf16[2,512,512]{2,1,0:T(8,128)(2,1)S(1)} custom-call(s32[3]{0:T(128)S(1)} %copy-done.6, bf16[256,1024]{1,0:T(8,128)(2,1)} %collective-permute-done.refs_0_, bf16[256,1024]{1,0:T(8,128)(2,1)} %collective-permute-done.1.refs_1_, bf16[2,2,1024,512]{3,2,1,0:T(8,128)(2,1)S(1)} %arrange_weights.1.refs_2_.refs_1_), custom_call_target="tpu_custom_call" | custom-call | flops 99999997952 | bytes 1 | tf_op jit(solution)/shard_map/early_away/pallas_call | solution.py:294
  36.7 0.1 collective-permute-start.2
  36.8 1.7 %fusion.7 = bf16[256,512]{1,0:T(8,128)(2,1)} fusion(f32[2,256,512]{2,1,0:T(8,128)S(1)} %own_kept.1, bf16[2,256,512]{2,1,0:T(8,128)(2,1)} %collective-permute-done.10), kind=kLoop, calls=%fused_computation.11 | loop fusion | flops 393216 | bytes 1048576 | tf_op jit(solution)/shard_map/convert_element_type | solution.py:584
  38.6 1.4 %collective-permute-start.11 = (bf16[256,512]{1,0:T(8,128)(2,1)}, bf16[256,512]{1,0:T(8,128)(2,1)}, u32[]{:S(2)}, u32[]{:S(2)}) collective-permute-start(bf16[256,512]{1,0:T(8,128)(2,1)} %fusion.7), channel_id=1, source_target_pairs={{0,2},{2,0},{1,3},{3,1},{4,6},{6,4},{5,7},{7,5},{8,10},{10,8},{9,1... | collective-permute-start | bytes 786440 | tf_op jit(solution)/shard_map/ppermute | solution.py:101
  39.9 3.3 %early_kept.1.refs_2_.refs_5_ = f32[2,512,512]{2,1,0:T(8,128)S(1)} custom-call(s32[3]{0:T(128)S(1)} %copy-done.6, bf16[256,1024]{1,0:T(8,128)(2,1)} %collective-permute-done.refs_0_, bf16[256,1024]{1,0:T(8,128)(2,1)} %collective-permute-done.1.refs_1_, bf16[2,2,1024,512]{3,2,1,0:T(8,128)(2,1)S(1)} %arrange_weights.1.refs_2_.refs_1_), custom_call_target="tpu_custom_call" | custom-call | flops 99999997952 | bytes 1 | tf_op jit(solution)/shard_map/early_kept/pallas_call | solution.py:294
  43.2 0.0 copy-start.2
  43.2 0.0 copy-start.12
  43.3 0.9 fusion.6
  44.2 0.6 collective-permute-start.5
  44.9 1.4 %collective-permute-start.6 = (bf16[256,512]{1,0:T(8,128)(2,1)}, bf16[256,512]{1,0:T(8,128)(2,1)}, u32[]{:S(2)}, u32[]{:S(2)}) collective-permute-start(bf16[256,512]{1,0:T(8,128)(2,1)} %get-tuple-element.82), channel_id=1, source_target_pairs={{0,2},{2,0},{1,3},{3,1},{4,6},{6,4},{5,7},{7,5},{8,10},{10,8},{9,1... | collective-permute-start | bytes 786440 | tf_op jit(solution)/shard_map/ppermute | solution.py:101
  46.2 3.0 %pick_blocks.1 = (bf16[1024,256]{1,0:T(8,128)(2,1)S(1)}, bf16[288,1024]{1,0:T(8,128)(2,1)S(1)}) custom-call(s32[3]{0:T(128)S(1)} %copy-done.6, s32[8]{0:T(128)S(1)} %bitcast.57, bf16[8,128,512]{2,1,0:T(8,128)(2,1)S(1)} %get-tuple-element.73.refs_0_, bf16[8,128,512]{2,1,0:T(8,128)(2,1)} %collective-permute-done.3.refs_1_), custom_call_target="tpu_custom_call" | custom-call | flops 99999997952 | bytes 1 | tf_op jit(solution)/shard_map/pick_blocks/pallas_call | solution.py:358
  49.3 0.0 copy-start.3
  49.3 7.8 %prefix_attend.3 = (f32[128,4096]{1,0:T(8,128)S(1)}, f32[8,4096]{1,0:T(8,128)S(1)}) custom-call(bf16[8192,128]{1,0:T(8,128)(2,1)S(1)} %bitcast.52, bf16[1024,256]{1,0:T(8,128)(2,1)S(1)} %get-tuple-element.84.keys, bf16[288,1024]{1,0:T(8,128)(2,1)S(1)} %get-tuple-element.85.values), custom_call_target="tpu_custom_call" | custom-call | flops 99999997952 | bytes 1 | tf_op jit(solution)/shard_map/prefix_attend/pallas_call | solution.py:428
  57.2 1.6 %collective-permute-done.6.refs_7_ = bf16[256,512]{1,0:T(8,128)(2,1)} collective-permute-done((bf16[256,512]{1,0:T(8,128)(2,1)}, bf16[256,512]{1,0:T(8,128)(2,1)}, u32[]{:S(2)}, u32[]{:S(2)}) %collective-permute-start.6) | collective-permute-done | bytes 262176 | tf_op jit(solution)/shard_map/ppermute | solution.py:101
  58.8 2.9 %late_away.1 = (bf16[2,256,512]{2,1,0:T(8,128)(2,1)S(1)}, bf16[256,512]{1,0:T(8,128)(2,1)S(1)}, bf16[256,512]{1,0:T(8,128)(2,1)S(1)}) custom-call(s32[3]{0:T(128)S(1)} %copy-done.6, bf16[256,1024]{1,0:T(8,128)(2,1)} %collective-permute-done.4.refs_0_, bf16[2,2,1024,512]{3,2,1,0:T(8,128)(2,1)S(1)} %copy-done.14, f32[2,512,512]{2,1,0:T(8,128)S(1)} %copy-done.3, ...), custom_call_target="tpu_custom_call" | custom-call | flops 99999997952 | bytes 1 | tf_op jit(solution)/shard_map/late_away/pallas_call | solution.py:294
  61.7 0.1 collective-permute-start.7
  61.8 2.5 %late_kept.1 = f32[2,256,512]{2,1,0:T(8,128)S(1)} custom-call(s32[3]{0:T(128)S(1)} %copy-done.6, bf16[256,1024]{1,0:T(8,128)(2,1)} %collective-permute-done.4.refs_0_, bf16[2,2,1024,512]{3,2,1,0:T(8,128)(2,1)S(1)} %copy-done.14), custom_call_target="tpu_custom_call" | custom-call | flops 99999997952 | bytes 1 | tf_op jit(solution)/shard_map/late_kept/pallas_call | solution.py:294
  64.3 1.8 %collective-permute-start.9 = (bf16[256,512]{1,0:T(8,128)(2,1)S(1)}, bf16[256,512]{1,0:T(8,128)(2,1)S(1)}, u32[]{:S(2)}, u32[]{:S(2)}) collective-permute-start(bf16[256,512]{1,0:T(8,128)(2,1)S(1)} %get-tuple-element.86), channel_id=1, source_target_pairs={{0,4},{4,0},{8,12},{12,8},{1,5},{5,1},{9,13},{13,9},{2,6},{6,2},{1... | collective-permute-start | bytes 786440 | tf_op jit(solution)/shard_map/ppermute | solution.py:105
  66.1 0.1 fusion.17
  66.2 1.6 %collective-permute-start.8 = (bf16[128,512]{1,0:T(8,128)(2,1)S(1)}, bf16[128,512]{1,0:T(8,128)(2,1)S(1)}, u32[]{:S(2)}, u32[]{:S(2)}) collective-permute-start(bf16[128,512]{1,0:T(8,128)(2,1)S(1)} %get-tuple-element.115), channel_id=1, source_target_pairs={{0,2},{2,0},{1,3},{3,1},{4,6},{6,4},{5,7},{7,5},{8,10},{10,8},{9,1... | collective-permute-start | bytes 393224 | tf_op jit(solution)/shard_map/ppermute | solution.py:101
  67.8 3.9 %prefix_attend.4 = (f32[128,4096]{1,0:T(8,128)S(1)}, f32[8,4096]{1,0:T(8,128)S(1)}) custom-call(bf16[8192,128]{1,0:T(8,128)(2,1)S(1)} %bitcast.53, bf16[1024,256]{1,0:T(8,128)(2,1)S(1)} %get-tuple-element.84.keys, bf16[288,1024]{1,0:T(8,128)(2,1)S(1)} %copy-done.16), custom_call_target="tpu_custom_call" | custom-call | flops 99999997952 | bytes 1 | tf_op jit(solution)/shard_map/prefix_attend/pallas_call | solution.py:428
  71.7 0.6 collective-permute-start.14
  72.3 0.3 collective-permute-start.12
  72.5 0.6 collective-permute-done.9
  73.1 0.1 fusion.12
  73.2 1.1 %collective-permute-start.13 = (bf16[128,512]{1,0:T(8,128)(2,1)S(1)}, bf16[128,512]{1,0:T(8,128)(2,1)S(1)}, u32[]{:S(2)}, u32[]{:S(2)}) collective-permute-start(bf16[128,512]{1,0:T(8,128)(2,1)S(1)} %fusion.12), channel_id=1, source_target_pairs={{0,8},{4,12},{8,0},{12,4},{1,9},{5,13},{9,1},{13,5},{2,10},{6,14},... | collective-permute-start | bytes 393224 | tf_op jit(solution)/shard_map/ppermute | solution.py:105
  74.3 3.9 %prefix_attend.5 = (f32[128,4096]{1,0:T(8,128)S(1)}, f32[8,4096]{1,0:T(8,128)S(1)}) custom-call(bf16[8192,128]{1,0:T(8,128)(2,1)S(1)} %bitcast.54, bf16[1024,256]{1,0:T(8,128)(2,1)S(1)} %get-tuple-element.84.keys, bf16[288,1024]{1,0:T(8,128)(2,1)S(1)} %copy-done.16, ...), custom_call_target="tpu_custom_call", output_to_operand_aliasing={{0}: (3, {}), {1}: (4, {})} | custom-call | flops 99999997952 | bytes 1 | tf_op jit(solution)/shard_map/prefix_attend/pallas_call | solution.py:428
  78.2 0.1 fusion.15
  78.2 4.7 %collective-permute-done.12 = bf16[256,512]{1,0:T(8,128)(2,1)S(1)} collective-permute-done((bf16[256,512]{1,0:T(8,128)(2,1)S(1)}, bf16[256,512]{1,0:T(8,128)(2,1)S(1)}, u32[]{:S(2)}, u32[]{:S(2)}) %collective-permute-start.12) | collective-permute-done | bytes 262176 | tf_op jit(solution)/shard_map/ppermute | solution.py:105
  82.9 1.2 %fusion.2.rest_0_.rest_1_ = f32[256,512]{1,0:T(8,128)S(1)} fusion(f32[2,256,512]{2,1,0:T(8,128)S(1)} %copy-done.1, bf16[256,512]{1,0:T(8,128)(2,1)S(1)} %collective-permute-done.12, bf16[256,512]{1,0:T(8,128)(2,1)} %collective-permute-done.11, bf16[2,256,512]{2,1,0:T(8,128)(2,1)} %collective-permute-done.10), kind=kLoop, calls=%fused_computation.4 | loop fusion | flops 786432 | bytes 1835008 | tf_op jit(solution)/shard_map/add | solution.py:646
  84.1 0.1 collective-permute-start.15
  84.2 4.7 %fresh_attend.2 = (bf16[8192,128]{1,0:T(8,128)(2,1)}, bf16[128,512]{1,0:T(8,128)(2,1)S(1)}) custom-call(s32[1]{0:T(128)S(6)} %copy.17.length_ref, bf16[8192,128]{1,0:T(8,128)(2,1)S(1)} %bitcast.55, f32[128,4096]{1,0:T(8,128)S(1)} %get-tuple-element.97.acc_ref, f32[8,4096]{1,0:T(8,128)S(1)} %get-tuple-element.98.stat_ref, ...), custom_call_target="tpu_custom_call" | custom-call | flops 99999997952 | bytes 1 | tf_op jit(solution)/shard_map/fresh_attend/pallas_call | solution.py:513
  88.9 2.2 %collective-permute-done.15.rest_2_ = bf16[128,512]{1,0:T(8,128)(2,1)S(1)} collective-permute-done((bf16[128,512]{1,0:T(8,128)(2,1)S(1)}, bf16[128,512]{1,0:T(8,128)(2,1)S(1)}, u32[]{:S(2)}, u32[]{:S(2)}) %collective-permute-start.15) | collective-permute-done | bytes 131104 | tf_op jit(solution)/shard_map/ppermute | solution.py:105
  91.0 5.3 %fresh_attend.3 = (bf16[8192,128]{1,0:T(8,128)(2,1)}, bf16[128,512]{1,0:T(8,128)(2,1)}) custom-call(s32[1]{0:T(128)S(6)} %copy.17.length_ref, bf16[8192,128]{1,0:T(8,128)(2,1)S(1)} %bitcast.56, f32[128,4096]{1,0:T(8,128)S(1)} %get-tuple-element.95.acc_ref, f32[8,4096]{1,0:T(8,128)S(1)} %get-tuple-element.96.stat_ref, ...), custom_call_target="tpu_custom_call", output_to_operand_aliasing={{0}: (7, {})} | custom-call | flops 99999997952 | bytes 1 | tf_op jit(solution)/shard_map/fresh_attend/pallas_call | solution.py:513
  (40 shorter events, 0.1 us)
Async XLA Ops:
  0.7 8.2 %copy-start.6 = (s32[3]{0:T(128)S(1)}, s32[3]{0:T(128)}, u32[]{:S(2)}) copy-start(s32[3]{0:T(128)} %pad_add_fusion.place_ref) | copy-start | bytes 40
  0.7 8.2 %copy-start.7 = (bf16[8,128,4,1,256]{4,2,3,1,0:T(4,128)(2,1)S(1)}, bf16[8,128,4,1,256]{4,2,3,1,0:T(4,128)(2,1)}, u32[]{:S(2)}) copy-start(bf16[8,128,4,1,256]{4,2,3,1,0:T(4,128)(2,1)} %param.11) | copy-start | bytes 6291460
  3.7 18.3 %collective-permute-start = (bf16[256,1024]{1,0:T(8,128)(2,1)}, bf16[256,1024]{1,0:T(8,128)(2,1)}, u32[]{:S(2)}, u32[]{:S(2)}) collective-permute-start(bf16[256,1024]{1,0:T(8,128)(2,1)} %get-tuple-element.62), channel_id=1, source_target_pairs={{0,12},{4,8},{8,4},{12,0},{1,13},{5,9},{9,5},{13,1},{2,14},{6,10},... | collective-permute-start | bytes 1572872 | tf_op jit(solution)/shard_map/ppermute | solution.py:105
  8.8 24.6 %collective-permute-start.1 = (bf16[256,1024]{1,0:T(8,128)(2,1)}, bf16[256,1024]{1,0:T(8,128)(2,1)}, u32[]{:S(2)}, u32[]{:S(2)}) collective-permute-start(bf16[256,1024]{1,0:T(8,128)(2,1)} %get-tuple-element.63), channel_id=1, source_target_pairs={{0,4},{4,0},{8,12},{12,8},{1,5},{5,1},{9,13},{13,9},{2,6},{6,2},{1... | collective-permute-start | bytes 1572872 | tf_op jit(solution)/shard_map/ppermute | solution.py:105
  8.8 4.5 %copy-start.8 = (bf16[1,1,1024,4,2,128]{5,4,3,2,1,0:T(2,128)(2,1)S(1)}, bf16[1,1,1024,4,2,128]{5,4,3,2,1,0:T(2,128)(2,1)}, u32[]{:S(2)}) copy-start(bf16[1,1,1024,4,2,128]{5,4,3,2,1,0:T(2,128)(2,1)} %param.8) | copy-start | bytes 6291460
  8.8 4.5 %copy-start.9 = (bf16[1,1,1024,4,2,128]{5,4,3,2,1,0:T(2,128)(2,1)S(1)}, bf16[1,1,1024,4,2,128]{5,4,3,2,1,0:T(2,128)(2,1)}, u32[]{:S(2)}) copy-start(bf16[1,1,1024,4,2,128]{5,4,3,2,1,0:T(2,128)(2,1)} %param.9) | copy-start | bytes 6291460
  11.8 32.4 %collective-permute-start.3 = (bf16[8,128,512]{2,1,0:T(8,128)(2,1)}, bf16[8,128,512]{2,1,0:T(8,128)(2,1)}, u32[]{:S(2)}, u32[]{:S(2)}) collective-permute-start(bf16[8,128,512]{2,1,0:T(8,128)(2,1)} %get-tuple-element.72), channel_id=1, source_target_pairs={{0,2},{2,0},{1,3},{3,1},{4,6},{6,4},{5,7},{7,5},{8,10},{10,8},{9,1... | collective-permute-start | bytes 3145736 | tf_op jit(solution)/shard_map/ppermute | solution.py:101
  13.3 3.3 %copy-start.10 = (bf16[256,4096]{1,0:T(8,128)(2,1)S(1)}, bf16[256,4096]{1,0:T(8,128)(2,1)}, u32[]{:S(2)}) copy-start(bf16[256,4096]{1,0:T(8,128)(2,1)} %refs_0_.3) | copy-start | bytes 6291460
  15.8 24.1 %copy-start.13 = (bf16[2,2,1024,512]{3,2,1,0:T(8,128)(2,1)}, bf16[2,2,1024,512]{3,2,1,0:T(8,128)(2,1)S(1)}, u32[]{:S(2)}) copy-start(bf16[2,2,1024,512]{3,2,1,0:T(8,128)(2,1)S(1)} %arrange_weights.1.refs_2_.refs_1_) | copy-start | bytes 12582916
  15.8 41.4 %collective-permute-start.4 = (bf16[256,1024]{1,0:T(8,128)(2,1)}, bf16[256,1024]{1,0:T(8,128)(2,1)}, u32[]{:S(2)}, u32[]{:S(2)}) collective-permute-start(bf16[256,1024]{1,0:T(8,128)(2,1)} %get-tuple-element.79), channel_id=1, source_target_pairs={{0,8},{4,12},{8,0},{12,4},{1,9},{5,13},{9,1},{13,5},{2,10},{6,14},... | collective-permute-start | bytes 1572872 | tf_op jit(solution)/shard_map/ppermute | solution.py:105
  18.9 17.9 %collective-permute-start.10 = (bf16[2,256,512]{2,1,0:T(8,128)(2,1)}, bf16[2,256,512]{2,1,0:T(8,128)(2,1)}, u32[]{:S(2)}, u32[]{:S(2)}) collective-permute-start(bf16[2,256,512]{2,1,0:T(8,128)(2,1)} %own_away.1), channel_id=1, source_target_pairs={{0,1},{1,0},{2,3},{3,2},{4,5},{5,4},{6,7},{7,6},{8,9},{9,8},{10,11... | collective-permute-start | bytes 1572872 | tf_op jit(solution)/shard_map/ppermute | solution.py:101
  20.4 16.4 %copy-start = (f32[2,256,512]{2,1,0:T(8,128)}, f32[2,256,512]{2,1,0:T(8,128)S(1)}, u32[]{:S(2)}) copy-start(f32[2,256,512]{2,1,0:T(8,128)S(1)} %own_kept.1) | copy-start | bytes 3145732
  36.7 6.5 %collective-permute-start.2 = (bf16[2,512,512]{2,1,0:T(8,128)(2,1)S(1)}, bf16[2,512,512]{2,1,0:T(8,128)(2,1)S(1)}, u32[]{:S(2)}, u32[]{:S(2)}) collective-permute-start(bf16[2,512,512]{2,1,0:T(8,128)(2,1)S(1)} %early_away.1), channel_id=1, source_target_pairs={{0,1},{1,0},{2,3},{3,2},{4,5},{5,4},{6,7},{7,6},{8,9},{9,8},{10,11... | collective-permute-start | bytes 3145736 | tf_op jit(solution)/shard_map/ppermute | solution.py:101
  38.6 39.7 %collective-permute-start.11 = (bf16[256,512]{1,0:T(8,128)(2,1)}, bf16[256,512]{1,0:T(8,128)(2,1)}, u32[]{:S(2)}, u32[]{:S(2)}) collective-permute-start(bf16[256,512]{1,0:T(8,128)(2,1)} %fusion.7), channel_id=1, source_target_pairs={{0,2},{2,0},{1,3},{3,1},{4,6},{6,4},{5,7},{7,5},{8,10},{10,8},{9,1... | collective-permute-start | bytes 786440 | tf_op jit(solution)/shard_map/ppermute | solution.py:101
  43.2 6.1 %copy-start.2 = (f32[2,512,512]{2,1,0:T(8,128)}, f32[2,512,512]{2,1,0:T(8,128)S(1)}, u32[]{:S(2)}) copy-start(f32[2,512,512]{2,1,0:T(8,128)S(1)} %early_kept.1.refs_2_.refs_5_) | copy-start | bytes 6291460
  43.2 3.0 %copy-start.12 = (s32[1,8]{1,0:T(1,128)S(1)}, s32[1,8]{1,0:T(1,128)}, u32[]{:S(2)}) copy-start(s32[1,8]{1,0:T(1,128)} %param.12) | copy-start | bytes 100
  43.2 6.0 %copy-start.4 = (bf16[2,512,512]{2,1,0:T(8,128)(2,1)}, bf16[2,512,512]{2,1,0:T(8,128)(2,1)S(1)}, u32[]{:S(2)}) copy-start(bf16[2,512,512]{2,1,0:T(8,128)(2,1)S(1)} %collective-permute-done.2.refs_3_.refs_6_) | copy-start | bytes 3145732
  44.2 13.0 %collective-permute-start.5 = (bf16[256,512]{1,0:T(8,128)(2,1)}, bf16[256,512]{1,0:T(8,128)(2,1)}, u32[]{:S(2)}, u32[]{:S(2)}) collective-permute-start(bf16[256,512]{1,0:T(8,128)(2,1)} %get-tuple-element.81), channel_id=1, source_target_pairs={{0,2},{2,0},{1,3},{3,1},{4,6},{6,4},{5,7},{7,5},{8,10},{10,8},{9,1... | collective-permute-start | bytes 786440 | tf_op jit(solution)/shard_map/ppermute | solution.py:101
  44.9 14.0 %collective-permute-start.6 = (bf16[256,512]{1,0:T(8,128)(2,1)}, bf16[256,512]{1,0:T(8,128)(2,1)}, u32[]{:S(2)}, u32[]{:S(2)}) collective-permute-start(bf16[256,512]{1,0:T(8,128)(2,1)} %get-tuple-element.82), channel_id=1, source_target_pairs={{0,2},{2,0},{1,3},{3,1},{4,6},{6,4},{5,7},{7,5},{8,10},{10,8},{9,1... | collective-permute-start | bytes 786440 | tf_op jit(solution)/shard_map/ppermute | solution.py:101
  46.2 3.1 %copy-start.11 = (bf16[256,2,1,2048]{3,1,2,0:T(2,128)(2,1)S(1)}, bf16[256,2,1,2048]{3,1,2,0:T(2,128)(2,1)}, u32[]{:S(2)}) copy-start(bf16[256,2,1,2048]{3,1,2,0:T(2,128)(2,1)} %param.10) | copy-start | bytes 6291460
  49.3 7.9 %copy-start.15 = (bf16[288,1024]{1,0:T(8,128)(2,1)}, bf16[288,1024]{1,0:T(8,128)(2,1)S(1)}, u32[]{:S(2)}) copy-start(bf16[288,1024]{1,0:T(8,128)(2,1)S(1)} %get-tuple-element.85.values) | copy-start | bytes 1769476
  49.3 9.5 %copy-start.3 = (f32[2,512,512]{2,1,0:T(8,128)S(1)}, f32[2,512,512]{2,1,0:T(8,128)}, u32[]{:S(2)}) copy-start(f32[2,512,512]{2,1,0:T(8,128)} %copy-done.2) | copy-start | bytes 6291460
  49.3 9.5 %copy-start.5 = (bf16[2,512,512]{2,1,0:T(8,128)(2,1)S(1)}, bf16[2,512,512]{2,1,0:T(8,128)(2,1)}, u32[]{:S(2)}) copy-start(bf16[2,512,512]{2,1,0:T(8,128)(2,1)} %copy-done.4) | copy-start | bytes 3145732
  49.3 9.5 %copy-start.14 = (bf16[2,2,1024,512]{3,2,1,0:T(8,128)(2,1)S(1)}, bf16[2,2,1024,512]{3,2,1,0:T(8,128)(2,1)}, u32[]{:S(2)}) copy-start(bf16[2,2,1024,512]{3,2,1,0:T(8,128)(2,1)} %copy-done.13) | copy-start | bytes 12582916
  61.7 6.1 %copy-start.16 = (bf16[288,1024]{1,0:T(8,128)(2,1)S(1)}, bf16[288,1024]{1,0:T(8,128)(2,1)}, u32[]{:S(2)}) copy-start(bf16[288,1024]{1,0:T(8,128)(2,1)} %copy-done.15) | copy-start | bytes 1769476
  61.7 4.4 %collective-permute-start.7 = (bf16[2,256,512]{2,1,0:T(8,128)(2,1)S(1)}, bf16[2,256,512]{2,1,0:T(8,128)(2,1)S(1)}, u32[]{:S(2)}, u32[]{:S(2)}) collective-permute-start(bf16[2,256,512]{2,1,0:T(8,128)(2,1)S(1)} %get-tuple-element.83), channel_id=1, source_target_pairs={{0,1},{1,0},{2,3},{3,2},{4,5},{5,4},{6,7},{7,6},{8,9},{9,8},{10,11... | collective-permute-start | bytes 1572872 | tf_op jit(solution)/shard_map/ppermute | solution.py:101
  64.3 8.8 %collective-permute-start.9 = (bf16[256,512]{1,0:T(8,128)(2,1)S(1)}, bf16[256,512]{1,0:T(8,128)(2,1)S(1)}, u32[]{:S(2)}, u32[]{:S(2)}) collective-permute-start(bf16[256,512]{1,0:T(8,128)(2,1)S(1)} %get-tuple-element.86), channel_id=1, source_target_pairs={{0,4},{4,0},{8,12},{12,8},{1,5},{5,1},{9,13},{13,9},{2,6},{6,2},{1... | collective-permute-start | bytes 786440 | tf_op jit(solution)/shard_map/ppermute | solution.py:105
  66.2 6.9 %collective-permute-start.8 = (bf16[128,512]{1,0:T(8,128)(2,1)S(1)}, bf16[128,512]{1,0:T(8,128)(2,1)S(1)}, u32[]{:S(2)}, u32[]{:S(2)}) collective-permute-start(bf16[128,512]{1,0:T(8,128)(2,1)S(1)} %get-tuple-element.115), channel_id=1, source_target_pairs={{0,2},{2,0},{1,3},{3,1},{4,6},{6,4},{5,7},{7,5},{8,10},{10,8},{9,1... | collective-permute-start | bytes 393224 | tf_op jit(solution)/shard_map/ppermute | solution.py:101
  71.7 6.5 %collective-permute-start.14 = (bf16[128,512]{1,0:T(8,128)(2,1)S(1)}, bf16[128,512]{1,0:T(8,128)(2,1)S(1)}, u32[]{:S(2)}, u32[]{:S(2)}) collective-permute-start(bf16[128,512]{1,0:T(8,128)(2,1)S(1)} %get-tuple-element.101), channel_id=1, source_target_pairs={{0,2},{2,0},{1,3},{3,1},{4,6},{6,4},{5,7},{7,5},{8,10},{10,8},{9,1... | collective-permute-start | bytes 393224 | tf_op jit(solution)/shard_map/ppermute | solution.py:101
  72.3 10.7 %collective-permute-start.12 = (bf16[256,512]{1,0:T(8,128)(2,1)S(1)}, bf16[256,512]{1,0:T(8,128)(2,1)S(1)}, u32[]{:S(2)}, u32[]{:S(2)}) collective-permute-start(bf16[256,512]{1,0:T(8,128)(2,1)S(1)} %get-tuple-element.99), channel_id=1, source_target_pairs={{0,4},{4,0},{8,12},{12,8},{1,5},{5,1},{9,13},{13,9},{2,6},{6,2},{1... | collective-permute-start | bytes 786440 | tf_op jit(solution)/shard_map/ppermute | solution.py:105
  73.2 9.8 %copy-start.1 = (f32[2,256,512]{2,1,0:T(8,128)S(1)}, f32[2,256,512]{2,1,0:T(8,128)}, u32[]{:S(2)}) copy-start(f32[2,256,512]{2,1,0:T(8,128)} %copy-done) | copy-start | bytes 3145732
  73.2 10.9 %collective-permute-start.13 = (bf16[128,512]{1,0:T(8,128)(2,1)S(1)}, bf16[128,512]{1,0:T(8,128)(2,1)S(1)}, u32[]{:S(2)}, u32[]{:S(2)}) collective-permute-start(bf16[128,512]{1,0:T(8,128)(2,1)S(1)} %fusion.12), channel_id=1, source_target_pairs={{0,8},{4,12},{8,0},{12,4},{1,9},{5,13},{9,1},{13,5},{2,10},{6,14},... | collective-permute-start | bytes 393224 | tf_op jit(solution)/shard_map/ppermute | solution.py:105
  84.1 6.9 %collective-permute-start.15 = (bf16[128,512]{1,0:T(8,128)(2,1)S(1)}, bf16[128,512]{1,0:T(8,128)(2,1)S(1)}, u32[]{:S(2)}, u32[]{:S(2)}) collective-permute-start(bf16[128,512]{1,0:T(8,128)(2,1)S(1)} %fusion.15), channel_id=1, source_target_pairs={{0,8},{4,12},{8,0},{12,4},{1,9},{5,13},{9,1},{13,5},{2,10},{6,14},... | collective-permute-start | bytes 393224 | tf_op jit(solution)/shard_map/ppermute | solution.py:105

commit v17 on v12

--- a/solution.py
+++ b/solution.py
@@ -619,15 +619,14 @@
     kept, *_ = late_project(0, jnp.float32, "late_kept", [])
     far, near = far[:1], far[1:]
     late = [kept, *terms]
-    far = [trade(part, "batch", 1) for part in far]
+    far, near = ([trade(part, "batch", 1) for part in parts] for parts in (far, near))
     own_at = slice(token_count, 2 * token_count)
     *late_others, own_others = [others(late, here) for here in [*parts_of, own_at]]
     late_others[0] = spread(late_others[0])
     late_others[1], (keys, values) = after(late_others[1], (keys, values))
     state = prefix_attend(query_rows, keys, values, 1, scale, heads, (0, 2))
-    state, (late_others[1], own_others, near) = after(state, (late_others[1], own_others, near))
-    late_others[1], own_others = spread(late_others[1]), spread(own_others)
-    near = [trade(part, "batch", 1) for part in near]
+    state, (late_others[1], own_others) = after(state, (late_others[1], own_others))
+    late_others[1] = spread(late_others[1])
 
     away = []
     for chunk, here in enumerate(parts_of):
@@ -636,7 +635,8 @@
         part = part.astype(jnp.bfloat16)
         if chunk == 0:
             (far, late), late_others[1] = after((far, late), late_others[1])
-            part, state = after(part, state)
+            part, (state, own_others) = after(part, (state, own_others))
+            own_others = spread(own_others)
         else:
             away[-1], part = after(away[-1], part)
         away.append(trade(part, "batch", top))

time: 93.8 us -> 94.9 us (1.012)
  Pallas kernels: 50.3 us -> 52.4 us
  starting transfers between devices: 19.8 us -> 18 us
    ppermute x7, starting transfers between devices: 12.5 us -> 10.7 us  [trade(): lax.ppermute(array, axis, [(i, i ^ bits) for i in range(lax.axis_size(axi...]
    pallas_call x2, Pallas kernels: 10 us -> 11.7 us  [fresh_attend(): pl.pallas_call(functools.partial(fresh_kernel, scale, heads, per_token, c...]
  transfers between devices with their start and end apart: 15 -> 15, of which waited for: 4 -> 6; matrix products, arithmetic and copies ran while one was open for 1% -> 1% of each run, Pallas kernels for 41% -> 42%
where the time goes in v17:
time: 94.9 us; the launch traced here: 94.7 us
  Pallas kernels  52.4 us (55%)
  waiting for transfers between devices  21.4 us (23%)
  starting transfers between devices  18 us (19%)
  other arithmetic  1.87 us (2%)
  between operations  0.98 us (1%)
    ppermute x7, waiting for transfers between devices, trade(): lax.ppermute(array, axis, [(i, i ^ bits) for i in range(lax.axis_size(axi...  19.6 us
    pallas_call x3, Pallas kernels, prefix_attend(): pl.pallas_call(functools.partial(prefix_kernel, scale, heads), grid=(step...  15.5 us
    pallas_call x4, Pallas kernels, project(): pl.pallas_call(functools.partial(project_kernel, len(blocks), [len(terms)...  13.7 us
    pallas_call x2, Pallas kernels, fresh_attend(): pl.pallas_call(functools.partial(fresh_kernel, scale, heads, per_token, c...  11.7 us
    ppermute x7, starting transfers between devices, trade(): lax.ppermute(array, axis, [(i, i ^ bits) for i in range(lax.axis_size(axi...  10.7 us
    ppermute x8, starting transfers between devices, shift(): lax.ppermute(array, axis, [(i, (i + step) % count) for i in range(count)])  7.26 us
    pallas_call x1, Pallas kernels, cut_tokens(): pl.pallas_call(functools.partial(cut_kernel, bits), grid_spec=pltpu.Prefe...  3.08 us
    pallas_call x1, Pallas kernels, pick_blocks(): pl.pallas_call(functools.partial(pick_kernel, heads, len(pools)), grid_sp...  3.02 us
  transfers between devices with their start and end apart: 15, of which 6 were waited for; matrix products, arithmetic and copies ran while one was open for 1% of the time, Pallas kernels for 42%

profile of v17, /device:TPU:0, one launch (start us, length us, event | category | flops | bytes accessed | tf_op | source)
XLA Modules:
  0.0 94.7 jit_solution(280112024579428481)
XLA Ops:
  0.0 0.7 pad_add_fusion.place_ref
  0.7 3.1 %cut_tokens.1 = (bf16[256,1024]{1,0:T(8,128)(2,1)}, bf16[256,1024]{1,0:T(8,128)(2,1)}, bf16[256,1024]{1,0:T(8,128)(2,1)}) custom-call(s32[3]{0:T(128)} %pad_add_fusion.place_ref, bf16[256,4096]{1,0:T(8,128)(2,1)} %refs_1_.3), custom_call_target="tpu_custom_call" | custom-call | flops 99999997952 | bytes 1 | tf_op jit(solution)/shard_map/cut_tokens/pallas_call | solution.py:184
  3.7 5.1 %collective-permute-start = (bf16[256,1024]{1,0:T(8,128)(2,1)}, bf16[256,1024]{1,0:T(8,128)(2,1)}, u32[]{:S(2)}, u32[]{:S(2)}) collective-permute-start(bf16[256,1024]{1,0:T(8,128)(2,1)} %get-tuple-element.61), channel_id=1, source_target_pairs={{0,12},{4,8},{8,4},{12,0},{1,13},{5,9},{9,5},{13,1},{2,14},{6,10},... | collective-permute-start | bytes 1572872 | tf_op jit(solution)/shard_map/ppermute | solution.py:105
  8.9 0.0 collective-permute-start.1
  8.9 0.0 copy-start.6
  8.9 0.0 copy-start.7
  8.9 3.0 %arrange_pool.1 = (bf16[8,128,512]{2,1,0:T(8,128)(2,1)S(1)}, bf16[8,128,512]{2,1,0:T(8,128)(2,1)}) custom-call(s32[3]{0:T(128)S(1)} %copy-done.4, bf16[8,128,8,128]{3,2,1,0:T(8,128)(2,1)S(1)} %bitcast.45), custom_call_target="tpu_custom_call" | custom-call | flops 99999997952 | bytes 1 | tf_op jit(solution)/shard_map/arrange_pool/pallas_call | solution.py:234
  11.9 1.5 %collective-permute-start.3 = (bf16[8,128,512]{2,1,0:T(8,128)(2,1)}, bf16[8,128,512]{2,1,0:T(8,128)(2,1)}, u32[]{:S(2)}, u32[]{:S(2)}) collective-permute-start(bf16[8,128,512]{2,1,0:T(8,128)(2,1)} %get-tuple-element.71), channel_id=1, source_target_pairs={{0,2},{2,0},{1,3},{3,1},{4,6},{6,4},{5,7},{7,5},{8,10},{10,8},{9,1... | collective-permute-start | bytes 3145736 | tf_op jit(solution)/shard_map/ppermute | solution.py:101
  13.4 2.5 %arrange_weights.1.refs_2_ = bf16[2,2,1024,512]{3,2,1,0:T(8,128)(2,1)S(1)} custom-call(bf16[1024,8,128]{2,1,0:T(8,128)(2,1)S(1)} %bitcast.46, bf16[1024,8,128]{2,1,0:T(8,128)(2,1)S(1)} %bitcast.47), custom_call_target="tpu_custom_call" | custom-call | flops 99999997952 | bytes 1 | tf_op jit(solution)/shard_map/arrange_weights/pallas_call | solution.py:150
  15.8 0.8 collective-permute-start.4
  17.4 4.7 %collective-permute-done.refs_0_ = bf16[256,1024]{1,0:T(8,128)(2,1)} collective-permute-done((bf16[256,1024]{1,0:T(8,128)(2,1)}, bf16[256,1024]{1,0:T(8,128)(2,1)}, u32[]{:S(2)}, u32[]{:S(2)}) %collective-permute-start) | collective-permute-done | bytes 524320 | tf_op jit(solution)/shard_map/ppermute | solution.py:105
  22.0 11.5 %collective-permute-done.1.refs_1_ = bf16[256,1024]{1,0:T(8,128)(2,1)} collective-permute-done((bf16[256,1024]{1,0:T(8,128)(2,1)}, bf16[256,1024]{1,0:T(8,128)(2,1)}, u32[]{:S(2)}, u32[]{:S(2)}) %collective-permute-start.1) | collective-permute-done | bytes 524320 | tf_op jit(solution)/shard_map/ppermute | solution.py:105
  33.5 3.3 %early_away.1 = bf16[2,512,512]{2,1,0:T(8,128)(2,1)S(1)} custom-call(s32[3]{0:T(128)S(1)} %copy-done.4, bf16[256,1024]{1,0:T(8,128)(2,1)} %collective-permute-done.refs_0_, bf16[256,1024]{1,0:T(8,128)(2,1)} %collective-permute-done.1.refs_1_, bf16[2,2,1024,512]{3,2,1,0:T(8,128)(2,1)S(1)} %arrange_weights.1.refs_2_), custom_call_target="tpu_custom_call" | custom-call | flops 99999997952 | bytes 1 | tf_op jit(solution)/shard_map/early_away/pallas_call | solution.py:294
  36.8 0.1 collective-permute-start.2
  36.8 3.3 %early_kept.1.refs_3_.refs_6_ = f32[2,512,512]{2,1,0:T(8,128)S(1)} custom-call(s32[3]{0:T(128)S(1)} %copy-done.4, bf16[256,1024]{1,0:T(8,128)(2,1)} %collective-permute-done.refs_0_, bf16[256,1024]{1,0:T(8,128)(2,1)} %collective-permute-done.1.refs_1_, bf16[2,2,1024,512]{3,2,1,0:T(8,128)(2,1)S(1)} %arrange_weights.1.refs_2_), custom_call_target="tpu_custom_call" | custom-call | flops 99999997952 | bytes 1 | tf_op jit(solution)/shard_map/early_kept/pallas_call | solution.py:294
  40.1 0.0 copy-start
  40.1 0.0 copy-start.11
  40.2 1.0 %fusion.4 = (bf16[256,512]{1,0:T(8,128)(2,1)}, bf16[256,512]{1,0:T(8,128)(2,1)}) fusion(f32[2,512,512]{2,1,0:T(8,128)S(1)} %early_kept.1.refs_3_.refs_6_, bf16[2,512,512]{2,1,0:T(8,128)(2,1)S(1)} %collective-permute-done.2.refs_4_.refs_7_), kind=kLoop, calls=%fused_computation.7 | loop fusion | flops 786432 | bytes 2097152 | tf_op jit(solution)/shard_map/convert_element_type | solution.py:586
  41.1 1.4 %collective-permute-start.5 = (bf16[256,512]{1,0:T(8,128)(2,1)}, bf16[256,512]{1,0:T(8,128)(2,1)}, u32[]{:S(2)}, u32[]{:S(2)}) collective-permute-start(bf16[256,512]{1,0:T(8,128)(2,1)} %get-tuple-element.80), channel_id=1, source_target_pairs={{0,2},{2,0},{1,3},{3,1},{4,6},{6,4},{5,7},{7,5},{8,10},{10,8},{9,1... | collective-permute-start | bytes 786440 | tf_op jit(solution)/shard_map/ppermute | solution.py:101
  42.5 0.6 collective-permute-start.6
  43.1 3.0 %pick_blocks.1 = (bf16[1024,256]{1,0:T(8,128)(2,1)S(1)}, bf16[288,1024]{1,0:T(8,128)(2,1)S(1)}) custom-call(s32[3]{0:T(128)S(1)} %copy-done.4, s32[8]{0:T(128)S(1)} %bitcast.53, bf16[8,128,512]{2,1,0:T(8,128)(2,1)S(1)} %get-tuple-element.72.refs_0_, bf16[8,128,512]{2,1,0:T(8,128)(2,1)} %collective-permute-done.3.refs_1_), custom_call_target="tpu_custom_call" | custom-call | flops 99999997952 | bytes 1 | tf_op jit(solution)/shard_map/pick_blocks/pallas_call | solution.py:358
  46.2 0.0 copy-start.1
  46.2 0.0 copy-start.8
  46.3 7.7 %prefix_attend.3 = (f32[128,4096]{1,0:T(8,128)S(1)}, f32[8,4096]{1,0:T(8,128)S(1)}) custom-call(bf16[8192,128]{1,0:T(8,128)(2,1)S(1)} %bitcast.48, bf16[1024,256]{1,0:T(8,128)(2,1)S(1)} %get-tuple-element.83.keys, bf16[288,1024]{1,0:T(8,128)(2,1)S(1)} %get-tuple-element.84.values), custom_call_target="tpu_custom_call" | custom-call | flops 99999997952 | bytes 1 | tf_op jit(solution)/shard_map/prefix_attend/pallas_call | solution.py:428
  54.0 0.0 collective-permute-done.4.refs_0_
  54.0 0.0 collective-permute-done.5.refs_5_
  54.0 1.7 %collective-permute-done.6.refs_8_ = bf16[256,512]{1,0:T(8,128)(2,1)} collective-permute-done((bf16[256,512]{1,0:T(8,128)(2,1)}, bf16[256,512]{1,0:T(8,128)(2,1)}, u32[]{:S(2)}, u32[]{:S(2)}) %collective-permute-start.6) | collective-permute-done | bytes 262176 | tf_op jit(solution)/shard_map/ppermute | solution.py:101
  55.8 3.8 %late_away.1 = (bf16[2,512,512]{2,1,0:T(8,128)(2,1)S(1)}, bf16[256,512]{1,0:T(8,128)(2,1)S(1)}, bf16[256,512]{1,0:T(8,128)(2,1)}) custom-call(s32[3]{0:T(128)S(1)} %copy-done.4, bf16[256,1024]{1,0:T(8,128)(2,1)} %collective-permute-done.4.refs_0_, bf16[256,4096]{1,0:T(8,128)(2,1)S(1)} %copy-done.8, bf16[2,2,1024,512]{3,2,1,0:T(8,128)(2,1)S(1)} %copy-done.13, ...), custom_call_target="tpu_custom_call" | custom-call | flops 99999997952 | bytes 1 | tf_op jit(solution)/shard_map/late_away/pallas_call | solution.py:294
  59.6 3.4 %late_kept.1.rest_0_.rest_1_ = f32[2,512,512]{2,1,0:T(8,128)S(1)} custom-call(s32[3]{0:T(128)S(1)} %copy-done.4, bf16[256,1024]{1,0:T(8,128)(2,1)} %collective-permute-done.4.refs_0_, bf16[256,4096]{1,0:T(8,128)(2,1)S(1)} %copy-done.8, bf16[2,2,1024,512]{3,2,1,0:T(8,128)(2,1)S(1)} %copy-done.13), custom_call_target="tpu_custom_call" | custom-call | flops 99999997952 | bytes 1 | tf_op jit(solution)/shard_map/late_kept/pallas_call | solution.py:294
  62.9 1.8 %collective-permute-start.9 = (bf16[256,512]{1,0:T(8,128)(2,1)S(1)}, bf16[256,512]{1,0:T(8,128)(2,1)S(1)}, u32[]{:S(2)}, u32[]{:S(2)}) collective-permute-start(bf16[256,512]{1,0:T(8,128)(2,1)S(1)} %get-tuple-element.85), channel_id=1, source_target_pairs={{0,4},{4,0},{8,12},{12,8},{1,5},{5,1},{9,13},{13,9},{2,6},{6,2},{1... | collective-permute-start | bytes 786440 | tf_op jit(solution)/shard_map/ppermute | solution.py:105
  64.7 0.3 collective-permute-start.12
  65.0 0.0 collective-permute-done.7.rest_1_.rest_2_
  65.0 0.1 fusion.15
  65.1 1.4 %collective-permute-start.8 = (bf16[128,512]{1,0:T(8,128)(2,1)S(1)}, bf16[128,512]{1,0:T(8,128)(2,1)S(1)}, u32[]{:S(2)}, u32[]{:S(2)}) collective-permute-start(bf16[128,512]{1,0:T(8,128)(2,1)S(1)} %get-tuple-element.111), channel_id=1, source_target_pairs={{0,2},{2,0},{1,3},{3,1},{4,6},{6,4},{5,7},{7,5},{8,10},{10,8},{9,1... | collective-permute-start | bytes 393224 | tf_op jit(solution)/shard_map/ppermute | solution.py:101
  66.5 3.8 %prefix_attend.4 = (f32[128,4096]{1,0:T(8,128)S(1)}, f32[8,4096]{1,0:T(8,128)S(1)}) custom-call(bf16[8192,128]{1,0:T(8,128)(2,1)S(1)} %bitcast.49, bf16[1024,256]{1,0:T(8,128)(2,1)S(1)} %copy-done.15, bf16[288,1024]{1,0:T(8,128)(2,1)S(1)} %get-tuple-element.84.values), custom_call_target="tpu_custom_call" | custom-call | flops 99999997952 | bytes 1 | tf_op jit(solution)/shard_map/prefix_attend/pallas_call | solution.py:428
  70.4 0.1 fusion.5
  70.5 0.7 collective-permute-start.10
  71.2 0.9 collective-permute-done.9
  72.1 0.1 fusion.10
  72.2 1.1 %collective-permute-start.13 = (bf16[128,512]{1,0:T(8,128)(2,1)S(1)}, bf16[128,512]{1,0:T(8,128)(2,1)S(1)}, u32[]{:S(2)}, u32[]{:S(2)}) collective-permute-start(bf16[128,512]{1,0:T(8,128)(2,1)S(1)} %fusion.10), channel_id=1, source_target_pairs={{0,8},{4,12},{8,0},{12,4},{1,9},{5,13},{9,1},{13,5},{2,10},{6,14},... | collective-permute-start | bytes 393224 | tf_op jit(solution)/shard_map/ppermute | solution.py:105
  73.3 1.5 %collective-permute-start.11 = (bf16[256,512]{1,0:T(8,128)(2,1)S(1)}, bf16[256,512]{1,0:T(8,128)(2,1)S(1)}, u32[]{:S(2)}, u32[]{:S(2)}) collective-permute-start(bf16[256,512]{1,0:T(8,128)(2,1)S(1)} %fusion.5), channel_id=1, source_target_pairs={{0,2},{2,0},{1,3},{3,1},{4,6},{6,4},{5,7},{7,5},{8,10},{10,8},{9,1... | collective-permute-start | bytes 786440 | tf_op jit(solution)/shard_map/ppermute | solution.py:101
  74.8 3.9 %prefix_attend.5 = (f32[128,4096]{1,0:T(8,128)S(1)}, f32[8,4096]{1,0:T(8,128)S(1)}) custom-call(bf16[8192,128]{1,0:T(8,128)(2,1)S(1)} %bitcast.50, bf16[1024,256]{1,0:T(8,128)(2,1)S(1)} %copy-done.15, bf16[288,1024]{1,0:T(8,128)(2,1)S(1)} %get-tuple-element.84.values, ...), custom_call_target="tpu_custom_call", output_to_operand_aliasing={{0}: (3, {}), {1}: (4, {})} | custom-call | flops 99999997952 | bytes 1 | tf_op jit(solution)/shard_map/prefix_attend/pallas_call | solution.py:428
  78.7 0.1 fusion.13
  78.7 2.2 %collective-permute-done.13.rest_4_ = bf16[128,512]{1,0:T(8,128)(2,1)S(1)} collective-permute-done((bf16[128,512]{1,0:T(8,128)(2,1)S(1)}, bf16[128,512]{1,0:T(8,128)(2,1)S(1)}, u32[]{:S(2)}, u32[]{:S(2)}) %collective-permute-start.13) | collective-permute-done | bytes 131104 | tf_op jit(solution)/shard_map/ppermute | solution.py:105
  80.9 1.6 %collective-permute-start.14 = (bf16[128,512]{1,0:T(8,128)(2,1)S(1)}, bf16[128,512]{1,0:T(8,128)(2,1)S(1)}, u32[]{:S(2)}, u32[]{:S(2)}) collective-permute-start(bf16[128,512]{1,0:T(8,128)(2,1)S(1)} %fusion.13), channel_id=1, source_target_pairs={{0,8},{4,12},{8,0},{12,4},{1,9},{5,13},{9,1},{13,5},{2,10},{6,14},... | collective-permute-start | bytes 393224 | tf_op jit(solution)/shard_map/ppermute | solution.py:105
  82.6 5.5 %fresh_attend.2 = (bf16[8192,128]{1,0:T(8,128)(2,1)}, bf16[128,512]{1,0:T(8,128)(2,1)S(1)}) custom-call(s32[1]{0:T(128)S(6)} %copy.17.length_ref, bf16[8192,128]{1,0:T(8,128)(2,1)S(1)} %bitcast.51, f32[128,4096]{1,0:T(8,128)S(1)} %get-tuple-element.96.acc_ref, f32[8,4096]{1,0:T(8,128)S(1)} %get-tuple-element.97.stat_ref, ...), custom_call_target="tpu_custom_call" | custom-call | flops 99999997952 | bytes 1 | tf_op jit(solution)/shard_map/fresh_attend/pallas_call | solution.py:513
  88.1 0.4 collective-permute-done.14.rest_5_
  88.5 6.2 %fresh_attend.3 = (bf16[8192,128]{1,0:T(8,128)(2,1)}, bf16[128,512]{1,0:T(8,128)(2,1)}) custom-call(s32[1]{0:T(128)S(6)} %copy.17.length_ref, bf16[8192,128]{1,0:T(8,128)(2,1)S(1)} %bitcast.52, f32[128,4096]{1,0:T(8,128)S(1)} %get-tuple-element.94.acc_ref, f32[8,4096]{1,0:T(8,128)S(1)} %get-tuple-element.95.stat_ref, ...), custom_call_target="tpu_custom_call", output_to_operand_aliasing={{0}: (10, {})} | custom-call | flops 99999997952 | bytes 1 | tf_op jit(solution)/shard_map/fresh_attend/pallas_call | solution.py:513
  (33 shorter events, 0.1 us)
Async XLA Ops:
  0.7 8.2 %copy-start.4 = (s32[3]{0:T(128)S(1)}, s32[3]{0:T(128)}, u32[]{:S(2)}) copy-start(s32[3]{0:T(128)} %pad_add_fusion.place_ref) | copy-start | bytes 40
  0.7 8.2 %copy-start.5 = (bf16[8,128,4,1,256]{4,2,3,1,0:T(4,128)(2,1)S(1)}, bf16[8,128,4,1,256]{4,2,3,1,0:T(4,128)(2,1)}, u32[]{:S(2)}) copy-start(bf16[8,128,4,1,256]{4,2,3,1,0:T(4,128)(2,1)} %param.11) | copy-start | bytes 6291460
  3.7 18.3 %collective-permute-start = (bf16[256,1024]{1,0:T(8,128)(2,1)}, bf16[256,1024]{1,0:T(8,128)(2,1)}, u32[]{:S(2)}, u32[]{:S(2)}) collective-permute-start(bf16[256,1024]{1,0:T(8,128)(2,1)} %get-tuple-element.61), channel_id=1, source_target_pairs={{0,12},{4,8},{8,4},{12,0},{1,13},{5,9},{9,5},{13,1},{2,14},{6,10},... | collective-permute-start | bytes 1572872 | tf_op jit(solution)/shard_map/ppermute | solution.py:105
  8.9 24.6 %collective-permute-start.1 = (bf16[256,1024]{1,0:T(8,128)(2,1)}, bf16[256,1024]{1,0:T(8,128)(2,1)}, u32[]{:S(2)}, u32[]{:S(2)}) collective-permute-start(bf16[256,1024]{1,0:T(8,128)(2,1)} %get-tuple-element.62), channel_id=1, source_target_pairs={{0,4},{4,0},{8,12},{12,8},{1,5},{5,1},{9,13},{13,9},{2,6},{6,2},{1... | collective-permute-start | bytes 1572872 | tf_op jit(solution)/shard_map/ppermute | solution.py:105
  8.9 4.5 %copy-start.6 = (bf16[1,1,1024,4,2,128]{5,4,3,2,1,0:T(2,128)(2,1)S(1)}, bf16[1,1,1024,4,2,128]{5,4,3,2,1,0:T(2,128)(2,1)}, u32[]{:S(2)}) copy-start(bf16[1,1,1024,4,2,128]{5,4,3,2,1,0:T(2,128)(2,1)} %param.8) | copy-start | bytes 6291460
  8.9 4.5 %copy-start.7 = (bf16[1,1,1024,4,2,128]{5,4,3,2,1,0:T(2,128)(2,1)S(1)}, bf16[1,1,1024,4,2,128]{5,4,3,2,1,0:T(2,128)(2,1)}, u32[]{:S(2)}) copy-start(bf16[1,1,1024,4,2,128]{5,4,3,2,1,0:T(2,128)(2,1)} %param.9) | copy-start | bytes 6291460
  11.9 29.3 %collective-permute-start.3 = (bf16[8,128,512]{2,1,0:T(8,128)(2,1)}, bf16[8,128,512]{2,1,0:T(8,128)(2,1)}, u32[]{:S(2)}, u32[]{:S(2)}) collective-permute-start(bf16[8,128,512]{2,1,0:T(8,128)(2,1)} %get-tuple-element.71), channel_id=1, source_target_pairs={{0,2},{2,0},{1,3},{3,1},{4,6},{6,4},{5,7},{7,5},{8,10},{10,8},{9,1... | collective-permute-start | bytes 3145736 | tf_op jit(solution)/shard_map/ppermute | solution.py:101
  15.8 21.0 %copy-start.12 = (bf16[2,2,1024,512]{3,2,1,0:T(8,128)(2,1)}, bf16[2,2,1024,512]{3,2,1,0:T(8,128)(2,1)S(1)}, u32[]{:S(2)}) copy-start(bf16[2,2,1024,512]{3,2,1,0:T(8,128)(2,1)S(1)} %arrange_weights.1.refs_2_) | copy-start | bytes 12582916
  15.8 38.2 %collective-permute-start.4 = (bf16[256,1024]{1,0:T(8,128)(2,1)}, bf16[256,1024]{1,0:T(8,128)(2,1)}, u32[]{:S(2)}, u32[]{:S(2)}) collective-permute-start(bf16[256,1024]{1,0:T(8,128)(2,1)} %get-tuple-element.78), channel_id=1, source_target_pairs={{0,8},{4,12},{8,0},{12,4},{1,9},{5,13},{9,1},{13,5},{2,10},{6,14},... | collective-permute-start | bytes 1572872 | tf_op jit(solution)/shard_map/ppermute | solution.py:105
  36.8 3.4 %collective-permute-start.2 = (bf16[2,512,512]{2,1,0:T(8,128)(2,1)S(1)}, bf16[2,512,512]{2,1,0:T(8,128)(2,1)S(1)}, u32[]{:S(2)}, u32[]{:S(2)}) collective-permute-start(bf16[2,512,512]{2,1,0:T(8,128)(2,1)S(1)} %early_away.1), channel_id=1, source_target_pairs={{0,1},{1,0},{2,3},{3,2},{4,5},{5,4},{6,7},{7,6},{8,9},{9,8},{10,11... | collective-permute-start | bytes 3145736 | tf_op jit(solution)/shard_map/ppermute | solution.py:101
  40.1 6.1 %copy-start = (f32[2,512,512]{2,1,0:T(8,128)}, f32[2,512,512]{2,1,0:T(8,128)S(1)}, u32[]{:S(2)}) copy-start(f32[2,512,512]{2,1,0:T(8,128)S(1)} %early_kept.1.refs_3_.refs_6_) | copy-start | bytes 6291460
  40.1 3.0 %copy-start.11 = (s32[1,8]{1,0:T(1,128)S(1)}, s32[1,8]{1,0:T(1,128)}, u32[]{:S(2)}) copy-start(s32[1,8]{1,0:T(1,128)} %param.12) | copy-start | bytes 100
  40.2 6.0 %copy-start.2 = (bf16[2,512,512]{2,1,0:T(8,128)(2,1)}, bf16[2,512,512]{2,1,0:T(8,128)(2,1)S(1)}, u32[]{:S(2)}) copy-start(bf16[2,512,512]{2,1,0:T(8,128)(2,1)S(1)} %collective-permute-done.2.refs_4_.refs_7_) | copy-start | bytes 3145732
  41.1 12.9 %collective-permute-start.5 = (bf16[256,512]{1,0:T(8,128)(2,1)}, bf16[256,512]{1,0:T(8,128)(2,1)}, u32[]{:S(2)}, u32[]{:S(2)}) collective-permute-start(bf16[256,512]{1,0:T(8,128)(2,1)} %get-tuple-element.80), channel_id=1, source_target_pairs={{0,2},{2,0},{1,3},{3,1},{4,6},{6,4},{5,7},{7,5},{8,10},{10,8},{9,1... | collective-permute-start | bytes 786440 | tf_op jit(solution)/shard_map/ppermute | solution.py:101
  42.5 13.2 %collective-permute-start.6 = (bf16[256,512]{1,0:T(8,128)(2,1)}, bf16[256,512]{1,0:T(8,128)(2,1)}, u32[]{:S(2)}, u32[]{:S(2)}) collective-permute-start(bf16[256,512]{1,0:T(8,128)(2,1)} %get-tuple-element.81), channel_id=1, source_target_pairs={{0,2},{2,0},{1,3},{3,1},{4,6},{6,4},{5,7},{7,5},{8,10},{10,8},{9,1... | collective-permute-start | bytes 786440 | tf_op jit(solution)/shard_map/ppermute | solution.py:101
  43.1 3.1 %copy-start.9 = (bf16[256,2,1,2048]{3,1,2,0:T(2,128)(2,1)S(1)}, bf16[256,2,1,2048]{3,1,2,0:T(2,128)(2,1)}, u32[]{:S(2)}) copy-start(bf16[256,2,1,2048]{3,1,2,0:T(2,128)(2,1)} %param.10) | copy-start | bytes 6291460
  46.2 7.8 %copy-start.14 = (bf16[1024,256]{1,0:T(8,128)(2,1)}, bf16[1024,256]{1,0:T(8,128)(2,1)S(1)}, u32[]{:S(2)}) copy-start(bf16[1024,256]{1,0:T(8,128)(2,1)S(1)} %get-tuple-element.83.keys) | copy-start | bytes 1572868
  46.2 9.5 %copy-start.1 = (f32[2,512,512]{2,1,0:T(8,128)S(1)}, f32[2,512,512]{2,1,0:T(8,128)}, u32[]{:S(2)}) copy-start(f32[2,512,512]{2,1,0:T(8,128)} %copy-done) | copy-start | bytes 6291460
  46.2 9.5 %copy-start.3 = (bf16[2,512,512]{2,1,0:T(8,128)(2,1)S(1)}, bf16[2,512,512]{2,1,0:T(8,128)(2,1)}, u32[]{:S(2)}) copy-start(bf16[2,512,512]{2,1,0:T(8,128)(2,1)} %copy-done.2) | copy-start | bytes 3145732
  46.2 9.5 %copy-start.8 = (bf16[256,4096]{1,0:T(8,128)(2,1)S(1)}, bf16[256,4096]{1,0:T(8,128)(2,1)}, u32[]{:S(2)}) copy-start(bf16[256,4096]{1,0:T(8,128)(2,1)} %refs_1_.3) | copy-start | bytes 6291460
  46.2 9.5 %copy-start.13 = (bf16[2,2,1024,512]{3,2,1,0:T(8,128)(2,1)S(1)}, bf16[2,2,1024,512]{3,2,1,0:T(8,128)(2,1)}, u32[]{:S(2)}) copy-start(bf16[2,2,1024,512]{3,2,1,0:T(8,128)(2,1)} %copy-done.12) | copy-start | bytes 12582916
  59.6 7.0 %copy-start.10 = (bf16[256,2,1,2048]{3,1,2,0:T(2,128)(2,1)S(1)}, bf16[256,2,1,2048]{3,1,2,0:T(2,128)(2,1)}, u32[]{:S(2)}) copy-start(bf16[256,2,1,2048]{3,1,2,0:T(2,128)(2,1)} %param.10) | copy-start | bytes 6291460
  59.6 7.0 %copy-start.15 = (bf16[1024,256]{1,0:T(8,128)(2,1)S(1)}, bf16[1024,256]{1,0:T(8,128)(2,1)}, u32[]{:S(2)}) copy-start(bf16[1024,256]{1,0:T(8,128)(2,1)} %copy-done.14) | copy-start | bytes 1572868
  59.6 5.5 %collective-permute-start.7 = (bf16[2,512,512]{2,1,0:T(8,128)(2,1)S(1)}, bf16[2,512,512]{2,1,0:T(8,128)(2,1)S(1)}, u32[]{:S(2)}, u32[]{:S(2)}) collective-permute-start(bf16[2,512,512]{2,1,0:T(8,128)(2,1)S(1)} %get-tuple-element.82), channel_id=1, source_target_pairs={{0,1},{1,0},{2,3},{3,2},{4,5},{5,4},{6,7},{7,6},{8,9},{9,8},{10,11... | collective-permute-start | bytes 3145736 | tf_op jit(solution)/shard_map/ppermute | solution.py:101
  62.9 9.2 %collective-permute-start.9 = (bf16[256,512]{1,0:T(8,128)(2,1)S(1)}, bf16[256,512]{1,0:T(8,128)(2,1)S(1)}, u32[]{:S(2)}, u32[]{:S(2)}) collective-permute-start(bf16[256,512]{1,0:T(8,128)(2,1)S(1)} %get-tuple-element.85), channel_id=1, source_target_pairs={{0,4},{4,0},{8,12},{12,8},{1,5},{5,1},{9,13},{13,9},{2,6},{6,2},{1... | collective-permute-start | bytes 786440 | tf_op jit(solution)/shard_map/ppermute | solution.py:105
  64.7 17.8 %collective-permute-start.12 = (bf16[256,512]{1,0:T(8,128)(2,1)}, bf16[256,512]{1,0:T(8,128)(2,1)}, u32[]{:S(2)}, u32[]{:S(2)}) collective-permute-start(bf16[256,512]{1,0:T(8,128)(2,1)} %get-tuple-element.102), channel_id=1, source_target_pairs={{0,4},{4,0},{8,12},{12,8},{1,5},{5,1},{9,13},{13,9},{2,6},{6,2},{1... | collective-permute-start | bytes 786440 | tf_op jit(solution)/shard_map/ppermute | solution.py:105
  65.1 7.0 %collective-permute-start.8 = (bf16[128,512]{1,0:T(8,128)(2,1)S(1)}, bf16[128,512]{1,0:T(8,128)(2,1)S(1)}, u32[]{:S(2)}, u32[]{:S(2)}) collective-permute-start(bf16[128,512]{1,0:T(8,128)(2,1)S(1)} %get-tuple-element.111), channel_id=1, source_target_pairs={{0,2},{2,0},{1,3},{3,1},{4,6},{6,4},{5,7},{7,5},{8,10},{10,8},{9,1... | collective-permute-start | bytes 393224 | tf_op jit(solution)/shard_map/ppermute | solution.py:101
  70.5 8.2 %collective-permute-start.10 = (bf16[128,512]{1,0:T(8,128)(2,1)S(1)}, bf16[128,512]{1,0:T(8,128)(2,1)S(1)}, u32[]{:S(2)}, u32[]{:S(2)}) collective-permute-start(bf16[128,512]{1,0:T(8,128)(2,1)S(1)} %get-tuple-element.98), channel_id=1, source_target_pairs={{0,2},{2,0},{1,3},{3,1},{4,6},{6,4},{5,7},{7,5},{8,10},{10,8},{9,1... | collective-permute-start | bytes 393224 | tf_op jit(solution)/shard_map/ppermute | solution.py:101
  72.2 8.7 %collective-permute-start.13 = (bf16[128,512]{1,0:T(8,128)(2,1)S(1)}, bf16[128,512]{1,0:T(8,128)(2,1)S(1)}, u32[]{:S(2)}, u32[]{:S(2)}) collective-permute-start(bf16[128,512]{1,0:T(8,128)(2,1)S(1)} %fusion.10), channel_id=1, source_target_pairs={{0,8},{4,12},{8,0},{12,4},{1,9},{5,13},{9,1},{13,5},{2,10},{6,14},... | collective-permute-start | bytes 393224 | tf_op jit(solution)/shard_map/ppermute | solution.py:105
  73.3 9.3 %collective-permute-start.11 = (bf16[256,512]{1,0:T(8,128)(2,1)S(1)}, bf16[256,512]{1,0:T(8,128)(2,1)S(1)}, u32[]{:S(2)}, u32[]{:S(2)}) collective-permute-start(bf16[256,512]{1,0:T(8,128)(2,1)S(1)} %fusion.5), channel_id=1, source_target_pairs={{0,2},{2,0},{1,3},{3,1},{4,6},{6,4},{5,7},{7,5},{8,10},{10,8},{9,1... | collective-permute-start | bytes 786440 | tf_op jit(solution)/shard_map/ppermute | solution.py:101
  80.9 7.5 %collective-permute-start.14 = (bf16[128,512]{1,0:T(8,128)(2,1)S(1)}, bf16[128,512]{1,0:T(8,128)(2,1)S(1)}, u32[]{:S(2)}, u32[]{:S(2)}) collective-permute-start(bf16[128,512]{1,0:T(8,128)(2,1)S(1)} %fusion.13), channel_id=1, source_target_pairs={{0,8},{4,12},{8,0},{12,4},{1,9},{5,13},{9,1},{13,5},{2,10},{6,14},... | collective-permute-start | bytes 393224 | tf_op jit(solution)/shard_map/ppermute | solution.py:105

commit v18 on v17

--- a/solution.py
+++ b/solution.py
@@ -13,7 +13,7 @@
 ONES = 16
 VMEM_BYTES = 16 * 1024 * 1024
 MOST_VMEM_BYTES = 60 * 1024 * 1024
-LONG = pl.CostEstimate(flops=10**11, bytes_accessed=1, transcendentals=0)
+LONG = pl.CostEstimate(flops=2 * 10**10, bytes_accessed=1, transcendentals=0)
 COSTS = {}
 
 

time: 94.9 us -> 88.4 us (0.932)
  Pallas kernels: 52.4 us -> 43.3 us
  waiting for transfers between devices: 21.4 us -> 23.8 us
  starting transfers between devices: 18 us -> 19.2 us
    pallas_call x4, Pallas kernels: 13.7 us -> 8.6 us  [project(): pl.pallas_call(functools.partial(project_kernel, len(blocks), [len(terms)...]
    ppermute x7, waiting for transfers between devices: 19.6 us -> 23.2 us  [trade(): lax.ppermute(array, axis, [(i, i ^ bits) for i in range(lax.axis_size(axi...]
    pallas_call x2, Pallas kernels: 11.7 us -> 9.98 us  [fresh_attend(): pl.pallas_call(functools.partial(fresh_kernel, scale, heads, per_token, c...]
    pallas_call x1, Pallas kernels: 3.02 us -> 1.71 us  [pick_blocks(): pl.pallas_call(functools.partial(pick_kernel, heads, len(pools)), grid_sp...]
    ppermute x8, waiting for transfers between devices: 1.72 us -> 0.56 us  [shift(): lax.ppermute(array, axis, [(i, (i + step) % count) for i in range(count)])]
    pallas_call x1, Pallas kernels: 2.97 us -> 1.9 us  [arrange_pool(): pl.pallas_call(functools.partial(pool_kernel, ctx_count, heads), grid_spe...]
    ppermute x7, starting transfers between devices: 10.7 us -> 11.8 us  [trade(): lax.ppermute(array, axis, [(i, i ^ bits) for i in range(lax.axis_size(axi...]
  transfers between devices with their start and end apart: 15 -> 15, of which waited for: 6 -> 6; matrix products, arithmetic and copies ran while one was open for 1% -> 1% of each run, Pallas kernels for 42% -> 37%
where the time goes in v18:
time: 88.4 us; the launch traced here: 88.3 us
  Pallas kernels  43.3 us (49%)
  waiting for transfers between devices  23.8 us (27%)
  starting transfers between devices  19.2 us (22%)
  other arithmetic  1.06 us (1%)
    ppermute x7, waiting for transfers between devices, trade(): lax.ppermute(array, axis, [(i, i ^ bits) for i in range(lax.axis_size(axi...  23.2 us
    pallas_call x3, Pallas kernels, prefix_attend(): pl.pallas_call(functools.partial(prefix_kernel, scale, heads), grid=(step...  15.6 us
    ppermute x7, starting transfers between devices, trade(): lax.ppermute(array, axis, [(i, i ^ bits) for i in range(lax.axis_size(axi...  11.8 us
    pallas_call x2, Pallas kernels, fresh_attend(): pl.pallas_call(functools.partial(fresh_kernel, scale, heads, per_token, c...  9.98 us
    pallas_call x4, Pallas kernels, project(): pl.pallas_call(functools.partial(project_kernel, len(blocks), [len(terms)...  8.6 us
    ppermute x8, starting transfers between devices, shift(): lax.ppermute(array, axis, [(i, (i + step) % count) for i in range(count)])  7.44 us
    pallas_call x1, Pallas kernels, cut_tokens(): pl.pallas_call(functools.partial(cut_kernel, bits), grid_spec=pltpu.Prefe...  3.04 us
    pallas_call x1, Pallas kernels, arrange_weights(): pl.pallas_call(functools.partial(weight_kernel, ctx_count, heads, head_co...  2.47 us
  transfers between devices with their start and end apart: 15, of which 6 were waited for; matrix products, arithmetic and copies ran while one was open for 1% of the time, Pallas kernels for 37%

profile of v18, /device:TPU:0, one launch (start us, length us, event | category | flops | bytes accessed | tf_op | source)
XLA Modules:
  0.0 88.3 jit_solution(14912608972230913916)
XLA Ops:
  0.0 0.6 pad_add_fusion.place_ref
  0.6 3.0 %cut_tokens.1 = (bf16[256,1024]{1,0:T(8,128)(2,1)}, bf16[256,1024]{1,0:T(8,128)(2,1)}, bf16[256,1024]{1,0:T(8,128)(2,1)}) custom-call(s32[3]{0:T(128)} %pad_add_fusion.place_ref, bf16[256,4096]{1,0:T(8,128)(2,1)} %refs_1_.3), custom_call_target="tpu_custom_call" | custom-call | flops 20000000000 | bytes 1 | tf_op jit(solution)/shard_map/cut_tokens/pallas_call | solution.py:184
  3.7 5.1 %collective-permute-start = (bf16[256,1024]{1,0:T(8,128)(2,1)}, bf16[256,1024]{1,0:T(8,128)(2,1)S(1)}, u32[]{:S(2)}, u32[]{:S(2)}) collective-permute-start(bf16[256,1024]{1,0:T(8,128)(2,1)} %get-tuple-element.61), channel_id=1, source_target_pairs={{0,12},{4,8},{8,4},{12,0},{1,13},{5,9},{9,5},{13,1},{2,14},{6,10},... | collective-permute-start | bytes 1572872 | tf_op jit(solution)/shard_map/ppermute | solution.py:105
  8.8 0.0 collective-permute-start.1
  8.8 0.0 copy-start.2
  8.8 0.0 copy-start.3
  8.8 1.9 %arrange_pool.1 = (bf16[8,128,512]{2,1,0:T(8,128)(2,1)S(1)}, bf16[8,128,512]{2,1,0:T(8,128)(2,1)S(1)}) custom-call(s32[3]{0:T(128)S(1)} %copy-done, bf16[8,128,8,128]{3,2,1,0:T(8,128)(2,1)S(1)} %bitcast.45), custom_call_target="tpu_custom_call" | custom-call | flops 20000000000 | bytes 1 | tf_op jit(solution)/shard_map/arrange_pool/pallas_call | solution.py:234
  10.7 1.6 %collective-permute-start.3 = (bf16[8,128,512]{2,1,0:T(8,128)(2,1)S(1)}, bf16[8,128,512]{2,1,0:T(8,128)(2,1)S(1)}, u32[]{:S(2)}, u32[]{:S(2)}) collective-permute-start(bf16[8,128,512]{2,1,0:T(8,128)(2,1)S(1)} %get-tuple-element.71), channel_id=1, source_target_pairs={{0,2},{2,0},{1,3},{3,1},{4,6},{6,4},{5,7},{7,5},{8,10},{10,8},{9,1... | collective-permute-start | bytes 3145736 | tf_op jit(solution)/shard_map/ppermute | solution.py:101
  12.3 2.5 %arrange_weights.1.refs_2_ = bf16[2,2,1024,512]{3,2,1,0:T(8,128)(2,1)S(1)} custom-call(bf16[1024,8,128]{2,1,0:T(8,128)(2,1)S(1)} %bitcast.46, bf16[1024,8,128]{2,1,0:T(8,128)(2,1)S(1)} %bitcast.47), custom_call_target="tpu_custom_call" | custom-call | flops 20000000000 | bytes 1 | tf_op jit(solution)/shard_map/arrange_weights/pallas_call | solution.py:150
  14.8 0.8 collective-permute-start.4
  16.3 5.6 %collective-permute-done.refs_0_ = bf16[256,1024]{1,0:T(8,128)(2,1)S(1)} collective-permute-done((bf16[256,1024]{1,0:T(8,128)(2,1)}, bf16[256,1024]{1,0:T(8,128)(2,1)S(1)}, u32[]{:S(2)}, u32[]{:S(2)}) %collective-permute-start) | collective-permute-done | bytes 524320 | tf_op jit(solution)/shard_map/ppermute | solution.py:105
  21.8 11.5 %collective-permute-done.1.refs_1_ = bf16[256,1024]{1,0:T(8,128)(2,1)S(1)} collective-permute-done((bf16[256,1024]{1,0:T(8,128)(2,1)}, bf16[256,1024]{1,0:T(8,128)(2,1)S(1)}, u32[]{:S(2)}, u32[]{:S(2)}) %collective-permute-start.1) | collective-permute-done | bytes 524320 | tf_op jit(solution)/shard_map/ppermute | solution.py:105
  33.3 2.1 %early_away.1 = bf16[2,512,512]{2,1,0:T(8,128)(2,1)S(1)} custom-call(s32[3]{0:T(128)S(1)} %copy-done, bf16[256,1024]{1,0:T(8,128)(2,1)S(1)} %collective-permute-done.refs_0_, bf16[256,1024]{1,0:T(8,128)(2,1)S(1)} %collective-permute-done.1.refs_1_, bf16[2,2,1024,512]{3,2,1,0:T(8,128)(2,1)S(1)} %arrange_weights.1.refs_2_), custom_call_target="tpu_custom_call" | custom-call | flops 20000000000 | bytes 1 | tf_op jit(solution)/shard_map/early_away/pallas_call | solution.py:294
  35.4 0.1 collective-permute-start.2
  35.5 2.1 %early_kept.1.refs_3_.refs_6_ = f32[2,512,512]{2,1,0:T(8,128)S(1)} custom-call(s32[3]{0:T(128)S(1)} %copy-done, bf16[256,1024]{1,0:T(8,128)(2,1)S(1)} %collective-permute-done.refs_0_, bf16[256,1024]{1,0:T(8,128)(2,1)S(1)} %collective-permute-done.1.refs_1_, bf16[2,2,1024,512]{3,2,1,0:T(8,128)(2,1)S(1)} %arrange_weights.1.refs_2_), custom_call_target="tpu_custom_call" | custom-call | flops 20000000000 | bytes 1 | tf_op jit(solution)/shard_map/early_kept/pallas_call | solution.py:294
  37.5 0.0 copy-start.6
  37.6 0.5 collective-permute-done.2.refs_4_.refs_7_
  38.1 0.2 fusion.4
  38.3 0.0 collective-permute-done.3.refs_1_
  38.3 1.4 %collective-permute-start.5 = (bf16[256,512]{1,0:T(8,128)(2,1)S(1)}, bf16[256,512]{1,0:T(8,128)(2,1)S(1)}, u32[]{:S(2)}, u32[]{:S(2)}) collective-permute-start(bf16[256,512]{1,0:T(8,128)(2,1)S(1)} %get-tuple-element.80), channel_id=1, source_target_pairs={{0,2},{2,0},{1,3},{3,1},{4,6},{6,4},{5,7},{7,5},{8,10},{10,8},{9,1... | collective-permute-start | bytes 786440 | tf_op jit(solution)/shard_map/ppermute | solution.py:101
  39.7 0.6 collective-permute-start.6
  40.4 1.7 %pick_blocks.1 = (bf16[1024,256]{1,0:T(8,128)(2,1)S(1)}, bf16[288,1024]{1,0:T(8,128)(2,1)S(1)}) custom-call(s32[3]{0:T(128)S(1)} %copy-done, s32[8]{0:T(128)S(1)} %bitcast.53, bf16[8,128,512]{2,1,0:T(8,128)(2,1)S(1)} %get-tuple-element.72.refs_0_, bf16[8,128,512]{2,1,0:T(8,128)(2,1)S(1)} %collective-permute-done.3.refs_1_), custom_call_target="tpu_custom_call" | custom-call | flops 20000000000 | bytes 1 | tf_op jit(solution)/shard_map/pick_blocks/pallas_call | solution.py:358
  42.1 0.0 copy-start.4
  42.1 7.8 %prefix_attend.3 = (f32[128,4096]{1,0:T(8,128)S(1)}, f32[8,4096]{1,0:T(8,128)S(1)}) custom-call(bf16[8192,128]{1,0:T(8,128)(2,1)S(1)} %bitcast.48, bf16[1024,256]{1,0:T(8,128)(2,1)S(1)} %get-tuple-element.83.keys, bf16[288,1024]{1,0:T(8,128)(2,1)S(1)} %get-tuple-element.84.values), custom_call_target="tpu_custom_call" | custom-call | flops 20000000000 | bytes 1 | tf_op jit(solution)/shard_map/prefix_attend/pallas_call | solution.py:428
  49.9 3.8 %collective-permute-done.4.refs_0_ = bf16[256,1024]{1,0:T(8,128)(2,1)S(1)} collective-permute-done((bf16[256,1024]{1,0:T(8,128)(2,1)S(1)}, bf16[256,1024]{1,0:T(8,128)(2,1)S(1)}, u32[]{:S(2)}, u32[]{:S(2)}) %collective-permute-start.4) | collective-permute-done | bytes 524320 | tf_op jit(solution)/shard_map/ppermute | solution.py:105
  53.8 2.3 %late_away.1 = (bf16[2,512,512]{2,1,0:T(8,128)(2,1)S(1)}, bf16[256,512]{1,0:T(8,128)(2,1)S(1)}, bf16[256,512]{1,0:T(8,128)(2,1)S(1)}) custom-call(s32[3]{0:T(128)S(1)} %copy-done, bf16[256,1024]{1,0:T(8,128)(2,1)S(1)} %collective-permute-done.4.refs_0_, bf16[256,4096]{1,0:T(8,128)(2,1)S(1)} %copy-done.4, ...), custom_call_target="tpu_custom_call" | custom-call | flops 20000000000 | bytes 1 | tf_op jit(solution)/shard_map/late_away/pallas_call | solution.py:294
  56.1 0.1 collective-permute-start.7
  56.2 2.1 %late_kept.1.rest_0_.rest_1_ = f32[2,512,512]{2,1,0:T(8,128)S(1)} custom-call(s32[3]{0:T(128)S(1)} %copy-done, bf16[256,1024]{1,0:T(8,128)(2,1)S(1)} %collective-permute-done.4.refs_0_, bf16[256,4096]{1,0:T(8,128)(2,1)S(1)} %copy-done.4, bf16[2,2,1024,512]{3,2,1,0:T(8,128)(2,1)S(1)} %arrange_weights.1.refs_2_), custom_call_target="tpu_custom_call" | custom-call | flops 20000000000 | bytes 1 | tf_op jit(solution)/shard_map/late_kept/pallas_call | solution.py:294
  58.3 0.4 collective-permute-start.9
  58.7 1.7 %collective-permute-start.12 = (bf16[256,512]{1,0:T(8,128)(2,1)S(1)}, bf16[256,512]{1,0:T(8,128)(2,1)S(1)}, u32[]{:S(2)}, u32[]{:S(2)}) collective-permute-start(bf16[256,512]{1,0:T(8,128)(2,1)S(1)} %get-tuple-element.102), channel_id=1, source_target_pairs={{0,4},{4,0},{8,12},{12,8},{1,5},{5,1},{9,13},{13,9},{2,6},{6,2},{1... | collective-permute-start | bytes 786440 | tf_op jit(solution)/shard_map/ppermute | solution.py:105
  60.4 0.0 collective-permute-done.7.rest_1_.rest_2_
  60.4 0.1 fusion.15
  60.5 1.6 %collective-permute-start.8 = (bf16[128,512]{1,0:T(8,128)(2,1)S(1)}, bf16[128,512]{1,0:T(8,128)(2,1)S(1)}, u32[]{:S(2)}, u32[]{:S(2)}) collective-permute-start(bf16[128,512]{1,0:T(8,128)(2,1)S(1)} %get-tuple-element.111), channel_id=1, source_target_pairs={{0,2},{2,0},{1,3},{3,1},{4,6},{6,4},{5,7},{7,5},{8,10},{10,8},{9,1... | collective-permute-start | bytes 393224 | tf_op jit(solution)/shard_map/ppermute | solution.py:101
  62.0 3.9 %prefix_attend.4 = (f32[128,4096]{1,0:T(8,128)S(1)}, f32[8,4096]{1,0:T(8,128)S(1)}) custom-call(bf16[8192,128]{1,0:T(8,128)(2,1)S(1)} %bitcast.49, bf16[1024,256]{1,0:T(8,128)(2,1)S(1)} %get-tuple-element.83.keys, bf16[288,1024]{1,0:T(8,128)(2,1)S(1)} %get-tuple-element.84.values), custom_call_target="tpu_custom_call" | custom-call | flops 20000000000 | bytes 1 | tf_op jit(solution)/shard_map/prefix_attend/pallas_call | solution.py:428
  65.9 0.1 fusion.5
  66.0 0.6 collective-permute-start.10
  66.6 0.9 collective-permute-done.9
  67.5 0.1 fusion.10
  67.5 1.2 %collective-permute-start.13 = (bf16[128,512]{1,0:T(8,128)(2,1)S(1)}, bf16[128,512]{1,0:T(8,128)(2,1)S(1)}, u32[]{:S(2)}, u32[]{:S(2)}) collective-permute-start(bf16[128,512]{1,0:T(8,128)(2,1)S(1)} %fusion.10), channel_id=1, source_target_pairs={{0,8},{4,12},{8,0},{12,4},{1,9},{5,13},{9,1},{13,5},{2,10},{6,14},... | collective-permute-start | bytes 393224 | tf_op jit(solution)/shard_map/ppermute | solution.py:105
  68.7 1.5 %collective-permute-start.11 = (bf16[256,512]{1,0:T(8,128)(2,1)S(1)}, bf16[256,512]{1,0:T(8,128)(2,1)S(1)}, u32[]{:S(2)}, u32[]{:S(2)}) collective-permute-start(bf16[256,512]{1,0:T(8,128)(2,1)S(1)} %fusion.5), channel_id=1, source_target_pairs={{0,2},{2,0},{1,3},{3,1},{4,6},{6,4},{5,7},{7,5},{8,10},{10,8},{9,1... | collective-permute-start | bytes 786440 | tf_op jit(solution)/shard_map/ppermute | solution.py:101
  70.2 3.9 %prefix_attend.5 = (f32[128,4096]{1,0:T(8,128)S(1)}, f32[8,4096]{1,0:T(8,128)S(1)}) custom-call(bf16[8192,128]{1,0:T(8,128)(2,1)S(1)} %bitcast.50, bf16[1024,256]{1,0:T(8,128)(2,1)S(1)} %get-tuple-element.83.keys, bf16[288,1024]{1,0:T(8,128)(2,1)S(1)} %get-tuple-element.84.values, ...), custom_call_target="tpu_custom_call", output_to_operand_aliasing={{0}: (3, {}), {1}: (4, {})} | custom-call | flops 20000000000 | bytes 1 | tf_op jit(solution)/shard_map/prefix_attend/pallas_call | solution.py:428
  74.1 0.0 collective-permute-done.10
  74.1 0.1 fusion.13
  74.2 0.0 collective-permute-done.13.rest_4_
  74.2 2.6 %collective-permute-start.14 = (bf16[128,512]{1,0:T(8,128)(2,1)S(1)}, bf16[128,512]{1,0:T(8,128)(2,1)S(1)}, u32[]{:S(2)}, u32[]{:S(2)}) collective-permute-start(bf16[128,512]{1,0:T(8,128)(2,1)S(1)} %fusion.13), channel_id=1, source_target_pairs={{0,8},{4,12},{8,0},{12,4},{1,9},{5,13},{9,1},{13,5},{2,10},{6,14},... | collective-permute-start | bytes 393224 | tf_op jit(solution)/shard_map/ppermute | solution.py:105
  76.8 4.7 %fresh_attend.2 = (bf16[8192,128]{1,0:T(8,128)(2,1)}, bf16[128,512]{1,0:T(8,128)(2,1)S(1)}) custom-call(s32[1]{0:T(128)S(6)} %copy.17.length_ref, bf16[8192,128]{1,0:T(8,128)(2,1)S(1)} %bitcast.51, f32[128,4096]{1,0:T(8,128)S(1)} %get-tuple-element.96.acc_ref, f32[8,4096]{1,0:T(8,128)S(1)} %get-tuple-element.97.stat_ref, ...), custom_call_target="tpu_custom_call" | custom-call | flops 20000000000 | bytes 1 | tf_op jit(solution)/shard_map/fresh_attend/pallas_call | solution.py:513
  81.5 1.5 %collective-permute-done.14.rest_5_ = bf16[128,512]{1,0:T(8,128)(2,1)S(1)} collective-permute-done((bf16[128,512]{1,0:T(8,128)(2,1)S(1)}, bf16[128,512]{1,0:T(8,128)(2,1)S(1)}, u32[]{:S(2)}, u32[]{:S(2)}) %collective-permute-start.14) | collective-permute-done | bytes 131104 | tf_op jit(solution)/shard_map/ppermute | solution.py:105
  83.0 5.3 %fresh_attend.3 = (bf16[8192,128]{1,0:T(8,128)(2,1)}, bf16[128,512]{1,0:T(8,128)(2,1)}) custom-call(s32[1]{0:T(128)S(6)} %copy.17.length_ref, bf16[8192,128]{1,0:T(8,128)(2,1)S(1)} %bitcast.52, f32[128,4096]{1,0:T(8,128)S(1)} %get-tuple-element.94.acc_ref, f32[8,4096]{1,0:T(8,128)S(1)} %get-tuple-element.95.stat_ref, ...), custom_call_target="tpu_custom_call", output_to_operand_aliasing={{0}: (10, {})} | custom-call | flops 20000000000 | bytes 1 | tf_op jit(solution)/shard_map/fresh_attend/pallas_call | solution.py:513
  (17 shorter events, 0.0 us)
Async XLA Ops:
  0.6 8.2 %copy-start = (s32[3]{0:T(128)S(1)}, s32[3]{0:T(128)}, u32[]{:S(2)}) copy-start(s32[3]{0:T(128)} %pad_add_fusion.place_ref) | copy-start | bytes 40
  0.6 8.2 %copy-start.1 = (bf16[8,128,4,1,256]{4,2,3,1,0:T(4,128)(2,1)S(1)}, bf16[8,128,4,1,256]{4,2,3,1,0:T(4,128)(2,1)}, u32[]{:S(2)}) copy-start(bf16[8,128,4,1,256]{4,2,3,1,0:T(4,128)(2,1)} %param.11) | copy-start | bytes 6291460
  3.7 18.2 %collective-permute-start = (bf16[256,1024]{1,0:T(8,128)(2,1)}, bf16[256,1024]{1,0:T(8,128)(2,1)S(1)}, u32[]{:S(2)}, u32[]{:S(2)}) collective-permute-start(bf16[256,1024]{1,0:T(8,128)(2,1)} %get-tuple-element.61), channel_id=1, source_target_pairs={{0,12},{4,8},{8,4},{12,0},{1,13},{5,9},{9,5},{13,1},{2,14},{6,10},... | collective-permute-start | bytes 1572872 | tf_op jit(solution)/shard_map/ppermute | solution.py:105
  8.8 24.5 %collective-permute-start.1 = (bf16[256,1024]{1,0:T(8,128)(2,1)}, bf16[256,1024]{1,0:T(8,128)(2,1)S(1)}, u32[]{:S(2)}, u32[]{:S(2)}) collective-permute-start(bf16[256,1024]{1,0:T(8,128)(2,1)} %get-tuple-element.62), channel_id=1, source_target_pairs={{0,4},{4,0},{8,12},{12,8},{1,5},{5,1},{9,13},{13,9},{2,6},{6,2},{1... | collective-permute-start | bytes 1572872 | tf_op jit(solution)/shard_map/ppermute | solution.py:105
  8.8 3.5 %copy-start.2 = (bf16[1,1,1024,4,2,128]{5,4,3,2,1,0:T(2,128)(2,1)S(1)}, bf16[1,1,1024,4,2,128]{5,4,3,2,1,0:T(2,128)(2,1)}, u32[]{:S(2)}) copy-start(bf16[1,1,1024,4,2,128]{5,4,3,2,1,0:T(2,128)(2,1)} %param.8) | copy-start | bytes 6291460
  8.8 3.5 %copy-start.3 = (bf16[1,1,1024,4,2,128]{5,4,3,2,1,0:T(2,128)(2,1)S(1)}, bf16[1,1,1024,4,2,128]{5,4,3,2,1,0:T(2,128)(2,1)}, u32[]{:S(2)}) copy-start(bf16[1,1,1024,4,2,128]{5,4,3,2,1,0:T(2,128)(2,1)} %param.9) | copy-start | bytes 6291460
  10.7 27.6 %collective-permute-start.3 = (bf16[8,128,512]{2,1,0:T(8,128)(2,1)S(1)}, bf16[8,128,512]{2,1,0:T(8,128)(2,1)S(1)}, u32[]{:S(2)}, u32[]{:S(2)}) collective-permute-start(bf16[8,128,512]{2,1,0:T(8,128)(2,1)S(1)} %get-tuple-element.71), channel_id=1, source_target_pairs={{0,2},{2,0},{1,3},{3,1},{4,6},{6,4},{5,7},{7,5},{8,10},{10,8},{9,1... | collective-permute-start | bytes 3145736 | tf_op jit(solution)/shard_map/ppermute | solution.py:101
  12.3 2.5 %copy-start.7 = (bf16[256,1024]{1,0:T(8,128)(2,1)S(1)}, bf16[256,1024]{1,0:T(8,128)(2,1)}, u32[]{:S(2)}) copy-start(bf16[256,1024]{1,0:T(8,128)(2,1)} %get-tuple-element.78) | copy-start | bytes 1572868
  14.8 39.0 %collective-permute-start.4 = (bf16[256,1024]{1,0:T(8,128)(2,1)S(1)}, bf16[256,1024]{1,0:T(8,128)(2,1)S(1)}, u32[]{:S(2)}, u32[]{:S(2)}) collective-permute-start(bf16[256,1024]{1,0:T(8,128)(2,1)S(1)} %copy-done.7), channel_id=1, source_target_pairs={{0,8},{4,12},{8,0},{12,4},{1,9},{5,13},{9,1},{13,5},{2,10},{6,14},... | collective-permute-start | bytes 1572872 | tf_op jit(solution)/shard_map/ppermute | solution.py:105
  35.4 2.7 %collective-permute-start.2 = (bf16[2,512,512]{2,1,0:T(8,128)(2,1)S(1)}, bf16[2,512,512]{2,1,0:T(8,128)(2,1)S(1)}, u32[]{:S(2)}, u32[]{:S(2)}) collective-permute-start(bf16[2,512,512]{2,1,0:T(8,128)(2,1)S(1)} %early_away.1), channel_id=1, source_target_pairs={{0,1},{1,0},{2,3},{3,2},{4,5},{5,4},{6,7},{7,6},{8,9},{9,8},{10,11... | collective-permute-start | bytes 3145736 | tf_op jit(solution)/shard_map/ppermute | solution.py:101
  37.5 2.8 %copy-start.6 = (s32[1,8]{1,0:T(1,128)S(1)}, s32[1,8]{1,0:T(1,128)}, u32[]{:S(2)}) copy-start(s32[1,8]{1,0:T(1,128)} %param.12) | copy-start | bytes 100
  38.3 15.5 %collective-permute-start.5 = (bf16[256,512]{1,0:T(8,128)(2,1)S(1)}, bf16[256,512]{1,0:T(8,128)(2,1)S(1)}, u32[]{:S(2)}, u32[]{:S(2)}) collective-permute-start(bf16[256,512]{1,0:T(8,128)(2,1)S(1)} %get-tuple-element.80), channel_id=1, source_target_pairs={{0,2},{2,0},{1,3},{3,1},{4,6},{6,4},{5,7},{7,5},{8,10},{10,8},{9,1... | collective-permute-start | bytes 786440 | tf_op jit(solution)/shard_map/ppermute | solution.py:101
  39.7 14.0 %collective-permute-start.6 = (bf16[256,512]{1,0:T(8,128)(2,1)S(1)}, bf16[256,512]{1,0:T(8,128)(2,1)S(1)}, u32[]{:S(2)}, u32[]{:S(2)}) collective-permute-start(bf16[256,512]{1,0:T(8,128)(2,1)S(1)} %get-tuple-element.81), channel_id=1, source_target_pairs={{0,2},{2,0},{1,3},{3,1},{4,6},{6,4},{5,7},{7,5},{8,10},{10,8},{9,1... | collective-permute-start | bytes 786440 | tf_op jit(solution)/shard_map/ppermute | solution.py:101
  40.4 1.7 %copy-start.5 = (bf16[256,2,1,2048]{3,1,2,0:T(2,128)(2,1)S(1)}, bf16[256,2,1,2048]{3,1,2,0:T(2,128)(2,1)}, u32[]{:S(2)}) copy-start(bf16[256,2,1,2048]{3,1,2,0:T(2,128)(2,1)} %param.10) | copy-start | bytes 6291460
  42.1 11.7 %copy-start.4 = (bf16[256,4096]{1,0:T(8,128)(2,1)S(1)}, bf16[256,4096]{1,0:T(8,128)(2,1)}, u32[]{:S(2)}) copy-start(bf16[256,4096]{1,0:T(8,128)(2,1)} %refs_1_.3) | copy-start | bytes 6291460
  56.1 4.3 %collective-permute-start.7 = (bf16[2,512,512]{2,1,0:T(8,128)(2,1)S(1)}, bf16[2,512,512]{2,1,0:T(8,128)(2,1)S(1)}, u32[]{:S(2)}, u32[]{:S(2)}) collective-permute-start(bf16[2,512,512]{2,1,0:T(8,128)(2,1)S(1)} %get-tuple-element.82), channel_id=1, source_target_pairs={{0,1},{1,0},{2,3},{3,2},{4,5},{5,4},{6,7},{7,6},{8,9},{9,8},{10,11... | collective-permute-start | bytes 3145736 | tf_op jit(solution)/shard_map/ppermute | solution.py:101
  58.3 9.2 %collective-permute-start.9 = (bf16[256,512]{1,0:T(8,128)(2,1)S(1)}, bf16[256,512]{1,0:T(8,128)(2,1)S(1)}, u32[]{:S(2)}, u32[]{:S(2)}) collective-permute-start(bf16[256,512]{1,0:T(8,128)(2,1)S(1)} %get-tuple-element.85), channel_id=1, source_target_pairs={{0,4},{4,0},{8,12},{12,8},{1,5},{5,1},{9,13},{13,9},{2,6},{6,2},{1... | collective-permute-start | bytes 786440 | tf_op jit(solution)/shard_map/ppermute | solution.py:105
  58.7 18.1 %collective-permute-start.12 = (bf16[256,512]{1,0:T(8,128)(2,1)S(1)}, bf16[256,512]{1,0:T(8,128)(2,1)S(1)}, u32[]{:S(2)}, u32[]{:S(2)}) collective-permute-start(bf16[256,512]{1,0:T(8,128)(2,1)S(1)} %get-tuple-element.102), channel_id=1, source_target_pairs={{0,4},{4,0},{8,12},{12,8},{1,5},{5,1},{9,13},{13,9},{2,6},{6,2},{1... | collective-permute-start | bytes 786440 | tf_op jit(solution)/shard_map/ppermute | solution.py:105
  60.5 7.0 %collective-permute-start.8 = (bf16[128,512]{1,0:T(8,128)(2,1)S(1)}, bf16[128,512]{1,0:T(8,128)(2,1)S(1)}, u32[]{:S(2)}, u32[]{:S(2)}) collective-permute-start(bf16[128,512]{1,0:T(8,128)(2,1)S(1)} %get-tuple-element.111), channel_id=1, source_target_pairs={{0,2},{2,0},{1,3},{3,1},{4,6},{6,4},{5,7},{7,5},{8,10},{10,8},{9,1... | collective-permute-start | bytes 393224 | tf_op jit(solution)/shard_map/ppermute | solution.py:101
  66.0 8.1 %collective-permute-start.10 = (bf16[128,512]{1,0:T(8,128)(2,1)S(1)}, bf16[128,512]{1,0:T(8,128)(2,1)S(1)}, u32[]{:S(2)}, u32[]{:S(2)}) collective-permute-start(bf16[128,512]{1,0:T(8,128)(2,1)S(1)} %get-tuple-element.98), channel_id=1, source_target_pairs={{0,2},{2,0},{1,3},{3,1},{4,6},{6,4},{5,7},{7,5},{8,10},{10,8},{9,1... | collective-permute-start | bytes 393224 | tf_op jit(solution)/shard_map/ppermute | solution.py:101
  67.5 6.7 %collective-permute-start.13 = (bf16[128,512]{1,0:T(8,128)(2,1)S(1)}, bf16[128,512]{1,0:T(8,128)(2,1)S(1)}, u32[]{:S(2)}, u32[]{:S(2)}) collective-permute-start(bf16[128,512]{1,0:T(8,128)(2,1)S(1)} %fusion.10), channel_id=1, source_target_pairs={{0,8},{4,12},{8,0},{12,4},{1,9},{5,13},{9,1},{13,5},{2,10},{6,14},... | collective-permute-start | bytes 393224 | tf_op jit(solution)/shard_map/ppermute | solution.py:105
  68.7 8.1 %collective-permute-start.11 = (bf16[256,512]{1,0:T(8,128)(2,1)S(1)}, bf16[256,512]{1,0:T(8,128)(2,1)S(1)}, u32[]{:S(2)}, u32[]{:S(2)}) collective-permute-start(bf16[256,512]{1,0:T(8,128)(2,1)S(1)} %fusion.5), channel_id=1, source_target_pairs={{0,2},{2,0},{1,3},{3,1},{4,6},{6,4},{5,7},{7,5},{8,10},{10,8},{9,1... | collective-permute-start | bytes 786440 | tf_op jit(solution)/shard_map/ppermute | solution.py:101
  74.2 8.7 %collective-permute-start.14 = (bf16[128,512]{1,0:T(8,128)(2,1)S(1)}, bf16[128,512]{1,0:T(8,128)(2,1)S(1)}, u32[]{:S(2)}, u32[]{:S(2)}) collective-permute-start(bf16[128,512]{1,0:T(8,128)(2,1)S(1)} %fusion.13), channel_id=1, source_target_pairs={{0,8},{4,12},{8,0},{12,4},{1,9},{5,13},{9,1},{13,5},{2,10},{6,14},... | collective-permute-start | bytes 393224 | tf_op jit(solution)/shard_map/ppermute | solution.py:105

commit v19 on v18

--- a/solution.py
+++ b/solution.py
@@ -251,6 +251,13 @@
     return sum(ref[...].astype(jnp.float32).reshape(ref.shape[-2:]) for ref in refs)
 
 
+def put_sums(terms, counts, sum_refs):
+    at = 0
+    for count, sum_ref in zip(counts, sum_refs):
+        sum_ref[...] = total_of(terms[at : at + count]).astype(sum_ref.dtype)
+        at += count
+
+
 def project_kernel(block_count, term_counts, place_ref, *refs):
     token_refs, weight_ref = refs[:block_count], refs[block_count]
     terms = refs[block_count + 1 : block_count + 1 + sum(term_counts)]
@@ -264,10 +271,7 @@
             rows = token_ref.shape[0]
             stacked[at : at + rows, :] = token_ref[...]
             at += rows
-        at = 0
-        for count, sum_ref in zip(term_counts, sum_refs):
-            sum_ref[...] = total_of(terms[at : at + count]).astype(sum_ref.dtype)
-            at += count
+        put_sums(terms, term_counts, sum_refs)
 
     out_ref[0] = jnp.dot(
         stacked[...], weight_ref[0, 0], preferred_element_type=jnp.float32
@@ -385,11 +389,17 @@
             yield head, pl.ds(low + head, each, stride=heads), slice(at, at + each)
 
 
-def prefix_kernel(scale, heads, query_ref, keys, values, *refs):
-    acc_ref, stat_ref, flat = refs[-3:]
+def prefix_kernel(scale, heads, term_counts, held, query_ref, keys, values, *refs):
+    terms = refs[held : held + sum(term_counts)]
+    acc_ref, stat_ref, *sum_refs, flat = refs[held + sum(term_counts) :]
     rows, width = query_ref.shape
     tall = width + ONES
     half = stat_ref.shape[0] // 2
+
+    @pl.when(pl.program_id(0) == 0)
+    def _():
+        put_sums(terms, term_counts, sum_refs)
+
     flat[...] = query_ref[...].astype(jnp.float32)
     for head, taken, here in each_part(rows, heads):
         query_block = flat[taken, :].astype(jnp.bfloat16)
@@ -403,7 +413,9 @@
         stat_ref[half:, here] = jnp.broadcast_to(mixed[width : width + 1], (half, row_max.shape[1]))
 
 
-def prefix_attend(query_rows, keys, values, chunk, scale, heads, part=(0, 1), state=None):
+def prefix_attend(
+    query_rows, keys, values, chunk, scale, heads, part=(0, 1), state=None, sums=()
+):
     all_rows, width = query_rows.shape
     row_total = all_rows // CHUNKS
     at, count = part
@@ -423,23 +435,32 @@
     aliases = {}
     if state is not None:
         in_specs += [pl.BlockSpec(memory_space=pl.ANY)] * 2
-        operands += state
+        operands += list(state)
         aliases = {3: 0, 4: 1}
-    return pl.pallas_call(
-        functools.partial(prefix_kernel, scale, heads),
+    pieces = [piece for terms in sums for piece in terms]
+    sum_shapes = [terms[0][1].block_shape[-2:] for terms in sums]
+    in_specs += [spec for _, spec in pieces]
+    operands += [array for array, _ in pieces]
+    out_specs += [pl.BlockSpec(shape, lambda i: (0, 0)) for shape in sum_shapes]
+    acc, stat, *made = pl.pallas_call(
+        functools.partial(
+            prefix_kernel, scale, heads, [len(terms) for terms in sums], len(aliases)
+        ),
         grid=(steps,),
         in_specs=in_specs,
         out_specs=out_specs,
         out_shape=[
             jax.ShapeDtypeStruct((width, row_total), jnp.float32),
             jax.ShapeDtypeStruct((8, row_total), jnp.float32),
-        ],
+        ]
+        + [jax.ShapeDtypeStruct(shape, jnp.bfloat16) for shape in sum_shapes],
         input_output_aliases=aliases,
         scratch_shapes=[pltpu.VMEM((rows, width), jnp.float32)],
         compiler_params=params(),
         cost_estimate=cost("prefix_attend"),
         name="prefix_attend",
     )(*operands)
+    return ([acc, stat], made) if sums else [acc, stat]
 
 
 def fresh_kernel(
@@ -606,27 +627,30 @@
         ]
     keys, values = pick_blocks(place, block_table[0], pools, heads)
     states = [prefix_attend(query_rows, keys, values, 0, scale, heads)]
-    states[0], last = after(states[0], last)
+    state, far = prefix_attend(
+        query_rows, keys, values, 1, scale, heads, (0, 2), None, sums[0]
+    )
+    far = [trade(part, "batch", 1) for part in far]
+    (states[0], state), last = after((states[0], state), last)
 
     def late_project(step, dtype, name, sums):
         result = project(place, [last, tokens], weights, step, dtype, name, sums)
         return result if sums else (result,)
 
-    terms = []
+    terms, near = [], []
     for step in range(1, head_count):
-        term, *far = late_project(step, jnp.bfloat16, "late_away", sums[0] + sums[1] if step == 1 else [])
+        term, *made = late_project(step, jnp.bfloat16, "late_away", sums[1] if step == 1 else [])
+        near += [trade(part, "batch", 1) for part in made]
         terms.append(shift(term, "head", step))
     kept, *_ = late_project(0, jnp.float32, "late_kept", [])
-    far, near = far[:1], far[1:]
     late = [kept, *terms]
-    far, near = ([trade(part, "batch", 1) for part in parts] for parts in (far, near))
     own_at = slice(token_count, 2 * token_count)
     *late_others, own_others = [others(late, here) for here in [*parts_of, own_at]]
     late_others[0] = spread(late_others[0])
     late_others[1], (keys, values) = after(late_others[1], (keys, values))
-    state = prefix_attend(query_rows, keys, values, 1, scale, heads, (0, 2))
+    state = prefix_attend(query_rows, keys, values, 1, scale, heads, (2, 4), state)
     state, (late_others[1], own_others) = after(state, (late_others[1], own_others))
-    late_others[1] = spread(late_others[1])
+    late_others[1], own_others = spread(late_others[1]), spread(own_others)
 
     away = []
     for chunk, here in enumerate(parts_of):
@@ -635,12 +659,11 @@
         part = part.astype(jnp.bfloat16)
         if chunk == 0:
             (far, late), late_others[1] = after((far, late), late_others[1])
-            part, (state, own_others) = after(part, (state, own_others))
-            own_others = spread(own_others)
+            part, state = after(part, state)
         else:
             away[-1], part = after(away[-1], part)
         away.append(trade(part, "batch", top))
-    states.append(prefix_attend(query_rows, keys, values, 1, scale, heads, (1, 2), state))
+    states.append(prefix_attend(query_rows, keys, values, 1, scale, heads, (3, 4), state))
 
     result = None
     fresh = []

time: 88.4 us -> 87.7 us (level)
  starting transfers between devices: 19.2 us -> 17.8 us
  waiting for transfers between devices: 23.8 us -> 24.7 us
    ppermute x7, starting transfers between devices: 11.8 us -> 10.4 us  [trade(): lax.ppermute(array, axis, [(i, i ^ bits) for i in range(lax.axis_size(axi...]
    ppermute x8, waiting for transfers between devices: 0.56 us -> 1.85 us  [shift(): lax.ppermute(array, axis, [(i, (i + step) % count) for i in range(count)])]
    pallas_call x3 -> x4, Pallas kernels: 15.6 us -> 15.4 us  [prefix_attend(): pl.pallas_call(functools.partial(prefix_kernel, scale, heads, [len(terms)...]
  transfers between devices with their start and end apart: 15 -> 15, of which waited for: 6 -> 6; matrix products, arithmetic and copies ran while one was open for 1% -> 0% of each run, Pallas kernels for 37% -> 37%
where the time goes in v19:
time: 87.7 us; the launch traced here: 87.5 us
  Pallas kernels  43 us (49%)
  waiting for transfers between devices  24.7 us (28%)
  starting transfers between devices  17.8 us (20%)
  other arithmetic  1.08 us (1%)
  between operations  0.91 us (1%)
    ppermute x7, waiting for transfers between devices, trade(): lax.ppermute(array, axis, [(i, i ^ bits) for i in range(lax.axis_size(axi...  22.8 us
    pallas_call x4, Pallas kernels, prefix_attend(): pl.pallas_call(functools.partial(prefix_kernel, scale, heads, [len(terms)...  15.4 us
    ppermute x7, starting transfers between devices, trade(): lax.ppermute(array, axis, [(i, i ^ bits) for i in range(lax.axis_size(axi...  10.4 us
    pallas_call x2, Pallas kernels, fresh_attend(): pl.pallas_call(functools.partial(fresh_kernel, scale, heads, per_token, c...  10 us
    pallas_call x4, Pallas kernels, project(): pl.pallas_call(functools.partial(project_kernel, len(blocks), [len(terms)...  8.54 us
    ppermute x8, starting transfers between devices, shift(): lax.ppermute(array, axis, [(i, (i + step) % count) for i in range(count)])  7.38 us
    pallas_call x1, Pallas kernels, cut_tokens(): pl.pallas_call(functools.partial(cut_kernel, bits), grid_spec=pltpu.Prefe...  3.03 us
    pallas_call x1, Pallas kernels, arrange_weights(): pl.pallas_call(functools.partial(weight_kernel, ctx_count, heads, head_co...  2.47 us
  transfers between devices with their start and end apart: 15, of which 6 were waited for; matrix products, arithmetic and copies ran while one was open for 0% of the time, Pallas kernels for 37%

profile of v19, /device:TPU:0, one launch (start us, length us, event | category | flops | bytes accessed | tf_op | source)
XLA Modules:
  0.0 87.5 jit_solution(8072469479921128124)
XLA Ops:
  0.0 0.7 pad_add_fusion.place_ref
  0.7 3.0 %cut_tokens.1 = (bf16[256,1024]{1,0:T(8,128)(2,1)}, bf16[256,1024]{1,0:T(8,128)(2,1)}, bf16[256,1024]{1,0:T(8,128)(2,1)}) custom-call(s32[3]{0:T(128)} %pad_add_fusion.place_ref, bf16[256,4096]{1,0:T(8,128)(2,1)} %refs_1_.3), custom_call_target="tpu_custom_call" | custom-call | flops 20000000000 | bytes 1 | tf_op jit(solution)/shard_map/cut_tokens/pallas_call | solution.py:184
  3.7 5.1 %collective-permute-start = (bf16[256,1024]{1,0:T(8,128)(2,1)}, bf16[256,1024]{1,0:T(8,128)(2,1)S(1)}, u32[]{:S(2)}, u32[]{:S(2)}) collective-permute-start(bf16[256,1024]{1,0:T(8,128)(2,1)} %get-tuple-element.64), channel_id=1, source_target_pairs={{0,12},{4,8},{8,4},{12,0},{1,13},{5,9},{9,5},{13,1},{2,14},{6,10},... | collective-permute-start | bytes 1572872 | tf_op jit(solution)/shard_map/ppermute | solution.py:105
  8.8 0.0 collective-permute-start.1
  8.8 0.0 copy-start.2
  8.8 0.0 copy-start.3
  8.8 1.9 %arrange_pool.1 = (bf16[8,128,512]{2,1,0:T(8,128)(2,1)S(1)}, bf16[8,128,512]{2,1,0:T(8,128)(2,1)S(1)}) custom-call(s32[3]{0:T(128)S(1)} %copy-done, bf16[8,128,8,128]{3,2,1,0:T(8,128)(2,1)S(1)} %bitcast.45), custom_call_target="tpu_custom_call" | custom-call | flops 20000000000 | bytes 1 | tf_op jit(solution)/shard_map/arrange_pool/pallas_call | solution.py:234
  10.8 1.6 %collective-permute-start.3 = (bf16[8,128,512]{2,1,0:T(8,128)(2,1)S(1)}, bf16[8,128,512]{2,1,0:T(8,128)(2,1)S(1)}, u32[]{:S(2)}, u32[]{:S(2)}) collective-permute-start(bf16[8,128,512]{2,1,0:T(8,128)(2,1)S(1)} %get-tuple-element.74), channel_id=1, source_target_pairs={{0,2},{2,0},{1,3},{3,1},{4,6},{6,4},{5,7},{7,5},{8,10},{10,8},{9,1... | collective-permute-start | bytes 3145736 | tf_op jit(solution)/shard_map/ppermute | solution.py:101
  12.3 2.5 %arrange_weights.1.refs_2_ = bf16[2,2,1024,512]{3,2,1,0:T(8,128)(2,1)S(1)} custom-call(bf16[1024,8,128]{2,1,0:T(8,128)(2,1)S(1)} %bitcast.46, bf16[1024,8,128]{2,1,0:T(8,128)(2,1)S(1)} %bitcast.47), custom_call_target="tpu_custom_call" | custom-call | flops 20000000000 | bytes 1 | tf_op jit(solution)/shard_map/arrange_weights/pallas_call | solution.py:150
  14.8 0.8 collective-permute-start.5
  16.3 5.6 %collective-permute-done.refs_0_ = bf16[256,1024]{1,0:T(8,128)(2,1)S(1)} collective-permute-done((bf16[256,1024]{1,0:T(8,128)(2,1)}, bf16[256,1024]{1,0:T(8,128)(2,1)S(1)}, u32[]{:S(2)}, u32[]{:S(2)}) %collective-permute-start) | collective-permute-done | bytes 524320 | tf_op jit(solution)/shard_map/ppermute | solution.py:105
  21.9 11.5 %collective-permute-done.1.refs_1_ = bf16[256,1024]{1,0:T(8,128)(2,1)S(1)} collective-permute-done((bf16[256,1024]{1,0:T(8,128)(2,1)}, bf16[256,1024]{1,0:T(8,128)(2,1)S(1)}, u32[]{:S(2)}, u32[]{:S(2)}) %collective-permute-start.1) | collective-permute-done | bytes 524320 | tf_op jit(solution)/shard_map/ppermute | solution.py:105
  33.3 2.1 %early_away.1 = bf16[2,512,512]{2,1,0:T(8,128)(2,1)S(1)} custom-call(s32[3]{0:T(128)S(1)} %copy-done, bf16[256,1024]{1,0:T(8,128)(2,1)S(1)} %collective-permute-done.refs_0_, bf16[256,1024]{1,0:T(8,128)(2,1)S(1)} %collective-permute-done.1.refs_1_, bf16[2,2,1024,512]{3,2,1,0:T(8,128)(2,1)S(1)} %arrange_weights.1.refs_2_), custom_call_target="tpu_custom_call" | custom-call | flops 20000000000 | bytes 1 | tf_op jit(solution)/shard_map/early_away/pallas_call | solution.py:298
  35.4 0.1 collective-permute-start.2
  35.5 2.1 %early_kept.1.refs_0_.refs_3_ = f32[2,512,512]{2,1,0:T(8,128)S(1)} custom-call(s32[3]{0:T(128)S(1)} %copy-done, bf16[256,1024]{1,0:T(8,128)(2,1)S(1)} %collective-permute-done.refs_0_, bf16[256,1024]{1,0:T(8,128)(2,1)S(1)} %collective-permute-done.1.refs_1_, bf16[2,2,1024,512]{3,2,1,0:T(8,128)(2,1)S(1)} %arrange_weights.1.refs_2_), custom_call_target="tpu_custom_call" | custom-call | flops 20000000000 | bytes 1 | tf_op jit(solution)/shard_map/early_kept/pallas_call | solution.py:298
  37.6 0.0 copy-start.6
  37.6 0.5 collective-permute-done.2.refs_1_.refs_4_
  38.1 0.2 fusion.4
  38.3 0.0 collective-permute-done.3.refs_1_
  38.3 1.4 %collective-permute-start.4 = (bf16[256,512]{1,0:T(8,128)(2,1)S(1)}, bf16[256,512]{1,0:T(8,128)(2,1)S(1)}, u32[]{:S(2)}, u32[]{:S(2)}) collective-permute-start(bf16[256,512]{1,0:T(8,128)(2,1)S(1)} %get-tuple-element.81), channel_id=1, source_target_pairs={{0,2},{2,0},{1,3},{3,1},{4,6},{6,4},{5,7},{7,5},{8,10},{10,8},{9,1... | collective-permute-start | bytes 786440 | tf_op jit(solution)/shard_map/ppermute | solution.py:101
  39.8 0.6 collective-permute-start.6
  40.4 1.7 %pick_blocks.1 = (bf16[1024,256]{1,0:T(8,128)(2,1)S(1)}, bf16[288,1024]{1,0:T(8,128)(2,1)S(1)}) custom-call(s32[3]{0:T(128)S(1)} %copy-done, s32[8]{0:T(128)S(1)} %bitcast.54, bf16[8,128,512]{2,1,0:T(8,128)(2,1)S(1)} %get-tuple-element.75.refs_0_, bf16[8,128,512]{2,1,0:T(8,128)(2,1)S(1)} %collective-permute-done.3.refs_1_), custom_call_target="tpu_custom_call" | custom-call | flops 20000000000 | bytes 1 | tf_op jit(solution)/shard_map/pick_blocks/pallas_call | solution.py:362
  42.1 7.7 %prefix_attend.4 = (f32[128,4096]{1,0:T(8,128)S(1)}, f32[8,4096]{1,0:T(8,128)S(1)}) custom-call(bf16[8192,128]{1,0:T(8,128)(2,1)S(1)} %bitcast.48, bf16[1024,256]{1,0:T(8,128)(2,1)S(1)} %get-tuple-element.88.keys, bf16[288,1024]{1,0:T(8,128)(2,1)S(1)} %get-tuple-element.89.values), custom_call_target="tpu_custom_call" | custom-call | flops 20000000000 | bytes 1 | tf_op jit(solution)/shard_map/prefix_attend/pallas_call | solution.py:445
  49.9 0.0 copy-start.4
  49.9 0.0 collective-permute-done.4.refs_2_
  49.9 3.9 %prefix_attend.5 = (f32[128,4096]{1,0:T(8,128)S(1)}, f32[8,4096]{1,0:T(8,128)S(1)}, bf16[256,512]{1,0:T(8,128)(2,1)S(1)}) custom-call(bf16[8192,128]{1,0:T(8,128)(2,1)S(1)} %bitcast.49, bf16[1024,256]{1,0:T(8,128)(2,1)S(1)} %get-tuple-element.88.keys, bf16[288,1024]{1,0:T(8,128)(2,1)S(1)} %get-tuple-element.89.values, ...), custom_call_target="tpu_custom_call" | custom-call | flops 20000000000 | bytes 1 | tf_op jit(solution)/shard_map/prefix_attend/pallas_call | solution.py:445
  53.8 0.0 collective-permute-done.5.refs_0_
  53.9 2.2 %late_away.1 = (bf16[2,512,512]{2,1,0:T(8,128)(2,1)S(1)}, bf16[256,512]{1,0:T(8,128)(2,1)S(1)}) custom-call(s32[3]{0:T(128)S(1)} %copy-done, bf16[256,1024]{1,0:T(8,128)(2,1)S(1)} %collective-permute-done.5.refs_0_, bf16[256,4096]{1,0:T(8,128)(2,1)S(1)} %copy-done.4, bf16[2,2,1024,512]{3,2,1,0:T(8,128)(2,1)S(1)} %arrange_weights.1.refs_2_, ...), custom_call_target="tpu_custom_call" | custom-call | flops 20000000000 | bytes 1 | tf_op jit(solution)/shard_map/late_away/pallas_call | solution.py:298
  56.1 0.1 collective-permute-start.7
  56.2 1.8 %collective-permute-start.9 = (bf16[256,512]{1,0:T(8,128)(2,1)S(1)}, bf16[256,512]{1,0:T(8,128)(2,1)S(1)}, u32[]{:S(2)}, u32[]{:S(2)}) collective-permute-start(bf16[256,512]{1,0:T(8,128)(2,1)S(1)} %get-tuple-element.90), channel_id=1, source_target_pairs={{0,4},{4,0},{8,12},{12,8},{1,5},{5,1},{9,13},{13,9},{2,6},{6,2},{1... | collective-permute-start | bytes 786440 | tf_op jit(solution)/shard_map/ppermute | solution.py:105
  58.0 0.3 collective-permute-start.12
  58.3 2.1 %late_kept.1.rest_0_.rest_1_ = f32[2,512,512]{2,1,0:T(8,128)S(1)} custom-call(s32[3]{0:T(128)S(1)} %copy-done, bf16[256,1024]{1,0:T(8,128)(2,1)S(1)} %collective-permute-done.5.refs_0_, bf16[256,4096]{1,0:T(8,128)(2,1)S(1)} %copy-done.4, bf16[2,2,1024,512]{3,2,1,0:T(8,128)(2,1)S(1)} %arrange_weights.1.refs_2_), custom_call_target="tpu_custom_call" | custom-call | flops 20000000000 | bytes 1 | tf_op jit(solution)/shard_map/late_kept/pallas_call | solution.py:298
  60.4 0.1 fusion.15
  60.5 1.5 %collective-permute-start.8 = (bf16[128,512]{1,0:T(8,128)(2,1)S(1)}, bf16[128,512]{1,0:T(8,128)(2,1)S(1)}, u32[]{:S(2)}, u32[]{:S(2)}) collective-permute-start(bf16[128,512]{1,0:T(8,128)(2,1)S(1)} %get-tuple-element.117), channel_id=1, source_target_pairs={{0,2},{2,0},{1,3},{3,1},{4,6},{6,4},{5,7},{7,5},{8,10},{10,8},{9,1... | collective-permute-start | bytes 393224 | tf_op jit(solution)/shard_map/ppermute | solution.py:101
  62.0 1.9 %prefix_attend.6 = (f32[128,4096]{1,0:T(8,128)S(1)}, f32[8,4096]{1,0:T(8,128)S(1)}) custom-call(bf16[8192,128]{1,0:T(8,128)(2,1)S(1)} %bitcast.50, bf16[1024,256]{1,0:T(8,128)(2,1)S(1)} %get-tuple-element.88.keys, bf16[288,1024]{1,0:T(8,128)(2,1)S(1)} %get-tuple-element.89.values, ...), custom_call_target="tpu_custom_call", output_to_operand_aliasing={{0}: (3, {}), {1}: (4, {})} | custom-call | flops 20000000000 | bytes 1 | tf_op jit(solution)/shard_map/prefix_attend/pallas_call | solution.py:445
  63.9 0.1 fusion.5
  63.9 0.7 collective-permute-start.10
  64.6 1.4 %collective-permute-start.11 = (bf16[256,512]{1,0:T(8,128)(2,1)S(1)}, bf16[256,512]{1,0:T(8,128)(2,1)S(1)}, u32[]{:S(2)}, u32[]{:S(2)}) collective-permute-start(bf16[256,512]{1,0:T(8,128)(2,1)S(1)} %fusion.5), channel_id=1, source_target_pairs={{0,2},{2,0},{1,3},{3,1},{4,6},{6,4},{5,7},{7,5},{8,10},{10,8},{9,1... | collective-permute-start | bytes 786440 | tf_op jit(solution)/shard_map/ppermute | solution.py:101
  66.0 0.1 fusion.10
  66.1 1.2 %collective-permute-start.13 = (bf16[128,512]{1,0:T(8,128)(2,1)S(1)}, bf16[128,512]{1,0:T(8,128)(2,1)S(1)}, u32[]{:S(2)}, u32[]{:S(2)}) collective-permute-start(bf16[128,512]{1,0:T(8,128)(2,1)S(1)} %fusion.10), channel_id=1, source_target_pairs={{0,8},{4,12},{8,0},{12,4},{1,9},{5,13},{9,1},{13,5},{2,10},{6,14},... | collective-permute-start | bytes 393224 | tf_op jit(solution)/shard_map/ppermute | solution.py:105
  67.3 1.8 %prefix_attend.7 = (f32[128,4096]{1,0:T(8,128)S(1)}, f32[8,4096]{1,0:T(8,128)S(1)}) custom-call(bf16[8192,128]{1,0:T(8,128)(2,1)S(1)} %bitcast.51, bf16[1024,256]{1,0:T(8,128)(2,1)S(1)} %get-tuple-element.88.keys, bf16[288,1024]{1,0:T(8,128)(2,1)S(1)} %get-tuple-element.89.values, ...), custom_call_target="tpu_custom_call", output_to_operand_aliasing={{0}: (3, {}), {1}: (4, {})} | custom-call | flops 20000000000 | bytes 1 | tf_op jit(solution)/shard_map/prefix_attend/pallas_call | solution.py:445
  69.1 1.3 %collective-permute-done.10 = bf16[128,512]{1,0:T(8,128)(2,1)S(1)} collective-permute-done((bf16[128,512]{1,0:T(8,128)(2,1)S(1)}, bf16[128,512]{1,0:T(8,128)(2,1)S(1)}, u32[]{:S(2)}, u32[]{:S(2)}) %collective-permute-start.10) | collective-permute-done | bytes 131104 | tf_op jit(solution)/shard_map/ppermute | solution.py:101
  70.4 0.1 fusion.13
  70.5 4.4 %collective-permute-done.13.rest_4_ = bf16[128,512]{1,0:T(8,128)(2,1)S(1)} collective-permute-done((bf16[128,512]{1,0:T(8,128)(2,1)S(1)}, bf16[128,512]{1,0:T(8,128)(2,1)S(1)}, u32[]{:S(2)}, u32[]{:S(2)}) %collective-permute-start.13) | collective-permute-done | bytes 131104 | tf_op jit(solution)/shard_map/ppermute | solution.py:105
  74.9 1.2 %collective-permute-start.14 = (bf16[128,512]{1,0:T(8,128)(2,1)S(1)}, bf16[128,512]{1,0:T(8,128)(2,1)S(1)}, u32[]{:S(2)}, u32[]{:S(2)}) collective-permute-start(bf16[128,512]{1,0:T(8,128)(2,1)S(1)} %fusion.13), channel_id=1, source_target_pairs={{0,8},{4,12},{8,0},{12,4},{1,9},{5,13},{9,1},{13,5},{2,10},{6,14},... | collective-permute-start | bytes 393224 | tf_op jit(solution)/shard_map/ppermute | solution.py:105
  76.1 4.7 %fresh_attend.2 = (bf16[8192,128]{1,0:T(8,128)(2,1)}, bf16[128,512]{1,0:T(8,128)(2,1)S(1)}) custom-call(s32[1]{0:T(128)S(6)} %copy.21.length_ref, bf16[8192,128]{1,0:T(8,128)(2,1)S(1)} %bitcast.52, f32[128,4096]{1,0:T(8,128)S(1)} %get-tuple-element.102.acc_ref, f32[8,4096]{1,0:T(8,128)S(1)} %get-tuple-element.103.stat_ref, ...), custom_call_target="tpu_custom_call" | custom-call | flops 20000000000 | bytes 1 | tf_op jit(solution)/shard_map/fresh_attend/pallas_call | solution.py:534
  80.8 1.4 %collective-permute-done.14.rest_5_ = bf16[128,512]{1,0:T(8,128)(2,1)S(1)} collective-permute-done((bf16[128,512]{1,0:T(8,128)(2,1)S(1)}, bf16[128,512]{1,0:T(8,128)(2,1)S(1)}, u32[]{:S(2)}, u32[]{:S(2)}) %collective-permute-start.14) | collective-permute-done | bytes 131104 | tf_op jit(solution)/shard_map/ppermute | solution.py:105
  82.2 5.3 %fresh_attend.3 = (bf16[8192,128]{1,0:T(8,128)(2,1)}, bf16[128,512]{1,0:T(8,128)(2,1)}) custom-call(s32[1]{0:T(128)S(6)} %copy.21.length_ref, bf16[8192,128]{1,0:T(8,128)(2,1)S(1)} %bitcast.53, f32[128,4096]{1,0:T(8,128)S(1)} %get-tuple-element.100.acc_ref, f32[8,4096]{1,0:T(8,128)S(1)} %get-tuple-element.101.stat_ref, ...), custom_call_target="tpu_custom_call", output_to_operand_aliasing={{0}: (10, {})} | custom-call | flops 20000000000 | bytes 1 | tf_op jit(solution)/shard_map/fresh_attend/pallas_call | solution.py:534
  (18 shorter events, 0.0 us)
Async XLA Ops:
  0.7 8.2 %copy-start = (s32[3]{0:T(128)S(1)}, s32[3]{0:T(128)}, u32[]{:S(2)}) copy-start(s32[3]{0:T(128)} %pad_add_fusion.place_ref) | copy-start | bytes 40
  0.7 8.2 %copy-start.1 = (bf16[8,128,4,1,256]{4,2,3,1,0:T(4,128)(2,1)S(1)}, bf16[8,128,4,1,256]{4,2,3,1,0:T(4,128)(2,1)}, u32[]{:S(2)}) copy-start(bf16[8,128,4,1,256]{4,2,3,1,0:T(4,128)(2,1)} %param.11) | copy-start | bytes 6291460
  3.7 18.2 %collective-permute-start = (bf16[256,1024]{1,0:T(8,128)(2,1)}, bf16[256,1024]{1,0:T(8,128)(2,1)S(1)}, u32[]{:S(2)}, u32[]{:S(2)}) collective-permute-start(bf16[256,1024]{1,0:T(8,128)(2,1)} %get-tuple-element.64), channel_id=1, source_target_pairs={{0,12},{4,8},{8,4},{12,0},{1,13},{5,9},{9,5},{13,1},{2,14},{6,10},... | collective-permute-start | bytes 1572872 | tf_op jit(solution)/shard_map/ppermute | solution.py:105
  8.8 24.5 %collective-permute-start.1 = (bf16[256,1024]{1,0:T(8,128)(2,1)}, bf16[256,1024]{1,0:T(8,128)(2,1)S(1)}, u32[]{:S(2)}, u32[]{:S(2)}) collective-permute-start(bf16[256,1024]{1,0:T(8,128)(2,1)} %get-tuple-element.65), channel_id=1, source_target_pairs={{0,4},{4,0},{8,12},{12,8},{1,5},{5,1},{9,13},{13,9},{2,6},{6,2},{1... | collective-permute-start | bytes 1572872 | tf_op jit(solution)/shard_map/ppermute | solution.py:105
  8.8 3.5 %copy-start.2 = (bf16[1,1,1024,4,2,128]{5,4,3,2,1,0:T(2,128)(2,1)S(1)}, bf16[1,1,1024,4,2,128]{5,4,3,2,1,0:T(2,128)(2,1)}, u32[]{:S(2)}) copy-start(bf16[1,1,1024,4,2,128]{5,4,3,2,1,0:T(2,128)(2,1)} %param.8) | copy-start | bytes 6291460
  8.8 3.5 %copy-start.3 = (bf16[1,1,1024,4,2,128]{5,4,3,2,1,0:T(2,128)(2,1)S(1)}, bf16[1,1,1024,4,2,128]{5,4,3,2,1,0:T(2,128)(2,1)}, u32[]{:S(2)}) copy-start(bf16[1,1,1024,4,2,128]{5,4,3,2,1,0:T(2,128)(2,1)} %param.9) | copy-start | bytes 6291460
  10.8 27.6 %collective-permute-start.3 = (bf16[8,128,512]{2,1,0:T(8,128)(2,1)S(1)}, bf16[8,128,512]{2,1,0:T(8,128)(2,1)S(1)}, u32[]{:S(2)}, u32[]{:S(2)}) collective-permute-start(bf16[8,128,512]{2,1,0:T(8,128)(2,1)S(1)} %get-tuple-element.74), channel_id=1, source_target_pairs={{0,2},{2,0},{1,3},{3,1},{4,6},{6,4},{5,7},{7,5},{8,10},{10,8},{9,1... | collective-permute-start | bytes 3145736 | tf_op jit(solution)/shard_map/ppermute | solution.py:101
  12.3 2.5 %copy-start.7 = (bf16[256,1024]{1,0:T(8,128)(2,1)S(1)}, bf16[256,1024]{1,0:T(8,128)(2,1)}, u32[]{:S(2)}) copy-start(bf16[256,1024]{1,0:T(8,128)(2,1)} %get-tuple-element.84) | copy-start | bytes 1572868
  14.8 39.0 %collective-permute-start.5 = (bf16[256,1024]{1,0:T(8,128)(2,1)S(1)}, bf16[256,1024]{1,0:T(8,128)(2,1)S(1)}, u32[]{:S(2)}, u32[]{:S(2)}) collective-permute-start(bf16[256,1024]{1,0:T(8,128)(2,1)S(1)} %copy-done.7), channel_id=1, source_target_pairs={{0,8},{4,12},{8,0},{12,4},{1,9},{5,13},{9,1},{13,5},{2,10},{6,14},... | collective-permute-start | bytes 1572872 | tf_op jit(solution)/shard_map/ppermute | solution.py:105
  35.4 2.7 %collective-permute-start.2 = (bf16[2,512,512]{2,1,0:T(8,128)(2,1)S(1)}, bf16[2,512,512]{2,1,0:T(8,128)(2,1)S(1)}, u32[]{:S(2)}, u32[]{:S(2)}) collective-permute-start(bf16[2,512,512]{2,1,0:T(8,128)(2,1)S(1)} %early_away.1), channel_id=1, source_target_pairs={{0,1},{1,0},{2,3},{3,2},{4,5},{5,4},{6,7},{7,6},{8,9},{9,8},{10,11... | collective-permute-start | bytes 3145736 | tf_op jit(solution)/shard_map/ppermute | solution.py:101
  37.6 2.8 %copy-start.6 = (s32[1,8]{1,0:T(1,128)S(1)}, s32[1,8]{1,0:T(1,128)}, u32[]{:S(2)}) copy-start(s32[1,8]{1,0:T(1,128)} %param.12) | copy-start | bytes 100
  38.3 11.6 %collective-permute-start.4 = (bf16[256,512]{1,0:T(8,128)(2,1)S(1)}, bf16[256,512]{1,0:T(8,128)(2,1)S(1)}, u32[]{:S(2)}, u32[]{:S(2)}) collective-permute-start(bf16[256,512]{1,0:T(8,128)(2,1)S(1)} %get-tuple-element.81), channel_id=1, source_target_pairs={{0,2},{2,0},{1,3},{3,1},{4,6},{6,4},{5,7},{7,5},{8,10},{10,8},{9,1... | collective-permute-start | bytes 786440 | tf_op jit(solution)/shard_map/ppermute | solution.py:101
  39.8 14.1 %collective-permute-start.6 = (bf16[256,512]{1,0:T(8,128)(2,1)S(1)}, bf16[256,512]{1,0:T(8,128)(2,1)S(1)}, u32[]{:S(2)}, u32[]{:S(2)}) collective-permute-start(bf16[256,512]{1,0:T(8,128)(2,1)S(1)} %get-tuple-element.86), channel_id=1, source_target_pairs={{0,2},{2,0},{1,3},{3,1},{4,6},{6,4},{5,7},{7,5},{8,10},{10,8},{9,1... | collective-permute-start | bytes 786440 | tf_op jit(solution)/shard_map/ppermute | solution.py:101
  40.4 1.7 %copy-start.5 = (bf16[256,2,1,2048]{3,1,2,0:T(2,128)(2,1)S(1)}, bf16[256,2,1,2048]{3,1,2,0:T(2,128)(2,1)}, u32[]{:S(2)}) copy-start(bf16[256,2,1,2048]{3,1,2,0:T(2,128)(2,1)} %param.10) | copy-start | bytes 6291460
  49.9 4.0 %copy-start.4 = (bf16[256,4096]{1,0:T(8,128)(2,1)S(1)}, bf16[256,4096]{1,0:T(8,128)(2,1)}, u32[]{:S(2)}) copy-start(bf16[256,4096]{1,0:T(8,128)(2,1)} %refs_1_.3) | copy-start | bytes 6291460
  56.1 4.3 %collective-permute-start.7 = (bf16[2,512,512]{2,1,0:T(8,128)(2,1)S(1)}, bf16[2,512,512]{2,1,0:T(8,128)(2,1)S(1)}, u32[]{:S(2)}, u32[]{:S(2)}) collective-permute-start(bf16[2,512,512]{2,1,0:T(8,128)(2,1)S(1)} %get-tuple-element.87), channel_id=1, source_target_pairs={{0,1},{1,0},{2,3},{3,2},{4,5},{5,4},{6,7},{7,6},{8,9},{9,8},{10,11... | collective-permute-start | bytes 3145736 | tf_op jit(solution)/shard_map/ppermute | solution.py:101
  56.2 9.8 %collective-permute-start.9 = (bf16[256,512]{1,0:T(8,128)(2,1)S(1)}, bf16[256,512]{1,0:T(8,128)(2,1)S(1)}, u32[]{:S(2)}, u32[]{:S(2)}) collective-permute-start(bf16[256,512]{1,0:T(8,128)(2,1)S(1)} %get-tuple-element.90), channel_id=1, source_target_pairs={{0,4},{4,0},{8,12},{12,8},{1,5},{5,1},{9,13},{13,9},{2,6},{6,2},{1... | collective-permute-start | bytes 786440 | tf_op jit(solution)/shard_map/ppermute | solution.py:105
  58.0 18.1 %collective-permute-start.12 = (bf16[256,512]{1,0:T(8,128)(2,1)S(1)}, bf16[256,512]{1,0:T(8,128)(2,1)S(1)}, u32[]{:S(2)}, u32[]{:S(2)}) collective-permute-start(bf16[256,512]{1,0:T(8,128)(2,1)S(1)} %get-tuple-element.108), channel_id=1, source_target_pairs={{0,4},{4,0},{8,12},{12,8},{1,5},{5,1},{9,13},{13,9},{2,6},{6,2},{1... | collective-permute-start | bytes 786440 | tf_op jit(solution)/shard_map/ppermute | solution.py:105
  60.5 5.5 %collective-permute-start.8 = (bf16[128,512]{1,0:T(8,128)(2,1)S(1)}, bf16[128,512]{1,0:T(8,128)(2,1)S(1)}, u32[]{:S(2)}, u32[]{:S(2)}) collective-permute-start(bf16[128,512]{1,0:T(8,128)(2,1)S(1)} %get-tuple-element.117), channel_id=1, source_target_pairs={{0,2},{2,0},{1,3},{3,1},{4,6},{6,4},{5,7},{7,5},{8,10},{10,8},{9,1... | collective-permute-start | bytes 393224 | tf_op jit(solution)/shard_map/ppermute | solution.py:101
  63.9 6.5 %collective-permute-start.10 = (bf16[128,512]{1,0:T(8,128)(2,1)S(1)}, bf16[128,512]{1,0:T(8,128)(2,1)S(1)}, u32[]{:S(2)}, u32[]{:S(2)}) collective-permute-start(bf16[128,512]{1,0:T(8,128)(2,1)S(1)} %get-tuple-element.104), channel_id=1, source_target_pairs={{0,2},{2,0},{1,3},{3,1},{4,6},{6,4},{5,7},{7,5},{8,10},{10,8},{9,1... | collective-permute-start | bytes 393224 | tf_op jit(solution)/shard_map/ppermute | solution.py:101
  64.6 11.5 %collective-permute-start.11 = (bf16[256,512]{1,0:T(8,128)(2,1)S(1)}, bf16[256,512]{1,0:T(8,128)(2,1)S(1)}, u32[]{:S(2)}, u32[]{:S(2)}) collective-permute-start(bf16[256,512]{1,0:T(8,128)(2,1)S(1)} %fusion.5), channel_id=1, source_target_pairs={{0,2},{2,0},{1,3},{3,1},{4,6},{6,4},{5,7},{7,5},{8,10},{10,8},{9,1... | collective-permute-start | bytes 786440 | tf_op jit(solution)/shard_map/ppermute | solution.py:101
  66.1 8.7 %collective-permute-start.13 = (bf16[128,512]{1,0:T(8,128)(2,1)S(1)}, bf16[128,512]{1,0:T(8,128)(2,1)S(1)}, u32[]{:S(2)}, u32[]{:S(2)}) collective-permute-start(bf16[128,512]{1,0:T(8,128)(2,1)S(1)} %fusion.10), channel_id=1, source_target_pairs={{0,8},{4,12},{8,0},{12,4},{1,9},{5,13},{9,1},{13,5},{2,10},{6,14},... | collective-permute-start | bytes 393224 | tf_op jit(solution)/shard_map/ppermute | solution.py:105
  74.9 7.3 %collective-permute-start.14 = (bf16[128,512]{1,0:T(8,128)(2,1)S(1)}, bf16[128,512]{1,0:T(8,128)(2,1)S(1)}, u32[]{:S(2)}, u32[]{:S(2)}) collective-permute-start(bf16[128,512]{1,0:T(8,128)(2,1)S(1)} %fusion.13), channel_id=1, source_target_pairs={{0,8},{4,12},{8,0},{12,4},{1,9},{5,13},{9,1},{13,5},{2,10},{6,14},... | collective-permute-start | bytes 393224 | tf_op jit(solution)/shard_map/ppermute | solution.py:105

commit v20 on v19

--- a/solution.py
+++ b/solution.py
@@ -419,7 +419,7 @@
     all_rows, width = query_rows.shape
     row_total = all_rows // CHUNKS
     at, count = part
-    rows = min(1024, row_total // count)
+    rows = min(2048, row_total // count)
     steps = row_total // rows // count
     first = chunk * count * steps + at * steps
     out_specs = [
@@ -512,7 +512,7 @@
 ):
     row_total, width = query_rows.shape
     chunk_rows = row_total // CHUNKS
-    rows = min(1024, chunk_rows)
+    rows = min(2048, chunk_rows)
     steps = chunk_rows // rows
     block = pl.BlockSpec((rows, width), lambda i, length: (chunk * steps + i, 0))
     fresh_shape = pieces[0][1].block_shape[-2:]
@@ -640,7 +640,7 @@
     terms, near = [], []
     for step in range(1, head_count):
         term, *made = late_project(step, jnp.bfloat16, "late_away", sums[1] if step == 1 else [])
-        near += [trade(part, "batch", 1) for part in made]
+        near += made
         terms.append(shift(term, "head", step))
     kept, *_ = late_project(0, jnp.float32, "late_kept", [])
     late = [kept, *terms]
@@ -659,7 +659,8 @@
         part = part.astype(jnp.bfloat16)
         if chunk == 0:
             (far, late), late_others[1] = after((far, late), late_others[1])
-            part, state = after(part, state)
+            part, (state, near) = after(part, (state, near))
+            near = [trade(piece, "batch", 1) for piece in near]
         else:
             away[-1], part = after(away[-1], part)
         away.append(trade(part, "batch", top))

time: 87.7 us -> 87.1 us (level)
  Pallas kernels: 43 us -> 41.1 us
  waiting for transfers between devices: 24.7 us -> 25.8 us
    ppermute x7, waiting for transfers between devices: 22.8 us -> 25.2 us  [trade(): lax.ppermute(array, axis, [(i, i ^ bits) for i in range(lax.axis_size(axi...]
    ppermute x8, waiting for transfers between devices: 1.85 us -> 0.57 us  [shift(): lax.ppermute(array, axis, [(i, (i + step) % count) for i in range(count)])]
    pallas_call x2, Pallas kernels: 10 us -> 8.75 us  [fresh_attend(): pl.pallas_call(functools.partial(fresh_kernel, scale, heads, per_token, c...]
  transfers between devices with their start and end apart: 15 -> 15, of which waited for: 6 -> 7; matrix products, arithmetic and copies ran while one was open for 0% -> 0% of each run, Pallas kernels for 37% -> 36%
where the time goes in v20:
time: 87.1 us; the launch traced here: 87 us
  Pallas kernels  41.1 us (47%)
  waiting for transfers between devices  25.8 us (30%)
  starting transfers between devices  18.1 us (21%)
  other arithmetic  1.08 us (1%)
  between operations  0.89 us (1%)
    ppermute x7, waiting for transfers between devices, trade(): lax.ppermute(array, axis, [(i, i ^ bits) for i in range(lax.axis_size(axi...  25.2 us
    pallas_call x4, Pallas kernels, prefix_attend(): pl.pallas_call(functools.partial(prefix_kernel, scale, heads, [len(terms)...  14.7 us
    ppermute x7, starting transfers between devices, trade(): lax.ppermute(array, axis, [(i, i ^ bits) for i in range(lax.axis_size(axi...  10.6 us
    pallas_call x2, Pallas kernels, fresh_attend(): pl.pallas_call(functools.partial(fresh_kernel, scale, heads, per_token, c...  8.75 us
    pallas_call x4, Pallas kernels, project(): pl.pallas_call(functools.partial(project_kernel, len(blocks), [len(terms)...  8.53 us
    ppermute x8, starting transfers between devices, shift(): lax.ppermute(array, axis, [(i, (i + step) % count) for i in range(count)])  7.46 us
    pallas_call x1, Pallas kernels, cut_tokens(): pl.pallas_call(functools.partial(cut_kernel, bits), grid_spec=pltpu.Prefe...  3.03 us
    pallas_call x1, Pallas kernels, arrange_weights(): pl.pallas_call(functools.partial(weight_kernel, ctx_count, heads, head_co...  2.47 us
  transfers between devices with their start and end apart: 15, of which 7 were waited for; matrix products, arithmetic and copies ran while one was open for 0% of the time, Pallas kernels for 36%

profile of v20, /device:TPU:0, one launch (start us, length us, event | category | flops | bytes accessed | tf_op | source)
XLA Modules:
  0.0 87.0 jit_solution(11596015994510955037)
XLA Ops:
  0.0 0.7 pad_add_fusion.place_ref
  0.7 3.0 %cut_tokens.1 = (bf16[256,1024]{1,0:T(8,128)(2,1)}, bf16[256,1024]{1,0:T(8,128)(2,1)}, bf16[256,1024]{1,0:T(8,128)(2,1)}) custom-call(s32[3]{0:T(128)} %pad_add_fusion.place_ref, bf16[256,4096]{1,0:T(8,128)(2,1)} %refs_1_.3), custom_call_target="tpu_custom_call" | custom-call | flops 20000000000 | bytes 1 | tf_op jit(solution)/shard_map/cut_tokens/pallas_call | solution.py:184
  3.7 5.1 %collective-permute-start = (bf16[256,1024]{1,0:T(8,128)(2,1)}, bf16[256,1024]{1,0:T(8,128)(2,1)S(1)}, u32[]{:S(2)}, u32[]{:S(2)}) collective-permute-start(bf16[256,1024]{1,0:T(8,128)(2,1)} %get-tuple-element.65), channel_id=1, source_target_pairs={{0,12},{4,8},{8,4},{12,0},{1,13},{5,9},{9,5},{13,1},{2,14},{6,10},... | collective-permute-start | bytes 1572872 | tf_op jit(solution)/shard_map/ppermute | solution.py:105
  8.8 0.0 collective-permute-start.1
  8.8 0.0 copy-start.2
  8.8 0.0 copy-start.3
  8.8 1.9 %arrange_pool.1 = (bf16[8,128,512]{2,1,0:T(8,128)(2,1)S(1)}, bf16[8,128,512]{2,1,0:T(8,128)(2,1)S(1)}) custom-call(s32[3]{0:T(128)S(1)} %copy-done, bf16[8,128,8,128]{3,2,1,0:T(8,128)(2,1)S(1)} %bitcast.45), custom_call_target="tpu_custom_call" | custom-call | flops 20000000000 | bytes 1 | tf_op jit(solution)/shard_map/arrange_pool/pallas_call | solution.py:234
  10.8 1.6 %collective-permute-start.3 = (bf16[8,128,512]{2,1,0:T(8,128)(2,1)S(1)}, bf16[8,128,512]{2,1,0:T(8,128)(2,1)S(1)}, u32[]{:S(2)}, u32[]{:S(2)}) collective-permute-start(bf16[8,128,512]{2,1,0:T(8,128)(2,1)S(1)} %get-tuple-element.75), channel_id=1, source_target_pairs={{0,2},{2,0},{1,3},{3,1},{4,6},{6,4},{5,7},{7,5},{8,10},{10,8},{9,1... | collective-permute-start | bytes 3145736 | tf_op jit(solution)/shard_map/ppermute | solution.py:101
  12.3 2.5 %arrange_weights.1.refs_2_ = bf16[2,2,1024,512]{3,2,1,0:T(8,128)(2,1)S(1)} custom-call(bf16[1024,8,128]{2,1,0:T(8,128)(2,1)S(1)} %bitcast.46, bf16[1024,8,128]{2,1,0:T(8,128)(2,1)S(1)} %bitcast.47), custom_call_target="tpu_custom_call" | custom-call | flops 20000000000 | bytes 1 | tf_op jit(solution)/shard_map/arrange_weights/pallas_call | solution.py:150
  14.8 0.8 collective-permute-start.5
  16.3 5.6 %collective-permute-done.refs_0_ = bf16[256,1024]{1,0:T(8,128)(2,1)S(1)} collective-permute-done((bf16[256,1024]{1,0:T(8,128)(2,1)}, bf16[256,1024]{1,0:T(8,128)(2,1)S(1)}, u32[]{:S(2)}, u32[]{:S(2)}) %collective-permute-start) | collective-permute-done | bytes 524320 | tf_op jit(solution)/shard_map/ppermute | solution.py:105
  21.9 11.5 %collective-permute-done.1.refs_1_ = bf16[256,1024]{1,0:T(8,128)(2,1)S(1)} collective-permute-done((bf16[256,1024]{1,0:T(8,128)(2,1)}, bf16[256,1024]{1,0:T(8,128)(2,1)S(1)}, u32[]{:S(2)}, u32[]{:S(2)}) %collective-permute-start.1) | collective-permute-done | bytes 524320 | tf_op jit(solution)/shard_map/ppermute | solution.py:105
  33.3 2.1 %early_away.1 = bf16[2,512,512]{2,1,0:T(8,128)(2,1)S(1)} custom-call(s32[3]{0:T(128)S(1)} %copy-done, bf16[256,1024]{1,0:T(8,128)(2,1)S(1)} %collective-permute-done.refs_0_, bf16[256,1024]{1,0:T(8,128)(2,1)S(1)} %collective-permute-done.1.refs_1_, bf16[2,2,1024,512]{3,2,1,0:T(8,128)(2,1)S(1)} %arrange_weights.1.refs_2_), custom_call_target="tpu_custom_call" | custom-call | flops 20000000000 | bytes 1 | tf_op jit(solution)/shard_map/early_away/pallas_call | solution.py:298
  35.4 0.1 collective-permute-start.2
  35.5 2.1 %early_kept.1.refs_0_.refs_3_ = f32[2,512,512]{2,1,0:T(8,128)S(1)} custom-call(s32[3]{0:T(128)S(1)} %copy-done, bf16[256,1024]{1,0:T(8,128)(2,1)S(1)} %collective-permute-done.refs_0_, bf16[256,1024]{1,0:T(8,128)(2,1)S(1)} %collective-permute-done.1.refs_1_, bf16[2,2,1024,512]{3,2,1,0:T(8,128)(2,1)S(1)} %arrange_weights.1.refs_2_), custom_call_target="tpu_custom_call" | custom-call | flops 20000000000 | bytes 1 | tf_op jit(solution)/shard_map/early_kept/pallas_call | solution.py:298
  37.6 0.0 copy-start.6
  37.6 0.5 collective-permute-done.2.refs_1_.refs_4_
  38.1 0.2 fusion.4
  38.3 0.0 collective-permute-done.3.refs_1_
  38.3 1.4 %collective-permute-start.4 = (bf16[256,512]{1,0:T(8,128)(2,1)S(1)}, bf16[256,512]{1,0:T(8,128)(2,1)S(1)}, u32[]{:S(2)}, u32[]{:S(2)}) collective-permute-start(bf16[256,512]{1,0:T(8,128)(2,1)S(1)} %get-tuple-element.82), channel_id=1, source_target_pairs={{0,2},{2,0},{1,3},{3,1},{4,6},{6,4},{5,7},{7,5},{8,10},{10,8},{9,1... | collective-permute-start | bytes 786440 | tf_op jit(solution)/shard_map/ppermute | solution.py:101
  39.8 0.6 collective-permute-start.6
  40.4 1.7 %pick_blocks.1 = (bf16[1024,256]{1,0:T(8,128)(2,1)S(1)}, bf16[288,1024]{1,0:T(8,128)(2,1)S(1)}) custom-call(s32[3]{0:T(128)S(1)} %copy-done, s32[8]{0:T(128)S(1)} %bitcast.54, bf16[8,128,512]{2,1,0:T(8,128)(2,1)S(1)} %get-tuple-element.76.refs_0_, bf16[8,128,512]{2,1,0:T(8,128)(2,1)S(1)} %collective-permute-done.3.refs_1_), custom_call_target="tpu_custom_call" | custom-call | flops 20000000000 | bytes 1 | tf_op jit(solution)/shard_map/pick_blocks/pallas_call | solution.py:362
  42.1 7.3 %prefix_attend.4 = (f32[128,4096]{1,0:T(8,128)S(1)}, f32[8,4096]{1,0:T(8,128)S(1)}) custom-call(bf16[8192,128]{1,0:T(8,128)(2,1)S(1)} %bitcast.48, bf16[1024,256]{1,0:T(8,128)(2,1)S(1)} %get-tuple-element.89.keys, bf16[288,1024]{1,0:T(8,128)(2,1)S(1)} %get-tuple-element.90.values), custom_call_target="tpu_custom_call" | custom-call | flops 20000000000 | bytes 1 | tf_op jit(solution)/shard_map/prefix_attend/pallas_call | solution.py:445
  49.4 0.0 copy-start.4
  49.5 3.7 %prefix_attend.5 = (f32[128,4096]{1,0:T(8,128)S(1)}, f32[8,4096]{1,0:T(8,128)S(1)}, bf16[256,512]{1,0:T(8,128)(2,1)S(1)}) custom-call(bf16[8192,128]{1,0:T(8,128)(2,1)S(1)} %bitcast.49, bf16[1024,256]{1,0:T(8,128)(2,1)S(1)} %get-tuple-element.89.keys, bf16[288,1024]{1,0:T(8,128)(2,1)S(1)} %get-tuple-element.90.values, ...), custom_call_target="tpu_custom_call" | custom-call | flops 20000000000 | bytes 1 | tf_op jit(solution)/shard_map/prefix_attend/pallas_call | solution.py:445
  53.2 0.6 collective-permute-done.5.refs_0_
  53.8 2.2 %late_away.1 = (bf16[2,512,512]{2,1,0:T(8,128)(2,1)S(1)}, bf16[256,512]{1,0:T(8,128)(2,1)S(1)}) custom-call(s32[3]{0:T(128)S(1)} %copy-done, bf16[256,1024]{1,0:T(8,128)(2,1)S(1)} %collective-permute-done.5.refs_0_, bf16[256,4096]{1,0:T(8,128)(2,1)S(1)} %copy-done.4, bf16[2,2,1024,512]{3,2,1,0:T(8,128)(2,1)S(1)} %arrange_weights.1.refs_2_, ...), custom_call_target="tpu_custom_call" | custom-call | flops 20000000000 | bytes 1 | tf_op jit(solution)/shard_map/late_away/pallas_call | solution.py:298
  56.0 0.1 collective-permute-start.7
  56.1 1.2 %collective-permute-start.9 = (bf16[256,512]{1,0:T(8,128)(2,1)S(1)}, bf16[256,512]{1,0:T(8,128)(2,1)S(1)}, u32[]{:S(2)}, u32[]{:S(2)}) collective-permute-start(bf16[256,512]{1,0:T(8,128)(2,1)S(1)} %get-tuple-element.91), channel_id=1, source_target_pairs={{0,4},{4,0},{8,12},{12,8},{1,5},{5,1},{9,13},{13,9},{2,6},{6,2},{1... | collective-permute-start | bytes 786440 | tf_op jit(solution)/shard_map/ppermute | solution.py:105
  57.3 2.1 %late_kept.1.rest_0_.rest_1_ = f32[2,512,512]{2,1,0:T(8,128)S(1)} custom-call(s32[3]{0:T(128)S(1)} %copy-done, bf16[256,1024]{1,0:T(8,128)(2,1)S(1)} %collective-permute-done.5.refs_0_, bf16[256,4096]{1,0:T(8,128)(2,1)S(1)} %copy-done.4, bf16[2,2,1024,512]{3,2,1,0:T(8,128)(2,1)S(1)} %arrange_weights.1.refs_2_), custom_call_target="tpu_custom_call" | custom-call | flops 20000000000 | bytes 1 | tf_op jit(solution)/shard_map/late_kept/pallas_call | solution.py:298
  59.5 0.1 fusion.15
  59.6 1.6 %collective-permute-start.8 = (bf16[128,512]{1,0:T(8,128)(2,1)S(1)}, bf16[128,512]{1,0:T(8,128)(2,1)S(1)}, u32[]{:S(2)}, u32[]{:S(2)}) collective-permute-start(bf16[128,512]{1,0:T(8,128)(2,1)S(1)} %get-tuple-element.119), channel_id=1, source_target_pairs={{0,2},{2,0},{1,3},{3,1},{4,6},{6,4},{5,7},{7,5},{8,10},{10,8},{9,1... | collective-permute-start | bytes 393224 | tf_op jit(solution)/shard_map/ppermute | solution.py:101
  61.1 1.9 %prefix_attend.6 = (f32[128,4096]{1,0:T(8,128)S(1)}, f32[8,4096]{1,0:T(8,128)S(1)}) custom-call(bf16[8192,128]{1,0:T(8,128)(2,1)S(1)} %bitcast.50, bf16[1024,256]{1,0:T(8,128)(2,1)S(1)} %get-tuple-element.89.keys, bf16[288,1024]{1,0:T(8,128)(2,1)S(1)} %get-tuple-element.90.values, ...), custom_call_target="tpu_custom_call", output_to_operand_aliasing={{0}: (3, {}), {1}: (4, {})} | custom-call | flops 20000000000 | bytes 1 | tf_op jit(solution)/shard_map/prefix_attend/pallas_call | solution.py:445
  63.0 0.1 fusion.5
  63.1 0.6 collective-permute-start.10
  63.7 1.5 %collective-permute-start.11 = (bf16[256,512]{1,0:T(8,128)(2,1)S(1)}, bf16[256,512]{1,0:T(8,128)(2,1)S(1)}, u32[]{:S(2)}, u32[]{:S(2)}) collective-permute-start(bf16[256,512]{1,0:T(8,128)(2,1)S(1)} %fusion.5), channel_id=1, source_target_pairs={{0,2},{2,0},{1,3},{3,1},{4,6},{6,4},{5,7},{7,5},{8,10},{10,8},{9,1... | collective-permute-start | bytes 786440 | tf_op jit(solution)/shard_map/ppermute | solution.py:101
  65.2 0.0 collective-permute-done.8
  65.2 0.1 fusion.10
  65.3 2.0 %collective-permute-start.13 = (bf16[128,512]{1,0:T(8,128)(2,1)S(1)}, bf16[128,512]{1,0:T(8,128)(2,1)S(1)}, u32[]{:S(2)}, u32[]{:S(2)}) collective-permute-start(bf16[128,512]{1,0:T(8,128)(2,1)S(1)} %fusion.10), channel_id=1, source_target_pairs={{0,8},{4,12},{8,0},{12,4},{1,9},{5,13},{9,1},{13,5},{2,10},{6,14},... | collective-permute-start | bytes 393224 | tf_op jit(solution)/shard_map/ppermute | solution.py:105
  67.2 0.8 collective-permute-start.12
  68.0 1.9 %prefix_attend.7 = (f32[128,4096]{1,0:T(8,128)S(1)}, f32[8,4096]{1,0:T(8,128)S(1)}) custom-call(bf16[8192,128]{1,0:T(8,128)(2,1)S(1)} %bitcast.51, bf16[1024,256]{1,0:T(8,128)(2,1)S(1)} %get-tuple-element.89.keys, bf16[288,1024]{1,0:T(8,128)(2,1)S(1)} %get-tuple-element.90.values, ...), custom_call_target="tpu_custom_call", output_to_operand_aliasing={{0}: (3, {}), {1}: (4, {})} | custom-call | flops 20000000000 | bytes 1 | tf_op jit(solution)/shard_map/prefix_attend/pallas_call | solution.py:445
  69.9 0.1 fusion.13
  70.0 3.9 %collective-permute-done.13.rest_4_ = bf16[128,512]{1,0:T(8,128)(2,1)S(1)} collective-permute-done((bf16[128,512]{1,0:T(8,128)(2,1)S(1)}, bf16[128,512]{1,0:T(8,128)(2,1)S(1)}, u32[]{:S(2)}, u32[]{:S(2)}) %collective-permute-start.13) | collective-permute-done | bytes 131104 | tf_op jit(solution)/shard_map/ppermute | solution.py:105
  73.9 0.7 collective-permute-start.14
  74.6 2.1 %collective-permute-done.12.rest_3_.rest_4_ = bf16[256,512]{1,0:T(8,128)(2,1)S(1)} collective-permute-done((bf16[256,512]{1,0:T(8,128)(2,1)S(1)}, bf16[256,512]{1,0:T(8,128)(2,1)S(1)}, u32[]{:S(2)}, u32[]{:S(2)}) %collective-permute-start.12) | collective-permute-done | bytes 262176 | tf_op jit(solution)/shard_map/ppermute | solution.py:105
  76.6 4.0 %fresh_attend.2 = (bf16[8192,128]{1,0:T(8,128)(2,1)}, bf16[128,512]{1,0:T(8,128)(2,1)S(1)}) custom-call(s32[1]{0:T(128)S(6)} %copy.21.length_ref, bf16[8192,128]{1,0:T(8,128)(2,1)S(1)} %bitcast.52, f32[128,4096]{1,0:T(8,128)S(1)} %get-tuple-element.104.acc_ref, f32[8,4096]{1,0:T(8,128)S(1)} %get-tuple-element.105.stat_ref, ...), custom_call_target="tpu_custom_call" | custom-call | flops 20000000000 | bytes 1 | tf_op jit(solution)/shard_map/fresh_attend/pallas_call | solution.py:534
  80.7 1.6 %collective-permute-done.14.rest_5_ = bf16[128,512]{1,0:T(8,128)(2,1)S(1)} collective-permute-done((bf16[128,512]{1,0:T(8,128)(2,1)S(1)}, bf16[128,512]{1,0:T(8,128)(2,1)S(1)}, u32[]{:S(2)}, u32[]{:S(2)}) %collective-permute-start.14) | collective-permute-done | bytes 131104 | tf_op jit(solution)/shard_map/ppermute | solution.py:105
  82.3 4.7 %fresh_attend.3 = (bf16[8192,128]{1,0:T(8,128)(2,1)}, bf16[128,512]{1,0:T(8,128)(2,1)}) custom-call(s32[1]{0:T(128)S(6)} %copy.21.length_ref, bf16[8192,128]{1,0:T(8,128)(2,1)S(1)} %bitcast.53, f32[128,4096]{1,0:T(8,128)S(1)} %get-tuple-element.102.acc_ref, f32[8,4096]{1,0:T(8,128)S(1)} %get-tuple-element.103.stat_ref, ...), custom_call_target="tpu_custom_call", output_to_operand_aliasing={{0}: (10, {})} | custom-call | flops 20000000000 | bytes 1 | tf_op jit(solution)/shard_map/fresh_attend/pallas_call | solution.py:534
  (18 shorter events, 0.0 us)
Async XLA Ops:
  0.7 8.2 %copy-start = (s32[3]{0:T(128)S(1)}, s32[3]{0:T(128)}, u32[]{:S(2)}) copy-start(s32[3]{0:T(128)} %pad_add_fusion.place_ref) | copy-start | bytes 40
  0.7 8.2 %copy-start.1 = (bf16[8,128,4,1,256]{4,2,3,1,0:T(4,128)(2,1)S(1)}, bf16[8,128,4,1,256]{4,2,3,1,0:T(4,128)(2,1)}, u32[]{:S(2)}) copy-start(bf16[8,128,4,1,256]{4,2,3,1,0:T(4,128)(2,1)} %param.11) | copy-start | bytes 6291460
  3.7 18.2 %collective-permute-start = (bf16[256,1024]{1,0:T(8,128)(2,1)}, bf16[256,1024]{1,0:T(8,128)(2,1)S(1)}, u32[]{:S(2)}, u32[]{:S(2)}) collective-permute-start(bf16[256,1024]{1,0:T(8,128)(2,1)} %get-tuple-element.65), channel_id=1, source_target_pairs={{0,12},{4,8},{8,4},{12,0},{1,13},{5,9},{9,5},{13,1},{2,14},{6,10},... | collective-permute-start | bytes 1572872 | tf_op jit(solution)/shard_map/ppermute | solution.py:105
  8.8 24.5 %collective-permute-start.1 = (bf16[256,1024]{1,0:T(8,128)(2,1)}, bf16[256,1024]{1,0:T(8,128)(2,1)S(1)}, u32[]{:S(2)}, u32[]{:S(2)}) collective-permute-start(bf16[256,1024]{1,0:T(8,128)(2,1)} %get-tuple-element.66), channel_id=1, source_target_pairs={{0,4},{4,0},{8,12},{12,8},{1,5},{5,1},{9,13},{13,9},{2,6},{6,2},{1... | collective-permute-start | bytes 1572872 | tf_op jit(solution)/shard_map/ppermute | solution.py:105
  8.8 3.5 %copy-start.2 = (bf16[1,1,1024,4,2,128]{5,4,3,2,1,0:T(2,128)(2,1)S(1)}, bf16[1,1,1024,4,2,128]{5,4,3,2,1,0:T(2,128)(2,1)}, u32[]{:S(2)}) copy-start(bf16[1,1,1024,4,2,128]{5,4,3,2,1,0:T(2,128)(2,1)} %param.8) | copy-start | bytes 6291460
  8.8 3.5 %copy-start.3 = (bf16[1,1,1024,4,2,128]{5,4,3,2,1,0:T(2,128)(2,1)S(1)}, bf16[1,1,1024,4,2,128]{5,4,3,2,1,0:T(2,128)(2,1)}, u32[]{:S(2)}) copy-start(bf16[1,1,1024,4,2,128]{5,4,3,2,1,0:T(2,128)(2,1)} %param.9) | copy-start | bytes 6291460
  10.8 27.6 %collective-permute-start.3 = (bf16[8,128,512]{2,1,0:T(8,128)(2,1)S(1)}, bf16[8,128,512]{2,1,0:T(8,128)(2,1)S(1)}, u32[]{:S(2)}, u32[]{:S(2)}) collective-permute-start(bf16[8,128,512]{2,1,0:T(8,128)(2,1)S(1)} %get-tuple-element.75), channel_id=1, source_target_pairs={{0,2},{2,0},{1,3},{3,1},{4,6},{6,4},{5,7},{7,5},{8,10},{10,8},{9,1... | collective-permute-start | bytes 3145736 | tf_op jit(solution)/shard_map/ppermute | solution.py:101
  12.3 2.5 %copy-start.7 = (bf16[256,1024]{1,0:T(8,128)(2,1)S(1)}, bf16[256,1024]{1,0:T(8,128)(2,1)}, u32[]{:S(2)}) copy-start(bf16[256,1024]{1,0:T(8,128)(2,1)} %get-tuple-element.85) | copy-start | bytes 1572868
  14.8 39.0 %collective-permute-start.5 = (bf16[256,1024]{1,0:T(8,128)(2,1)S(1)}, bf16[256,1024]{1,0:T(8,128)(2,1)S(1)}, u32[]{:S(2)}, u32[]{:S(2)}) collective-permute-start(bf16[256,1024]{1,0:T(8,128)(2,1)S(1)} %copy-done.7), channel_id=1, source_target_pairs={{0,8},{4,12},{8,0},{12,4},{1,9},{5,13},{9,1},{13,5},{2,10},{6,14},... | collective-permute-start | bytes 1572872 | tf_op jit(solution)/shard_map/ppermute | solution.py:105
  35.4 2.7 %collective-permute-start.2 = (bf16[2,512,512]{2,1,0:T(8,128)(2,1)S(1)}, bf16[2,512,512]{2,1,0:T(8,128)(2,1)S(1)}, u32[]{:S(2)}, u32[]{:S(2)}) collective-permute-start(bf16[2,512,512]{2,1,0:T(8,128)(2,1)S(1)} %early_away.1), channel_id=1, source_target_pairs={{0,1},{1,0},{2,3},{3,2},{4,5},{5,4},{6,7},{7,6},{8,9},{9,8},{10,11... | collective-permute-start | bytes 3145736 | tf_op jit(solution)/shard_map/ppermute | solution.py:101
  37.6 2.8 %copy-start.6 = (s32[1,8]{1,0:T(1,128)S(1)}, s32[1,8]{1,0:T(1,128)}, u32[]{:S(2)}) copy-start(s32[1,8]{1,0:T(1,128)} %param.12) | copy-start | bytes 100
  38.3 11.1 %collective-permute-start.4 = (bf16[256,512]{1,0:T(8,128)(2,1)S(1)}, bf16[256,512]{1,0:T(8,128)(2,1)S(1)}, u32[]{:S(2)}, u32[]{:S(2)}) collective-permute-start(bf16[256,512]{1,0:T(8,128)(2,1)S(1)} %get-tuple-element.82), channel_id=1, source_target_pairs={{0,2},{2,0},{1,3},{3,1},{4,6},{6,4},{5,7},{7,5},{8,10},{10,8},{9,1... | collective-permute-start | bytes 786440 | tf_op jit(solution)/shard_map/ppermute | solution.py:101
  39.8 14.0 %collective-permute-start.6 = (bf16[256,512]{1,0:T(8,128)(2,1)S(1)}, bf16[256,512]{1,0:T(8,128)(2,1)S(1)}, u32[]{:S(2)}, u32[]{:S(2)}) collective-permute-start(bf16[256,512]{1,0:T(8,128)(2,1)S(1)} %get-tuple-element.87), channel_id=1, source_target_pairs={{0,2},{2,0},{1,3},{3,1},{4,6},{6,4},{5,7},{7,5},{8,10},{10,8},{9,1... | collective-permute-start | bytes 786440 | tf_op jit(solution)/shard_map/ppermute | solution.py:101
  40.4 1.7 %copy-start.5 = (bf16[256,2,1,2048]{3,1,2,0:T(2,128)(2,1)S(1)}, bf16[256,2,1,2048]{3,1,2,0:T(2,128)(2,1)}, u32[]{:S(2)}) copy-start(bf16[256,2,1,2048]{3,1,2,0:T(2,128)(2,1)} %param.10) | copy-start | bytes 6291460
  49.4 4.4 %copy-start.4 = (bf16[256,4096]{1,0:T(8,128)(2,1)S(1)}, bf16[256,4096]{1,0:T(8,128)(2,1)}, u32[]{:S(2)}) copy-start(bf16[256,4096]{1,0:T(8,128)(2,1)} %refs_1_.3) | copy-start | bytes 6291460
  56.0 3.4 %collective-permute-start.7 = (bf16[2,512,512]{2,1,0:T(8,128)(2,1)S(1)}, bf16[2,512,512]{2,1,0:T(8,128)(2,1)S(1)}, u32[]{:S(2)}, u32[]{:S(2)}) collective-permute-start(bf16[2,512,512]{2,1,0:T(8,128)(2,1)S(1)} %get-tuple-element.88), channel_id=1, source_target_pairs={{0,1},{1,0},{2,3},{3,2},{4,5},{5,4},{6,7},{7,6},{8,9},{9,8},{10,11... | collective-permute-start | bytes 3145736 | tf_op jit(solution)/shard_map/ppermute | solution.py:101
  56.1 9.1 %collective-permute-start.9 = (bf16[256,512]{1,0:T(8,128)(2,1)S(1)}, bf16[256,512]{1,0:T(8,128)(2,1)S(1)}, u32[]{:S(2)}, u32[]{:S(2)}) collective-permute-start(bf16[256,512]{1,0:T(8,128)(2,1)S(1)} %get-tuple-element.91), channel_id=1, source_target_pairs={{0,4},{4,0},{8,12},{12,8},{1,5},{5,1},{9,13},{13,9},{2,6},{6,2},{1... | collective-permute-start | bytes 786440 | tf_op jit(solution)/shard_map/ppermute | solution.py:105
  59.6 5.6 %collective-permute-start.8 = (bf16[128,512]{1,0:T(8,128)(2,1)S(1)}, bf16[128,512]{1,0:T(8,128)(2,1)S(1)}, u32[]{:S(2)}, u32[]{:S(2)}) collective-permute-start(bf16[128,512]{1,0:T(8,128)(2,1)S(1)} %get-tuple-element.119), channel_id=1, source_target_pairs={{0,2},{2,0},{1,3},{3,1},{4,6},{6,4},{5,7},{7,5},{8,10},{10,8},{9,1... | collective-permute-start | bytes 393224 | tf_op jit(solution)/shard_map/ppermute | solution.py:101
  63.1 6.8 %collective-permute-start.10 = (bf16[128,512]{1,0:T(8,128)(2,1)S(1)}, bf16[128,512]{1,0:T(8,128)(2,1)S(1)}, u32[]{:S(2)}, u32[]{:S(2)}) collective-permute-start(bf16[128,512]{1,0:T(8,128)(2,1)S(1)} %get-tuple-element.106), channel_id=1, source_target_pairs={{0,2},{2,0},{1,3},{3,1},{4,6},{6,4},{5,7},{7,5},{8,10},{10,8},{9,1... | collective-permute-start | bytes 393224 | tf_op jit(solution)/shard_map/ppermute | solution.py:101
  63.7 10.9 %collective-permute-start.11 = (bf16[256,512]{1,0:T(8,128)(2,1)S(1)}, bf16[256,512]{1,0:T(8,128)(2,1)S(1)}, u32[]{:S(2)}, u32[]{:S(2)}) collective-permute-start(bf16[256,512]{1,0:T(8,128)(2,1)S(1)} %fusion.5), channel_id=1, source_target_pairs={{0,2},{2,0},{1,3},{3,1},{4,6},{6,4},{5,7},{7,5},{8,10},{10,8},{9,1... | collective-permute-start | bytes 786440 | tf_op jit(solution)/shard_map/ppermute | solution.py:101
  65.3 8.6 %collective-permute-start.13 = (bf16[128,512]{1,0:T(8,128)(2,1)S(1)}, bf16[128,512]{1,0:T(8,128)(2,1)S(1)}, u32[]{:S(2)}, u32[]{:S(2)}) collective-permute-start(bf16[128,512]{1,0:T(8,128)(2,1)S(1)} %fusion.10), channel_id=1, source_target_pairs={{0,8},{4,12},{8,0},{12,4},{1,9},{5,13},{9,1},{13,5},{2,10},{6,14},... | collective-permute-start | bytes 393224 | tf_op jit(solution)/shard_map/ppermute | solution.py:105
  67.2 9.4 %collective-permute-start.12 = (bf16[256,512]{1,0:T(8,128)(2,1)S(1)}, bf16[256,512]{1,0:T(8,128)(2,1)S(1)}, u32[]{:S(2)}, u32[]{:S(2)}) collective-permute-start(bf16[256,512]{1,0:T(8,128)(2,1)S(1)} %get-tuple-element.110), channel_id=1, source_target_pairs={{0,4},{4,0},{8,12},{12,8},{1,5},{5,1},{9,13},{13,9},{2,6},{6,2},{1... | collective-permute-start | bytes 786440 | tf_op jit(solution)/shard_map/ppermute | solution.py:105
  73.9 8.4 %collective-permute-start.14 = (bf16[128,512]{1,0:T(8,128)(2,1)S(1)}, bf16[128,512]{1,0:T(8,128)(2,1)S(1)}, u32[]{:S(2)}, u32[]{:S(2)}) collective-permute-start(bf16[128,512]{1,0:T(8,128)(2,1)S(1)} %fusion.13), channel_id=1, source_target_pairs={{0,8},{4,12},{8,0},{12,4},{1,9},{5,13},{9,1},{13,5},{2,10},{6,14},... | collective-permute-start | bytes 393224 | tf_op jit(solution)/shard_map/ppermute | solution.py:105

commit v21 on v19

--- a/solution.py
+++ b/solution.py
@@ -161,20 +161,16 @@
 
 
 def cut_kernel(bits, place_ref, tokens_ref, *refs):
-    pieces, (held, sems) = refs[:-2], refs[-2:]
+    pieces, sems = refs[:-1], refs[-1]
     depth = pieces[0].shape[1]
-    inward, outward = [], []
+    copies = []
     for index, piece in enumerate(pieces):
         start = pl.multiple_of((place_ref[0] ^ bits[index]) * depth, depth)
         source = tokens_ref.at[:, pl.ds(start, depth)]
-        inward.append(pltpu.make_async_copy(source, held.at[index], sems.at[0, index]))
-        outward.append(pltpu.make_async_copy(held.at[index], piece, sems.at[1, index]))
-    for copy in inward:
+        copies.append(pltpu.make_async_copy(source, piece, sems.at[index]))
+    for copy in copies:
         copy.start()
-    for copy, onward in zip(inward, outward):
-        copy.wait()
-        onward.start()
-    for copy in outward:
+    for copy in copies:
         copy.wait()
 
 
@@ -187,14 +183,11 @@
             num_scalar_prefetch=1,
             grid=(1,),
             in_specs=[far],
-            out_specs=[far] * len(bits),
-            scratch_shapes=[
-                pltpu.VMEM((len(bits), *piece.shape), tokens.dtype),
-                pltpu.SemaphoreType.DMA((2, len(bits))),
-            ],
+            out_specs=[pl.BlockSpec(piece.shape, lambda i, place: (0, 0))] * len(bits),
+            scratch_shapes=[pltpu.SemaphoreType.DMA((len(bits),))],
         ),
         out_shape=[piece] * len(bits),
-        compiler_params=params(MOST_VMEM_BYTES),
+        compiler_params=params(),
         cost_estimate=cost("cut_tokens"),
         name="cut_tokens",
     )(place, tokens)
@@ -419,7 +412,7 @@
     all_rows, width = query_rows.shape
     row_total = all_rows // CHUNKS
     at, count = part
-    rows = min(1024, row_total // count)
+    rows = min(2048, row_total // count)
     steps = row_total // rows // count
     first = chunk * count * steps + at * steps
     out_specs = [
@@ -512,7 +505,7 @@
 ):
     row_total, width = query_rows.shape
     chunk_rows = row_total // CHUNKS
-    rows = min(1024, chunk_rows)
+    rows = min(2048, chunk_rows)
     steps = chunk_rows // rows
     block = pl.BlockSpec((rows, width), lambda i, length: (chunk * steps + i, 0))
     fresh_shape = pieces[0][1].block_shape[-2:]

time: 87.7 us -> 84.9 us (0.968)
  Pallas kernels: 43 us -> 38.7 us
  local copies, waits for them, and re-layouts: 0.04 us -> 1.62 us
  waiting for transfers between devices: 24.7 us -> 26 us
    pallas_call x1, Pallas kernels: 3.03 us -> 0.7 us  [cut_tokens(): pl.pallas_call(functools.partial(cut_kernel, bits), grid_spec=pltpu.Prefe...]
    unnamed x16 -> x14, local copies, waits for them, and re-layouts: 0.04 us -> 1.62 us
    ppermute x7, waiting for transfers between devices: 22.8 us -> 24.1 us  [trade(): lax.ppermute(array, axis, [(i, i ^ bits) for i in range(lax.axis_size(axi...]
    pallas_call x2, Pallas kernels: 10 us -> 8.87 us  [fresh_attend(): pl.pallas_call(functools.partial(fresh_kernel, scale, heads, per_token, c...]
  transfers between devices with their start and end apart: 15 -> 15, of which waited for: 6 -> 7; matrix products, arithmetic and copies ran while one was open for 0% -> 1% of each run, Pallas kernels for 37% -> 37%
where the time goes in v21:
time: 84.9 us; the launch traced here: 84.8 us
  Pallas kernels  38.7 us (46%)
  waiting for transfers between devices  26 us (31%)
  starting transfers between devices  17.1 us (20%)
  local copies, waits for them, and re-layouts  1.62 us (2%)
  between operations  0.86 us (1%)
    ppermute x7, waiting for transfers between devices, trade(): lax.ppermute(array, axis, [(i, i ^ bits) for i in range(lax.axis_size(axi...  24.1 us
    pallas_call x4, Pallas kernels, prefix_attend(): pl.pallas_call(functools.partial(prefix_kernel, scale, heads, [len(terms)...  14.6 us
    ppermute x7, starting transfers between devices, trade(): lax.ppermute(array, axis, [(i, i ^ bits) for i in range(lax.axis_size(axi...  9.68 us
    pallas_call x2, Pallas kernels, fresh_attend(): pl.pallas_call(functools.partial(fresh_kernel, scale, heads, per_token, c...  8.87 us
    pallas_call x4, Pallas kernels, project(): pl.pallas_call(functools.partial(project_kernel, len(blocks), [len(terms)...  8.45 us
    ppermute x8, starting transfers between devices, shift(): lax.ppermute(array, axis, [(i, (i + step) % count) for i in range(count)])  7.44 us
    pallas_call x1, Pallas kernels, arrange_weights(): pl.pallas_call(functools.partial(weight_kernel, ctx_count, heads, head_co...  2.47 us
    pallas_call x1, Pallas kernels, arrange_pool(): pl.pallas_call(functools.partial(pool_kernel, ctx_count, heads), grid_spe...  1.91 us
  transfers between devices with their start and end apart: 15, of which 7 were waited for; matrix products, arithmetic and copies ran while one was open for 1% of the time, Pallas kernels for 37%

profile of v21, /device:TPU:0, one launch (start us, length us, event | category | flops | bytes accessed | tf_op | source)
XLA Modules:
  0.0 84.8 jit_solution(9948272457898349442)
XLA Ops:
  0.0 0.1 pad_add_fusion.place_ref
  0.1 1.6 %copy-done.3 = bf16[256,4096]{1,0:T(8,128)(2,1)S(1)} copy-done((bf16[256,4096]{1,0:T(8,128)(2,1)S(1)}, bf16[256,4096]{1,0:T(8,128)(2,1)}, u32[]{:S(2)}) %copy-start.3) | copy-done | bytes 2097176
  1.7 0.7 cut_tokens.1
  2.4 5.1 %collective-permute-start = (bf16[256,1024]{1,0:T(8,128)(2,1)S(1)}, bf16[256,1024]{1,0:T(8,128)(2,1)S(1)}, u32[]{:S(2)}, u32[]{:S(2)}) collective-permute-start(bf16[256,1024]{1,0:T(8,128)(2,1)S(1)} %get-tuple-element.64), channel_id=1, source_target_pairs={{0,12},{4,8},{8,4},{12,0},{1,13},{5,9},{9,5},{13,1},{2,14},{6,10},... | collective-permute-start | bytes 1572872 | tf_op jit(solution)/shard_map/ppermute | solution.py:105
  7.5 0.0 collective-permute-start.1
  7.5 1.9 %arrange_pool.1 = (bf16[8,128,512]{2,1,0:T(8,128)(2,1)S(1)}, bf16[8,128,512]{2,1,0:T(8,128)(2,1)S(1)}) custom-call(s32[3]{0:T(128)S(1)} %pad_add_fusion.place_ref, bf16[8,128,8,128]{3,2,1,0:T(8,128)(2,1)S(1)} %bitcast.45), custom_call_target="tpu_custom_call" | custom-call | flops 20000000000 | bytes 1 | tf_op jit(solution)/shard_map/arrange_pool/pallas_call | solution.py:227
  9.4 1.6 %collective-permute-start.3 = (bf16[8,128,512]{2,1,0:T(8,128)(2,1)S(1)}, bf16[8,128,512]{2,1,0:T(8,128)(2,1)S(1)}, u32[]{:S(2)}, u32[]{:S(2)}) collective-permute-start(bf16[8,128,512]{2,1,0:T(8,128)(2,1)S(1)} %get-tuple-element.74), channel_id=1, source_target_pairs={{0,2},{2,0},{1,3},{3,1},{4,6},{6,4},{5,7},{7,5},{8,10},{10,8},{9,1... | collective-permute-start | bytes 3145736 | tf_op jit(solution)/shard_map/ppermute | solution.py:101
  11.0 2.5 %arrange_weights.1.refs_2_ = bf16[2,2,1024,512]{3,2,1,0:T(8,128)(2,1)S(1)} custom-call(bf16[1024,8,128]{2,1,0:T(8,128)(2,1)S(1)} %bitcast.46, bf16[1024,8,128]{2,1,0:T(8,128)(2,1)S(1)} %bitcast.47), custom_call_target="tpu_custom_call" | custom-call | flops 20000000000 | bytes 1 | tf_op jit(solution)/shard_map/arrange_weights/pallas_call | solution.py:150
  13.5 0.8 collective-permute-start.5
  15.0 5.4 %collective-permute-done.refs_0_ = bf16[256,1024]{1,0:T(8,128)(2,1)S(1)} collective-permute-done((bf16[256,1024]{1,0:T(8,128)(2,1)S(1)}, bf16[256,1024]{1,0:T(8,128)(2,1)S(1)}, u32[]{:S(2)}, u32[]{:S(2)}) %collective-permute-start) | collective-permute-done | bytes 524320 | tf_op jit(solution)/shard_map/ppermute | solution.py:105
  20.3 11.5 %collective-permute-done.1.refs_1_ = bf16[256,1024]{1,0:T(8,128)(2,1)S(1)} collective-permute-done((bf16[256,1024]{1,0:T(8,128)(2,1)S(1)}, bf16[256,1024]{1,0:T(8,128)(2,1)S(1)}, u32[]{:S(2)}, u32[]{:S(2)}) %collective-permute-start.1) | collective-permute-done | bytes 524320 | tf_op jit(solution)/shard_map/ppermute | solution.py:105
  31.8 2.1 %early_away.1 = bf16[2,512,512]{2,1,0:T(8,128)(2,1)S(1)} custom-call(s32[3]{0:T(128)S(1)} %pad_add_fusion.place_ref, bf16[256,1024]{1,0:T(8,128)(2,1)S(1)} %collective-permute-done.refs_0_, bf16[256,1024]{1,0:T(8,128)(2,1)S(1)} %collective-permute-done.1.refs_1_, bf16[2,2,1024,512]{3,2,1,0:T(8,128)(2,1)S(1)} %arrange_weights.1.refs_2_), custom_call_target="tpu_custom_call" | custom-call | flops 20000000000 | bytes 1 | tf_op jit(solution)/shard_map/early_away/pallas_call | solution.py:291
  33.9 0.1 collective-permute-start.2
  33.9 2.1 %early_kept.1.refs_0_.refs_3_ = f32[2,512,512]{2,1,0:T(8,128)S(1)} custom-call(s32[3]{0:T(128)S(1)} %pad_add_fusion.place_ref, bf16[256,1024]{1,0:T(8,128)(2,1)S(1)} %collective-permute-done.refs_0_, bf16[256,1024]{1,0:T(8,128)(2,1)S(1)} %collective-permute-done.1.refs_1_, bf16[2,2,1024,512]{3,2,1,0:T(8,128)(2,1)S(1)} %arrange_weights.1.refs_2_), custom_call_target="tpu_custom_call" | custom-call | flops 20000000000 | bytes 1 | tf_op jit(solution)/shard_map/early_kept/pallas_call | solution.py:291
  36.0 0.0 copy-start.6
  36.0 0.6 collective-permute-done.2.refs_1_.refs_4_
  36.6 0.2 fusion.4
  36.8 0.0 collective-permute-done.3.refs_1_
  36.8 1.4 %collective-permute-start.4 = (bf16[256,512]{1,0:T(8,128)(2,1)S(1)}, bf16[256,512]{1,0:T(8,128)(2,1)S(1)}, u32[]{:S(2)}, u32[]{:S(2)}) collective-permute-start(bf16[256,512]{1,0:T(8,128)(2,1)S(1)} %get-tuple-element.81), channel_id=1, source_target_pairs={{0,2},{2,0},{1,3},{3,1},{4,6},{6,4},{5,7},{7,5},{8,10},{10,8},{9,1... | collective-permute-start | bytes 786440 | tf_op jit(solution)/shard_map/ppermute | solution.py:101
  38.2 0.6 collective-permute-start.6
  38.9 1.7 %pick_blocks.1 = (bf16[1024,256]{1,0:T(8,128)(2,1)S(1)}, bf16[288,1024]{1,0:T(8,128)(2,1)S(1)}) custom-call(s32[3]{0:T(128)S(1)} %pad_add_fusion.place_ref, s32[8]{0:T(128)S(1)} %bitcast.54, bf16[8,128,512]{2,1,0:T(8,128)(2,1)S(1)} %get-tuple-element.75.refs_0_, bf16[8,128,512]{2,1,0:T(8,128)(2,1)S(1)} %collective-permute-done.3.refs_1_), custom_call_target="tpu_custom_call" | custom-call | flops 20000000000 | bytes 1 | tf_op jit(solution)/shard_map/pick_blocks/pallas_call | solution.py:355
  40.6 7.2 %prefix_attend.4 = (f32[128,4096]{1,0:T(8,128)S(1)}, f32[8,4096]{1,0:T(8,128)S(1)}) custom-call(bf16[8192,128]{1,0:T(8,128)(2,1)S(1)} %bitcast.48, bf16[1024,256]{1,0:T(8,128)(2,1)S(1)} %get-tuple-element.88.keys, bf16[288,1024]{1,0:T(8,128)(2,1)S(1)} %get-tuple-element.89.values), custom_call_target="tpu_custom_call" | custom-call | flops 20000000000 | bytes 1 | tf_op jit(solution)/shard_map/prefix_attend/pallas_call | solution.py:438
  47.8 0.0 copy-start.4
  47.8 3.7 %prefix_attend.5 = (f32[128,4096]{1,0:T(8,128)S(1)}, f32[8,4096]{1,0:T(8,128)S(1)}, bf16[256,512]{1,0:T(8,128)(2,1)S(1)}) custom-call(bf16[8192,128]{1,0:T(8,128)(2,1)S(1)} %bitcast.49, bf16[1024,256]{1,0:T(8,128)(2,1)S(1)} %get-tuple-element.88.keys, bf16[288,1024]{1,0:T(8,128)(2,1)S(1)} %get-tuple-element.89.values, ...), custom_call_target="tpu_custom_call" | custom-call | flops 20000000000 | bytes 1 | tf_op jit(solution)/shard_map/prefix_attend/pallas_call | solution.py:438
  51.5 0.8 collective-permute-done.5.refs_0_
  52.3 2.2 %late_away.1 = (bf16[2,512,512]{2,1,0:T(8,128)(2,1)S(1)}, bf16[256,512]{1,0:T(8,128)(2,1)S(1)}) custom-call(s32[3]{0:T(128)S(1)} %pad_add_fusion.place_ref, bf16[256,1024]{1,0:T(8,128)(2,1)S(1)} %collective-permute-done.5.refs_0_, bf16[256,4096]{1,0:T(8,128)(2,1)S(1)} %copy-done.4, bf16[2,2,1024,512]{3,2,1,0:T(8,128)(2,1)S(1)} %arrange_weights.1.refs_2_, ...), custom_call_target="tpu_custom_call" | custom-call | flops 20000000000 | bytes 1 | tf_op jit(solution)/shard_map/late_away/pallas_call | solution.py:291
  54.5 0.1 collective-permute-start.7
  54.6 1.1 %collective-permute-start.9 = (bf16[256,512]{1,0:T(8,128)(2,1)S(1)}, bf16[256,512]{1,0:T(8,128)(2,1)S(1)}, u32[]{:S(2)}, u32[]{:S(2)}) collective-permute-start(bf16[256,512]{1,0:T(8,128)(2,1)S(1)} %get-tuple-element.90), channel_id=1, source_target_pairs={{0,4},{4,0},{8,12},{12,8},{1,5},{5,1},{9,13},{13,9},{2,6},{6,2},{1... | collective-permute-start | bytes 786440 | tf_op jit(solution)/shard_map/ppermute | solution.py:105
  55.7 1.0 %collective-permute-start.12 = (bf16[256,512]{1,0:T(8,128)(2,1)S(1)}, bf16[256,512]{1,0:T(8,128)(2,1)S(1)}, u32[]{:S(2)}, u32[]{:S(2)}) collective-permute-start(bf16[256,512]{1,0:T(8,128)(2,1)S(1)} %get-tuple-element.108), channel_id=1, source_target_pairs={{0,4},{4,0},{8,12},{12,8},{1,5},{5,1},{9,13},{13,9},{2,6},{6,2},{1... | collective-permute-start | bytes 786440 | tf_op jit(solution)/shard_map/ppermute | solution.py:105
  56.7 2.1 %late_kept.1.rest_0_.rest_1_ = f32[2,512,512]{2,1,0:T(8,128)S(1)} custom-call(s32[3]{0:T(128)S(1)} %pad_add_fusion.place_ref, bf16[256,1024]{1,0:T(8,128)(2,1)S(1)} %collective-permute-done.5.refs_0_, bf16[256,4096]{1,0:T(8,128)(2,1)S(1)} %copy-done.4, bf16[2,2,1024,512]{3,2,1,0:T(8,128)(2,1)S(1)} %arrange_weights.1.refs_2_), custom_call_target="tpu_custom_call" | custom-call | flops 20000000000 | bytes 1 | tf_op jit(solution)/shard_map/late_kept/pallas_call | solution.py:291
  58.8 0.0 collective-permute-done.7.rest_1_.rest_2_
  58.8 0.1 fusion.15
  58.9 1.6 %collective-permute-start.8 = (bf16[128,512]{1,0:T(8,128)(2,1)S(1)}, bf16[128,512]{1,0:T(8,128)(2,1)S(1)}, u32[]{:S(2)}, u32[]{:S(2)}) collective-permute-start(bf16[128,512]{1,0:T(8,128)(2,1)S(1)} %get-tuple-element.117), channel_id=1, source_target_pairs={{0,2},{2,0},{1,3},{3,1},{4,6},{6,4},{5,7},{7,5},{8,10},{10,8},{9,1... | collective-permute-start | bytes 393224 | tf_op jit(solution)/shard_map/ppermute | solution.py:101
  60.4 1.9 %prefix_attend.6 = (f32[128,4096]{1,0:T(8,128)S(1)}, f32[8,4096]{1,0:T(8,128)S(1)}) custom-call(bf16[8192,128]{1,0:T(8,128)(2,1)S(1)} %bitcast.50, bf16[1024,256]{1,0:T(8,128)(2,1)S(1)} %get-tuple-element.88.keys, bf16[288,1024]{1,0:T(8,128)(2,1)S(1)} %get-tuple-element.89.values, ...), custom_call_target="tpu_custom_call", output_to_operand_aliasing={{0}: (3, {}), {1}: (4, {})} | custom-call | flops 20000000000 | bytes 1 | tf_op jit(solution)/shard_map/prefix_attend/pallas_call | solution.py:438
  62.3 0.1 fusion.5
  62.4 0.6 collective-permute-start.10
  63.0 1.5 %collective-permute-start.11 = (bf16[256,512]{1,0:T(8,128)(2,1)S(1)}, bf16[256,512]{1,0:T(8,128)(2,1)S(1)}, u32[]{:S(2)}, u32[]{:S(2)}) collective-permute-start(bf16[256,512]{1,0:T(8,128)(2,1)S(1)} %fusion.5), channel_id=1, source_target_pairs={{0,2},{2,0},{1,3},{3,1},{4,6},{6,4},{5,7},{7,5},{8,10},{10,8},{9,1... | collective-permute-start | bytes 786440 | tf_op jit(solution)/shard_map/ppermute | solution.py:101
  64.5 0.0 collective-permute-done.9
  64.5 0.1 fusion.10
  64.5 1.2 %collective-permute-start.13 = (bf16[128,512]{1,0:T(8,128)(2,1)S(1)}, bf16[128,512]{1,0:T(8,128)(2,1)S(1)}, u32[]{:S(2)}, u32[]{:S(2)}) collective-permute-start(bf16[128,512]{1,0:T(8,128)(2,1)S(1)} %fusion.10), channel_id=1, source_target_pairs={{0,8},{4,12},{8,0},{12,4},{1,9},{5,13},{9,1},{13,5},{2,10},{6,14},... | collective-permute-start | bytes 393224 | tf_op jit(solution)/shard_map/ppermute | solution.py:105
  65.7 1.8 %prefix_attend.7 = (f32[128,4096]{1,0:T(8,128)S(1)}, f32[8,4096]{1,0:T(8,128)S(1)}) custom-call(bf16[8192,128]{1,0:T(8,128)(2,1)S(1)} %bitcast.51, bf16[1024,256]{1,0:T(8,128)(2,1)S(1)} %get-tuple-element.88.keys, bf16[288,1024]{1,0:T(8,128)(2,1)S(1)} %get-tuple-element.89.values, ...), custom_call_target="tpu_custom_call", output_to_operand_aliasing={{0}: (3, {}), {1}: (4, {})} | custom-call | flops 20000000000 | bytes 1 | tf_op jit(solution)/shard_map/prefix_attend/pallas_call | solution.py:438
  67.6 1.3 %collective-permute-done.10 = bf16[128,512]{1,0:T(8,128)(2,1)S(1)} collective-permute-done((bf16[128,512]{1,0:T(8,128)(2,1)S(1)}, bf16[128,512]{1,0:T(8,128)(2,1)S(1)}, u32[]{:S(2)}, u32[]{:S(2)}) %collective-permute-start.10) | collective-permute-done | bytes 131104 | tf_op jit(solution)/shard_map/ppermute | solution.py:101
  68.9 0.1 fusion.13
  68.9 4.4 %collective-permute-done.13.rest_4_ = bf16[128,512]{1,0:T(8,128)(2,1)S(1)} collective-permute-done((bf16[128,512]{1,0:T(8,128)(2,1)S(1)}, bf16[128,512]{1,0:T(8,128)(2,1)S(1)}, u32[]{:S(2)}, u32[]{:S(2)}) %collective-permute-start.13) | collective-permute-done | bytes 131104 | tf_op jit(solution)/shard_map/ppermute | solution.py:105
  73.3 0.5 collective-permute-start.14
  73.8 4.1 %fresh_attend.2 = (bf16[8192,128]{1,0:T(8,128)(2,1)}, bf16[128,512]{1,0:T(8,128)(2,1)S(1)}) custom-call(s32[1]{0:T(128)S(6)} %copy.21.length_ref, bf16[8192,128]{1,0:T(8,128)(2,1)S(1)} %bitcast.52, f32[128,4096]{1,0:T(8,128)S(1)} %get-tuple-element.102.acc_ref, f32[8,4096]{1,0:T(8,128)S(1)} %get-tuple-element.103.stat_ref, ...), custom_call_target="tpu_custom_call" | custom-call | flops 20000000000 | bytes 1 | tf_op jit(solution)/shard_map/fresh_attend/pallas_call | solution.py:527
  77.9 2.1 %collective-permute-done.14.rest_5_ = bf16[128,512]{1,0:T(8,128)(2,1)S(1)} collective-permute-done((bf16[128,512]{1,0:T(8,128)(2,1)S(1)}, bf16[128,512]{1,0:T(8,128)(2,1)S(1)}, u32[]{:S(2)}, u32[]{:S(2)}) %collective-permute-start.14) | collective-permute-done | bytes 131104 | tf_op jit(solution)/shard_map/ppermute | solution.py:105
  80.0 4.7 %fresh_attend.3 = (bf16[8192,128]{1,0:T(8,128)(2,1)}, bf16[128,512]{1,0:T(8,128)(2,1)}) custom-call(s32[1]{0:T(128)S(6)} %copy.21.length_ref, bf16[8192,128]{1,0:T(8,128)(2,1)S(1)} %bitcast.53, f32[128,4096]{1,0:T(8,128)S(1)} %get-tuple-element.100.acc_ref, f32[8,4096]{1,0:T(8,128)S(1)} %get-tuple-element.101.stat_ref, ...), custom_call_target="tpu_custom_call", output_to_operand_aliasing={{0}: (10, {})} | custom-call | flops 20000000000 | bytes 1 | tf_op jit(solution)/shard_map/fresh_attend/pallas_call | solution.py:527
  (16 shorter events, 0.0 us)
Async XLA Ops:
  0.1 1.6 %copy-start.3 = (bf16[256,4096]{1,0:T(8,128)(2,1)S(1)}, bf16[256,4096]{1,0:T(8,128)(2,1)}, u32[]{:S(2)}) copy-start(bf16[256,4096]{1,0:T(8,128)(2,1)} %refs_1_.3) | copy-start | bytes 6291460
  1.7 5.8 %copy-start = (bf16[8,128,4,1,256]{4,2,3,1,0:T(4,128)(2,1)S(1)}, bf16[8,128,4,1,256]{4,2,3,1,0:T(4,128)(2,1)}, u32[]{:S(2)}) copy-start(bf16[8,128,4,1,256]{4,2,3,1,0:T(4,128)(2,1)} %param.11) | copy-start | bytes 6291460
  2.4 18.0 %collective-permute-start = (bf16[256,1024]{1,0:T(8,128)(2,1)S(1)}, bf16[256,1024]{1,0:T(8,128)(2,1)S(1)}, u32[]{:S(2)}, u32[]{:S(2)}) collective-permute-start(bf16[256,1024]{1,0:T(8,128)(2,1)S(1)} %get-tuple-element.64), channel_id=1, source_target_pairs={{0,12},{4,8},{8,4},{12,0},{1,13},{5,9},{9,5},{13,1},{2,14},{6,10},... | collective-permute-start | bytes 1572872 | tf_op jit(solution)/shard_map/ppermute | solution.py:105
  7.5 24.3 %collective-permute-start.1 = (bf16[256,1024]{1,0:T(8,128)(2,1)S(1)}, bf16[256,1024]{1,0:T(8,128)(2,1)S(1)}, u32[]{:S(2)}, u32[]{:S(2)}) collective-permute-start(bf16[256,1024]{1,0:T(8,128)(2,1)S(1)} %get-tuple-element.65), channel_id=1, source_target_pairs={{0,4},{4,0},{8,12},{12,8},{1,5},{5,1},{9,13},{13,9},{2,6},{6,2},{1... | collective-permute-start | bytes 1572872 | tf_op jit(solution)/shard_map/ppermute | solution.py:105
  7.5 3.5 %copy-start.1 = (bf16[1,1,1024,4,2,128]{5,4,3,2,1,0:T(2,128)(2,1)S(1)}, bf16[1,1,1024,4,2,128]{5,4,3,2,1,0:T(2,128)(2,1)}, u32[]{:S(2)}) copy-start(bf16[1,1,1024,4,2,128]{5,4,3,2,1,0:T(2,128)(2,1)} %param.8) | copy-start | bytes 6291460
  7.5 3.5 %copy-start.2 = (bf16[1,1,1024,4,2,128]{5,4,3,2,1,0:T(2,128)(2,1)S(1)}, bf16[1,1,1024,4,2,128]{5,4,3,2,1,0:T(2,128)(2,1)}, u32[]{:S(2)}) copy-start(bf16[1,1,1024,4,2,128]{5,4,3,2,1,0:T(2,128)(2,1)} %param.9) | copy-start | bytes 6291460
  9.4 27.3 %collective-permute-start.3 = (bf16[8,128,512]{2,1,0:T(8,128)(2,1)S(1)}, bf16[8,128,512]{2,1,0:T(8,128)(2,1)S(1)}, u32[]{:S(2)}, u32[]{:S(2)}) collective-permute-start(bf16[8,128,512]{2,1,0:T(8,128)(2,1)S(1)} %get-tuple-element.74), channel_id=1, source_target_pairs={{0,2},{2,0},{1,3},{3,1},{4,6},{6,4},{5,7},{7,5},{8,10},{10,8},{9,1... | collective-permute-start | bytes 3145736 | tf_op jit(solution)/shard_map/ppermute | solution.py:101
  13.5 38.8 %collective-permute-start.5 = (bf16[256,1024]{1,0:T(8,128)(2,1)S(1)}, bf16[256,1024]{1,0:T(8,128)(2,1)S(1)}, u32[]{:S(2)}, u32[]{:S(2)}) collective-permute-start(bf16[256,1024]{1,0:T(8,128)(2,1)S(1)} %get-tuple-element.84), channel_id=1, source_target_pairs={{0,8},{4,12},{8,0},{12,4},{1,9},{5,13},{9,1},{13,5},{2,10},{6,14},... | collective-permute-start | bytes 1572872 | tf_op jit(solution)/shard_map/ppermute | solution.py:105
  33.9 2.7 %collective-permute-start.2 = (bf16[2,512,512]{2,1,0:T(8,128)(2,1)S(1)}, bf16[2,512,512]{2,1,0:T(8,128)(2,1)S(1)}, u32[]{:S(2)}, u32[]{:S(2)}) collective-permute-start(bf16[2,512,512]{2,1,0:T(8,128)(2,1)S(1)} %early_away.1), channel_id=1, source_target_pairs={{0,1},{1,0},{2,3},{3,2},{4,5},{5,4},{6,7},{7,6},{8,9},{9,8},{10,11... | collective-permute-start | bytes 3145736 | tf_op jit(solution)/shard_map/ppermute | solution.py:101
  36.0 2.9 %copy-start.6 = (s32[1,8]{1,0:T(1,128)S(1)}, s32[1,8]{1,0:T(1,128)}, u32[]{:S(2)}) copy-start(s32[1,8]{1,0:T(1,128)} %param.12) | copy-start | bytes 100
  36.8 11.1 %collective-permute-start.4 = (bf16[256,512]{1,0:T(8,128)(2,1)S(1)}, bf16[256,512]{1,0:T(8,128)(2,1)S(1)}, u32[]{:S(2)}, u32[]{:S(2)}) collective-permute-start(bf16[256,512]{1,0:T(8,128)(2,1)S(1)} %get-tuple-element.81), channel_id=1, source_target_pairs={{0,2},{2,0},{1,3},{3,1},{4,6},{6,4},{5,7},{7,5},{8,10},{10,8},{9,1... | collective-permute-start | bytes 786440 | tf_op jit(solution)/shard_map/ppermute | solution.py:101
  38.2 14.1 %collective-permute-start.6 = (bf16[256,512]{1,0:T(8,128)(2,1)S(1)}, bf16[256,512]{1,0:T(8,128)(2,1)S(1)}, u32[]{:S(2)}, u32[]{:S(2)}) collective-permute-start(bf16[256,512]{1,0:T(8,128)(2,1)S(1)} %get-tuple-element.86), channel_id=1, source_target_pairs={{0,2},{2,0},{1,3},{3,1},{4,6},{6,4},{5,7},{7,5},{8,10},{10,8},{9,1... | collective-permute-start | bytes 786440 | tf_op jit(solution)/shard_map/ppermute | solution.py:101
  38.9 1.7 %copy-start.5 = (bf16[256,2,1,2048]{3,1,2,0:T(2,128)(2,1)S(1)}, bf16[256,2,1,2048]{3,1,2,0:T(2,128)(2,1)}, u32[]{:S(2)}) copy-start(bf16[256,2,1,2048]{3,1,2,0:T(2,128)(2,1)} %param.10) | copy-start | bytes 6291460
  47.8 4.5 %copy-start.4 = (bf16[256,4096]{1,0:T(8,128)(2,1)S(1)}, bf16[256,4096]{1,0:T(8,128)(2,1)}, u32[]{:S(2)}) copy-start(bf16[256,4096]{1,0:T(8,128)(2,1)} %refs_1_.3) | copy-start | bytes 6291460
  54.5 4.3 %collective-permute-start.7 = (bf16[2,512,512]{2,1,0:T(8,128)(2,1)S(1)}, bf16[2,512,512]{2,1,0:T(8,128)(2,1)S(1)}, u32[]{:S(2)}, u32[]{:S(2)}) collective-permute-start(bf16[2,512,512]{2,1,0:T(8,128)(2,1)S(1)} %get-tuple-element.87), channel_id=1, source_target_pairs={{0,1},{1,0},{2,3},{3,2},{4,5},{5,4},{6,7},{7,6},{8,9},{9,8},{10,11... | collective-permute-start | bytes 3145736 | tf_op jit(solution)/shard_map/ppermute | solution.py:101
  54.6 9.9 %collective-permute-start.9 = (bf16[256,512]{1,0:T(8,128)(2,1)S(1)}, bf16[256,512]{1,0:T(8,128)(2,1)S(1)}, u32[]{:S(2)}, u32[]{:S(2)}) collective-permute-start(bf16[256,512]{1,0:T(8,128)(2,1)S(1)} %get-tuple-element.90), channel_id=1, source_target_pairs={{0,4},{4,0},{8,12},{12,8},{1,5},{5,1},{9,13},{13,9},{2,6},{6,2},{1... | collective-permute-start | bytes 786440 | tf_op jit(solution)/shard_map/ppermute | solution.py:105
  55.7 18.1 %collective-permute-start.12 = (bf16[256,512]{1,0:T(8,128)(2,1)S(1)}, bf16[256,512]{1,0:T(8,128)(2,1)S(1)}, u32[]{:S(2)}, u32[]{:S(2)}) collective-permute-start(bf16[256,512]{1,0:T(8,128)(2,1)S(1)} %get-tuple-element.108), channel_id=1, source_target_pairs={{0,4},{4,0},{8,12},{12,8},{1,5},{5,1},{9,13},{13,9},{2,6},{6,2},{1... | collective-permute-start | bytes 786440 | tf_op jit(solution)/shard_map/ppermute | solution.py:105
  58.9 5.6 %collective-permute-start.8 = (bf16[128,512]{1,0:T(8,128)(2,1)S(1)}, bf16[128,512]{1,0:T(8,128)(2,1)S(1)}, u32[]{:S(2)}, u32[]{:S(2)}) collective-permute-start(bf16[128,512]{1,0:T(8,128)(2,1)S(1)} %get-tuple-element.117), channel_id=1, source_target_pairs={{0,2},{2,0},{1,3},{3,1},{4,6},{6,4},{5,7},{7,5},{8,10},{10,8},{9,1... | collective-permute-start | bytes 393224 | tf_op jit(solution)/shard_map/ppermute | solution.py:101
  62.4 6.5 %collective-permute-start.10 = (bf16[128,512]{1,0:T(8,128)(2,1)S(1)}, bf16[128,512]{1,0:T(8,128)(2,1)S(1)}, u32[]{:S(2)}, u32[]{:S(2)}) collective-permute-start(bf16[128,512]{1,0:T(8,128)(2,1)S(1)} %get-tuple-element.104), channel_id=1, source_target_pairs={{0,2},{2,0},{1,3},{3,1},{4,6},{6,4},{5,7},{7,5},{8,10},{10,8},{9,1... | collective-permute-start | bytes 393224 | tf_op jit(solution)/shard_map/ppermute | solution.py:101
  63.0 10.8 %collective-permute-start.11 = (bf16[256,512]{1,0:T(8,128)(2,1)S(1)}, bf16[256,512]{1,0:T(8,128)(2,1)S(1)}, u32[]{:S(2)}, u32[]{:S(2)}) collective-permute-start(bf16[256,512]{1,0:T(8,128)(2,1)S(1)} %fusion.5), channel_id=1, source_target_pairs={{0,2},{2,0},{1,3},{3,1},{4,6},{6,4},{5,7},{7,5},{8,10},{10,8},{9,1... | collective-permute-start | bytes 786440 | tf_op jit(solution)/shard_map/ppermute | solution.py:101
  64.5 8.7 %collective-permute-start.13 = (bf16[128,512]{1,0:T(8,128)(2,1)S(1)}, bf16[128,512]{1,0:T(8,128)(2,1)S(1)}, u32[]{:S(2)}, u32[]{:S(2)}) collective-permute-start(bf16[128,512]{1,0:T(8,128)(2,1)S(1)} %fusion.10), channel_id=1, source_target_pairs={{0,8},{4,12},{8,0},{12,4},{1,9},{5,13},{9,1},{13,5},{2,10},{6,14},... | collective-permute-start | bytes 393224 | tf_op jit(solution)/shard_map/ppermute | solution.py:105
  73.3 6.8 %collective-permute-start.14 = (bf16[128,512]{1,0:T(8,128)(2,1)S(1)}, bf16[128,512]{1,0:T(8,128)(2,1)S(1)}, u32[]{:S(2)}, u32[]{:S(2)}) collective-permute-start(bf16[128,512]{1,0:T(8,128)(2,1)S(1)} %fusion.13), channel_id=1, source_target_pairs={{0,8},{4,12},{8,0},{12,4},{1,9},{5,13},{9,1},{13,5},{2,10},{6,14},... | collective-permute-start | bytes 393224 | tf_op jit(solution)/shard_map/ppermute | solution.py:105

commit v22 on v21

--- a/solution.py
+++ b/solution.py
@@ -12,7 +12,7 @@
 PART = 1024
 ONES = 16
 VMEM_BYTES = 16 * 1024 * 1024
-MOST_VMEM_BYTES = 60 * 1024 * 1024
+MOST_VMEM_BYTES = 52 * 1024 * 1024
 LONG = pl.CostEstimate(flops=2 * 10**10, bytes_accessed=1, transcendentals=0)
 COSTS = {}
 
@@ -187,7 +187,7 @@
             scratch_shapes=[pltpu.SemaphoreType.DMA((len(bits),))],
         ),
         out_shape=[piece] * len(bits),
-        compiler_params=params(),
+        compiler_params=params(MOST_VMEM_BYTES),
         cost_estimate=cost("cut_tokens"),
         name="cut_tokens",
     )(place, tokens)

time: 84.9 us -> 84.7 us (level)
  local copies, waits for them, and re-layouts: 1.62 us -> 0.03 us
  Pallas kernels: 38.7 us -> 40.1 us
    unnamed x14 -> x12, local copies, waits for them, and re-layouts: 1.62 us -> 0.03 us
    pallas_call x1, Pallas kernels: 0.7 us -> 2.02 us  [cut_tokens(): pl.pallas_call(functools.partial(cut_kernel, bits), grid_spec=pltpu.Prefe...]
where the time goes in v22:
time: 84.7 us; the launch traced here: 84.5 us
  Pallas kernels  40.1 us (47%)
  waiting for transfers between devices  25.9 us (31%)
  starting transfers between devices  17.1 us (20%)
  between operations  0.86 us (1%)
    ppermute x7, waiting for transfers between devices, trade(): lax.ppermute(array, axis, [(i, i ^ bits) for i in range(lax.axis_size(axi...  24.1 us
    pallas_call x4, Pallas kernels, prefix_attend(): pl.pallas_call(functools.partial(prefix_kernel, scale, heads, [len(terms)...  14.6 us
    ppermute x7, starting transfers between devices, trade(): lax.ppermute(array, axis, [(i, i ^ bits) for i in range(lax.axis_size(axi...  9.66 us
    pallas_call x2, Pallas kernels, fresh_attend(): pl.pallas_call(functools.partial(fresh_kernel, scale, heads, per_token, c...  8.86 us
    pallas_call x4, Pallas kernels, project(): pl.pallas_call(functools.partial(project_kernel, len(blocks), [len(terms)...  8.53 us
    ppermute x8, starting transfers between devices, shift(): lax.ppermute(array, axis, [(i, (i + step) % count) for i in range(count)])  7.44 us
    pallas_call x1, Pallas kernels, arrange_weights(): pl.pallas_call(functools.partial(weight_kernel, ctx_count, heads, head_co...  2.47 us
    pallas_call x1, Pallas kernels, cut_tokens(): pl.pallas_call(functools.partial(cut_kernel, bits), grid_spec=pltpu.Prefe...  2.02 us
  transfers between devices with their start and end apart: 15, of which 7 were waited for; matrix products, arithmetic and copies ran while one was open for 1% of the time, Pallas kernels for 37%

profile of v22, /device:TPU:0, one launch (start us, length us, event | category | flops | bytes accessed | tf_op | source)
XLA Modules:
  0.0 84.5 jit_solution(16464312625200729213)
XLA Ops:
  0.0 0.1 pad_add_fusion.place_ref
  0.1 2.0 %cut_tokens.1 = (bf16[256,1024]{1,0:T(8,128)(2,1)S(1)}, bf16[256,1024]{1,0:T(8,128)(2,1)S(1)}, bf16[256,1024]{1,0:T(8,128)(2,1)S(1)}) custom-call(s32[3]{0:T(128)S(1)} %pad_add_fusion.place_ref, bf16[256,4096]{1,0:T(8,128)(2,1)} %refs_1_.3), custom_call_target="tpu_custom_call" | custom-call | flops 20000000000 | bytes 1 | tf_op jit(solution)/shard_map/cut_tokens/pallas_call | solution.py:180
  2.1 5.1 %collective-permute-start = (bf16[256,1024]{1,0:T(8,128)(2,1)S(1)}, bf16[256,1024]{1,0:T(8,128)(2,1)S(1)}, u32[]{:S(2)}, u32[]{:S(2)}) collective-permute-start(bf16[256,1024]{1,0:T(8,128)(2,1)S(1)} %get-tuple-element.64), channel_id=1, source_target_pairs={{0,12},{4,8},{8,4},{12,0},{1,13},{5,9},{9,5},{13,1},{2,14},{6,10},... | collective-permute-start | bytes 1572872 | tf_op jit(solution)/shard_map/ppermute | solution.py:105
  7.2 0.0 collective-permute-start.1
  7.2 1.9 %arrange_pool.1 = (bf16[8,128,512]{2,1,0:T(8,128)(2,1)S(1)}, bf16[8,128,512]{2,1,0:T(8,128)(2,1)S(1)}) custom-call(s32[3]{0:T(128)S(1)} %pad_add_fusion.place_ref, bf16[8,128,8,128]{3,2,1,0:T(8,128)(2,1)S(1)} %bitcast.45), custom_call_target="tpu_custom_call" | custom-call | flops 20000000000 | bytes 1 | tf_op jit(solution)/shard_map/arrange_pool/pallas_call | solution.py:227
  9.1 1.6 %collective-permute-start.3 = (bf16[8,128,512]{2,1,0:T(8,128)(2,1)S(1)}, bf16[8,128,512]{2,1,0:T(8,128)(2,1)S(1)}, u32[]{:S(2)}, u32[]{:S(2)}) collective-permute-start(bf16[8,128,512]{2,1,0:T(8,128)(2,1)S(1)} %get-tuple-element.74), channel_id=1, source_target_pairs={{0,2},{2,0},{1,3},{3,1},{4,6},{6,4},{5,7},{7,5},{8,10},{10,8},{9,1... | collective-permute-start | bytes 3145736 | tf_op jit(solution)/shard_map/ppermute | solution.py:101
  10.7 2.5 %arrange_weights.1.refs_2_ = bf16[2,2,1024,512]{3,2,1,0:T(8,128)(2,1)S(1)} custom-call(bf16[1024,8,128]{2,1,0:T(8,128)(2,1)S(1)} %bitcast.46, bf16[1024,8,128]{2,1,0:T(8,128)(2,1)S(1)} %bitcast.47), custom_call_target="tpu_custom_call" | custom-call | flops 20000000000 | bytes 1 | tf_op jit(solution)/shard_map/arrange_weights/pallas_call | solution.py:150
  13.2 0.8 collective-permute-start.5
  14.7 5.4 %collective-permute-done.refs_0_ = bf16[256,1024]{1,0:T(8,128)(2,1)S(1)} collective-permute-done((bf16[256,1024]{1,0:T(8,128)(2,1)S(1)}, bf16[256,1024]{1,0:T(8,128)(2,1)S(1)}, u32[]{:S(2)}, u32[]{:S(2)}) %collective-permute-start) | collective-permute-done | bytes 524320 | tf_op jit(solution)/shard_map/ppermute | solution.py:105
  20.1 11.5 %collective-permute-done.1.refs_1_ = bf16[256,1024]{1,0:T(8,128)(2,1)S(1)} collective-permute-done((bf16[256,1024]{1,0:T(8,128)(2,1)S(1)}, bf16[256,1024]{1,0:T(8,128)(2,1)S(1)}, u32[]{:S(2)}, u32[]{:S(2)}) %collective-permute-start.1) | collective-permute-done | bytes 524320 | tf_op jit(solution)/shard_map/ppermute | solution.py:105
  31.5 2.1 %early_away.1 = bf16[2,512,512]{2,1,0:T(8,128)(2,1)S(1)} custom-call(s32[3]{0:T(128)S(1)} %pad_add_fusion.place_ref, bf16[256,1024]{1,0:T(8,128)(2,1)S(1)} %collective-permute-done.refs_0_, bf16[256,1024]{1,0:T(8,128)(2,1)S(1)} %collective-permute-done.1.refs_1_, bf16[2,2,1024,512]{3,2,1,0:T(8,128)(2,1)S(1)} %arrange_weights.1.refs_2_), custom_call_target="tpu_custom_call" | custom-call | flops 20000000000 | bytes 1 | tf_op jit(solution)/shard_map/early_away/pallas_call | solution.py:291
  33.6 0.1 collective-permute-start.2
  33.7 2.1 %early_kept.1.refs_0_.refs_3_ = f32[2,512,512]{2,1,0:T(8,128)S(1)} custom-call(s32[3]{0:T(128)S(1)} %pad_add_fusion.place_ref, bf16[256,1024]{1,0:T(8,128)(2,1)S(1)} %collective-permute-done.refs_0_, bf16[256,1024]{1,0:T(8,128)(2,1)S(1)} %collective-permute-done.1.refs_1_, bf16[2,2,1024,512]{3,2,1,0:T(8,128)(2,1)S(1)} %arrange_weights.1.refs_2_), custom_call_target="tpu_custom_call" | custom-call | flops 20000000000 | bytes 1 | tf_op jit(solution)/shard_map/early_kept/pallas_call | solution.py:291
  35.8 0.0 copy-start.5
  35.8 0.5 collective-permute-done.2.refs_1_.refs_4_
  36.3 0.2 fusion.4
  36.5 0.0 collective-permute-done.3.refs_1_
  36.5 1.4 %collective-permute-start.4 = (bf16[256,512]{1,0:T(8,128)(2,1)S(1)}, bf16[256,512]{1,0:T(8,128)(2,1)S(1)}, u32[]{:S(2)}, u32[]{:S(2)}) collective-permute-start(bf16[256,512]{1,0:T(8,128)(2,1)S(1)} %get-tuple-element.81), channel_id=1, source_target_pairs={{0,2},{2,0},{1,3},{3,1},{4,6},{6,4},{5,7},{7,5},{8,10},{10,8},{9,1... | collective-permute-start | bytes 786440 | tf_op jit(solution)/shard_map/ppermute | solution.py:101
  38.0 0.6 collective-permute-start.6
  38.6 1.7 %pick_blocks.1 = (bf16[1024,256]{1,0:T(8,128)(2,1)S(1)}, bf16[288,1024]{1,0:T(8,128)(2,1)S(1)}) custom-call(s32[3]{0:T(128)S(1)} %pad_add_fusion.place_ref, s32[8]{0:T(128)S(1)} %bitcast.54, bf16[8,128,512]{2,1,0:T(8,128)(2,1)S(1)} %get-tuple-element.75.refs_0_, bf16[8,128,512]{2,1,0:T(8,128)(2,1)S(1)} %collective-permute-done.3.refs_1_), custom_call_target="tpu_custom_call" | custom-call | flops 20000000000 | bytes 1 | tf_op jit(solution)/shard_map/pick_blocks/pallas_call | solution.py:355
  40.3 7.2 %prefix_attend.4 = (f32[128,4096]{1,0:T(8,128)S(1)}, f32[8,4096]{1,0:T(8,128)S(1)}) custom-call(bf16[8192,128]{1,0:T(8,128)(2,1)S(1)} %bitcast.48, bf16[1024,256]{1,0:T(8,128)(2,1)S(1)} %get-tuple-element.88.keys, bf16[288,1024]{1,0:T(8,128)(2,1)S(1)} %get-tuple-element.89.values), custom_call_target="tpu_custom_call" | custom-call | flops 20000000000 | bytes 1 | tf_op jit(solution)/shard_map/prefix_attend/pallas_call | solution.py:438
  47.6 0.0 copy-start.3
  47.6 3.7 %prefix_attend.5 = (f32[128,4096]{1,0:T(8,128)S(1)}, f32[8,4096]{1,0:T(8,128)S(1)}, bf16[256,512]{1,0:T(8,128)(2,1)S(1)}) custom-call(bf16[8192,128]{1,0:T(8,128)(2,1)S(1)} %bitcast.49, bf16[1024,256]{1,0:T(8,128)(2,1)S(1)} %get-tuple-element.88.keys, bf16[288,1024]{1,0:T(8,128)(2,1)S(1)} %get-tuple-element.89.values, ...), custom_call_target="tpu_custom_call" | custom-call | flops 20000000000 | bytes 1 | tf_op jit(solution)/shard_map/prefix_attend/pallas_call | solution.py:438
  51.3 0.7 collective-permute-done.5.refs_0_
  52.0 2.2 %late_away.1 = (bf16[2,512,512]{2,1,0:T(8,128)(2,1)S(1)}, bf16[256,512]{1,0:T(8,128)(2,1)S(1)}) custom-call(s32[3]{0:T(128)S(1)} %pad_add_fusion.place_ref, bf16[256,1024]{1,0:T(8,128)(2,1)S(1)} %collective-permute-done.5.refs_0_, bf16[256,4096]{1,0:T(8,128)(2,1)S(1)} %copy-done.3, bf16[2,2,1024,512]{3,2,1,0:T(8,128)(2,1)S(1)} %arrange_weights.1.refs_2_, ...), custom_call_target="tpu_custom_call" | custom-call | flops 20000000000 | bytes 1 | tf_op jit(solution)/shard_map/late_away/pallas_call | solution.py:291
  54.2 0.1 collective-permute-start.7
  54.3 1.1 %collective-permute-start.9 = (bf16[256,512]{1,0:T(8,128)(2,1)S(1)}, bf16[256,512]{1,0:T(8,128)(2,1)S(1)}, u32[]{:S(2)}, u32[]{:S(2)}) collective-permute-start(bf16[256,512]{1,0:T(8,128)(2,1)S(1)} %get-tuple-element.90), channel_id=1, source_target_pairs={{0,4},{4,0},{8,12},{12,8},{1,5},{5,1},{9,13},{13,9},{2,6},{6,2},{1... | collective-permute-start | bytes 786440 | tf_op jit(solution)/shard_map/ppermute | solution.py:105
  55.4 1.0 %collective-permute-start.12 = (bf16[256,512]{1,0:T(8,128)(2,1)S(1)}, bf16[256,512]{1,0:T(8,128)(2,1)S(1)}, u32[]{:S(2)}, u32[]{:S(2)}) collective-permute-start(bf16[256,512]{1,0:T(8,128)(2,1)S(1)} %get-tuple-element.108), channel_id=1, source_target_pairs={{0,4},{4,0},{8,12},{12,8},{1,5},{5,1},{9,13},{13,9},{2,6},{6,2},{1... | collective-permute-start | bytes 786440 | tf_op jit(solution)/shard_map/ppermute | solution.py:105
  56.4 2.1 %late_kept.1.rest_0_.rest_1_ = f32[2,512,512]{2,1,0:T(8,128)S(1)} custom-call(s32[3]{0:T(128)S(1)} %pad_add_fusion.place_ref, bf16[256,1024]{1,0:T(8,128)(2,1)S(1)} %collective-permute-done.5.refs_0_, bf16[256,4096]{1,0:T(8,128)(2,1)S(1)} %copy-done.3, bf16[2,2,1024,512]{3,2,1,0:T(8,128)(2,1)S(1)} %arrange_weights.1.refs_2_), custom_call_target="tpu_custom_call" | custom-call | flops 20000000000 | bytes 1 | tf_op jit(solution)/shard_map/late_kept/pallas_call | solution.py:291
  58.5 0.0 collective-permute-done.7.rest_1_.rest_2_
  58.6 0.1 fusion.15
  58.6 1.6 %collective-permute-start.8 = (bf16[128,512]{1,0:T(8,128)(2,1)S(1)}, bf16[128,512]{1,0:T(8,128)(2,1)S(1)}, u32[]{:S(2)}, u32[]{:S(2)}) collective-permute-start(bf16[128,512]{1,0:T(8,128)(2,1)S(1)} %get-tuple-element.117), channel_id=1, source_target_pairs={{0,2},{2,0},{1,3},{3,1},{4,6},{6,4},{5,7},{7,5},{8,10},{10,8},{9,1... | collective-permute-start | bytes 393224 | tf_op jit(solution)/shard_map/ppermute | solution.py:101
  60.2 1.9 %prefix_attend.6 = (f32[128,4096]{1,0:T(8,128)S(1)}, f32[8,4096]{1,0:T(8,128)S(1)}) custom-call(bf16[8192,128]{1,0:T(8,128)(2,1)S(1)} %bitcast.50, bf16[1024,256]{1,0:T(8,128)(2,1)S(1)} %get-tuple-element.88.keys, bf16[288,1024]{1,0:T(8,128)(2,1)S(1)} %get-tuple-element.89.values, ...), custom_call_target="tpu_custom_call", output_to_operand_aliasing={{0}: (3, {}), {1}: (4, {})} | custom-call | flops 20000000000 | bytes 1 | tf_op jit(solution)/shard_map/prefix_attend/pallas_call | solution.py:438
  62.1 0.1 fusion.5
  62.1 0.6 collective-permute-start.10
  62.7 1.5 %collective-permute-start.11 = (bf16[256,512]{1,0:T(8,128)(2,1)S(1)}, bf16[256,512]{1,0:T(8,128)(2,1)S(1)}, u32[]{:S(2)}, u32[]{:S(2)}) collective-permute-start(bf16[256,512]{1,0:T(8,128)(2,1)S(1)} %fusion.5), channel_id=1, source_target_pairs={{0,2},{2,0},{1,3},{3,1},{4,6},{6,4},{5,7},{7,5},{8,10},{10,8},{9,1... | collective-permute-start | bytes 786440 | tf_op jit(solution)/shard_map/ppermute | solution.py:101
  64.2 0.1 fusion.10
  64.3 1.2 %collective-permute-start.13 = (bf16[128,512]{1,0:T(8,128)(2,1)S(1)}, bf16[128,512]{1,0:T(8,128)(2,1)S(1)}, u32[]{:S(2)}, u32[]{:S(2)}) collective-permute-start(bf16[128,512]{1,0:T(8,128)(2,1)S(1)} %fusion.10), channel_id=1, source_target_pairs={{0,8},{4,12},{8,0},{12,4},{1,9},{5,13},{9,1},{13,5},{2,10},{6,14},... | collective-permute-start | bytes 393224 | tf_op jit(solution)/shard_map/ppermute | solution.py:105
  65.5 1.8 %prefix_attend.7 = (f32[128,4096]{1,0:T(8,128)S(1)}, f32[8,4096]{1,0:T(8,128)S(1)}) custom-call(bf16[8192,128]{1,0:T(8,128)(2,1)S(1)} %bitcast.51, bf16[1024,256]{1,0:T(8,128)(2,1)S(1)} %get-tuple-element.88.keys, bf16[288,1024]{1,0:T(8,128)(2,1)S(1)} %get-tuple-element.89.values, ...), custom_call_target="tpu_custom_call", output_to_operand_aliasing={{0}: (3, {}), {1}: (4, {})} | custom-call | flops 20000000000 | bytes 1 | tf_op jit(solution)/shard_map/prefix_attend/pallas_call | solution.py:438
  67.3 1.3 %collective-permute-done.10 = bf16[128,512]{1,0:T(8,128)(2,1)S(1)} collective-permute-done((bf16[128,512]{1,0:T(8,128)(2,1)S(1)}, bf16[128,512]{1,0:T(8,128)(2,1)S(1)}, u32[]{:S(2)}, u32[]{:S(2)}) %collective-permute-start.10) | collective-permute-done | bytes 131104 | tf_op jit(solution)/shard_map/ppermute | solution.py:101
  68.6 0.1 fusion.13
  68.7 4.4 %collective-permute-done.13.rest_4_ = bf16[128,512]{1,0:T(8,128)(2,1)S(1)} collective-permute-done((bf16[128,512]{1,0:T(8,128)(2,1)S(1)}, bf16[128,512]{1,0:T(8,128)(2,1)S(1)}, u32[]{:S(2)}, u32[]{:S(2)}) %collective-permute-start.13) | collective-permute-done | bytes 131104 | tf_op jit(solution)/shard_map/ppermute | solution.py:105
  73.0 0.5 collective-permute-start.14
  73.5 0.0 collective-permute-done.12.rest_3_.rest_4_
  73.5 0.0 collective-permute-done.11.rest_2_.rest_3_
  73.5 4.1 %fresh_attend.2 = (bf16[8192,128]{1,0:T(8,128)(2,1)}, bf16[128,512]{1,0:T(8,128)(2,1)S(1)}) custom-call(s32[1]{0:T(128)S(6)} %copy.21.length_ref, bf16[8192,128]{1,0:T(8,128)(2,1)S(1)} %bitcast.52, f32[128,4096]{1,0:T(8,128)S(1)} %get-tuple-element.102.acc_ref, f32[8,4096]{1,0:T(8,128)S(1)} %get-tuple-element.103.stat_ref, ...), custom_call_target="tpu_custom_call" | custom-call | flops 20000000000 | bytes 1 | tf_op jit(solution)/shard_map/fresh_attend/pallas_call | solution.py:527
  77.6 2.1 %collective-permute-done.14.rest_5_ = bf16[128,512]{1,0:T(8,128)(2,1)S(1)} collective-permute-done((bf16[128,512]{1,0:T(8,128)(2,1)S(1)}, bf16[128,512]{1,0:T(8,128)(2,1)S(1)}, u32[]{:S(2)}, u32[]{:S(2)}) %collective-permute-start.14) | collective-permute-done | bytes 131104 | tf_op jit(solution)/shard_map/ppermute | solution.py:105
  79.8 4.7 %fresh_attend.3 = (bf16[8192,128]{1,0:T(8,128)(2,1)}, bf16[128,512]{1,0:T(8,128)(2,1)}) custom-call(s32[1]{0:T(128)S(6)} %copy.21.length_ref, bf16[8192,128]{1,0:T(8,128)(2,1)S(1)} %bitcast.53, f32[128,4096]{1,0:T(8,128)S(1)} %get-tuple-element.100.acc_ref, f32[8,4096]{1,0:T(8,128)S(1)} %get-tuple-element.101.stat_ref, ...), custom_call_target="tpu_custom_call", output_to_operand_aliasing={{0}: (10, {})} | custom-call | flops 20000000000 | bytes 1 | tf_op jit(solution)/shard_map/fresh_attend/pallas_call | solution.py:527
  (14 shorter events, 0.0 us)
Async XLA Ops:
  0.1 7.1 %copy-start = (bf16[8,128,4,1,256]{4,2,3,1,0:T(4,128)(2,1)S(1)}, bf16[8,128,4,1,256]{4,2,3,1,0:T(4,128)(2,1)}, u32[]{:S(2)}) copy-start(bf16[8,128,4,1,256]{4,2,3,1,0:T(4,128)(2,1)} %param.11) | copy-start | bytes 6291460
  2.1 18.0 %collective-permute-start = (bf16[256,1024]{1,0:T(8,128)(2,1)S(1)}, bf16[256,1024]{1,0:T(8,128)(2,1)S(1)}, u32[]{:S(2)}, u32[]{:S(2)}) collective-permute-start(bf16[256,1024]{1,0:T(8,128)(2,1)S(1)} %get-tuple-element.64), channel_id=1, source_target_pairs={{0,12},{4,8},{8,4},{12,0},{1,13},{5,9},{9,5},{13,1},{2,14},{6,10},... | collective-permute-start | bytes 1572872 | tf_op jit(solution)/shard_map/ppermute | solution.py:105
  7.2 24.3 %collective-permute-start.1 = (bf16[256,1024]{1,0:T(8,128)(2,1)S(1)}, bf16[256,1024]{1,0:T(8,128)(2,1)S(1)}, u32[]{:S(2)}, u32[]{:S(2)}) collective-permute-start(bf16[256,1024]{1,0:T(8,128)(2,1)S(1)} %get-tuple-element.65), channel_id=1, source_target_pairs={{0,4},{4,0},{8,12},{12,8},{1,5},{5,1},{9,13},{13,9},{2,6},{6,2},{1... | collective-permute-start | bytes 1572872 | tf_op jit(solution)/shard_map/ppermute | solution.py:105
  7.2 3.5 %copy-start.1 = (bf16[1,1,1024,4,2,128]{5,4,3,2,1,0:T(2,128)(2,1)S(1)}, bf16[1,1,1024,4,2,128]{5,4,3,2,1,0:T(2,128)(2,1)}, u32[]{:S(2)}) copy-start(bf16[1,1,1024,4,2,128]{5,4,3,2,1,0:T(2,128)(2,1)} %param.8) | copy-start | bytes 6291460
  7.2 3.5 %copy-start.2 = (bf16[1,1,1024,4,2,128]{5,4,3,2,1,0:T(2,128)(2,1)S(1)}, bf16[1,1,1024,4,2,128]{5,4,3,2,1,0:T(2,128)(2,1)}, u32[]{:S(2)}) copy-start(bf16[1,1,1024,4,2,128]{5,4,3,2,1,0:T(2,128)(2,1)} %param.9) | copy-start | bytes 6291460
  9.1 27.4 %collective-permute-start.3 = (bf16[8,128,512]{2,1,0:T(8,128)(2,1)S(1)}, bf16[8,128,512]{2,1,0:T(8,128)(2,1)S(1)}, u32[]{:S(2)}, u32[]{:S(2)}) collective-permute-start(bf16[8,128,512]{2,1,0:T(8,128)(2,1)S(1)} %get-tuple-element.74), channel_id=1, source_target_pairs={{0,2},{2,0},{1,3},{3,1},{4,6},{6,4},{5,7},{7,5},{8,10},{10,8},{9,1... | collective-permute-start | bytes 3145736 | tf_op jit(solution)/shard_map/ppermute | solution.py:101
  13.2 38.8 %collective-permute-start.5 = (bf16[256,1024]{1,0:T(8,128)(2,1)S(1)}, bf16[256,1024]{1,0:T(8,128)(2,1)S(1)}, u32[]{:S(2)}, u32[]{:S(2)}) collective-permute-start(bf16[256,1024]{1,0:T(8,128)(2,1)S(1)} %get-tuple-element.84), channel_id=1, source_target_pairs={{0,8},{4,12},{8,0},{12,4},{1,9},{5,13},{9,1},{13,5},{2,10},{6,14},... | collective-permute-start | bytes 1572872 | tf_op jit(solution)/shard_map/ppermute | solution.py:105
  33.6 2.7 %collective-permute-start.2 = (bf16[2,512,512]{2,1,0:T(8,128)(2,1)S(1)}, bf16[2,512,512]{2,1,0:T(8,128)(2,1)S(1)}, u32[]{:S(2)}, u32[]{:S(2)}) collective-permute-start(bf16[2,512,512]{2,1,0:T(8,128)(2,1)S(1)} %early_away.1), channel_id=1, source_target_pairs={{0,1},{1,0},{2,3},{3,2},{4,5},{5,4},{6,7},{7,6},{8,9},{9,8},{10,11... | collective-permute-start | bytes 3145736 | tf_op jit(solution)/shard_map/ppermute | solution.py:101
  35.8 2.8 %copy-start.5 = (s32[1,8]{1,0:T(1,128)S(1)}, s32[1,8]{1,0:T(1,128)}, u32[]{:S(2)}) copy-start(s32[1,8]{1,0:T(1,128)} %param.12) | copy-start | bytes 100
  36.5 11.1 %collective-permute-start.4 = (bf16[256,512]{1,0:T(8,128)(2,1)S(1)}, bf16[256,512]{1,0:T(8,128)(2,1)S(1)}, u32[]{:S(2)}, u32[]{:S(2)}) collective-permute-start(bf16[256,512]{1,0:T(8,128)(2,1)S(1)} %get-tuple-element.81), channel_id=1, source_target_pairs={{0,2},{2,0},{1,3},{3,1},{4,6},{6,4},{5,7},{7,5},{8,10},{10,8},{9,1... | collective-permute-start | bytes 786440 | tf_op jit(solution)/shard_map/ppermute | solution.py:101
  38.0 14.0 %collective-permute-start.6 = (bf16[256,512]{1,0:T(8,128)(2,1)S(1)}, bf16[256,512]{1,0:T(8,128)(2,1)S(1)}, u32[]{:S(2)}, u32[]{:S(2)}) collective-permute-start(bf16[256,512]{1,0:T(8,128)(2,1)S(1)} %get-tuple-element.86), channel_id=1, source_target_pairs={{0,2},{2,0},{1,3},{3,1},{4,6},{6,4},{5,7},{7,5},{8,10},{10,8},{9,1... | collective-permute-start | bytes 786440 | tf_op jit(solution)/shard_map/ppermute | solution.py:101
  38.6 1.7 %copy-start.4 = (bf16[256,2,1,2048]{3,1,2,0:T(2,128)(2,1)S(1)}, bf16[256,2,1,2048]{3,1,2,0:T(2,128)(2,1)}, u32[]{:S(2)}) copy-start(bf16[256,2,1,2048]{3,1,2,0:T(2,128)(2,1)} %param.10) | copy-start | bytes 6291460
  47.6 4.4 %copy-start.3 = (bf16[256,4096]{1,0:T(8,128)(2,1)S(1)}, bf16[256,4096]{1,0:T(8,128)(2,1)}, u32[]{:S(2)}) copy-start(bf16[256,4096]{1,0:T(8,128)(2,1)} %refs_1_.3) | copy-start | bytes 6291460
  54.2 4.3 %collective-permute-start.7 = (bf16[2,512,512]{2,1,0:T(8,128)(2,1)S(1)}, bf16[2,512,512]{2,1,0:T(8,128)(2,1)S(1)}, u32[]{:S(2)}, u32[]{:S(2)}) collective-permute-start(bf16[2,512,512]{2,1,0:T(8,128)(2,1)S(1)} %get-tuple-element.87), channel_id=1, source_target_pairs={{0,1},{1,0},{2,3},{3,2},{4,5},{5,4},{6,7},{7,6},{8,9},{9,8},{10,11... | collective-permute-start | bytes 3145736 | tf_op jit(solution)/shard_map/ppermute | solution.py:101
  54.3 9.9 %collective-permute-start.9 = (bf16[256,512]{1,0:T(8,128)(2,1)S(1)}, bf16[256,512]{1,0:T(8,128)(2,1)S(1)}, u32[]{:S(2)}, u32[]{:S(2)}) collective-permute-start(bf16[256,512]{1,0:T(8,128)(2,1)S(1)} %get-tuple-element.90), channel_id=1, source_target_pairs={{0,4},{4,0},{8,12},{12,8},{1,5},{5,1},{9,13},{13,9},{2,6},{6,2},{1... | collective-permute-start | bytes 786440 | tf_op jit(solution)/shard_map/ppermute | solution.py:105
  55.4 18.1 %collective-permute-start.12 = (bf16[256,512]{1,0:T(8,128)(2,1)S(1)}, bf16[256,512]{1,0:T(8,128)(2,1)S(1)}, u32[]{:S(2)}, u32[]{:S(2)}) collective-permute-start(bf16[256,512]{1,0:T(8,128)(2,1)S(1)} %get-tuple-element.108), channel_id=1, source_target_pairs={{0,4},{4,0},{8,12},{12,8},{1,5},{5,1},{9,13},{13,9},{2,6},{6,2},{1... | collective-permute-start | bytes 786440 | tf_op jit(solution)/shard_map/ppermute | solution.py:105
  58.6 5.6 %collective-permute-start.8 = (bf16[128,512]{1,0:T(8,128)(2,1)S(1)}, bf16[128,512]{1,0:T(8,128)(2,1)S(1)}, u32[]{:S(2)}, u32[]{:S(2)}) collective-permute-start(bf16[128,512]{1,0:T(8,128)(2,1)S(1)} %get-tuple-element.117), channel_id=1, source_target_pairs={{0,2},{2,0},{1,3},{3,1},{4,6},{6,4},{5,7},{7,5},{8,10},{10,8},{9,1... | collective-permute-start | bytes 393224 | tf_op jit(solution)/shard_map/ppermute | solution.py:101
  62.1 6.5 %collective-permute-start.10 = (bf16[128,512]{1,0:T(8,128)(2,1)S(1)}, bf16[128,512]{1,0:T(8,128)(2,1)S(1)}, u32[]{:S(2)}, u32[]{:S(2)}) collective-permute-start(bf16[128,512]{1,0:T(8,128)(2,1)S(1)} %get-tuple-element.104), channel_id=1, source_target_pairs={{0,2},{2,0},{1,3},{3,1},{4,6},{6,4},{5,7},{7,5},{8,10},{10,8},{9,1... | collective-permute-start | bytes 393224 | tf_op jit(solution)/shard_map/ppermute | solution.py:101
  62.7 10.8 %collective-permute-start.11 = (bf16[256,512]{1,0:T(8,128)(2,1)S(1)}, bf16[256,512]{1,0:T(8,128)(2,1)S(1)}, u32[]{:S(2)}, u32[]{:S(2)}) collective-permute-start(bf16[256,512]{1,0:T(8,128)(2,1)S(1)} %fusion.5), channel_id=1, source_target_pairs={{0,2},{2,0},{1,3},{3,1},{4,6},{6,4},{5,7},{7,5},{8,10},{10,8},{9,1... | collective-permute-start | bytes 786440 | tf_op jit(solution)/shard_map/ppermute | solution.py:101
  64.3 8.7 %collective-permute-start.13 = (bf16[128,512]{1,0:T(8,128)(2,1)S(1)}, bf16[128,512]{1,0:T(8,128)(2,1)S(1)}, u32[]{:S(2)}, u32[]{:S(2)}) collective-permute-start(bf16[128,512]{1,0:T(8,128)(2,1)S(1)} %fusion.10), channel_id=1, source_target_pairs={{0,8},{4,12},{8,0},{12,4},{1,9},{5,13},{9,1},{13,5},{2,10},{6,14},... | collective-permute-start | bytes 393224 | tf_op jit(solution)/shard_map/ppermute | solution.py:105
  73.0 6.7 %collective-permute-start.14 = (bf16[128,512]{1,0:T(8,128)(2,1)S(1)}, bf16[128,512]{1,0:T(8,128)(2,1)S(1)}, u32[]{:S(2)}, u32[]{:S(2)}) collective-permute-start(bf16[128,512]{1,0:T(8,128)(2,1)S(1)} %fusion.13), channel_id=1, source_target_pairs={{0,8},{4,12},{8,0},{12,4},{1,9},{5,13},{9,1},{13,5},{2,10},{6,14},... | collective-permute-start | bytes 393224 | tf_op jit(solution)/shard_map/ppermute | solution.py:105

commit v23 on v22

--- a/solution.py
+++ b/solution.py
@@ -643,7 +643,7 @@
     late_others[1], (keys, values) = after(late_others[1], (keys, values))
     state = prefix_attend(query_rows, keys, values, 1, scale, heads, (2, 4), state)
     state, (late_others[1], own_others) = after(state, (late_others[1], own_others))
-    late_others[1], own_others = spread(late_others[1]), spread(own_others)
+    late_others[1] = spread(late_others[1])
 
     away = []
     for chunk, here in enumerate(parts_of):
@@ -652,7 +652,8 @@
         part = part.astype(jnp.bfloat16)
         if chunk == 0:
             (far, late), late_others[1] = after((far, late), late_others[1])
-            part, state = after(part, state)
+            part, (state, own_others) = after(part, (state, own_others))
+            own_others = spread(own_others)
         else:
             away[-1], part = after(away[-1], part)
         away.append(trade(part, "batch", top))

time: 84.7 us -> 84.7 us (level)
  starting transfers between devices: 17.1 us -> 18 us
  waiting for transfers between devices: 25.9 us -> 25 us
  transfers between devices with their start and end apart: 15 -> 15, of which waited for: 7 -> 8; matrix products, arithmetic and copies ran while one was open for 1% -> 1% of each run, Pallas kernels for 37% -> 37%
where the time goes in v23:
time: 84.7 us; the launch traced here: 84.5 us
  Pallas kernels  40 us (47%)
  waiting for transfers between devices  25 us (30%)
  starting transfers between devices  18 us (21%)
  between operations  0.87 us (1%)
    ppermute x7, waiting for transfers between devices, trade(): lax.ppermute(array, axis, [(i, i ^ bits) for i in range(lax.axis_size(axi...  24 us
    pallas_call x4, Pallas kernels, prefix_attend(): pl.pallas_call(functools.partial(prefix_kernel, scale, heads, [len(terms)...  14.6 us
    ppermute x7, starting transfers between devices, trade(): lax.ppermute(array, axis, [(i, i ^ bits) for i in range(lax.axis_size(axi...  10.1 us
    pallas_call x2, Pallas kernels, fresh_attend(): pl.pallas_call(functools.partial(fresh_kernel, scale, heads, per_token, c...  8.78 us
    pallas_call x4, Pallas kernels, project(): pl.pallas_call(functools.partial(project_kernel, len(blocks), [len(terms)...  8.53 us
    ppermute x8, starting transfers between devices, shift(): lax.ppermute(array, axis, [(i, (i + step) % count) for i in range(count)])  7.92 us
    pallas_call x1, Pallas kernels, arrange_weights(): pl.pallas_call(functools.partial(weight_kernel, ctx_count, heads, head_co...  2.47 us
    pallas_call x1, Pallas kernels, cut_tokens(): pl.pallas_call(functools.partial(cut_kernel, bits), grid_spec=pltpu.Prefe...  2.02 us
  transfers between devices with their start and end apart: 15, of which 8 were waited for; matrix products, arithmetic and copies ran while one was open for 1% of the time, Pallas kernels for 37%

profile of v23, /device:TPU:0, one launch (start us, length us, event | category | flops | bytes accessed | tf_op | source)
XLA Modules:
  0.0 84.5 jit_solution(7813580794731090927)
XLA Ops:
  0.0 0.1 pad_add_fusion.place_ref
  0.1 2.0 %cut_tokens.1 = (bf16[256,1024]{1,0:T(8,128)(2,1)S(1)}, bf16[256,1024]{1,0:T(8,128)(2,1)S(1)}, bf16[256,1024]{1,0:T(8,128)(2,1)S(1)}) custom-call(s32[3]{0:T(128)S(1)} %pad_add_fusion.place_ref, bf16[256,4096]{1,0:T(8,128)(2,1)} %refs_1_.3), custom_call_target="tpu_custom_call" | custom-call | flops 20000000000 | bytes 1 | tf_op jit(solution)/shard_map/cut_tokens/pallas_call | solution.py:180
  2.1 5.1 %collective-permute-start = (bf16[256,1024]{1,0:T(8,128)(2,1)S(1)}, bf16[256,1024]{1,0:T(8,128)(2,1)S(1)}, u32[]{:S(2)}, u32[]{:S(2)}) collective-permute-start(bf16[256,1024]{1,0:T(8,128)(2,1)S(1)} %get-tuple-element.65), channel_id=1, source_target_pairs={{0,12},{4,8},{8,4},{12,0},{1,13},{5,9},{9,5},{13,1},{2,14},{6,10},... | collective-permute-start | bytes 1572872 | tf_op jit(solution)/shard_map/ppermute | solution.py:105
  7.2 0.0 collective-permute-start.1
  7.2 1.9 %arrange_pool.1 = (bf16[8,128,512]{2,1,0:T(8,128)(2,1)S(1)}, bf16[8,128,512]{2,1,0:T(8,128)(2,1)S(1)}) custom-call(s32[3]{0:T(128)S(1)} %pad_add_fusion.place_ref, bf16[8,128,8,128]{3,2,1,0:T(8,128)(2,1)S(1)} %bitcast.45), custom_call_target="tpu_custom_call" | custom-call | flops 20000000000 | bytes 1 | tf_op jit(solution)/shard_map/arrange_pool/pallas_call | solution.py:227
  9.1 1.6 %collective-permute-start.3 = (bf16[8,128,512]{2,1,0:T(8,128)(2,1)S(1)}, bf16[8,128,512]{2,1,0:T(8,128)(2,1)S(1)}, u32[]{:S(2)}, u32[]{:S(2)}) collective-permute-start(bf16[8,128,512]{2,1,0:T(8,128)(2,1)S(1)} %get-tuple-element.75), channel_id=1, source_target_pairs={{0,2},{2,0},{1,3},{3,1},{4,6},{6,4},{5,7},{7,5},{8,10},{10,8},{9,1... | collective-permute-start | bytes 3145736 | tf_op jit(solution)/shard_map/ppermute | solution.py:101
  10.7 2.5 %arrange_weights.1.refs_2_ = bf16[2,2,1024,512]{3,2,1,0:T(8,128)(2,1)S(1)} custom-call(bf16[1024,8,128]{2,1,0:T(8,128)(2,1)S(1)} %bitcast.46, bf16[1024,8,128]{2,1,0:T(8,128)(2,1)S(1)} %bitcast.47), custom_call_target="tpu_custom_call" | custom-call | flops 20000000000 | bytes 1 | tf_op jit(solution)/shard_map/arrange_weights/pallas_call | solution.py:150
  13.2 0.8 collective-permute-start.5
  14.7 5.4 %collective-permute-done.refs_0_ = bf16[256,1024]{1,0:T(8,128)(2,1)S(1)} collective-permute-done((bf16[256,1024]{1,0:T(8,128)(2,1)S(1)}, bf16[256,1024]{1,0:T(8,128)(2,1)S(1)}, u32[]{:S(2)}, u32[]{:S(2)}) %collective-permute-start) | collective-permute-done | bytes 524320 | tf_op jit(solution)/shard_map/ppermute | solution.py:105
  20.1 11.5 %collective-permute-done.1.refs_1_ = bf16[256,1024]{1,0:T(8,128)(2,1)S(1)} collective-permute-done((bf16[256,1024]{1,0:T(8,128)(2,1)S(1)}, bf16[256,1024]{1,0:T(8,128)(2,1)S(1)}, u32[]{:S(2)}, u32[]{:S(2)}) %collective-permute-start.1) | collective-permute-done | bytes 524320 | tf_op jit(solution)/shard_map/ppermute | solution.py:105
  31.5 2.1 %early_away.1 = bf16[2,512,512]{2,1,0:T(8,128)(2,1)S(1)} custom-call(s32[3]{0:T(128)S(1)} %pad_add_fusion.place_ref, bf16[256,1024]{1,0:T(8,128)(2,1)S(1)} %collective-permute-done.refs_0_, bf16[256,1024]{1,0:T(8,128)(2,1)S(1)} %collective-permute-done.1.refs_1_, bf16[2,2,1024,512]{3,2,1,0:T(8,128)(2,1)S(1)} %arrange_weights.1.refs_2_), custom_call_target="tpu_custom_call" | custom-call | flops 20000000000 | bytes 1 | tf_op jit(solution)/shard_map/early_away/pallas_call | solution.py:291
  33.6 0.1 collective-permute-start.2
  33.7 2.1 %early_kept.1.refs_0_.refs_3_ = f32[2,512,512]{2,1,0:T(8,128)S(1)} custom-call(s32[3]{0:T(128)S(1)} %pad_add_fusion.place_ref, bf16[256,1024]{1,0:T(8,128)(2,1)S(1)} %collective-permute-done.refs_0_, bf16[256,1024]{1,0:T(8,128)(2,1)S(1)} %collective-permute-done.1.refs_1_, bf16[2,2,1024,512]{3,2,1,0:T(8,128)(2,1)S(1)} %arrange_weights.1.refs_2_), custom_call_target="tpu_custom_call" | custom-call | flops 20000000000 | bytes 1 | tf_op jit(solution)/shard_map/early_kept/pallas_call | solution.py:291
  35.8 0.0 copy-start.5
  35.8 0.5 collective-permute-done.2.refs_1_.refs_4_
  36.3 0.2 fusion.4
  36.5 0.0 collective-permute-done.3.refs_1_
  36.5 1.4 %collective-permute-start.4 = (bf16[256,512]{1,0:T(8,128)(2,1)S(1)}, bf16[256,512]{1,0:T(8,128)(2,1)S(1)}, u32[]{:S(2)}, u32[]{:S(2)}) collective-permute-start(bf16[256,512]{1,0:T(8,128)(2,1)S(1)} %get-tuple-element.82), channel_id=1, source_target_pairs={{0,2},{2,0},{1,3},{3,1},{4,6},{6,4},{5,7},{7,5},{8,10},{10,8},{9,1... | collective-permute-start | bytes 786440 | tf_op jit(solution)/shard_map/ppermute | solution.py:101
  38.0 0.6 collective-permute-start.6
  38.6 1.7 %pick_blocks.1 = (bf16[1024,256]{1,0:T(8,128)(2,1)S(1)}, bf16[288,1024]{1,0:T(8,128)(2,1)S(1)}) custom-call(s32[3]{0:T(128)S(1)} %pad_add_fusion.place_ref, s32[8]{0:T(128)S(1)} %bitcast.54, bf16[8,128,512]{2,1,0:T(8,128)(2,1)S(1)} %get-tuple-element.76.refs_0_, bf16[8,128,512]{2,1,0:T(8,128)(2,1)S(1)} %collective-permute-done.3.refs_1_), custom_call_target="tpu_custom_call" | custom-call | flops 20000000000 | bytes 1 | tf_op jit(solution)/shard_map/pick_blocks/pallas_call | solution.py:355
  40.3 7.2 %prefix_attend.4 = (f32[128,4096]{1,0:T(8,128)S(1)}, f32[8,4096]{1,0:T(8,128)S(1)}) custom-call(bf16[8192,128]{1,0:T(8,128)(2,1)S(1)} %bitcast.48, bf16[1024,256]{1,0:T(8,128)(2,1)S(1)} %get-tuple-element.89.keys, bf16[288,1024]{1,0:T(8,128)(2,1)S(1)} %get-tuple-element.90.values), custom_call_target="tpu_custom_call" | custom-call | flops 20000000000 | bytes 1 | tf_op jit(solution)/shard_map/prefix_attend/pallas_call | solution.py:438
  47.6 0.0 copy-start.3
  47.6 0.0 collective-permute-done.4.refs_2_
  47.6 3.7 %prefix_attend.5 = (f32[128,4096]{1,0:T(8,128)S(1)}, f32[8,4096]{1,0:T(8,128)S(1)}, bf16[256,512]{1,0:T(8,128)(2,1)S(1)}) custom-call(bf16[8192,128]{1,0:T(8,128)(2,1)S(1)} %bitcast.49, bf16[1024,256]{1,0:T(8,128)(2,1)S(1)} %get-tuple-element.89.keys, bf16[288,1024]{1,0:T(8,128)(2,1)S(1)} %get-tuple-element.90.values, ...), custom_call_target="tpu_custom_call" | custom-call | flops 20000000000 | bytes 1 | tf_op jit(solution)/shard_map/prefix_attend/pallas_call | solution.py:438
  51.3 0.7 collective-permute-done.5.refs_0_
  52.0 2.2 %late_away.1 = (bf16[2,512,512]{2,1,0:T(8,128)(2,1)S(1)}, bf16[256,512]{1,0:T(8,128)(2,1)S(1)}) custom-call(s32[3]{0:T(128)S(1)} %pad_add_fusion.place_ref, bf16[256,1024]{1,0:T(8,128)(2,1)S(1)} %collective-permute-done.5.refs_0_, bf16[256,4096]{1,0:T(8,128)(2,1)S(1)} %copy-done.3, bf16[2,2,1024,512]{3,2,1,0:T(8,128)(2,1)S(1)} %arrange_weights.1.refs_2_, ...), custom_call_target="tpu_custom_call" | custom-call | flops 20000000000 | bytes 1 | tf_op jit(solution)/shard_map/late_away/pallas_call | solution.py:291
  54.2 0.1 collective-permute-start.7
  54.3 1.1 %collective-permute-start.9 = (bf16[256,512]{1,0:T(8,128)(2,1)S(1)}, bf16[256,512]{1,0:T(8,128)(2,1)S(1)}, u32[]{:S(2)}, u32[]{:S(2)}) collective-permute-start(bf16[256,512]{1,0:T(8,128)(2,1)S(1)} %get-tuple-element.91), channel_id=1, source_target_pairs={{0,4},{4,0},{8,12},{12,8},{1,5},{5,1},{9,13},{13,9},{2,6},{6,2},{1... | collective-permute-start | bytes 786440 | tf_op jit(solution)/shard_map/ppermute | solution.py:105
  55.4 1.0 %collective-permute-start.12 = (bf16[256,512]{1,0:T(8,128)(2,1)S(1)}, bf16[256,512]{1,0:T(8,128)(2,1)S(1)}, u32[]{:S(2)}, u32[]{:S(2)}) collective-permute-start(bf16[256,512]{1,0:T(8,128)(2,1)S(1)} %get-tuple-element.110), channel_id=1, source_target_pairs={{0,4},{4,0},{8,12},{12,8},{1,5},{5,1},{9,13},{13,9},{2,6},{6,2},{1... | collective-permute-start | bytes 786440 | tf_op jit(solution)/shard_map/ppermute | solution.py:105
  56.4 2.1 %late_kept.1.rest_0_.rest_1_ = f32[2,512,512]{2,1,0:T(8,128)S(1)} custom-call(s32[3]{0:T(128)S(1)} %pad_add_fusion.place_ref, bf16[256,1024]{1,0:T(8,128)(2,1)S(1)} %collective-permute-done.5.refs_0_, bf16[256,4096]{1,0:T(8,128)(2,1)S(1)} %copy-done.3, bf16[2,2,1024,512]{3,2,1,0:T(8,128)(2,1)S(1)} %arrange_weights.1.refs_2_), custom_call_target="tpu_custom_call" | custom-call | flops 20000000000 | bytes 1 | tf_op jit(solution)/shard_map/late_kept/pallas_call | solution.py:291
  58.5 0.0 collective-permute-done.7.rest_1_.rest_2_
  58.6 0.1 fusion.15
  58.6 1.6 %collective-permute-start.8 = (bf16[128,512]{1,0:T(8,128)(2,1)S(1)}, bf16[128,512]{1,0:T(8,128)(2,1)S(1)}, u32[]{:S(2)}, u32[]{:S(2)}) collective-permute-start(bf16[128,512]{1,0:T(8,128)(2,1)S(1)} %get-tuple-element.119), channel_id=1, source_target_pairs={{0,2},{2,0},{1,3},{3,1},{4,6},{6,4},{5,7},{7,5},{8,10},{10,8},{9,1... | collective-permute-start | bytes 393224 | tf_op jit(solution)/shard_map/ppermute | solution.py:101
  60.2 1.9 %prefix_attend.6 = (f32[128,4096]{1,0:T(8,128)S(1)}, f32[8,4096]{1,0:T(8,128)S(1)}) custom-call(bf16[8192,128]{1,0:T(8,128)(2,1)S(1)} %bitcast.50, bf16[1024,256]{1,0:T(8,128)(2,1)S(1)} %get-tuple-element.89.keys, bf16[288,1024]{1,0:T(8,128)(2,1)S(1)} %get-tuple-element.90.values, ...), custom_call_target="tpu_custom_call", output_to_operand_aliasing={{0}: (3, {}), {1}: (4, {})} | custom-call | flops 20000000000 | bytes 1 | tf_op jit(solution)/shard_map/prefix_attend/pallas_call | solution.py:438
  62.1 0.1 fusion.5
  62.1 0.6 collective-permute-start.10
  62.7 0.8 collective-permute-done.9
  63.5 0.5 collective-permute-done.8
  64.0 0.1 fusion.10
  64.1 1.4 %collective-permute-start.13 = (bf16[128,512]{1,0:T(8,128)(2,1)S(1)}, bf16[128,512]{1,0:T(8,128)(2,1)S(1)}, u32[]{:S(2)}, u32[]{:S(2)}) collective-permute-start(bf16[128,512]{1,0:T(8,128)(2,1)S(1)} %fusion.10), channel_id=1, source_target_pairs={{0,8},{4,12},{8,0},{12,4},{1,9},{5,13},{9,1},{13,5},{2,10},{6,14},... | collective-permute-start | bytes 393224 | tf_op jit(solution)/shard_map/ppermute | solution.py:105
  65.4 2.0 %collective-permute-start.11 = (bf16[256,512]{1,0:T(8,128)(2,1)S(1)}, bf16[256,512]{1,0:T(8,128)(2,1)S(1)}, u32[]{:S(2)}, u32[]{:S(2)}) collective-permute-start(bf16[256,512]{1,0:T(8,128)(2,1)S(1)} %fusion.5), channel_id=1, source_target_pairs={{0,2},{2,0},{1,3},{3,1},{4,6},{6,4},{5,7},{7,5},{8,10},{10,8},{9,1... | collective-permute-start | bytes 786440 | tf_op jit(solution)/shard_map/ppermute | solution.py:101
  67.4 1.9 %prefix_attend.7 = (f32[128,4096]{1,0:T(8,128)S(1)}, f32[8,4096]{1,0:T(8,128)S(1)}) custom-call(bf16[8192,128]{1,0:T(8,128)(2,1)S(1)} %bitcast.51, bf16[1024,256]{1,0:T(8,128)(2,1)S(1)} %get-tuple-element.89.keys, bf16[288,1024]{1,0:T(8,128)(2,1)S(1)} %get-tuple-element.90.values, ...), custom_call_target="tpu_custom_call", output_to_operand_aliasing={{0}: (3, {}), {1}: (4, {})} | custom-call | flops 20000000000 | bytes 1 | tf_op jit(solution)/shard_map/prefix_attend/pallas_call | solution.py:438
  69.3 0.1 fusion.13
  69.4 3.4 %collective-permute-done.13.rest_4_ = bf16[128,512]{1,0:T(8,128)(2,1)S(1)} collective-permute-done((bf16[128,512]{1,0:T(8,128)(2,1)S(1)}, bf16[128,512]{1,0:T(8,128)(2,1)S(1)}, u32[]{:S(2)}, u32[]{:S(2)}) %collective-permute-start.13) | collective-permute-done | bytes 131104 | tf_op jit(solution)/shard_map/ppermute | solution.py:105
  72.8 0.7 collective-permute-start.14
  73.5 4.1 %fresh_attend.2 = (bf16[8192,128]{1,0:T(8,128)(2,1)}, bf16[128,512]{1,0:T(8,128)(2,1)S(1)}) custom-call(s32[1]{0:T(128)S(6)} %copy.21.length_ref, bf16[8192,128]{1,0:T(8,128)(2,1)S(1)} %bitcast.52, f32[128,4096]{1,0:T(8,128)S(1)} %get-tuple-element.104.acc_ref, f32[8,4096]{1,0:T(8,128)S(1)} %get-tuple-element.105.stat_ref, ...), custom_call_target="tpu_custom_call" | custom-call | flops 20000000000 | bytes 1 | tf_op jit(solution)/shard_map/fresh_attend/pallas_call | solution.py:527
  77.6 2.2 %collective-permute-done.14.rest_5_ = bf16[128,512]{1,0:T(8,128)(2,1)S(1)} collective-permute-done((bf16[128,512]{1,0:T(8,128)(2,1)S(1)}, bf16[128,512]{1,0:T(8,128)(2,1)S(1)}, u32[]{:S(2)}, u32[]{:S(2)}) %collective-permute-start.14) | collective-permute-done | bytes 131104 | tf_op jit(solution)/shard_map/ppermute | solution.py:105
  79.8 4.7 %fresh_attend.3 = (bf16[8192,128]{1,0:T(8,128)(2,1)}, bf16[128,512]{1,0:T(8,128)(2,1)}) custom-call(s32[1]{0:T(128)S(6)} %copy.21.length_ref, bf16[8192,128]{1,0:T(8,128)(2,1)S(1)} %bitcast.53, f32[128,4096]{1,0:T(8,128)S(1)} %get-tuple-element.102.acc_ref, f32[8,4096]{1,0:T(8,128)S(1)} %get-tuple-element.103.stat_ref, ...), custom_call_target="tpu_custom_call", output_to_operand_aliasing={{0}: (10, {})} | custom-call | flops 20000000000 | bytes 1 | tf_op jit(solution)/shard_map/fresh_attend/pallas_call | solution.py:527
  (14 shorter events, 0.0 us)
Async XLA Ops:
  0.1 7.1 %copy-start = (bf16[8,128,4,1,256]{4,2,3,1,0:T(4,128)(2,1)S(1)}, bf16[8,128,4,1,256]{4,2,3,1,0:T(4,128)(2,1)}, u32[]{:S(2)}) copy-start(bf16[8,128,4,1,256]{4,2,3,1,0:T(4,128)(2,1)} %param.11) | copy-start | bytes 6291460
  2.1 18.0 %collective-permute-start = (bf16[256,1024]{1,0:T(8,128)(2,1)S(1)}, bf16[256,1024]{1,0:T(8,128)(2,1)S(1)}, u32[]{:S(2)}, u32[]{:S(2)}) collective-permute-start(bf16[256,1024]{1,0:T(8,128)(2,1)S(1)} %get-tuple-element.65), channel_id=1, source_target_pairs={{0,12},{4,8},{8,4},{12,0},{1,13},{5,9},{9,5},{13,1},{2,14},{6,10},... | collective-permute-start | bytes 1572872 | tf_op jit(solution)/shard_map/ppermute | solution.py:105
  7.2 24.3 %collective-permute-start.1 = (bf16[256,1024]{1,0:T(8,128)(2,1)S(1)}, bf16[256,1024]{1,0:T(8,128)(2,1)S(1)}, u32[]{:S(2)}, u32[]{:S(2)}) collective-permute-start(bf16[256,1024]{1,0:T(8,128)(2,1)S(1)} %get-tuple-element.66), channel_id=1, source_target_pairs={{0,4},{4,0},{8,12},{12,8},{1,5},{5,1},{9,13},{13,9},{2,6},{6,2},{1... | collective-permute-start | bytes 1572872 | tf_op jit(solution)/shard_map/ppermute | solution.py:105
  7.2 3.5 %copy-start.1 = (bf16[1,1,1024,4,2,128]{5,4,3,2,1,0:T(2,128)(2,1)S(1)}, bf16[1,1,1024,4,2,128]{5,4,3,2,1,0:T(2,128)(2,1)}, u32[]{:S(2)}) copy-start(bf16[1,1,1024,4,2,128]{5,4,3,2,1,0:T(2,128)(2,1)} %param.8) | copy-start | bytes 6291460
  7.2 3.5 %copy-start.2 = (bf16[1,1,1024,4,2,128]{5,4,3,2,1,0:T(2,128)(2,1)S(1)}, bf16[1,1,1024,4,2,128]{5,4,3,2,1,0:T(2,128)(2,1)}, u32[]{:S(2)}) copy-start(bf16[1,1,1024,4,2,128]{5,4,3,2,1,0:T(2,128)(2,1)} %param.9) | copy-start | bytes 6291460
  9.1 27.4 %collective-permute-start.3 = (bf16[8,128,512]{2,1,0:T(8,128)(2,1)S(1)}, bf16[8,128,512]{2,1,0:T(8,128)(2,1)S(1)}, u32[]{:S(2)}, u32[]{:S(2)}) collective-permute-start(bf16[8,128,512]{2,1,0:T(8,128)(2,1)S(1)} %get-tuple-element.75), channel_id=1, source_target_pairs={{0,2},{2,0},{1,3},{3,1},{4,6},{6,4},{5,7},{7,5},{8,10},{10,8},{9,1... | collective-permute-start | bytes 3145736 | tf_op jit(solution)/shard_map/ppermute | solution.py:101
  13.2 38.8 %collective-permute-start.5 = (bf16[256,1024]{1,0:T(8,128)(2,1)S(1)}, bf16[256,1024]{1,0:T(8,128)(2,1)S(1)}, u32[]{:S(2)}, u32[]{:S(2)}) collective-permute-start(bf16[256,1024]{1,0:T(8,128)(2,1)S(1)} %get-tuple-element.85), channel_id=1, source_target_pairs={{0,8},{4,12},{8,0},{12,4},{1,9},{5,13},{9,1},{13,5},{2,10},{6,14},... | collective-permute-start | bytes 1572872 | tf_op jit(solution)/shard_map/ppermute | solution.py:105
  33.6 2.7 %collective-permute-start.2 = (bf16[2,512,512]{2,1,0:T(8,128)(2,1)S(1)}, bf16[2,512,512]{2,1,0:T(8,128)(2,1)S(1)}, u32[]{:S(2)}, u32[]{:S(2)}) collective-permute-start(bf16[2,512,512]{2,1,0:T(8,128)(2,1)S(1)} %early_away.1), channel_id=1, source_target_pairs={{0,1},{1,0},{2,3},{3,2},{4,5},{5,4},{6,7},{7,6},{8,9},{9,8},{10,11... | collective-permute-start | bytes 3145736 | tf_op jit(solution)/shard_map/ppermute | solution.py:101
  35.8 2.8 %copy-start.5 = (s32[1,8]{1,0:T(1,128)S(1)}, s32[1,8]{1,0:T(1,128)}, u32[]{:S(2)}) copy-start(s32[1,8]{1,0:T(1,128)} %param.12) | copy-start | bytes 100
  36.5 11.1 %collective-permute-start.4 = (bf16[256,512]{1,0:T(8,128)(2,1)S(1)}, bf16[256,512]{1,0:T(8,128)(2,1)S(1)}, u32[]{:S(2)}, u32[]{:S(2)}) collective-permute-start(bf16[256,512]{1,0:T(8,128)(2,1)S(1)} %get-tuple-element.82), channel_id=1, source_target_pairs={{0,2},{2,0},{1,3},{3,1},{4,6},{6,4},{5,7},{7,5},{8,10},{10,8},{9,1... | collective-permute-start | bytes 786440 | tf_op jit(solution)/shard_map/ppermute | solution.py:101
  38.0 14.0 %collective-permute-start.6 = (bf16[256,512]{1,0:T(8,128)(2,1)S(1)}, bf16[256,512]{1,0:T(8,128)(2,1)S(1)}, u32[]{:S(2)}, u32[]{:S(2)}) collective-permute-start(bf16[256,512]{1,0:T(8,128)(2,1)S(1)} %get-tuple-element.87), channel_id=1, source_target_pairs={{0,2},{2,0},{1,3},{3,1},{4,6},{6,4},{5,7},{7,5},{8,10},{10,8},{9,1... | collective-permute-start | bytes 786440 | tf_op jit(solution)/shard_map/ppermute | solution.py:101
  38.6 1.7 %copy-start.4 = (bf16[256,2,1,2048]{3,1,2,0:T(2,128)(2,1)S(1)}, bf16[256,2,1,2048]{3,1,2,0:T(2,128)(2,1)}, u32[]{:S(2)}) copy-start(bf16[256,2,1,2048]{3,1,2,0:T(2,128)(2,1)} %param.10) | copy-start | bytes 6291460
  47.6 4.4 %copy-start.3 = (bf16[256,4096]{1,0:T(8,128)(2,1)S(1)}, bf16[256,4096]{1,0:T(8,128)(2,1)}, u32[]{:S(2)}) copy-start(bf16[256,4096]{1,0:T(8,128)(2,1)} %refs_1_.3) | copy-start | bytes 6291460
  54.2 4.3 %collective-permute-start.7 = (bf16[2,512,512]{2,1,0:T(8,128)(2,1)S(1)}, bf16[2,512,512]{2,1,0:T(8,128)(2,1)S(1)}, u32[]{:S(2)}, u32[]{:S(2)}) collective-permute-start(bf16[2,512,512]{2,1,0:T(8,128)(2,1)S(1)} %get-tuple-element.88), channel_id=1, source_target_pairs={{0,1},{1,0},{2,3},{3,2},{4,5},{5,4},{6,7},{7,6},{8,9},{9,8},{10,11... | collective-permute-start | bytes 3145736 | tf_op jit(solution)/shard_map/ppermute | solution.py:101
  54.3 9.2 %collective-permute-start.9 = (bf16[256,512]{1,0:T(8,128)(2,1)S(1)}, bf16[256,512]{1,0:T(8,128)(2,1)S(1)}, u32[]{:S(2)}, u32[]{:S(2)}) collective-permute-start(bf16[256,512]{1,0:T(8,128)(2,1)S(1)} %get-tuple-element.91), channel_id=1, source_target_pairs={{0,4},{4,0},{8,12},{12,8},{1,5},{5,1},{9,13},{13,9},{2,6},{6,2},{1... | collective-permute-start | bytes 786440 | tf_op jit(solution)/shard_map/ppermute | solution.py:105
  55.4 18.1 %collective-permute-start.12 = (bf16[256,512]{1,0:T(8,128)(2,1)S(1)}, bf16[256,512]{1,0:T(8,128)(2,1)S(1)}, u32[]{:S(2)}, u32[]{:S(2)}) collective-permute-start(bf16[256,512]{1,0:T(8,128)(2,1)S(1)} %get-tuple-element.110), channel_id=1, source_target_pairs={{0,4},{4,0},{8,12},{12,8},{1,5},{5,1},{9,13},{13,9},{2,6},{6,2},{1... | collective-permute-start | bytes 786440 | tf_op jit(solution)/shard_map/ppermute | solution.py:105
  58.6 5.4 %collective-permute-start.8 = (bf16[128,512]{1,0:T(8,128)(2,1)S(1)}, bf16[128,512]{1,0:T(8,128)(2,1)S(1)}, u32[]{:S(2)}, u32[]{:S(2)}) collective-permute-start(bf16[128,512]{1,0:T(8,128)(2,1)S(1)} %get-tuple-element.119), channel_id=1, source_target_pairs={{0,2},{2,0},{1,3},{3,1},{4,6},{6,4},{5,7},{7,5},{8,10},{10,8},{9,1... | collective-permute-start | bytes 393224 | tf_op jit(solution)/shard_map/ppermute | solution.py:101
  62.1 7.2 %collective-permute-start.10 = (bf16[128,512]{1,0:T(8,128)(2,1)S(1)}, bf16[128,512]{1,0:T(8,128)(2,1)S(1)}, u32[]{:S(2)}, u32[]{:S(2)}) collective-permute-start(bf16[128,512]{1,0:T(8,128)(2,1)S(1)} %get-tuple-element.106), channel_id=1, source_target_pairs={{0,2},{2,0},{1,3},{3,1},{4,6},{6,4},{5,7},{7,5},{8,10},{10,8},{9,1... | collective-permute-start | bytes 393224 | tf_op jit(solution)/shard_map/ppermute | solution.py:101
  64.1 8.7 %collective-permute-start.13 = (bf16[128,512]{1,0:T(8,128)(2,1)S(1)}, bf16[128,512]{1,0:T(8,128)(2,1)S(1)}, u32[]{:S(2)}, u32[]{:S(2)}) collective-permute-start(bf16[128,512]{1,0:T(8,128)(2,1)S(1)} %fusion.10), channel_id=1, source_target_pairs={{0,8},{4,12},{8,0},{12,4},{1,9},{5,13},{9,1},{13,5},{2,10},{6,14},... | collective-permute-start | bytes 393224 | tf_op jit(solution)/shard_map/ppermute | solution.py:105
  65.4 8.1 %collective-permute-start.11 = (bf16[256,512]{1,0:T(8,128)(2,1)S(1)}, bf16[256,512]{1,0:T(8,128)(2,1)S(1)}, u32[]{:S(2)}, u32[]{:S(2)}) collective-permute-start(bf16[256,512]{1,0:T(8,128)(2,1)S(1)} %fusion.5), channel_id=1, source_target_pairs={{0,2},{2,0},{1,3},{3,1},{4,6},{6,4},{5,7},{7,5},{8,10},{10,8},{9,1... | collective-permute-start | bytes 786440 | tf_op jit(solution)/shard_map/ppermute | solution.py:101
  72.8 7.0 %collective-permute-start.14 = (bf16[128,512]{1,0:T(8,128)(2,1)S(1)}, bf16[128,512]{1,0:T(8,128)(2,1)S(1)}, u32[]{:S(2)}, u32[]{:S(2)}) collective-permute-start(bf16[128,512]{1,0:T(8,128)(2,1)S(1)} %fusion.13), channel_id=1, source_target_pairs={{0,8},{4,12},{8,0},{12,4},{1,9},{5,13},{9,1},{13,5},{2,10},{6,14},... | collective-permute-start | bytes 393224 | tf_op jit(solution)/shard_map/ppermute | solution.py:105

commit v24 on v23

--- a/solution.py
+++ b/solution.py
@@ -10,7 +10,6 @@
 
 CHUNKS = 2
 PART = 1024
-ONES = 16
 VMEM_BYTES = 16 * 1024 * 1024
 MOST_VMEM_BYTES = 52 * 1024 * 1024
 LONG = pl.CostEstimate(flops=2 * 10**10, bytes_accessed=1, transcendentals=0)
@@ -113,7 +112,8 @@
     row_max = jnp.max(scores, axis=0, keepdims=True)
     if old_max is not None:
         row_max = jnp.maximum(row_max, old_max)
-    return row_max, jnp.exp2(scores - row_max).astype(jnp.bfloat16)
+    weights = jnp.exp2(scores - row_max)
+    return row_max, weights.astype(jnp.bfloat16), jnp.sum(weights, axis=0, keepdims=True)
 
 
 def dot_queries(keys, query_block):
@@ -324,7 +324,6 @@
     blocks, length, columns = pool_refs[0].shape
     wide = columns // 2
     width = wide // heads
-    values[...] = jnp.ones_like(values)
     for at in range(table_ref.shape[0]):
         entry = table_ref[at]
         here = slice(at * length, (at + 1) * length)
@@ -341,7 +340,7 @@
 def put_values(values, here, block, heads):
     width = block.shape[1] // heads
     for head in range(heads):
-        low = head * (width + ONES)
+        low = head * width
         values[low : low + width, here] = (
             block[:, head * width : (head + 1) * width].astype(jnp.float32).T.astype(jnp.bfloat16)
         )
@@ -351,7 +350,7 @@
     length, columns = pools[0].shape[1:]
     count = table.shape[0] * length
     wide = columns // 2
-    tall = wide + heads * ONES
+    tall = wide
     return pl.pallas_call(
         functools.partial(pick_kernel, heads, len(pools)),
         grid_spec=pltpu.PrefetchScalarGridSpec(
@@ -386,7 +385,7 @@
     terms = refs[held : held + sum(term_counts)]
     acc_ref, stat_ref, *sum_refs, flat = refs[held + sum(term_counts) :]
     rows, width = query_ref.shape
-    tall = width + ONES
+    tall = width
     half = stat_ref.shape[0] // 2
 
     @pl.when(pl.program_id(0) == 0)
@@ -397,13 +396,13 @@
     for head, taken, here in each_part(rows, heads):
         query_block = flat[taken, :].astype(jnp.bfloat16)
         scores = dot_queries(keys[:, head * width : (head + 1) * width], query_block) * scale
-        row_max, weights = softmax_parts(scores)
+        row_max, weights, total = softmax_parts(scores)
         mixed = jnp.dot(
             values[head * tall : (head + 1) * tall, :], weights, preferred_element_type=jnp.float32
         )
         acc_ref[:, here] = mixed[:width]
         stat_ref[:half, here] = jnp.broadcast_to(row_max, (half, row_max.shape[1]))
-        stat_ref[half:, here] = jnp.broadcast_to(mixed[width : width + 1], (half, row_max.shape[1]))
+        stat_ref[half:, here] = jnp.broadcast_to(total, (half, row_max.shape[1]))
 
 
 def prefix_attend(
@@ -463,12 +462,11 @@
     earlier, terms = rest[:early_count], rest[early_count : early_count + term_count]
     out_ref, fresh_ref, keys, values, flat, mixed_rows = rest[-6:]
     rows, width = query_ref.shape
-    wide, tall = heads * width, width + ONES
+    wide, tall = heads * width, width
     step = pl.program_id(0)
 
     @pl.when(step == 0)
     def _():
-        values[...] = jnp.ones_like(values)
         fresh_ref[...] = total_of(terms).astype(fresh_ref.dtype)
         for index, ref in enumerate([*earlier, fresh_ref]):
             here = slice(index * ref.shape[0], (index + 1) * ref.shape[0])
@@ -488,12 +486,12 @@
         key_at = lax.broadcasted_iota(jnp.int32, scores.shape, 0)
         scores = jnp.where(key_at <= token, scores, -jnp.inf)
         old_max, old_total = stat_ref[:1, here], stat_ref[half : half + 1, here]
-        row_max, weights = softmax_parts(scores, old_max)
+        row_max, weights, total = softmax_parts(scores, old_max)
         fade = jnp.exp2(old_max - row_max)
         mixed = jnp.dot(
             values[head * tall : (head + 1) * tall, :], weights, preferred_element_type=jnp.float32
         )
-        row_total = old_total * fade + mixed[width : width + 1]
+        row_total = old_total * fade + total
         share = jnp.where(token < length_ref[0], 1.0 / row_total, 0.0)
         result = acc_ref[:, here] * (fade * share) + mixed[:width] * share
         mixed_rows[taken, :] = result.T
@@ -540,7 +538,7 @@
             out_specs=[block, whole],
             scratch_shapes=[
                 pltpu.VMEM((key_count, heads * width), jnp.bfloat16),
-                pltpu.VMEM((heads * (width + ONES), key_count), jnp.bfloat16),
+                pltpu.VMEM((heads * width, key_count), jnp.bfloat16),
                 pltpu.VMEM((rows, width), jnp.float32),
                 pltpu.VMEM((rows, width), jnp.float32),
             ],

time: 84.7 us -> 84.7 us (level)
    pallas_call x4, Pallas kernels: 14.6 us -> 15.4 us  [prefix_attend(): pl.pallas_call(functools.partial(prefix_kernel, scale, heads, [len(terms)...]
where the time goes in v24:
time: 84.7 us; the launch traced here: 84.6 us
  Pallas kernels  40.4 us (48%)
  waiting for transfers between devices  24.4 us (29%)
  starting transfers between devices  18.2 us (21%)
  between operations  0.87 us (1%)
    ppermute x7, waiting for transfers between devices, trade(): lax.ppermute(array, axis, [(i, i ^ bits) for i in range(lax.axis_size(axi...  23.2 us
    pallas_call x4, Pallas kernels, prefix_attend(): pl.pallas_call(functools.partial(prefix_kernel, scale, heads, [len(terms)...  15.4 us
    ppermute x7, starting transfers between devices, trade(): lax.ppermute(array, axis, [(i, i ^ bits) for i in range(lax.axis_size(axi...  10.4 us
    pallas_call x4, Pallas kernels, project(): pl.pallas_call(functools.partial(project_kernel, len(blocks), [len(terms)...  8.71 us
    pallas_call x2, Pallas kernels, fresh_attend(): pl.pallas_call(functools.partial(fresh_kernel, scale, heads, per_token, c...  8.39 us
    ppermute x8, starting transfers between devices, shift(): lax.ppermute(array, axis, [(i, (i + step) % count) for i in range(count)])  7.81 us
    pallas_call x1, Pallas kernels, arrange_weights(): pl.pallas_call(functools.partial(weight_kernel, ctx_count, heads, head_co...  2.47 us
    pallas_call x1, Pallas kernels, cut_tokens(): pl.pallas_call(functools.partial(cut_kernel, bits), grid_spec=pltpu.Prefe...  2.02 us
  transfers between devices with their start and end apart: 15, of which 8 were waited for; matrix products, arithmetic and copies ran while one was open for 1% of the time, Pallas kernels for 37%

profile of v24, /device:TPU:0, one launch (start us, length us, event | category | flops | bytes accessed | tf_op | source)
XLA Modules:
  0.0 84.6 jit_solution(6372290732288562063)
XLA Ops:
  0.0 0.1 pad_add_fusion.place_ref
  0.1 2.0 %cut_tokens.1 = (bf16[256,1024]{1,0:T(8,128)(2,1)S(1)}, bf16[256,1024]{1,0:T(8,128)(2,1)S(1)}, bf16[256,1024]{1,0:T(8,128)(2,1)S(1)}) custom-call(s32[3]{0:T(128)S(1)} %pad_add_fusion.place_ref, bf16[256,4096]{1,0:T(8,128)(2,1)} %refs_1_.3), custom_call_target="tpu_custom_call" | custom-call | flops 20000000000 | bytes 1 | tf_op jit(solution)/shard_map/cut_tokens/pallas_call | solution.py:180
  2.1 5.1 %collective-permute-start = (bf16[256,1024]{1,0:T(8,128)(2,1)S(1)}, bf16[256,1024]{1,0:T(8,128)(2,1)S(1)}, u32[]{:S(2)}, u32[]{:S(2)}) collective-permute-start(bf16[256,1024]{1,0:T(8,128)(2,1)S(1)} %get-tuple-element.65), channel_id=1, source_target_pairs={{0,12},{4,8},{8,4},{12,0},{1,13},{5,9},{9,5},{13,1},{2,14},{6,10},... | collective-permute-start | bytes 1572872 | tf_op jit(solution)/shard_map/ppermute | solution.py:104
  7.2 0.0 collective-permute-start.1
  7.2 1.9 %arrange_pool.1 = (bf16[8,128,512]{2,1,0:T(8,128)(2,1)S(1)}, bf16[8,128,512]{2,1,0:T(8,128)(2,1)S(1)}) custom-call(s32[3]{0:T(128)S(1)} %pad_add_fusion.place_ref, bf16[8,128,8,128]{3,2,1,0:T(8,128)(2,1)S(1)} %bitcast.45), custom_call_target="tpu_custom_call" | custom-call | flops 20000000000 | bytes 1 | tf_op jit(solution)/shard_map/arrange_pool/pallas_call | solution.py:227
  9.1 1.6 %collective-permute-start.3 = (bf16[8,128,512]{2,1,0:T(8,128)(2,1)S(1)}, bf16[8,128,512]{2,1,0:T(8,128)(2,1)S(1)}, u32[]{:S(2)}, u32[]{:S(2)}) collective-permute-start(bf16[8,128,512]{2,1,0:T(8,128)(2,1)S(1)} %get-tuple-element.75), channel_id=1, source_target_pairs={{0,2},{2,0},{1,3},{3,1},{4,6},{6,4},{5,7},{7,5},{8,10},{10,8},{9,1... | collective-permute-start | bytes 3145736 | tf_op jit(solution)/shard_map/ppermute | solution.py:100
  10.7 2.5 %arrange_weights.1.refs_2_ = bf16[2,2,1024,512]{3,2,1,0:T(8,128)(2,1)S(1)} custom-call(bf16[1024,8,128]{2,1,0:T(8,128)(2,1)S(1)} %bitcast.46, bf16[1024,8,128]{2,1,0:T(8,128)(2,1)S(1)} %bitcast.47), custom_call_target="tpu_custom_call" | custom-call | flops 20000000000 | bytes 1 | tf_op jit(solution)/shard_map/arrange_weights/pallas_call | solution.py:150
  13.2 0.8 collective-permute-start.5
  14.7 5.4 %collective-permute-done.refs_0_ = bf16[256,1024]{1,0:T(8,128)(2,1)S(1)} collective-permute-done((bf16[256,1024]{1,0:T(8,128)(2,1)S(1)}, bf16[256,1024]{1,0:T(8,128)(2,1)S(1)}, u32[]{:S(2)}, u32[]{:S(2)}) %collective-permute-start) | collective-permute-done | bytes 524320 | tf_op jit(solution)/shard_map/ppermute | solution.py:104
  20.1 11.5 %collective-permute-done.1.refs_1_ = bf16[256,1024]{1,0:T(8,128)(2,1)S(1)} collective-permute-done((bf16[256,1024]{1,0:T(8,128)(2,1)S(1)}, bf16[256,1024]{1,0:T(8,128)(2,1)S(1)}, u32[]{:S(2)}, u32[]{:S(2)}) %collective-permute-start.1) | collective-permute-done | bytes 524320 | tf_op jit(solution)/shard_map/ppermute | solution.py:104
  31.5 2.1 %early_away.1 = bf16[2,512,512]{2,1,0:T(8,128)(2,1)S(1)} custom-call(s32[3]{0:T(128)S(1)} %pad_add_fusion.place_ref, bf16[256,1024]{1,0:T(8,128)(2,1)S(1)} %collective-permute-done.refs_0_, bf16[256,1024]{1,0:T(8,128)(2,1)S(1)} %collective-permute-done.1.refs_1_, bf16[2,2,1024,512]{3,2,1,0:T(8,128)(2,1)S(1)} %arrange_weights.1.refs_2_), custom_call_target="tpu_custom_call" | custom-call | flops 20000000000 | bytes 1 | tf_op jit(solution)/shard_map/early_away/pallas_call | solution.py:291
  33.6 0.1 collective-permute-start.2
  33.7 2.1 %early_kept.1.refs_0_.refs_3_ = f32[2,512,512]{2,1,0:T(8,128)S(1)} custom-call(s32[3]{0:T(128)S(1)} %pad_add_fusion.place_ref, bf16[256,1024]{1,0:T(8,128)(2,1)S(1)} %collective-permute-done.refs_0_, bf16[256,1024]{1,0:T(8,128)(2,1)S(1)} %collective-permute-done.1.refs_1_, bf16[2,2,1024,512]{3,2,1,0:T(8,128)(2,1)S(1)} %arrange_weights.1.refs_2_), custom_call_target="tpu_custom_call" | custom-call | flops 20000000000 | bytes 1 | tf_op jit(solution)/shard_map/early_kept/pallas_call | solution.py:291
  35.8 0.0 copy-start.5
  35.8 0.5 collective-permute-done.2.refs_1_.refs_4_
  36.3 0.2 fusion.4
  36.5 0.0 collective-permute-done.3.refs_1_
  36.5 1.4 %collective-permute-start.4 = (bf16[256,512]{1,0:T(8,128)(2,1)S(1)}, bf16[256,512]{1,0:T(8,128)(2,1)S(1)}, u32[]{:S(2)}, u32[]{:S(2)}) collective-permute-start(bf16[256,512]{1,0:T(8,128)(2,1)S(1)} %get-tuple-element.82), channel_id=1, source_target_pairs={{0,2},{2,0},{1,3},{3,1},{4,6},{6,4},{5,7},{7,5},{8,10},{10,8},{9,1... | collective-permute-start | bytes 786440 | tf_op jit(solution)/shard_map/ppermute | solution.py:100
  38.0 0.6 collective-permute-start.6
  38.6 1.5 %pick_blocks.1 = (bf16[1024,256]{1,0:T(8,128)(2,1)S(1)}, bf16[256,1024]{1,0:T(8,128)(2,1)S(1)}) custom-call(s32[3]{0:T(128)S(1)} %pad_add_fusion.place_ref, s32[8]{0:T(128)S(1)} %bitcast.54, bf16[8,128,512]{2,1,0:T(8,128)(2,1)S(1)} %get-tuple-element.76.refs_0_, bf16[8,128,512]{2,1,0:T(8,128)(2,1)S(1)} %collective-permute-done.3.refs_1_), custom_call_target="tpu_custom_call" | custom-call | flops 20000000000 | bytes 1 | tf_op jit(solution)/shard_map/pick_blocks/pallas_call | solution.py:354
  40.1 0.1 copy-done.4
  40.2 7.6 %prefix_attend.4 = (f32[128,4096]{1,0:T(8,128)S(1)}, f32[8,4096]{1,0:T(8,128)S(1)}) custom-call(bf16[8192,128]{1,0:T(8,128)(2,1)S(1)} %bitcast.48, bf16[1024,256]{1,0:T(8,128)(2,1)S(1)} %get-tuple-element.89.keys, bf16[256,1024]{1,0:T(8,128)(2,1)S(1)} %get-tuple-element.90.values), custom_call_target="tpu_custom_call" | custom-call | flops 20000000000 | bytes 1 | tf_op jit(solution)/shard_map/prefix_attend/pallas_call | solution.py:437
  47.8 0.0 copy-start.3
  47.9 3.9 %prefix_attend.5 = (f32[128,4096]{1,0:T(8,128)S(1)}, f32[8,4096]{1,0:T(8,128)S(1)}, bf16[256,512]{1,0:T(8,128)(2,1)S(1)}) custom-call(bf16[8192,128]{1,0:T(8,128)(2,1)S(1)} %bitcast.49, bf16[1024,256]{1,0:T(8,128)(2,1)S(1)} %get-tuple-element.89.keys, bf16[256,1024]{1,0:T(8,128)(2,1)S(1)} %get-tuple-element.90.values, ...), custom_call_target="tpu_custom_call" | custom-call | flops 20000000000 | bytes 1 | tf_op jit(solution)/shard_map/prefix_attend/pallas_call | solution.py:437
  51.8 0.2 collective-permute-done.5.refs_0_
  52.0 2.2 %late_away.1 = (bf16[2,512,512]{2,1,0:T(8,128)(2,1)S(1)}, bf16[256,512]{1,0:T(8,128)(2,1)S(1)}) custom-call(s32[3]{0:T(128)S(1)} %pad_add_fusion.place_ref, bf16[256,1024]{1,0:T(8,128)(2,1)S(1)} %collective-permute-done.5.refs_0_, bf16[256,4096]{1,0:T(8,128)(2,1)S(1)} %copy-done.3, bf16[2,2,1024,512]{3,2,1,0:T(8,128)(2,1)S(1)} %arrange_weights.1.refs_2_, ...), custom_call_target="tpu_custom_call" | custom-call | flops 20000000000 | bytes 1 | tf_op jit(solution)/shard_map/late_away/pallas_call | solution.py:291
  54.2 0.1 collective-permute-start.7
  54.3 1.6 %collective-permute-start.9 = (bf16[256,512]{1,0:T(8,128)(2,1)S(1)}, bf16[256,512]{1,0:T(8,128)(2,1)S(1)}, u32[]{:S(2)}, u32[]{:S(2)}) collective-permute-start(bf16[256,512]{1,0:T(8,128)(2,1)S(1)} %get-tuple-element.91), channel_id=1, source_target_pairs={{0,4},{4,0},{8,12},{12,8},{1,5},{5,1},{9,13},{13,9},{2,6},{6,2},{1... | collective-permute-start | bytes 786440 | tf_op jit(solution)/shard_map/ppermute | solution.py:104
  55.9 0.5 collective-permute-start.12
  56.4 2.3 %late_kept.1.rest_0_.rest_1_ = f32[2,512,512]{2,1,0:T(8,128)S(1)} custom-call(s32[3]{0:T(128)S(1)} %pad_add_fusion.place_ref, bf16[256,1024]{1,0:T(8,128)(2,1)S(1)} %collective-permute-done.5.refs_0_, bf16[256,4096]{1,0:T(8,128)(2,1)S(1)} %copy-done.3, bf16[2,2,1024,512]{3,2,1,0:T(8,128)(2,1)S(1)} %arrange_weights.1.refs_2_), custom_call_target="tpu_custom_call" | custom-call | flops 20000000000 | bytes 1 | tf_op jit(solution)/shard_map/late_kept/pallas_call | solution.py:291
  58.7 0.1 fusion.15
  58.8 1.5 %collective-permute-start.8 = (bf16[128,512]{1,0:T(8,128)(2,1)S(1)}, bf16[128,512]{1,0:T(8,128)(2,1)S(1)}, u32[]{:S(2)}, u32[]{:S(2)}) collective-permute-start(bf16[128,512]{1,0:T(8,128)(2,1)S(1)} %get-tuple-element.119), channel_id=1, source_target_pairs={{0,2},{2,0},{1,3},{3,1},{4,6},{6,4},{5,7},{7,5},{8,10},{10,8},{9,1... | collective-permute-start | bytes 393224 | tf_op jit(solution)/shard_map/ppermute | solution.py:100
  60.4 2.0 %prefix_attend.6 = (f32[128,4096]{1,0:T(8,128)S(1)}, f32[8,4096]{1,0:T(8,128)S(1)}) custom-call(bf16[8192,128]{1,0:T(8,128)(2,1)S(1)} %bitcast.50, bf16[1024,256]{1,0:T(8,128)(2,1)S(1)} %get-tuple-element.89.keys, bf16[256,1024]{1,0:T(8,128)(2,1)S(1)} %get-tuple-element.90.values, ...), custom_call_target="tpu_custom_call", output_to_operand_aliasing={{0}: (3, {}), {1}: (4, {})} | custom-call | flops 20000000000 | bytes 1 | tf_op jit(solution)/shard_map/prefix_attend/pallas_call | solution.py:437
  62.3 0.1 fusion.5
  62.4 0.6 collective-permute-start.10
  63.0 0.5 collective-permute-done.9
  63.5 0.7 collective-permute-done.8
  64.2 0.1 fusion.10
  64.2 1.4 %collective-permute-start.13 = (bf16[128,512]{1,0:T(8,128)(2,1)S(1)}, bf16[128,512]{1,0:T(8,128)(2,1)S(1)}, u32[]{:S(2)}, u32[]{:S(2)}) collective-permute-start(bf16[128,512]{1,0:T(8,128)(2,1)S(1)} %fusion.10), channel_id=1, source_target_pairs={{0,8},{4,12},{8,0},{12,4},{1,9},{5,13},{9,1},{13,5},{2,10},{6,14},... | collective-permute-start | bytes 393224 | tf_op jit(solution)/shard_map/ppermute | solution.py:104
  65.6 1.9 %collective-permute-start.11 = (bf16[256,512]{1,0:T(8,128)(2,1)S(1)}, bf16[256,512]{1,0:T(8,128)(2,1)S(1)}, u32[]{:S(2)}, u32[]{:S(2)}) collective-permute-start(bf16[256,512]{1,0:T(8,128)(2,1)S(1)} %fusion.5), channel_id=1, source_target_pairs={{0,2},{2,0},{1,3},{3,1},{4,6},{6,4},{5,7},{7,5},{8,10},{10,8},{9,1... | collective-permute-start | bytes 786440 | tf_op jit(solution)/shard_map/ppermute | solution.py:100
  67.5 2.0 %prefix_attend.7 = (f32[128,4096]{1,0:T(8,128)S(1)}, f32[8,4096]{1,0:T(8,128)S(1)}) custom-call(bf16[8192,128]{1,0:T(8,128)(2,1)S(1)} %bitcast.51, bf16[1024,256]{1,0:T(8,128)(2,1)S(1)} %get-tuple-element.89.keys, bf16[256,1024]{1,0:T(8,128)(2,1)S(1)} %get-tuple-element.90.values, ...), custom_call_target="tpu_custom_call", output_to_operand_aliasing={{0}: (3, {}), {1}: (4, {})} | custom-call | flops 20000000000 | bytes 1 | tf_op jit(solution)/shard_map/prefix_attend/pallas_call | solution.py:437
  69.5 0.1 fusion.13
  69.5 3.5 %collective-permute-done.13.rest_4_ = bf16[128,512]{1,0:T(8,128)(2,1)S(1)} collective-permute-done((bf16[128,512]{1,0:T(8,128)(2,1)S(1)}, bf16[128,512]{1,0:T(8,128)(2,1)S(1)}, u32[]{:S(2)}, u32[]{:S(2)}) %collective-permute-start.13) | collective-permute-done | bytes 131104 | tf_op jit(solution)/shard_map/ppermute | solution.py:104
  73.0 1.0 %collective-permute-start.14 = (bf16[128,512]{1,0:T(8,128)(2,1)S(1)}, bf16[128,512]{1,0:T(8,128)(2,1)S(1)}, u32[]{:S(2)}, u32[]{:S(2)}) collective-permute-start(bf16[128,512]{1,0:T(8,128)(2,1)S(1)} %fusion.13), channel_id=1, source_target_pairs={{0,8},{4,12},{8,0},{12,4},{1,9},{5,13},{9,1},{13,5},{2,10},{6,14},... | collective-permute-start | bytes 393224 | tf_op jit(solution)/shard_map/ppermute | solution.py:104
  74.0 0.0 collective-permute-done.12.rest_3_.rest_4_
  74.0 3.9 %fresh_attend.2 = (bf16[8192,128]{1,0:T(8,128)(2,1)}, bf16[128,512]{1,0:T(8,128)(2,1)S(1)}) custom-call(s32[1]{0:T(128)S(6)} %copy.21.length_ref, bf16[8192,128]{1,0:T(8,128)(2,1)S(1)} %bitcast.52, f32[128,4096]{1,0:T(8,128)S(1)} %get-tuple-element.104.acc_ref, f32[8,4096]{1,0:T(8,128)S(1)} %get-tuple-element.105.stat_ref, ...), custom_call_target="tpu_custom_call" | custom-call | flops 20000000000 | bytes 1 | tf_op jit(solution)/shard_map/fresh_attend/pallas_call | solution.py:525
  77.9 2.2 %collective-permute-done.14.rest_5_ = bf16[128,512]{1,0:T(8,128)(2,1)S(1)} collective-permute-done((bf16[128,512]{1,0:T(8,128)(2,1)S(1)}, bf16[128,512]{1,0:T(8,128)(2,1)S(1)}, u32[]{:S(2)}, u32[]{:S(2)}) %collective-permute-start.14) | collective-permute-done | bytes 131104 | tf_op jit(solution)/shard_map/ppermute | solution.py:104
  80.1 4.5 %fresh_attend.3 = (bf16[8192,128]{1,0:T(8,128)(2,1)}, bf16[128,512]{1,0:T(8,128)(2,1)}) custom-call(s32[1]{0:T(128)S(6)} %copy.21.length_ref, bf16[8192,128]{1,0:T(8,128)(2,1)S(1)} %bitcast.53, f32[128,4096]{1,0:T(8,128)S(1)} %get-tuple-element.102.acc_ref, f32[8,4096]{1,0:T(8,128)S(1)} %get-tuple-element.103.stat_ref, ...), custom_call_target="tpu_custom_call", output_to_operand_aliasing={{0}: (10, {})} | custom-call | flops 20000000000 | bytes 1 | tf_op jit(solution)/shard_map/fresh_attend/pallas_call | solution.py:525
  (14 shorter events, 0.0 us)
Async XLA Ops:
  0.1 7.1 %copy-start = (bf16[8,128,4,1,256]{4,2,3,1,0:T(4,128)(2,1)S(1)}, bf16[8,128,4,1,256]{4,2,3,1,0:T(4,128)(2,1)}, u32[]{:S(2)}) copy-start(bf16[8,128,4,1,256]{4,2,3,1,0:T(4,128)(2,1)} %param.11) | copy-start | bytes 6291460
  2.1 18.0 %collective-permute-start = (bf16[256,1024]{1,0:T(8,128)(2,1)S(1)}, bf16[256,1024]{1,0:T(8,128)(2,1)S(1)}, u32[]{:S(2)}, u32[]{:S(2)}) collective-permute-start(bf16[256,1024]{1,0:T(8,128)(2,1)S(1)} %get-tuple-element.65), channel_id=1, source_target_pairs={{0,12},{4,8},{8,4},{12,0},{1,13},{5,9},{9,5},{13,1},{2,14},{6,10},... | collective-permute-start | bytes 1572872 | tf_op jit(solution)/shard_map/ppermute | solution.py:104
  7.2 24.3 %collective-permute-start.1 = (bf16[256,1024]{1,0:T(8,128)(2,1)S(1)}, bf16[256,1024]{1,0:T(8,128)(2,1)S(1)}, u32[]{:S(2)}, u32[]{:S(2)}) collective-permute-start(bf16[256,1024]{1,0:T(8,128)(2,1)S(1)} %get-tuple-element.66), channel_id=1, source_target_pairs={{0,4},{4,0},{8,12},{12,8},{1,5},{5,1},{9,13},{13,9},{2,6},{6,2},{1... | collective-permute-start | bytes 1572872 | tf_op jit(solution)/shard_map/ppermute | solution.py:104
  7.2 3.5 %copy-start.1 = (bf16[1,1,1024,4,2,128]{5,4,3,2,1,0:T(2,128)(2,1)S(1)}, bf16[1,1,1024,4,2,128]{5,4,3,2,1,0:T(2,128)(2,1)}, u32[]{:S(2)}) copy-start(bf16[1,1,1024,4,2,128]{5,4,3,2,1,0:T(2,128)(2,1)} %param.8) | copy-start | bytes 6291460
  7.2 3.5 %copy-start.2 = (bf16[1,1,1024,4,2,128]{5,4,3,2,1,0:T(2,128)(2,1)S(1)}, bf16[1,1,1024,4,2,128]{5,4,3,2,1,0:T(2,128)(2,1)}, u32[]{:S(2)}) copy-start(bf16[1,1,1024,4,2,128]{5,4,3,2,1,0:T(2,128)(2,1)} %param.9) | copy-start | bytes 6291460
  9.1 27.4 %collective-permute-start.3 = (bf16[8,128,512]{2,1,0:T(8,128)(2,1)S(1)}, bf16[8,128,512]{2,1,0:T(8,128)(2,1)S(1)}, u32[]{:S(2)}, u32[]{:S(2)}) collective-permute-start(bf16[8,128,512]{2,1,0:T(8,128)(2,1)S(1)} %get-tuple-element.75), channel_id=1, source_target_pairs={{0,2},{2,0},{1,3},{3,1},{4,6},{6,4},{5,7},{7,5},{8,10},{10,8},{9,1... | collective-permute-start | bytes 3145736 | tf_op jit(solution)/shard_map/ppermute | solution.py:100
  13.2 38.8 %collective-permute-start.5 = (bf16[256,1024]{1,0:T(8,128)(2,1)S(1)}, bf16[256,1024]{1,0:T(8,128)(2,1)S(1)}, u32[]{:S(2)}, u32[]{:S(2)}) collective-permute-start(bf16[256,1024]{1,0:T(8,128)(2,1)S(1)} %get-tuple-element.85), channel_id=1, source_target_pairs={{0,8},{4,12},{8,0},{12,4},{1,9},{5,13},{9,1},{13,5},{2,10},{6,14},... | collective-permute-start | bytes 1572872 | tf_op jit(solution)/shard_map/ppermute | solution.py:104
  33.6 2.7 %collective-permute-start.2 = (bf16[2,512,512]{2,1,0:T(8,128)(2,1)S(1)}, bf16[2,512,512]{2,1,0:T(8,128)(2,1)S(1)}, u32[]{:S(2)}, u32[]{:S(2)}) collective-permute-start(bf16[2,512,512]{2,1,0:T(8,128)(2,1)S(1)} %early_away.1), channel_id=1, source_target_pairs={{0,1},{1,0},{2,3},{3,2},{4,5},{5,4},{6,7},{7,6},{8,9},{9,8},{10,11... | collective-permute-start | bytes 3145736 | tf_op jit(solution)/shard_map/ppermute | solution.py:100
  35.8 2.8 %copy-start.5 = (s32[1,8]{1,0:T(1,128)S(1)}, s32[1,8]{1,0:T(1,128)}, u32[]{:S(2)}) copy-start(s32[1,8]{1,0:T(1,128)} %param.12) | copy-start | bytes 100
  36.5 11.3 %collective-permute-start.4 = (bf16[256,512]{1,0:T(8,128)(2,1)S(1)}, bf16[256,512]{1,0:T(8,128)(2,1)S(1)}, u32[]{:S(2)}, u32[]{:S(2)}) collective-permute-start(bf16[256,512]{1,0:T(8,128)(2,1)S(1)} %get-tuple-element.82), channel_id=1, source_target_pairs={{0,2},{2,0},{1,3},{3,1},{4,6},{6,4},{5,7},{7,5},{8,10},{10,8},{9,1... | collective-permute-start | bytes 786440 | tf_op jit(solution)/shard_map/ppermute | solution.py:100
  38.0 14.0 %collective-permute-start.6 = (bf16[256,512]{1,0:T(8,128)(2,1)S(1)}, bf16[256,512]{1,0:T(8,128)(2,1)S(1)}, u32[]{:S(2)}, u32[]{:S(2)}) collective-permute-start(bf16[256,512]{1,0:T(8,128)(2,1)S(1)} %get-tuple-element.87), channel_id=1, source_target_pairs={{0,2},{2,0},{1,3},{3,1},{4,6},{6,4},{5,7},{7,5},{8,10},{10,8},{9,1... | collective-permute-start | bytes 786440 | tf_op jit(solution)/shard_map/ppermute | solution.py:100
  38.6 1.6 %copy-start.4 = (bf16[256,2,1,2048]{3,1,2,0:T(2,128)(2,1)S(1)}, bf16[256,2,1,2048]{3,1,2,0:T(2,128)(2,1)}, u32[]{:S(2)}) copy-start(bf16[256,2,1,2048]{3,1,2,0:T(2,128)(2,1)} %param.10) | copy-start | bytes 6291460
  47.8 4.2 %copy-start.3 = (bf16[256,4096]{1,0:T(8,128)(2,1)S(1)}, bf16[256,4096]{1,0:T(8,128)(2,1)}, u32[]{:S(2)}) copy-start(bf16[256,4096]{1,0:T(8,128)(2,1)} %refs_1_.3) | copy-start | bytes 6291460
  54.2 4.5 %collective-permute-start.7 = (bf16[2,512,512]{2,1,0:T(8,128)(2,1)S(1)}, bf16[2,512,512]{2,1,0:T(8,128)(2,1)S(1)}, u32[]{:S(2)}, u32[]{:S(2)}) collective-permute-start(bf16[2,512,512]{2,1,0:T(8,128)(2,1)S(1)} %get-tuple-element.88), channel_id=1, source_target_pairs={{0,1},{1,0},{2,3},{3,2},{4,5},{5,4},{6,7},{7,6},{8,9},{9,8},{10,11... | collective-permute-start | bytes 3145736 | tf_op jit(solution)/shard_map/ppermute | solution.py:100
  54.3 9.2 %collective-permute-start.9 = (bf16[256,512]{1,0:T(8,128)(2,1)S(1)}, bf16[256,512]{1,0:T(8,128)(2,1)S(1)}, u32[]{:S(2)}, u32[]{:S(2)}) collective-permute-start(bf16[256,512]{1,0:T(8,128)(2,1)S(1)} %get-tuple-element.91), channel_id=1, source_target_pairs={{0,4},{4,0},{8,12},{12,8},{1,5},{5,1},{9,13},{13,9},{2,6},{6,2},{1... | collective-permute-start | bytes 786440 | tf_op jit(solution)/shard_map/ppermute | solution.py:104
  55.9 18.1 %collective-permute-start.12 = (bf16[256,512]{1,0:T(8,128)(2,1)S(1)}, bf16[256,512]{1,0:T(8,128)(2,1)S(1)}, u32[]{:S(2)}, u32[]{:S(2)}) collective-permute-start(bf16[256,512]{1,0:T(8,128)(2,1)S(1)} %get-tuple-element.110), channel_id=1, source_target_pairs={{0,4},{4,0},{8,12},{12,8},{1,5},{5,1},{9,13},{13,9},{2,6},{6,2},{1... | collective-permute-start | bytes 786440 | tf_op jit(solution)/shard_map/ppermute | solution.py:104
  58.8 5.4 %collective-permute-start.8 = (bf16[128,512]{1,0:T(8,128)(2,1)S(1)}, bf16[128,512]{1,0:T(8,128)(2,1)S(1)}, u32[]{:S(2)}, u32[]{:S(2)}) collective-permute-start(bf16[128,512]{1,0:T(8,128)(2,1)S(1)} %get-tuple-element.119), channel_id=1, source_target_pairs={{0,2},{2,0},{1,3},{3,1},{4,6},{6,4},{5,7},{7,5},{8,10},{10,8},{9,1... | collective-permute-start | bytes 393224 | tf_op jit(solution)/shard_map/ppermute | solution.py:100
  62.4 7.0 %collective-permute-start.10 = (bf16[128,512]{1,0:T(8,128)(2,1)S(1)}, bf16[128,512]{1,0:T(8,128)(2,1)S(1)}, u32[]{:S(2)}, u32[]{:S(2)}) collective-permute-start(bf16[128,512]{1,0:T(8,128)(2,1)S(1)} %get-tuple-element.106), channel_id=1, source_target_pairs={{0,2},{2,0},{1,3},{3,1},{4,6},{6,4},{5,7},{7,5},{8,10},{10,8},{9,1... | collective-permute-start | bytes 393224 | tf_op jit(solution)/shard_map/ppermute | solution.py:100
  64.2 8.7 %collective-permute-start.13 = (bf16[128,512]{1,0:T(8,128)(2,1)S(1)}, bf16[128,512]{1,0:T(8,128)(2,1)S(1)}, u32[]{:S(2)}, u32[]{:S(2)}) collective-permute-start(bf16[128,512]{1,0:T(8,128)(2,1)S(1)} %fusion.10), channel_id=1, source_target_pairs={{0,8},{4,12},{8,0},{12,4},{1,9},{5,13},{9,1},{13,5},{2,10},{6,14},... | collective-permute-start | bytes 393224 | tf_op jit(solution)/shard_map/ppermute | solution.py:104
  65.6 8.4 %collective-permute-start.11 = (bf16[256,512]{1,0:T(8,128)(2,1)S(1)}, bf16[256,512]{1,0:T(8,128)(2,1)S(1)}, u32[]{:S(2)}, u32[]{:S(2)}) collective-permute-start(bf16[256,512]{1,0:T(8,128)(2,1)S(1)} %fusion.5), channel_id=1, source_target_pairs={{0,2},{2,0},{1,3},{3,1},{4,6},{6,4},{5,7},{7,5},{8,10},{10,8},{9,1... | collective-permute-start | bytes 786440 | tf_op jit(solution)/shard_map/ppermute | solution.py:100
  73.0 7.1 %collective-permute-start.14 = (bf16[128,512]{1,0:T(8,128)(2,1)S(1)}, bf16[128,512]{1,0:T(8,128)(2,1)S(1)}, u32[]{:S(2)}, u32[]{:S(2)}) collective-permute-start(bf16[128,512]{1,0:T(8,128)(2,1)S(1)} %fusion.13), channel_id=1, source_target_pairs={{0,8},{4,12},{8,0},{12,4},{1,9},{5,13},{9,1},{13,5},{2,10},{6,14},... | collective-permute-start | bytes 393224 | tf_op jit(solution)/shard_map/ppermute | solution.py:104
